TPU v7x, 32 devices: a whole 2x2x4 slice. The times are simulated.
32 devices in a mesh: section: 2 (over y), expert: 16 (over z, x, core).
Axes of the slice: x: 2, y: 2, z: 4, core: 2. Of those that a mesh axis runs over, the one named last changes fastest.
Arguments:
- fresh: bfloat16 [2048, 2048], P('expert'), may hold values from -6 to 6
- previous: bfloat16 [2, 2048, 2048], P('section', 'expert'), may hold values from -6 to 6
- norm_gain: float32 [2, 2048], P('section'), may hold values from 0.1 to 1.9
- routes: int32 [2, 2048, 8], P('section', 'expert'), may hold values from 0 to 15, all different within a row; in each aligned block of 128 rows (0 to 127, 128 to 255, ..., all dimensions but the last counted through in order) at most 68 rows name the same one
- gate_weights: float32 [2, 2048, 8], P('section', 'expert'), may hold values from 0.03 to 0.3
- w_gate_up: bfloat16 [2, 16, 2048, 1536], P('section', 'expert'), may hold values from -0.125 to 0.125
- w_down: bfloat16 [2, 16, 768, 2048], P('section', 'expert'), may hold values from -0.21875 to 0.21875
Outputs:
- section_output: bfloat16 [2, 2048, 2048], P('section', 'expert')
Inputs may be any that keep to these rules, and one draw needn't show every extreme that they name: `routes`: within one section, among the 128 tokens of one device (aligned blocks of tokens) no expert is chosen by more than 68 tokens, and some expert is chosen by exactly 68 of them; the 8 experts of a token differ.
All inputs are finite; a program needn't handle non-finite values.
Results may differ from a plain program's by a relative error of at most 0.0033.
Values may be sent and summed in bfloat16 or wider, within the bound.
No kernel may reach another device: no remote copies, remote signals or barrier semaphores. Data moves between devices by JAX's collectives and lax.ppermute only.
A program may use at most 64 MiB of HBM per device.

v0:
```python
import jax
import jax.numpy as jnp
from jax import lax
from jax.sharding import PartitionSpec as P

epsilon = 1e-06


def from_behind(value, axis, by):
    peers = lax.axis_size(axis)
    pairs = [(i, i + by) for i in range(peers) if 0 <= i + by < peers]
    return lax.ppermute(value, axis, pairs)


def body(fresh, previous, norm_gain, routes, gate_weights, w_gate_up, w_down):
    devices_exp = lax.axis_size("expert")
    section_id = lax.axis_index("section")
    tok_dev = fresh.shape[0]
    width = fresh.shape[1]
    topk_count = routes.shape[2]
    local_experts = w_gate_up.shape[1]
    hidden_units = w_down.shape[2]
    experts_total = devices_exp * local_experts
    capacity = min(tok_dev, 17 * tok_dev * topk_count // (16 * experts_total))
    total_rows = tok_dev * topk_count
    arrived = from_behind(previous[0], "section", 1)
    arrival = jnp.where(section_id == 0, fresh, arrived)
    wide_input = arrival.astype(jnp.float32)
    scale = lax.rsqrt(jnp.mean(wide_input * wide_input, axis=-1, keepdims=True) + epsilon)
    normed = (wide_input * scale * norm_gain[0][None, :]).astype(jnp.bfloat16)
    flat_ids = routes[0].reshape(-1)
    one_hot = (flat_ids[:, None] == jnp.arange(experts_total, dtype=jnp.int32)[None, :]).astype(
        jnp.int32
    )
    slot_rank = jnp.sum(jnp.cumsum(one_hot, axis=0) * one_hot, axis=1) - 1
    position = flat_ids * capacity + slot_rank
    source_row = (
        jnp.full((experts_total * capacity,), total_rows, jnp.int32)
        .at[position]
        .set(jnp.arange(total_rows, dtype=jnp.int32))
    )
    padded = jnp.concatenate([normed, jnp.zeros((1, width), jnp.bfloat16)], axis=0)
    send_buffer = padded[source_row // topk_count].reshape(
        devices_exp, local_experts, capacity, width
    )
    received = lax.all_to_all(send_buffer, "expert", split_axis=0, concat_axis=0, tiled=True)
    projected = jnp.einsum(
        "secd,edf->secf", received, w_gate_up[0], preferred_element_type=jnp.float32
    )
    hidden = (jax.nn.silu(projected[..., :hidden_units]) * projected[..., hidden_units:]).astype(
        jnp.bfloat16
    )
    returned = lax.all_to_all(
        jnp.einsum("secf,efd->secd", hidden, w_down[0], preferred_element_type=jnp.float32).astype(
            jnp.bfloat16
        ),
        "expert",
        split_axis=0,
        concat_axis=0,
        tiled=True,
    )
    flat_back = returned.reshape(experts_total * capacity, width)
    picked = flat_back[position].reshape(tok_dev, topk_count, width).astype(jnp.float32)
    mixed = jnp.sum(picked * gate_weights[0][:, :, None], axis=1)
    return (wide_input + mixed).astype(jnp.bfloat16)[None]


def solution(mesh):
    return jax.shard_map(
        body,
        mesh=mesh,
        in_specs=(
            P("expert", None),
            P("section", "expert", None),
            P("section", None),
            P("section", "expert", None),
            P("section", "expert", None),
            P("section", "expert", None, None),
            P("section", "expert", None, None),
        ),
        out_specs=P("section", "expert", None),
        check_vma=False,
    )
```

profile of v0, /device:TPU:15, one launch (start us, length us, event | category | flops | bytes accessed | tf_op | source)
XLA Modules:
  0.0 299.7 jit_solution(8841609895756373831)
XLA Ops:
  0.0 0.0 copy-start
  0.0 1.5 collective-permute-start
  1.6 0.8 copy.18
  2.3 0.1 eq.33
  2.4 0.1 eq.29
  2.5 0.7 broadcast_multiply_fusion
  3.2 4.5 %reduce-window.6 = s32[16,8,128]{2,1,0:T(8,128)S(1)} reduce-window(s32[16,8,128]{2,1,0:T(8,128)S(1)} %fusion.20, s32[]{:T(128)} %constant.21.clone.1), window={size=1x1x128 pad=0_0x0_0x127_0}, to_apply=%region_1.2 | reduce-window | flops 2080768 | bytes 131076 | tf_op jit(solution)/shard_map/reduce-window
  7.8 0.1 slice.20
  7.8 0.1 copy.20
  8.0 0.1 copy.21
  8.1 0.1 broadcast_add_fusion
  8.2 0.1 copy.17
  8.3 0.1 mul.65
  8.4 4.3 %scatter_custom_fusion = s32[1088]{0:T(1024)S(1)} fusion(s32[1024]{0:T(1024)S(1)} %bitcast.62, s32[1024]{0:T(1024)S(1)} %iota.11, s32[]{:T(128)} %constant.42.clone.1), kind=kCustom, calls=%fused_computation.40 | custom fusion | bytes 4356 | tf_op jit(solution)/shard_map/scatter | solution.py:40
  12.8 2.5 collective-permute-done
  15.3 1.3 fusion.13
  16.6 0.0 copy-start.1
  16.6 0.8 copy-done.1
  17.4 0.9 fusion.15
  18.3 0.8 concatenate.3
  19.1 11.7 %gather_fusion = bf16[1088,2048]{1,0:T(8,128)(2,1)} fusion(bf16[129,2048]{1,0:T(8,128)(2,1)} %concatenate.3, s32[2048]{0:T(1024)S(1)} %pad_clamp_fusion), kind=kCustom, calls=%fused_computation | custom fusion | bytes 8917248 | tf_op jit(solution)/shard_map/gather | solution.py:43
  30.8 7.0 %reshape.86 = bf16[16,1,68,2048]{3,2,0,1:T(8,128)(2,1)} reshape(bf16[1088,2048]{1,0:T(8,128)(2,1)} %gather_fusion) | data formatting | bytes 8912896 | tf_op jit(solution)/shard_map/reshape | solution.py:43
  37.9 110.9 %all_to_all.10 = bf16[16,1,68,2048]{3,2,1,0:T(8,128)(2,1)S(1)} all-to-all(bf16[16,1,68,2048]{3,2,1,0:T(8,128)(2,1)} %bitcast.59), channel_id=1, replica_groups=mesh['section'=2,'expert'=16] {'expert'}, dimensions={0} | all-to-all | bytes 8912896 | tf_op jit(solution)/shard_map/all_to_all | solution.py:46
  148.8 9.8 %fusion.4 = f32[16,1,68,1536]{3,2,0,1:T(8,128)S(1)} fusion(bf16[1,1,2048,1536]{3,2,1,0:T(8,128)(2,1)} %param.12, bf16[16,1,68,2048]{3,2,1,0:T(8,128)(2,1)S(1)} %all_to_all.10), kind=kOutput, calls=%fused_computation.9 | convolution fusion | flops 6845104128 | bytes 17432576 | tf_op jit(solution)/shard_map/secd,edf->secf/dot_general | solution.py:47
  158.5 0.0 copy-done
  158.5 5.7 %convert_bitcast_fusion = bf16[16,1,68,2048]{3,2,1,0:T(8,128)(2,1)} fusion(bf16[1,1,768,2048]{3,2,1,0:T(8,128)(2,1)S(1)} %copy-done, f32[16,1,68,1536]{3,2,0,1:T(8,128)S(1)} %fusion.4), kind=kOutput, calls=%fused_computation.8 | convolution fusion | flops 3429793792 | bytes 14286848 | tf_op jit(solution)/shard_map/secf,efd->secd/dot_general | solution.py:54
  164.3 0.0 copy-start.3
  164.3 5.5 %all-to-all-start.1 = ((bf16[16,1,68,2048]{3,2,1,0:T(8,128)(2,1)}), bf16[16,1,68,2048]{3,2,1,0:T(8,128)(2,1)}, u32[]{:S(2)}, u32[]{:S(2)}) async-start(bf16[16,1,68,2048]{3,2,1,0:T(8,128)(2,1)} %convert_bitcast_fusion), calls=%async_computation.1 | async-start | bytes 9437184 | tf_op jit(solution)/shard_map/all_to_all | solution.py:53
  169.7 0.0 copy-done.3
  169.7 0.1 copy.24
  169.9 103.6 %all-to-all-done.1 = bf16[16,1,68,2048]{3,2,1,0:T(8,128)(2,1)} async-done(((bf16[16,1,68,2048]{3,2,1,0:T(8,128)(2,1)}), bf16[16,1,68,2048]{3,2,1,0:T(8,128)(2,1)}, u32[]{:S(2)}, u32[]{:S(2)}) %all-to-all-start.1) | async-done | bytes 4456480 | tf_op jit(solution)/shard_map/all_to_all | solution.py:53
  273.4 7.1 %reshape.91 = bf16[1088,2048]{1,0:T(8,128)(2,1)} reshape(bf16[16,1,68,2048]{3,2,1,0:T(8,128)(2,1)} %all-to-all-done.1) | data formatting | bytes 8912896 | tf_op jit(solution)/shard_map/reshape | solution.py:62
  280.5 11.7 %gather_fusion.1 = bf16[1024,2048]{1,0:T(8,128)(2,1)} fusion(bf16[1088,2048]{1,0:T(8,128)(2,1)} %reshape.91, s32[1024]{0:T(1024)S(1)} %broadcast_clamp_fusion), kind=kCustom, calls=%fused_computation.1 | custom fusion | bytes 8392704 | tf_op jit(solution)/shard_map/gather | solution.py:63
  292.2 0.0 copy-start.2
  292.2 6.6 %fusion = f32[128,2048]{1,0:T(8,128)S(1)} fusion(bf16[1024,2048]{1,0:T(8,128)(2,1)} %gather_fusion.1, f32[128,8]{1,0:T(8,128)S(1)} %copy.24), kind=kLoop, calls=%fused_computation.4 | loop fusion | flops 6029312 | bytes 5246976 | tf_op jit(solution)/shard_map/reduce_sum | solution.py:64
  298.8 0.0 copy-done.2
  298.8 0.9 fusion.17
  (11 shorter events, 0.1 us)
Async XLA Ops:
  0.0 158.5 %copy-start = (bf16[1,1,768,2048]{3,2,1,0:T(8,128)(2,1)S(1)}, bf16[1,1,768,2048]{3,2,1,0:T(8,128)(2,1)}, u32[]{:S(2)}) copy-start(bf16[1,1,768,2048]{3,2,1,0:T(8,128)(2,1)} %param.13) | copy-start | bytes 9437188
  0.0 15.3 %collective-permute-start = (bf16[128,2048]{1,0:T(8,128)(2,1)}, bf16[128,2048]{1,0:T(8,128)(2,1)}, u32[]{:S(2)}, u32[]{:S(2)}) collective-permute-start(bf16[128,2048]{1,0:T(8,128)(2,1)} %bitcast.67), channel_id=1, source_target_pairs={{0,16},{1,17},{2,18},{3,19},{4,20},{5,21},{6,22},{7,23},{8,24},{9,... | collective-permute-start | bytes 1572872 | tf_op jit(solution)/shard_map/ppermute | solution.py:12
  16.6 0.8 copy-start.1
  164.3 5.5 %copy-start.3 = (f32[1,128,8]{1,2,0:T(8,128)S(1)}, f32[1,128,8]{1,2,0:T(8,128)}, u32[]{:S(2)}) copy-start(f32[1,128,8]{1,2,0:T(8,128)} %param.11) | copy-start | bytes 12292
  164.3 109.2 %all-to-all-start.1 = ((bf16[16,1,68,2048]{3,2,1,0:T(8,128)(2,1)}), bf16[16,1,68,2048]{3,2,1,0:T(8,128)(2,1)}, u32[]{:S(2)}, u32[]{:S(2)}) async-start(bf16[16,1,68,2048]{3,2,1,0:T(8,128)(2,1)} %convert_bitcast_fusion), calls=%async_computation.1 | async-start | bytes 9437184 | tf_op jit(solution)/shard_map/all_to_all | solution.py:53
  292.2 6.6 %copy-start.2 = (bf16[128,2048]{1,0:T(8,128)(2,1)S(1)}, bf16[128,2048]{1,0:T(8,128)(2,1)}, u32[]{:S(2)}) copy-start(bf16[128,2048]{1,0:T(8,128)(2,1)} %copy-done.1) | copy-start | bytes 1572868
where the time goes:
time: 301 us; the launch traced here: 300 us
  blocking collectives  111 us (37%)
  waiting for transfers between devices  106 us (35%)
  local copies, waits for them, and re-layouts  45 us (15%)
  matrix products  15.5 us (5%)
  other arithmetic  15.1 us (5%)
  starting transfers between devices  7.03 us (2%)
    all_to_all x1, blocking collectives, body(): lax.all_to_all(send_buffer, 'expert', split_axis=0, concat_axis=0, tiled=...  111 us
    all_to_all x1, waiting for transfers between devices, body(): lax.all_to_all(jnp.einsum('secf,efd->secd', hidden, w_down[0], preferred_...  104 us
    gather x1, local copies, waits for them, and re-layouts, body(): padded[source_row // topk_count]  11.7 us
    gather x1, local copies, waits for them, and re-layouts, body(): flat_back[position].reshape(tok_dev, topk_count, width).astype(jnp.float32)  11.7 us
    dot_general x1, matrix products, body(): jnp.einsum('secd,edf->secf', received, w_gate_up[0], preferred_element_ty...  9.76 us
    reshape x1, local copies, waits for them, and re-layouts, body(): flat_back = returned.reshape(experts_total * capacity, width)  7.08 us
    reshape x1, local copies, waits for them, and re-layouts, body(): padded[source_row // topk_count]  7.05 us
    reduce_sum x1, other arithmetic, body(): mixed = jnp.sum(picked * gate_weights[0][:, :, None], axis=1)  6.57 us
  transfers between devices with their start and end apart: 2, of which 2 were waited for; matrix products, arithmetic and copies ran while one was open for 4% of the time, Pallas kernels for 0%

commit v1 on v0

--- a/solution.py
+++ b/solution.py
@@ -1,9 +1,15 @@
+import functools
+
 import jax
 import jax.numpy as jnp
 from jax import lax
+from jax.experimental import pallas as pl
+from jax.experimental.pallas import tpu as pltpu
 from jax.sharding import PartitionSpec as P
 
 epsilon = 1e-06
+LANES = 128
+CORES = 2
 
 
 def from_behind(value, axis, by):
@@ -12,7 +18,7 @@
     return lax.ppermute(value, axis, pairs)
 
 
-def body(fresh, previous, norm_gain, routes, gate_weights, w_gate_up, w_down):
+def routed_body(fresh, previous, norm_gain, routes, gate_weights, w_gate_up, w_down):
     devices_exp = lax.axis_size("expert")
     section_id = lax.axis_index("section")
     tok_dev = fresh.shape[0]
@@ -65,7 +71,195 @@
     return (wide_input + mixed).astype(jnp.bfloat16)[None]
 
 
+def norm_kernel(section_ref, fresh_ref, arrived_ref, gain_ref, routes_ref, gates_ref, rows_ref, *, experts):
+    width = fresh_ref.shape[1]
+    rows = fresh_ref.shape[0]
+    first = section_ref[0] == 0
+    wide = jnp.where(first, fresh_ref[...], arrived_ref[...]).astype(jnp.float32)
+    scale = lax.rsqrt(jnp.mean(wide * wide, axis=-1, keepdims=True) + epsilon)
+    rows_ref[:, :width] = (wide * scale * gain_ref[...]).astype(jnp.bfloat16)
+    lane = lax.broadcasted_iota(jnp.int32, (rows, LANES), 1)
+    expert = lane % experts
+    term = lane // experts
+    weight = jnp.zeros((rows, LANES), jnp.float32)
+    for k in range(routes_ref.shape[1]):
+        weight += jnp.where(routes_ref[:, k : k + 1] == expert, gates_ref[:, k : k + 1], 0.0)
+    high = weight.astype(jnp.bfloat16).astype(jnp.float32)
+    middle = (weight - high).astype(jnp.bfloat16).astype(jnp.float32)
+    low = weight - high - middle
+    terms = jnp.where(term == 0, high, jnp.where(term == 1, middle, jnp.where(term == 2, low, 0.0)))
+    rows_ref[:, width:] = terms.astype(jnp.bfloat16)
+
+
+def norm_rows(section_id, fresh, arrived, gain, routes, gates, experts):
+    rows, width = fresh.shape
+    vmem = pl.BlockSpec(memory_space=pltpu.VMEM)
+    return pl.pallas_call(
+        functools.partial(norm_kernel, experts=experts),
+        out_shape=jax.ShapeDtypeStruct((rows, width + LANES), jnp.bfloat16),
+        in_specs=[pl.BlockSpec(memory_space=pltpu.SMEM)] + [vmem] * 5,
+        out_specs=vmem,
+        compiler_params=pltpu.CompilerParams(vmem_limit_bytes=32 << 20),
+        cost_estimate=pl.CostEstimate(flops=rows * width * 6, bytes_accessed=rows * width * 6, transcendentals=rows),
+        name="norm_rows",
+    )(section_id.reshape(1), fresh, arrived, gain, routes, gates)
+
+
+def mlp_kernel(ids_ref, *refs, parts, tiles, experts):
+    payloads = refs[:parts]
+    weights = refs[parts : parts + 6]
+    out_ref, x_ref, coef_ref = refs[parts + 6 :]
+    step = pl.program_id(0)
+    width = out_ref.shape[1]
+
+    @pl.when(step == 0)
+    def _():
+        start = 0
+        for payload in payloads:
+            count = payload.shape[0]
+            x_ref[start : start + count, :] = payload[:, :width]
+            tail = payload[:, width:].astype(jnp.float32)
+            lane = lax.broadcasted_iota(jnp.int32, tail.shape, 1) % experts
+            for which in range(2):
+                value = jnp.sum(jnp.where(lane == ids_ref[which], tail, 0.0), axis=1, keepdims=True)
+                coef_ref[which, start : start + count, :] = jnp.broadcast_to(value, (count, LANES))
+            start += count
+
+    def expert(which, gate_ref, up_ref, down_ref):
+        gate = jnp.dot(x_ref[...], gate_ref[...], preferred_element_type=jnp.float32)
+        up = jnp.dot(x_ref[...], up_ref[...], preferred_element_type=jnp.float32)
+        hidden = jax.nn.silu(gate) * up * coef_ref[which][:, :1]
+        return jnp.dot(hidden.astype(jnp.bfloat16), down_ref[...], preferred_element_type=jnp.float32)
+
+    @pl.when(step == 0)
+    def _():
+        out_ref[...] = expert(0, *weights[:3])
+
+    @pl.when((step > 0) & (step < tiles))
+    def _():
+        out_ref[...] += expert(0, *weights[:3])
+
+    @pl.when(step >= tiles)
+    def _():
+        out_ref[...] += expert(1, *weights[3:])
+
+
+def expert_rows(ids, payloads, weights, experts):
+    (own_gate_up, own_down), (other_gate_up, other_down) = weights
+    width = own_gate_up.shape[0]
+    hidden = own_down.shape[0]
+    tile = 256
+    tiles = hidden // tile
+    rows = sum(p.shape[0] for p in payloads)
+
+    def first(step):
+        return jnp.minimum(step, tiles - 1)
+
+    def second(step):
+        return jnp.maximum(step - tiles, 0)
+
+    def specs(index):
+        return [
+            pl.BlockSpec((width, tile), lambda i: (0, index(i))),
+            pl.BlockSpec((width, tile), lambda i: (0, tiles + index(i))),
+            pl.BlockSpec((tile, width), lambda i: (index(i), 0)),
+        ]
+
+    return pl.pallas_call(
+        functools.partial(mlp_kernel, parts=len(payloads), tiles=tiles, experts=experts),
+        grid=(2 * tiles,),
+        out_shape=jax.ShapeDtypeStruct((rows, width), jnp.float32),
+        in_specs=[pl.BlockSpec(memory_space=pltpu.SMEM)]
+        + [pl.BlockSpec(p.shape, lambda i: (0, 0)) for p in payloads]
+        + specs(first)
+        + specs(second),
+        out_specs=pl.BlockSpec((rows, width), lambda i: (0, 0)),
+        scratch_shapes=[
+            pltpu.VMEM((rows, width), jnp.bfloat16),
+            pltpu.VMEM((2, rows, LANES), jnp.float32),
+        ],
+        compiler_params=pltpu.CompilerParams(vmem_limit_bytes=40 << 20),
+        cost_estimate=pl.CostEstimate(
+            flops=2 * rows * width * hidden * 6,
+            bytes_accessed=width * hidden * 12 + rows * width * 6,
+            transcendentals=rows * hidden * 2,
+        ),
+        name="expert_rows",
+    )(ids, *payloads, own_gate_up, own_gate_up, own_down, other_gate_up, other_gate_up, other_down)
+
+
+def chip_ring(depth, across):
+    walk = []
+    for z in range(depth):
+        xs = list(range(1, across))
+        walk += [(z, x) for x in (xs if z % 2 == 0 else xs[::-1])]
+    return [z * across + x for z, x in walk + [(z, 0) for z in reversed(range(depth))]]
+
+
+def relay_body(fresh, previous, norm_gain, routes, gate_weights, w_gate_up, w_down, *, across):
+    devices_exp = lax.axis_size("expert")
+    section_id = lax.axis_index("section")
+    expert_id = lax.axis_index("expert")
+    rows = fresh.shape[0]
+    half = rows // 2
+    chips = devices_exp // CORES
+    ring = chip_ring(chips // across, across)
+    links = list(zip(ring, ring[1:] + ring[:1]))
+    up = [(a * CORES + c, b * CORES + c) for a, b in links for c in range(CORES)]
+    down = [(b, a) for a, b in up]
+    swap = [(i, i ^ 1) for i in range(devices_exp)]
+
+    def move(value, pairs):
+        return lax.ppermute(value, "expert", pairs)
+
+    arrived = from_behind(previous[0], "section", 1)
+    own = (w_gate_up[0, 0], w_down[0, 0])
+    other = tuple(move(w, swap) for w in own)
+    ids = jnp.stack([expert_id, expert_id ^ 1]).astype(jnp.int32)
+    packed = norm_rows(section_id, fresh, arrived, norm_gain, routes[0], gate_weights[0], devices_exp)
+
+    def mlp(payloads):
+        return expert_rows(ids, payloads, (own, other), devices_exp)
+
+    hops = chips // 2
+    ups, downs = [packed], [packed]
+    for _ in range(hops - 1):
+        ups.append(move(ups[-1], up))
+        downs.append(move(downs[-1], down))
+    far = [move(ups[-1][:half], up), move(downs[-1][half:], down)]
+
+    sums = [mlp([ups[s], downs[s]]) for s in range(1, hops)]
+    far_sum = mlp(far)
+    own_sum = mlp([packed])
+
+    going_up = move(far_sum[:half].astype(jnp.bfloat16), up)
+    going_down = move(far_sum[half:].astype(jnp.bfloat16), down)
+    for s in reversed(range(1, hops)):
+        to_up = sums[s - 1][rows:]
+        to_down = sums[s - 1][:rows]
+        if s == hops - 1:
+            going_up = jnp.concatenate([to_up[:half] + going_up, to_up[half:]], axis=0)
+            going_down = jnp.concatenate([to_down[:half], to_down[half:] + going_down], axis=0)
+        else:
+            going_up = to_up + going_up
+            going_down = to_down + going_down
+        going_up = move(going_up.astype(jnp.bfloat16), up)
+        going_down = move(going_down.astype(jnp.bfloat16), down)
+
+    arrival = jnp.where(section_id == 0, fresh, arrived).astype(jnp.float32)
+    return (arrival + (own_sum + going_up + going_down)).astype(jnp.bfloat16)[None]
+
+
 def solution(mesh):
+    across = mesh.shape["section"]
+    devices_exp = mesh.shape["expert"]
+
+    def body(*args):
+        topk_count, local_experts = args[3].shape[2], args[5].shape[1]
+        if local_experts == 1 and devices_exp <= 2 * topk_count and devices_exp % (2 * CORES * across) == 0:
+            return relay_body(*args, across=across)
+        return routed_body(*args)
+
     return jax.shard_map(
         body,
         mesh=mesh,

time: 301 us -> 144 us (0.48)
  the two profiles are of different devices: /device:TPU:15 before, /device:TPU:0 now
where the time goes in v1:
time: 144 us; the launch traced here: 143 us
  Pallas kernels  46.7 us (32%)
  waiting for transfers between devices  44.9 us (31%)
  local copies, waits for them, and re-layouts  23.8 us (17%)
  starting transfers between devices  22.6 us (16%)
  other arithmetic  4.5 us (3%)
    pallas_call x5, Pallas kernels, expert_rows(): pl.pallas_call(functools.partial(mlp_kernel, parts=len(payloads), tiles=t...  45.2 us
    ppermute x18, waiting for transfers between devices, move(): return lax.ppermute(value, 'expert', pairs)  35.6 us
    unnamed x52, local copies, waits for them, and re-layouts  22.3 us
    ppermute x18, starting transfers between devices, move(): return lax.ppermute(value, 'expert', pairs)  17 us
    ppermute x1, waiting for transfers between devices, from_behind(): return lax.ppermute(value, axis, pairs)  9.28 us
    ppermute x1, starting transfers between devices, from_behind(): return lax.ppermute(value, axis, pairs)  5.66 us
  transfers between devices with their start and end apart: 19, of which 7 were waited for; matrix products, arithmetic and copies ran while one was open for 2% of the time, Pallas kernels for 27%

profile of v1, /device:TPU:0, one launch (start us, length us, event | category | flops | bytes accessed | tf_op | source)
XLA Modules:
  0.0 142.8 jit_solution(434706441953539811)
XLA Ops:
  0.0 0.5 collective-permute-start.1
  0.5 0.1 collective-permute-start.2
  0.5 5.7 %collective-permute-start = (bf16[128,2048]{1,0:T(8,128)(2,1)}, bf16[128,2048]{1,0:T(8,128)(2,1)}, u32[]{:S(2)}, u32[]{:S(2)}) collective-permute-start(bf16[128,2048]{1,0:T(8,128)(2,1)} %bitcast.29), channel_id=1, source_target_pairs={{0,16},{1,17},{2,18},{3,19},{4,20},{5,21},{6,22},{7,23},{8,24},{9,... | collective-permute-start | bytes 1572872 | tf_op jit(solution)/shard_map/ppermute | solution.py:18
  6.2 0.8 copy.8
  7.0 0.8 copy.9
  7.7 9.3 %collective-permute-done.arrived_ref = bf16[128,2048]{1,0:T(8,128)(2,1)} collective-permute-done((bf16[128,2048]{1,0:T(8,128)(2,1)}, bf16[128,2048]{1,0:T(8,128)(2,1)}, u32[]{:S(2)}, u32[]{:S(2)}) %collective-permute-start) | collective-permute-done | bytes 524320 | tf_op jit(solution)/shard_map/ppermute | solution.py:18
  17.0 1.0 copy-done.10
  18.1 0.7 copy-done.24
  18.8 1.6 %norm_rows.1.refs_0_ = bf16[128,2176]{1,0:T(8,128)(2,1)S(1)} custom-call(s32[1]{0:T(128)} %bitcast.3.section_ref, bf16[128,2048]{1,0:T(8,128)(2,1)S(1)} %copy-done.10, bf16[128,2048]{1,0:T(8,128)(2,1)} %collective-permute-done.arrived_ref, f32[1,2048]{1,0:T(1,128)S(1)} %copy-done.24, s32[128,8]{1,0:T(8,128)S(1)} %bitcast.27, f32[128,8]{1,0:T(8,128)S(1)} %bitcast.28), custom_call_target="tpu_custom_call" | custom-call | flops 1572864 | bytes 1572864 | tf_op jit(solution)/shard_map/norm_rows/pallas_call | solution.py:97
  20.3 1.6 %collective-permute-start.4 = (bf16[128,2176]{1,0:T(8,128)(2,1)S(1)}, bf16[128,2176]{1,0:T(8,128)(2,1)S(1)}, u32[]{:S(2)}, u32[]{:S(2)}) collective-permute-start(bf16[128,2176]{1,0:T(8,128)(2,1)S(1)} %norm_rows.1.refs_0_), channel_id=1, source_target_pairs={{6,2},{7,3},{10,6},{11,7},{14,10},{15,11},{12,14},{13,15},{8,12},{... | collective-permute-start | bytes 1671176 | tf_op jit(solution)/shard_map/ppermute | solution.py:213
  22.0 0.4 collective-permute-start.3
  22.4 0.8 copy-done.8
  23.2 10.8 %collective-permute-done.4.refs_1_ = bf16[128,2176]{1,0:T(8,128)(2,1)S(1)} collective-permute-done((bf16[128,2176]{1,0:T(8,128)(2,1)S(1)}, bf16[128,2176]{1,0:T(8,128)(2,1)S(1)}, u32[]{:S(2)}, u32[]{:S(2)}) %collective-permute-start.4) | collective-permute-done | bytes 557088 | tf_op jit(solution)/shard_map/ppermute | solution.py:213
  34.1 1.6 %collective-permute-start.6 = (bf16[128,2176]{1,0:T(8,128)(2,1)S(1)}, bf16[128,2176]{1,0:T(8,128)(2,1)S(1)}, u32[]{:S(2)}, u32[]{:S(2)}) collective-permute-start(bf16[128,2176]{1,0:T(8,128)(2,1)S(1)} %collective-permute-done.4.refs_1_), channel_id=1, source_target_pairs={{6,2},{7,3},{10,6},{11,7},{14,10},{15,11},{12,14},{13,15},{8,12},{... | collective-permute-start | bytes 1671176 | tf_op jit(solution)/shard_map/ppermute | solution.py:213
  35.7 0.0 collective-permute-done.3.refs_0_
  35.7 0.5 collective-permute-start.5
  36.1 0.8 copy-done.18
  36.9 10.0 %collective-permute-done.6.refs_1_ = bf16[128,2176]{1,0:T(8,128)(2,1)S(1)} collective-permute-done((bf16[128,2176]{1,0:T(8,128)(2,1)S(1)}, bf16[128,2176]{1,0:T(8,128)(2,1)S(1)}, u32[]{:S(2)}, u32[]{:S(2)}) %collective-permute-start.6) | collective-permute-done | bytes 557088 | tf_op jit(solution)/shard_map/ppermute | solution.py:213
  46.9 1.6 %collective-permute-start.8 = (bf16[128,2176]{1,0:T(8,128)(2,1)S(1)}, bf16[128,2176]{1,0:T(8,128)(2,1)S(1)}, u32[]{:S(2)}, u32[]{:S(2)}) collective-permute-start(bf16[128,2176]{1,0:T(8,128)(2,1)S(1)} %collective-permute-done.6.refs_1_), channel_id=1, source_target_pairs={{6,2},{7,3},{10,6},{11,7},{14,10},{15,11},{12,14},{13,15},{8,12},{... | collective-permute-start | bytes 1671176 | tf_op jit(solution)/shard_map/ppermute | solution.py:213
  48.4 0.8 copy-done.20
  49.3 0.0 collective-permute-done.5.refs_0_
  49.3 0.5 collective-permute-start.7
  49.7 0.8 copy-done.22
  50.5 8.2 %collective-permute-done.8.refs_1_ = bf16[128,2176]{1,0:T(8,128)(2,1)S(1)} collective-permute-done((bf16[128,2176]{1,0:T(8,128)(2,1)S(1)}, bf16[128,2176]{1,0:T(8,128)(2,1)S(1)}, u32[]{:S(2)}, u32[]{:S(2)}) %collective-permute-start.8) | collective-permute-done | bytes 557088 | tf_op jit(solution)/shard_map/ppermute | solution.py:213
  58.8 0.8 slice.62
  59.5 0.8 copy-done.12
  60.3 1.6 %collective-permute-start.10 = (bf16[64,2176]{1,0:T(8,128)(2,1)}, bf16[64,2176]{1,0:T(8,128)(2,1)S(1)}, u32[]{:S(2)}, u32[]{:S(2)}) collective-permute-start(bf16[64,2176]{1,0:T(8,128)(2,1)} %slice.62), channel_id=1, source_target_pairs={{6,2},{7,3},{10,6},{11,7},{14,10},{15,11},{12,14},{13,15},{8,12},{... | collective-permute-start | bytes 835592 | tf_op jit(solution)/shard_map/ppermute | solution.py:213
  61.9 0.0 collective-permute-done.7.refs_0_
  61.9 0.7 slice.61
  62.6 0.9 copy-done.14
  63.5 0.4 collective-permute-start.9
  64.0 0.1 pad_add_fusion.ids_ref
  64.0 3.1 %collective-permute-done.10.refs_1_ = bf16[64,2176]{1,0:T(8,128)(2,1)S(1)} collective-permute-done((bf16[64,2176]{1,0:T(8,128)(2,1)}, bf16[64,2176]{1,0:T(8,128)(2,1)S(1)}, u32[]{:S(2)}, u32[]{:S(2)}) %collective-permute-start.10) | collective-permute-done | bytes 278560 | tf_op jit(solution)/shard_map/ppermute | solution.py:213
  67.1 3.3 %collective-permute-done.9.refs_0_ = bf16[64,2176]{1,0:T(8,128)(2,1)} collective-permute-done((bf16[64,2176]{1,0:T(8,128)(2,1)}, bf16[64,2176]{1,0:T(8,128)(2,1)}, u32[]{:S(2)}, u32[]{:S(2)}) %collective-permute-start.9) | collective-permute-done | bytes 278560 | tf_op jit(solution)/shard_map/ppermute | solution.py:213
  70.4 1.7 %copy-done.4 = bf16[768,2048]{1,0:T(8,128)(2,1)} copy-done((bf16[768,2048]{1,0:T(8,128)(2,1)}, bf16[768,2048]{1,0:T(8,128)(2,1)S(1)}, u32[]{:S(2)}) %copy-start.4) | copy-done | bytes 3145752
  72.1 0.0 collective-permute-done.1.refs_4_.refs_5_.refs_6_
  72.1 2.8 %copy-done = bf16[1,1,2048,1536]{3,2,1,0:T(8,128)(2,1)S(1)} copy-done((bf16[1,1,2048,1536]{3,2,1,0:T(8,128)(2,1)S(1)}, bf16[1,1,2048,1536]{3,2,1,0:T(8,128)(2,1)}, u32[]{:S(2)}) %copy-start) | copy-done | bytes 6291480
  74.9 1.9 %copy-done.2 = bf16[1,1,768,2048]{3,2,1,0:T(8,128)(2,1)S(1)} copy-done((bf16[1,1,768,2048]{3,2,1,0:T(8,128)(2,1)S(1)}, bf16[1,1,768,2048]{3,2,1,0:T(8,128)(2,1)}, u32[]{:S(2)}) %copy-start.2) | copy-done | bytes 3145752
  76.8 1.9 %copy-done.5 = bf16[768,2048]{1,0:T(8,128)(2,1)S(1)} copy-done((bf16[768,2048]{1,0:T(8,128)(2,1)S(1)}, bf16[768,2048]{1,0:T(8,128)(2,1)}, u32[]{:S(2)}) %copy-start.5) | copy-done | bytes 3145752
  78.6 7.6 %expert_rows.9 = f32[128,2048]{1,0:T(8,128)S(1)} custom-call(s32[2]{0:T(128)S(1)} %pad_add_fusion.ids_ref, bf16[64,2176]{1,0:T(8,128)(2,1)} %collective-permute-done.9.refs_0_, bf16[64,2176]{1,0:T(8,128)(2,1)S(1)} %collective-permute-done.10.refs_1_, bf16[2048,1536]{1,0:T(8,128)(2,1)S(1)} %bitcast.17, bf16[2048,1536]{1,0:T(8,128)(2,1)S(1)} %bitcast.18, ...), custom_call_target="tpu_custom_call" | custom-call | flops 2415919104 | bytes 20447232 | tf_op jit(solution)/shard_map/expert_rows/pallas_call | solution.py:168
  86.3 0.1 convert.16
  86.4 0.5 collective-permute-start.11
  86.9 1.6 %collective-permute-start.15 = (bf16[64,2048]{1,0:T(8,128)(2,1)S(1)}, bf16[64,2048]{1,0:T(8,128)(2,1)S(1)}, u32[]{:S(2)}, u32[]{:S(2)}) collective-permute-start(bf16[64,2048]{1,0:T(8,128)(2,1)S(1)} %get-tuple-element.14), channel_id=1, source_target_pairs={{6,2},{7,3},{10,6},{11,7},{14,10},{15,11},{12,14},{13,15},{8,12},{... | collective-permute-start | bytes 786440 | tf_op jit(solution)/shard_map/ppermute | solution.py:213
  88.5 10.0 %expert_rows.8 = f32[256,2048]{1,0:T(8,128)S(1)} custom-call(s32[2]{0:T(128)S(1)} %pad_add_fusion.ids_ref, bf16[128,2176]{1,0:T(8,128)(2,1)S(1)} %copy-done.15, bf16[128,2176]{1,0:T(8,128)(2,1)S(1)} %copy-done.13, bf16[2048,1536]{1,0:T(8,128)(2,1)} %bitcast.11, bf16[2048,1536]{1,0:T(8,128)(2,1)} %bitcast.12, bf16[768,2048]{1,0:T(8,128)(2,1)S(1)} %bitcast.23, ...), custom_call_target="tpu_custom_call" | custom-call | flops 4831838208 | bytes 22020096 | tf_op jit(solution)/shard_map/expert_rows/pallas_call | solution.py:168
  98.6 0.1 convert.18
  98.8 0.0 collective-permute-done.11
  98.8 0.0 collective-permute-done.15
  98.8 0.1 fusion.6
  99.0 1.6 %collective-permute-start.16 = (bf16[128,2048]{1,0:T(8,128)(2,1)S(1)}, bf16[128,2048]{1,0:T(8,128)(2,1)S(1)}, u32[]{:S(2)}, u32[]{:S(2)}) collective-permute-start(bf16[128,2048]{1,0:T(8,128)(2,1)S(1)} %pad_maximum_fusion.1), channel_id=1, source_target_pairs={{6,2},{7,3},{10,6},{11,7},{14,10},{15,11},{12,14},{13,15},{8,12},{... | collective-permute-start | bytes 1572872 | tf_op jit(solution)/shard_map/ppermute | solution.py:213
  100.7 0.5 collective-permute-start.12
  101.2 10.0 %expert_rows.7 = f32[256,2048]{1,0:T(8,128)S(1)} custom-call(s32[2]{0:T(128)S(1)} %pad_add_fusion.ids_ref, bf16[128,2176]{1,0:T(8,128)(2,1)S(1)} %copy-done.23, bf16[128,2176]{1,0:T(8,128)(2,1)S(1)} %copy-done.21, bf16[2048,1536]{1,0:T(8,128)(2,1)} %bitcast.13, bf16[2048,1536]{1,0:T(8,128)(2,1)} %bitcast.14, bf16[768,2048]{1,0:T(8,128)(2,1)S(1)} %bitcast.24, ...), custom_call_target="tpu_custom_call" | custom-call | flops 4831838208 | bytes 22020096 | tf_op jit(solution)/shard_map/expert_rows/pallas_call | solution.py:168
  111.2 0.2 collective-permute-done.12
  111.4 0.3 fusion.2
  111.7 0.5 collective-permute-start.13
  112.2 1.6 %collective-permute-start.17 = (bf16[128,2048]{1,0:T(8,128)(2,1)S(1)}, bf16[128,2048]{1,0:T(8,128)(2,1)S(1)}, u32[]{:S(2)}, u32[]{:S(2)}) collective-permute-start(bf16[128,2048]{1,0:T(8,128)(2,1)S(1)} %get-tuple-element.8), channel_id=1, source_target_pairs={{6,2},{7,3},{10,6},{11,7},{14,10},{15,11},{12,14},{13,15},{8,12},{... | collective-permute-start | bytes 1572872 | tf_op jit(solution)/shard_map/ppermute | solution.py:213
  113.8 10.0 %expert_rows.6 = f32[256,2048]{1,0:T(8,128)S(1)} custom-call(s32[2]{0:T(128)S(1)} %pad_add_fusion.ids_ref, bf16[128,2176]{1,0:T(8,128)(2,1)S(1)} %copy-done.19, bf16[128,2176]{1,0:T(8,128)(2,1)S(1)} %copy-done.17, bf16[2048,1536]{1,0:T(8,128)(2,1)} %bitcast.15, bf16[2048,1536]{1,0:T(8,128)(2,1)} %bitcast.16, bf16[768,2048]{1,0:T(8,128)(2,1)S(1)} %bitcast.25, ...), custom_call_target="tpu_custom_call" | custom-call | flops 4831838208 | bytes 22020096 | tf_op jit(solution)/shard_map/expert_rows/pallas_call | solution.py:168
  123.9 1.3 fusion.3
  125.2 0.5 collective-permute-start.14
  125.6 1.6 %collective-permute-start.18 = (bf16[128,2048]{1,0:T(8,128)(2,1)}, bf16[128,2048]{1,0:T(8,128)(2,1)}, u32[]{:S(2)}, u32[]{:S(2)}) collective-permute-start(bf16[128,2048]{1,0:T(8,128)(2,1)} %get-tuple-element.6), channel_id=1, source_target_pairs={{6,2},{7,3},{10,6},{11,7},{14,10},{15,11},{12,14},{13,15},{8,12},{... | collective-permute-start | bytes 1572872 | tf_op jit(solution)/shard_map/ppermute | solution.py:213
  127.2 2.8 %copy-done.1 = bf16[1,1,2048,1536]{3,2,1,0:T(8,128)(2,1)S(1)} copy-done((bf16[1,1,2048,1536]{3,2,1,0:T(8,128)(2,1)S(1)}, bf16[1,1,2048,1536]{3,2,1,0:T(8,128)(2,1)}, u32[]{:S(2)}) %copy-start.1) | copy-done | bytes 6291480
  130.0 1.9 %copy-done.7 = bf16[768,2048]{1,0:T(8,128)(2,1)S(1)} copy-done((bf16[768,2048]{1,0:T(8,128)(2,1)S(1)}, bf16[768,2048]{1,0:T(8,128)(2,1)}, u32[]{:S(2)}) %copy-start.7) | copy-done | bytes 3145752
  131.9 1.1 copy-done.9
  132.9 7.4 %expert_rows.5 = f32[128,2048]{1,0:T(8,128)S(1)} custom-call(s32[2]{0:T(128)S(1)} %pad_add_fusion.ids_ref, bf16[128,2176]{1,0:T(8,128)(2,1)S(1)} %copy-done.9, bf16[2048,1536]{1,0:T(8,128)(2,1)S(1)} %bitcast.19, bf16[2048,1536]{1,0:T(8,128)(2,1)S(1)} %bitcast.20, bf16[768,2048]{1,0:T(8,128)(2,1)S(1)} %bitcast.26, ...), custom_call_target="tpu_custom_call" | custom-call | flops 2415919104 | bytes 20447232 | tf_op jit(solution)/shard_map/expert_rows/pallas_call | solution.py:168
  140.4 2.4 %fusion.4 = bf16[1,128,2048]{2,1,0:T(8,128)(2,1)} fusion(bf16[128,2048]{1,0:T(8,128)(2,1)} %collective-permute-done.18, f32[128,2048]{1,0:T(8,128)S(1)} %expert_rows.5, bf16[128,2048]{1,0:T(8,128)(2,1)} %collective-permute-done.14, bf16[128,2048]{1,0:T(8,128)(2,1)S(1)} %copy-done.11, bf16[128,2048]{1,0:T(8,128)(2,1)} %collective-permute-done.arrived_ref, ...), kind=kLoop, calls=%fused_computation.9 | loop fusion | flops 2097152 | bytes 3670017 | tf_op jit(solution)/shard_map/broadcast_in_dim | solution.py:250
  (45 shorter events, 0.2 us)
Async XLA Ops:
  0.0 72.1 %collective-permute-start.1 = (bf16[2048,1536]{1,0:T(8,128)(2,1)}, bf16[2048,1536]{1,0:T(8,128)(2,1)}, u32[]{:S(2)}, u32[]{:S(2)}) collective-permute-start(bf16[2048,1536]{1,0:T(8,128)(2,1)} %bitcast.10), channel_id=1, source_target_pairs={{0,1},{1,0},{2,3},{3,2},{4,5},{5,4},{6,7},{7,6},{8,9},{9,8},{10,11... | collective-permute-start | bytes 18874376 | tf_op jit(solution)/shard_map/ppermute | solution.py:213
  0.5 69.9 %collective-permute-start.2 = (bf16[768,2048]{1,0:T(8,128)(2,1)}, bf16[768,2048]{1,0:T(8,128)(2,1)S(1)}, u32[]{:S(2)}, u32[]{:S(2)}) collective-permute-start(bf16[768,2048]{1,0:T(8,128)(2,1)} %bitcast.21), channel_id=1, source_target_pairs={{0,1},{1,0},{2,3},{3,2},{4,5},{5,4},{6,7},{7,6},{8,9},{9,8},{10,11... | collective-permute-start | bytes 9437192 | tf_op jit(solution)/shard_map/ppermute | solution.py:213
  0.5 16.5 %collective-permute-start = (bf16[128,2048]{1,0:T(8,128)(2,1)}, bf16[128,2048]{1,0:T(8,128)(2,1)}, u32[]{:S(2)}, u32[]{:S(2)}) collective-permute-start(bf16[128,2048]{1,0:T(8,128)(2,1)} %bitcast.29), channel_id=1, source_target_pairs={{0,16},{1,17},{2,18},{3,19},{4,20},{5,21},{6,22},{7,23},{8,24},{9,... | collective-permute-start | bytes 1572872 | tf_op jit(solution)/shard_map/ppermute | solution.py:18
  17.0 1.0 copy-start.10
  18.1 0.7 copy-start.24
  20.3 13.7 %collective-permute-start.4 = (bf16[128,2176]{1,0:T(8,128)(2,1)S(1)}, bf16[128,2176]{1,0:T(8,128)(2,1)S(1)}, u32[]{:S(2)}, u32[]{:S(2)}) collective-permute-start(bf16[128,2176]{1,0:T(8,128)(2,1)S(1)} %norm_rows.1.refs_0_), channel_id=1, source_target_pairs={{6,2},{7,3},{10,6},{11,7},{14,10},{15,11},{12,14},{13,15},{8,12},{... | collective-permute-start | bytes 1671176 | tf_op jit(solution)/shard_map/ppermute | solution.py:213
  22.0 13.7 %collective-permute-start.3 = (bf16[128,2176]{1,0:T(8,128)(2,1)S(1)}, bf16[128,2176]{1,0:T(8,128)(2,1)S(1)}, u32[]{:S(2)}, u32[]{:S(2)}) collective-permute-start(bf16[128,2176]{1,0:T(8,128)(2,1)S(1)} %norm_rows.1.refs_0_), channel_id=1, source_target_pairs={{2,6},{3,7},{6,10},{7,11},{10,14},{11,15},{14,12},{15,13},{12,8},{... | collective-permute-start | bytes 1671176 | tf_op jit(solution)/shard_map/ppermute | solution.py:213
  22.4 0.8 copy-start.8
  34.1 28.6 %copy-start.16 = (bf16[128,2176]{1,0:T(8,128)(2,1)}, bf16[128,2176]{1,0:T(8,128)(2,1)S(1)}, u32[]{:S(2)}) copy-start(bf16[128,2176]{1,0:T(8,128)(2,1)S(1)} %collective-permute-done.4.refs_1_) | copy-start | bytes 1671172
  34.1 12.8 %collective-permute-start.6 = (bf16[128,2176]{1,0:T(8,128)(2,1)S(1)}, bf16[128,2176]{1,0:T(8,128)(2,1)S(1)}, u32[]{:S(2)}, u32[]{:S(2)}) collective-permute-start(bf16[128,2176]{1,0:T(8,128)(2,1)S(1)} %collective-permute-done.4.refs_1_), channel_id=1, source_target_pairs={{6,2},{7,3},{10,6},{11,7},{14,10},{15,11},{12,14},{13,15},{8,12},{... | collective-permute-start | bytes 1671176 | tf_op jit(solution)/shard_map/ppermute | solution.py:213
  35.7 13.6 %collective-permute-start.5 = (bf16[128,2176]{1,0:T(8,128)(2,1)S(1)}, bf16[128,2176]{1,0:T(8,128)(2,1)S(1)}, u32[]{:S(2)}, u32[]{:S(2)}) collective-permute-start(bf16[128,2176]{1,0:T(8,128)(2,1)S(1)} %collective-permute-done.3.refs_0_), channel_id=1, source_target_pairs={{2,6},{3,7},{6,10},{7,11},{10,14},{11,15},{14,12},{15,13},{12,8},{... | collective-permute-start | bytes 1671176 | tf_op jit(solution)/shard_map/ppermute | solution.py:213
  36.1 0.8 copy-start.18
  46.9 11.9 %collective-permute-start.8 = (bf16[128,2176]{1,0:T(8,128)(2,1)S(1)}, bf16[128,2176]{1,0:T(8,128)(2,1)S(1)}, u32[]{:S(2)}, u32[]{:S(2)}) collective-permute-start(bf16[128,2176]{1,0:T(8,128)(2,1)S(1)} %collective-permute-done.6.refs_1_), channel_id=1, source_target_pairs={{6,2},{7,3},{10,6},{11,7},{14,10},{15,11},{12,14},{13,15},{8,12},{... | collective-permute-start | bytes 1671176 | tf_op jit(solution)/shard_map/ppermute | solution.py:213
  48.4 0.8 copy-start.20
  49.3 12.6 %collective-permute-start.7 = (bf16[128,2176]{1,0:T(8,128)(2,1)S(1)}, bf16[128,2176]{1,0:T(8,128)(2,1)S(1)}, u32[]{:S(2)}, u32[]{:S(2)}) collective-permute-start(bf16[128,2176]{1,0:T(8,128)(2,1)S(1)} %collective-permute-done.5.refs_0_), channel_id=1, source_target_pairs={{2,6},{3,7},{6,10},{7,11},{10,14},{11,15},{14,12},{15,13},{12,8},{... | collective-permute-start | bytes 1671176 | tf_op jit(solution)/shard_map/ppermute | solution.py:213
  49.7 0.8 copy-start.22
  59.5 0.8 copy-start.12
  60.3 6.8 %collective-permute-start.10 = (bf16[64,2176]{1,0:T(8,128)(2,1)}, bf16[64,2176]{1,0:T(8,128)(2,1)S(1)}, u32[]{:S(2)}, u32[]{:S(2)}) collective-permute-start(bf16[64,2176]{1,0:T(8,128)(2,1)} %slice.62), channel_id=1, source_target_pairs={{6,2},{7,3},{10,6},{11,7},{14,10},{15,11},{12,14},{13,15},{8,12},{... | collective-permute-start | bytes 835592 | tf_op jit(solution)/shard_map/ppermute | solution.py:213
  62.6 0.9 copy-start.14
  63.5 6.9 %collective-permute-start.9 = (bf16[64,2176]{1,0:T(8,128)(2,1)}, bf16[64,2176]{1,0:T(8,128)(2,1)}, u32[]{:S(2)}, u32[]{:S(2)}) collective-permute-start(bf16[64,2176]{1,0:T(8,128)(2,1)} %slice.61), channel_id=1, source_target_pairs={{2,6},{3,7},{6,10},{7,11},{10,14},{11,15},{14,12},{15,13},{12,8},{... | collective-permute-start | bytes 835592 | tf_op jit(solution)/shard_map/ppermute | solution.py:213
  70.4 1.7 %copy-start.4 = (bf16[768,2048]{1,0:T(8,128)(2,1)}, bf16[768,2048]{1,0:T(8,128)(2,1)S(1)}, u32[]{:S(2)}) copy-start(bf16[768,2048]{1,0:T(8,128)(2,1)S(1)} %collective-permute-done.2.refs_6_.refs_7_) | copy-start | bytes 9437188
  72.1 2.8 %copy-start = (bf16[1,1,2048,1536]{3,2,1,0:T(8,128)(2,1)S(1)}, bf16[1,1,2048,1536]{3,2,1,0:T(8,128)(2,1)}, u32[]{:S(2)}) copy-start(bf16[1,1,2048,1536]{3,2,1,0:T(8,128)(2,1)} %param.12) | copy-start | bytes 18874372
  74.9 1.9 %copy-start.2 = (bf16[1,1,768,2048]{3,2,1,0:T(8,128)(2,1)S(1)}, bf16[1,1,768,2048]{3,2,1,0:T(8,128)(2,1)}, u32[]{:S(2)}) copy-start(bf16[1,1,768,2048]{3,2,1,0:T(8,128)(2,1)} %param.13) | copy-start | bytes 9437188
  76.7 1.9 %copy-start.5 = (bf16[768,2048]{1,0:T(8,128)(2,1)S(1)}, bf16[768,2048]{1,0:T(8,128)(2,1)}, u32[]{:S(2)}) copy-start(bf16[768,2048]{1,0:T(8,128)(2,1)} %copy-done.4) | copy-start | bytes 9437188
  78.6 9.9 %copy-start.3 = (bf16[1,1,768,2048]{3,2,1,0:T(8,128)(2,1)S(1)}, bf16[1,1,768,2048]{3,2,1,0:T(8,128)(2,1)}, u32[]{:S(2)}) copy-start(bf16[1,1,768,2048]{3,2,1,0:T(8,128)(2,1)} %param.13) | copy-start | bytes 9437188
  78.6 9.9 %copy-start.6 = (bf16[768,2048]{1,0:T(8,128)(2,1)S(1)}, bf16[768,2048]{1,0:T(8,128)(2,1)}, u32[]{:S(2)}) copy-start(bf16[768,2048]{1,0:T(8,128)(2,1)} %copy-done.4) | copy-start | bytes 9437188
  86.3 2.2 %copy-start.13 = (bf16[128,2176]{1,0:T(8,128)(2,1)S(1)}, bf16[128,2176]{1,0:T(8,128)(2,1)}, u32[]{:S(2)}) copy-start(bf16[128,2176]{1,0:T(8,128)(2,1)} %copy-done.12) | copy-start | bytes 1671172
  86.3 2.2 %copy-start.15 = (bf16[128,2176]{1,0:T(8,128)(2,1)S(1)}, bf16[128,2176]{1,0:T(8,128)(2,1)}, u32[]{:S(2)}) copy-start(bf16[128,2176]{1,0:T(8,128)(2,1)} %copy-done.14) | copy-start | bytes 1671172
  86.4 12.4 %collective-permute-start.11 = (bf16[64,2048]{1,0:T(8,128)(2,1)S(1)}, bf16[64,2048]{1,0:T(8,128)(2,1)S(1)}, u32[]{:S(2)}, u32[]{:S(2)}) collective-permute-start(bf16[64,2048]{1,0:T(8,128)(2,1)S(1)} %get-tuple-element.13), channel_id=1, source_target_pairs={{2,6},{3,7},{6,10},{7,11},{10,14},{11,15},{14,12},{15,13},{12,8},{... | collective-permute-start | bytes 786440 | tf_op jit(solution)/shard_map/ppermute | solution.py:213
  86.9 11.9 %collective-permute-start.15 = (bf16[64,2048]{1,0:T(8,128)(2,1)S(1)}, bf16[64,2048]{1,0:T(8,128)(2,1)S(1)}, u32[]{:S(2)}, u32[]{:S(2)}) collective-permute-start(bf16[64,2048]{1,0:T(8,128)(2,1)S(1)} %get-tuple-element.14), channel_id=1, source_target_pairs={{6,2},{7,3},{10,6},{11,7},{14,10},{15,11},{12,14},{13,15},{8,12},{... | collective-permute-start | bytes 786440 | tf_op jit(solution)/shard_map/ppermute | solution.py:213
  98.8 2.4 %copy-start.21 = (bf16[128,2176]{1,0:T(8,128)(2,1)S(1)}, bf16[128,2176]{1,0:T(8,128)(2,1)}, u32[]{:S(2)}) copy-start(bf16[128,2176]{1,0:T(8,128)(2,1)} %copy-done.20) | copy-start | bytes 1671172
  98.8 2.4 %copy-start.23 = (bf16[128,2176]{1,0:T(8,128)(2,1)S(1)}, bf16[128,2176]{1,0:T(8,128)(2,1)}, u32[]{:S(2)}) copy-start(bf16[128,2176]{1,0:T(8,128)(2,1)} %copy-done.22) | copy-start | bytes 1671172
  99.0 12.2 %collective-permute-start.16 = (bf16[128,2048]{1,0:T(8,128)(2,1)S(1)}, bf16[128,2048]{1,0:T(8,128)(2,1)S(1)}, u32[]{:S(2)}, u32[]{:S(2)}) collective-permute-start(bf16[128,2048]{1,0:T(8,128)(2,1)S(1)} %pad_maximum_fusion.1), channel_id=1, source_target_pairs={{6,2},{7,3},{10,6},{11,7},{14,10},{15,11},{12,14},{13,15},{8,12},{... | collective-permute-start | bytes 1572872 | tf_op jit(solution)/shard_map/ppermute | solution.py:213
  100.7 10.8 %collective-permute-start.12 = (bf16[128,2048]{1,0:T(8,128)(2,1)S(1)}, bf16[128,2048]{1,0:T(8,128)(2,1)S(1)}, u32[]{:S(2)}, u32[]{:S(2)}) collective-permute-start(bf16[128,2048]{1,0:T(8,128)(2,1)S(1)} %pad_maximum_fusion), channel_id=1, source_target_pairs={{2,6},{3,7},{6,10},{7,11},{10,14},{11,15},{14,12},{15,13},{12,8},{... | collective-permute-start | bytes 1572872 | tf_op jit(solution)/shard_map/ppermute | solution.py:213
  111.2 2.6 %copy-start.17 = (bf16[128,2176]{1,0:T(8,128)(2,1)S(1)}, bf16[128,2176]{1,0:T(8,128)(2,1)}, u32[]{:S(2)}) copy-start(bf16[128,2176]{1,0:T(8,128)(2,1)} %copy-done.16) | copy-start | bytes 1671172
  111.2 2.6 %copy-start.19 = (bf16[128,2176]{1,0:T(8,128)(2,1)S(1)}, bf16[128,2176]{1,0:T(8,128)(2,1)}, u32[]{:S(2)}) copy-start(bf16[128,2176]{1,0:T(8,128)(2,1)} %copy-done.18) | copy-start | bytes 1671172
  111.7 12.1 %collective-permute-start.13 = (bf16[128,2048]{1,0:T(8,128)(2,1)S(1)}, bf16[128,2048]{1,0:T(8,128)(2,1)S(1)}, u32[]{:S(2)}, u32[]{:S(2)}) collective-permute-start(bf16[128,2048]{1,0:T(8,128)(2,1)S(1)} %get-tuple-element.7), channel_id=1, source_target_pairs={{2,6},{3,7},{6,10},{7,11},{10,14},{11,15},{14,12},{15,13},{12,8},{... | collective-permute-start | bytes 1572872 | tf_op jit(solution)/shard_map/ppermute | solution.py:213
  112.2 11.6 %collective-permute-start.17 = (bf16[128,2048]{1,0:T(8,128)(2,1)S(1)}, bf16[128,2048]{1,0:T(8,128)(2,1)S(1)}, u32[]{:S(2)}, u32[]{:S(2)}) collective-permute-start(bf16[128,2048]{1,0:T(8,128)(2,1)S(1)} %get-tuple-element.8), channel_id=1, source_target_pairs={{6,2},{7,3},{10,6},{11,7},{14,10},{15,11},{12,14},{13,15},{8,12},{... | collective-permute-start | bytes 1572872 | tf_op jit(solution)/shard_map/ppermute | solution.py:213
  125.2 15.2 %collective-permute-start.14 = (bf16[128,2048]{1,0:T(8,128)(2,1)}, bf16[128,2048]{1,0:T(8,128)(2,1)}, u32[]{:S(2)}, u32[]{:S(2)}) collective-permute-start(bf16[128,2048]{1,0:T(8,128)(2,1)} %get-tuple-element.5), channel_id=1, source_target_pairs={{2,6},{3,7},{6,10},{7,11},{10,14},{11,15},{14,12},{15,13},{12,8},{... | collective-permute-start | bytes 1572872 | tf_op jit(solution)/shard_map/ppermute | solution.py:213
  125.6 14.8 %collective-permute-start.18 = (bf16[128,2048]{1,0:T(8,128)(2,1)}, bf16[128,2048]{1,0:T(8,128)(2,1)}, u32[]{:S(2)}, u32[]{:S(2)}) collective-permute-start(bf16[128,2048]{1,0:T(8,128)(2,1)} %get-tuple-element.6), channel_id=1, source_target_pairs={{6,2},{7,3},{10,6},{11,7},{14,10},{15,11},{12,14},{13,15},{8,12},{... | collective-permute-start | bytes 1572872 | tf_op jit(solution)/shard_map/ppermute | solution.py:213
  127.2 2.8 %copy-start.1 = (bf16[1,1,2048,1536]{3,2,1,0:T(8,128)(2,1)S(1)}, bf16[1,1,2048,1536]{3,2,1,0:T(8,128)(2,1)}, u32[]{:S(2)}) copy-start(bf16[1,1,2048,1536]{3,2,1,0:T(8,128)(2,1)} %param.12) | copy-start | bytes 18874372
  130.0 1.9 %copy-start.7 = (bf16[768,2048]{1,0:T(8,128)(2,1)S(1)}, bf16[768,2048]{1,0:T(8,128)(2,1)}, u32[]{:S(2)}) copy-start(bf16[768,2048]{1,0:T(8,128)(2,1)} %copy-done.4) | copy-start | bytes 9437188
  131.9 1.1 copy-start.9
  132.9 7.5 %copy-start.11 = (bf16[128,2048]{1,0:T(8,128)(2,1)S(1)}, bf16[128,2048]{1,0:T(8,128)(2,1)}, u32[]{:S(2)}) copy-start(bf16[128,2048]{1,0:T(8,128)(2,1)} %fresh_ref.1) | copy-start | bytes 1572868

commit v2 on v0

--- a/solution.py
+++ b/solution.py
@@ -1,9 +1,15 @@
+import functools
+
 import jax
 import jax.numpy as jnp
 from jax import lax
+from jax.experimental import pallas as pl
+from jax.experimental.pallas import tpu as pltpu
 from jax.sharding import PartitionSpec as P
 
 epsilon = 1e-06
+LANES = 128
+CORES = 2
 
 
 def from_behind(value, axis, by):
@@ -12,7 +18,7 @@
     return lax.ppermute(value, axis, pairs)
 
 
-def body(fresh, previous, norm_gain, routes, gate_weights, w_gate_up, w_down):
+def routed_body(fresh, previous, norm_gain, routes, gate_weights, w_gate_up, w_down):
     devices_exp = lax.axis_size("expert")
     section_id = lax.axis_index("section")
     tok_dev = fresh.shape[0]
@@ -65,7 +71,234 @@
     return (wide_input + mixed).astype(jnp.bfloat16)[None]
 
 
+def base_kernel(fresh_ref, gain_ref, routes_ref, gates_ref, rows_ref, gain_out_ref, *, experts):
+    width = fresh_ref.shape[1]
+    rows = fresh_ref.shape[0]
+    rows_ref[:, :width] = normed_rows(fresh_ref[...], gain_ref[...])
+    lane = lax.broadcasted_iota(jnp.int32, (rows, LANES), 1)
+    expert = lane % experts
+    term = lane // experts
+    weight = jnp.zeros((rows, LANES), jnp.float32)
+    for k in range(routes_ref.shape[1]):
+        weight += jnp.where(routes_ref[:, k : k + 1] == expert, gates_ref[:, k : k + 1], 0.0)
+    high = weight.astype(jnp.bfloat16).astype(jnp.float32)
+    middle = (weight - high).astype(jnp.bfloat16).astype(jnp.float32)
+    low = weight - high - middle
+    terms = jnp.where(term == 0, high, jnp.where(term == 1, middle, jnp.where(term == 2, low, 0.0)))
+    rows_ref[:, width:] = terms.astype(jnp.bfloat16)
+    gain_out_ref[...] = gain_ref[...]
+
+
+def normed_rows(rows, gain):
+    wide = rows.astype(jnp.float32)
+    scale = lax.rsqrt(jnp.mean(wide * wide, axis=-1, keepdims=True) + epsilon)
+    return (wide * scale * gain).astype(jnp.bfloat16)
+
+
+def base_rows(fresh, gain, routes, gates, experts):
+    rows, width = fresh.shape
+    vmem = pl.BlockSpec(memory_space=pltpu.VMEM)
+    return pl.pallas_call(
+        functools.partial(base_kernel, experts=experts),
+        out_shape=(
+            jax.ShapeDtypeStruct((rows, width + LANES), jnp.bfloat16),
+            jax.ShapeDtypeStruct(gain.shape, jnp.float32),
+        ),
+        in_specs=[vmem] * 4,
+        out_specs=(vmem, vmem),
+        compiler_params=pltpu.CompilerParams(vmem_limit_bytes=12 << 20),
+        cost_estimate=pl.CostEstimate(flops=rows * width * 6, bytes_accessed=rows * width * 4, transcendentals=rows),
+        name="base_rows",
+    )(fresh, gain, routes, gates)
+
+
+def norm_kernel(section_ref, base_ref, arrived_ref, gain_ref, rows_ref, *, start):
+    rows, width = arrived_ref.shape
+    here = slice(start, start + rows)
+
+    @pl.when(section_ref[0] == 0)
+    def _():
+        rows_ref[:, :width] = base_ref[here, :width]
+
+    @pl.when(section_ref[0] != 0)
+    def _():
+        rows_ref[:, :width] = normed_rows(arrived_ref[...], gain_ref[...])
+
+    rows_ref[:, width:] = base_ref[here, width:]
+
+
+def norm_rows(section_id, base, arrived, gain, start):
+    rows, width = arrived.shape
+    vmem = pl.BlockSpec(memory_space=pltpu.VMEM)
+    return pl.pallas_call(
+        functools.partial(norm_kernel, start=start),
+        out_shape=jax.ShapeDtypeStruct((rows, base.shape[1]), jnp.bfloat16),
+        in_specs=[pl.BlockSpec(memory_space=pltpu.SMEM)] + [vmem] * 3,
+        out_specs=vmem,
+        compiler_params=pltpu.CompilerParams(vmem_limit_bytes=12 << 20),
+        cost_estimate=pl.CostEstimate(flops=rows * width * 6, bytes_accessed=rows * width * 6, transcendentals=rows),
+        name="norm_rows",
+    )(section_id.reshape(1), base, arrived, gain)
+
+
+def mlp_kernel(ids_ref, *refs, parts, chained, experts):
+    payloads = refs[:parts]
+    weights = (refs[parts : parts + 2], refs[parts + 2 : parts + 4])
+    refs = refs[parts + 4 + chained :]
+    outs = refs[:parts]
+    x_ref, coef_ref, hidden_ref = refs[parts:]
+    width = x_ref.shape[1]
+    hidden = weights[0][1].shape[0]
+    bounds = []
+    start = 0
+    for payload in payloads:
+        here = slice(start, start + payload.shape[0])
+        bounds.append(here)
+        start += payload.shape[0]
+        x_ref[here, :] = payload[:, :width]
+        tail = payload[:, width:].astype(jnp.float32)
+        lane = lax.broadcasted_iota(jnp.int32, tail.shape, 1) % experts
+        for which in range(2):
+            value = jnp.sum(jnp.where(lane == ids_ref[which], tail, 0.0), axis=1, keepdims=True)
+            coef_ref[which, here, :] = jnp.broadcast_to(value, tail.shape)
+    tile = 256
+    for which, (gate_up, _) in enumerate(weights):
+        for t in range(0, hidden, tile):
+            gate = jnp.dot(x_ref[...], gate_up[:, t : t + tile], preferred_element_type=jnp.float32)
+            up = jnp.dot(x_ref[...], gate_up[:, hidden + t : hidden + t + tile], preferred_element_type=jnp.float32)
+            value = jax.nn.silu(gate) * up * coef_ref[which][:, :1]
+            hidden_ref[:, which * hidden + t : which * hidden + t + tile] = value.astype(jnp.bfloat16)
+    tile = 512
+    for t in range(0, width, tile):
+        total = jnp.zeros((x_ref.shape[0], tile), jnp.float32)
+        for which, (_, down) in enumerate(weights):
+            rows = hidden_ref[:, which * hidden : (which + 1) * hidden]
+            total += jnp.dot(rows, down[:, t : t + tile], preferred_element_type=jnp.float32)
+        for here, out in zip(bounds, outs):
+            out[:, t : t + tile] = total[here, :]
+
+
+def expert_rows(ids, payloads, weights, after, experts):
+    (own_gate_up, own_down), (other_gate_up, other_down) = weights
+    width = own_gate_up.shape[0]
+    hidden = own_down.shape[0]
+    rows = sum(p.shape[0] for p in payloads)
+    vmem = pl.BlockSpec(memory_space=pltpu.VMEM)
+    chain = [] if after is None else [after]
+    return pl.pallas_call(
+        functools.partial(mlp_kernel, parts=len(payloads), chained=len(chain), experts=experts),
+        out_shape=[jax.ShapeDtypeStruct((p.shape[0], width), jnp.float32) for p in payloads],
+        in_specs=[pl.BlockSpec(memory_space=pltpu.SMEM)]
+        + [vmem] * (len(payloads) + 4)
+        + [pl.BlockSpec(memory_space=pl.ANY)] * len(chain),
+        out_specs=[vmem] * len(payloads),
+        scratch_shapes=[
+            pltpu.VMEM((rows, width), jnp.bfloat16),
+            pltpu.VMEM((2, rows, LANES), jnp.float32),
+            pltpu.VMEM((rows, 2 * hidden), jnp.bfloat16),
+        ],
+        compiler_params=pltpu.CompilerParams(vmem_limit_bytes=12 << 20),
+        cost_estimate=pl.CostEstimate(
+            flops=2 * rows * width * hidden * 6,
+            bytes_accessed=rows * width * 6,
+            transcendentals=rows * hidden * 2,
+        ),
+        name="expert_rows",
+    )(ids, *payloads, own_gate_up, own_down, other_gate_up, other_down, *chain)
+
+
+def chip_ring(depth, across):
+    walk = []
+    for z in range(depth):
+        xs = list(range(1, across))
+        walk += [(z, x) for x in (xs if z % 2 == 0 else xs[::-1])]
+    return [z * across + x for z, x in walk + [(z, 0) for z in reversed(range(depth))]]
+
+
+def relay_body(fresh, previous, norm_gain, routes, gate_weights, w_gate_up, w_down, *, across):
+    devices_exp = lax.axis_size("expert")
+    section_id = lax.axis_index("section")
+    expert_id = lax.axis_index("expert")
+    rows = fresh.shape[0]
+    half = rows // 2
+    chips = devices_exp // CORES
+    ring = chip_ring(chips // across, across)
+    links = list(zip(ring, ring[1:] + ring[:1]))
+    up = [(a * CORES + c, b * CORES + c) for a, b in links for c in range(CORES)]
+    down = [(b, a) for a, b in up]
+    swap = [(i, i ^ 1) for i in range(devices_exp)]
+
+    def move(value, pairs):
+        return lax.ppermute(value, "expert", pairs)
+
+    cuts = [slice(0, half), slice(half, rows)]
+    arrived = [from_behind(previous[0, cut], "section", 1) for cut in cuts]
+    own = (w_gate_up[0, 0], w_down[0, 0])
+    other = tuple(move(w, swap) for w in own)
+    ids = jnp.stack([expert_id, expert_id ^ 1]).astype(jnp.int32)
+    base, gain = base_rows(fresh, norm_gain, routes[0], gate_weights[0], devices_exp)
+    packed = [norm_rows(section_id, base, arrived[c], gain, cuts[c].start) for c in range(2)]
+
+    last = None
+
+    def mlp(payloads):
+        nonlocal last
+        sums = expert_rows(ids, payloads, (own, other), last, devices_exp)
+        last = sums[0]
+        return sums
+
+    hops = chips // 2
+    ups = [packed] + [[None, None] for _ in range(hops)]
+    downs = [packed] + [[None, None] for _ in range(hops)]
+    to_down, to_up, own_sums = {}, {}, None
+    for s in range(hops):
+        for c in range(2):
+            rising, falling = lax.optimization_barrier((ups[s][c], downs[s][c], last))[:2]
+            if s < hops - 1 or c == 0:
+                ups[s + 1][c] = move(rising, up)
+            if s < hops - 1 or c == 1:
+                downs[s + 1][c] = move(falling, down)
+            if s > 0:
+                to_down[s, c], to_up[s, c] = mlp([ups[s][c], downs[s][c]])
+            elif c == 1:
+                own_sums = mlp(packed)
+    to_up[hops, 0], to_down[hops, 1] = mlp([ups[hops][0], downs[hops][1]])
+
+    flows = [(to_down, 0, down), (to_up, 1, up), (to_up, 0, up), (to_down, 1, down)]
+    totals = [None] * len(flows)
+    for s in reversed(range(1, hops + 1)):
+        for i, (terms, c, pairs) in enumerate(flows):
+            place = s if (hops, c) in terms else s - 1
+            if place == 0:
+                continue
+            if totals[i] is None:
+                total = terms[place, c]
+            else:
+                carried = lax.optimization_barrier((totals[i], last))[0]
+                total = terms[place, c] + carried.astype(jnp.float32)
+            totals[i] = move(total.astype(jnp.bfloat16), pairs)
+
+    outs = []
+    for c in range(2):
+        arrival = jnp.where(section_id == 0, fresh[cuts[c]], arrived[c]).astype(jnp.float32)
+        mixed = own_sums[c]
+        for total, flow in zip(totals, flows):
+            if flow[1] == c:
+                mixed += total.astype(jnp.float32)
+        outs.append((arrival + mixed).astype(jnp.bfloat16))
+    return jnp.concatenate(outs, axis=0)[None]
+
+
 def solution(mesh):
+    across = mesh.shape["section"]
+    devices_exp = mesh.shape["expert"]
+
+    def body(*args):
+        topk_count, local_experts = args[3].shape[2], args[5].shape[1]
+        if local_experts == 1 and devices_exp <= 2 * topk_count and devices_exp % (2 * CORES * across) == 0:
+            return relay_body(*args, across=across)
+        return routed_body(*args)
+
     return jax.shard_map(
         body,
         mesh=mesh,

time: 301 us -> 128 us (0.43)
  the two profiles are of different devices: /device:TPU:15 before, /device:TPU:0 now
where the time goes in v2:
time: 128 us; the launch traced here: 126 us
  Pallas kernels  46.5 us (36%)
  starting transfers between devices  38.2 us (30%)
  waiting for transfers between devices  28.1 us (22%)
  local copies, waits for them, and re-layouts  9.88 us (8%)
  other arithmetic  2.92 us (2%)
    pallas_call x8, Pallas kernels, expert_rows(): pl.pallas_call(functools.partial(mlp_kernel, parts=len(payloads), chained...  45 us
    ppermute x30, starting transfers between devices, move(): return lax.ppermute(value, 'expert', pairs)  31.3 us
    ppermute x30, waiting for transfers between devices, move(): return lax.ppermute(value, 'expert', pairs)  24.5 us
    unnamed x24, local copies, waits for them, and re-layouts  8.01 us
    ppermute x2, starting transfers between devices, from_behind(): return lax.ppermute(value, axis, pairs)  6.86 us
    ppermute x2, waiting for transfers between devices, from_behind(): return lax.ppermute(value, axis, pairs)  3.64 us
  transfers between devices with their start and end apart: 32, of which 11 were waited for; matrix products, arithmetic and copies ran while one was open for 3% of the time, Pallas kernels for 37%

profile of v2, /device:TPU:0, one launch (start us, length us, event | category | flops | bytes accessed | tf_op | source)
XLA Modules:
  0.0 126.0 jit_solution(66343111335412336)
XLA Ops:
  0.0 0.5 collective-permute-start.2
  0.5 0.1 collective-permute-start.3
  0.5 1.9 %slice_bitcast_fusion.1 = (bf16[64,2048]{1,0:T(8,128)(2,1)}, bf16[64,2048]{1,0:T(8,128)(2,1)}) fusion(bf16[1,128,2048]{2,1,0:T(8,128)(2,1)} %param.8), kind=kLoop, calls=%fused_computation.14 | loop fusion | bytes 1048576 | tf_op jit(solution)/shard_map/squeeze | solution.py:235
  2.4 4.9 %collective-permute-start = (bf16[64,2048]{1,0:T(8,128)(2,1)}, bf16[64,2048]{1,0:T(8,128)(2,1)S(1)}, u32[]{:S(2)}, u32[]{:S(2)}) collective-permute-start(bf16[64,2048]{1,0:T(8,128)(2,1)} %get-tuple-element.91), channel_id=1, source_target_pairs={{0,16},{1,17},{2,18},{3,19},{4,20},{5,21},{6,22},{7,23},{8,24},{9,... | collective-permute-start | bytes 786440 | tf_op jit(solution)/shard_map/ppermute | solution.py:18
  7.3 2.0 %collective-permute-start.1 = (bf16[64,2048]{1,0:T(8,128)(2,1)}, bf16[64,2048]{1,0:T(8,128)(2,1)}, u32[]{:S(2)}, u32[]{:S(2)}) collective-permute-start(bf16[64,2048]{1,0:T(8,128)(2,1)} %get-tuple-element.92), channel_id=1, source_target_pairs={{0,16},{1,17},{2,18},{3,19},{4,20},{5,21},{6,22},{7,23},{8,24},{9,... | collective-permute-start | bytes 786440 | tf_op jit(solution)/shard_map/ppermute | solution.py:18
  9.3 0.8 copy.8
  10.0 0.8 copy.9
  10.8 1.0 copy-done.6
  11.9 0.7 copy-done.10
  12.6 0.5 base_rows.1
  13.1 1.2 collective-permute-done.arrived_ref
  14.3 1.5 %collective-permute-start.4 = (bf16[64,2176]{1,0:T(8,128)(2,1)S(1)}, bf16[64,2176]{1,0:T(8,128)(2,1)S(1)}, u32[]{:S(2)}, u32[]{:S(2)}) collective-permute-start(bf16[64,2176]{1,0:T(8,128)(2,1)S(1)} %norm_rows.2.refs_0_), channel_id=1, source_target_pairs={{2,6},{3,7},{6,10},{7,11},{10,14},{11,15},{14,12},{15,13},{12,8},{... | collective-permute-start | bytes 835592 | tf_op jit(solution)/shard_map/ppermute | solution.py:232
  15.8 0.5 collective-permute-start.5
  16.3 0.1 pad_add_fusion.ids_ref
  16.4 2.5 %collective-permute-done.1.arrived_ref = bf16[64,2048]{1,0:T(8,128)(2,1)} collective-permute-done((bf16[64,2048]{1,0:T(8,128)(2,1)}, bf16[64,2048]{1,0:T(8,128)(2,1)}, u32[]{:S(2)}, u32[]{:S(2)}) %collective-permute-start.1) | collective-permute-done | bytes 262176 | tf_op jit(solution)/shard_map/ppermute | solution.py:18
  18.9 1.0 norm_rows.3.refs_1_
  19.9 1.5 %collective-permute-start.8 = (bf16[64,2176]{1,0:T(8,128)(2,1)S(1)}, bf16[64,2176]{1,0:T(8,128)(2,1)S(1)}, u32[]{:S(2)}, u32[]{:S(2)}) collective-permute-start(bf16[64,2176]{1,0:T(8,128)(2,1)S(1)} %norm_rows.3.refs_1_), channel_id=1, source_target_pairs={{2,6},{3,7},{6,10},{7,11},{10,14},{11,15},{14,12},{15,13},{12,8},{... | collective-permute-start | bytes 835592 | tf_op jit(solution)/shard_map/ppermute | solution.py:232
  21.4 0.5 collective-permute-start.9
  22.0 2.8 %copy-done = bf16[1,1,2048,1536]{3,2,1,0:T(8,128)(2,1)S(1)} copy-done((bf16[1,1,2048,1536]{3,2,1,0:T(8,128)(2,1)S(1)}, bf16[1,1,2048,1536]{3,2,1,0:T(8,128)(2,1)}, u32[]{:S(2)}) %copy-start) | copy-done | bytes 6291480
  24.8 1.9 %copy-done.2 = bf16[1,1,768,2048]{3,2,1,0:T(8,128)(2,1)S(1)} copy-done((bf16[1,1,768,2048]{3,2,1,0:T(8,128)(2,1)S(1)}, bf16[1,1,768,2048]{3,2,1,0:T(8,128)(2,1)}, u32[]{:S(2)}) %copy-start.2) | copy-done | bytes 3145752
  26.6 5.7 %expert_rows.8 = (f32[64,2048]{1,0:T(8,128)S(1)}, f32[64,2048]{1,0:T(8,128)S(1)}) custom-call(s32[2]{0:T(128)S(1)} %pad_add_fusion.ids_ref, bf16[64,2176]{1,0:T(8,128)(2,1)S(1)} %norm_rows.2.refs_0_, bf16[64,2176]{1,0:T(8,128)(2,1)S(1)} %norm_rows.3.refs_1_, bf16[2048,1536]{1,0:T(8,128)(2,1)S(1)} %bitcast.14, bf16[768,2048]{1,0:T(8,128)(2,1)S(1)} %bitcast.23, ...), custom_call_target="tpu_custom_call" | custom-call | flops 2415919104 | bytes 1572864 | tf_op jit(solution)/shard_map/expert_rows/pallas_call | solution.py:188
  32.4 1.5 %collective-permute-start.6 = (bf16[64,2176]{1,0:T(8,128)(2,1)S(1)}, bf16[64,2176]{1,0:T(8,128)(2,1)S(1)}, u32[]{:S(2)}, u32[]{:S(2)}) collective-permute-start(bf16[64,2176]{1,0:T(8,128)(2,1)S(1)} %collective-permute-done.4.refs_0_), channel_id=1, source_target_pairs={{2,6},{3,7},{6,10},{7,11},{10,14},{11,15},{14,12},{15,13},{12,8},{... | collective-permute-start | bytes 835592 | tf_op jit(solution)/shard_map/ppermute | solution.py:232
  34.0 0.5 collective-permute-start.7
  34.5 5.6 %expert_rows.9 = (f32[64,2048]{1,0:T(8,128)S(1)}, f32[64,2048]{1,0:T(8,128)S(1)}) custom-call(s32[2]{0:T(128)S(1)} %pad_add_fusion.ids_ref, bf16[64,2176]{1,0:T(8,128)(2,1)S(1)} %collective-permute-done.4.refs_0_, bf16[64,2176]{1,0:T(8,128)(2,1)S(1)} %collective-permute-done.5.refs_1_, bf16[2048,1536]{1,0:T(8,128)(2,1)S(1)} %bitcast.15, ...), custom_call_target="tpu_custom_call" | custom-call | flops 2415919104 | bytes 1572864 | tf_op jit(solution)/shard_map/expert_rows/pallas_call | solution.py:188
  40.2 1.5 %collective-permute-start.12 = (bf16[64,2176]{1,0:T(8,128)(2,1)S(1)}, bf16[64,2176]{1,0:T(8,128)(2,1)S(1)}, u32[]{:S(2)}, u32[]{:S(2)}) collective-permute-start(bf16[64,2176]{1,0:T(8,128)(2,1)S(1)} %collective-permute-done.8.refs_0_), channel_id=1, source_target_pairs={{2,6},{3,7},{6,10},{7,11},{10,14},{11,15},{14,12},{15,13},{12,8},{... | collective-permute-start | bytes 835592 | tf_op jit(solution)/shard_map/ppermute | solution.py:232
  41.7 0.5 collective-permute-start.13
  42.3 5.6 %expert_rows.10 = (f32[64,2048]{1,0:T(8,128)S(1)}, f32[64,2048]{1,0:T(8,128)S(1)}) custom-call(s32[2]{0:T(128)S(1)} %pad_add_fusion.ids_ref, bf16[64,2176]{1,0:T(8,128)(2,1)S(1)} %collective-permute-done.8.refs_0_, bf16[64,2176]{1,0:T(8,128)(2,1)S(1)} %collective-permute-done.9.refs_1_, bf16[2048,1536]{1,0:T(8,128)(2,1)S(1)} %bitcast.16, ...), custom_call_target="tpu_custom_call" | custom-call | flops 2415919104 | bytes 1572864 | tf_op jit(solution)/shard_map/expert_rows/pallas_call | solution.py:188
  47.9 1.5 %collective-permute-start.10 = (bf16[64,2176]{1,0:T(8,128)(2,1)S(1)}, bf16[64,2176]{1,0:T(8,128)(2,1)S(1)}, u32[]{:S(2)}, u32[]{:S(2)}) collective-permute-start(bf16[64,2176]{1,0:T(8,128)(2,1)S(1)} %collective-permute-done.6.refs_0_), channel_id=1, source_target_pairs={{2,6},{3,7},{6,10},{7,11},{10,14},{11,15},{14,12},{15,13},{12,8},{... | collective-permute-start | bytes 835592 | tf_op jit(solution)/shard_map/ppermute | solution.py:232
  49.4 0.5 collective-permute-start.11
  50.0 5.6 %expert_rows.11 = (f32[64,2048]{1,0:T(8,128)S(1)}, f32[64,2048]{1,0:T(8,128)S(1)}) custom-call(s32[2]{0:T(128)S(1)} %pad_add_fusion.ids_ref, bf16[64,2176]{1,0:T(8,128)(2,1)S(1)} %collective-permute-done.6.refs_0_, bf16[64,2176]{1,0:T(8,128)(2,1)S(1)} %collective-permute-done.7.refs_1_, bf16[2048,1536]{1,0:T(8,128)(2,1)S(1)} %bitcast.17, ...), custom_call_target="tpu_custom_call" | custom-call | flops 2415919104 | bytes 1572864 | tf_op jit(solution)/shard_map/expert_rows/pallas_call | solution.py:188
  55.6 1.5 %collective-permute-start.16 = (bf16[64,2176]{1,0:T(8,128)(2,1)S(1)}, bf16[64,2176]{1,0:T(8,128)(2,1)S(1)}, u32[]{:S(2)}, u32[]{:S(2)}) collective-permute-start(bf16[64,2176]{1,0:T(8,128)(2,1)S(1)} %collective-permute-done.12.refs_0_), channel_id=1, source_target_pairs={{2,6},{3,7},{6,10},{7,11},{10,14},{11,15},{14,12},{15,13},{12,8},{... | collective-permute-start | bytes 835592 | tf_op jit(solution)/shard_map/ppermute | solution.py:232
  57.2 0.5 collective-permute-start.17
  57.7 5.6 %expert_rows.12 = (f32[64,2048]{1,0:T(8,128)S(1)}, f32[64,2048]{1,0:T(8,128)S(1)}) custom-call(s32[2]{0:T(128)S(1)} %pad_add_fusion.ids_ref, bf16[64,2176]{1,0:T(8,128)(2,1)S(1)} %collective-permute-done.12.refs_0_, bf16[64,2176]{1,0:T(8,128)(2,1)S(1)} %collective-permute-done.13.refs_1_, bf16[2048,1536]{1,0:T(8,128)(2,1)S(1)} %bitcast.18, ...), custom_call_target="tpu_custom_call" | custom-call | flops 2415919104 | bytes 1572864 | tf_op jit(solution)/shard_map/expert_rows/pallas_call | solution.py:188
  63.3 1.5 %collective-permute-start.15 = (bf16[64,2176]{1,0:T(8,128)(2,1)S(1)}, bf16[64,2176]{1,0:T(8,128)(2,1)S(1)}, u32[]{:S(2)}, u32[]{:S(2)}) collective-permute-start(bf16[64,2176]{1,0:T(8,128)(2,1)S(1)} %collective-permute-done.10.refs_0_), channel_id=1, source_target_pairs={{2,6},{3,7},{6,10},{7,11},{10,14},{11,15},{14,12},{15,13},{12,8},{... | collective-permute-start | bytes 835592 | tf_op jit(solution)/shard_map/ppermute | solution.py:232
  64.9 5.6 %expert_rows.13 = (f32[64,2048]{1,0:T(8,128)S(1)}, f32[64,2048]{1,0:T(8,128)S(1)}) custom-call(s32[2]{0:T(128)S(1)} %pad_add_fusion.ids_ref, bf16[64,2176]{1,0:T(8,128)(2,1)S(1)} %collective-permute-done.10.refs_0_, bf16[64,2176]{1,0:T(8,128)(2,1)S(1)} %collective-permute-done.11.refs_1_, bf16[2048,1536]{1,0:T(8,128)(2,1)S(1)} %bitcast.19, ...), custom_call_target="tpu_custom_call" | custom-call | flops 2415919104 | bytes 1572864 | tf_op jit(solution)/shard_map/expert_rows/pallas_call | solution.py:188
  70.5 0.6 collective-permute-start.18
  71.1 5.6 %expert_rows.14 = (f32[64,2048]{1,0:T(8,128)S(1)}, f32[64,2048]{1,0:T(8,128)S(1)}) custom-call(s32[2]{0:T(128)S(1)} %pad_add_fusion.ids_ref, bf16[64,2176]{1,0:T(8,128)(2,1)S(1)} %collective-permute-done.16.refs_0_, bf16[64,2176]{1,0:T(8,128)(2,1)S(1)} %collective-permute-done.17.refs_1_, bf16[2048,1536]{1,0:T(8,128)(2,1)S(1)} %bitcast.20, ...), custom_call_target="tpu_custom_call" | custom-call | flops 2415919104 | bytes 1572864 | tf_op jit(solution)/shard_map/expert_rows/pallas_call | solution.py:188
  76.7 1.5 %collective-permute-start.25 = (bf16[64,2048]{1,0:T(8,128)(2,1)S(1)}, bf16[64,2048]{1,0:T(8,128)(2,1)S(1)}, u32[]{:S(2)}, u32[]{:S(2)}) collective-permute-start(bf16[64,2048]{1,0:T(8,128)(2,1)S(1)} %convert_element_type.113), channel_id=1, source_target_pairs={{2,6},{3,7},{6,10},{7,11},{10,14},{11,15},{14,12},{15,13},{12,8},{... | collective-permute-start | bytes 786440 | tf_op jit(solution)/shard_map/ppermute | solution.py:232
  78.3 0.8 collective-permute-start.14
  79.1 5.6 %expert_rows.15 = (f32[64,2048]{1,0:T(8,128)S(1)}, f32[64,2048]{1,0:T(8,128)S(1)}) custom-call(s32[2]{0:T(128)S(1)} %pad_add_fusion.ids_ref, bf16[64,2176]{1,0:T(8,128)(2,1)S(1)} %collective-permute-done.15.refs_0_, bf16[64,2176]{1,0:T(8,128)(2,1)S(1)} %collective-permute-done.18.refs_1_, bf16[2048,1536]{1,0:T(8,128)(2,1)S(1)} %bitcast.21, ...), custom_call_target="tpu_custom_call" | custom-call | flops 2415919104 | bytes 1572864 | tf_op jit(solution)/shard_map/expert_rows/pallas_call | solution.py:188
  84.9 1.0 collective-permute-done.14
  85.9 1.6 %collective-permute-start.21 = (bf16[64,2048]{1,0:T(8,128)(2,1)S(1)}, bf16[64,2048]{1,0:T(8,128)(2,1)S(1)}, u32[]{:S(2)}, u32[]{:S(2)}) collective-permute-start(bf16[64,2048]{1,0:T(8,128)(2,1)S(1)} %convert_element_type.103), channel_id=1, source_target_pairs={{2,6},{3,7},{6,10},{7,11},{10,14},{11,15},{14,12},{15,13},{12,8},{... | collective-permute-start | bytes 786440 | tf_op jit(solution)/shard_map/ppermute | solution.py:232
  87.5 0.4 collective-permute-start.19
  88.0 1.6 %collective-permute-start.26 = (bf16[64,2048]{1,0:T(8,128)(2,1)S(1)}, bf16[64,2048]{1,0:T(8,128)(2,1)S(1)}, u32[]{:S(2)}, u32[]{:S(2)}) collective-permute-start(bf16[64,2048]{1,0:T(8,128)(2,1)S(1)} %add_convert_fusion.5), channel_id=1, source_target_pairs={{2,6},{3,7},{6,10},{7,11},{10,14},{11,15},{14,12},{15,13},{12,8},{... | collective-permute-start | bytes 786440 | tf_op jit(solution)/shard_map/ppermute | solution.py:232
  89.7 0.4 collective-permute-start.28
  90.1 5.1 %collective-permute-done.21 = bf16[64,2048]{1,0:T(8,128)(2,1)S(1)} collective-permute-done((bf16[64,2048]{1,0:T(8,128)(2,1)S(1)}, bf16[64,2048]{1,0:T(8,128)(2,1)S(1)}, u32[]{:S(2)}, u32[]{:S(2)}) %collective-permute-start.21) | collective-permute-done | bytes 262176 | tf_op jit(solution)/shard_map/ppermute | solution.py:232
  95.3 1.6 %collective-permute-start.22 = (bf16[64,2048]{1,0:T(8,128)(2,1)S(1)}, bf16[64,2048]{1,0:T(8,128)(2,1)S(1)}, u32[]{:S(2)}, u32[]{:S(2)}) collective-permute-start(bf16[64,2048]{1,0:T(8,128)(2,1)S(1)} %add_convert_fusion.9), channel_id=1, source_target_pairs={{2,6},{3,7},{6,10},{7,11},{10,14},{11,15},{14,12},{15,13},{12,8},{... | collective-permute-start | bytes 786440 | tf_op jit(solution)/shard_map/ppermute | solution.py:232
  96.9 0.1 add_convert_fusion.10
  97.0 0.5 collective-permute-start.20
  97.5 3.4 %collective-permute-done.26 = bf16[64,2048]{1,0:T(8,128)(2,1)S(1)} collective-permute-done((bf16[64,2048]{1,0:T(8,128)(2,1)S(1)}, bf16[64,2048]{1,0:T(8,128)(2,1)S(1)}, u32[]{:S(2)}, u32[]{:S(2)}) %collective-permute-start.26) | collective-permute-done | bytes 262176 | tf_op jit(solution)/shard_map/ppermute | solution.py:232
  100.9 1.6 %collective-permute-start.27 = (bf16[64,2048]{1,0:T(8,128)(2,1)S(1)}, bf16[64,2048]{1,0:T(8,128)(2,1)S(1)}, u32[]{:S(2)}, u32[]{:S(2)}) collective-permute-start(bf16[64,2048]{1,0:T(8,128)(2,1)S(1)} %add_convert_fusion.4), channel_id=1, source_target_pairs={{2,6},{3,7},{6,10},{7,11},{10,14},{11,15},{14,12},{15,13},{12,8},{... | collective-permute-start | bytes 786440 | tf_op jit(solution)/shard_map/ppermute | solution.py:232
  102.6 0.5 collective-permute-start.29
  103.1 2.6 %collective-permute-done.22 = bf16[64,2048]{1,0:T(8,128)(2,1)S(1)} collective-permute-done((bf16[64,2048]{1,0:T(8,128)(2,1)S(1)}, bf16[64,2048]{1,0:T(8,128)(2,1)S(1)}, u32[]{:S(2)}, u32[]{:S(2)}) %collective-permute-start.22) | collective-permute-done | bytes 262176 | tf_op jit(solution)/shard_map/ppermute | solution.py:232
  105.7 1.5 %collective-permute-start.23 = (bf16[64,2048]{1,0:T(8,128)(2,1)S(1)}, bf16[64,2048]{1,0:T(8,128)(2,1)S(1)}, u32[]{:S(2)}, u32[]{:S(2)}) collective-permute-start(bf16[64,2048]{1,0:T(8,128)(2,1)S(1)} %add_convert_fusion.8), channel_id=1, source_target_pairs={{2,6},{3,7},{6,10},{7,11},{10,14},{11,15},{14,12},{15,13},{12,8},{... | collective-permute-start | bytes 786440 | tf_op jit(solution)/shard_map/ppermute | solution.py:232
  107.2 3.0 %collective-permute-done.29 = bf16[64,2048]{1,0:T(8,128)(2,1)S(1)} collective-permute-done((bf16[64,2048]{1,0:T(8,128)(2,1)S(1)}, bf16[64,2048]{1,0:T(8,128)(2,1)S(1)}, u32[]{:S(2)}, u32[]{:S(2)}) %collective-permute-start.29) | collective-permute-done | bytes 262176 | tf_op jit(solution)/shard_map/ppermute | solution.py:232
  110.3 0.6 collective-permute-start.30
  110.9 3.2 %collective-permute-done.23 = bf16[64,2048]{1,0:T(8,128)(2,1)S(1)} collective-permute-done((bf16[64,2048]{1,0:T(8,128)(2,1)S(1)}, bf16[64,2048]{1,0:T(8,128)(2,1)S(1)}, u32[]{:S(2)}, u32[]{:S(2)}) %collective-permute-start.23) | collective-permute-done | bytes 262176 | tf_op jit(solution)/shard_map/ppermute | solution.py:232
  114.1 1.5 %collective-permute-start.24 = (bf16[64,2048]{1,0:T(8,128)(2,1)S(1)}, bf16[64,2048]{1,0:T(8,128)(2,1)}, u32[]{:S(2)}, u32[]{:S(2)}) collective-permute-start(bf16[64,2048]{1,0:T(8,128)(2,1)S(1)} %add_convert_fusion.7), channel_id=1, source_target_pairs={{2,6},{3,7},{6,10},{7,11},{10,14},{11,15},{14,12},{15,13},{12,8},{... | collective-permute-start | bytes 786440 | tf_op jit(solution)/shard_map/ppermute | solution.py:232
  115.7 1.4 %collective-permute-done.30 = bf16[64,2048]{1,0:T(8,128)(2,1)S(1)} collective-permute-done((bf16[64,2048]{1,0:T(8,128)(2,1)S(1)}, bf16[64,2048]{1,0:T(8,128)(2,1)S(1)}, u32[]{:S(2)}, u32[]{:S(2)}) %collective-permute-start.30) | collective-permute-done | bytes 262176 | tf_op jit(solution)/shard_map/ppermute | solution.py:232
  117.1 1.8 %collective-permute-start.31 = (bf16[64,2048]{1,0:T(8,128)(2,1)S(1)}, bf16[64,2048]{1,0:T(8,128)(2,1)}, u32[]{:S(2)}, u32[]{:S(2)}) collective-permute-start(bf16[64,2048]{1,0:T(8,128)(2,1)S(1)} %add_convert_fusion.1), channel_id=1, source_target_pairs={{6,2},{7,3},{10,6},{11,7},{14,10},{15,11},{12,14},{13,15},{8,12},{... | collective-permute-start | bytes 786440 | tf_op jit(solution)/shard_map/ppermute | solution.py:232
  118.9 1.8 %collective-permute-done.24 = bf16[64,2048]{1,0:T(8,128)(2,1)} collective-permute-done((bf16[64,2048]{1,0:T(8,128)(2,1)S(1)}, bf16[64,2048]{1,0:T(8,128)(2,1)}, u32[]{:S(2)}, u32[]{:S(2)}) %collective-permute-start.24) | collective-permute-done | bytes 262176 | tf_op jit(solution)/shard_map/ppermute | solution.py:232
  120.7 3.1 %collective-permute-done.31 = bf16[64,2048]{1,0:T(8,128)(2,1)} collective-permute-done((bf16[64,2048]{1,0:T(8,128)(2,1)S(1)}, bf16[64,2048]{1,0:T(8,128)(2,1)}, u32[]{:S(2)}, u32[]{:S(2)}) %collective-permute-start.31) | collective-permute-done | bytes 262176 | tf_op jit(solution)/shard_map/ppermute | solution.py:232
  123.7 1.4 %add_convert_fusion.6 = (bf16[64,2048]{1,0:T(8,128)(2,1)S(1)}, bf16[64,2048]{1,0:T(8,128)(2,1)S(1)}) fusion(bf16[64,2048]{1,0:T(8,128)(2,1)} %collective-permute-done.24, f32[64,2048]{1,0:T(8,128)S(1)} %copy-done.5, bf16[64,2048]{1,0:T(8,128)(2,1)S(1)} %collective-permute-done.20, bf16[64,2048]{1,0:T(8,128)(2,1)S(1)} %collective-permute-done.arrived_ref, ...), kind=kLoop, calls=%fused_computation.7 | loop fusion | flops 2097152 | bytes 3670017 | tf_op jit(solution)/shard_map/convert_element_type | solution.py:288
  125.1 0.8 maximum_bitcast_fusion
  (53 shorter events, 0.7 us)
Async XLA Ops:
  0.0 22.0 %collective-permute-start.2 = (bf16[2048,1536]{1,0:T(8,128)(2,1)}, bf16[2048,1536]{1,0:T(8,128)(2,1)}, u32[]{:S(2)}, u32[]{:S(2)}) collective-permute-start(bf16[2048,1536]{1,0:T(8,128)(2,1)} %bitcast.13), channel_id=1, source_target_pairs={{0,1},{1,0},{2,3},{3,2},{4,5},{5,4},{6,7},{7,6},{8,9},{9,8},{10,11... | collective-permute-start | bytes 18874376 | tf_op jit(solution)/shard_map/ppermute | solution.py:232
  0.5 21.0 %collective-permute-start.3 = (bf16[768,2048]{1,0:T(8,128)(2,1)}, bf16[768,2048]{1,0:T(8,128)(2,1)S(1)}, u32[]{:S(2)}, u32[]{:S(2)}) collective-permute-start(bf16[768,2048]{1,0:T(8,128)(2,1)} %bitcast.22), channel_id=1, source_target_pairs={{0,1},{1,0},{2,3},{3,2},{4,5},{5,4},{6,7},{7,6},{8,9},{9,8},{10,11... | collective-permute-start | bytes 9437192 | tf_op jit(solution)/shard_map/ppermute | solution.py:232
  2.4 11.9 %collective-permute-start = (bf16[64,2048]{1,0:T(8,128)(2,1)}, bf16[64,2048]{1,0:T(8,128)(2,1)S(1)}, u32[]{:S(2)}, u32[]{:S(2)}) collective-permute-start(bf16[64,2048]{1,0:T(8,128)(2,1)} %get-tuple-element.91), channel_id=1, source_target_pairs={{0,16},{1,17},{2,18},{3,19},{4,20},{5,21},{6,22},{7,23},{8,24},{9,... | collective-permute-start | bytes 786440 | tf_op jit(solution)/shard_map/ppermute | solution.py:18
  7.3 11.6 %collective-permute-start.1 = (bf16[64,2048]{1,0:T(8,128)(2,1)}, bf16[64,2048]{1,0:T(8,128)(2,1)}, u32[]{:S(2)}, u32[]{:S(2)}) collective-permute-start(bf16[64,2048]{1,0:T(8,128)(2,1)} %get-tuple-element.92), channel_id=1, source_target_pairs={{0,16},{1,17},{2,18},{3,19},{4,20},{5,21},{6,22},{7,23},{8,24},{9,... | collective-permute-start | bytes 786440 | tf_op jit(solution)/shard_map/ppermute | solution.py:18
  10.8 1.0 copy-start.6
  11.9 0.7 copy-start.10
  14.3 18.2 %collective-permute-start.4 = (bf16[64,2176]{1,0:T(8,128)(2,1)S(1)}, bf16[64,2176]{1,0:T(8,128)(2,1)S(1)}, u32[]{:S(2)}, u32[]{:S(2)}) collective-permute-start(bf16[64,2176]{1,0:T(8,128)(2,1)S(1)} %norm_rows.2.refs_0_), channel_id=1, source_target_pairs={{2,6},{3,7},{6,10},{7,11},{10,14},{11,15},{14,12},{15,13},{12,8},{... | collective-permute-start | bytes 835592 | tf_op jit(solution)/shard_map/ppermute | solution.py:232
  15.8 16.6 %collective-permute-start.5 = (bf16[64,2176]{1,0:T(8,128)(2,1)S(1)}, bf16[64,2176]{1,0:T(8,128)(2,1)S(1)}, u32[]{:S(2)}, u32[]{:S(2)}) collective-permute-start(bf16[64,2176]{1,0:T(8,128)(2,1)S(1)} %norm_rows.2.refs_0_), channel_id=1, source_target_pairs={{6,2},{7,3},{10,6},{11,7},{14,10},{15,11},{12,14},{13,15},{8,12},{... | collective-permute-start | bytes 835592 | tf_op jit(solution)/shard_map/ppermute | solution.py:232
  19.9 20.3 %collective-permute-start.8 = (bf16[64,2176]{1,0:T(8,128)(2,1)S(1)}, bf16[64,2176]{1,0:T(8,128)(2,1)S(1)}, u32[]{:S(2)}, u32[]{:S(2)}) collective-permute-start(bf16[64,2176]{1,0:T(8,128)(2,1)S(1)} %norm_rows.3.refs_1_), channel_id=1, source_target_pairs={{2,6},{3,7},{6,10},{7,11},{10,14},{11,15},{14,12},{15,13},{12,8},{... | collective-permute-start | bytes 835592 | tf_op jit(solution)/shard_map/ppermute | solution.py:232
  21.4 18.8 %collective-permute-start.9 = (bf16[64,2176]{1,0:T(8,128)(2,1)S(1)}, bf16[64,2176]{1,0:T(8,128)(2,1)S(1)}, u32[]{:S(2)}, u32[]{:S(2)}) collective-permute-start(bf16[64,2176]{1,0:T(8,128)(2,1)S(1)} %norm_rows.3.refs_1_), channel_id=1, source_target_pairs={{6,2},{7,3},{10,6},{11,7},{14,10},{15,11},{12,14},{13,15},{8,12},{... | collective-permute-start | bytes 835592 | tf_op jit(solution)/shard_map/ppermute | solution.py:232
  22.0 2.8 %copy-start = (bf16[1,1,2048,1536]{3,2,1,0:T(8,128)(2,1)S(1)}, bf16[1,1,2048,1536]{3,2,1,0:T(8,128)(2,1)}, u32[]{:S(2)}) copy-start(bf16[1,1,2048,1536]{3,2,1,0:T(8,128)(2,1)} %param.12) | copy-start | bytes 18874372
  24.7 1.9 %copy-start.2 = (bf16[1,1,768,2048]{3,2,1,0:T(8,128)(2,1)S(1)}, bf16[1,1,768,2048]{3,2,1,0:T(8,128)(2,1)}, u32[]{:S(2)}) copy-start(bf16[1,1,768,2048]{3,2,1,0:T(8,128)(2,1)} %param.13) | copy-start | bytes 9437188
  26.6 7.9 %copy-start.1 = (bf16[1,1,2048,1536]{3,2,1,0:T(8,128)(2,1)S(1)}, bf16[1,1,2048,1536]{3,2,1,0:T(8,128)(2,1)}, u32[]{:S(2)}) copy-start(bf16[1,1,2048,1536]{3,2,1,0:T(8,128)(2,1)} %param.12) | copy-start | bytes 18874372
  26.6 7.9 %copy-start.3 = (bf16[1,1,768,2048]{3,2,1,0:T(8,128)(2,1)S(1)}, bf16[1,1,768,2048]{3,2,1,0:T(8,128)(2,1)}, u32[]{:S(2)}) copy-start(bf16[1,1,768,2048]{3,2,1,0:T(8,128)(2,1)} %param.13) | copy-start | bytes 9437188
  32.4 7.8 %copy-start.4 = (f32[64,2048]{1,0:T(8,128)}, f32[64,2048]{1,0:T(8,128)S(1)}, u32[]{:S(2)}) copy-start(f32[64,2048]{1,0:T(8,128)S(1)} %get-tuple-element.49.refs_6_) | copy-start | bytes 1572868
  32.4 7.7 %copy-start.8 = (f32[64,2048]{1,0:T(8,128)}, f32[64,2048]{1,0:T(8,128)S(1)}, u32[]{:S(2)}) copy-start(f32[64,2048]{1,0:T(8,128)S(1)} %get-tuple-element.79) | copy-start | bytes 1572868
  32.4 15.4 %collective-permute-start.6 = (bf16[64,2176]{1,0:T(8,128)(2,1)S(1)}, bf16[64,2176]{1,0:T(8,128)(2,1)S(1)}, u32[]{:S(2)}, u32[]{:S(2)}) collective-permute-start(bf16[64,2176]{1,0:T(8,128)(2,1)S(1)} %collective-permute-done.4.refs_0_), channel_id=1, source_target_pairs={{2,6},{3,7},{6,10},{7,11},{10,14},{11,15},{14,12},{15,13},{12,8},{... | collective-permute-start | bytes 835592 | tf_op jit(solution)/shard_map/ppermute | solution.py:232
  34.0 13.9 %collective-permute-start.7 = (bf16[64,2176]{1,0:T(8,128)(2,1)S(1)}, bf16[64,2176]{1,0:T(8,128)(2,1)S(1)}, u32[]{:S(2)}, u32[]{:S(2)}) collective-permute-start(bf16[64,2176]{1,0:T(8,128)(2,1)S(1)} %collective-permute-done.5.refs_1_), channel_id=1, source_target_pairs={{6,2},{7,3},{10,6},{11,7},{14,10},{15,11},{12,14},{13,15},{8,12},{... | collective-permute-start | bytes 835592 | tf_op jit(solution)/shard_map/ppermute | solution.py:232
  40.2 15.4 %collective-permute-start.12 = (bf16[64,2176]{1,0:T(8,128)(2,1)S(1)}, bf16[64,2176]{1,0:T(8,128)(2,1)S(1)}, u32[]{:S(2)}, u32[]{:S(2)}) collective-permute-start(bf16[64,2176]{1,0:T(8,128)(2,1)S(1)} %collective-permute-done.8.refs_0_), channel_id=1, source_target_pairs={{2,6},{3,7},{6,10},{7,11},{10,14},{11,15},{14,12},{15,13},{12,8},{... | collective-permute-start | bytes 835592 | tf_op jit(solution)/shard_map/ppermute | solution.py:232
  41.7 13.9 %collective-permute-start.13 = (bf16[64,2176]{1,0:T(8,128)(2,1)S(1)}, bf16[64,2176]{1,0:T(8,128)(2,1)S(1)}, u32[]{:S(2)}, u32[]{:S(2)}) collective-permute-start(bf16[64,2176]{1,0:T(8,128)(2,1)S(1)} %collective-permute-done.9.refs_1_), channel_id=1, source_target_pairs={{6,2},{7,3},{10,6},{11,7},{14,10},{15,11},{12,14},{13,15},{8,12},{... | collective-permute-start | bytes 835592 | tf_op jit(solution)/shard_map/ppermute | solution.py:232
  47.9 15.4 %collective-permute-start.10 = (bf16[64,2176]{1,0:T(8,128)(2,1)S(1)}, bf16[64,2176]{1,0:T(8,128)(2,1)S(1)}, u32[]{:S(2)}, u32[]{:S(2)}) collective-permute-start(bf16[64,2176]{1,0:T(8,128)(2,1)S(1)} %collective-permute-done.6.refs_0_), channel_id=1, source_target_pairs={{2,6},{3,7},{6,10},{7,11},{10,14},{11,15},{14,12},{15,13},{12,8},{... | collective-permute-start | bytes 835592 | tf_op jit(solution)/shard_map/ppermute | solution.py:232
  49.4 13.9 %collective-permute-start.11 = (bf16[64,2176]{1,0:T(8,128)(2,1)S(1)}, bf16[64,2176]{1,0:T(8,128)(2,1)S(1)}, u32[]{:S(2)}, u32[]{:S(2)}) collective-permute-start(bf16[64,2176]{1,0:T(8,128)(2,1)S(1)} %collective-permute-done.7.refs_1_), channel_id=1, source_target_pairs={{6,2},{7,3},{10,6},{11,7},{14,10},{15,11},{12,14},{13,15},{8,12},{... | collective-permute-start | bytes 835592 | tf_op jit(solution)/shard_map/ppermute | solution.py:232
  55.6 14.9 %collective-permute-start.16 = (bf16[64,2176]{1,0:T(8,128)(2,1)S(1)}, bf16[64,2176]{1,0:T(8,128)(2,1)S(1)}, u32[]{:S(2)}, u32[]{:S(2)}) collective-permute-start(bf16[64,2176]{1,0:T(8,128)(2,1)S(1)} %collective-permute-done.12.refs_0_), channel_id=1, source_target_pairs={{2,6},{3,7},{6,10},{7,11},{10,14},{11,15},{14,12},{15,13},{12,8},{... | collective-permute-start | bytes 835592 | tf_op jit(solution)/shard_map/ppermute | solution.py:232
  57.2 13.3 %collective-permute-start.17 = (bf16[64,2176]{1,0:T(8,128)(2,1)S(1)}, bf16[64,2176]{1,0:T(8,128)(2,1)S(1)}, u32[]{:S(2)}, u32[]{:S(2)}) collective-permute-start(bf16[64,2176]{1,0:T(8,128)(2,1)S(1)} %collective-permute-done.13.refs_1_), channel_id=1, source_target_pairs={{6,2},{7,3},{10,6},{11,7},{14,10},{15,11},{12,14},{13,15},{8,12},{... | collective-permute-start | bytes 835592 | tf_op jit(solution)/shard_map/ppermute | solution.py:232
  63.3 15.8 %collective-permute-start.15 = (bf16[64,2176]{1,0:T(8,128)(2,1)S(1)}, bf16[64,2176]{1,0:T(8,128)(2,1)S(1)}, u32[]{:S(2)}, u32[]{:S(2)}) collective-permute-start(bf16[64,2176]{1,0:T(8,128)(2,1)S(1)} %collective-permute-done.10.refs_0_), channel_id=1, source_target_pairs={{2,6},{3,7},{6,10},{7,11},{10,14},{11,15},{14,12},{15,13},{12,8},{... | collective-permute-start | bytes 835592 | tf_op jit(solution)/shard_map/ppermute | solution.py:232
  70.5 8.6 %collective-permute-start.18 = (bf16[64,2176]{1,0:T(8,128)(2,1)S(1)}, bf16[64,2176]{1,0:T(8,128)(2,1)S(1)}, u32[]{:S(2)}, u32[]{:S(2)}) collective-permute-start(bf16[64,2176]{1,0:T(8,128)(2,1)S(1)} %collective-permute-done.17.refs_1_), channel_id=1, source_target_pairs={{6,2},{7,3},{10,6},{11,7},{14,10},{15,11},{12,14},{13,15},{8,12},{... | collective-permute-start | bytes 835592 | tf_op jit(solution)/shard_map/ppermute | solution.py:232
  76.7 8.1 %collective-permute-start.25 = (bf16[64,2048]{1,0:T(8,128)(2,1)S(1)}, bf16[64,2048]{1,0:T(8,128)(2,1)S(1)}, u32[]{:S(2)}, u32[]{:S(2)}) collective-permute-start(bf16[64,2048]{1,0:T(8,128)(2,1)S(1)} %convert_element_type.113), channel_id=1, source_target_pairs={{2,6},{3,7},{6,10},{7,11},{10,14},{11,15},{14,12},{15,13},{12,8},{... | collective-permute-start | bytes 786440 | tf_op jit(solution)/shard_map/ppermute | solution.py:232
  78.3 7.5 %collective-permute-start.14 = (bf16[64,2048]{1,0:T(8,128)(2,1)S(1)}, bf16[64,2048]{1,0:T(8,128)(2,1)S(1)}, u32[]{:S(2)}, u32[]{:S(2)}) collective-permute-start(bf16[64,2048]{1,0:T(8,128)(2,1)S(1)} %convert_element_type.97), channel_id=1, source_target_pairs={{6,2},{7,3},{10,6},{11,7},{14,10},{15,11},{12,14},{13,15},{8,12},{... | collective-permute-start | bytes 786440 | tf_op jit(solution)/shard_map/ppermute | solution.py:232
  84.7 39.0 %copy-start.5 = (f32[64,2048]{1,0:T(8,128)S(1)}, f32[64,2048]{1,0:T(8,128)}, u32[]{:S(2)}) copy-start(f32[64,2048]{1,0:T(8,128)} %copy-done.4) | copy-start | bytes 1572868
  84.8 39.0 %copy-start.7 = (bf16[128,2048]{1,0:T(8,128)(2,1)S(1)}, bf16[128,2048]{1,0:T(8,128)(2,1)}, u32[]{:S(2)}) copy-start(bf16[128,2048]{1,0:T(8,128)(2,1)} %fresh_ref.1) | copy-start | bytes 1572868
  84.8 38.9 %copy-start.9 = (f32[64,2048]{1,0:T(8,128)S(1)}, f32[64,2048]{1,0:T(8,128)}, u32[]{:S(2)}) copy-start(f32[64,2048]{1,0:T(8,128)} %copy-done.8) | copy-start | bytes 1572868
  85.9 9.3 %collective-permute-start.21 = (bf16[64,2048]{1,0:T(8,128)(2,1)S(1)}, bf16[64,2048]{1,0:T(8,128)(2,1)S(1)}, u32[]{:S(2)}, u32[]{:S(2)}) collective-permute-start(bf16[64,2048]{1,0:T(8,128)(2,1)S(1)} %convert_element_type.103), channel_id=1, source_target_pairs={{2,6},{3,7},{6,10},{7,11},{10,14},{11,15},{14,12},{15,13},{12,8},{... | collective-permute-start | bytes 786440 | tf_op jit(solution)/shard_map/ppermute | solution.py:232
  87.5 9.3 %collective-permute-start.19 = (bf16[64,2048]{1,0:T(8,128)(2,1)S(1)}, bf16[64,2048]{1,0:T(8,128)(2,1)S(1)}, u32[]{:S(2)}, u32[]{:S(2)}) collective-permute-start(bf16[64,2048]{1,0:T(8,128)(2,1)S(1)} %add_convert_fusion.11), channel_id=1, source_target_pairs={{6,2},{7,3},{10,6},{11,7},{14,10},{15,11},{12,14},{13,15},{8,12},{... | collective-permute-start | bytes 786440 | tf_op jit(solution)/shard_map/ppermute | solution.py:232
  88.0 12.8 %collective-permute-start.26 = (bf16[64,2048]{1,0:T(8,128)(2,1)S(1)}, bf16[64,2048]{1,0:T(8,128)(2,1)S(1)}, u32[]{:S(2)}, u32[]{:S(2)}) collective-permute-start(bf16[64,2048]{1,0:T(8,128)(2,1)S(1)} %add_convert_fusion.5), channel_id=1, source_target_pairs={{2,6},{3,7},{6,10},{7,11},{10,14},{11,15},{14,12},{15,13},{12,8},{... | collective-permute-start | bytes 786440 | tf_op jit(solution)/shard_map/ppermute | solution.py:232
  89.7 12.8 %collective-permute-start.28 = (bf16[64,2048]{1,0:T(8,128)(2,1)S(1)}, bf16[64,2048]{1,0:T(8,128)(2,1)S(1)}, u32[]{:S(2)}, u32[]{:S(2)}) collective-permute-start(bf16[64,2048]{1,0:T(8,128)(2,1)S(1)} %convert_element_type.119), channel_id=1, source_target_pairs={{6,2},{7,3},{10,6},{11,7},{14,10},{15,11},{12,14},{13,15},{8,12},{... | collective-permute-start | bytes 786440 | tf_op jit(solution)/shard_map/ppermute | solution.py:232
  95.3 10.4 %collective-permute-start.22 = (bf16[64,2048]{1,0:T(8,128)(2,1)S(1)}, bf16[64,2048]{1,0:T(8,128)(2,1)S(1)}, u32[]{:S(2)}, u32[]{:S(2)}) collective-permute-start(bf16[64,2048]{1,0:T(8,128)(2,1)S(1)} %add_convert_fusion.9), channel_id=1, source_target_pairs={{2,6},{3,7},{6,10},{7,11},{10,14},{11,15},{14,12},{15,13},{12,8},{... | collective-permute-start | bytes 786440 | tf_op jit(solution)/shard_map/ppermute | solution.py:232
  97.0 21.9 %collective-permute-start.20 = (bf16[64,2048]{1,0:T(8,128)(2,1)S(1)}, bf16[64,2048]{1,0:T(8,128)(2,1)S(1)}, u32[]{:S(2)}, u32[]{:S(2)}) collective-permute-start(bf16[64,2048]{1,0:T(8,128)(2,1)S(1)} %add_convert_fusion.10), channel_id=1, source_target_pairs={{6,2},{7,3},{10,6},{11,7},{14,10},{15,11},{12,14},{13,15},{8,12},{... | collective-permute-start | bytes 786440 | tf_op jit(solution)/shard_map/ppermute | solution.py:232
  100.9 18.0 %collective-permute-start.27 = (bf16[64,2048]{1,0:T(8,128)(2,1)S(1)}, bf16[64,2048]{1,0:T(8,128)(2,1)S(1)}, u32[]{:S(2)}, u32[]{:S(2)}) collective-permute-start(bf16[64,2048]{1,0:T(8,128)(2,1)S(1)} %add_convert_fusion.4), channel_id=1, source_target_pairs={{2,6},{3,7},{6,10},{7,11},{10,14},{11,15},{14,12},{15,13},{12,8},{... | collective-permute-start | bytes 786440 | tf_op jit(solution)/shard_map/ppermute | solution.py:232
  102.6 7.7 %collective-permute-start.29 = (bf16[64,2048]{1,0:T(8,128)(2,1)S(1)}, bf16[64,2048]{1,0:T(8,128)(2,1)S(1)}, u32[]{:S(2)}, u32[]{:S(2)}) collective-permute-start(bf16[64,2048]{1,0:T(8,128)(2,1)S(1)} %add_convert_fusion.3), channel_id=1, source_target_pairs={{6,2},{7,3},{10,6},{11,7},{14,10},{15,11},{12,14},{13,15},{8,12},{... | collective-permute-start | bytes 786440 | tf_op jit(solution)/shard_map/ppermute | solution.py:232
  105.7 8.4 %collective-permute-start.23 = (bf16[64,2048]{1,0:T(8,128)(2,1)S(1)}, bf16[64,2048]{1,0:T(8,128)(2,1)S(1)}, u32[]{:S(2)}, u32[]{:S(2)}) collective-permute-start(bf16[64,2048]{1,0:T(8,128)(2,1)S(1)} %add_convert_fusion.8), channel_id=1, source_target_pairs={{2,6},{3,7},{6,10},{7,11},{10,14},{11,15},{14,12},{15,13},{12,8},{... | collective-permute-start | bytes 786440 | tf_op jit(solution)/shard_map/ppermute | solution.py:232
  110.3 6.7 %collective-permute-start.30 = (bf16[64,2048]{1,0:T(8,128)(2,1)S(1)}, bf16[64,2048]{1,0:T(8,128)(2,1)S(1)}, u32[]{:S(2)}, u32[]{:S(2)}) collective-permute-start(bf16[64,2048]{1,0:T(8,128)(2,1)S(1)} %add_convert_fusion.2), channel_id=1, source_target_pairs={{6,2},{7,3},{10,6},{11,7},{14,10},{15,11},{12,14},{13,15},{8,12},{... | collective-permute-start | bytes 786440 | tf_op jit(solution)/shard_map/ppermute | solution.py:232
  114.1 6.5 %collective-permute-start.24 = (bf16[64,2048]{1,0:T(8,128)(2,1)S(1)}, bf16[64,2048]{1,0:T(8,128)(2,1)}, u32[]{:S(2)}, u32[]{:S(2)}) collective-permute-start(bf16[64,2048]{1,0:T(8,128)(2,1)S(1)} %add_convert_fusion.7), channel_id=1, source_target_pairs={{2,6},{3,7},{6,10},{7,11},{10,14},{11,15},{14,12},{15,13},{12,8},{... | collective-permute-start | bytes 786440 | tf_op jit(solution)/shard_map/ppermute | solution.py:232
  117.1 6.6 %collective-permute-start.31 = (bf16[64,2048]{1,0:T(8,128)(2,1)S(1)}, bf16[64,2048]{1,0:T(8,128)(2,1)}, u32[]{:S(2)}, u32[]{:S(2)}) collective-permute-start(bf16[64,2048]{1,0:T(8,128)(2,1)S(1)} %add_convert_fusion.1), channel_id=1, source_target_pairs={{6,2},{7,3},{10,6},{11,7},{14,10},{15,11},{12,14},{13,15},{8,12},{... | collective-permute-start | bytes 786440 | tf_op jit(solution)/shard_map/ppermute | solution.py:232

commit v3 on v2

--- a/solution.py
+++ b/solution.py
@@ -10,6 +10,7 @@
 epsilon = 1e-06
 LANES = 128
 CORES = 2
+MIB = 1 << 20
 
 
 def from_behind(value, axis, by):
@@ -71,7 +72,8 @@
     return (wide_input + mixed).astype(jnp.bfloat16)[None]
 
 
-def base_kernel(fresh_ref, gain_ref, routes_ref, gates_ref, rows_ref, gain_out_ref, *, experts):
+def base_kernel(fresh_ref, gain_ref, routes_ref, gates_ref, gate_up_ref, down_ref, rows_ref, gain_out_ref, *, experts):
+    del gate_up_ref, down_ref
     width = fresh_ref.shape[1]
     rows = fresh_ref.shape[0]
     rows_ref[:, :width] = normed_rows(fresh_ref[...], gain_ref[...])
@@ -95,7 +97,7 @@
     return (wide * scale * gain).astype(jnp.bfloat16)
 
 
-def base_rows(fresh, gain, routes, gates, experts):
+def base_rows(fresh, gain, routes, gates, weights, experts):
     rows, width = fresh.shape
     vmem = pl.BlockSpec(memory_space=pltpu.VMEM)
     return pl.pallas_call(
@@ -104,12 +106,14 @@
             jax.ShapeDtypeStruct((rows, width + LANES), jnp.bfloat16),
             jax.ShapeDtypeStruct(gain.shape, jnp.float32),
         ),
-        in_specs=[vmem] * 4,
+        in_specs=[vmem] * 6,
         out_specs=(vmem, vmem),
-        compiler_params=pltpu.CompilerParams(vmem_limit_bytes=12 << 20),
-        cost_estimate=pl.CostEstimate(flops=rows * width * 6, bytes_accessed=rows * width * 4, transcendentals=rows),
+        compiler_params=pltpu.CompilerParams(vmem_limit_bytes=16 * MIB),
+        cost_estimate=pl.CostEstimate(
+            flops=rows * width * 6, bytes_accessed=weights[0].size * 6, transcendentals=rows
+        ),
         name="base_rows",
-    )(fresh, gain, routes, gates)
+    )(fresh, gain, routes, gates, *weights)
 
 
 def norm_kernel(section_ref, base_ref, arrived_ref, gain_ref, rows_ref, *, start):
@@ -135,20 +139,26 @@
         out_shape=jax.ShapeDtypeStruct((rows, base.shape[1]), jnp.bfloat16),
         in_specs=[pl.BlockSpec(memory_space=pltpu.SMEM)] + [vmem] * 3,
         out_specs=vmem,
-        compiler_params=pltpu.CompilerParams(vmem_limit_bytes=12 << 20),
+        compiler_params=pltpu.CompilerParams(vmem_limit_bytes=12 * MIB),
         cost_estimate=pl.CostEstimate(flops=rows * width * 6, bytes_accessed=rows * width * 6, transcendentals=rows),
         name="norm_rows",
     )(section_id.reshape(1), base, arrived, gain)
 
 
-def mlp_kernel(ids_ref, *refs, parts, chained, experts):
+def mlp_kernel(ids_ref, *refs, parts, chained, held, experts):
     payloads = refs[:parts]
-    weights = (refs[parts : parts + 2], refs[parts + 2 : parts + 4])
+    own, other = refs[parts : parts + 2], refs[parts + 2 : parts + 4]
     refs = refs[parts + 4 + chained :]
     outs = refs[:parts]
-    x_ref, coef_ref, hidden_ref = refs[parts:]
+    refs = refs[parts:]
+    if held:
+        copy = pltpu.make_async_copy(other[0], refs[0], refs[-1])
+        copy.start()
+        refs = refs[1:-1]
+    weights = (own, other)
+    x_ref, coef_ref, hidden_ref = refs
     width = x_ref.shape[1]
-    hidden = weights[0][1].shape[0]
+    hidden = own[1].shape[0]
     bounds = []
     start = 0
     for payload in payloads:
@@ -176,35 +186,60 @@
             total += jnp.dot(rows, down[:, t : t + tile], preferred_element_type=jnp.float32)
         for here, out in zip(bounds, outs):
             out[:, t : t + tile] = total[here, :]
-
-
-def expert_rows(ids, payloads, weights, after, experts):
-    (own_gate_up, own_down), (other_gate_up, other_down) = weights
-    width = own_gate_up.shape[0]
-    hidden = own_down.shape[0]
+    if held:
+        copy.wait()
+
+
+def expert_rows(ids, payloads, own, other, after, experts, hold=False):
+    width = own[0].shape[0]
+    hidden = own[1].shape[0]
     rows = sum(p.shape[0] for p in payloads)
     vmem = pl.BlockSpec(memory_space=pltpu.VMEM)
     chain = [] if after is None else [after]
-    return pl.pallas_call(
-        functools.partial(mlp_kernel, parts=len(payloads), chained=len(chain), experts=experts),
-        out_shape=[jax.ShapeDtypeStruct((p.shape[0], width), jnp.float32) for p in payloads],
+    held = [jax.ShapeDtypeStruct(other[0].shape, other[0].dtype)] if hold else []
+    results = pl.pallas_call(
+        functools.partial(mlp_kernel, parts=len(payloads), chained=len(chain), held=hold, experts=experts),
+        out_shape=[jax.ShapeDtypeStruct((p.shape[0], width), jnp.float32) for p in payloads] + held,
         in_specs=[pl.BlockSpec(memory_space=pltpu.SMEM)]
         + [vmem] * (len(payloads) + 4)
         + [pl.BlockSpec(memory_space=pl.ANY)] * len(chain),
-        out_specs=[vmem] * len(payloads),
+        out_specs=[vmem] * (len(payloads) + len(held)),
         scratch_shapes=[
             pltpu.VMEM((rows, width), jnp.bfloat16),
             pltpu.VMEM((2, rows, LANES), jnp.float32),
             pltpu.VMEM((rows, 2 * hidden), jnp.bfloat16),
-        ],
-        compiler_params=pltpu.CompilerParams(vmem_limit_bytes=12 << 20),
+        ]
+        + ([pltpu.SemaphoreType.DMA] if hold else []),
+        compiler_params=pltpu.CompilerParams(vmem_limit_bytes=16 * MIB),
         cost_estimate=pl.CostEstimate(
             flops=2 * rows * width * hidden * 6,
             bytes_accessed=rows * width * 6,
             transcendentals=rows * hidden * 2,
         ),
         name="expert_rows",
-    )(ids, *payloads, own_gate_up, own_down, other_gate_up, other_down, *chain)
+    )(ids, *payloads, *own, *other, *chain)
+    return (results[:-1], results[-1]) if hold else results
+
+
+def last_kernel(base_ref, first_ref, second_ref, out_ref):
+    half = first_ref.shape[0]
+    for start, total_ref in ((0, first_ref), (half, second_ref)):
+        here = slice(start, start + half)
+        out_ref[here, :] = (base_ref[here, :] + total_ref[...].astype(jnp.float32)).astype(jnp.bfloat16)
+
+
+def last_rows(base, first, second):
+    rows, width = base.shape
+    vmem = pl.BlockSpec(memory_space=pltpu.VMEM)
+    return pl.pallas_call(
+        last_kernel,
+        out_shape=jax.ShapeDtypeStruct((rows, width), jnp.bfloat16),
+        in_specs=[vmem] * 3,
+        out_specs=vmem,
+        compiler_params=pltpu.CompilerParams(vmem_limit_bytes=8 * MIB),
+        cost_estimate=pl.CostEstimate(flops=rows * width, bytes_accessed=rows * width * 8, transcendentals=0),
+        name="last_rows",
+    )(base, first, second)
 
 
 def chip_ring(depth, across):
@@ -231,37 +266,47 @@
     def move(value, pairs):
         return lax.ppermute(value, "expert", pairs)
 
+    own = (w_gate_up[0, 0], w_down[0, 0])
+    far_other = tuple(move(w, swap) for w in own)
     cuts = [slice(0, half), slice(half, rows)]
-    arrived = [from_behind(previous[0, cut], "section", 1) for cut in cuts]
-    own = (w_gate_up[0, 0], w_down[0, 0])
-    other = tuple(move(w, swap) for w in own)
+    first_cut = previous[0, cuts[0]]
+    second_cut = lax.optimization_barrier((previous, first_cut))[0][0, cuts[1]]
+    arrived = [from_behind(cut, "section", 1) for cut in (first_cut, second_cut)]
     ids = jnp.stack([expert_id, expert_id ^ 1]).astype(jnp.int32)
-    base, gain = base_rows(fresh, norm_gain, routes[0], gate_weights[0], devices_exp)
+    base, gain = base_rows(fresh, norm_gain, routes[0], gate_weights[0], own, devices_exp)
     packed = [norm_rows(section_id, base, arrived[c], gain, cuts[c].start) for c in range(2)]
-
-    last = None
-
-    def mlp(payloads):
-        nonlocal last
-        sums = expert_rows(ids, payloads, (own, other), last, devices_exp)
-        last = sums[0]
-        return sums
 
     hops = chips // 2
     ups = [packed] + [[None, None] for _ in range(hops)]
     downs = [packed] + [[None, None] for _ in range(hops)]
-    to_down, to_up, own_sums = {}, {}, None
-    for s in range(hops):
-        for c in range(2):
-            rising, falling = lax.optimization_barrier((ups[s][c], downs[s][c], last))[:2]
-            if s < hops - 1 or c == 0:
-                ups[s + 1][c] = move(rising, up)
-            if s < hops - 1 or c == 1:
-                downs[s + 1][c] = move(falling, down)
-            if s > 0:
-                to_down[s, c], to_up[s, c] = mlp([ups[s][c], downs[s][c]])
-            elif c == 1:
-                own_sums = mlp(packed)
+
+    def pass_on(s, c, after):
+        rising, falling = lax.optimization_barrier((ups[s][c], downs[s][c], after))[:2]
+        if s < hops - 1 or c == 0:
+            ups[s + 1][c] = move(rising, up)
+        if s < hops - 1 or c == 1:
+            downs[s + 1][c] = move(falling, down)
+
+    pass_on(0, 0, None)
+    pass_on(0, 1, None)
+    own_sums, other_gate_up = expert_rows(ids, packed, own, far_other, None, devices_exp, hold=True)
+    other = (other_gate_up, far_other[1])
+    last = own_sums[0]
+
+    def mlp(payloads):
+        nonlocal last
+        sums = expert_rows(ids, payloads, own, other, last, devices_exp)
+        last = sums[0]
+        return sums
+
+    to_down, to_up = {}, {}
+    for s in range(1, hops - 1):
+        pass_on(s, 0, last)
+        pass_on(s, 1, (last, ups[s][0], downs[s][0]))
+        to_down[s, 0], to_down[s, 1], to_up[s, 0], to_up[s, 1] = mlp(ups[s] + downs[s])
+    for c in range(2):
+        pass_on(hops - 1, c, (last, ups[hops - 1][0], downs[hops - 1][0]))
+        to_down[hops - 1, c], to_up[hops - 1, c] = mlp([ups[hops - 1][c], downs[hops - 1][c]])
     to_up[hops, 0], to_down[hops, 1] = mlp([ups[hops][0], downs[hops][1]])
 
     flows = [(to_down, 0, down), (to_up, 1, up), (to_up, 0, up), (to_down, 1, down)]
@@ -278,15 +323,10 @@
                 total = terms[place, c] + carried.astype(jnp.float32)
             totals[i] = move(total.astype(jnp.bfloat16), pairs)
 
-    outs = []
-    for c in range(2):
-        arrival = jnp.where(section_id == 0, fresh[cuts[c]], arrived[c]).astype(jnp.float32)
-        mixed = own_sums[c]
-        for total, flow in zip(totals, flows):
-            if flow[1] == c:
-                mixed += total.astype(jnp.float32)
-        outs.append((arrival + mixed).astype(jnp.bfloat16))
-    return jnp.concatenate(outs, axis=0)[None]
+    arrival = jnp.where(section_id == 0, fresh, jnp.concatenate(arrived, axis=0)).astype(jnp.float32)
+    near = [own_sums[c] + totals[c].astype(jnp.float32) for c in range(2)]
+    near = lax.optimization_barrier(arrival + jnp.concatenate(near, axis=0))
+    return last_rows(near, totals[2], totals[3])[None]
 
 
 def solution(mesh):

time: 128 us -> 136 us (1.062); the launches traced: 126 us -> 135 us
  local copies, waits for them, and re-layouts: 9.88 us -> 24.4 us
  Pallas kernels: 46.5 us -> 38.3 us
  waiting for transfers between devices: 28.1 us -> 30.8 us
  other arithmetic: 2.92 us -> 4.83 us
  starting transfers between devices: 38.2 us -> 36.6 us
    unnamed x24 -> x72, local copies, waits for them, and re-layouts: 8.01 us -> 21 us
    pallas_call x8 -> x6, Pallas kernels: 45 us -> 35.3 us  [expert_rows(): pl.pallas_call(functools.partial(mlp_kernel, parts=len(payloads), chained...]
    ppermute x30, waiting for transfers between devices: 24.5 us -> 30.8 us  [move(): return lax.ppermute(value, 'expert', pairs)]
    ppermute x2, waiting for transfers between devices: 3.64 us -> 0.01 us  [from_behind(): return lax.ppermute(value, axis, pairs)]
    convert_element_type x14, other arithmetic: 0.61 us -> 3.5 us  [relay_body(): totals[i] = move(total.astype(jnp.bfloat16), pairs)]
    ppermute x30, starting transfers between devices: 31.3 us -> 29.8 us  [move(): return lax.ppermute(value, 'expert', pairs)]
    squeeze x1 -> x2, local copies, waits for them, and re-layouts: 1.87 us -> 3.35 us  [the longest x1 1.68 us: relay_body(): second_cut = lax.optimization_barrier((previous, first_cut))[0][0, cuts[1]]]
    convert_element_type x1 -> x0, other arithmetic: 1.41 us -> none  [relay_body(): outs.append((arrival + mixed).astype(jnp.bfloat16))]
  transfers between devices with their start and end apart: 32 -> 32, of which waited for: 11 -> 9; matrix products, arithmetic and copies ran while one was open for 3% -> 7% of each run, Pallas kernels for 37% -> 28%
where the time goes in v3:
time: 136 us; the launch traced here: 135 us
  Pallas kernels  38.3 us (28%)
  starting transfers between devices  36.6 us (27%)
  waiting for transfers between devices  30.8 us (23%)
  local copies, waits for them, and re-layouts  24.4 us (18%)
  other arithmetic  4.83 us (4%)
    pallas_call x6, Pallas kernels, expert_rows(): pl.pallas_call(functools.partial(mlp_kernel, parts=len(payloads), chained...  35.3 us
    ppermute x30, waiting for transfers between devices, move(): return lax.ppermute(value, 'expert', pairs)  30.8 us
    ppermute x30, starting transfers between devices, move(): return lax.ppermute(value, 'expert', pairs)  29.8 us
    unnamed x72, local copies, waits for them, and re-layouts  21 us
    ppermute x2, starting transfers between devices, from_behind(): return lax.ppermute(value, axis, pairs)  6.87 us
    convert_element_type x14, other arithmetic, relay_body(): totals[i] = move(total.astype(jnp.bfloat16), pairs)  3.5 us
  transfers between devices with their start and end apart: 32, of which 9 were waited for; matrix products, arithmetic and copies ran while one was open for 7% of the time, Pallas kernels for 28%

profile of v3, /device:TPU:0, one launch (start us, length us, event | category | flops | bytes accessed | tf_op | source)
XLA Modules:
  0.0 135.4 jit_solution(16768530774938365771)
XLA Ops:
  0.5 1.7 %slice_bitcast_fusion.1 = bf16[64,2048]{1,0:T(8,128)(2,1)} fusion(bf16[1,128,2048]{2,1,0:T(8,128)(2,1)} %param.8), kind=kLoop, calls=%fused_computation.15 | loop fusion | bytes 524288 | tf_op jit(solution)/shard_map/squeeze | solution.py:272
  2.2 4.9 %collective-permute-start = (bf16[64,2048]{1,0:T(8,128)(2,1)}, bf16[64,2048]{1,0:T(8,128)(2,1)S(1)}, u32[]{:S(2)}, u32[]{:S(2)}) collective-permute-start(bf16[64,2048]{1,0:T(8,128)(2,1)} %slice_bitcast_fusion.1), channel_id=1, source_target_pairs={{0,16},{1,17},{2,18},{3,19},{4,20},{5,21},{6,22},{7,23},{8,24},{9,... | collective-permute-start | bytes 786440 | tf_op jit(solution)/shard_map/ppermute | solution.py:19
  7.1 1.7 %slice_bitcast_fusion = bf16[64,2048]{1,0:T(8,128)(2,1)} fusion(bf16[1,128,2048]{2,1,0:T(8,128)(2,1)} %param.8), kind=kLoop, calls=%fused_computation.14 | loop fusion | bytes 524288 | tf_op jit(solution)/shard_map/squeeze | solution.py:273
  8.7 2.0 %collective-permute-start.1 = (bf16[64,2048]{1,0:T(8,128)(2,1)}, bf16[64,2048]{1,0:T(8,128)(2,1)}, u32[]{:S(2)}, u32[]{:S(2)}) collective-permute-start(bf16[64,2048]{1,0:T(8,128)(2,1)} %slice_bitcast_fusion), channel_id=1, source_target_pairs={{0,16},{1,17},{2,18},{3,19},{4,20},{5,21},{6,22},{7,23},{8,24},{9,... | collective-permute-start | bytes 786440 | tf_op jit(solution)/shard_map/ppermute | solution.py:19
  10.7 0.8 copy.8
  11.5 0.8 copy.9
  12.3 2.8 %copy-done = bf16[1,1,2048,1536]{3,2,1,0:T(8,128)(2,1)S(1)} copy-done((bf16[1,1,2048,1536]{3,2,1,0:T(8,128)(2,1)S(1)}, bf16[1,1,2048,1536]{3,2,1,0:T(8,128)(2,1)}, u32[]{:S(2)}) %copy-start) | copy-done | bytes 6291480
  15.1 1.9 %copy-done.5 = bf16[1,1,768,2048]{3,2,1,0:T(8,128)(2,1)S(1)} copy-done((bf16[1,1,768,2048]{3,2,1,0:T(8,128)(2,1)S(1)}, bf16[1,1,768,2048]{3,2,1,0:T(8,128)(2,1)}, u32[]{:S(2)}) %copy-start.5) | copy-done | bytes 3145752
  17.0 1.0 copy-done.16
  18.0 0.7 copy-done.34
  18.7 0.5 base_rows.1
  19.3 1.5 %collective-permute-start.4 = (bf16[64,2176]{1,0:T(8,128)(2,1)S(1)}, bf16[64,2176]{1,0:T(8,128)(2,1)S(1)}, u32[]{:S(2)}, u32[]{:S(2)}) collective-permute-start(bf16[64,2176]{1,0:T(8,128)(2,1)S(1)} %norm_rows.2.refs_0_), channel_id=1, source_target_pairs={{2,6},{3,7},{6,10},{7,11},{10,14},{11,15},{14,12},{15,13},{12,8},{... | collective-permute-start | bytes 835592 | tf_op jit(solution)/shard_map/ppermute | solution.py:267
  20.8 1.6 %norm_rows.3.refs_1_ = bf16[64,2176]{1,0:T(8,128)(2,1)S(1)} custom-call(s32[1]{0:T(128)} %bitcast.4.section_ref, bf16[128,2176]{1,0:T(8,128)(2,1)S(1)} %get-tuple-element.50.base_ref, bf16[64,2048]{1,0:T(8,128)(2,1)} %collective-permute-done.1.arrived_ref, f32[1,2048]{1,0:T(1,128)S(1)} %get-tuple-element.51.gain_ref), custom_call_target="tpu_custom_call" | custom-call | flops 786432 | bytes 786432 | tf_op jit(solution)/shard_map/norm_rows/pallas_call | solution.py:137
  22.4 1.5 %collective-permute-start.5 = (bf16[64,2176]{1,0:T(8,128)(2,1)S(1)}, bf16[64,2176]{1,0:T(8,128)(2,1)S(1)}, u32[]{:S(2)}, u32[]{:S(2)}) collective-permute-start(bf16[64,2176]{1,0:T(8,128)(2,1)S(1)} %norm_rows.3.refs_1_), channel_id=1, source_target_pairs={{2,6},{3,7},{6,10},{7,11},{10,14},{11,15},{14,12},{15,13},{12,8},{... | collective-permute-start | bytes 835592 | tf_op jit(solution)/shard_map/ppermute | solution.py:267
  24.0 0.5 collective-permute-start.6
  25.0 7.0 %expert_rows.6 = (f32[64,2048]{1,0:T(8,128)S(1)}, f32[64,2048]{1,0:T(8,128)S(1)}, bf16[2048,1536]{1,0:T(8,128)(2,1)S(1)}) custom-call(s32[2]{0:T(128)S(1)} %pad_add_fusion.ids_ref, bf16[64,2176]{1,0:T(8,128)(2,1)S(1)} %norm_rows.2.refs_0_, bf16[64,2176]{1,0:T(8,128)(2,1)S(1)} %norm_rows.3.refs_1_, bf16[2048,1536]{1,0:T(8,128)(2,1)S(1)} %bitcast.14, ...), custom_call_target="tpu_custom_call" | custom-call | flops 2415919104 | bytes 1572864 | tf_op jit(solution)/shard_map/expert_rows/pallas_call | solution.py:200
  32.0 1.6 %collective-permute-done.6.refs_2_ = bf16[64,2176]{1,0:T(8,128)(2,1)S(1)} collective-permute-done((bf16[64,2176]{1,0:T(8,128)(2,1)S(1)}, bf16[64,2176]{1,0:T(8,128)(2,1)S(1)}, u32[]{:S(2)}, u32[]{:S(2)}) %collective-permute-start.6) | collective-permute-done | bytes 278560 | tf_op jit(solution)/shard_map/ppermute | solution.py:267
  33.6 1.6 %collective-permute-start.8 = (bf16[64,2176]{1,0:T(8,128)(2,1)S(1)}, bf16[64,2176]{1,0:T(8,128)(2,1)S(1)}, u32[]{:S(2)}, u32[]{:S(2)}) collective-permute-start(bf16[64,2176]{1,0:T(8,128)(2,1)S(1)} %collective-permute-done.4.refs_0_), channel_id=1, source_target_pairs={{2,6},{3,7},{6,10},{7,11},{10,14},{11,15},{14,12},{15,13},{12,8},{... | collective-permute-start | bytes 835592 | tf_op jit(solution)/shard_map/ppermute | solution.py:267
  35.1 2.8 %collective-permute-done.7.refs_3_ = bf16[64,2176]{1,0:T(8,128)(2,1)S(1)} collective-permute-done((bf16[64,2176]{1,0:T(8,128)(2,1)S(1)}, bf16[64,2176]{1,0:T(8,128)(2,1)S(1)}, u32[]{:S(2)}, u32[]{:S(2)}) %collective-permute-start.7) | collective-permute-done | bytes 278560 | tf_op jit(solution)/shard_map/ppermute | solution.py:267
  37.9 1.6 %collective-permute-start.9 = (bf16[64,2176]{1,0:T(8,128)(2,1)S(1)}, bf16[64,2176]{1,0:T(8,128)(2,1)S(1)}, u32[]{:S(2)}, u32[]{:S(2)}) collective-permute-start(bf16[64,2176]{1,0:T(8,128)(2,1)S(1)} %collective-permute-done.5.refs_1_), channel_id=1, source_target_pairs={{2,6},{3,7},{6,10},{7,11},{10,14},{11,15},{14,12},{15,13},{12,8},{... | collective-permute-start | bytes 835592 | tf_op jit(solution)/shard_map/ppermute | solution.py:267
  40.4 7.0 %expert_rows.7 = (f32[64,2048]{1,0:T(8,128)S(1)}, f32[64,2048]{1,0:T(8,128)S(1)}, f32[64,2048]{1,0:T(8,128)S(1)}, f32[64,2048]{1,0:T(8,128)S(1)}) custom-call(s32[2]{0:T(128)S(1)} %pad_add_fusion.ids_ref, bf16[64,2176]{1,0:T(8,128)(2,1)S(1)} %collective-permute-done.4.refs_0_, bf16[64,2176]{1,0:T(8,128)(2,1)S(1)} %collective-permute-done.5.refs_1_, ...), custom_call_target="tpu_custom_call" | custom-call | flops 4831838208 | bytes 3145728 | tf_op jit(solution)/shard_map/expert_rows/pallas_call | solution.py:200
  47.4 0.8 copy-done.20
  48.2 0.8 copy-done.22
  49.0 0.8 copy-done.28
  49.8 2.4 %collective-permute-done.11.refs_3_ = bf16[64,2176]{1,0:T(8,128)(2,1)S(1)} collective-permute-done((bf16[64,2176]{1,0:T(8,128)(2,1)S(1)}, bf16[64,2176]{1,0:T(8,128)(2,1)S(1)}, u32[]{:S(2)}, u32[]{:S(2)}) %collective-permute-start.11) | collective-permute-done | bytes 278560 | tf_op jit(solution)/shard_map/ppermute | solution.py:267
  52.2 1.6 %collective-permute-start.16 = (bf16[64,2176]{1,0:T(8,128)(2,1)S(1)}, bf16[64,2176]{1,0:T(8,128)(2,1)S(1)}, u32[]{:S(2)}, u32[]{:S(2)}) collective-permute-start(bf16[64,2176]{1,0:T(8,128)(2,1)S(1)} %collective-permute-done.9.refs_1_), channel_id=1, source_target_pairs={{2,6},{3,7},{6,10},{7,11},{10,14},{11,15},{14,12},{15,13},{12,8},{... | collective-permute-start | bytes 835592 | tf_op jit(solution)/shard_map/ppermute | solution.py:267
  54.2 1.6 %collective-permute-start.12 = (bf16[64,2176]{1,0:T(8,128)(2,1)S(1)}, bf16[64,2176]{1,0:T(8,128)(2,1)}, u32[]{:S(2)}, u32[]{:S(2)}) collective-permute-start(bf16[64,2176]{1,0:T(8,128)(2,1)S(1)} %collective-permute-done.8.refs_0_), channel_id=1, source_target_pairs={{2,6},{3,7},{6,10},{7,11},{10,14},{11,15},{14,12},{15,13},{12,8},{... | collective-permute-start | bytes 835592 | tf_op jit(solution)/shard_map/ppermute | solution.py:267
  56.3 7.0 %expert_rows.8 = (f32[64,2048]{1,0:T(8,128)S(1)}, f32[64,2048]{1,0:T(8,128)S(1)}, f32[64,2048]{1,0:T(8,128)S(1)}, f32[64,2048]{1,0:T(8,128)S(1)}) custom-call(s32[2]{0:T(128)S(1)} %pad_add_fusion.ids_ref, bf16[64,2176]{1,0:T(8,128)(2,1)S(1)} %collective-permute-done.8.refs_0_, bf16[64,2176]{1,0:T(8,128)(2,1)S(1)} %collective-permute-done.9.refs_1_, ...), custom_call_target="tpu_custom_call" | custom-call | flops 4831838208 | bytes 3145728 | tf_op jit(solution)/shard_map/expert_rows/pallas_call | solution.py:200
  63.3 0.8 copy-done.24
  64.1 0.8 copy-done.26
  64.9 0.8 copy-done.32
  65.7 1.9 %collective-permute-start.15 = (bf16[64,2176]{1,0:T(8,128)(2,1)}, bf16[64,2176]{1,0:T(8,128)(2,1)}, u32[]{:S(2)}, u32[]{:S(2)}) collective-permute-start(bf16[64,2176]{1,0:T(8,128)(2,1)} %collective-permute-done.12.refs_0_), channel_id=1, source_target_pairs={{2,6},{3,7},{6,10},{7,11},{10,14},{11,15},{14,12},{15,13},{12,8},{... | collective-permute-start | bytes 835592 | tf_op jit(solution)/shard_map/ppermute | solution.py:267
  67.6 4.7 %expert_rows.9 = (f32[64,2048]{1,0:T(8,128)S(1)}, f32[64,2048]{1,0:T(8,128)S(1)}) custom-call(s32[2]{0:T(128)S(1)} %pad_add_fusion.ids_ref, bf16[64,2176]{1,0:T(8,128)(2,1)} %collective-permute-done.12.refs_0_, bf16[64,2176]{1,0:T(8,128)(2,1)S(1)} %collective-permute-done.13.refs_1_, bf16[2048,1536]{1,0:T(8,128)(2,1)S(1)} %bitcast.17, ...), custom_call_target="tpu_custom_call" | custom-call | flops 2415919104 | bytes 1572864 | tf_op jit(solution)/shard_map/expert_rows/pallas_call | solution.py:200
  72.3 0.8 copy-done.30
  73.5 4.7 %expert_rows.10 = (f32[64,2048]{1,0:T(8,128)S(1)}, f32[64,2048]{1,0:T(8,128)S(1)}) custom-call(s32[2]{0:T(128)S(1)} %pad_add_fusion.ids_ref, bf16[64,2176]{1,0:T(8,128)(2,1)S(1)} %collective-permute-done.16.refs_0_, bf16[64,2176]{1,0:T(8,128)(2,1)} %collective-permute-done.17.refs_1_, bf16[2048,1536]{1,0:T(8,128)(2,1)S(1)} %bitcast.18, ...), custom_call_target="tpu_custom_call" | custom-call | flops 2415919104 | bytes 1572864 | tf_op jit(solution)/shard_map/expert_rows/pallas_call | solution.py:200
  78.3 0.8 copy-done.11
  79.1 0.7 convert_element_type.88
  79.8 1.6 %collective-permute-start.21 = (bf16[64,2048]{1,0:T(8,128)(2,1)}, bf16[64,2048]{1,0:T(8,128)(2,1)}, u32[]{:S(2)}, u32[]{:S(2)}) collective-permute-start(bf16[64,2048]{1,0:T(8,128)(2,1)} %convert_element_type.88), channel_id=1, source_target_pairs={{2,6},{3,7},{6,10},{7,11},{10,14},{11,15},{14,12},{15,13},{12,8},{... | collective-permute-start | bytes 786440 | tf_op jit(solution)/shard_map/ppermute | solution.py:267
  81.5 1.1 convert_element_type.82
  83.0 2.8 %copy-done.2 = bf16[1,1,2048,1536]{3,2,1,0:T(8,128)(2,1)S(1)} copy-done((bf16[1,1,2048,1536]{3,2,1,0:T(8,128)(2,1)S(1)}, bf16[1,1,2048,1536]{3,2,1,0:T(8,128)(2,1)}, u32[]{:S(2)}) %copy-start.2) | copy-done | bytes 6291480
  85.8 2.8 %copy-done.4 = bf16[2048,1536]{1,0:T(8,128)(2,1)S(1)} copy-done((bf16[2048,1536]{1,0:T(8,128)(2,1)S(1)}, bf16[2048,1536]{1,0:T(8,128)(2,1)}, u32[]{:S(2)}) %copy-start.4) | copy-done | bytes 6291480
  88.6 1.0 copy-done.12
  89.6 5.0 %expert_rows.11 = (f32[64,2048]{1,0:T(8,128)S(1)}, f32[64,2048]{1,0:T(8,128)S(1)}) custom-call(s32[2]{0:T(128)S(1)} %pad_add_fusion.ids_ref, bf16[64,2176]{1,0:T(8,128)(2,1)} %collective-permute-done.15.refs_0_, bf16[64,2176]{1,0:T(8,128)(2,1)} %collective-permute-done.18.refs_1_, bf16[2048,1536]{1,0:T(8,128)(2,1)S(1)} %bitcast.19, ...), custom_call_target="tpu_custom_call" | custom-call | flops 2415919104 | bytes 1572864 | tf_op jit(solution)/shard_map/expert_rows/pallas_call | solution.py:200
  94.7 1.2 add_convert_fusion.7
  95.9 1.7 %collective-permute-start.22 = (bf16[64,2048]{1,0:T(8,128)(2,1)S(1)}, bf16[64,2048]{1,0:T(8,128)(2,1)S(1)}, u32[]{:S(2)}, u32[]{:S(2)}) collective-permute-start(bf16[64,2048]{1,0:T(8,128)(2,1)S(1)} %add_convert_fusion.7), channel_id=1, source_target_pairs={{2,6},{3,7},{6,10},{7,11},{10,14},{11,15},{14,12},{15,13},{12,8},{... | collective-permute-start | bytes 786440 | tf_op jit(solution)/shard_map/ppermute | solution.py:267
  97.6 0.5 collective-permute-start.19
  98.1 1.6 %collective-permute-start.24 = (bf16[64,2048]{1,0:T(8,128)(2,1)S(1)}, bf16[64,2048]{1,0:T(8,128)(2,1)S(1)}, u32[]{:S(2)}, u32[]{:S(2)}) collective-permute-start(bf16[64,2048]{1,0:T(8,128)(2,1)S(1)} %convert_element_type.94), channel_id=1, source_target_pairs={{2,6},{3,7},{6,10},{7,11},{10,14},{11,15},{14,12},{15,13},{12,8},{... | collective-permute-start | bytes 786440 | tf_op jit(solution)/shard_map/ppermute | solution.py:267
  99.7 0.5 collective-permute-start.28
  100.2 5.0 %collective-permute-done.22 = bf16[64,2048]{1,0:T(8,128)(2,1)S(1)} collective-permute-done((bf16[64,2048]{1,0:T(8,128)(2,1)S(1)}, bf16[64,2048]{1,0:T(8,128)(2,1)S(1)}, u32[]{:S(2)}, u32[]{:S(2)}) %collective-permute-start.22) | collective-permute-done | bytes 262176 | tf_op jit(solution)/shard_map/ppermute | solution.py:267
  105.2 1.7 %collective-permute-start.23 = (bf16[64,2048]{1,0:T(8,128)(2,1)S(1)}, bf16[64,2048]{1,0:T(8,128)(2,1)S(1)}, u32[]{:S(2)}, u32[]{:S(2)}) collective-permute-start(bf16[64,2048]{1,0:T(8,128)(2,1)S(1)} %add_convert_fusion.6), channel_id=1, source_target_pairs={{2,6},{3,7},{6,10},{7,11},{10,14},{11,15},{14,12},{15,13},{12,8},{... | collective-permute-start | bytes 786440 | tf_op jit(solution)/shard_map/ppermute | solution.py:267
  107.0 0.5 collective-permute-start.20
  107.5 3.0 %collective-permute-done.24 = bf16[64,2048]{1,0:T(8,128)(2,1)S(1)} collective-permute-done((bf16[64,2048]{1,0:T(8,128)(2,1)S(1)}, bf16[64,2048]{1,0:T(8,128)(2,1)S(1)}, u32[]{:S(2)}, u32[]{:S(2)}) %collective-permute-start.24) | collective-permute-done | bytes 262176 | tf_op jit(solution)/shard_map/ppermute | solution.py:267
  110.5 1.6 %collective-permute-start.25 = (bf16[64,2048]{1,0:T(8,128)(2,1)S(1)}, bf16[64,2048]{1,0:T(8,128)(2,1)S(1)}, u32[]{:S(2)}, u32[]{:S(2)}) collective-permute-start(bf16[64,2048]{1,0:T(8,128)(2,1)S(1)} %add_convert_fusion.5), channel_id=1, source_target_pairs={{2,6},{3,7},{6,10},{7,11},{10,14},{11,15},{14,12},{15,13},{12,8},{... | collective-permute-start | bytes 786440 | tf_op jit(solution)/shard_map/ppermute | solution.py:267
  112.2 0.5 collective-permute-start.29
  112.7 6.2 %collective-permute-done.25 = bf16[64,2048]{1,0:T(8,128)(2,1)S(1)} collective-permute-done((bf16[64,2048]{1,0:T(8,128)(2,1)S(1)}, bf16[64,2048]{1,0:T(8,128)(2,1)S(1)}, u32[]{:S(2)}, u32[]{:S(2)}) %collective-permute-start.25) | collective-permute-done | bytes 262176 | tf_op jit(solution)/shard_map/ppermute | solution.py:267
  118.9 1.6 %collective-permute-start.26 = (bf16[64,2048]{1,0:T(8,128)(2,1)S(1)}, bf16[64,2048]{1,0:T(8,128)(2,1)S(1)}, u32[]{:S(2)}, u32[]{:S(2)}) collective-permute-start(bf16[64,2048]{1,0:T(8,128)(2,1)S(1)} %add_convert_fusion.4), channel_id=1, source_target_pairs={{2,6},{3,7},{6,10},{7,11},{10,14},{11,15},{14,12},{15,13},{12,8},{... | collective-permute-start | bytes 786440 | tf_op jit(solution)/shard_map/ppermute | solution.py:267
  120.6 0.5 collective-permute-start.30
  121.2 5.1 %collective-permute-done.26 = bf16[64,2048]{1,0:T(8,128)(2,1)S(1)} collective-permute-done((bf16[64,2048]{1,0:T(8,128)(2,1)S(1)}, bf16[64,2048]{1,0:T(8,128)(2,1)S(1)}, u32[]{:S(2)}, u32[]{:S(2)}) %collective-permute-start.26) | collective-permute-done | bytes 262176 | tf_op jit(solution)/shard_map/ppermute | solution.py:267
  126.4 1.6 %collective-permute-start.27 = (bf16[64,2048]{1,0:T(8,128)(2,1)S(1)}, bf16[64,2048]{1,0:T(8,128)(2,1)S(1)}, u32[]{:S(2)}, u32[]{:S(2)}) collective-permute-start(bf16[64,2048]{1,0:T(8,128)(2,1)S(1)} %add_convert_fusion.3), channel_id=1, source_target_pairs={{2,6},{3,7},{6,10},{7,11},{10,14},{11,15},{14,12},{15,13},{12,8},{... | collective-permute-start | bytes 786440 | tf_op jit(solution)/shard_map/ppermute | solution.py:267
  128.1 0.5 collective-permute-start.31
  128.6 1.1 maximum_add_fusion.base_ref
  129.8 3.1 %collective-permute-done.27.first_ref = bf16[64,2048]{1,0:T(8,128)(2,1)S(1)} collective-permute-done((bf16[64,2048]{1,0:T(8,128)(2,1)S(1)}, bf16[64,2048]{1,0:T(8,128)(2,1)S(1)}, u32[]{:S(2)}, u32[]{:S(2)}) %collective-permute-start.27) | collective-permute-done | bytes 262176 | tf_op jit(solution)/shard_map/ppermute | solution.py:267
  132.9 1.7 %collective-permute-done.31.second_ref = bf16[64,2048]{1,0:T(8,128)(2,1)S(1)} collective-permute-done((bf16[64,2048]{1,0:T(8,128)(2,1)S(1)}, bf16[64,2048]{1,0:T(8,128)(2,1)S(1)}, u32[]{:S(2)}, u32[]{:S(2)}) %collective-permute-start.31) | collective-permute-done | bytes 262176 | tf_op jit(solution)/shard_map/ppermute | solution.py:267
  134.5 0.9 last_rows.1
  (102 shorter events, 4.4 us)
Async XLA Ops:
  0.0 25.0 %collective-permute-start.2 = (bf16[2048,1536]{1,0:T(8,128)(2,1)}, bf16[2048,1536]{1,0:T(8,128)(2,1)}, u32[]{:S(2)}, u32[]{:S(2)}) collective-permute-start(bf16[2048,1536]{1,0:T(8,128)(2,1)} %bitcast.12), channel_id=1, source_target_pairs={{0,1},{1,0},{2,3},{3,2},{4,5},{5,4},{6,7},{7,6},{8,9},{9,8},{10,11... | collective-permute-start | bytes 18874376 | tf_op jit(solution)/shard_map/ppermute | solution.py:267
  0.5 24.1 %collective-permute-start.3 = (bf16[768,2048]{1,0:T(8,128)(2,1)}, bf16[768,2048]{1,0:T(8,128)(2,1)}, u32[]{:S(2)}, u32[]{:S(2)}) collective-permute-start(bf16[768,2048]{1,0:T(8,128)(2,1)} %bitcast.20), channel_id=1, source_target_pairs={{0,1},{1,0},{2,3},{3,2},{4,5},{5,4},{6,7},{7,6},{8,9},{9,8},{10,11... | collective-permute-start | bytes 9437192 | tf_op jit(solution)/shard_map/ppermute | solution.py:267
  2.2 17.1 %collective-permute-start = (bf16[64,2048]{1,0:T(8,128)(2,1)}, bf16[64,2048]{1,0:T(8,128)(2,1)S(1)}, u32[]{:S(2)}, u32[]{:S(2)}) collective-permute-start(bf16[64,2048]{1,0:T(8,128)(2,1)} %slice_bitcast_fusion.1), channel_id=1, source_target_pairs={{0,16},{1,17},{2,18},{3,19},{4,20},{5,21},{6,22},{7,23},{8,24},{9,... | collective-permute-start | bytes 786440 | tf_op jit(solution)/shard_map/ppermute | solution.py:19
  8.7 12.1 %collective-permute-start.1 = (bf16[64,2048]{1,0:T(8,128)(2,1)}, bf16[64,2048]{1,0:T(8,128)(2,1)}, u32[]{:S(2)}, u32[]{:S(2)}) collective-permute-start(bf16[64,2048]{1,0:T(8,128)(2,1)} %slice_bitcast_fusion), channel_id=1, source_target_pairs={{0,16},{1,17},{2,18},{3,19},{4,20},{5,21},{6,22},{7,23},{8,24},{9,... | collective-permute-start | bytes 786440 | tf_op jit(solution)/shard_map/ppermute | solution.py:19
  12.3 2.8 %copy-start = (bf16[1,1,2048,1536]{3,2,1,0:T(8,128)(2,1)S(1)}, bf16[1,1,2048,1536]{3,2,1,0:T(8,128)(2,1)}, u32[]{:S(2)}) copy-start(bf16[1,1,2048,1536]{3,2,1,0:T(8,128)(2,1)} %param.12) | copy-start | bytes 18874372
  15.1 1.9 %copy-start.5 = (bf16[1,1,768,2048]{3,2,1,0:T(8,128)(2,1)S(1)}, bf16[1,1,768,2048]{3,2,1,0:T(8,128)(2,1)}, u32[]{:S(2)}) copy-start(bf16[1,1,768,2048]{3,2,1,0:T(8,128)(2,1)} %param.13) | copy-start | bytes 9437188
  17.0 1.0 copy-start.16
  18.7 6.2 %copy-start.1 = (bf16[1,1,2048,1536]{3,2,1,0:T(8,128)(2,1)S(1)}, bf16[1,1,2048,1536]{3,2,1,0:T(8,128)(2,1)}, u32[]{:S(2)}) copy-start(bf16[1,1,2048,1536]{3,2,1,0:T(8,128)(2,1)} %param.12) | copy-start | bytes 18874372
  18.7 6.2 %copy-start.6 = (bf16[1,1,768,2048]{3,2,1,0:T(8,128)(2,1)S(1)}, bf16[1,1,768,2048]{3,2,1,0:T(8,128)(2,1)}, u32[]{:S(2)}) copy-start(bf16[1,1,768,2048]{3,2,1,0:T(8,128)(2,1)} %param.13) | copy-start | bytes 9437188
  19.3 12.7 %collective-permute-start.4 = (bf16[64,2176]{1,0:T(8,128)(2,1)S(1)}, bf16[64,2176]{1,0:T(8,128)(2,1)S(1)}, u32[]{:S(2)}, u32[]{:S(2)}) collective-permute-start(bf16[64,2176]{1,0:T(8,128)(2,1)S(1)} %norm_rows.2.refs_0_), channel_id=1, source_target_pairs={{2,6},{3,7},{6,10},{7,11},{10,14},{11,15},{14,12},{15,13},{12,8},{... | collective-permute-start | bytes 835592 | tf_op jit(solution)/shard_map/ppermute | solution.py:267
  22.4 12.7 %collective-permute-start.5 = (bf16[64,2176]{1,0:T(8,128)(2,1)S(1)}, bf16[64,2176]{1,0:T(8,128)(2,1)S(1)}, u32[]{:S(2)}, u32[]{:S(2)}) collective-permute-start(bf16[64,2176]{1,0:T(8,128)(2,1)S(1)} %norm_rows.3.refs_1_), channel_id=1, source_target_pairs={{2,6},{3,7},{6,10},{7,11},{10,14},{11,15},{14,12},{15,13},{12,8},{... | collective-permute-start | bytes 835592 | tf_op jit(solution)/shard_map/ppermute | solution.py:267
  24.0 9.6 %collective-permute-start.6 = (bf16[64,2176]{1,0:T(8,128)(2,1)S(1)}, bf16[64,2176]{1,0:T(8,128)(2,1)S(1)}, u32[]{:S(2)}, u32[]{:S(2)}) collective-permute-start(bf16[64,2176]{1,0:T(8,128)(2,1)S(1)} %norm_rows.2.refs_0_), channel_id=1, source_target_pairs={{6,2},{7,3},{10,6},{11,7},{14,10},{15,11},{12,14},{13,15},{8,12},{... | collective-permute-start | bytes 835592 | tf_op jit(solution)/shard_map/ppermute | solution.py:267
  24.5 13.4 %collective-permute-start.7 = (bf16[64,2176]{1,0:T(8,128)(2,1)S(1)}, bf16[64,2176]{1,0:T(8,128)(2,1)S(1)}, u32[]{:S(2)}, u32[]{:S(2)}) collective-permute-start(bf16[64,2176]{1,0:T(8,128)(2,1)S(1)} %norm_rows.3.refs_1_), channel_id=1, source_target_pairs={{6,2},{7,3},{10,6},{11,7},{14,10},{15,11},{12,14},{13,15},{8,12},{... | collective-permute-start | bytes 835592 | tf_op jit(solution)/shard_map/ppermute | solution.py:267
  31.9 15.4 %copy-start.7 = (f32[64,2048]{1,0:T(8,128)}, f32[64,2048]{1,0:T(8,128)S(1)}, u32[]{:S(2)}) copy-start(f32[64,2048]{1,0:T(8,128)S(1)} %get-tuple-element.52.refs_8_) | copy-start | bytes 1572868
  32.0 15.4 %copy-start.18 = (f32[64,2048]{1,0:T(8,128)}, f32[64,2048]{1,0:T(8,128)S(1)}, u32[]{:S(2)}) copy-start(f32[64,2048]{1,0:T(8,128)S(1)} %get-tuple-element.75) | copy-start | bytes 1572868
  32.0 41.6 %copy-start.3 = (bf16[2048,1536]{1,0:T(8,128)(2,1)}, bf16[2048,1536]{1,0:T(8,128)(2,1)S(1)}, u32[]{:S(2)}) copy-start(bf16[2048,1536]{1,0:T(8,128)(2,1)S(1)} %get-tuple-element.57.refs_6_.refs_4_) | copy-start | bytes 18874372
  33.6 16.2 %collective-permute-start.8 = (bf16[64,2176]{1,0:T(8,128)(2,1)S(1)}, bf16[64,2176]{1,0:T(8,128)(2,1)S(1)}, u32[]{:S(2)}, u32[]{:S(2)}) collective-permute-start(bf16[64,2176]{1,0:T(8,128)(2,1)S(1)} %collective-permute-done.4.refs_0_), channel_id=1, source_target_pairs={{2,6},{3,7},{6,10},{7,11},{10,14},{11,15},{14,12},{15,13},{12,8},{... | collective-permute-start | bytes 835592 | tf_op jit(solution)/shard_map/ppermute | solution.py:267
  37.9 11.9 %collective-permute-start.9 = (bf16[64,2176]{1,0:T(8,128)(2,1)S(1)}, bf16[64,2176]{1,0:T(8,128)(2,1)S(1)}, u32[]{:S(2)}, u32[]{:S(2)}) collective-permute-start(bf16[64,2176]{1,0:T(8,128)(2,1)S(1)} %collective-permute-done.5.refs_1_), channel_id=1, source_target_pairs={{2,6},{3,7},{6,10},{7,11},{10,14},{11,15},{14,12},{15,13},{12,8},{... | collective-permute-start | bytes 835592 | tf_op jit(solution)/shard_map/ppermute | solution.py:267
  39.5 10.3 %collective-permute-start.10 = (bf16[64,2176]{1,0:T(8,128)(2,1)S(1)}, bf16[64,2176]{1,0:T(8,128)(2,1)S(1)}, u32[]{:S(2)}, u32[]{:S(2)}) collective-permute-start(bf16[64,2176]{1,0:T(8,128)(2,1)S(1)} %collective-permute-done.6.refs_2_), channel_id=1, source_target_pairs={{6,2},{7,3},{10,6},{11,7},{14,10},{15,11},{12,14},{13,15},{8,12},{... | collective-permute-start | bytes 835592 | tf_op jit(solution)/shard_map/ppermute | solution.py:267
  39.9 12.3 %collective-permute-start.11 = (bf16[64,2176]{1,0:T(8,128)(2,1)S(1)}, bf16[64,2176]{1,0:T(8,128)(2,1)S(1)}, u32[]{:S(2)}, u32[]{:S(2)}) collective-permute-start(bf16[64,2176]{1,0:T(8,128)(2,1)S(1)} %collective-permute-done.7.refs_3_), channel_id=1, source_target_pairs={{6,2},{7,3},{10,6},{11,7},{14,10},{15,11},{12,14},{13,15},{8,12},{... | collective-permute-start | bytes 835592 | tf_op jit(solution)/shard_map/ppermute | solution.py:267
  48.2 0.8 copy-start.22
  49.0 0.8 copy-start.28
  49.8 13.5 %copy-start.9 = (f32[64,2048]{1,0:T(8,128)}, f32[64,2048]{1,0:T(8,128)S(1)}, u32[]{:S(2)}) copy-start(f32[64,2048]{1,0:T(8,128)S(1)} %get-tuple-element.58.refs_8_) | copy-start | bytes 1572868
  52.2 20.9 %collective-permute-start.16 = (bf16[64,2176]{1,0:T(8,128)(2,1)S(1)}, bf16[64,2176]{1,0:T(8,128)(2,1)S(1)}, u32[]{:S(2)}, u32[]{:S(2)}) collective-permute-start(bf16[64,2176]{1,0:T(8,128)(2,1)S(1)} %collective-permute-done.9.refs_1_), channel_id=1, source_target_pairs={{2,6},{3,7},{6,10},{7,11},{10,14},{11,15},{14,12},{15,13},{12,8},{... | collective-permute-start | bytes 835592 | tf_op jit(solution)/shard_map/ppermute | solution.py:267
  53.8 19.2 %collective-permute-start.17 = (bf16[64,2176]{1,0:T(8,128)(2,1)S(1)}, bf16[64,2176]{1,0:T(8,128)(2,1)}, u32[]{:S(2)}, u32[]{:S(2)}) collective-permute-start(bf16[64,2176]{1,0:T(8,128)(2,1)S(1)} %collective-permute-done.11.refs_3_), channel_id=1, source_target_pairs={{6,2},{7,3},{10,6},{11,7},{14,10},{15,11},{12,14},{13,15},{8,12},{... | collective-permute-start | bytes 835592 | tf_op jit(solution)/shard_map/ppermute | solution.py:267
  54.2 11.4 %collective-permute-start.12 = (bf16[64,2176]{1,0:T(8,128)(2,1)S(1)}, bf16[64,2176]{1,0:T(8,128)(2,1)}, u32[]{:S(2)}, u32[]{:S(2)}) collective-permute-start(bf16[64,2176]{1,0:T(8,128)(2,1)S(1)} %collective-permute-done.8.refs_0_), channel_id=1, source_target_pairs={{2,6},{3,7},{6,10},{7,11},{10,14},{11,15},{14,12},{15,13},{12,8},{... | collective-permute-start | bytes 835592 | tf_op jit(solution)/shard_map/ppermute | solution.py:267
  55.9 9.8 %collective-permute-start.13 = (bf16[64,2176]{1,0:T(8,128)(2,1)S(1)}, bf16[64,2176]{1,0:T(8,128)(2,1)S(1)}, u32[]{:S(2)}, u32[]{:S(2)}) collective-permute-start(bf16[64,2176]{1,0:T(8,128)(2,1)S(1)} %collective-permute-done.10.refs_2_), channel_id=1, source_target_pairs={{6,2},{7,3},{10,6},{11,7},{14,10},{15,11},{12,14},{13,15},{8,12},{... | collective-permute-start | bytes 835592 | tf_op jit(solution)/shard_map/ppermute | solution.py:267
  63.3 0.8 copy-start.24
  64.1 0.8 copy-start.26
  64.9 0.8 copy-start.32
  65.7 6.6 %copy-start.13 = (f32[64,2048]{1,0:T(8,128)}, f32[64,2048]{1,0:T(8,128)S(1)}, u32[]{:S(2)}) copy-start(f32[64,2048]{1,0:T(8,128)S(1)} %get-tuple-element.63.refs_6_) | copy-start | bytes 1572868
  65.7 17.3 %collective-permute-start.15 = (bf16[64,2176]{1,0:T(8,128)(2,1)}, bf16[64,2176]{1,0:T(8,128)(2,1)}, u32[]{:S(2)}, u32[]{:S(2)}) collective-permute-start(bf16[64,2176]{1,0:T(8,128)(2,1)} %collective-permute-done.12.refs_0_), channel_id=1, source_target_pairs={{2,6},{3,7},{6,10},{7,11},{10,14},{11,15},{14,12},{15,13},{12,8},{... | collective-permute-start | bytes 835592 | tf_op jit(solution)/shard_map/ppermute | solution.py:267
  73.1 5.2 %copy-start.15 = (f32[64,2048]{1,0:T(8,128)}, f32[64,2048]{1,0:T(8,128)S(1)}, u32[]{:S(2)}) copy-start(f32[64,2048]{1,0:T(8,128)S(1)} %get-tuple-element.66.refs_6_) | copy-start | bytes 1572868
  73.1 9.9 %collective-permute-start.18 = (bf16[64,2176]{1,0:T(8,128)(2,1)}, bf16[64,2176]{1,0:T(8,128)(2,1)}, u32[]{:S(2)}, u32[]{:S(2)}) collective-permute-start(bf16[64,2176]{1,0:T(8,128)(2,1)} %collective-permute-done.17.refs_1_), channel_id=1, source_target_pairs={{6,2},{7,3},{10,6},{11,7},{14,10},{15,11},{12,14},{13,15},{8,12},{... | collective-permute-start | bytes 835592 | tf_op jit(solution)/shard_map/ppermute | solution.py:267
  78.3 0.8 copy-start.11
  79.8 14.8 %collective-permute-start.21 = (bf16[64,2048]{1,0:T(8,128)(2,1)}, bf16[64,2048]{1,0:T(8,128)(2,1)}, u32[]{:S(2)}, u32[]{:S(2)}) collective-permute-start(bf16[64,2048]{1,0:T(8,128)(2,1)} %convert_element_type.88), channel_id=1, source_target_pairs={{2,6},{3,7},{6,10},{7,11},{10,14},{11,15},{14,12},{15,13},{12,8},{... | collective-permute-start | bytes 786440 | tf_op jit(solution)/shard_map/ppermute | solution.py:267
  82.5 15.0 %collective-permute-start.14 = (bf16[64,2048]{1,0:T(8,128)(2,1)S(1)}, bf16[64,2048]{1,0:T(8,128)(2,1)S(1)}, u32[]{:S(2)}, u32[]{:S(2)}) collective-permute-start(bf16[64,2048]{1,0:T(8,128)(2,1)S(1)} %convert_element_type.82), channel_id=1, source_target_pairs={{6,2},{7,3},{10,6},{11,7},{14,10},{15,11},{12,14},{13,15},{8,12},{... | collective-permute-start | bytes 786440 | tf_op jit(solution)/shard_map/ppermute | solution.py:267
  83.0 2.8 %copy-start.2 = (bf16[1,1,2048,1536]{3,2,1,0:T(8,128)(2,1)S(1)}, bf16[1,1,2048,1536]{3,2,1,0:T(8,128)(2,1)}, u32[]{:S(2)}) copy-start(bf16[1,1,2048,1536]{3,2,1,0:T(8,128)(2,1)} %param.12) | copy-start | bytes 18874372
  85.8 2.8 %copy-start.4 = (bf16[2048,1536]{1,0:T(8,128)(2,1)S(1)}, bf16[2048,1536]{1,0:T(8,128)(2,1)}, u32[]{:S(2)}) copy-start(bf16[2048,1536]{1,0:T(8,128)(2,1)} %copy-done.3) | copy-start | bytes 18874372
  88.6 1.0 copy-start.12
  89.6 5.1 %copy-start.33 = (f32[64,2048]{1,0:T(8,128)S(1)}, f32[64,2048]{1,0:T(8,128)}, u32[]{:S(2)}) copy-start(f32[64,2048]{1,0:T(8,128)} %copy-done.32) | copy-start | bytes 1572868
  89.6 8.0 %copy-start.14 = (f32[64,2048]{1,0:T(8,128)S(1)}, f32[64,2048]{1,0:T(8,128)}, u32[]{:S(2)}) copy-start(f32[64,2048]{1,0:T(8,128)} %copy-done.13) | copy-start | bytes 1572868
  89.6 15.6 %copy-start.29 = (f32[64,2048]{1,0:T(8,128)S(1)}, f32[64,2048]{1,0:T(8,128)}, u32[]{:S(2)}) copy-start(f32[64,2048]{1,0:T(8,128)} %copy-done.28) | copy-start | bytes 1572868
  89.6 17.3 %copy-start.10 = (f32[64,2048]{1,0:T(8,128)S(1)}, f32[64,2048]{1,0:T(8,128)}, u32[]{:S(2)}) copy-start(f32[64,2048]{1,0:T(8,128)} %copy-done.9) | copy-start | bytes 1572868
  89.6 20.8 %copy-start.31 = (f32[64,2048]{1,0:T(8,128)S(1)}, f32[64,2048]{1,0:T(8,128)}, u32[]{:S(2)}) copy-start(f32[64,2048]{1,0:T(8,128)} %copy-done.30) | copy-start | bytes 1572868
  94.6 24.3 %copy-start.27 = (f32[64,2048]{1,0:T(8,128)S(1)}, f32[64,2048]{1,0:T(8,128)}, u32[]{:S(2)}) copy-start(f32[64,2048]{1,0:T(8,128)} %copy-done.26) | copy-start | bytes 1572868
  94.6 25.9 %copy-start.25 = (f32[64,2048]{1,0:T(8,128)S(1)}, f32[64,2048]{1,0:T(8,128)}, u32[]{:S(2)}) copy-start(f32[64,2048]{1,0:T(8,128)} %copy-done.24) | copy-start | bytes 1572868
  94.6 26.5 %copy-start.8 = (f32[64,2048]{1,0:T(8,128)S(1)}, f32[64,2048]{1,0:T(8,128)}, u32[]{:S(2)}) copy-start(f32[64,2048]{1,0:T(8,128)} %copy-done.7) | copy-start | bytes 1572868
  94.6 26.5 %copy-start.19 = (f32[64,2048]{1,0:T(8,128)S(1)}, f32[64,2048]{1,0:T(8,128)}, u32[]{:S(2)}) copy-start(f32[64,2048]{1,0:T(8,128)} %copy-done.18) | copy-start | bytes 1572868
  94.6 31.7 %copy-start.23 = (f32[64,2048]{1,0:T(8,128)S(1)}, f32[64,2048]{1,0:T(8,128)}, u32[]{:S(2)}) copy-start(f32[64,2048]{1,0:T(8,128)} %copy-done.22) | copy-start | bytes 1572868
  94.7 33.4 %copy-start.21 = (f32[64,2048]{1,0:T(8,128)S(1)}, f32[64,2048]{1,0:T(8,128)}, u32[]{:S(2)}) copy-start(f32[64,2048]{1,0:T(8,128)} %copy-done.20) | copy-start | bytes 1572868
  95.9 32.7 %copy-start.17 = (bf16[128,2048]{1,0:T(8,128)(2,1)S(1)}, bf16[128,2048]{1,0:T(8,128)(2,1)}, u32[]{:S(2)}) copy-start(bf16[128,2048]{1,0:T(8,128)(2,1)} %fresh_ref.1) | copy-start | bytes 1572868
  95.9 9.3 %collective-permute-start.22 = (bf16[64,2048]{1,0:T(8,128)(2,1)S(1)}, bf16[64,2048]{1,0:T(8,128)(2,1)S(1)}, u32[]{:S(2)}, u32[]{:S(2)}) collective-permute-start(bf16[64,2048]{1,0:T(8,128)(2,1)S(1)} %add_convert_fusion.7), channel_id=1, source_target_pairs={{2,6},{3,7},{6,10},{7,11},{10,14},{11,15},{14,12},{15,13},{12,8},{... | collective-permute-start | bytes 786440 | tf_op jit(solution)/shard_map/ppermute | solution.py:267
  97.6 9.3 %collective-permute-start.19 = (bf16[64,2048]{1,0:T(8,128)(2,1)S(1)}, bf16[64,2048]{1,0:T(8,128)(2,1)S(1)}, u32[]{:S(2)}, u32[]{:S(2)}) collective-permute-start(bf16[64,2048]{1,0:T(8,128)(2,1)S(1)} %add_convert_fusion.9), channel_id=1, source_target_pairs={{6,2},{7,3},{10,6},{11,7},{14,10},{15,11},{12,14},{13,15},{8,12},{... | collective-permute-start | bytes 786440 | tf_op jit(solution)/shard_map/ppermute | solution.py:267
  98.1 12.3 %collective-permute-start.24 = (bf16[64,2048]{1,0:T(8,128)(2,1)S(1)}, bf16[64,2048]{1,0:T(8,128)(2,1)S(1)}, u32[]{:S(2)}, u32[]{:S(2)}) collective-permute-start(bf16[64,2048]{1,0:T(8,128)(2,1)S(1)} %convert_element_type.94), channel_id=1, source_target_pairs={{2,6},{3,7},{6,10},{7,11},{10,14},{11,15},{14,12},{15,13},{12,8},{... | collective-permute-start | bytes 786440 | tf_op jit(solution)/shard_map/ppermute | solution.py:267
  99.7 12.4 %collective-permute-start.28 = (bf16[64,2048]{1,0:T(8,128)(2,1)S(1)}, bf16[64,2048]{1,0:T(8,128)(2,1)S(1)}, u32[]{:S(2)}, u32[]{:S(2)}) collective-permute-start(bf16[64,2048]{1,0:T(8,128)(2,1)S(1)} %convert_element_type.101), channel_id=1, source_target_pairs={{6,2},{7,3},{10,6},{11,7},{14,10},{15,11},{12,14},{13,15},{8,12},{... | collective-permute-start | bytes 786440 | tf_op jit(solution)/shard_map/ppermute | solution.py:267
  105.2 15.9 %collective-permute-start.23 = (bf16[64,2048]{1,0:T(8,128)(2,1)S(1)}, bf16[64,2048]{1,0:T(8,128)(2,1)S(1)}, u32[]{:S(2)}, u32[]{:S(2)}) collective-permute-start(bf16[64,2048]{1,0:T(8,128)(2,1)S(1)} %add_convert_fusion.6), channel_id=1, source_target_pairs={{2,6},{3,7},{6,10},{7,11},{10,14},{11,15},{14,12},{15,13},{12,8},{... | collective-permute-start | bytes 786440 | tf_op jit(solution)/shard_map/ppermute | solution.py:267
  107.0 14.1 %collective-permute-start.20 = (bf16[64,2048]{1,0:T(8,128)(2,1)S(1)}, bf16[64,2048]{1,0:T(8,128)(2,1)S(1)}, u32[]{:S(2)}, u32[]{:S(2)}) collective-permute-start(bf16[64,2048]{1,0:T(8,128)(2,1)S(1)} %add_convert_fusion.8), channel_id=1, source_target_pairs={{6,2},{7,3},{10,6},{11,7},{14,10},{15,11},{12,14},{13,15},{8,12},{... | collective-permute-start | bytes 786440 | tf_op jit(solution)/shard_map/ppermute | solution.py:267
  110.5 8.4 %collective-permute-start.25 = (bf16[64,2048]{1,0:T(8,128)(2,1)S(1)}, bf16[64,2048]{1,0:T(8,128)(2,1)S(1)}, u32[]{:S(2)}, u32[]{:S(2)}) collective-permute-start(bf16[64,2048]{1,0:T(8,128)(2,1)S(1)} %add_convert_fusion.5), channel_id=1, source_target_pairs={{2,6},{3,7},{6,10},{7,11},{10,14},{11,15},{14,12},{15,13},{12,8},{... | collective-permute-start | bytes 786440 | tf_op jit(solution)/shard_map/ppermute | solution.py:267
  112.2 8.4 %collective-permute-start.29 = (bf16[64,2048]{1,0:T(8,128)(2,1)S(1)}, bf16[64,2048]{1,0:T(8,128)(2,1)S(1)}, u32[]{:S(2)}, u32[]{:S(2)}) collective-permute-start(bf16[64,2048]{1,0:T(8,128)(2,1)S(1)} %add_convert_fusion.2), channel_id=1, source_target_pairs={{6,2},{7,3},{10,6},{11,7},{14,10},{15,11},{12,14},{13,15},{8,12},{... | collective-permute-start | bytes 786440 | tf_op jit(solution)/shard_map/ppermute | solution.py:267
  118.9 7.5 %collective-permute-start.26 = (bf16[64,2048]{1,0:T(8,128)(2,1)S(1)}, bf16[64,2048]{1,0:T(8,128)(2,1)S(1)}, u32[]{:S(2)}, u32[]{:S(2)}) collective-permute-start(bf16[64,2048]{1,0:T(8,128)(2,1)S(1)} %add_convert_fusion.4), channel_id=1, source_target_pairs={{2,6},{3,7},{6,10},{7,11},{10,14},{11,15},{14,12},{15,13},{12,8},{... | collective-permute-start | bytes 786440 | tf_op jit(solution)/shard_map/ppermute | solution.py:267
  120.6 7.5 %collective-permute-start.30 = (bf16[64,2048]{1,0:T(8,128)(2,1)S(1)}, bf16[64,2048]{1,0:T(8,128)(2,1)S(1)}, u32[]{:S(2)}, u32[]{:S(2)}) collective-permute-start(bf16[64,2048]{1,0:T(8,128)(2,1)S(1)} %add_convert_fusion.1), channel_id=1, source_target_pairs={{6,2},{7,3},{10,6},{11,7},{14,10},{15,11},{12,14},{13,15},{8,12},{... | collective-permute-start | bytes 786440 | tf_op jit(solution)/shard_map/ppermute | solution.py:267
  126.4 6.4 %collective-permute-start.27 = (bf16[64,2048]{1,0:T(8,128)(2,1)S(1)}, bf16[64,2048]{1,0:T(8,128)(2,1)S(1)}, u32[]{:S(2)}, u32[]{:S(2)}) collective-permute-start(bf16[64,2048]{1,0:T(8,128)(2,1)S(1)} %add_convert_fusion.3), channel_id=1, source_target_pairs={{2,6},{3,7},{6,10},{7,11},{10,14},{11,15},{14,12},{15,13},{12,8},{... | collective-permute-start | bytes 786440 | tf_op jit(solution)/shard_map/ppermute | solution.py:267
  128.1 6.4 %collective-permute-start.31 = (bf16[64,2048]{1,0:T(8,128)(2,1)S(1)}, bf16[64,2048]{1,0:T(8,128)(2,1)S(1)}, u32[]{:S(2)}, u32[]{:S(2)}) collective-permute-start(bf16[64,2048]{1,0:T(8,128)(2,1)S(1)} %add_convert_fusion), channel_id=1, source_target_pairs={{6,2},{7,3},{10,6},{11,7},{14,10},{15,11},{12,14},{13,15},{8,12},{... | collective-permute-start | bytes 786440 | tf_op jit(solution)/shard_map/ppermute | solution.py:267
  (3 other events, 2.3 us)

commit v4 on v3

--- a/solution.py
+++ b/solution.py
@@ -11,6 +11,7 @@
 LANES = 128
 CORES = 2
 MIB = 1 << 20
+HOLD = False
 
 
 def from_behind(value, axis, by):
@@ -72,80 +73,84 @@
     return (wide_input + mixed).astype(jnp.bfloat16)[None]
 
 
-def base_kernel(fresh_ref, gain_ref, routes_ref, gates_ref, gate_up_ref, down_ref, rows_ref, gain_out_ref, *, experts):
-    del gate_up_ref, down_ref
+def normed_rows(rows, gain):
+    wide = rows.astype(jnp.float32)
+    scale = lax.rsqrt(jnp.mean(wide * wide, axis=-1, keepdims=True) + epsilon)
+    return (wide * scale * gain).astype(jnp.bfloat16)
+
+
+def base_kernel(fresh_ref, gain_ref, routes_ref, gates_ref, rows_ref, fresh_out_ref, gain_out_ref, *, experts):
     width = fresh_ref.shape[1]
     rows = fresh_ref.shape[0]
     rows_ref[:, :width] = normed_rows(fresh_ref[...], gain_ref[...])
-    lane = lax.broadcasted_iota(jnp.int32, (rows, LANES), 1)
-    expert = lane % experts
-    term = lane // experts
-    weight = jnp.zeros((rows, LANES), jnp.float32)
-    for k in range(routes_ref.shape[1]):
-        weight += jnp.where(routes_ref[:, k : k + 1] == expert, gates_ref[:, k : k + 1], 0.0)
+    line = lax.broadcasted_iota(jnp.int32, (LANES, rows), 0)
+    expert = line % experts
+    term = line // experts
+    weight = jnp.zeros((LANES, rows), jnp.float32)
+    for k in range(routes_ref.shape[0]):
+        weight += jnp.where(routes_ref[k : k + 1, :] == expert, gates_ref[k : k + 1, :], 0.0)
     high = weight.astype(jnp.bfloat16).astype(jnp.float32)
     middle = (weight - high).astype(jnp.bfloat16).astype(jnp.float32)
     low = weight - high - middle
     terms = jnp.where(term == 0, high, jnp.where(term == 1, middle, jnp.where(term == 2, low, 0.0)))
-    rows_ref[:, width:] = terms.astype(jnp.bfloat16)
+    rows_ref[:, width:] = terms.T.astype(jnp.bfloat16)
+    fresh_out_ref[...] = fresh_ref[...]
     gain_out_ref[...] = gain_ref[...]
 
 
-def normed_rows(rows, gain):
-    wide = rows.astype(jnp.float32)
-    scale = lax.rsqrt(jnp.mean(wide * wide, axis=-1, keepdims=True) + epsilon)
-    return (wide * scale * gain).astype(jnp.bfloat16)
-
-
-def base_rows(fresh, gain, routes, gates, weights, experts):
+def base_rows(fresh, gain, routes, gates, experts):
     rows, width = fresh.shape
     vmem = pl.BlockSpec(memory_space=pltpu.VMEM)
     return pl.pallas_call(
         functools.partial(base_kernel, experts=experts),
         out_shape=(
             jax.ShapeDtypeStruct((rows, width + LANES), jnp.bfloat16),
+            jax.ShapeDtypeStruct(fresh.shape, fresh.dtype),
             jax.ShapeDtypeStruct(gain.shape, jnp.float32),
         ),
-        in_specs=[vmem] * 6,
-        out_specs=(vmem, vmem),
-        compiler_params=pltpu.CompilerParams(vmem_limit_bytes=16 * MIB),
-        cost_estimate=pl.CostEstimate(
-            flops=rows * width * 6, bytes_accessed=weights[0].size * 6, transcendentals=rows
-        ),
+        in_specs=[vmem] * 4,
+        out_specs=(vmem,) * 3,
+        compiler_params=pltpu.CompilerParams(vmem_limit_bytes=12 * MIB),
+        cost_estimate=pl.CostEstimate(flops=rows * width * 6, bytes_accessed=rows * width * 8, transcendentals=rows),
         name="base_rows",
-    )(fresh, gain, routes, gates, *weights)
-
-
-def norm_kernel(section_ref, base_ref, arrived_ref, gain_ref, rows_ref, *, start):
+    )(fresh, gain, routes, gates)
+
+
+def norm_kernel(section_ref, base_ref, fresh_ref, arrived_ref, gain_ref, rows_ref, arrival_ref, *, start):
     rows, width = arrived_ref.shape
     here = slice(start, start + rows)
 
     @pl.when(section_ref[0] == 0)
     def _():
         rows_ref[:, :width] = base_ref[here, :width]
+        arrival_ref[...] = fresh_ref[here, :]
 
     @pl.when(section_ref[0] != 0)
     def _():
         rows_ref[:, :width] = normed_rows(arrived_ref[...], gain_ref[...])
+        arrival_ref[...] = arrived_ref[...]
 
     rows_ref[:, width:] = base_ref[here, width:]
 
 
-def norm_rows(section_id, base, arrived, gain, start):
+def norm_rows(section_id, base, fresh, arrived, gain, start):
     rows, width = arrived.shape
     vmem = pl.BlockSpec(memory_space=pltpu.VMEM)
     return pl.pallas_call(
         functools.partial(norm_kernel, start=start),
-        out_shape=jax.ShapeDtypeStruct((rows, base.shape[1]), jnp.bfloat16),
-        in_specs=[pl.BlockSpec(memory_space=pltpu.SMEM)] + [vmem] * 3,
-        out_specs=vmem,
+        out_shape=(
+            jax.ShapeDtypeStruct((rows, base.shape[1]), jnp.bfloat16),
+            jax.ShapeDtypeStruct((rows, width), jnp.bfloat16),
+        ),
+        in_specs=[pl.BlockSpec(memory_space=pltpu.SMEM)] + [vmem] * 4,
+        out_specs=(vmem, vmem),
         compiler_params=pltpu.CompilerParams(vmem_limit_bytes=12 * MIB),
-        cost_estimate=pl.CostEstimate(flops=rows * width * 6, bytes_accessed=rows * width * 6, transcendentals=rows),
+        cost_estimate=pl.CostEstimate(flops=rows * width * 6, bytes_accessed=rows * width * 8, transcendentals=rows),
         name="norm_rows",
-    )(section_id.reshape(1), base, arrived, gain)
-
-
-def mlp_kernel(ids_ref, *refs, parts, chained, held, experts):
+    )(section_id, base, fresh, arrived, gain)
+
+
+def mlp_kernel(expert_ref, *refs, parts, chained, held, experts):
     payloads = refs[:parts]
     own, other = refs[parts : parts + 2], refs[parts + 2 : parts + 4]
     refs = refs[parts + 4 + chained :]
@@ -169,7 +174,7 @@
         tail = payload[:, width:].astype(jnp.float32)
         lane = lax.broadcasted_iota(jnp.int32, tail.shape, 1) % experts
         for which in range(2):
-            value = jnp.sum(jnp.where(lane == ids_ref[which], tail, 0.0), axis=1, keepdims=True)
+            value = jnp.sum(jnp.where(lane == expert_ref[0] ^ which, tail, 0.0), axis=1, keepdims=True)
             coef_ref[which, here, :] = jnp.broadcast_to(value, tail.shape)
     tile = 256
     for which, (gate_up, _) in enumerate(weights):
@@ -190,7 +195,7 @@
         copy.wait()
 
 
-def expert_rows(ids, payloads, own, other, after, experts, hold=False):
+def expert_rows(expert_id, payloads, own, other, after, experts, hold=False):
     width = own[0].shape[0]
     hidden = own[1].shape[0]
     rows = sum(p.shape[0] for p in payloads)
@@ -217,29 +222,29 @@
             transcendentals=rows * hidden * 2,
         ),
         name="expert_rows",
-    )(ids, *payloads, *own, *other, *chain)
+    )(expert_id, *payloads, *own, *other, *chain)
     return (results[:-1], results[-1]) if hold else results
 
 
-def last_kernel(base_ref, first_ref, second_ref, out_ref):
-    half = first_ref.shape[0]
-    for start, total_ref in ((0, first_ref), (half, second_ref)):
-        here = slice(start, start + half)
-        out_ref[here, :] = (base_ref[here, :] + total_ref[...].astype(jnp.float32)).astype(jnp.bfloat16)
-
-
-def last_rows(base, first, second):
-    rows, width = base.shape
+def last_kernel(near0_ref, near1_ref, total0_ref, total1_ref, out_ref):
+    half = near0_ref.shape[0]
+    for start, near_ref, total_ref in ((0, near0_ref, total0_ref), (half, near1_ref, total1_ref)):
+        total = near_ref[...] + total_ref[...].astype(jnp.float32)
+        out_ref[start : start + half, :] = total.astype(jnp.bfloat16)
+
+
+def last_rows(nears, totals):
+    rows, width = nears[0].shape
     vmem = pl.BlockSpec(memory_space=pltpu.VMEM)
     return pl.pallas_call(
         last_kernel,
-        out_shape=jax.ShapeDtypeStruct((rows, width), jnp.bfloat16),
-        in_specs=[vmem] * 3,
+        out_shape=jax.ShapeDtypeStruct((2 * rows, width), jnp.bfloat16),
+        in_specs=[vmem] * 4,
         out_specs=vmem,
         compiler_params=pltpu.CompilerParams(vmem_limit_bytes=8 * MIB),
-        cost_estimate=pl.CostEstimate(flops=rows * width, bytes_accessed=rows * width * 8, transcendentals=0),
+        cost_estimate=pl.CostEstimate(flops=2 * rows * width, bytes_accessed=rows * width * 16, transcendentals=0),
         name="last_rows",
-    )(base, first, second)
+    )(*nears, *totals)
 
 
 def chip_ring(depth, across):
@@ -252,8 +257,8 @@
 
 def relay_body(fresh, previous, norm_gain, routes, gate_weights, w_gate_up, w_down, *, across):
     devices_exp = lax.axis_size("expert")
-    section_id = lax.axis_index("section")
-    expert_id = lax.axis_index("expert")
+    section_id = lax.axis_index("section").astype(jnp.int32).reshape(1)
+    expert_id = lax.axis_index("expert").astype(jnp.int32).reshape(1)
     rows = fresh.shape[0]
     half = rows // 2
     chips = devices_exp // CORES
@@ -266,15 +271,14 @@
     def move(value, pairs):
         return lax.ppermute(value, "expert", pairs)
 
+    cuts = [slice(0, half), slice(half, rows)]
+    arrived = [from_behind(previous[0, cut], "section", 1) for cut in cuts]
     own = (w_gate_up[0, 0], w_down[0, 0])
-    far_other = tuple(move(w, swap) for w in own)
-    cuts = [slice(0, half), slice(half, rows)]
-    first_cut = previous[0, cuts[0]]
-    second_cut = lax.optimization_barrier((previous, first_cut))[0][0, cuts[1]]
-    arrived = [from_behind(cut, "section", 1) for cut in (first_cut, second_cut)]
-    ids = jnp.stack([expert_id, expert_id ^ 1]).astype(jnp.int32)
-    base, gain = base_rows(fresh, norm_gain, routes[0], gate_weights[0], own, devices_exp)
-    packed = [norm_rows(section_id, base, arrived[c], gain, cuts[c].start) for c in range(2)]
+    swapped = lax.optimization_barrier((*own, section_id, expert_id))[:2]
+    other = tuple(move(w, swap) for w in swapped)
+    base, fresh, gain = base_rows(fresh, norm_gain, routes[0].T, gate_weights[0].T, devices_exp)
+    packed, arrival = zip(*(norm_rows(section_id, base, fresh, arrived[c], gain, cuts[c].start) for c in range(2)))
+    packed = list(packed)
 
     hops = chips // 2
     ups = [packed] + [[None, None] for _ in range(hops)]
@@ -287,26 +291,25 @@
         if s < hops - 1 or c == 1:
             downs[s + 1][c] = move(falling, down)
 
+    last = None
+
+    def mlp(payloads, hold=False):
+        nonlocal last, other
+        sums = expert_rows(expert_id, payloads, own, other, last, devices_exp, hold)
+        if hold:
+            sums, other_gate_up = sums
+            other = (other_gate_up, other[1])
+        last = sums[0]
+        return sums
+
+    to_down, to_up = {}, {}
     pass_on(0, 0, None)
     pass_on(0, 1, None)
-    own_sums, other_gate_up = expert_rows(ids, packed, own, far_other, None, devices_exp, hold=True)
-    other = (other_gate_up, far_other[1])
-    last = own_sums[0]
-
-    def mlp(payloads):
-        nonlocal last
-        sums = expert_rows(ids, payloads, own, other, last, devices_exp)
-        last = sums[0]
-        return sums
-
-    to_down, to_up = {}, {}
-    for s in range(1, hops - 1):
-        pass_on(s, 0, last)
-        pass_on(s, 1, (last, ups[s][0], downs[s][0]))
-        to_down[s, 0], to_down[s, 1], to_up[s, 0], to_up[s, 1] = mlp(ups[s] + downs[s])
-    for c in range(2):
-        pass_on(hops - 1, c, (last, ups[hops - 1][0], downs[hops - 1][0]))
-        to_down[hops - 1, c], to_up[hops - 1, c] = mlp([ups[hops - 1][c], downs[hops - 1][c]])
+    own_sums = mlp(packed, HOLD)
+    for s in range(1, hops):
+        for c in range(2):
+            pass_on(s, c, last)
+            to_down[s, c], to_up[s, c] = mlp([ups[s][c], downs[s][c]])
     to_up[hops, 0], to_down[hops, 1] = mlp([ups[hops][0], downs[hops][1]])
 
     flows = [(to_down, 0, down), (to_up, 1, up), (to_up, 0, up), (to_down, 1, down)]
@@ -323,10 +326,11 @@
                 total = terms[place, c] + carried.astype(jnp.float32)
             totals[i] = move(total.astype(jnp.bfloat16), pairs)
 
-    arrival = jnp.where(section_id == 0, fresh, jnp.concatenate(arrived, axis=0)).astype(jnp.float32)
-    near = [own_sums[c] + totals[c].astype(jnp.float32) for c in range(2)]
-    near = lax.optimization_barrier(arrival + jnp.concatenate(near, axis=0))
-    return last_rows(near, totals[2], totals[3])[None]
+    nears = [
+        arrival[c].astype(jnp.float32) + (own_sums[c] + totals[c].astype(jnp.float32)) for c in range(2)
+    ]
+    nears = lax.optimization_barrier(nears)
+    return last_rows(nears, totals[2:])[None]
 
 
 def solution(mesh):

time: 136 us -> 105 us (0.77)
  local copies, waits for them, and re-layouts: 24.4 us -> 7.22 us
  Pallas kernels: 38.3 us -> 23.9 us
  waiting for transfers between devices: 30.8 us -> 35.3 us
  other arithmetic: 4.83 us -> 0.75 us
    unnamed x72 -> x12, local copies, waits for them, and re-layouts: 21 us -> 5.9 us
    pallas_call x6 -> x8, Pallas kernels: 35.3 us -> 22.7 us  [expert_rows(): pl.pallas_call(functools.partial(mlp_kernel, parts=len(payloads), chained...]
    ppermute x2, waiting for transfers between devices: 0.01 us -> 4.5 us  [from_behind(): return lax.ppermute(value, axis, pairs)]
    convert_element_type x14, other arithmetic: 3.5 us -> 0.61 us  [relay_body(): totals[i] = move(total.astype(jnp.bfloat16), pairs)]
    squeeze x2 -> x1, local copies, waits for them, and re-layouts: 3.35 us -> 1.32 us  [relay_body(): arrived = [from_behind(previous[0, cut], 'section', 1) for cut in cuts]]
    pallas_call x3, Pallas kernels: 2.49 us -> 0.96 us  [the longest x1 0.88 us: last_rows(): pl.pallas_call(last_kernel, out_shape=jax.ShapeDtypeStruct((2 * rows, wid...]
    ppermute x30, starting transfers between devices: 29.8 us -> 31.1 us  [move(): return lax.ppermute(value, 'expert', pairs)]
  transfers between devices with their start and end apart: 32 -> 32, of which waited for: 9 -> 17; matrix products, arithmetic and copies ran while one was open for 7% -> 2% of each run, Pallas kernels for 28% -> 22%
where the time goes in v4:
time: 105 us
  starting transfers between devices  37.3 us (36%)
  waiting for transfers between devices  35.3 us (34%)
  Pallas kernels  23.9 us (23%)
  local copies, waits for them, and re-layouts  7.22 us (7%)
    ppermute x30, starting transfers between devices, move(): return lax.ppermute(value, 'expert', pairs)  31.1 us
    ppermute x30, waiting for transfers between devices, move(): return lax.ppermute(value, 'expert', pairs)  30.8 us
    pallas_call x8, Pallas kernels, expert_rows(): pl.pallas_call(functools.partial(mlp_kernel, parts=len(payloads), chained...  22.7 us
    ppermute x2, starting transfers between devices, from_behind(): return lax.ppermute(value, axis, pairs)  6.18 us
    unnamed x12, local copies, waits for them, and re-layouts  5.9 us
    ppermute x2, waiting for transfers between devices, from_behind(): return lax.ppermute(value, axis, pairs)  4.5 us
  transfers between devices with their start and end apart: 32, of which 17 were waited for; matrix products, arithmetic and copies ran while one was open for 2% of the time, Pallas kernels for 22%

profile of v4, /device:TPU:0, one launch (start us, length us, event | category | flops | bytes accessed | tf_op | source)
XLA Modules:
  0.0 104.8 jit_solution(7179123987537728724)
XLA Ops:
  0.0 0.5 collective-permute-start.2
  0.5 1.3 %slice_bitcast_fusion = (bf16[64,2048]{1,0:T(8,128)(2,1)S(1)}, bf16[64,2048]{1,0:T(8,128)(2,1)S(1)}) fusion(bf16[1,128,2048]{2,1,0:T(8,128)(2,1)} %param.8), kind=kLoop, calls=%fused_computation.12 | loop fusion | bytes 1048576 | tf_op jit(solution)/shard_map/squeeze | solution.py:275
  1.8 4.9 %collective-permute-start = (bf16[64,2048]{1,0:T(8,128)(2,1)S(1)}, bf16[64,2048]{1,0:T(8,128)(2,1)S(1)}, u32[]{:S(2)}, u32[]{:S(2)}) collective-permute-start(bf16[64,2048]{1,0:T(8,128)(2,1)S(1)} %get-tuple-element.108), channel_id=1, source_target_pairs={{0,16},{1,17},{2,18},{3,19},{4,20},{5,21},{6,22},{7,23},{8,24},{9,... | collective-permute-start | bytes 786440 | tf_op jit(solution)/shard_map/ppermute | solution.py:20
  6.7 1.3 %collective-permute-start.1 = (bf16[64,2048]{1,0:T(8,128)(2,1)S(1)}, bf16[64,2048]{1,0:T(8,128)(2,1)S(1)}, u32[]{:S(2)}, u32[]{:S(2)}) collective-permute-start(bf16[64,2048]{1,0:T(8,128)(2,1)S(1)} %get-tuple-element.107), channel_id=1, source_target_pairs={{0,16},{1,17},{2,18},{3,19},{4,20},{5,21},{6,22},{7,23},{8,24},{9,... | collective-permute-start | bytes 786440 | tf_op jit(solution)/shard_map/ppermute | solution.py:20
  8.1 1.0 copy-done.2
  9.1 0.7 copy-done.3
  9.8 0.7 copy-done.4
  10.5 0.7 copy-done.5
  11.2 0.3 base_rows.1
  11.4 2.0 %collective-permute-done.arrived_ref = bf16[64,2048]{1,0:T(8,128)(2,1)S(1)} collective-permute-done((bf16[64,2048]{1,0:T(8,128)(2,1)S(1)}, bf16[64,2048]{1,0:T(8,128)(2,1)S(1)}, u32[]{:S(2)}, u32[]{:S(2)}) %collective-permute-start) | collective-permute-done | bytes 262176 | tf_op jit(solution)/shard_map/ppermute | solution.py:20
  13.4 1.5 %collective-permute-start.4 = (bf16[64,2176]{1,0:T(8,128)(2,1)S(1)}, bf16[64,2176]{1,0:T(8,128)(2,1)S(1)}, u32[]{:S(2)}, u32[]{:S(2)}) collective-permute-start(bf16[64,2176]{1,0:T(8,128)(2,1)S(1)} %get-tuple-element.66.refs_0_), channel_id=1, source_target_pairs={{2,6},{3,7},{6,10},{7,11},{10,14},{11,15},{14,12},{15,13},{12,8},{... | collective-permute-start | bytes 835592 | tf_op jit(solution)/shard_map/ppermute | solution.py:272
  15.0 0.5 collective-permute-start.5
  15.5 2.5 %collective-permute-done.1.arrived_ref = bf16[64,2048]{1,0:T(8,128)(2,1)S(1)} collective-permute-done((bf16[64,2048]{1,0:T(8,128)(2,1)S(1)}, bf16[64,2048]{1,0:T(8,128)(2,1)S(1)}, u32[]{:S(2)}, u32[]{:S(2)}) %collective-permute-start.1) | collective-permute-done | bytes 262176 | tf_op jit(solution)/shard_map/ppermute | solution.py:20
  18.1 1.5 %collective-permute-start.8 = (bf16[64,2176]{1,0:T(8,128)(2,1)S(1)}, bf16[64,2176]{1,0:T(8,128)(2,1)S(1)}, u32[]{:S(2)}, u32[]{:S(2)}) collective-permute-start(bf16[64,2176]{1,0:T(8,128)(2,1)S(1)} %get-tuple-element.71.refs_1_), channel_id=1, source_target_pairs={{2,6},{3,7},{6,10},{7,11},{10,14},{11,15},{14,12},{15,13},{12,8},{... | collective-permute-start | bytes 835592 | tf_op jit(solution)/shard_map/ppermute | solution.py:272
  19.7 0.5 collective-permute-start.9
  20.2 2.8 %copy-done = bf16[1,1,2048,1536]{3,2,1,0:T(8,128)(2,1)S(1)} copy-done((bf16[1,1,2048,1536]{3,2,1,0:T(8,128)(2,1)S(1)}, bf16[1,1,2048,1536]{3,2,1,0:T(8,128)(2,1)}, u32[]{:S(2)}) %copy-start) | copy-done | bytes 6291480
  23.0 2.8 %expert_rows.8 = (f32[64,2048]{1,0:T(8,128)S(1)}, f32[64,2048]{1,0:T(8,128)S(1)}) custom-call(s32[1]{0:T(128)} %bitcast.6.expert_ref, bf16[64,2176]{1,0:T(8,128)(2,1)S(1)} %get-tuple-element.66.refs_0_, bf16[64,2176]{1,0:T(8,128)(2,1)S(1)} %get-tuple-element.71.refs_1_, bf16[2048,1536]{1,0:T(8,128)(2,1)S(1)} %bitcast.16, bf16[768,2048]{1,0:T(8,128)(2,1)S(1)} %bitcast.25, ...), custom_call_target="tpu_custom_call" | custom-call | flops 2415919104 | bytes 1572864 | tf_op jit(solution)/shard_map/expert_rows/pallas_call | solution.py:205
  25.8 1.5 %collective-permute-start.6 = (bf16[64,2176]{1,0:T(8,128)(2,1)S(1)}, bf16[64,2176]{1,0:T(8,128)(2,1)S(1)}, u32[]{:S(2)}, u32[]{:S(2)}) collective-permute-start(bf16[64,2176]{1,0:T(8,128)(2,1)S(1)} %collective-permute-done.4.refs_0_), channel_id=1, source_target_pairs={{2,6},{3,7},{6,10},{7,11},{10,14},{11,15},{14,12},{15,13},{12,8},{... | collective-permute-start | bytes 835592 | tf_op jit(solution)/shard_map/ppermute | solution.py:272
  27.4 0.5 collective-permute-start.7
  27.9 2.8 %expert_rows.9 = (f32[64,2048]{1,0:T(8,128)S(1)}, f32[64,2048]{1,0:T(8,128)S(1)}) custom-call(s32[1]{0:T(128)} %bitcast.6.expert_ref, bf16[64,2176]{1,0:T(8,128)(2,1)S(1)} %collective-permute-done.4.refs_0_, bf16[64,2176]{1,0:T(8,128)(2,1)S(1)} %collective-permute-done.5.refs_1_, bf16[2048,1536]{1,0:T(8,128)(2,1)S(1)} %bitcast.17, ...), custom_call_target="tpu_custom_call" | custom-call | flops 2415919104 | bytes 1572864 | tf_op jit(solution)/shard_map/expert_rows/pallas_call | solution.py:205
  30.8 1.6 %collective-permute-start.12 = (bf16[64,2176]{1,0:T(8,128)(2,1)S(1)}, bf16[64,2176]{1,0:T(8,128)(2,1)S(1)}, u32[]{:S(2)}, u32[]{:S(2)}) collective-permute-start(bf16[64,2176]{1,0:T(8,128)(2,1)S(1)} %collective-permute-done.8.refs_0_), channel_id=1, source_target_pairs={{2,6},{3,7},{6,10},{7,11},{10,14},{11,15},{14,12},{15,13},{12,8},{... | collective-permute-start | bytes 835592 | tf_op jit(solution)/shard_map/ppermute | solution.py:272
  32.3 0.5 collective-permute-start.13
  32.9 2.8 %expert_rows.10 = (f32[64,2048]{1,0:T(8,128)S(1)}, f32[64,2048]{1,0:T(8,128)S(1)}) custom-call(s32[1]{0:T(128)} %bitcast.6.expert_ref, bf16[64,2176]{1,0:T(8,128)(2,1)S(1)} %collective-permute-done.8.refs_0_, bf16[64,2176]{1,0:T(8,128)(2,1)S(1)} %collective-permute-done.9.refs_1_, bf16[2048,1536]{1,0:T(8,128)(2,1)S(1)} %bitcast.18, ...), custom_call_target="tpu_custom_call" | custom-call | flops 2415919104 | bytes 1572864 | tf_op jit(solution)/shard_map/expert_rows/pallas_call | solution.py:205
  35.8 1.6 %collective-permute-start.10 = (bf16[64,2176]{1,0:T(8,128)(2,1)S(1)}, bf16[64,2176]{1,0:T(8,128)(2,1)S(1)}, u32[]{:S(2)}, u32[]{:S(2)}) collective-permute-start(bf16[64,2176]{1,0:T(8,128)(2,1)S(1)} %collective-permute-done.6.refs_0_), channel_id=1, source_target_pairs={{2,6},{3,7},{6,10},{7,11},{10,14},{11,15},{14,12},{15,13},{12,8},{... | collective-permute-start | bytes 835592 | tf_op jit(solution)/shard_map/ppermute | solution.py:272
  37.4 0.5 collective-permute-start.11
  37.8 2.8 %expert_rows.11 = (f32[64,2048]{1,0:T(8,128)S(1)}, f32[64,2048]{1,0:T(8,128)S(1)}) custom-call(s32[1]{0:T(128)} %bitcast.6.expert_ref, bf16[64,2176]{1,0:T(8,128)(2,1)S(1)} %collective-permute-done.6.refs_0_, bf16[64,2176]{1,0:T(8,128)(2,1)S(1)} %collective-permute-done.7.refs_1_, bf16[2048,1536]{1,0:T(8,128)(2,1)S(1)} %bitcast.19, ...), custom_call_target="tpu_custom_call" | custom-call | flops 2415919104 | bytes 1572864 | tf_op jit(solution)/shard_map/expert_rows/pallas_call | solution.py:205
  40.7 1.3 %collective-permute-done.13.refs_1_ = bf16[64,2176]{1,0:T(8,128)(2,1)S(1)} collective-permute-done((bf16[64,2176]{1,0:T(8,128)(2,1)S(1)}, bf16[64,2176]{1,0:T(8,128)(2,1)S(1)}, u32[]{:S(2)}, u32[]{:S(2)}) %collective-permute-start.13) | collective-permute-done | bytes 278560 | tf_op jit(solution)/shard_map/ppermute | solution.py:272
  41.9 1.6 %collective-permute-start.16 = (bf16[64,2176]{1,0:T(8,128)(2,1)S(1)}, bf16[64,2176]{1,0:T(8,128)(2,1)S(1)}, u32[]{:S(2)}, u32[]{:S(2)}) collective-permute-start(bf16[64,2176]{1,0:T(8,128)(2,1)S(1)} %collective-permute-done.12.refs_0_), channel_id=1, source_target_pairs={{2,6},{3,7},{6,10},{7,11},{10,14},{11,15},{14,12},{15,13},{12,8},{... | collective-permute-start | bytes 835592 | tf_op jit(solution)/shard_map/ppermute | solution.py:272
  43.5 0.5 collective-permute-start.17
  44.0 2.8 %expert_rows.12 = (f32[64,2048]{1,0:T(8,128)S(1)}, f32[64,2048]{1,0:T(8,128)S(1)}) custom-call(s32[1]{0:T(128)} %bitcast.6.expert_ref, bf16[64,2176]{1,0:T(8,128)(2,1)S(1)} %collective-permute-done.12.refs_0_, bf16[64,2176]{1,0:T(8,128)(2,1)S(1)} %collective-permute-done.13.refs_1_, bf16[2048,1536]{1,0:T(8,128)(2,1)S(1)} %bitcast.20, ...), custom_call_target="tpu_custom_call" | custom-call | flops 2415919104 | bytes 1572864 | tf_op jit(solution)/shard_map/expert_rows/pallas_call | solution.py:205
  46.8 1.1 %collective-permute-done.11.refs_1_ = bf16[64,2176]{1,0:T(8,128)(2,1)S(1)} collective-permute-done((bf16[64,2176]{1,0:T(8,128)(2,1)S(1)}, bf16[64,2176]{1,0:T(8,128)(2,1)S(1)}, u32[]{:S(2)}, u32[]{:S(2)}) %collective-permute-start.11) | collective-permute-done | bytes 278560 | tf_op jit(solution)/shard_map/ppermute | solution.py:272
  47.9 1.6 %collective-permute-start.15 = (bf16[64,2176]{1,0:T(8,128)(2,1)S(1)}, bf16[64,2176]{1,0:T(8,128)(2,1)S(1)}, u32[]{:S(2)}, u32[]{:S(2)}) collective-permute-start(bf16[64,2176]{1,0:T(8,128)(2,1)S(1)} %collective-permute-done.10.refs_0_), channel_id=1, source_target_pairs={{2,6},{3,7},{6,10},{7,11},{10,14},{11,15},{14,12},{15,13},{12,8},{... | collective-permute-start | bytes 835592 | tf_op jit(solution)/shard_map/ppermute | solution.py:272
  49.5 2.8 %expert_rows.13 = (f32[64,2048]{1,0:T(8,128)S(1)}, f32[64,2048]{1,0:T(8,128)S(1)}) custom-call(s32[1]{0:T(128)} %bitcast.6.expert_ref, bf16[64,2176]{1,0:T(8,128)(2,1)S(1)} %collective-permute-done.10.refs_0_, bf16[64,2176]{1,0:T(8,128)(2,1)S(1)} %collective-permute-done.11.refs_1_, bf16[2048,1536]{1,0:T(8,128)(2,1)S(1)} %bitcast.21, ...), custom_call_target="tpu_custom_call" | custom-call | flops 2415919104 | bytes 1572864 | tf_op jit(solution)/shard_map/expert_rows/pallas_call | solution.py:205
  52.3 0.2 collective-permute-done.16.refs_0_
  52.5 1.6 %collective-permute-start.18 = (bf16[64,2176]{1,0:T(8,128)(2,1)S(1)}, bf16[64,2176]{1,0:T(8,128)(2,1)S(1)}, u32[]{:S(2)}, u32[]{:S(2)}) collective-permute-start(bf16[64,2176]{1,0:T(8,128)(2,1)S(1)} %collective-permute-done.17.refs_1_), channel_id=1, source_target_pairs={{6,2},{7,3},{10,6},{11,7},{14,10},{15,11},{12,14},{13,15},{8,12},{... | collective-permute-start | bytes 835592 | tf_op jit(solution)/shard_map/ppermute | solution.py:272
  54.1 2.8 %expert_rows.14 = (f32[64,2048]{1,0:T(8,128)S(1)}, f32[64,2048]{1,0:T(8,128)S(1)}) custom-call(s32[1]{0:T(128)} %bitcast.6.expert_ref, bf16[64,2176]{1,0:T(8,128)(2,1)S(1)} %collective-permute-done.16.refs_0_, bf16[64,2176]{1,0:T(8,128)(2,1)S(1)} %collective-permute-done.17.refs_1_, bf16[2048,1536]{1,0:T(8,128)(2,1)S(1)} %bitcast.22, ...), custom_call_target="tpu_custom_call" | custom-call | flops 2415919104 | bytes 1572864 | tf_op jit(solution)/shard_map/expert_rows/pallas_call | solution.py:205
  57.0 0.5 collective-permute-start.21
  57.5 1.8 %collective-permute-start.14 = (bf16[64,2048]{1,0:T(8,128)(2,1)S(1)}, bf16[64,2048]{1,0:T(8,128)(2,1)S(1)}, u32[]{:S(2)}, u32[]{:S(2)}) collective-permute-start(bf16[64,2048]{1,0:T(8,128)(2,1)S(1)} %convert_element_type.85), channel_id=1, source_target_pairs={{6,2},{7,3},{10,6},{11,7},{14,10},{15,11},{12,14},{13,15},{8,12},{... | collective-permute-start | bytes 786440 | tf_op jit(solution)/shard_map/ppermute | solution.py:272
  59.3 1.0 collective-permute-done.18.refs_1_
  60.4 2.8 %expert_rows.15 = (f32[64,2048]{1,0:T(8,128)S(1)}, f32[64,2048]{1,0:T(8,128)S(1)}) custom-call(s32[1]{0:T(128)} %bitcast.6.expert_ref, bf16[64,2176]{1,0:T(8,128)(2,1)S(1)} %collective-permute-done.15.refs_0_, bf16[64,2176]{1,0:T(8,128)(2,1)S(1)} %collective-permute-done.18.refs_1_, bf16[2048,1536]{1,0:T(8,128)(2,1)S(1)} %bitcast.23, ...), custom_call_target="tpu_custom_call" | custom-call | flops 2415919104 | bytes 1572864 | tf_op jit(solution)/shard_map/expert_rows/pallas_call | solution.py:205
  63.3 0.1 collective-permute-done.21
  63.4 1.4 %collective-permute-done.14 = bf16[64,2048]{1,0:T(8,128)(2,1)S(1)} collective-permute-done((bf16[64,2048]{1,0:T(8,128)(2,1)S(1)}, bf16[64,2048]{1,0:T(8,128)(2,1)S(1)}, u32[]{:S(2)}, u32[]{:S(2)}) %collective-permute-start.14) | collective-permute-done | bytes 262176 | tf_op jit(solution)/shard_map/ppermute | solution.py:272
  64.8 1.6 %collective-permute-start.24 = (bf16[64,2048]{1,0:T(8,128)(2,1)S(1)}, bf16[64,2048]{1,0:T(8,128)(2,1)S(1)}, u32[]{:S(2)}, u32[]{:S(2)}) collective-permute-start(bf16[64,2048]{1,0:T(8,128)(2,1)S(1)} %convert_element_type.98), channel_id=1, source_target_pairs={{2,6},{3,7},{6,10},{7,11},{10,14},{11,15},{14,12},{15,13},{12,8},{... | collective-permute-start | bytes 786440 | tf_op jit(solution)/shard_map/ppermute | solution.py:272
  66.5 0.5 collective-permute-start.19
  67.0 1.6 %collective-permute-start.22 = (bf16[64,2048]{1,0:T(8,128)(2,1)S(1)}, bf16[64,2048]{1,0:T(8,128)(2,1)S(1)}, u32[]{:S(2)}, u32[]{:S(2)}) collective-permute-start(bf16[64,2048]{1,0:T(8,128)(2,1)S(1)} %add_convert_fusion.7), channel_id=1, source_target_pairs={{2,6},{3,7},{6,10},{7,11},{10,14},{11,15},{14,12},{15,13},{12,8},{... | collective-permute-start | bytes 786440 | tf_op jit(solution)/shard_map/ppermute | solution.py:272
  68.6 0.5 collective-permute-start.28
  69.1 5.1 %collective-permute-done.24 = bf16[64,2048]{1,0:T(8,128)(2,1)S(1)} collective-permute-done((bf16[64,2048]{1,0:T(8,128)(2,1)S(1)}, bf16[64,2048]{1,0:T(8,128)(2,1)S(1)}, u32[]{:S(2)}, u32[]{:S(2)}) %collective-permute-start.24) | collective-permute-done | bytes 262176 | tf_op jit(solution)/shard_map/ppermute | solution.py:272
  74.2 1.6 %collective-permute-start.25 = (bf16[64,2048]{1,0:T(8,128)(2,1)S(1)}, bf16[64,2048]{1,0:T(8,128)(2,1)S(1)}, u32[]{:S(2)}, u32[]{:S(2)}) collective-permute-start(bf16[64,2048]{1,0:T(8,128)(2,1)S(1)} %add_convert_fusion.5), channel_id=1, source_target_pairs={{2,6},{3,7},{6,10},{7,11},{10,14},{11,15},{14,12},{15,13},{12,8},{... | collective-permute-start | bytes 786440 | tf_op jit(solution)/shard_map/ppermute | solution.py:272
  75.9 0.5 collective-permute-start.20
  76.4 3.4 %collective-permute-done.22 = bf16[64,2048]{1,0:T(8,128)(2,1)S(1)} collective-permute-done((bf16[64,2048]{1,0:T(8,128)(2,1)S(1)}, bf16[64,2048]{1,0:T(8,128)(2,1)S(1)}, u32[]{:S(2)}, u32[]{:S(2)}) %collective-permute-start.22) | collective-permute-done | bytes 262176 | tf_op jit(solution)/shard_map/ppermute | solution.py:272
  79.8 1.6 %collective-permute-start.23 = (bf16[64,2048]{1,0:T(8,128)(2,1)S(1)}, bf16[64,2048]{1,0:T(8,128)(2,1)S(1)}, u32[]{:S(2)}, u32[]{:S(2)}) collective-permute-start(bf16[64,2048]{1,0:T(8,128)(2,1)S(1)} %add_convert_fusion.6), channel_id=1, source_target_pairs={{2,6},{3,7},{6,10},{7,11},{10,14},{11,15},{14,12},{15,13},{12,8},{... | collective-permute-start | bytes 786440 | tf_op jit(solution)/shard_map/ppermute | solution.py:272
  81.5 0.5 collective-permute-start.29
  82.0 3.4 %collective-permute-done.25 = bf16[64,2048]{1,0:T(8,128)(2,1)S(1)} collective-permute-done((bf16[64,2048]{1,0:T(8,128)(2,1)S(1)}, bf16[64,2048]{1,0:T(8,128)(2,1)S(1)}, u32[]{:S(2)}, u32[]{:S(2)}) %collective-permute-start.25) | collective-permute-done | bytes 262176 | tf_op jit(solution)/shard_map/ppermute | solution.py:272
  85.4 1.6 %collective-permute-start.26 = (bf16[64,2048]{1,0:T(8,128)(2,1)S(1)}, bf16[64,2048]{1,0:T(8,128)(2,1)S(1)}, u32[]{:S(2)}, u32[]{:S(2)}) collective-permute-start(bf16[64,2048]{1,0:T(8,128)(2,1)S(1)} %add_convert_fusion.4), channel_id=1, source_target_pairs={{2,6},{3,7},{6,10},{7,11},{10,14},{11,15},{14,12},{15,13},{12,8},{... | collective-permute-start | bytes 786440 | tf_op jit(solution)/shard_map/ppermute | solution.py:272
  87.1 2.6 %collective-permute-done.29 = bf16[64,2048]{1,0:T(8,128)(2,1)S(1)} collective-permute-done((bf16[64,2048]{1,0:T(8,128)(2,1)S(1)}, bf16[64,2048]{1,0:T(8,128)(2,1)S(1)}, u32[]{:S(2)}, u32[]{:S(2)}) %collective-permute-start.29) | collective-permute-done | bytes 262176 | tf_op jit(solution)/shard_map/ppermute | solution.py:272
  89.7 0.5 collective-permute-start.30
  90.3 0.1 add_add_fusion.1.near0_ref
  90.3 3.4 %collective-permute-done.26 = bf16[64,2048]{1,0:T(8,128)(2,1)S(1)} collective-permute-done((bf16[64,2048]{1,0:T(8,128)(2,1)S(1)}, bf16[64,2048]{1,0:T(8,128)(2,1)S(1)}, u32[]{:S(2)}, u32[]{:S(2)}) %collective-permute-start.26) | collective-permute-done | bytes 262176 | tf_op jit(solution)/shard_map/ppermute | solution.py:272
  93.8 1.6 %collective-permute-start.27 = (bf16[64,2048]{1,0:T(8,128)(2,1)S(1)}, bf16[64,2048]{1,0:T(8,128)(2,1)S(1)}, u32[]{:S(2)}, u32[]{:S(2)}) collective-permute-start(bf16[64,2048]{1,0:T(8,128)(2,1)S(1)} %add_convert_fusion.3), channel_id=1, source_target_pairs={{2,6},{3,7},{6,10},{7,11},{10,14},{11,15},{14,12},{15,13},{12,8},{... | collective-permute-start | bytes 786440 | tf_op jit(solution)/shard_map/ppermute | solution.py:272
  95.4 2.0 %collective-permute-done.30 = bf16[64,2048]{1,0:T(8,128)(2,1)S(1)} collective-permute-done((bf16[64,2048]{1,0:T(8,128)(2,1)S(1)}, bf16[64,2048]{1,0:T(8,128)(2,1)S(1)}, u32[]{:S(2)}, u32[]{:S(2)}) %collective-permute-start.30) | collective-permute-done | bytes 262176 | tf_op jit(solution)/shard_map/ppermute | solution.py:272
  97.5 0.6 collective-permute-start.31
  98.1 2.1 %collective-permute-done.27.total0_ref = bf16[64,2048]{1,0:T(8,128)(2,1)S(1)} collective-permute-done((bf16[64,2048]{1,0:T(8,128)(2,1)S(1)}, bf16[64,2048]{1,0:T(8,128)(2,1)S(1)}, u32[]{:S(2)}, u32[]{:S(2)}) %collective-permute-start.27) | collective-permute-done | bytes 262176 | tf_op jit(solution)/shard_map/ppermute | solution.py:272
  100.2 3.7 %collective-permute-done.31.total1_ref = bf16[64,2048]{1,0:T(8,128)(2,1)S(1)} collective-permute-done((bf16[64,2048]{1,0:T(8,128)(2,1)S(1)}, bf16[64,2048]{1,0:T(8,128)(2,1)S(1)}, u32[]{:S(2)}, u32[]{:S(2)}) %collective-permute-start.31) | collective-permute-done | bytes 262176 | tf_op jit(solution)/shard_map/ppermute | solution.py:272
  103.9 0.9 last_rows.1
  (41 shorter events, 1.0 us)
Async XLA Ops:
  0.0 20.2 %copy-start.1 = (bf16[1,1,768,2048]{3,2,1,0:T(8,128)(2,1)S(1)}, bf16[1,1,768,2048]{3,2,1,0:T(8,128)(2,1)}, u32[]{:S(2)}) copy-start(bf16[1,1,768,2048]{3,2,1,0:T(8,128)(2,1)} %param.13) | copy-start | bytes 9437188
  0.0 20.2 %collective-permute-start.2 = (bf16[2048,1536]{1,0:T(8,128)(2,1)}, bf16[2048,1536]{1,0:T(8,128)(2,1)S(1)}, u32[]{:S(2)}, u32[]{:S(2)}) collective-permute-start(bf16[2048,1536]{1,0:T(8,128)(2,1)} %bitcast.15), channel_id=1, source_target_pairs={{0,1},{1,0},{2,3},{3,2},{4,5},{5,4},{6,7},{7,6},{8,9},{9,8},{10,11... | collective-permute-start | bytes 18874376 | tf_op jit(solution)/shard_map/ppermute | solution.py:272
  0.5 19.2 %collective-permute-start.3 = (bf16[768,2048]{1,0:T(8,128)(2,1)}, bf16[768,2048]{1,0:T(8,128)(2,1)S(1)}, u32[]{:S(2)}, u32[]{:S(2)}) collective-permute-start(bf16[768,2048]{1,0:T(8,128)(2,1)} %bitcast.24), channel_id=1, source_target_pairs={{0,1},{1,0},{2,3},{3,2},{4,5},{5,4},{6,7},{7,6},{8,9},{9,8},{10,11... | collective-permute-start | bytes 9437192 | tf_op jit(solution)/shard_map/ppermute | solution.py:272
  1.8 11.5 %collective-permute-start = (bf16[64,2048]{1,0:T(8,128)(2,1)S(1)}, bf16[64,2048]{1,0:T(8,128)(2,1)S(1)}, u32[]{:S(2)}, u32[]{:S(2)}) collective-permute-start(bf16[64,2048]{1,0:T(8,128)(2,1)S(1)} %get-tuple-element.108), channel_id=1, source_target_pairs={{0,16},{1,17},{2,18},{3,19},{4,20},{5,21},{6,22},{7,23},{8,24},{9,... | collective-permute-start | bytes 786440 | tf_op jit(solution)/shard_map/ppermute | solution.py:20
  6.7 11.3 %collective-permute-start.1 = (bf16[64,2048]{1,0:T(8,128)(2,1)S(1)}, bf16[64,2048]{1,0:T(8,128)(2,1)S(1)}, u32[]{:S(2)}, u32[]{:S(2)}) collective-permute-start(bf16[64,2048]{1,0:T(8,128)(2,1)S(1)} %get-tuple-element.107), channel_id=1, source_target_pairs={{0,16},{1,17},{2,18},{3,19},{4,20},{5,21},{6,22},{7,23},{8,24},{9,... | collective-permute-start | bytes 786440 | tf_op jit(solution)/shard_map/ppermute | solution.py:20
  8.0 1.0 copy-start.2
  9.1 0.7 copy-start.3
  9.8 0.7 copy-start.4
  10.5 0.7 copy-start.5
  13.4 12.4 %collective-permute-start.4 = (bf16[64,2176]{1,0:T(8,128)(2,1)S(1)}, bf16[64,2176]{1,0:T(8,128)(2,1)S(1)}, u32[]{:S(2)}, u32[]{:S(2)}) collective-permute-start(bf16[64,2176]{1,0:T(8,128)(2,1)S(1)} %get-tuple-element.66.refs_0_), channel_id=1, source_target_pairs={{2,6},{3,7},{6,10},{7,11},{10,14},{11,15},{14,12},{15,13},{12,8},{... | collective-permute-start | bytes 835592 | tf_op jit(solution)/shard_map/ppermute | solution.py:272
  15.0 10.9 %collective-permute-start.5 = (bf16[64,2176]{1,0:T(8,128)(2,1)S(1)}, bf16[64,2176]{1,0:T(8,128)(2,1)S(1)}, u32[]{:S(2)}, u32[]{:S(2)}) collective-permute-start(bf16[64,2176]{1,0:T(8,128)(2,1)S(1)} %get-tuple-element.66.refs_0_), channel_id=1, source_target_pairs={{6,2},{7,3},{10,6},{11,7},{14,10},{15,11},{12,14},{13,15},{8,12},{... | collective-permute-start | bytes 835592 | tf_op jit(solution)/shard_map/ppermute | solution.py:272
  18.1 12.7 %collective-permute-start.8 = (bf16[64,2176]{1,0:T(8,128)(2,1)S(1)}, bf16[64,2176]{1,0:T(8,128)(2,1)S(1)}, u32[]{:S(2)}, u32[]{:S(2)}) collective-permute-start(bf16[64,2176]{1,0:T(8,128)(2,1)S(1)} %get-tuple-element.71.refs_1_), channel_id=1, source_target_pairs={{2,6},{3,7},{6,10},{7,11},{10,14},{11,15},{14,12},{15,13},{12,8},{... | collective-permute-start | bytes 835592 | tf_op jit(solution)/shard_map/ppermute | solution.py:272
  19.7 11.1 %collective-permute-start.9 = (bf16[64,2176]{1,0:T(8,128)(2,1)S(1)}, bf16[64,2176]{1,0:T(8,128)(2,1)S(1)}, u32[]{:S(2)}, u32[]{:S(2)}) collective-permute-start(bf16[64,2176]{1,0:T(8,128)(2,1)S(1)} %get-tuple-element.71.refs_1_), channel_id=1, source_target_pairs={{6,2},{7,3},{10,6},{11,7},{14,10},{15,11},{12,14},{13,15},{8,12},{... | collective-permute-start | bytes 835592 | tf_op jit(solution)/shard_map/ppermute | solution.py:272
  20.2 2.8 %copy-start = (bf16[1,1,2048,1536]{3,2,1,0:T(8,128)(2,1)S(1)}, bf16[1,1,2048,1536]{3,2,1,0:T(8,128)(2,1)}, u32[]{:S(2)}) copy-start(bf16[1,1,2048,1536]{3,2,1,0:T(8,128)(2,1)} %param.12) | copy-start | bytes 18874372
  25.8 9.9 %collective-permute-start.6 = (bf16[64,2176]{1,0:T(8,128)(2,1)S(1)}, bf16[64,2176]{1,0:T(8,128)(2,1)S(1)}, u32[]{:S(2)}, u32[]{:S(2)}) collective-permute-start(bf16[64,2176]{1,0:T(8,128)(2,1)S(1)} %collective-permute-done.4.refs_0_), channel_id=1, source_target_pairs={{2,6},{3,7},{6,10},{7,11},{10,14},{11,15},{14,12},{15,13},{12,8},{... | collective-permute-start | bytes 835592 | tf_op jit(solution)/shard_map/ppermute | solution.py:272
  27.4 8.4 %collective-permute-start.7 = (bf16[64,2176]{1,0:T(8,128)(2,1)S(1)}, bf16[64,2176]{1,0:T(8,128)(2,1)S(1)}, u32[]{:S(2)}, u32[]{:S(2)}) collective-permute-start(bf16[64,2176]{1,0:T(8,128)(2,1)S(1)} %collective-permute-done.5.refs_1_), channel_id=1, source_target_pairs={{6,2},{7,3},{10,6},{11,7},{14,10},{15,11},{12,14},{13,15},{8,12},{... | collective-permute-start | bytes 835592 | tf_op jit(solution)/shard_map/ppermute | solution.py:272
  30.8 9.9 %collective-permute-start.12 = (bf16[64,2176]{1,0:T(8,128)(2,1)S(1)}, bf16[64,2176]{1,0:T(8,128)(2,1)S(1)}, u32[]{:S(2)}, u32[]{:S(2)}) collective-permute-start(bf16[64,2176]{1,0:T(8,128)(2,1)S(1)} %collective-permute-done.8.refs_0_), channel_id=1, source_target_pairs={{2,6},{3,7},{6,10},{7,11},{10,14},{11,15},{14,12},{15,13},{12,8},{... | collective-permute-start | bytes 835592 | tf_op jit(solution)/shard_map/ppermute | solution.py:272
  32.3 9.6 %collective-permute-start.13 = (bf16[64,2176]{1,0:T(8,128)(2,1)S(1)}, bf16[64,2176]{1,0:T(8,128)(2,1)S(1)}, u32[]{:S(2)}, u32[]{:S(2)}) collective-permute-start(bf16[64,2176]{1,0:T(8,128)(2,1)S(1)} %collective-permute-done.9.refs_1_), channel_id=1, source_target_pairs={{6,2},{7,3},{10,6},{11,7},{14,10},{15,11},{12,14},{13,15},{8,12},{... | collective-permute-start | bytes 835592 | tf_op jit(solution)/shard_map/ppermute | solution.py:272
  35.8 11.0 %collective-permute-start.10 = (bf16[64,2176]{1,0:T(8,128)(2,1)S(1)}, bf16[64,2176]{1,0:T(8,128)(2,1)S(1)}, u32[]{:S(2)}, u32[]{:S(2)}) collective-permute-start(bf16[64,2176]{1,0:T(8,128)(2,1)S(1)} %collective-permute-done.6.refs_0_), channel_id=1, source_target_pairs={{2,6},{3,7},{6,10},{7,11},{10,14},{11,15},{14,12},{15,13},{12,8},{... | collective-permute-start | bytes 835592 | tf_op jit(solution)/shard_map/ppermute | solution.py:272
  37.4 10.5 %collective-permute-start.11 = (bf16[64,2176]{1,0:T(8,128)(2,1)S(1)}, bf16[64,2176]{1,0:T(8,128)(2,1)S(1)}, u32[]{:S(2)}, u32[]{:S(2)}) collective-permute-start(bf16[64,2176]{1,0:T(8,128)(2,1)S(1)} %collective-permute-done.7.refs_1_), channel_id=1, source_target_pairs={{6,2},{7,3},{10,6},{11,7},{14,10},{15,11},{12,14},{13,15},{8,12},{... | collective-permute-start | bytes 835592 | tf_op jit(solution)/shard_map/ppermute | solution.py:272
  41.9 10.6 %collective-permute-start.16 = (bf16[64,2176]{1,0:T(8,128)(2,1)S(1)}, bf16[64,2176]{1,0:T(8,128)(2,1)S(1)}, u32[]{:S(2)}, u32[]{:S(2)}) collective-permute-start(bf16[64,2176]{1,0:T(8,128)(2,1)S(1)} %collective-permute-done.12.refs_0_), channel_id=1, source_target_pairs={{2,6},{3,7},{6,10},{7,11},{10,14},{11,15},{14,12},{15,13},{12,8},{... | collective-permute-start | bytes 835592 | tf_op jit(solution)/shard_map/ppermute | solution.py:272
  43.5 9.0 %collective-permute-start.17 = (bf16[64,2176]{1,0:T(8,128)(2,1)S(1)}, bf16[64,2176]{1,0:T(8,128)(2,1)S(1)}, u32[]{:S(2)}, u32[]{:S(2)}) collective-permute-start(bf16[64,2176]{1,0:T(8,128)(2,1)S(1)} %collective-permute-done.13.refs_1_), channel_id=1, source_target_pairs={{6,2},{7,3},{10,6},{11,7},{14,10},{15,11},{12,14},{13,15},{8,12},{... | collective-permute-start | bytes 835592 | tf_op jit(solution)/shard_map/ppermute | solution.py:272
  47.9 11.4 %collective-permute-start.15 = (bf16[64,2176]{1,0:T(8,128)(2,1)S(1)}, bf16[64,2176]{1,0:T(8,128)(2,1)S(1)}, u32[]{:S(2)}, u32[]{:S(2)}) collective-permute-start(bf16[64,2176]{1,0:T(8,128)(2,1)S(1)} %collective-permute-done.10.refs_0_), channel_id=1, source_target_pairs={{2,6},{3,7},{6,10},{7,11},{10,14},{11,15},{14,12},{15,13},{12,8},{... | collective-permute-start | bytes 835592 | tf_op jit(solution)/shard_map/ppermute | solution.py:272
  52.5 7.9 %collective-permute-start.18 = (bf16[64,2176]{1,0:T(8,128)(2,1)S(1)}, bf16[64,2176]{1,0:T(8,128)(2,1)S(1)}, u32[]{:S(2)}, u32[]{:S(2)}) collective-permute-start(bf16[64,2176]{1,0:T(8,128)(2,1)S(1)} %collective-permute-done.17.refs_1_), channel_id=1, source_target_pairs={{6,2},{7,3},{10,6},{11,7},{14,10},{15,11},{12,14},{13,15},{8,12},{... | collective-permute-start | bytes 835592 | tf_op jit(solution)/shard_map/ppermute | solution.py:272
  57.0 6.4 %collective-permute-start.21 = (bf16[64,2048]{1,0:T(8,128)(2,1)S(1)}, bf16[64,2048]{1,0:T(8,128)(2,1)S(1)}, u32[]{:S(2)}, u32[]{:S(2)}) collective-permute-start(bf16[64,2048]{1,0:T(8,128)(2,1)S(1)} %convert_element_type.92), channel_id=1, source_target_pairs={{2,6},{3,7},{6,10},{7,11},{10,14},{11,15},{14,12},{15,13},{12,8},{... | collective-permute-start | bytes 786440 | tf_op jit(solution)/shard_map/ppermute | solution.py:272
  57.5 7.3 %collective-permute-start.14 = (bf16[64,2048]{1,0:T(8,128)(2,1)S(1)}, bf16[64,2048]{1,0:T(8,128)(2,1)S(1)}, u32[]{:S(2)}, u32[]{:S(2)}) collective-permute-start(bf16[64,2048]{1,0:T(8,128)(2,1)S(1)} %convert_element_type.85), channel_id=1, source_target_pairs={{6,2},{7,3},{10,6},{11,7},{14,10},{15,11},{12,14},{13,15},{8,12},{... | collective-permute-start | bytes 786440 | tf_op jit(solution)/shard_map/ppermute | solution.py:272
  64.8 9.3 %collective-permute-start.24 = (bf16[64,2048]{1,0:T(8,128)(2,1)S(1)}, bf16[64,2048]{1,0:T(8,128)(2,1)S(1)}, u32[]{:S(2)}, u32[]{:S(2)}) collective-permute-start(bf16[64,2048]{1,0:T(8,128)(2,1)S(1)} %convert_element_type.98), channel_id=1, source_target_pairs={{2,6},{3,7},{6,10},{7,11},{10,14},{11,15},{14,12},{15,13},{12,8},{... | collective-permute-start | bytes 786440 | tf_op jit(solution)/shard_map/ppermute | solution.py:272
  66.5 9.3 %collective-permute-start.19 = (bf16[64,2048]{1,0:T(8,128)(2,1)S(1)}, bf16[64,2048]{1,0:T(8,128)(2,1)S(1)}, u32[]{:S(2)}, u32[]{:S(2)}) collective-permute-start(bf16[64,2048]{1,0:T(8,128)(2,1)S(1)} %add_convert_fusion.9), channel_id=1, source_target_pairs={{6,2},{7,3},{10,6},{11,7},{14,10},{15,11},{12,14},{13,15},{8,12},{... | collective-permute-start | bytes 786440 | tf_op jit(solution)/shard_map/ppermute | solution.py:272
  67.0 12.8 %collective-permute-start.22 = (bf16[64,2048]{1,0:T(8,128)(2,1)S(1)}, bf16[64,2048]{1,0:T(8,128)(2,1)S(1)}, u32[]{:S(2)}, u32[]{:S(2)}) collective-permute-start(bf16[64,2048]{1,0:T(8,128)(2,1)S(1)} %add_convert_fusion.7), channel_id=1, source_target_pairs={{2,6},{3,7},{6,10},{7,11},{10,14},{11,15},{14,12},{15,13},{12,8},{... | collective-permute-start | bytes 786440 | tf_op jit(solution)/shard_map/ppermute | solution.py:272
  68.6 12.8 %collective-permute-start.28 = (bf16[64,2048]{1,0:T(8,128)(2,1)S(1)}, bf16[64,2048]{1,0:T(8,128)(2,1)S(1)}, u32[]{:S(2)}, u32[]{:S(2)}) collective-permute-start(bf16[64,2048]{1,0:T(8,128)(2,1)S(1)} %convert_element_type.105), channel_id=1, source_target_pairs={{6,2},{7,3},{10,6},{11,7},{14,10},{15,11},{12,14},{13,15},{8,12},{... | collective-permute-start | bytes 786440 | tf_op jit(solution)/shard_map/ppermute | solution.py:272
  74.2 11.2 %collective-permute-start.25 = (bf16[64,2048]{1,0:T(8,128)(2,1)S(1)}, bf16[64,2048]{1,0:T(8,128)(2,1)S(1)}, u32[]{:S(2)}, u32[]{:S(2)}) collective-permute-start(bf16[64,2048]{1,0:T(8,128)(2,1)S(1)} %add_convert_fusion.5), channel_id=1, source_target_pairs={{2,6},{3,7},{6,10},{7,11},{10,14},{11,15},{14,12},{15,13},{12,8},{... | collective-permute-start | bytes 786440 | tf_op jit(solution)/shard_map/ppermute | solution.py:272
  75.9 14.4 %collective-permute-start.20 = (bf16[64,2048]{1,0:T(8,128)(2,1)S(1)}, bf16[64,2048]{1,0:T(8,128)(2,1)S(1)}, u32[]{:S(2)}, u32[]{:S(2)}) collective-permute-start(bf16[64,2048]{1,0:T(8,128)(2,1)S(1)} %add_convert_fusion.8), channel_id=1, source_target_pairs={{6,2},{7,3},{10,6},{11,7},{14,10},{15,11},{12,14},{13,15},{8,12},{... | collective-permute-start | bytes 786440 | tf_op jit(solution)/shard_map/ppermute | solution.py:272
  79.8 18.2 %collective-permute-start.23 = (bf16[64,2048]{1,0:T(8,128)(2,1)S(1)}, bf16[64,2048]{1,0:T(8,128)(2,1)S(1)}, u32[]{:S(2)}, u32[]{:S(2)}) collective-permute-start(bf16[64,2048]{1,0:T(8,128)(2,1)S(1)} %add_convert_fusion.6), channel_id=1, source_target_pairs={{2,6},{3,7},{6,10},{7,11},{10,14},{11,15},{14,12},{15,13},{12,8},{... | collective-permute-start | bytes 786440 | tf_op jit(solution)/shard_map/ppermute | solution.py:272
  81.5 8.2 %collective-permute-start.29 = (bf16[64,2048]{1,0:T(8,128)(2,1)S(1)}, bf16[64,2048]{1,0:T(8,128)(2,1)S(1)}, u32[]{:S(2)}, u32[]{:S(2)}) collective-permute-start(bf16[64,2048]{1,0:T(8,128)(2,1)S(1)} %add_convert_fusion.2), channel_id=1, source_target_pairs={{6,2},{7,3},{10,6},{11,7},{14,10},{15,11},{12,14},{13,15},{8,12},{... | collective-permute-start | bytes 786440 | tf_op jit(solution)/shard_map/ppermute | solution.py:272
  85.4 8.3 %collective-permute-start.26 = (bf16[64,2048]{1,0:T(8,128)(2,1)S(1)}, bf16[64,2048]{1,0:T(8,128)(2,1)S(1)}, u32[]{:S(2)}, u32[]{:S(2)}) collective-permute-start(bf16[64,2048]{1,0:T(8,128)(2,1)S(1)} %add_convert_fusion.4), channel_id=1, source_target_pairs={{2,6},{3,7},{6,10},{7,11},{10,14},{11,15},{14,12},{15,13},{12,8},{... | collective-permute-start | bytes 786440 | tf_op jit(solution)/shard_map/ppermute | solution.py:272
  89.7 7.7 %collective-permute-start.30 = (bf16[64,2048]{1,0:T(8,128)(2,1)S(1)}, bf16[64,2048]{1,0:T(8,128)(2,1)S(1)}, u32[]{:S(2)}, u32[]{:S(2)}) collective-permute-start(bf16[64,2048]{1,0:T(8,128)(2,1)S(1)} %add_convert_fusion.1), channel_id=1, source_target_pairs={{6,2},{7,3},{10,6},{11,7},{14,10},{15,11},{12,14},{13,15},{8,12},{... | collective-permute-start | bytes 786440 | tf_op jit(solution)/shard_map/ppermute | solution.py:272
  93.8 6.4 %collective-permute-start.27 = (bf16[64,2048]{1,0:T(8,128)(2,1)S(1)}, bf16[64,2048]{1,0:T(8,128)(2,1)S(1)}, u32[]{:S(2)}, u32[]{:S(2)}) collective-permute-start(bf16[64,2048]{1,0:T(8,128)(2,1)S(1)} %add_convert_fusion.3), channel_id=1, source_target_pairs={{2,6},{3,7},{6,10},{7,11},{10,14},{11,15},{14,12},{15,13},{12,8},{... | collective-permute-start | bytes 786440 | tf_op jit(solution)/shard_map/ppermute | solution.py:272
  97.5 6.4 %collective-permute-start.31 = (bf16[64,2048]{1,0:T(8,128)(2,1)S(1)}, bf16[64,2048]{1,0:T(8,128)(2,1)S(1)}, u32[]{:S(2)}, u32[]{:S(2)}) collective-permute-start(bf16[64,2048]{1,0:T(8,128)(2,1)S(1)} %add_convert_fusion), channel_id=1, source_target_pairs={{6,2},{7,3},{10,6},{11,7},{14,10},{15,11},{12,14},{13,15},{8,12},{... | collective-permute-start | bytes 786440 | tf_op jit(solution)/shard_map/ppermute | solution.py:272

commit v5 on v4

--- a/solution.py
+++ b/solution.py
@@ -11,7 +11,6 @@
 LANES = 128
 CORES = 2
 MIB = 1 << 20
-HOLD = False
 
 
 def from_behind(value, axis, by):
@@ -150,16 +149,12 @@
     )(section_id, base, fresh, arrived, gain)
 
 
-def mlp_kernel(expert_ref, *refs, parts, chained, held, experts):
+def mlp_kernel(expert_ref, *refs, parts, chained, experts):
     payloads = refs[:parts]
     own, other = refs[parts : parts + 2], refs[parts + 2 : parts + 4]
     refs = refs[parts + 4 + chained :]
     outs = refs[:parts]
     refs = refs[parts:]
-    if held:
-        copy = pltpu.make_async_copy(other[0], refs[0], refs[-1])
-        copy.start()
-        refs = refs[1:-1]
     weights = (own, other)
     x_ref, coef_ref, hidden_ref = refs
     width = x_ref.shape[1]
@@ -191,30 +186,26 @@
             total += jnp.dot(rows, down[:, t : t + tile], preferred_element_type=jnp.float32)
         for here, out in zip(bounds, outs):
             out[:, t : t + tile] = total[here, :]
-    if held:
-        copy.wait()
-
-
-def expert_rows(expert_id, payloads, own, other, after, experts, hold=False):
+
+
+def expert_rows(expert_id, payloads, own, other, after, experts):
     width = own[0].shape[0]
     hidden = own[1].shape[0]
     rows = sum(p.shape[0] for p in payloads)
     vmem = pl.BlockSpec(memory_space=pltpu.VMEM)
     chain = [] if after is None else [after]
-    held = [jax.ShapeDtypeStruct(other[0].shape, other[0].dtype)] if hold else []
-    results = pl.pallas_call(
-        functools.partial(mlp_kernel, parts=len(payloads), chained=len(chain), held=hold, experts=experts),
-        out_shape=[jax.ShapeDtypeStruct((p.shape[0], width), jnp.float32) for p in payloads] + held,
+    return pl.pallas_call(
+        functools.partial(mlp_kernel, parts=len(payloads), chained=len(chain), experts=experts),
+        out_shape=[jax.ShapeDtypeStruct((p.shape[0], width), jnp.float32) for p in payloads],
         in_specs=[pl.BlockSpec(memory_space=pltpu.SMEM)]
         + [vmem] * (len(payloads) + 4)
         + [pl.BlockSpec(memory_space=pl.ANY)] * len(chain),
-        out_specs=[vmem] * (len(payloads) + len(held)),
+        out_specs=[vmem] * len(payloads),
         scratch_shapes=[
             pltpu.VMEM((rows, width), jnp.bfloat16),
             pltpu.VMEM((2, rows, LANES), jnp.float32),
             pltpu.VMEM((rows, 2 * hidden), jnp.bfloat16),
-        ]
-        + ([pltpu.SemaphoreType.DMA] if hold else []),
+        ],
         compiler_params=pltpu.CompilerParams(vmem_limit_bytes=16 * MIB),
         cost_estimate=pl.CostEstimate(
             flops=2 * rows * width * hidden * 6,
@@ -223,7 +214,6 @@
         ),
         name="expert_rows",
     )(expert_id, *payloads, *own, *other, *chain)
-    return (results[:-1], results[-1]) if hold else results
 
 
 def last_kernel(near0_ref, near1_ref, total0_ref, total1_ref, out_ref):
@@ -272,11 +262,11 @@
         return lax.ppermute(value, "expert", pairs)
 
     cuts = [slice(0, half), slice(half, rows)]
-    arrived = [from_behind(previous[0, cut], "section", 1) for cut in cuts]
     own = (w_gate_up[0, 0], w_down[0, 0])
     swapped = lax.optimization_barrier((*own, section_id, expert_id))[:2]
     other = tuple(move(w, swap) for w in swapped)
     base, fresh, gain = base_rows(fresh, norm_gain, routes[0].T, gate_weights[0].T, devices_exp)
+    arrived = [from_behind(previous[0, cut], "section", 1) for cut in cuts]
     packed, arrival = zip(*(norm_rows(section_id, base, fresh, arrived[c], gain, cuts[c].start) for c in range(2)))
     packed = list(packed)
 
@@ -293,44 +283,48 @@
 
     last = None
 
-    def mlp(payloads, hold=False):
-        nonlocal last, other
-        sums = expert_rows(expert_id, payloads, own, other, last, devices_exp, hold)
-        if hold:
-            sums, other_gate_up = sums
-            other = (other_gate_up, other[1])
+    def mlp(payloads):
+        nonlocal last
+        sums = expert_rows(expert_id, payloads, own, other, last, devices_exp)
         last = sums[0]
         return sums
 
     to_down, to_up = {}, {}
     pass_on(0, 0, None)
     pass_on(0, 1, None)
-    own_sums = mlp(packed, HOLD)
     for s in range(1, hops):
         for c in range(2):
             pass_on(s, c, last)
             to_down[s, c], to_up[s, c] = mlp([ups[s][c], downs[s][c]])
     to_up[hops, 0], to_down[hops, 1] = mlp([ups[hops][0], downs[hops][1]])
-
-    flows = [(to_down, 0, down), (to_up, 1, up), (to_up, 0, up), (to_down, 1, down)]
-    totals = [None] * len(flows)
-    for s in reversed(range(1, hops + 1)):
-        for i, (terms, c, pairs) in enumerate(flows):
-            place = s if (hops, c) in terms else s - 1
-            if place == 0:
-                continue
-            if totals[i] is None:
-                total = terms[place, c]
-            else:
-                carried = lax.optimization_barrier((totals[i], last))[0]
-                total = terms[place, c] + carried.astype(jnp.float32)
-            totals[i] = move(total.astype(jnp.bfloat16), pairs)
+    own_sums = mlp(packed)
+
+    def send_on(flow, place, total, after):
+        terms, c, pairs = flow
+        if total is None:
+            total = terms[place, c]
+        else:
+            carried = lax.optimization_barrier((total, after))[0]
+            total = terms[place, c] + carried.astype(jnp.float32)
+        total = total.astype(jnp.bfloat16)
+        return total, move(total, pairs)
+
+    short = [(to_down, 0, down), (to_up, 1, up)]
+    long = [(to_up, 0, up), (to_down, 1, down)]
+    short_totals = [send_on(flow, hops - 1, None, None)[1] for flow in short]
+    long_totals = [send_on(flow, hops, None, None)[1] for flow in long]
+    after = to_up[hops, 0]
+    for s in reversed(range(1, hops)):
+        if s > 1:
+            sent, short_totals = zip(*(send_on(f, s - 1, t, after) for f, t in zip(short, short_totals)))
+        sent, long_totals = zip(*(send_on(f, s, t, sent) for f, t in zip(long, long_totals)))
+        after = sent
 
     nears = [
-        arrival[c].astype(jnp.float32) + (own_sums[c] + totals[c].astype(jnp.float32)) for c in range(2)
+        arrival[c].astype(jnp.float32) + (own_sums[c] + short_totals[c].astype(jnp.float32)) for c in range(2)
     ]
     nears = lax.optimization_barrier(nears)
-    return last_rows(nears, totals[2:])[None]
+    return last_rows(nears, long_totals)[None]
 
 
 def solution(mesh):

time: 105 us -> 109 us (1.038)
  starting transfers between devices: 37.3 us -> 39.2 us
  waiting for transfers between devices: 35.3 us -> 36.4 us
    ppermute x2, starting transfers between devices: 6.18 us -> 9.39 us  [from_behind(): return lax.ppermute(value, axis, pairs)]
    ppermute x2, waiting for transfers between devices: 4.5 us -> 6.32 us  [from_behind(): return lax.ppermute(value, axis, pairs)]
    ppermute x30, starting transfers between devices: 31.1 us -> 29.8 us  [move(): return lax.ppermute(value, 'expert', pairs)]
  transfers between devices with their start and end apart: 32 -> 32, of which waited for: 17 -> 16; matrix products, arithmetic and copies ran while one was open for 2% -> 2% of each run, Pallas kernels for 22% -> 21%
where the time goes in v5:
time: 109 us; the launch traced here: 108 us
  starting transfers between devices  39.2 us (36%)
  waiting for transfers between devices  36.4 us (33%)
  Pallas kernels  23.9 us (22%)
  local copies, waits for them, and re-layouts  7.22 us (7%)
    ppermute x30, waiting for transfers between devices, move(): return lax.ppermute(value, 'expert', pairs)  30.1 us
    ppermute x30, starting transfers between devices, move(): return lax.ppermute(value, 'expert', pairs)  29.8 us
    pallas_call x8, Pallas kernels, expert_rows(): pl.pallas_call(functools.partial(mlp_kernel, parts=len(payloads), chained...  22.7 us
    ppermute x2, starting transfers between devices, from_behind(): return lax.ppermute(value, axis, pairs)  9.39 us
    ppermute x2, waiting for transfers between devices, from_behind(): return lax.ppermute(value, axis, pairs)  6.32 us
    unnamed x12, local copies, waits for them, and re-layouts  5.9 us
  transfers between devices with their start and end apart: 32, of which 16 were waited for; matrix products, arithmetic and copies ran while one was open for 2% of the time, Pallas kernels for 21%

profile of v5, /device:TPU:0, one launch (start us, length us, event | category | flops | bytes accessed | tf_op | source)
XLA Modules:
  0.0 107.8 jit_solution(12208428765780122479)
XLA Ops:
  0.0 0.5 collective-permute-start.2
  0.5 1.3 %slice_bitcast_fusion = (bf16[64,2048]{1,0:T(8,128)(2,1)S(1)}, bf16[64,2048]{1,0:T(8,128)(2,1)S(1)}) fusion(bf16[1,128,2048]{2,1,0:T(8,128)(2,1)} %param.8), kind=kLoop, calls=%fused_computation.12 | loop fusion | bytes 1048576 | tf_op jit(solution)/shard_map/squeeze | solution.py:269
  1.8 4.9 %collective-permute-start = (bf16[64,2048]{1,0:T(8,128)(2,1)S(1)}, bf16[64,2048]{1,0:T(8,128)(2,1)S(1)}, u32[]{:S(2)}, u32[]{:S(2)}) collective-permute-start(bf16[64,2048]{1,0:T(8,128)(2,1)S(1)} %get-tuple-element.108), channel_id=1, source_target_pairs={{0,16},{1,17},{2,18},{3,19},{4,20},{5,21},{6,22},{7,23},{8,24},{9,... | collective-permute-start | bytes 786440 | tf_op jit(solution)/shard_map/ppermute | solution.py:19
  6.7 1.0 copy-done.2
  7.8 0.7 copy-done.3
  8.5 0.7 copy-done.4
  9.2 0.7 copy-done.5
  9.8 0.3 base_rows.1
  10.1 2.3 %collective-permute-done.arrived_ref = bf16[64,2048]{1,0:T(8,128)(2,1)S(1)} collective-permute-done((bf16[64,2048]{1,0:T(8,128)(2,1)S(1)}, bf16[64,2048]{1,0:T(8,128)(2,1)S(1)}, u32[]{:S(2)}, u32[]{:S(2)}) %collective-permute-start) | collective-permute-done | bytes 262176 | tf_op jit(solution)/shard_map/ppermute | solution.py:19
  12.5 1.5 %collective-permute-start.4 = (bf16[64,2176]{1,0:T(8,128)(2,1)S(1)}, bf16[64,2176]{1,0:T(8,128)(2,1)S(1)}, u32[]{:S(2)}, u32[]{:S(2)}) collective-permute-start(bf16[64,2176]{1,0:T(8,128)(2,1)S(1)} %get-tuple-element.65.refs_0_), channel_id=1, source_target_pairs={{2,6},{3,7},{6,10},{7,11},{10,14},{11,15},{14,12},{15,13},{12,8},{... | collective-permute-start | bytes 835592 | tf_op jit(solution)/shard_map/ppermute | solution.py:262
  14.0 4.5 %collective-permute-start.1 = (bf16[64,2048]{1,0:T(8,128)(2,1)S(1)}, bf16[64,2048]{1,0:T(8,128)(2,1)S(1)}, u32[]{:S(2)}, u32[]{:S(2)}) collective-permute-start(bf16[64,2048]{1,0:T(8,128)(2,1)S(1)} %get-tuple-element.107), channel_id=1, source_target_pairs={{0,16},{1,17},{2,18},{3,19},{4,20},{5,21},{6,22},{7,23},{8,24},{9,... | collective-permute-start | bytes 786440 | tf_op jit(solution)/shard_map/ppermute | solution.py:19
  18.6 0.6 collective-permute-start.5
  19.1 4.0 %collective-permute-done.1.arrived_ref = bf16[64,2048]{1,0:T(8,128)(2,1)S(1)} collective-permute-done((bf16[64,2048]{1,0:T(8,128)(2,1)S(1)}, bf16[64,2048]{1,0:T(8,128)(2,1)S(1)}, u32[]{:S(2)}, u32[]{:S(2)}) %collective-permute-start.1) | collective-permute-done | bytes 262176 | tf_op jit(solution)/shard_map/ppermute | solution.py:19
  23.2 1.6 %collective-permute-start.8 = (bf16[64,2176]{1,0:T(8,128)(2,1)S(1)}, bf16[64,2176]{1,0:T(8,128)(2,1)S(1)}, u32[]{:S(2)}, u32[]{:S(2)}) collective-permute-start(bf16[64,2176]{1,0:T(8,128)(2,1)S(1)} %get-tuple-element.69.refs_1_), channel_id=1, source_target_pairs={{2,6},{3,7},{6,10},{7,11},{10,14},{11,15},{14,12},{15,13},{12,8},{... | collective-permute-start | bytes 835592 | tf_op jit(solution)/shard_map/ppermute | solution.py:262
  24.8 0.5 collective-permute-start.9
  25.3 1.1 %collective-permute-done.5.refs_1_ = bf16[64,2176]{1,0:T(8,128)(2,1)S(1)} collective-permute-done((bf16[64,2176]{1,0:T(8,128)(2,1)S(1)}, bf16[64,2176]{1,0:T(8,128)(2,1)S(1)}, u32[]{:S(2)}, u32[]{:S(2)}) %collective-permute-start.5) | collective-permute-done | bytes 278560 | tf_op jit(solution)/shard_map/ppermute | solution.py:262
  26.4 1.6 %collective-permute-start.6 = (bf16[64,2176]{1,0:T(8,128)(2,1)S(1)}, bf16[64,2176]{1,0:T(8,128)(2,1)S(1)}, u32[]{:S(2)}, u32[]{:S(2)}) collective-permute-start(bf16[64,2176]{1,0:T(8,128)(2,1)S(1)} %collective-permute-done.4.refs_0_), channel_id=1, source_target_pairs={{2,6},{3,7},{6,10},{7,11},{10,14},{11,15},{14,12},{15,13},{12,8},{... | collective-permute-start | bytes 835592 | tf_op jit(solution)/shard_map/ppermute | solution.py:262
  28.0 0.5 collective-permute-start.7
  28.4 2.8 %copy-done = bf16[1,1,2048,1536]{3,2,1,0:T(8,128)(2,1)S(1)} copy-done((bf16[1,1,2048,1536]{3,2,1,0:T(8,128)(2,1)S(1)}, bf16[1,1,2048,1536]{3,2,1,0:T(8,128)(2,1)}, u32[]{:S(2)}) %copy-start) | copy-done | bytes 6291480
  31.2 2.8 %expert_rows.8 = (f32[64,2048]{1,0:T(8,128)S(1)}, f32[64,2048]{1,0:T(8,128)S(1)}) custom-call(s32[1]{0:T(128)} %bitcast.6.expert_ref, bf16[64,2176]{1,0:T(8,128)(2,1)S(1)} %collective-permute-done.4.refs_0_, bf16[64,2176]{1,0:T(8,128)(2,1)S(1)} %collective-permute-done.5.refs_1_, bf16[2048,1536]{1,0:T(8,128)(2,1)S(1)} %bitcast.16, ...), custom_call_target="tpu_custom_call" | custom-call | flops 2415919104 | bytes 1572864 | tf_op jit(solution)/shard_map/expert_rows/pallas_call | solution.py:197
  34.1 0.4 collective-permute-done.9.refs_1_
  34.4 1.6 %collective-permute-start.12 = (bf16[64,2176]{1,0:T(8,128)(2,1)S(1)}, bf16[64,2176]{1,0:T(8,128)(2,1)S(1)}, u32[]{:S(2)}, u32[]{:S(2)}) collective-permute-start(bf16[64,2176]{1,0:T(8,128)(2,1)S(1)} %collective-permute-done.8.refs_0_), channel_id=1, source_target_pairs={{2,6},{3,7},{6,10},{7,11},{10,14},{11,15},{14,12},{15,13},{12,8},{... | collective-permute-start | bytes 835592 | tf_op jit(solution)/shard_map/ppermute | solution.py:262
  36.0 0.4 collective-permute-start.13
  36.4 2.8 %expert_rows.9 = (f32[64,2048]{1,0:T(8,128)S(1)}, f32[64,2048]{1,0:T(8,128)S(1)}) custom-call(s32[1]{0:T(128)} %bitcast.6.expert_ref, bf16[64,2176]{1,0:T(8,128)(2,1)S(1)} %collective-permute-done.8.refs_0_, bf16[64,2176]{1,0:T(8,128)(2,1)S(1)} %collective-permute-done.9.refs_1_, bf16[2048,1536]{1,0:T(8,128)(2,1)S(1)} %bitcast.17, ...), custom_call_target="tpu_custom_call" | custom-call | flops 2415919104 | bytes 1572864 | tf_op jit(solution)/shard_map/expert_rows/pallas_call | solution.py:197
  39.3 1.1 %collective-permute-done.7.refs_1_ = bf16[64,2176]{1,0:T(8,128)(2,1)S(1)} collective-permute-done((bf16[64,2176]{1,0:T(8,128)(2,1)S(1)}, bf16[64,2176]{1,0:T(8,128)(2,1)S(1)}, u32[]{:S(2)}, u32[]{:S(2)}) %collective-permute-start.7) | collective-permute-done | bytes 278560 | tf_op jit(solution)/shard_map/ppermute | solution.py:262
  40.4 1.6 %collective-permute-start.10 = (bf16[64,2176]{1,0:T(8,128)(2,1)S(1)}, bf16[64,2176]{1,0:T(8,128)(2,1)S(1)}, u32[]{:S(2)}, u32[]{:S(2)}) collective-permute-start(bf16[64,2176]{1,0:T(8,128)(2,1)S(1)} %collective-permute-done.6.refs_0_), channel_id=1, source_target_pairs={{2,6},{3,7},{6,10},{7,11},{10,14},{11,15},{14,12},{15,13},{12,8},{... | collective-permute-start | bytes 835592 | tf_op jit(solution)/shard_map/ppermute | solution.py:262
  42.0 0.4 collective-permute-start.11
  42.4 2.8 %expert_rows.10 = (f32[64,2048]{1,0:T(8,128)S(1)}, f32[64,2048]{1,0:T(8,128)S(1)}) custom-call(s32[1]{0:T(128)} %bitcast.6.expert_ref, bf16[64,2176]{1,0:T(8,128)(2,1)S(1)} %collective-permute-done.6.refs_0_, bf16[64,2176]{1,0:T(8,128)(2,1)S(1)} %collective-permute-done.7.refs_1_, bf16[2048,1536]{1,0:T(8,128)(2,1)S(1)} %bitcast.18, ...), custom_call_target="tpu_custom_call" | custom-call | flops 2415919104 | bytes 1572864 | tf_op jit(solution)/shard_map/expert_rows/pallas_call | solution.py:197
  45.3 1.1 %collective-permute-done.13.refs_1_ = bf16[64,2176]{1,0:T(8,128)(2,1)S(1)} collective-permute-done((bf16[64,2176]{1,0:T(8,128)(2,1)S(1)}, bf16[64,2176]{1,0:T(8,128)(2,1)S(1)}, u32[]{:S(2)}, u32[]{:S(2)}) %collective-permute-start.13) | collective-permute-done | bytes 278560 | tf_op jit(solution)/shard_map/ppermute | solution.py:262
  46.3 1.6 %collective-permute-start.15 = (bf16[64,2176]{1,0:T(8,128)(2,1)S(1)}, bf16[64,2176]{1,0:T(8,128)(2,1)S(1)}, u32[]{:S(2)}, u32[]{:S(2)}) collective-permute-start(bf16[64,2176]{1,0:T(8,128)(2,1)S(1)} %collective-permute-done.12.refs_0_), channel_id=1, source_target_pairs={{2,6},{3,7},{6,10},{7,11},{10,14},{11,15},{14,12},{15,13},{12,8},{... | collective-permute-start | bytes 835592 | tf_op jit(solution)/shard_map/ppermute | solution.py:262
  47.9 0.5 collective-permute-start.16
  48.4 2.8 %expert_rows.11 = (f32[64,2048]{1,0:T(8,128)S(1)}, f32[64,2048]{1,0:T(8,128)S(1)}) custom-call(s32[1]{0:T(128)} %bitcast.6.expert_ref, bf16[64,2176]{1,0:T(8,128)(2,1)S(1)} %collective-permute-done.12.refs_0_, bf16[64,2176]{1,0:T(8,128)(2,1)S(1)} %collective-permute-done.13.refs_1_, bf16[2048,1536]{1,0:T(8,128)(2,1)S(1)} %bitcast.19, ...), custom_call_target="tpu_custom_call" | custom-call | flops 2415919104 | bytes 1572864 | tf_op jit(solution)/shard_map/expert_rows/pallas_call | solution.py:197
  51.2 1.1 %collective-permute-done.11.refs_1_ = bf16[64,2176]{1,0:T(8,128)(2,1)S(1)} collective-permute-done((bf16[64,2176]{1,0:T(8,128)(2,1)S(1)}, bf16[64,2176]{1,0:T(8,128)(2,1)S(1)}, u32[]{:S(2)}, u32[]{:S(2)}) %collective-permute-start.11) | collective-permute-done | bytes 278560 | tf_op jit(solution)/shard_map/ppermute | solution.py:262
  52.3 1.6 %collective-permute-start.14 = (bf16[64,2176]{1,0:T(8,128)(2,1)S(1)}, bf16[64,2176]{1,0:T(8,128)(2,1)S(1)}, u32[]{:S(2)}, u32[]{:S(2)}) collective-permute-start(bf16[64,2176]{1,0:T(8,128)(2,1)S(1)} %collective-permute-done.10.refs_0_), channel_id=1, source_target_pairs={{2,6},{3,7},{6,10},{7,11},{10,14},{11,15},{14,12},{15,13},{12,8},{... | collective-permute-start | bytes 835592 | tf_op jit(solution)/shard_map/ppermute | solution.py:262
  53.9 2.8 %expert_rows.12 = (f32[64,2048]{1,0:T(8,128)S(1)}, f32[64,2048]{1,0:T(8,128)S(1)}) custom-call(s32[1]{0:T(128)} %bitcast.6.expert_ref, bf16[64,2176]{1,0:T(8,128)(2,1)S(1)} %collective-permute-done.10.refs_0_, bf16[64,2176]{1,0:T(8,128)(2,1)S(1)} %collective-permute-done.11.refs_1_, bf16[2048,1536]{1,0:T(8,128)(2,1)S(1)} %bitcast.20, ...), custom_call_target="tpu_custom_call" | custom-call | flops 2415919104 | bytes 1572864 | tf_op jit(solution)/shard_map/expert_rows/pallas_call | solution.py:197
  56.8 0.5 collective-permute-start.17
  57.3 2.8 %expert_rows.13 = (f32[64,2048]{1,0:T(8,128)S(1)}, f32[64,2048]{1,0:T(8,128)S(1)}) custom-call(s32[1]{0:T(128)} %bitcast.6.expert_ref, bf16[64,2176]{1,0:T(8,128)(2,1)S(1)} %collective-permute-done.15.refs_0_, bf16[64,2176]{1,0:T(8,128)(2,1)S(1)} %collective-permute-done.16.refs_1_, bf16[2048,1536]{1,0:T(8,128)(2,1)S(1)} %bitcast.21, ...), custom_call_target="tpu_custom_call" | custom-call | flops 2415919104 | bytes 1572864 | tf_op jit(solution)/shard_map/expert_rows/pallas_call | solution.py:197
  60.1 1.6 %collective-permute-start.21 = (bf16[64,2048]{1,0:T(8,128)(2,1)S(1)}, bf16[64,2048]{1,0:T(8,128)(2,1)S(1)}, u32[]{:S(2)}, u32[]{:S(2)}) collective-permute-start(bf16[64,2048]{1,0:T(8,128)(2,1)S(1)} %convert_element_type.89), channel_id=1, source_target_pairs={{2,6},{3,7},{6,10},{7,11},{10,14},{11,15},{14,12},{15,13},{12,8},{... | collective-permute-start | bytes 786440 | tf_op jit(solution)/shard_map/ppermute | solution.py:262
  61.8 0.5 collective-permute-start.18
  62.3 3.6 %collective-permute-done.17.refs_1_ = bf16[64,2176]{1,0:T(8,128)(2,1)S(1)} collective-permute-done((bf16[64,2176]{1,0:T(8,128)(2,1)S(1)}, bf16[64,2176]{1,0:T(8,128)(2,1)S(1)}, u32[]{:S(2)}, u32[]{:S(2)}) %collective-permute-start.17) | collective-permute-done | bytes 278560 | tf_op jit(solution)/shard_map/ppermute | solution.py:262
  65.9 2.8 %expert_rows.14 = (f32[64,2048]{1,0:T(8,128)S(1)}, f32[64,2048]{1,0:T(8,128)S(1)}) custom-call(s32[1]{0:T(128)} %bitcast.6.expert_ref, bf16[64,2176]{1,0:T(8,128)(2,1)S(1)} %collective-permute-done.14.refs_0_, bf16[64,2176]{1,0:T(8,128)(2,1)S(1)} %collective-permute-done.17.refs_1_, bf16[2048,1536]{1,0:T(8,128)(2,1)S(1)} %bitcast.22, ...), custom_call_target="tpu_custom_call" | custom-call | flops 2415919104 | bytes 1572864 | tf_op jit(solution)/shard_map/expert_rows/pallas_call | solution.py:197
  68.9 1.7 %collective-permute-start.20 = (bf16[64,2048]{1,0:T(8,128)(2,1)S(1)}, bf16[64,2048]{1,0:T(8,128)(2,1)S(1)}, u32[]{:S(2)}, u32[]{:S(2)}) collective-permute-start(bf16[64,2048]{1,0:T(8,128)(2,1)S(1)} %convert_element_type.88), channel_id=1, source_target_pairs={{2,6},{3,7},{6,10},{7,11},{10,14},{11,15},{14,12},{15,13},{12,8},{... | collective-permute-start | bytes 786440 | tf_op jit(solution)/shard_map/ppermute | solution.py:262
  70.7 0.3 collective-permute-start.19
  71.0 0.6 collective-permute-start.22
  71.6 1.7 %collective-permute-start.24 = (bf16[64,2048]{1,0:T(8,128)(2,1)S(1)}, bf16[64,2048]{1,0:T(8,128)(2,1)S(1)}, u32[]{:S(2)}, u32[]{:S(2)}) collective-permute-start(bf16[64,2048]{1,0:T(8,128)(2,1)S(1)} %add_convert_fusion.8), channel_id=1, source_target_pairs={{2,6},{3,7},{6,10},{7,11},{10,14},{11,15},{14,12},{15,13},{12,8},{... | collective-permute-start | bytes 786440 | tf_op jit(solution)/shard_map/ppermute | solution.py:262
  73.3 2.8 %expert_rows.15 = (f32[64,2048]{1,0:T(8,128)S(1)}, f32[64,2048]{1,0:T(8,128)S(1)}) custom-call(s32[1]{0:T(128)} %bitcast.6.expert_ref, bf16[64,2176]{1,0:T(8,128)(2,1)S(1)} %get-tuple-element.65.refs_0_, bf16[64,2176]{1,0:T(8,128)(2,1)S(1)} %get-tuple-element.69.refs_1_, bf16[2048,1536]{1,0:T(8,128)(2,1)S(1)} %bitcast.23, bf16[768,2048]{1,0:T(8,128)(2,1)S(1)} %bitcast.32, ...), custom_call_target="tpu_custom_call" | custom-call | flops 2415919104 | bytes 1572864 | tf_op jit(solution)/shard_map/expert_rows/pallas_call | solution.py:197
  76.2 0.9 collective-permute-done.20
  77.0 5.1 %collective-permute-done.22 = bf16[64,2048]{1,0:T(8,128)(2,1)S(1)} collective-permute-done((bf16[64,2048]{1,0:T(8,128)(2,1)S(1)}, bf16[64,2048]{1,0:T(8,128)(2,1)S(1)}, u32[]{:S(2)}, u32[]{:S(2)}) %collective-permute-start.22) | collective-permute-done | bytes 262176 | tf_op jit(solution)/shard_map/ppermute | solution.py:262
  82.1 0.1 add_convert_fusion.6
  82.2 0.8 collective-permute-start.28
  83.0 1.3 %collective-permute-start.26 = (bf16[64,2048]{1,0:T(8,128)(2,1)S(1)}, bf16[64,2048]{1,0:T(8,128)(2,1)S(1)}, u32[]{:S(2)}, u32[]{:S(2)}) collective-permute-start(bf16[64,2048]{1,0:T(8,128)(2,1)S(1)} %get-tuple-element.110), channel_id=1, source_target_pairs={{2,6},{3,7},{6,10},{7,11},{10,14},{11,15},{14,12},{15,13},{12,8},{... | collective-permute-start | bytes 786440 | tf_op jit(solution)/shard_map/ppermute | solution.py:262
  84.4 0.8 collective-permute-start.23
  85.2 1.4 %collective-permute-start.25 = (bf16[64,2048]{1,0:T(8,128)(2,1)S(1)}, bf16[64,2048]{1,0:T(8,128)(2,1)S(1)}, u32[]{:S(2)}, u32[]{:S(2)}) collective-permute-start(bf16[64,2048]{1,0:T(8,128)(2,1)S(1)} %add_convert_fusion.4), channel_id=1, source_target_pairs={{2,6},{3,7},{6,10},{7,11},{10,14},{11,15},{14,12},{15,13},{12,8},{... | collective-permute-start | bytes 786440 | tf_op jit(solution)/shard_map/ppermute | solution.py:262
  86.6 5.0 %collective-permute-done.28 = bf16[64,2048]{1,0:T(8,128)(2,1)S(1)} collective-permute-done((bf16[64,2048]{1,0:T(8,128)(2,1)S(1)}, bf16[64,2048]{1,0:T(8,128)(2,1)S(1)}, u32[]{:S(2)}, u32[]{:S(2)}) %collective-permute-start.28) | collective-permute-done | bytes 262176 | tf_op jit(solution)/shard_map/ppermute | solution.py:262
  91.6 0.8 collective-permute-start.30
  92.4 1.4 %collective-permute-start.27 = (bf16[64,2048]{1,0:T(8,128)(2,1)S(1)}, bf16[64,2048]{1,0:T(8,128)(2,1)S(1)}, u32[]{:S(2)}, u32[]{:S(2)}) collective-permute-start(bf16[64,2048]{1,0:T(8,128)(2,1)S(1)} %add_convert_fusion.3), channel_id=1, source_target_pairs={{2,6},{3,7},{6,10},{7,11},{10,14},{11,15},{14,12},{15,13},{12,8},{... | collective-permute-start | bytes 786440 | tf_op jit(solution)/shard_map/ppermute | solution.py:262
  93.8 2.0 %collective-permute-done.23 = bf16[64,2048]{1,0:T(8,128)(2,1)S(1)} collective-permute-done((bf16[64,2048]{1,0:T(8,128)(2,1)S(1)}, bf16[64,2048]{1,0:T(8,128)(2,1)S(1)}, u32[]{:S(2)}, u32[]{:S(2)}) %collective-permute-start.23) | collective-permute-done | bytes 262176 | tf_op jit(solution)/shard_map/ppermute | solution.py:262
  95.8 4.1 %collective-permute-done.30 = bf16[64,2048]{1,0:T(8,128)(2,1)S(1)} collective-permute-done((bf16[64,2048]{1,0:T(8,128)(2,1)S(1)}, bf16[64,2048]{1,0:T(8,128)(2,1)S(1)}, u32[]{:S(2)}, u32[]{:S(2)}) %collective-permute-start.30) | collective-permute-done | bytes 262176 | tf_op jit(solution)/shard_map/ppermute | solution.py:262
  99.9 0.3 collective-permute-start.31
  100.3 0.1 collective-permute-done.27
  100.4 1.7 %collective-permute-start.29 = (bf16[64,2048]{1,0:T(8,128)(2,1)S(1)}, bf16[64,2048]{1,0:T(8,128)(2,1)S(1)}, u32[]{:S(2)}, u32[]{:S(2)}) collective-permute-start(bf16[64,2048]{1,0:T(8,128)(2,1)S(1)} %add_convert_fusion.1), channel_id=1, source_target_pairs={{2,6},{3,7},{6,10},{7,11},{10,14},{11,15},{14,12},{15,13},{12,8},{... | collective-permute-start | bytes 786440 | tf_op jit(solution)/shard_map/ppermute | solution.py:262
  102.2 4.2 %collective-permute-done.31.total1_ref = bf16[64,2048]{1,0:T(8,128)(2,1)S(1)} collective-permute-done((bf16[64,2048]{1,0:T(8,128)(2,1)S(1)}, bf16[64,2048]{1,0:T(8,128)(2,1)S(1)}, u32[]{:S(2)}, u32[]{:S(2)}) %collective-permute-start.31) | collective-permute-done | bytes 262176 | tf_op jit(solution)/shard_map/ppermute | solution.py:262
  106.4 0.5 collective-permute-done.29.total0_ref
  106.9 0.9 last_rows.1
  (40 shorter events, 0.8 us)
Async XLA Ops:
  0.0 28.4 %copy-start.1 = (bf16[1,1,768,2048]{3,2,1,0:T(8,128)(2,1)S(1)}, bf16[1,1,768,2048]{3,2,1,0:T(8,128)(2,1)}, u32[]{:S(2)}) copy-start(bf16[1,1,768,2048]{3,2,1,0:T(8,128)(2,1)} %param.13) | copy-start | bytes 9437188
  0.0 28.4 %collective-permute-start.2 = (bf16[2048,1536]{1,0:T(8,128)(2,1)}, bf16[2048,1536]{1,0:T(8,128)(2,1)S(1)}, u32[]{:S(2)}, u32[]{:S(2)}) collective-permute-start(bf16[2048,1536]{1,0:T(8,128)(2,1)} %bitcast.15), channel_id=1, source_target_pairs={{0,1},{1,0},{2,3},{3,2},{4,5},{5,4},{6,7},{7,6},{8,9},{9,8},{10,11... | collective-permute-start | bytes 18874376 | tf_op jit(solution)/shard_map/ppermute | solution.py:262
  0.5 27.5 %collective-permute-start.3 = (bf16[768,2048]{1,0:T(8,128)(2,1)}, bf16[768,2048]{1,0:T(8,128)(2,1)S(1)}, u32[]{:S(2)}, u32[]{:S(2)}) collective-permute-start(bf16[768,2048]{1,0:T(8,128)(2,1)} %bitcast.24), channel_id=1, source_target_pairs={{0,1},{1,0},{2,3},{3,2},{4,5},{5,4},{6,7},{7,6},{8,9},{9,8},{10,11... | collective-permute-start | bytes 9437192 | tf_op jit(solution)/shard_map/ppermute | solution.py:262
  1.8 10.6 %collective-permute-start = (bf16[64,2048]{1,0:T(8,128)(2,1)S(1)}, bf16[64,2048]{1,0:T(8,128)(2,1)S(1)}, u32[]{:S(2)}, u32[]{:S(2)}) collective-permute-start(bf16[64,2048]{1,0:T(8,128)(2,1)S(1)} %get-tuple-element.108), channel_id=1, source_target_pairs={{0,16},{1,17},{2,18},{3,19},{4,20},{5,21},{6,22},{7,23},{8,24},{9,... | collective-permute-start | bytes 786440 | tf_op jit(solution)/shard_map/ppermute | solution.py:19
  6.7 1.0 copy-start.2
  7.8 0.7 copy-start.3
  8.5 0.7 copy-start.4
  9.2 0.7 copy-start.5
  12.5 12.3 %collective-permute-start.4 = (bf16[64,2176]{1,0:T(8,128)(2,1)S(1)}, bf16[64,2176]{1,0:T(8,128)(2,1)S(1)}, u32[]{:S(2)}, u32[]{:S(2)}) collective-permute-start(bf16[64,2176]{1,0:T(8,128)(2,1)S(1)} %get-tuple-element.65.refs_0_), channel_id=1, source_target_pairs={{2,6},{3,7},{6,10},{7,11},{10,14},{11,15},{14,12},{15,13},{12,8},{... | collective-permute-start | bytes 835592 | tf_op jit(solution)/shard_map/ppermute | solution.py:262
  14.0 9.1 %collective-permute-start.1 = (bf16[64,2048]{1,0:T(8,128)(2,1)S(1)}, bf16[64,2048]{1,0:T(8,128)(2,1)S(1)}, u32[]{:S(2)}, u32[]{:S(2)}) collective-permute-start(bf16[64,2048]{1,0:T(8,128)(2,1)S(1)} %get-tuple-element.107), channel_id=1, source_target_pairs={{0,16},{1,17},{2,18},{3,19},{4,20},{5,21},{6,22},{7,23},{8,24},{9,... | collective-permute-start | bytes 786440 | tf_op jit(solution)/shard_map/ppermute | solution.py:19
  18.6 7.8 %collective-permute-start.5 = (bf16[64,2176]{1,0:T(8,128)(2,1)S(1)}, bf16[64,2176]{1,0:T(8,128)(2,1)S(1)}, u32[]{:S(2)}, u32[]{:S(2)}) collective-permute-start(bf16[64,2176]{1,0:T(8,128)(2,1)S(1)} %get-tuple-element.65.refs_0_), channel_id=1, source_target_pairs={{6,2},{7,3},{10,6},{11,7},{14,10},{15,11},{12,14},{13,15},{8,12},{... | collective-permute-start | bytes 835592 | tf_op jit(solution)/shard_map/ppermute | solution.py:262
  23.2 10.9 %collective-permute-start.8 = (bf16[64,2176]{1,0:T(8,128)(2,1)S(1)}, bf16[64,2176]{1,0:T(8,128)(2,1)S(1)}, u32[]{:S(2)}, u32[]{:S(2)}) collective-permute-start(bf16[64,2176]{1,0:T(8,128)(2,1)S(1)} %get-tuple-element.69.refs_1_), channel_id=1, source_target_pairs={{2,6},{3,7},{6,10},{7,11},{10,14},{11,15},{14,12},{15,13},{12,8},{... | collective-permute-start | bytes 835592 | tf_op jit(solution)/shard_map/ppermute | solution.py:262
  24.8 9.6 %collective-permute-start.9 = (bf16[64,2176]{1,0:T(8,128)(2,1)S(1)}, bf16[64,2176]{1,0:T(8,128)(2,1)S(1)}, u32[]{:S(2)}, u32[]{:S(2)}) collective-permute-start(bf16[64,2176]{1,0:T(8,128)(2,1)S(1)} %get-tuple-element.69.refs_1_), channel_id=1, source_target_pairs={{6,2},{7,3},{10,6},{11,7},{14,10},{15,11},{12,14},{13,15},{8,12},{... | collective-permute-start | bytes 835592 | tf_op jit(solution)/shard_map/ppermute | solution.py:262
  26.4 12.9 %collective-permute-start.6 = (bf16[64,2176]{1,0:T(8,128)(2,1)S(1)}, bf16[64,2176]{1,0:T(8,128)(2,1)S(1)}, u32[]{:S(2)}, u32[]{:S(2)}) collective-permute-start(bf16[64,2176]{1,0:T(8,128)(2,1)S(1)} %collective-permute-done.4.refs_0_), channel_id=1, source_target_pairs={{2,6},{3,7},{6,10},{7,11},{10,14},{11,15},{14,12},{15,13},{12,8},{... | collective-permute-start | bytes 835592 | tf_op jit(solution)/shard_map/ppermute | solution.py:262
  28.0 12.4 %collective-permute-start.7 = (bf16[64,2176]{1,0:T(8,128)(2,1)S(1)}, bf16[64,2176]{1,0:T(8,128)(2,1)S(1)}, u32[]{:S(2)}, u32[]{:S(2)}) collective-permute-start(bf16[64,2176]{1,0:T(8,128)(2,1)S(1)} %collective-permute-done.5.refs_1_), channel_id=1, source_target_pairs={{6,2},{7,3},{10,6},{11,7},{14,10},{15,11},{12,14},{13,15},{8,12},{... | collective-permute-start | bytes 835592 | tf_op jit(solution)/shard_map/ppermute | solution.py:262
  28.4 2.8 %copy-start = (bf16[1,1,2048,1536]{3,2,1,0:T(8,128)(2,1)S(1)}, bf16[1,1,2048,1536]{3,2,1,0:T(8,128)(2,1)}, u32[]{:S(2)}) copy-start(bf16[1,1,2048,1536]{3,2,1,0:T(8,128)(2,1)} %param.12) | copy-start | bytes 18874372
  34.4 10.8 %collective-permute-start.12 = (bf16[64,2176]{1,0:T(8,128)(2,1)S(1)}, bf16[64,2176]{1,0:T(8,128)(2,1)S(1)}, u32[]{:S(2)}, u32[]{:S(2)}) collective-permute-start(bf16[64,2176]{1,0:T(8,128)(2,1)S(1)} %collective-permute-done.8.refs_0_), channel_id=1, source_target_pairs={{2,6},{3,7},{6,10},{7,11},{10,14},{11,15},{14,12},{15,13},{12,8},{... | collective-permute-start | bytes 835592 | tf_op jit(solution)/shard_map/ppermute | solution.py:262
  36.0 10.4 %collective-permute-start.13 = (bf16[64,2176]{1,0:T(8,128)(2,1)S(1)}, bf16[64,2176]{1,0:T(8,128)(2,1)S(1)}, u32[]{:S(2)}, u32[]{:S(2)}) collective-permute-start(bf16[64,2176]{1,0:T(8,128)(2,1)S(1)} %collective-permute-done.9.refs_1_), channel_id=1, source_target_pairs={{6,2},{7,3},{10,6},{11,7},{14,10},{15,11},{12,14},{13,15},{8,12},{... | collective-permute-start | bytes 835592 | tf_op jit(solution)/shard_map/ppermute | solution.py:262
  40.4 10.8 %collective-permute-start.10 = (bf16[64,2176]{1,0:T(8,128)(2,1)S(1)}, bf16[64,2176]{1,0:T(8,128)(2,1)S(1)}, u32[]{:S(2)}, u32[]{:S(2)}) collective-permute-start(bf16[64,2176]{1,0:T(8,128)(2,1)S(1)} %collective-permute-done.6.refs_0_), channel_id=1, source_target_pairs={{2,6},{3,7},{6,10},{7,11},{10,14},{11,15},{14,12},{15,13},{12,8},{... | collective-permute-start | bytes 835592 | tf_op jit(solution)/shard_map/ppermute | solution.py:262
  42.0 10.4 %collective-permute-start.11 = (bf16[64,2176]{1,0:T(8,128)(2,1)S(1)}, bf16[64,2176]{1,0:T(8,128)(2,1)S(1)}, u32[]{:S(2)}, u32[]{:S(2)}) collective-permute-start(bf16[64,2176]{1,0:T(8,128)(2,1)S(1)} %collective-permute-done.7.refs_1_), channel_id=1, source_target_pairs={{6,2},{7,3},{10,6},{11,7},{14,10},{15,11},{12,14},{13,15},{8,12},{... | collective-permute-start | bytes 835592 | tf_op jit(solution)/shard_map/ppermute | solution.py:262
  46.3 10.4 %collective-permute-start.15 = (bf16[64,2176]{1,0:T(8,128)(2,1)S(1)}, bf16[64,2176]{1,0:T(8,128)(2,1)S(1)}, u32[]{:S(2)}, u32[]{:S(2)}) collective-permute-start(bf16[64,2176]{1,0:T(8,128)(2,1)S(1)} %collective-permute-done.12.refs_0_), channel_id=1, source_target_pairs={{2,6},{3,7},{6,10},{7,11},{10,14},{11,15},{14,12},{15,13},{12,8},{... | collective-permute-start | bytes 835592 | tf_op jit(solution)/shard_map/ppermute | solution.py:262
  47.9 8.8 %collective-permute-start.16 = (bf16[64,2176]{1,0:T(8,128)(2,1)S(1)}, bf16[64,2176]{1,0:T(8,128)(2,1)S(1)}, u32[]{:S(2)}, u32[]{:S(2)}) collective-permute-start(bf16[64,2176]{1,0:T(8,128)(2,1)S(1)} %collective-permute-done.13.refs_1_), channel_id=1, source_target_pairs={{6,2},{7,3},{10,6},{11,7},{14,10},{15,11},{12,14},{13,15},{8,12},{... | collective-permute-start | bytes 835592 | tf_op jit(solution)/shard_map/ppermute | solution.py:262
  52.3 10.0 %collective-permute-start.14 = (bf16[64,2176]{1,0:T(8,128)(2,1)S(1)}, bf16[64,2176]{1,0:T(8,128)(2,1)S(1)}, u32[]{:S(2)}, u32[]{:S(2)}) collective-permute-start(bf16[64,2176]{1,0:T(8,128)(2,1)S(1)} %collective-permute-done.10.refs_0_), channel_id=1, source_target_pairs={{2,6},{3,7},{6,10},{7,11},{10,14},{11,15},{14,12},{15,13},{12,8},{... | collective-permute-start | bytes 835592 | tf_op jit(solution)/shard_map/ppermute | solution.py:262
  56.8 9.2 %collective-permute-start.17 = (bf16[64,2176]{1,0:T(8,128)(2,1)S(1)}, bf16[64,2176]{1,0:T(8,128)(2,1)S(1)}, u32[]{:S(2)}, u32[]{:S(2)}) collective-permute-start(bf16[64,2176]{1,0:T(8,128)(2,1)S(1)} %collective-permute-done.16.refs_1_), channel_id=1, source_target_pairs={{6,2},{7,3},{10,6},{11,7},{14,10},{15,11},{12,14},{13,15},{8,12},{... | collective-permute-start | bytes 835592 | tf_op jit(solution)/shard_map/ppermute | solution.py:262
  60.1 8.7 %collective-permute-start.21 = (bf16[64,2048]{1,0:T(8,128)(2,1)S(1)}, bf16[64,2048]{1,0:T(8,128)(2,1)S(1)}, u32[]{:S(2)}, u32[]{:S(2)}) collective-permute-start(bf16[64,2048]{1,0:T(8,128)(2,1)S(1)} %convert_element_type.89), channel_id=1, source_target_pairs={{2,6},{3,7},{6,10},{7,11},{10,14},{11,15},{14,12},{15,13},{12,8},{... | collective-permute-start | bytes 786440 | tf_op jit(solution)/shard_map/ppermute | solution.py:262
  61.8 7.0 %collective-permute-start.18 = (bf16[64,2048]{1,0:T(8,128)(2,1)S(1)}, bf16[64,2048]{1,0:T(8,128)(2,1)S(1)}, u32[]{:S(2)}, u32[]{:S(2)}) collective-permute-start(bf16[64,2048]{1,0:T(8,128)(2,1)S(1)} %convert_element_type.85), channel_id=1, source_target_pairs={{6,2},{7,3},{10,6},{11,7},{14,10},{15,11},{12,14},{13,15},{8,12},{... | collective-permute-start | bytes 786440 | tf_op jit(solution)/shard_map/ppermute | solution.py:262
  68.9 8.1 %collective-permute-start.20 = (bf16[64,2048]{1,0:T(8,128)(2,1)S(1)}, bf16[64,2048]{1,0:T(8,128)(2,1)S(1)}, u32[]{:S(2)}, u32[]{:S(2)}) collective-permute-start(bf16[64,2048]{1,0:T(8,128)(2,1)S(1)} %convert_element_type.88), channel_id=1, source_target_pairs={{2,6},{3,7},{6,10},{7,11},{10,14},{11,15},{14,12},{15,13},{12,8},{... | collective-permute-start | bytes 786440 | tf_op jit(solution)/shard_map/ppermute | solution.py:262
  70.7 13.7 %collective-permute-start.19 = (bf16[64,2048]{1,0:T(8,128)(2,1)S(1)}, bf16[64,2048]{1,0:T(8,128)(2,1)S(1)}, u32[]{:S(2)}, u32[]{:S(2)}) collective-permute-start(bf16[64,2048]{1,0:T(8,128)(2,1)S(1)} %add_convert_fusion.9), channel_id=1, source_target_pairs={{6,2},{7,3},{10,6},{11,7},{14,10},{15,11},{12,14},{13,15},{8,12},{... | collective-permute-start | bytes 786440 | tf_op jit(solution)/shard_map/ppermute | solution.py:262
  71.0 11.1 %collective-permute-start.22 = (bf16[64,2048]{1,0:T(8,128)(2,1)S(1)}, bf16[64,2048]{1,0:T(8,128)(2,1)S(1)}, u32[]{:S(2)}, u32[]{:S(2)}) collective-permute-start(bf16[64,2048]{1,0:T(8,128)(2,1)S(1)} %convert_element_type.94), channel_id=1, source_target_pairs={{6,2},{7,3},{10,6},{11,7},{14,10},{15,11},{12,14},{13,15},{8,12},{... | collective-permute-start | bytes 786440 | tf_op jit(solution)/shard_map/ppermute | solution.py:262
  71.6 12.7 %collective-permute-start.24 = (bf16[64,2048]{1,0:T(8,128)(2,1)S(1)}, bf16[64,2048]{1,0:T(8,128)(2,1)S(1)}, u32[]{:S(2)}, u32[]{:S(2)}) collective-permute-start(bf16[64,2048]{1,0:T(8,128)(2,1)S(1)} %add_convert_fusion.8), channel_id=1, source_target_pairs={{2,6},{3,7},{6,10},{7,11},{10,14},{11,15},{14,12},{15,13},{12,8},{... | collective-permute-start | bytes 786440 | tf_op jit(solution)/shard_map/ppermute | solution.py:262
  82.2 9.3 %collective-permute-start.28 = (bf16[64,2048]{1,0:T(8,128)(2,1)S(1)}, bf16[64,2048]{1,0:T(8,128)(2,1)S(1)}, u32[]{:S(2)}, u32[]{:S(2)}) collective-permute-start(bf16[64,2048]{1,0:T(8,128)(2,1)S(1)} %get-tuple-element.109), channel_id=1, source_target_pairs={{6,2},{7,3},{10,6},{11,7},{14,10},{15,11},{12,14},{13,15},{8,12},{... | collective-permute-start | bytes 786440 | tf_op jit(solution)/shard_map/ppermute | solution.py:262
  83.0 9.4 %collective-permute-start.26 = (bf16[64,2048]{1,0:T(8,128)(2,1)S(1)}, bf16[64,2048]{1,0:T(8,128)(2,1)S(1)}, u32[]{:S(2)}, u32[]{:S(2)}) collective-permute-start(bf16[64,2048]{1,0:T(8,128)(2,1)S(1)} %get-tuple-element.110), channel_id=1, source_target_pairs={{2,6},{3,7},{6,10},{7,11},{10,14},{11,15},{14,12},{15,13},{12,8},{... | collective-permute-start | bytes 786440 | tf_op jit(solution)/shard_map/ppermute | solution.py:262
  84.4 11.4 %collective-permute-start.23 = (bf16[64,2048]{1,0:T(8,128)(2,1)S(1)}, bf16[64,2048]{1,0:T(8,128)(2,1)S(1)}, u32[]{:S(2)}, u32[]{:S(2)}) collective-permute-start(bf16[64,2048]{1,0:T(8,128)(2,1)S(1)} %add_convert_fusion.5), channel_id=1, source_target_pairs={{6,2},{7,3},{10,6},{11,7},{14,10},{15,11},{12,14},{13,15},{8,12},{... | collective-permute-start | bytes 786440 | tf_op jit(solution)/shard_map/ppermute | solution.py:262
  85.2 16.9 %collective-permute-start.25 = (bf16[64,2048]{1,0:T(8,128)(2,1)S(1)}, bf16[64,2048]{1,0:T(8,128)(2,1)S(1)}, u32[]{:S(2)}, u32[]{:S(2)}) collective-permute-start(bf16[64,2048]{1,0:T(8,128)(2,1)S(1)} %add_convert_fusion.4), channel_id=1, source_target_pairs={{2,6},{3,7},{6,10},{7,11},{10,14},{11,15},{14,12},{15,13},{12,8},{... | collective-permute-start | bytes 786440 | tf_op jit(solution)/shard_map/ppermute | solution.py:262
  91.6 8.3 %collective-permute-start.30 = (bf16[64,2048]{1,0:T(8,128)(2,1)S(1)}, bf16[64,2048]{1,0:T(8,128)(2,1)S(1)}, u32[]{:S(2)}, u32[]{:S(2)}) collective-permute-start(bf16[64,2048]{1,0:T(8,128)(2,1)S(1)} %add_convert_fusion.2), channel_id=1, source_target_pairs={{6,2},{7,3},{10,6},{11,7},{14,10},{15,11},{12,14},{13,15},{8,12},{... | collective-permute-start | bytes 786440 | tf_op jit(solution)/shard_map/ppermute | solution.py:262
  92.4 8.0 %collective-permute-start.27 = (bf16[64,2048]{1,0:T(8,128)(2,1)S(1)}, bf16[64,2048]{1,0:T(8,128)(2,1)S(1)}, u32[]{:S(2)}, u32[]{:S(2)}) collective-permute-start(bf16[64,2048]{1,0:T(8,128)(2,1)S(1)} %add_convert_fusion.3), channel_id=1, source_target_pairs={{2,6},{3,7},{6,10},{7,11},{10,14},{11,15},{14,12},{15,13},{12,8},{... | collective-permute-start | bytes 786440 | tf_op jit(solution)/shard_map/ppermute | solution.py:262
  99.9 6.4 %collective-permute-start.31 = (bf16[64,2048]{1,0:T(8,128)(2,1)S(1)}, bf16[64,2048]{1,0:T(8,128)(2,1)S(1)}, u32[]{:S(2)}, u32[]{:S(2)}) collective-permute-start(bf16[64,2048]{1,0:T(8,128)(2,1)S(1)} %add_convert_fusion), channel_id=1, source_target_pairs={{6,2},{7,3},{10,6},{11,7},{14,10},{15,11},{12,14},{13,15},{8,12},{... | collective-permute-start | bytes 786440 | tf_op jit(solution)/shard_map/ppermute | solution.py:262
  100.4 6.4 %collective-permute-start.29 = (bf16[64,2048]{1,0:T(8,128)(2,1)S(1)}, bf16[64,2048]{1,0:T(8,128)(2,1)S(1)}, u32[]{:S(2)}, u32[]{:S(2)}) collective-permute-start(bf16[64,2048]{1,0:T(8,128)(2,1)S(1)} %add_convert_fusion.1), channel_id=1, source_target_pairs={{2,6},{3,7},{6,10},{7,11},{10,14},{11,15},{14,12},{15,13},{12,8},{... | collective-permute-start | bytes 786440 | tf_op jit(solution)/shard_map/ppermute | solution.py:262

commit v6 on v5

--- a/solution.py
+++ b/solution.py
@@ -292,12 +292,13 @@
     to_down, to_up = {}, {}
     pass_on(0, 0, None)
     pass_on(0, 1, None)
+    own_sums = mlp(packed)
     for s in range(1, hops):
         for c in range(2):
             pass_on(s, c, last)
             to_down[s, c], to_up[s, c] = mlp([ups[s][c], downs[s][c]])
-    to_up[hops, 0], to_down[hops, 1] = mlp([ups[hops][0], downs[hops][1]])
-    own_sums = mlp(packed)
+    to_up[hops, 0] = mlp([ups[hops][0]])[0]
+    to_down[hops, 1] = mlp([downs[hops][1]])[0]
 
     def send_on(flow, place, total, after):
         terms, c, pairs = flow
@@ -313,7 +314,7 @@
     long = [(to_up, 0, up), (to_down, 1, down)]
     short_totals = [send_on(flow, hops - 1, None, None)[1] for flow in short]
     long_totals = [send_on(flow, hops, None, None)[1] for flow in long]
-    after = to_up[hops, 0]
+    after = last
     for s in reversed(range(1, hops)):
         if s > 1:
             sent, short_totals = zip(*(send_on(f, s - 1, t, after) for f, t in zip(short, short_totals)))

time: 109 us -> 105 us (0.963); the launches traced: 108 us -> 105 us
  waiting for transfers between devices: 36.4 us -> 31.5 us
  Pallas kernels: 23.9 us -> 27.9 us
  starting transfers between devices: 39.2 us -> 37.3 us
    pallas_call x8 -> x9, Pallas kernels: 22.7 us -> 26.7 us  [expert_rows(): pl.pallas_call(functools.partial(mlp_kernel, parts=len(payloads), chained...]
    ppermute x2, starting transfers between devices: 9.39 us -> 6.18 us  [from_behind(): return lax.ppermute(value, axis, pairs)]
    ppermute x30, waiting for transfers between devices: 30.1 us -> 27 us  [move(): return lax.ppermute(value, 'expert', pairs)]
    ppermute x2, waiting for transfers between devices: 6.32 us -> 4.5 us  [from_behind(): return lax.ppermute(value, axis, pairs)]
    ppermute x30, starting transfers between devices: 29.8 us -> 31.1 us  [move(): return lax.ppermute(value, 'expert', pairs)]
  transfers between devices with their start and end apart: 32 -> 32, of which waited for: 16 -> 14; matrix products, arithmetic and copies ran while one was open for 2% -> 2% of each run, Pallas kernels for 21% -> 26%
where the time goes in v6:
time: 105 us
  starting transfers between devices  37.3 us (36%)
  waiting for transfers between devices  31.5 us (30%)
  Pallas kernels  27.9 us (27%)
  local copies, waits for them, and re-layouts  7.22 us (7%)
    ppermute x30, starting transfers between devices, move(): return lax.ppermute(value, 'expert', pairs)  31.1 us
    ppermute x30, waiting for transfers between devices, move(): return lax.ppermute(value, 'expert', pairs)  27 us
    pallas_call x9, Pallas kernels, expert_rows(): pl.pallas_call(functools.partial(mlp_kernel, parts=len(payloads), chained...  26.7 us
    ppermute x2, starting transfers between devices, from_behind(): return lax.ppermute(value, axis, pairs)  6.18 us
    unnamed x12, local copies, waits for them, and re-layouts  5.9 us
    ppermute x2, waiting for transfers between devices, from_behind(): return lax.ppermute(value, axis, pairs)  4.5 us
  transfers between devices with their start and end apart: 32, of which 14 were waited for; matrix products, arithmetic and copies ran while one was open for 2% of the time, Pallas kernels for 26%

profile of v6, /device:TPU:0, one launch (start us, length us, event | category | flops | bytes accessed | tf_op | source)
XLA Modules:
  0.0 105.0 jit_solution(8174441424684974080)
XLA Ops:
  0.0 0.5 collective-permute-start.2
  0.5 1.3 %slice_bitcast_fusion = (bf16[64,2048]{1,0:T(8,128)(2,1)S(1)}, bf16[64,2048]{1,0:T(8,128)(2,1)S(1)}) fusion(bf16[1,128,2048]{2,1,0:T(8,128)(2,1)} %param.8), kind=kLoop, calls=%fused_computation.12 | loop fusion | bytes 1048576 | tf_op jit(solution)/shard_map/squeeze | solution.py:269
  1.8 4.9 %collective-permute-start = (bf16[64,2048]{1,0:T(8,128)(2,1)S(1)}, bf16[64,2048]{1,0:T(8,128)(2,1)S(1)}, u32[]{:S(2)}, u32[]{:S(2)}) collective-permute-start(bf16[64,2048]{1,0:T(8,128)(2,1)S(1)} %get-tuple-element.104), channel_id=1, source_target_pairs={{0,16},{1,17},{2,18},{3,19},{4,20},{5,21},{6,22},{7,23},{8,24},{9,... | collective-permute-start | bytes 786440 | tf_op jit(solution)/shard_map/ppermute | solution.py:19
  6.7 1.3 %collective-permute-start.1 = (bf16[64,2048]{1,0:T(8,128)(2,1)S(1)}, bf16[64,2048]{1,0:T(8,128)(2,1)S(1)}, u32[]{:S(2)}, u32[]{:S(2)}) collective-permute-start(bf16[64,2048]{1,0:T(8,128)(2,1)S(1)} %get-tuple-element.103), channel_id=1, source_target_pairs={{0,16},{1,17},{2,18},{3,19},{4,20},{5,21},{6,22},{7,23},{8,24},{9,... | collective-permute-start | bytes 786440 | tf_op jit(solution)/shard_map/ppermute | solution.py:19
  8.1 1.0 copy-done.2
  9.1 0.7 copy-done.3
  9.8 0.7 copy-done.4
  10.5 0.7 copy-done.5
  11.2 0.3 base_rows.1
  11.4 2.0 %collective-permute-done.arrived_ref = bf16[64,2048]{1,0:T(8,128)(2,1)S(1)} collective-permute-done((bf16[64,2048]{1,0:T(8,128)(2,1)S(1)}, bf16[64,2048]{1,0:T(8,128)(2,1)S(1)}, u32[]{:S(2)}, u32[]{:S(2)}) %collective-permute-start) | collective-permute-done | bytes 262176 | tf_op jit(solution)/shard_map/ppermute | solution.py:19
  13.4 1.5 %collective-permute-start.4 = (bf16[64,2176]{1,0:T(8,128)(2,1)S(1)}, bf16[64,2176]{1,0:T(8,128)(2,1)S(1)}, u32[]{:S(2)}, u32[]{:S(2)}) collective-permute-start(bf16[64,2176]{1,0:T(8,128)(2,1)S(1)} %get-tuple-element.64.refs_0_), channel_id=1, source_target_pairs={{2,6},{3,7},{6,10},{7,11},{10,14},{11,15},{14,12},{15,13},{12,8},{... | collective-permute-start | bytes 835592 | tf_op jit(solution)/shard_map/ppermute | solution.py:262
  15.0 0.5 collective-permute-start.5
  15.5 2.5 %collective-permute-done.1.arrived_ref = bf16[64,2048]{1,0:T(8,128)(2,1)S(1)} collective-permute-done((bf16[64,2048]{1,0:T(8,128)(2,1)S(1)}, bf16[64,2048]{1,0:T(8,128)(2,1)S(1)}, u32[]{:S(2)}, u32[]{:S(2)}) %collective-permute-start.1) | collective-permute-done | bytes 262176 | tf_op jit(solution)/shard_map/ppermute | solution.py:19
  18.1 1.5 %collective-permute-start.8 = (bf16[64,2176]{1,0:T(8,128)(2,1)S(1)}, bf16[64,2176]{1,0:T(8,128)(2,1)S(1)}, u32[]{:S(2)}, u32[]{:S(2)}) collective-permute-start(bf16[64,2176]{1,0:T(8,128)(2,1)S(1)} %get-tuple-element.69.refs_1_), channel_id=1, source_target_pairs={{2,6},{3,7},{6,10},{7,11},{10,14},{11,15},{14,12},{15,13},{12,8},{... | collective-permute-start | bytes 835592 | tf_op jit(solution)/shard_map/ppermute | solution.py:262
  19.7 0.5 collective-permute-start.9
  20.2 2.8 %copy-done = bf16[1,1,2048,1536]{3,2,1,0:T(8,128)(2,1)S(1)} copy-done((bf16[1,1,2048,1536]{3,2,1,0:T(8,128)(2,1)S(1)}, bf16[1,1,2048,1536]{3,2,1,0:T(8,128)(2,1)}, u32[]{:S(2)}) %copy-start) | copy-done | bytes 6291480
  23.0 2.8 %expert_rows.9 = (f32[64,2048]{1,0:T(8,128)S(1)}, f32[64,2048]{1,0:T(8,128)S(1)}) custom-call(s32[1]{0:T(128)} %bitcast.6.expert_ref, bf16[64,2176]{1,0:T(8,128)(2,1)S(1)} %get-tuple-element.64.refs_0_, bf16[64,2176]{1,0:T(8,128)(2,1)S(1)} %get-tuple-element.69.refs_1_, bf16[2048,1536]{1,0:T(8,128)(2,1)S(1)} %bitcast.16, bf16[768,2048]{1,0:T(8,128)(2,1)S(1)} %bitcast.26, ...), custom_call_target="tpu_custom_call" | custom-call | flops 2415919104 | bytes 1572864 | tf_op jit(solution)/shard_map/expert_rows/pallas_call | solution.py:197
  25.8 1.5 %collective-permute-start.6 = (bf16[64,2176]{1,0:T(8,128)(2,1)S(1)}, bf16[64,2176]{1,0:T(8,128)(2,1)S(1)}, u32[]{:S(2)}, u32[]{:S(2)}) collective-permute-start(bf16[64,2176]{1,0:T(8,128)(2,1)S(1)} %collective-permute-done.4.refs_0_), channel_id=1, source_target_pairs={{2,6},{3,7},{6,10},{7,11},{10,14},{11,15},{14,12},{15,13},{12,8},{... | collective-permute-start | bytes 835592 | tf_op jit(solution)/shard_map/ppermute | solution.py:262
  27.4 0.5 collective-permute-start.7
  27.9 2.8 %expert_rows.10 = (f32[64,2048]{1,0:T(8,128)S(1)}, f32[64,2048]{1,0:T(8,128)S(1)}) custom-call(s32[1]{0:T(128)} %bitcast.6.expert_ref, bf16[64,2176]{1,0:T(8,128)(2,1)S(1)} %collective-permute-done.4.refs_0_, bf16[64,2176]{1,0:T(8,128)(2,1)S(1)} %collective-permute-done.5.refs_1_, bf16[2048,1536]{1,0:T(8,128)(2,1)S(1)} %bitcast.17, ...), custom_call_target="tpu_custom_call" | custom-call | flops 2415919104 | bytes 1572864 | tf_op jit(solution)/shard_map/expert_rows/pallas_call | solution.py:197
  30.8 1.6 %collective-permute-start.12 = (bf16[64,2176]{1,0:T(8,128)(2,1)S(1)}, bf16[64,2176]{1,0:T(8,128)(2,1)S(1)}, u32[]{:S(2)}, u32[]{:S(2)}) collective-permute-start(bf16[64,2176]{1,0:T(8,128)(2,1)S(1)} %collective-permute-done.8.refs_0_), channel_id=1, source_target_pairs={{2,6},{3,7},{6,10},{7,11},{10,14},{11,15},{14,12},{15,13},{12,8},{... | collective-permute-start | bytes 835592 | tf_op jit(solution)/shard_map/ppermute | solution.py:262
  32.3 0.5 collective-permute-start.13
  32.9 2.8 %expert_rows.11 = (f32[64,2048]{1,0:T(8,128)S(1)}, f32[64,2048]{1,0:T(8,128)S(1)}) custom-call(s32[1]{0:T(128)} %bitcast.6.expert_ref, bf16[64,2176]{1,0:T(8,128)(2,1)S(1)} %collective-permute-done.8.refs_0_, bf16[64,2176]{1,0:T(8,128)(2,1)S(1)} %collective-permute-done.9.refs_1_, bf16[2048,1536]{1,0:T(8,128)(2,1)S(1)} %bitcast.18, ...), custom_call_target="tpu_custom_call" | custom-call | flops 2415919104 | bytes 1572864 | tf_op jit(solution)/shard_map/expert_rows/pallas_call | solution.py:197
  35.8 1.6 %collective-permute-start.10 = (bf16[64,2176]{1,0:T(8,128)(2,1)S(1)}, bf16[64,2176]{1,0:T(8,128)(2,1)S(1)}, u32[]{:S(2)}, u32[]{:S(2)}) collective-permute-start(bf16[64,2176]{1,0:T(8,128)(2,1)S(1)} %collective-permute-done.6.refs_0_), channel_id=1, source_target_pairs={{2,6},{3,7},{6,10},{7,11},{10,14},{11,15},{14,12},{15,13},{12,8},{... | collective-permute-start | bytes 835592 | tf_op jit(solution)/shard_map/ppermute | solution.py:262
  37.4 0.5 collective-permute-start.11
  37.8 2.8 %expert_rows.12 = (f32[64,2048]{1,0:T(8,128)S(1)}, f32[64,2048]{1,0:T(8,128)S(1)}) custom-call(s32[1]{0:T(128)} %bitcast.6.expert_ref, bf16[64,2176]{1,0:T(8,128)(2,1)S(1)} %collective-permute-done.6.refs_0_, bf16[64,2176]{1,0:T(8,128)(2,1)S(1)} %collective-permute-done.7.refs_1_, bf16[2048,1536]{1,0:T(8,128)(2,1)S(1)} %bitcast.19, ...), custom_call_target="tpu_custom_call" | custom-call | flops 2415919104 | bytes 1572864 | tf_op jit(solution)/shard_map/expert_rows/pallas_call | solution.py:197
  40.7 1.3 %collective-permute-done.13.refs_1_ = bf16[64,2176]{1,0:T(8,128)(2,1)S(1)} collective-permute-done((bf16[64,2176]{1,0:T(8,128)(2,1)S(1)}, bf16[64,2176]{1,0:T(8,128)(2,1)S(1)}, u32[]{:S(2)}, u32[]{:S(2)}) %collective-permute-start.13) | collective-permute-done | bytes 278560 | tf_op jit(solution)/shard_map/ppermute | solution.py:262
  41.9 1.6 %collective-permute-start.15 = (bf16[64,2176]{1,0:T(8,128)(2,1)S(1)}, bf16[64,2176]{1,0:T(8,128)(2,1)S(1)}, u32[]{:S(2)}, u32[]{:S(2)}) collective-permute-start(bf16[64,2176]{1,0:T(8,128)(2,1)S(1)} %collective-permute-done.12.refs_0_), channel_id=1, source_target_pairs={{2,6},{3,7},{6,10},{7,11},{10,14},{11,15},{14,12},{15,13},{12,8},{... | collective-permute-start | bytes 835592 | tf_op jit(solution)/shard_map/ppermute | solution.py:262
  43.5 0.5 collective-permute-start.16
  44.0 2.8 %expert_rows.13 = (f32[64,2048]{1,0:T(8,128)S(1)}, f32[64,2048]{1,0:T(8,128)S(1)}) custom-call(s32[1]{0:T(128)} %bitcast.6.expert_ref, bf16[64,2176]{1,0:T(8,128)(2,1)S(1)} %collective-permute-done.12.refs_0_, bf16[64,2176]{1,0:T(8,128)(2,1)S(1)} %collective-permute-done.13.refs_1_, bf16[2048,1536]{1,0:T(8,128)(2,1)S(1)} %bitcast.20, ...), custom_call_target="tpu_custom_call" | custom-call | flops 2415919104 | bytes 1572864 | tf_op jit(solution)/shard_map/expert_rows/pallas_call | solution.py:197
  46.8 1.1 %collective-permute-done.11.refs_1_ = bf16[64,2176]{1,0:T(8,128)(2,1)S(1)} collective-permute-done((bf16[64,2176]{1,0:T(8,128)(2,1)S(1)}, bf16[64,2176]{1,0:T(8,128)(2,1)S(1)}, u32[]{:S(2)}, u32[]{:S(2)}) %collective-permute-start.11) | collective-permute-done | bytes 278560 | tf_op jit(solution)/shard_map/ppermute | solution.py:262
  47.9 1.6 %collective-permute-start.18 = (bf16[64,2176]{1,0:T(8,128)(2,1)S(1)}, bf16[64,2176]{1,0:T(8,128)(2,1)S(1)}, u32[]{:S(2)}, u32[]{:S(2)}) collective-permute-start(bf16[64,2176]{1,0:T(8,128)(2,1)S(1)} %collective-permute-done.10.refs_0_), channel_id=1, source_target_pairs={{2,6},{3,7},{6,10},{7,11},{10,14},{11,15},{14,12},{15,13},{12,8},{... | collective-permute-start | bytes 835592 | tf_op jit(solution)/shard_map/ppermute | solution.py:262
  49.5 2.8 %expert_rows.14 = (f32[64,2048]{1,0:T(8,128)S(1)}, f32[64,2048]{1,0:T(8,128)S(1)}) custom-call(s32[1]{0:T(128)} %bitcast.6.expert_ref, bf16[64,2176]{1,0:T(8,128)(2,1)S(1)} %collective-permute-done.10.refs_0_, bf16[64,2176]{1,0:T(8,128)(2,1)S(1)} %collective-permute-done.11.refs_1_, bf16[2048,1536]{1,0:T(8,128)(2,1)S(1)} %bitcast.21, ...), custom_call_target="tpu_custom_call" | custom-call | flops 2415919104 | bytes 1572864 | tf_op jit(solution)/shard_map/expert_rows/pallas_call | solution.py:197
  52.3 0.2 collective-permute-done.15.refs_0_
  52.5 1.6 %collective-permute-start.17 = (bf16[64,2176]{1,0:T(8,128)(2,1)S(1)}, bf16[64,2176]{1,0:T(8,128)(2,1)S(1)}, u32[]{:S(2)}, u32[]{:S(2)}) collective-permute-start(bf16[64,2176]{1,0:T(8,128)(2,1)S(1)} %collective-permute-done.16.refs_1_), channel_id=1, source_target_pairs={{6,2},{7,3},{10,6},{11,7},{14,10},{15,11},{12,14},{13,15},{8,12},{... | collective-permute-start | bytes 835592 | tf_op jit(solution)/shard_map/ppermute | solution.py:262
  54.1 2.8 %expert_rows.15 = (f32[64,2048]{1,0:T(8,128)S(1)}, f32[64,2048]{1,0:T(8,128)S(1)}) custom-call(s32[1]{0:T(128)} %bitcast.6.expert_ref, bf16[64,2176]{1,0:T(8,128)(2,1)S(1)} %collective-permute-done.15.refs_0_, bf16[64,2176]{1,0:T(8,128)(2,1)S(1)} %collective-permute-done.16.refs_1_, bf16[2048,1536]{1,0:T(8,128)(2,1)S(1)} %bitcast.22, ...), custom_call_target="tpu_custom_call" | custom-call | flops 2415919104 | bytes 1572864 | tf_op jit(solution)/shard_map/expert_rows/pallas_call | solution.py:197
  57.0 0.5 collective-permute-start.21
  57.5 1.8 %collective-permute-start.14 = (bf16[64,2048]{1,0:T(8,128)(2,1)S(1)}, bf16[64,2048]{1,0:T(8,128)(2,1)S(1)}, u32[]{:S(2)}, u32[]{:S(2)}) collective-permute-start(bf16[64,2048]{1,0:T(8,128)(2,1)S(1)} %convert_element_type.85), channel_id=1, source_target_pairs={{6,2},{7,3},{10,6},{11,7},{14,10},{15,11},{12,14},{13,15},{8,12},{... | collective-permute-start | bytes 786440 | tf_op jit(solution)/shard_map/ppermute | solution.py:262
  59.3 3.4 %expert_rows.16.refs_5_ = f32[64,2048]{1,0:T(8,128)S(1)} custom-call(s32[1]{0:T(128)} %bitcast.6.expert_ref, bf16[64,2176]{1,0:T(8,128)(2,1)S(1)} %collective-permute-done.18.refs_0_, bf16[2048,1536]{1,0:T(8,128)(2,1)S(1)} %bitcast.23, bf16[768,2048]{1,0:T(8,128)(2,1)S(1)} %bitcast.33, bf16[2048,1536]{1,0:T(8,128)(2,1)S(1)} %collective-permute-done.2.refs_4_.refs_3_, ...), custom_call_target="tpu_custom_call" | custom-call | flops 1207959552 | bytes 786432 | tf_op jit(solution)/shard_map/expert_rows/pallas_call | solution.py:197
  62.8 0.5 collective-permute-start.20
  63.3 3.4 %expert_rows.17 = f32[64,2048]{1,0:T(8,128)S(1)} custom-call(s32[1]{0:T(128)} %bitcast.6.expert_ref, bf16[64,2176]{1,0:T(8,128)(2,1)S(1)} %collective-permute-done.17.refs_0_, bf16[2048,1536]{1,0:T(8,128)(2,1)S(1)} %bitcast.24, bf16[768,2048]{1,0:T(8,128)(2,1)S(1)} %bitcast.34, bf16[2048,1536]{1,0:T(8,128)(2,1)S(1)} %collective-permute-done.2.refs_4_.refs_3_, ...), custom_call_target="tpu_custom_call" | custom-call | flops 1207959552 | bytes 786432 | tf_op jit(solution)/shard_map/expert_rows/pallas_call | solution.py:197
  66.8 1.6 %collective-permute-start.22 = (bf16[64,2048]{1,0:T(8,128)(2,1)S(1)}, bf16[64,2048]{1,0:T(8,128)(2,1)S(1)}, u32[]{:S(2)}, u32[]{:S(2)}) collective-permute-start(bf16[64,2048]{1,0:T(8,128)(2,1)S(1)} %convert_element_type.94), channel_id=1, source_target_pairs={{6,2},{7,3},{10,6},{11,7},{14,10},{15,11},{12,14},{13,15},{8,12},{... | collective-permute-start | bytes 786440 | tf_op jit(solution)/shard_map/ppermute | solution.py:262
  68.5 1.6 %collective-permute-start.19 = (bf16[64,2048]{1,0:T(8,128)(2,1)S(1)}, bf16[64,2048]{1,0:T(8,128)(2,1)S(1)}, u32[]{:S(2)}, u32[]{:S(2)}) collective-permute-start(bf16[64,2048]{1,0:T(8,128)(2,1)S(1)} %add_convert_fusion.9), channel_id=1, source_target_pairs={{6,2},{7,3},{10,6},{11,7},{14,10},{15,11},{12,14},{13,15},{8,12},{... | collective-permute-start | bytes 786440 | tf_op jit(solution)/shard_map/ppermute | solution.py:262
  70.1 0.5 collective-permute-start.24
  70.6 5.5 %collective-permute-done.22 = bf16[64,2048]{1,0:T(8,128)(2,1)S(1)} collective-permute-done((bf16[64,2048]{1,0:T(8,128)(2,1)S(1)}, bf16[64,2048]{1,0:T(8,128)(2,1)S(1)}, u32[]{:S(2)}, u32[]{:S(2)}) %collective-permute-start.22) | collective-permute-done | bytes 262176 | tf_op jit(solution)/shard_map/ppermute | solution.py:262
  76.2 1.6 %collective-permute-start.28 = (bf16[64,2048]{1,0:T(8,128)(2,1)S(1)}, bf16[64,2048]{1,0:T(8,128)(2,1)S(1)}, u32[]{:S(2)}, u32[]{:S(2)}) collective-permute-start(bf16[64,2048]{1,0:T(8,128)(2,1)S(1)} %add_convert_fusion.6), channel_id=1, source_target_pairs={{6,2},{7,3},{10,6},{11,7},{14,10},{15,11},{12,14},{13,15},{8,12},{... | collective-permute-start | bytes 786440 | tf_op jit(solution)/shard_map/ppermute | solution.py:262
  77.9 0.5 collective-permute-start.26
  78.4 3.4 %collective-permute-done.19 = bf16[64,2048]{1,0:T(8,128)(2,1)S(1)} collective-permute-done((bf16[64,2048]{1,0:T(8,128)(2,1)S(1)}, bf16[64,2048]{1,0:T(8,128)(2,1)S(1)}, u32[]{:S(2)}, u32[]{:S(2)}) %collective-permute-start.19) | collective-permute-done | bytes 262176 | tf_op jit(solution)/shard_map/ppermute | solution.py:262
  81.8 0.1 add_convert_fusion.4
  81.9 1.5 %collective-permute-start.25 = (bf16[64,2048]{1,0:T(8,128)(2,1)S(1)}, bf16[64,2048]{1,0:T(8,128)(2,1)S(1)}, u32[]{:S(2)}, u32[]{:S(2)}) collective-permute-start(bf16[64,2048]{1,0:T(8,128)(2,1)S(1)} %get-tuple-element.105), channel_id=1, source_target_pairs={{2,6},{3,7},{6,10},{7,11},{10,14},{11,15},{14,12},{15,13},{12,8},{... | collective-permute-start | bytes 786440 | tf_op jit(solution)/shard_map/ppermute | solution.py:262
  83.4 0.5 collective-permute-start.23
  83.9 3.4 %collective-permute-done.28 = bf16[64,2048]{1,0:T(8,128)(2,1)S(1)} collective-permute-done((bf16[64,2048]{1,0:T(8,128)(2,1)S(1)}, bf16[64,2048]{1,0:T(8,128)(2,1)S(1)}, u32[]{:S(2)}, u32[]{:S(2)}) %collective-permute-start.28) | collective-permute-done | bytes 262176 | tf_op jit(solution)/shard_map/ppermute | solution.py:262
  87.4 1.5 %collective-permute-start.27 = (bf16[64,2048]{1,0:T(8,128)(2,1)S(1)}, bf16[64,2048]{1,0:T(8,128)(2,1)S(1)}, u32[]{:S(2)}, u32[]{:S(2)}) collective-permute-start(bf16[64,2048]{1,0:T(8,128)(2,1)S(1)} %add_convert_fusion.3), channel_id=1, source_target_pairs={{2,6},{3,7},{6,10},{7,11},{10,14},{11,15},{14,12},{15,13},{12,8},{... | collective-permute-start | bytes 786440 | tf_op jit(solution)/shard_map/ppermute | solution.py:262
  89.0 0.6 collective-permute-start.30
  89.6 2.2 %collective-permute-done.23 = bf16[64,2048]{1,0:T(8,128)(2,1)S(1)} collective-permute-done((bf16[64,2048]{1,0:T(8,128)(2,1)S(1)}, bf16[64,2048]{1,0:T(8,128)(2,1)S(1)}, u32[]{:S(2)}, u32[]{:S(2)}) %collective-permute-start.23) | collective-permute-done | bytes 262176 | tf_op jit(solution)/shard_map/ppermute | solution.py:262
  91.8 0.1 add_add_fusion.1.near0_ref
  91.8 4.3 %collective-permute-done.27 = bf16[64,2048]{1,0:T(8,128)(2,1)S(1)} collective-permute-done((bf16[64,2048]{1,0:T(8,128)(2,1)S(1)}, bf16[64,2048]{1,0:T(8,128)(2,1)S(1)}, u32[]{:S(2)}, u32[]{:S(2)}) %collective-permute-start.27) | collective-permute-done | bytes 262176 | tf_op jit(solution)/shard_map/ppermute | solution.py:262
  96.2 1.3 %collective-permute-start.29 = (bf16[64,2048]{1,0:T(8,128)(2,1)S(1)}, bf16[64,2048]{1,0:T(8,128)(2,1)S(1)}, u32[]{:S(2)}, u32[]{:S(2)}) collective-permute-start(bf16[64,2048]{1,0:T(8,128)(2,1)S(1)} %add_convert_fusion.1), channel_id=1, source_target_pairs={{2,6},{3,7},{6,10},{7,11},{10,14},{11,15},{14,12},{15,13},{12,8},{... | collective-permute-start | bytes 786440 | tf_op jit(solution)/shard_map/ppermute | solution.py:262
  97.5 0.1 collective-permute-done.30
  97.6 0.9 collective-permute-start.31
  98.5 0.1 add_add_fusion.near1_ref
  98.6 4.0 %collective-permute-done.29.total0_ref = bf16[64,2048]{1,0:T(8,128)(2,1)S(1)} collective-permute-done((bf16[64,2048]{1,0:T(8,128)(2,1)S(1)}, bf16[64,2048]{1,0:T(8,128)(2,1)S(1)}, u32[]{:S(2)}, u32[]{:S(2)}) %collective-permute-start.29) | collective-permute-done | bytes 262176 | tf_op jit(solution)/shard_map/ppermute | solution.py:262
  102.6 1.5 %collective-permute-done.31.total1_ref = bf16[64,2048]{1,0:T(8,128)(2,1)S(1)} collective-permute-done((bf16[64,2048]{1,0:T(8,128)(2,1)S(1)}, bf16[64,2048]{1,0:T(8,128)(2,1)S(1)}, u32[]{:S(2)}, u32[]{:S(2)}) %collective-permute-start.31) | collective-permute-done | bytes 262176 | tf_op jit(solution)/shard_map/ppermute | solution.py:262
  104.1 0.9 last_rows.1
  (41 shorter events, 0.8 us)
Async XLA Ops:
  0.0 20.2 %copy-start.1 = (bf16[1,1,768,2048]{3,2,1,0:T(8,128)(2,1)S(1)}, bf16[1,1,768,2048]{3,2,1,0:T(8,128)(2,1)}, u32[]{:S(2)}) copy-start(bf16[1,1,768,2048]{3,2,1,0:T(8,128)(2,1)} %param.13) | copy-start | bytes 9437188
  0.0 20.2 %collective-permute-start.2 = (bf16[2048,1536]{1,0:T(8,128)(2,1)}, bf16[2048,1536]{1,0:T(8,128)(2,1)S(1)}, u32[]{:S(2)}, u32[]{:S(2)}) collective-permute-start(bf16[2048,1536]{1,0:T(8,128)(2,1)} %bitcast.15), channel_id=1, source_target_pairs={{0,1},{1,0},{2,3},{3,2},{4,5},{5,4},{6,7},{7,6},{8,9},{9,8},{10,11... | collective-permute-start | bytes 18874376 | tf_op jit(solution)/shard_map/ppermute | solution.py:262
  0.5 19.2 %collective-permute-start.3 = (bf16[768,2048]{1,0:T(8,128)(2,1)}, bf16[768,2048]{1,0:T(8,128)(2,1)S(1)}, u32[]{:S(2)}, u32[]{:S(2)}) collective-permute-start(bf16[768,2048]{1,0:T(8,128)(2,1)} %bitcast.25), channel_id=1, source_target_pairs={{0,1},{1,0},{2,3},{3,2},{4,5},{5,4},{6,7},{7,6},{8,9},{9,8},{10,11... | collective-permute-start | bytes 9437192 | tf_op jit(solution)/shard_map/ppermute | solution.py:262
  1.8 11.5 %collective-permute-start = (bf16[64,2048]{1,0:T(8,128)(2,1)S(1)}, bf16[64,2048]{1,0:T(8,128)(2,1)S(1)}, u32[]{:S(2)}, u32[]{:S(2)}) collective-permute-start(bf16[64,2048]{1,0:T(8,128)(2,1)S(1)} %get-tuple-element.104), channel_id=1, source_target_pairs={{0,16},{1,17},{2,18},{3,19},{4,20},{5,21},{6,22},{7,23},{8,24},{9,... | collective-permute-start | bytes 786440 | tf_op jit(solution)/shard_map/ppermute | solution.py:19
  6.7 11.3 %collective-permute-start.1 = (bf16[64,2048]{1,0:T(8,128)(2,1)S(1)}, bf16[64,2048]{1,0:T(8,128)(2,1)S(1)}, u32[]{:S(2)}, u32[]{:S(2)}) collective-permute-start(bf16[64,2048]{1,0:T(8,128)(2,1)S(1)} %get-tuple-element.103), channel_id=1, source_target_pairs={{0,16},{1,17},{2,18},{3,19},{4,20},{5,21},{6,22},{7,23},{8,24},{9,... | collective-permute-start | bytes 786440 | tf_op jit(solution)/shard_map/ppermute | solution.py:19
  8.0 1.0 copy-start.2
  9.1 0.7 copy-start.3
  9.8 0.7 copy-start.4
  10.5 0.7 copy-start.5
  13.4 12.4 %collective-permute-start.4 = (bf16[64,2176]{1,0:T(8,128)(2,1)S(1)}, bf16[64,2176]{1,0:T(8,128)(2,1)S(1)}, u32[]{:S(2)}, u32[]{:S(2)}) collective-permute-start(bf16[64,2176]{1,0:T(8,128)(2,1)S(1)} %get-tuple-element.64.refs_0_), channel_id=1, source_target_pairs={{2,6},{3,7},{6,10},{7,11},{10,14},{11,15},{14,12},{15,13},{12,8},{... | collective-permute-start | bytes 835592 | tf_op jit(solution)/shard_map/ppermute | solution.py:262
  15.0 10.9 %collective-permute-start.5 = (bf16[64,2176]{1,0:T(8,128)(2,1)S(1)}, bf16[64,2176]{1,0:T(8,128)(2,1)S(1)}, u32[]{:S(2)}, u32[]{:S(2)}) collective-permute-start(bf16[64,2176]{1,0:T(8,128)(2,1)S(1)} %get-tuple-element.64.refs_0_), channel_id=1, source_target_pairs={{6,2},{7,3},{10,6},{11,7},{14,10},{15,11},{12,14},{13,15},{8,12},{... | collective-permute-start | bytes 835592 | tf_op jit(solution)/shard_map/ppermute | solution.py:262
  18.1 12.7 %collective-permute-start.8 = (bf16[64,2176]{1,0:T(8,128)(2,1)S(1)}, bf16[64,2176]{1,0:T(8,128)(2,1)S(1)}, u32[]{:S(2)}, u32[]{:S(2)}) collective-permute-start(bf16[64,2176]{1,0:T(8,128)(2,1)S(1)} %get-tuple-element.69.refs_1_), channel_id=1, source_target_pairs={{2,6},{3,7},{6,10},{7,11},{10,14},{11,15},{14,12},{15,13},{12,8},{... | collective-permute-start | bytes 835592 | tf_op jit(solution)/shard_map/ppermute | solution.py:262
  19.7 11.1 %collective-permute-start.9 = (bf16[64,2176]{1,0:T(8,128)(2,1)S(1)}, bf16[64,2176]{1,0:T(8,128)(2,1)S(1)}, u32[]{:S(2)}, u32[]{:S(2)}) collective-permute-start(bf16[64,2176]{1,0:T(8,128)(2,1)S(1)} %get-tuple-element.69.refs_1_), channel_id=1, source_target_pairs={{6,2},{7,3},{10,6},{11,7},{14,10},{15,11},{12,14},{13,15},{8,12},{... | collective-permute-start | bytes 835592 | tf_op jit(solution)/shard_map/ppermute | solution.py:262
  20.2 2.8 %copy-start = (bf16[1,1,2048,1536]{3,2,1,0:T(8,128)(2,1)S(1)}, bf16[1,1,2048,1536]{3,2,1,0:T(8,128)(2,1)}, u32[]{:S(2)}) copy-start(bf16[1,1,2048,1536]{3,2,1,0:T(8,128)(2,1)} %param.12) | copy-start | bytes 18874372
  25.8 9.9 %collective-permute-start.6 = (bf16[64,2176]{1,0:T(8,128)(2,1)S(1)}, bf16[64,2176]{1,0:T(8,128)(2,1)S(1)}, u32[]{:S(2)}, u32[]{:S(2)}) collective-permute-start(bf16[64,2176]{1,0:T(8,128)(2,1)S(1)} %collective-permute-done.4.refs_0_), channel_id=1, source_target_pairs={{2,6},{3,7},{6,10},{7,11},{10,14},{11,15},{14,12},{15,13},{12,8},{... | collective-permute-start | bytes 835592 | tf_op jit(solution)/shard_map/ppermute | solution.py:262
  27.4 8.4 %collective-permute-start.7 = (bf16[64,2176]{1,0:T(8,128)(2,1)S(1)}, bf16[64,2176]{1,0:T(8,128)(2,1)S(1)}, u32[]{:S(2)}, u32[]{:S(2)}) collective-permute-start(bf16[64,2176]{1,0:T(8,128)(2,1)S(1)} %collective-permute-done.5.refs_1_), channel_id=1, source_target_pairs={{6,2},{7,3},{10,6},{11,7},{14,10},{15,11},{12,14},{13,15},{8,12},{... | collective-permute-start | bytes 835592 | tf_op jit(solution)/shard_map/ppermute | solution.py:262
  30.8 9.9 %collective-permute-start.12 = (bf16[64,2176]{1,0:T(8,128)(2,1)S(1)}, bf16[64,2176]{1,0:T(8,128)(2,1)S(1)}, u32[]{:S(2)}, u32[]{:S(2)}) collective-permute-start(bf16[64,2176]{1,0:T(8,128)(2,1)S(1)} %collective-permute-done.8.refs_0_), channel_id=1, source_target_pairs={{2,6},{3,7},{6,10},{7,11},{10,14},{11,15},{14,12},{15,13},{12,8},{... | collective-permute-start | bytes 835592 | tf_op jit(solution)/shard_map/ppermute | solution.py:262
  32.3 9.6 %collective-permute-start.13 = (bf16[64,2176]{1,0:T(8,128)(2,1)S(1)}, bf16[64,2176]{1,0:T(8,128)(2,1)S(1)}, u32[]{:S(2)}, u32[]{:S(2)}) collective-permute-start(bf16[64,2176]{1,0:T(8,128)(2,1)S(1)} %collective-permute-done.9.refs_1_), channel_id=1, source_target_pairs={{6,2},{7,3},{10,6},{11,7},{14,10},{15,11},{12,14},{13,15},{8,12},{... | collective-permute-start | bytes 835592 | tf_op jit(solution)/shard_map/ppermute | solution.py:262
  35.8 11.0 %collective-permute-start.10 = (bf16[64,2176]{1,0:T(8,128)(2,1)S(1)}, bf16[64,2176]{1,0:T(8,128)(2,1)S(1)}, u32[]{:S(2)}, u32[]{:S(2)}) collective-permute-start(bf16[64,2176]{1,0:T(8,128)(2,1)S(1)} %collective-permute-done.6.refs_0_), channel_id=1, source_target_pairs={{2,6},{3,7},{6,10},{7,11},{10,14},{11,15},{14,12},{15,13},{12,8},{... | collective-permute-start | bytes 835592 | tf_op jit(solution)/shard_map/ppermute | solution.py:262
  37.4 10.5 %collective-permute-start.11 = (bf16[64,2176]{1,0:T(8,128)(2,1)S(1)}, bf16[64,2176]{1,0:T(8,128)(2,1)S(1)}, u32[]{:S(2)}, u32[]{:S(2)}) collective-permute-start(bf16[64,2176]{1,0:T(8,128)(2,1)S(1)} %collective-permute-done.7.refs_1_), channel_id=1, source_target_pairs={{6,2},{7,3},{10,6},{11,7},{14,10},{15,11},{12,14},{13,15},{8,12},{... | collective-permute-start | bytes 835592 | tf_op jit(solution)/shard_map/ppermute | solution.py:262
  41.9 10.6 %collective-permute-start.15 = (bf16[64,2176]{1,0:T(8,128)(2,1)S(1)}, bf16[64,2176]{1,0:T(8,128)(2,1)S(1)}, u32[]{:S(2)}, u32[]{:S(2)}) collective-permute-start(bf16[64,2176]{1,0:T(8,128)(2,1)S(1)} %collective-permute-done.12.refs_0_), channel_id=1, source_target_pairs={{2,6},{3,7},{6,10},{7,11},{10,14},{11,15},{14,12},{15,13},{12,8},{... | collective-permute-start | bytes 835592 | tf_op jit(solution)/shard_map/ppermute | solution.py:262
  43.5 9.0 %collective-permute-start.16 = (bf16[64,2176]{1,0:T(8,128)(2,1)S(1)}, bf16[64,2176]{1,0:T(8,128)(2,1)S(1)}, u32[]{:S(2)}, u32[]{:S(2)}) collective-permute-start(bf16[64,2176]{1,0:T(8,128)(2,1)S(1)} %collective-permute-done.13.refs_1_), channel_id=1, source_target_pairs={{6,2},{7,3},{10,6},{11,7},{14,10},{15,11},{12,14},{13,15},{8,12},{... | collective-permute-start | bytes 835592 | tf_op jit(solution)/shard_map/ppermute | solution.py:262
  47.9 11.4 %collective-permute-start.18 = (bf16[64,2176]{1,0:T(8,128)(2,1)S(1)}, bf16[64,2176]{1,0:T(8,128)(2,1)S(1)}, u32[]{:S(2)}, u32[]{:S(2)}) collective-permute-start(bf16[64,2176]{1,0:T(8,128)(2,1)S(1)} %collective-permute-done.10.refs_0_), channel_id=1, source_target_pairs={{2,6},{3,7},{6,10},{7,11},{10,14},{11,15},{14,12},{15,13},{12,8},{... | collective-permute-start | bytes 835592 | tf_op jit(solution)/shard_map/ppermute | solution.py:262
  52.5 10.8 %collective-permute-start.17 = (bf16[64,2176]{1,0:T(8,128)(2,1)S(1)}, bf16[64,2176]{1,0:T(8,128)(2,1)S(1)}, u32[]{:S(2)}, u32[]{:S(2)}) collective-permute-start(bf16[64,2176]{1,0:T(8,128)(2,1)S(1)} %collective-permute-done.16.refs_1_), channel_id=1, source_target_pairs={{6,2},{7,3},{10,6},{11,7},{14,10},{15,11},{12,14},{13,15},{8,12},{... | collective-permute-start | bytes 835592 | tf_op jit(solution)/shard_map/ppermute | solution.py:262
  57.0 9.8 %collective-permute-start.21 = (bf16[64,2048]{1,0:T(8,128)(2,1)S(1)}, bf16[64,2048]{1,0:T(8,128)(2,1)S(1)}, u32[]{:S(2)}, u32[]{:S(2)}) collective-permute-start(bf16[64,2048]{1,0:T(8,128)(2,1)S(1)} %convert_element_type.89), channel_id=1, source_target_pairs={{2,6},{3,7},{6,10},{7,11},{10,14},{11,15},{14,12},{15,13},{12,8},{... | collective-permute-start | bytes 786440 | tf_op jit(solution)/shard_map/ppermute | solution.py:262
  57.5 9.3 %collective-permute-start.14 = (bf16[64,2048]{1,0:T(8,128)(2,1)S(1)}, bf16[64,2048]{1,0:T(8,128)(2,1)S(1)}, u32[]{:S(2)}, u32[]{:S(2)}) collective-permute-start(bf16[64,2048]{1,0:T(8,128)(2,1)S(1)} %convert_element_type.85), channel_id=1, source_target_pairs={{6,2},{7,3},{10,6},{11,7},{14,10},{15,11},{12,14},{13,15},{8,12},{... | collective-permute-start | bytes 786440 | tf_op jit(solution)/shard_map/ppermute | solution.py:262
  62.8 7.8 %collective-permute-start.20 = (bf16[64,2048]{1,0:T(8,128)(2,1)S(1)}, bf16[64,2048]{1,0:T(8,128)(2,1)S(1)}, u32[]{:S(2)}, u32[]{:S(2)}) collective-permute-start(bf16[64,2048]{1,0:T(8,128)(2,1)S(1)} %convert_element_type.88), channel_id=1, source_target_pairs={{2,6},{3,7},{6,10},{7,11},{10,14},{11,15},{14,12},{15,13},{12,8},{... | collective-permute-start | bytes 786440 | tf_op jit(solution)/shard_map/ppermute | solution.py:262
  66.8 9.3 %collective-permute-start.22 = (bf16[64,2048]{1,0:T(8,128)(2,1)S(1)}, bf16[64,2048]{1,0:T(8,128)(2,1)S(1)}, u32[]{:S(2)}, u32[]{:S(2)}) collective-permute-start(bf16[64,2048]{1,0:T(8,128)(2,1)S(1)} %convert_element_type.94), channel_id=1, source_target_pairs={{6,2},{7,3},{10,6},{11,7},{14,10},{15,11},{12,14},{13,15},{8,12},{... | collective-permute-start | bytes 786440 | tf_op jit(solution)/shard_map/ppermute | solution.py:262
  68.5 13.3 %collective-permute-start.19 = (bf16[64,2048]{1,0:T(8,128)(2,1)S(1)}, bf16[64,2048]{1,0:T(8,128)(2,1)S(1)}, u32[]{:S(2)}, u32[]{:S(2)}) collective-permute-start(bf16[64,2048]{1,0:T(8,128)(2,1)S(1)} %add_convert_fusion.9), channel_id=1, source_target_pairs={{6,2},{7,3},{10,6},{11,7},{14,10},{15,11},{12,14},{13,15},{8,12},{... | collective-permute-start | bytes 786440 | tf_op jit(solution)/shard_map/ppermute | solution.py:262
  70.1 11.7 %collective-permute-start.24 = (bf16[64,2048]{1,0:T(8,128)(2,1)S(1)}, bf16[64,2048]{1,0:T(8,128)(2,1)S(1)}, u32[]{:S(2)}, u32[]{:S(2)}) collective-permute-start(bf16[64,2048]{1,0:T(8,128)(2,1)S(1)} %add_convert_fusion.8), channel_id=1, source_target_pairs={{2,6},{3,7},{6,10},{7,11},{10,14},{11,15},{14,12},{15,13},{12,8},{... | collective-permute-start | bytes 786440 | tf_op jit(solution)/shard_map/ppermute | solution.py:262
  76.2 11.2 %collective-permute-start.28 = (bf16[64,2048]{1,0:T(8,128)(2,1)S(1)}, bf16[64,2048]{1,0:T(8,128)(2,1)S(1)}, u32[]{:S(2)}, u32[]{:S(2)}) collective-permute-start(bf16[64,2048]{1,0:T(8,128)(2,1)S(1)} %add_convert_fusion.6), channel_id=1, source_target_pairs={{6,2},{7,3},{10,6},{11,7},{14,10},{15,11},{12,14},{13,15},{8,12},{... | collective-permute-start | bytes 786440 | tf_op jit(solution)/shard_map/ppermute | solution.py:262
  77.9 9.5 %collective-permute-start.26 = (bf16[64,2048]{1,0:T(8,128)(2,1)S(1)}, bf16[64,2048]{1,0:T(8,128)(2,1)S(1)}, u32[]{:S(2)}, u32[]{:S(2)}) collective-permute-start(bf16[64,2048]{1,0:T(8,128)(2,1)S(1)} %add_convert_fusion.7), channel_id=1, source_target_pairs={{2,6},{3,7},{6,10},{7,11},{10,14},{11,15},{14,12},{15,13},{12,8},{... | collective-permute-start | bytes 786440 | tf_op jit(solution)/shard_map/ppermute | solution.py:262
  81.9 16.6 %collective-permute-start.25 = (bf16[64,2048]{1,0:T(8,128)(2,1)S(1)}, bf16[64,2048]{1,0:T(8,128)(2,1)S(1)}, u32[]{:S(2)}, u32[]{:S(2)}) collective-permute-start(bf16[64,2048]{1,0:T(8,128)(2,1)S(1)} %get-tuple-element.105), channel_id=1, source_target_pairs={{2,6},{3,7},{6,10},{7,11},{10,14},{11,15},{14,12},{15,13},{12,8},{... | collective-permute-start | bytes 786440 | tf_op jit(solution)/shard_map/ppermute | solution.py:262
  83.4 8.3 %collective-permute-start.23 = (bf16[64,2048]{1,0:T(8,128)(2,1)S(1)}, bf16[64,2048]{1,0:T(8,128)(2,1)S(1)}, u32[]{:S(2)}, u32[]{:S(2)}) collective-permute-start(bf16[64,2048]{1,0:T(8,128)(2,1)S(1)} %get-tuple-element.106), channel_id=1, source_target_pairs={{6,2},{7,3},{10,6},{11,7},{14,10},{15,11},{12,14},{13,15},{8,12},{... | collective-permute-start | bytes 786440 | tf_op jit(solution)/shard_map/ppermute | solution.py:262
  87.4 8.7 %collective-permute-start.27 = (bf16[64,2048]{1,0:T(8,128)(2,1)S(1)}, bf16[64,2048]{1,0:T(8,128)(2,1)S(1)}, u32[]{:S(2)}, u32[]{:S(2)}) collective-permute-start(bf16[64,2048]{1,0:T(8,128)(2,1)S(1)} %add_convert_fusion.3), channel_id=1, source_target_pairs={{2,6},{3,7},{6,10},{7,11},{10,14},{11,15},{14,12},{15,13},{12,8},{... | collective-permute-start | bytes 786440 | tf_op jit(solution)/shard_map/ppermute | solution.py:262
  89.0 8.6 %collective-permute-start.30 = (bf16[64,2048]{1,0:T(8,128)(2,1)S(1)}, bf16[64,2048]{1,0:T(8,128)(2,1)S(1)}, u32[]{:S(2)}, u32[]{:S(2)}) collective-permute-start(bf16[64,2048]{1,0:T(8,128)(2,1)S(1)} %add_convert_fusion.2), channel_id=1, source_target_pairs={{6,2},{7,3},{10,6},{11,7},{14,10},{15,11},{12,14},{13,15},{8,12},{... | collective-permute-start | bytes 786440 | tf_op jit(solution)/shard_map/ppermute | solution.py:262
  96.2 6.4 %collective-permute-start.29 = (bf16[64,2048]{1,0:T(8,128)(2,1)S(1)}, bf16[64,2048]{1,0:T(8,128)(2,1)S(1)}, u32[]{:S(2)}, u32[]{:S(2)}) collective-permute-start(bf16[64,2048]{1,0:T(8,128)(2,1)S(1)} %add_convert_fusion.1), channel_id=1, source_target_pairs={{2,6},{3,7},{6,10},{7,11},{10,14},{11,15},{14,12},{15,13},{12,8},{... | collective-permute-start | bytes 786440 | tf_op jit(solution)/shard_map/ppermute | solution.py:262
  97.6 6.4 %collective-permute-start.31 = (bf16[64,2048]{1,0:T(8,128)(2,1)S(1)}, bf16[64,2048]{1,0:T(8,128)(2,1)S(1)}, u32[]{:S(2)}, u32[]{:S(2)}) collective-permute-start(bf16[64,2048]{1,0:T(8,128)(2,1)S(1)} %add_convert_fusion), channel_id=1, source_target_pairs={{6,2},{7,3},{10,6},{11,7},{14,10},{15,11},{12,14},{13,15},{8,12},{... | collective-permute-start | bytes 786440 | tf_op jit(solution)/shard_map/ppermute | solution.py:262

commit v7 on v5

--- a/solution.py
+++ b/solution.py
@@ -9,6 +9,7 @@
 
 epsilon = 1e-06
 LANES = 128
+HALF = LANES // 2
 CORES = 2
 MIB = 1 << 20
 
@@ -78,21 +79,18 @@
     return (wide * scale * gain).astype(jnp.bfloat16)
 
 
-def base_kernel(fresh_ref, gain_ref, routes_ref, gates_ref, rows_ref, fresh_out_ref, gain_out_ref, *, experts):
-    width = fresh_ref.shape[1]
-    rows = fresh_ref.shape[0]
-    rows_ref[:, :width] = normed_rows(fresh_ref[...], gain_ref[...])
-    line = lax.broadcasted_iota(jnp.int32, (LANES, rows), 0)
-    expert = line % experts
-    term = line // experts
-    weight = jnp.zeros((LANES, rows), jnp.float32)
+def base_kernel(fresh_ref, gain_ref, routes_ref, gates_ref, rows_ref, coefs_ref, fresh_out_ref, gain_out_ref):
+    rows_ref[...] = normed_rows(fresh_ref[...], gain_ref[...])
+    shape = coefs_ref.shape[1:]
+    expert = lax.broadcasted_iota(jnp.int32, shape, 0)
+    weight = jnp.zeros(shape, jnp.float32)
     for k in range(routes_ref.shape[0]):
         weight += jnp.where(routes_ref[k : k + 1, :] == expert, gates_ref[k : k + 1, :], 0.0)
     high = weight.astype(jnp.bfloat16).astype(jnp.float32)
-    middle = (weight - high).astype(jnp.bfloat16).astype(jnp.float32)
-    low = weight - high - middle
-    terms = jnp.where(term == 0, high, jnp.where(term == 1, middle, jnp.where(term == 2, low, 0.0)))
-    rows_ref[:, width:] = terms.T.astype(jnp.bfloat16)
+    low = weight - high
+    left = lax.broadcasted_iota(jnp.int32, shape, 1) < HALF
+    coefs_ref[0] = jnp.where(left, high, pltpu.roll(low, HALF, 1)).astype(jnp.bfloat16)
+    coefs_ref[1] = jnp.where(left, pltpu.roll(high, HALF, 1), low).astype(jnp.bfloat16)
     fresh_out_ref[...] = fresh_ref[...]
     gain_out_ref[...] = gain_ref[...]
 
@@ -101,76 +99,81 @@
     rows, width = fresh.shape
     vmem = pl.BlockSpec(memory_space=pltpu.VMEM)
     return pl.pallas_call(
-        functools.partial(base_kernel, experts=experts),
+        base_kernel,
         out_shape=(
-            jax.ShapeDtypeStruct((rows, width + LANES), jnp.bfloat16),
+            jax.ShapeDtypeStruct((rows, width), jnp.bfloat16),
+            jax.ShapeDtypeStruct((2, experts, rows), jnp.bfloat16),
             jax.ShapeDtypeStruct(fresh.shape, fresh.dtype),
             jax.ShapeDtypeStruct(gain.shape, jnp.float32),
         ),
         in_specs=[vmem] * 4,
-        out_specs=(vmem,) * 3,
+        out_specs=(vmem,) * 4,
         compiler_params=pltpu.CompilerParams(vmem_limit_bytes=12 * MIB),
         cost_estimate=pl.CostEstimate(flops=rows * width * 6, bytes_accessed=rows * width * 8, transcendentals=rows),
         name="base_rows",
     )(fresh, gain, routes, gates)
 
 
-def norm_kernel(section_ref, base_ref, fresh_ref, arrived_ref, gain_ref, rows_ref, arrival_ref, *, start):
+def norm_kernel(section_ref, base_ref, coefs_ref, fresh_ref, arrived_ref, gain_ref, rows_ref, arrival_ref, *, chunk):
     rows, width = arrived_ref.shape
-    here = slice(start, start + rows)
+    here = slice(chunk * rows, (chunk + 1) * rows)
+
+    def pack(normed):
+        for i in range(width // LANES):
+            rows_ref[i * rows : (i + 1) * rows, :] = normed[:, i * LANES : (i + 1) * LANES]
 
     @pl.when(section_ref[0] == 0)
     def _():
-        rows_ref[:, :width] = base_ref[here, :width]
+        pack(base_ref[here, :])
         arrival_ref[...] = fresh_ref[here, :]
 
     @pl.when(section_ref[0] != 0)
     def _():
-        rows_ref[:, :width] = normed_rows(arrived_ref[...], gain_ref[...])
+        pack(normed_rows(arrived_ref[...], gain_ref[...]))
         arrival_ref[...] = arrived_ref[...]
 
-    rows_ref[:, width:] = base_ref[here, width:]
-
-
-def norm_rows(section_id, base, fresh, arrived, gain, start):
+    rows_ref[rows * (width // LANES) :, :] = coefs_ref[chunk]
+
+
+def norm_rows(section_id, base, coefs, fresh, arrived, gain, chunk):
     rows, width = arrived.shape
     vmem = pl.BlockSpec(memory_space=pltpu.VMEM)
     return pl.pallas_call(
-        functools.partial(norm_kernel, start=start),
+        functools.partial(norm_kernel, chunk=chunk),
         out_shape=(
-            jax.ShapeDtypeStruct((rows, base.shape[1]), jnp.bfloat16),
+            jax.ShapeDtypeStruct((rows * (width // LANES) + coefs.shape[1], LANES), jnp.bfloat16),
             jax.ShapeDtypeStruct((rows, width), jnp.bfloat16),
         ),
-        in_specs=[pl.BlockSpec(memory_space=pltpu.SMEM)] + [vmem] * 4,
+        in_specs=[pl.BlockSpec(memory_space=pltpu.SMEM)] + [vmem] * 5,
         out_specs=(vmem, vmem),
         compiler_params=pltpu.CompilerParams(vmem_limit_bytes=12 * MIB),
         cost_estimate=pl.CostEstimate(flops=rows * width * 6, bytes_accessed=rows * width * 8, transcendentals=rows),
         name="norm_rows",
-    )(section_id, base, fresh, arrived, gain)
-
-
-def mlp_kernel(expert_ref, *refs, parts, chained, experts):
+    )(section_id, base, coefs, fresh, arrived, gain)
+
+
+def mlp_kernel(expert_ref, *refs, parts, chained):
     payloads = refs[:parts]
-    own, other = refs[parts : parts + 2], refs[parts + 2 : parts + 4]
+    weights = (refs[parts : parts + 2], refs[parts + 2 : parts + 4])
     refs = refs[parts + 4 + chained :]
     outs = refs[:parts]
-    refs = refs[parts:]
-    weights = (own, other)
-    x_ref, coef_ref, hidden_ref = refs
+    x_ref, coef_ref, hidden_ref = refs[parts:]
     width = x_ref.shape[1]
-    hidden = own[1].shape[0]
+    hidden = weights[0][1].shape[0]
+    line = lax.broadcasted_iota(jnp.int32, (HALF, LANES), 0)
+    token = line == lax.broadcasted_iota(jnp.int32, (HALF, LANES), 1) % HALF
     bounds = []
-    start = 0
-    for payload in payloads:
-        here = slice(start, start + payload.shape[0])
+    for part, payload in enumerate(payloads):
+        here = slice(part * HALF, (part + 1) * HALF)
         bounds.append(here)
-        start += payload.shape[0]
-        x_ref[here, :] = payload[:, :width]
-        tail = payload[:, width:].astype(jnp.float32)
-        lane = lax.broadcasted_iota(jnp.int32, tail.shape, 1) % experts
+        for i in range(width // LANES):
+            x_ref[here, i * LANES : (i + 1) * LANES] = payload[i * HALF : (i + 1) * HALF, :]
+        block = payload[HALF * (width // LANES) :, :].astype(jnp.float32)
+        expert = lax.broadcasted_iota(jnp.int32, block.shape, 0)
         for which in range(2):
-            value = jnp.sum(jnp.where(lane == expert_ref[0] ^ which, tail, 0.0), axis=1, keepdims=True)
-            coef_ref[which, here, :] = jnp.broadcast_to(value, tail.shape)
+            terms = jnp.sum(jnp.where(expert == expert_ref[0] ^ which, block, 0.0), axis=0, keepdims=True)
+            value = jnp.sum(jnp.where(token, terms, 0.0), axis=1, keepdims=True)
+            coef_ref[which, here, :] = jnp.broadcast_to(value, (HALF, LANES))
     tile = 256
     for which, (gate_up, _) in enumerate(weights):
         for t in range(0, hidden, tile):
@@ -188,15 +191,15 @@
             out[:, t : t + tile] = total[here, :]
 
 
-def expert_rows(expert_id, payloads, own, other, after, experts):
+def expert_rows(expert_id, payloads, own, other, after):
     width = own[0].shape[0]
     hidden = own[1].shape[0]
-    rows = sum(p.shape[0] for p in payloads)
+    rows = HALF * len(payloads)
     vmem = pl.BlockSpec(memory_space=pltpu.VMEM)
     chain = [] if after is None else [after]
     return pl.pallas_call(
-        functools.partial(mlp_kernel, parts=len(payloads), chained=len(chain), experts=experts),
-        out_shape=[jax.ShapeDtypeStruct((p.shape[0], width), jnp.float32) for p in payloads],
+        functools.partial(mlp_kernel, parts=len(payloads), chained=len(chain)),
+        out_shape=[jax.ShapeDtypeStruct((HALF, width), jnp.float32)] * len(payloads),
         in_specs=[pl.BlockSpec(memory_space=pltpu.SMEM)]
         + [vmem] * (len(payloads) + 4)
         + [pl.BlockSpec(memory_space=pl.ANY)] * len(chain),
@@ -250,7 +253,7 @@
     section_id = lax.axis_index("section").astype(jnp.int32).reshape(1)
     expert_id = lax.axis_index("expert").astype(jnp.int32).reshape(1)
     rows = fresh.shape[0]
-    half = rows // 2
+    half = HALF
     chips = devices_exp // CORES
     ring = chip_ring(chips // across, across)
     links = list(zip(ring, ring[1:] + ring[:1]))
@@ -265,9 +268,9 @@
     own = (w_gate_up[0, 0], w_down[0, 0])
     swapped = lax.optimization_barrier((*own, section_id, expert_id))[:2]
     other = tuple(move(w, swap) for w in swapped)
-    base, fresh, gain = base_rows(fresh, norm_gain, routes[0].T, gate_weights[0].T, devices_exp)
+    base, coefs, fresh, gain = base_rows(fresh, norm_gain, routes[0].T, gate_weights[0].T, devices_exp)
     arrived = [from_behind(previous[0, cut], "section", 1) for cut in cuts]
-    packed, arrival = zip(*(norm_rows(section_id, base, fresh, arrived[c], gain, cuts[c].start) for c in range(2)))
+    packed, arrival = zip(*(norm_rows(section_id, base, coefs, fresh, arrived[c], gain, c) for c in range(2)))
     packed = list(packed)
 
     hops = chips // 2
@@ -285,19 +288,19 @@
 
     def mlp(payloads):
         nonlocal last
-        sums = expert_rows(expert_id, payloads, own, other, last, devices_exp)
+        sums = expert_rows(expert_id, payloads, own, other, last)
         last = sums[0]
         return sums
 
     to_down, to_up = {}, {}
     pass_on(0, 0, None)
     pass_on(0, 1, None)
+    own_sums = mlp(packed)
     for s in range(1, hops):
         for c in range(2):
             pass_on(s, c, last)
             to_down[s, c], to_up[s, c] = mlp([ups[s][c], downs[s][c]])
     to_up[hops, 0], to_down[hops, 1] = mlp([ups[hops][0], downs[hops][1]])
-    own_sums = mlp(packed)
 
     def send_on(flow, place, total, after):
         terms, c, pairs = flow
@@ -333,7 +336,8 @@
 
     def body(*args):
         topk_count, local_experts = args[3].shape[2], args[5].shape[1]
-        if local_experts == 1 and devices_exp <= 2 * topk_count and devices_exp % (2 * CORES * across) == 0:
+        regular = devices_exp % (2 * CORES * across) == 0 and devices_exp % 16 == 0 and args[0].shape[0] == LANES
+        if local_experts == 1 and devices_exp <= 2 * topk_count and regular:
             return relay_body(*args, across=across)
         return routed_body(*args)
 

time: 109 us -> 103 us (0.945); the launches traced: 108 us -> 103 us
  starting transfers between devices: 39.2 us -> 36.8 us
  waiting for transfers between devices: 36.4 us -> 34.4 us
    ppermute x2, starting transfers between devices: 9.39 us -> 6.18 us  [from_behind(): return lax.ppermute(value, axis, pairs)]
    ppermute x2, waiting for transfers between devices: 6.32 us -> 4.5 us  [from_behind(): return lax.ppermute(value, axis, pairs)]
  transfers between devices with their start and end apart: 32 -> 32, of which waited for: 16 -> 13; matrix products, arithmetic and copies ran while one was open for 2% -> 2% of each run, Pallas kernels for 21% -> 22%
where the time goes in v7:
time: 103 us
  starting transfers between devices  36.8 us (36%)
  waiting for transfers between devices  34.4 us (33%)
  Pallas kernels  23.5 us (23%)
  local copies, waits for them, and re-layouts  7.22 us (7%)
    ppermute x30, starting transfers between devices, move(): return lax.ppermute(value, 'expert', pairs)  30.7 us
    ppermute x30, waiting for transfers between devices, move(): return lax.ppermute(value, 'expert', pairs)  29.9 us
    pallas_call x8, Pallas kernels, expert_rows(): pl.pallas_call(functools.partial(mlp_kernel, parts=len(payloads), chained...  22.3 us
    ppermute x2, starting transfers between devices, from_behind(): return lax.ppermute(value, axis, pairs)  6.18 us
    unnamed x12, local copies, waits for them, and re-layouts  5.9 us
    ppermute x2, waiting for transfers between devices, from_behind(): return lax.ppermute(value, axis, pairs)  4.5 us
  transfers between devices with their start and end apart: 32, of which 13 were waited for; matrix products, arithmetic and copies ran while one was open for 2% of the time, Pallas kernels for 22%

profile of v7, /device:TPU:0, one launch (start us, length us, event | category | flops | bytes accessed | tf_op | source)
XLA Modules:
  0.0 103.1 jit_solution(9003258447571491822)
XLA Ops:
  0.0 0.5 collective-permute-start.2
  0.5 0.1 collective-permute-start.3
  0.5 1.3 %slice_bitcast_fusion = (bf16[64,2048]{1,0:T(8,128)(2,1)S(1)}, bf16[64,2048]{1,0:T(8,128)(2,1)S(1)}) fusion(bf16[1,128,2048]{2,1,0:T(8,128)(2,1)} %param.8), kind=kLoop, calls=%fused_computation.12 | loop fusion | bytes 1048576 | tf_op jit(solution)/shard_map/squeeze | solution.py:272
  1.9 4.9 %collective-permute-start = (bf16[64,2048]{1,0:T(8,128)(2,1)S(1)}, bf16[64,2048]{1,0:T(8,128)(2,1)S(1)}, u32[]{:S(2)}, u32[]{:S(2)}) collective-permute-start(bf16[64,2048]{1,0:T(8,128)(2,1)S(1)} %get-tuple-element.110), channel_id=1, source_target_pairs={{0,16},{1,17},{2,18},{3,19},{4,20},{5,21},{6,22},{7,23},{8,24},{9,... | collective-permute-start | bytes 786440 | tf_op jit(solution)/shard_map/ppermute | solution.py:20
  6.7 1.3 %collective-permute-start.1 = (bf16[64,2048]{1,0:T(8,128)(2,1)S(1)}, bf16[64,2048]{1,0:T(8,128)(2,1)S(1)}, u32[]{:S(2)}, u32[]{:S(2)}) collective-permute-start(bf16[64,2048]{1,0:T(8,128)(2,1)S(1)} %get-tuple-element.109), channel_id=1, source_target_pairs={{0,16},{1,17},{2,18},{3,19},{4,20},{5,21},{6,22},{7,23},{8,24},{9,... | collective-permute-start | bytes 786440 | tf_op jit(solution)/shard_map/ppermute | solution.py:20
  8.1 1.0 %copy-done.2 = bf16[128,2048]{1,0:T(8,128)(2,1)S(1)} copy-done((bf16[128,2048]{1,0:T(8,128)(2,1)S(1)}, bf16[128,2048]{1,0:T(8,128)(2,1)}, u32[]{:S(2)}) %copy-start.2) | copy-done | bytes 524312
  9.1 0.7 copy-done.3
  9.8 0.7 copy-done.4
  10.5 0.7 copy-done.5
  11.2 0.2 base_rows.1
  11.4 2.0 %collective-permute-done.arrived_ref = bf16[64,2048]{1,0:T(8,128)(2,1)S(1)} collective-permute-done((bf16[64,2048]{1,0:T(8,128)(2,1)S(1)}, bf16[64,2048]{1,0:T(8,128)(2,1)S(1)}, u32[]{:S(2)}, u32[]{:S(2)}) %collective-permute-start) | collective-permute-done | bytes 262176 | tf_op jit(solution)/shard_map/ppermute | solution.py:20
  13.5 1.5 %collective-permute-start.4 = (bf16[1040,128]{1,0:T(8,128)(2,1)S(1)}, bf16[1040,128]{1,0:T(8,128)(2,1)S(1)}, u32[]{:S(2)}, u32[]{:S(2)}) collective-permute-start(bf16[1040,128]{1,0:T(8,128)(2,1)S(1)} %get-tuple-element.68.refs_0_), channel_id=1, source_target_pairs={{2,6},{3,7},{6,10},{7,11},{10,14},{11,15},{14,12},{15,13},{12,8},{... | collective-permute-start | bytes 798728 | tf_op jit(solution)/shard_map/ppermute | solution.py:265
  15.0 0.5 collective-permute-start.5
  15.5 2.5 %collective-permute-done.1.arrived_ref = bf16[64,2048]{1,0:T(8,128)(2,1)S(1)} collective-permute-done((bf16[64,2048]{1,0:T(8,128)(2,1)S(1)}, bf16[64,2048]{1,0:T(8,128)(2,1)S(1)}, u32[]{:S(2)}, u32[]{:S(2)}) %collective-permute-start.1) | collective-permute-done | bytes 262176 | tf_op jit(solution)/shard_map/ppermute | solution.py:20
  18.1 1.5 %collective-permute-start.8 = (bf16[1040,128]{1,0:T(8,128)(2,1)S(1)}, bf16[1040,128]{1,0:T(8,128)(2,1)S(1)}, u32[]{:S(2)}, u32[]{:S(2)}) collective-permute-start(bf16[1040,128]{1,0:T(8,128)(2,1)S(1)} %get-tuple-element.73.refs_1_), channel_id=1, source_target_pairs={{2,6},{3,7},{6,10},{7,11},{10,14},{11,15},{14,12},{15,13},{12,8},{... | collective-permute-start | bytes 798728 | tf_op jit(solution)/shard_map/ppermute | solution.py:265
  19.7 0.5 collective-permute-start.9
  20.2 2.8 %copy-done = bf16[1,1,2048,1536]{3,2,1,0:T(8,128)(2,1)S(1)} copy-done((bf16[1,1,2048,1536]{3,2,1,0:T(8,128)(2,1)S(1)}, bf16[1,1,2048,1536]{3,2,1,0:T(8,128)(2,1)}, u32[]{:S(2)}) %copy-start) | copy-done | bytes 6291480
  23.0 2.8 %expert_rows.8 = (f32[64,2048]{1,0:T(8,128)S(1)}, f32[64,2048]{1,0:T(8,128)S(1)}) custom-call(s32[1]{0:T(128)} %bitcast.6.expert_ref, bf16[1040,128]{1,0:T(8,128)(2,1)S(1)} %get-tuple-element.68.refs_0_, bf16[1040,128]{1,0:T(8,128)(2,1)S(1)} %get-tuple-element.73.refs_1_, bf16[2048,1536]{1,0:T(8,128)(2,1)S(1)} %bitcast.16, bf16[768,2048]{1,0:T(8,128)(2,1)S(1)} %bitcast.25, ...), custom_call_target="tpu_custom_call" | custom-call | flops 2415919104 | bytes 1572864 | tf_op jit(solution)/shard_map/expert_rows/pallas_call | solution.py:200
  25.8 1.5 %collective-permute-start.6 = (bf16[1040,128]{1,0:T(8,128)(2,1)S(1)}, bf16[1040,128]{1,0:T(8,128)(2,1)S(1)}, u32[]{:S(2)}, u32[]{:S(2)}) collective-permute-start(bf16[1040,128]{1,0:T(8,128)(2,1)S(1)} %collective-permute-done.4.refs_0_), channel_id=1, source_target_pairs={{2,6},{3,7},{6,10},{7,11},{10,14},{11,15},{14,12},{15,13},{12,8},{... | collective-permute-start | bytes 798728 | tf_op jit(solution)/shard_map/ppermute | solution.py:265
  27.4 0.5 collective-permute-start.7
  27.9 2.8 %expert_rows.9 = (f32[64,2048]{1,0:T(8,128)S(1)}, f32[64,2048]{1,0:T(8,128)S(1)}) custom-call(s32[1]{0:T(128)} %bitcast.6.expert_ref, bf16[1040,128]{1,0:T(8,128)(2,1)S(1)} %collective-permute-done.4.refs_0_, bf16[1040,128]{1,0:T(8,128)(2,1)S(1)} %collective-permute-done.5.refs_1_, bf16[2048,1536]{1,0:T(8,128)(2,1)S(1)} %bitcast.17, ...), custom_call_target="tpu_custom_call" | custom-call | flops 2415919104 | bytes 1572864 | tf_op jit(solution)/shard_map/expert_rows/pallas_call | solution.py:200
  30.7 1.5 %collective-permute-start.12 = (bf16[1040,128]{1,0:T(8,128)(2,1)S(1)}, bf16[1040,128]{1,0:T(8,128)(2,1)S(1)}, u32[]{:S(2)}, u32[]{:S(2)}) collective-permute-start(bf16[1040,128]{1,0:T(8,128)(2,1)S(1)} %collective-permute-done.8.refs_0_), channel_id=1, source_target_pairs={{2,6},{3,7},{6,10},{7,11},{10,14},{11,15},{14,12},{15,13},{12,8},{... | collective-permute-start | bytes 798728 | tf_op jit(solution)/shard_map/ppermute | solution.py:265
  32.3 0.5 collective-permute-start.13
  32.8 2.8 %expert_rows.10 = (f32[64,2048]{1,0:T(8,128)S(1)}, f32[64,2048]{1,0:T(8,128)S(1)}) custom-call(s32[1]{0:T(128)} %bitcast.6.expert_ref, bf16[1040,128]{1,0:T(8,128)(2,1)S(1)} %collective-permute-done.8.refs_0_, bf16[1040,128]{1,0:T(8,128)(2,1)S(1)} %collective-permute-done.9.refs_1_, bf16[2048,1536]{1,0:T(8,128)(2,1)S(1)} %bitcast.18, ...), custom_call_target="tpu_custom_call" | custom-call | flops 2415919104 | bytes 1572864 | tf_op jit(solution)/shard_map/expert_rows/pallas_call | solution.py:200
  35.6 1.5 %collective-permute-start.10 = (bf16[1040,128]{1,0:T(8,128)(2,1)S(1)}, bf16[1040,128]{1,0:T(8,128)(2,1)S(1)}, u32[]{:S(2)}, u32[]{:S(2)}) collective-permute-start(bf16[1040,128]{1,0:T(8,128)(2,1)S(1)} %collective-permute-done.6.refs_0_), channel_id=1, source_target_pairs={{2,6},{3,7},{6,10},{7,11},{10,14},{11,15},{14,12},{15,13},{12,8},{... | collective-permute-start | bytes 798728 | tf_op jit(solution)/shard_map/ppermute | solution.py:265
  37.1 0.5 collective-permute-start.11
  37.7 2.8 %expert_rows.11 = (f32[64,2048]{1,0:T(8,128)S(1)}, f32[64,2048]{1,0:T(8,128)S(1)}) custom-call(s32[1]{0:T(128)} %bitcast.6.expert_ref, bf16[1040,128]{1,0:T(8,128)(2,1)S(1)} %collective-permute-done.6.refs_0_, bf16[1040,128]{1,0:T(8,128)(2,1)S(1)} %collective-permute-done.7.refs_1_, bf16[2048,1536]{1,0:T(8,128)(2,1)S(1)} %bitcast.19, ...), custom_call_target="tpu_custom_call" | custom-call | flops 2415919104 | bytes 1572864 | tf_op jit(solution)/shard_map/expert_rows/pallas_call | solution.py:200
  40.5 1.1 %collective-permute-done.13.refs_1_ = bf16[1040,128]{1,0:T(8,128)(2,1)S(1)} collective-permute-done((bf16[1040,128]{1,0:T(8,128)(2,1)S(1)}, bf16[1040,128]{1,0:T(8,128)(2,1)S(1)}, u32[]{:S(2)}, u32[]{:S(2)}) %collective-permute-start.13) | collective-permute-done | bytes 266272 | tf_op jit(solution)/shard_map/ppermute | solution.py:265
  41.6 1.6 %collective-permute-start.16 = (bf16[1040,128]{1,0:T(8,128)(2,1)S(1)}, bf16[1040,128]{1,0:T(8,128)(2,1)S(1)}, u32[]{:S(2)}, u32[]{:S(2)}) collective-permute-start(bf16[1040,128]{1,0:T(8,128)(2,1)S(1)} %collective-permute-done.12.refs_0_), channel_id=1, source_target_pairs={{2,6},{3,7},{6,10},{7,11},{10,14},{11,15},{14,12},{15,13},{12,8},{... | collective-permute-start | bytes 798728 | tf_op jit(solution)/shard_map/ppermute | solution.py:265
  43.2 0.4 collective-permute-start.17
  43.6 2.8 %expert_rows.12 = (f32[64,2048]{1,0:T(8,128)S(1)}, f32[64,2048]{1,0:T(8,128)S(1)}) custom-call(s32[1]{0:T(128)} %bitcast.6.expert_ref, bf16[1040,128]{1,0:T(8,128)(2,1)S(1)} %collective-permute-done.12.refs_0_, bf16[1040,128]{1,0:T(8,128)(2,1)S(1)} %collective-permute-done.13.refs_1_, bf16[2048,1536]{1,0:T(8,128)(2,1)S(1)} %bitcast.20, ...), custom_call_target="tpu_custom_call" | custom-call | flops 2415919104 | bytes 1572864 | tf_op jit(solution)/shard_map/expert_rows/pallas_call | solution.py:200
  46.4 0.9 collective-permute-done.11.refs_1_
  47.3 1.6 %collective-permute-start.15 = (bf16[1040,128]{1,0:T(8,128)(2,1)S(1)}, bf16[1040,128]{1,0:T(8,128)(2,1)S(1)}, u32[]{:S(2)}, u32[]{:S(2)}) collective-permute-start(bf16[1040,128]{1,0:T(8,128)(2,1)S(1)} %collective-permute-done.10.refs_0_), channel_id=1, source_target_pairs={{2,6},{3,7},{6,10},{7,11},{10,14},{11,15},{14,12},{15,13},{12,8},{... | collective-permute-start | bytes 798728 | tf_op jit(solution)/shard_map/ppermute | solution.py:265
  48.9 2.8 %expert_rows.13 = (f32[64,2048]{1,0:T(8,128)S(1)}, f32[64,2048]{1,0:T(8,128)S(1)}) custom-call(s32[1]{0:T(128)} %bitcast.6.expert_ref, bf16[1040,128]{1,0:T(8,128)(2,1)S(1)} %collective-permute-done.10.refs_0_, bf16[1040,128]{1,0:T(8,128)(2,1)S(1)} %collective-permute-done.11.refs_1_, bf16[2048,1536]{1,0:T(8,128)(2,1)S(1)} %bitcast.21, ...), custom_call_target="tpu_custom_call" | custom-call | flops 2415919104 | bytes 1572864 | tf_op jit(solution)/shard_map/expert_rows/pallas_call | solution.py:200
  51.7 1.4 %collective-permute-start.18 = (bf16[1040,128]{1,0:T(8,128)(2,1)S(1)}, bf16[1040,128]{1,0:T(8,128)(2,1)S(1)}, u32[]{:S(2)}, u32[]{:S(2)}) collective-permute-start(bf16[1040,128]{1,0:T(8,128)(2,1)S(1)} %collective-permute-done.17.refs_1_), channel_id=1, source_target_pairs={{6,2},{7,3},{10,6},{11,7},{14,10},{15,11},{12,14},{13,15},{8,12},{... | collective-permute-start | bytes 798728 | tf_op jit(solution)/shard_map/ppermute | solution.py:265
  53.1 2.8 %expert_rows.14 = (f32[64,2048]{1,0:T(8,128)S(1)}, f32[64,2048]{1,0:T(8,128)S(1)}) custom-call(s32[1]{0:T(128)} %bitcast.6.expert_ref, bf16[1040,128]{1,0:T(8,128)(2,1)S(1)} %collective-permute-done.16.refs_0_, bf16[1040,128]{1,0:T(8,128)(2,1)S(1)} %collective-permute-done.17.refs_1_, bf16[2048,1536]{1,0:T(8,128)(2,1)S(1)} %bitcast.22, ...), custom_call_target="tpu_custom_call" | custom-call | flops 2415919104 | bytes 1572864 | tf_op jit(solution)/shard_map/expert_rows/pallas_call | solution.py:200
  55.9 0.7 collective-permute-start.21
  56.7 1.4 %collective-permute-start.14 = (bf16[64,2048]{1,0:T(8,128)(2,1)S(1)}, bf16[64,2048]{1,0:T(8,128)(2,1)S(1)}, u32[]{:S(2)}, u32[]{:S(2)}) collective-permute-start(bf16[64,2048]{1,0:T(8,128)(2,1)S(1)} %convert_element_type.85), channel_id=1, source_target_pairs={{6,2},{7,3},{10,6},{11,7},{14,10},{15,11},{12,14},{13,15},{8,12},{... | collective-permute-start | bytes 786440 | tf_op jit(solution)/shard_map/ppermute | solution.py:265
  58.1 1.8 %collective-permute-done.18.refs_1_ = bf16[1040,128]{1,0:T(8,128)(2,1)S(1)} collective-permute-done((bf16[1040,128]{1,0:T(8,128)(2,1)S(1)}, bf16[1040,128]{1,0:T(8,128)(2,1)S(1)}, u32[]{:S(2)}, u32[]{:S(2)}) %collective-permute-start.18) | collective-permute-done | bytes 266272 | tf_op jit(solution)/shard_map/ppermute | solution.py:265
  59.9 2.8 %expert_rows.15 = (f32[64,2048]{1,0:T(8,128)S(1)}, f32[64,2048]{1,0:T(8,128)S(1)}) custom-call(s32[1]{0:T(128)} %bitcast.6.expert_ref, bf16[1040,128]{1,0:T(8,128)(2,1)S(1)} %collective-permute-done.15.refs_0_, bf16[1040,128]{1,0:T(8,128)(2,1)S(1)} %collective-permute-done.18.refs_1_, bf16[2048,1536]{1,0:T(8,128)(2,1)S(1)} %bitcast.23, ...), custom_call_target="tpu_custom_call" | custom-call | flops 2415919104 | bytes 1572864 | tf_op jit(solution)/shard_map/expert_rows/pallas_call | solution.py:200
  62.8 1.0 collective-permute-done.14
  63.8 1.6 %collective-permute-start.20 = (bf16[64,2048]{1,0:T(8,128)(2,1)S(1)}, bf16[64,2048]{1,0:T(8,128)(2,1)S(1)}, u32[]{:S(2)}, u32[]{:S(2)}) collective-permute-start(bf16[64,2048]{1,0:T(8,128)(2,1)S(1)} %convert_element_type.88), channel_id=1, source_target_pairs={{2,6},{3,7},{6,10},{7,11},{10,14},{11,15},{14,12},{15,13},{12,8},{... | collective-permute-start | bytes 786440 | tf_op jit(solution)/shard_map/ppermute | solution.py:265
  65.4 0.5 collective-permute-start.19
  65.9 1.4 %collective-permute-start.22 = (bf16[64,2048]{1,0:T(8,128)(2,1)S(1)}, bf16[64,2048]{1,0:T(8,128)(2,1)S(1)}, u32[]{:S(2)}, u32[]{:S(2)}) collective-permute-start(bf16[64,2048]{1,0:T(8,128)(2,1)S(1)} %convert_element_type.94), channel_id=1, source_target_pairs={{6,2},{7,3},{10,6},{11,7},{14,10},{15,11},{12,14},{13,15},{8,12},{... | collective-permute-start | bytes 786440 | tf_op jit(solution)/shard_map/ppermute | solution.py:265
  67.3 0.7 collective-permute-start.24
  68.0 4.8 %collective-permute-done.20 = bf16[64,2048]{1,0:T(8,128)(2,1)S(1)} collective-permute-done((bf16[64,2048]{1,0:T(8,128)(2,1)S(1)}, bf16[64,2048]{1,0:T(8,128)(2,1)S(1)}, u32[]{:S(2)}, u32[]{:S(2)}) %collective-permute-start.20) | collective-permute-done | bytes 262176 | tf_op jit(solution)/shard_map/ppermute | solution.py:265
  72.8 4.6 %collective-permute-done.22 = bf16[64,2048]{1,0:T(8,128)(2,1)S(1)} collective-permute-done((bf16[64,2048]{1,0:T(8,128)(2,1)S(1)}, bf16[64,2048]{1,0:T(8,128)(2,1)S(1)}, u32[]{:S(2)}, u32[]{:S(2)}) %collective-permute-start.22) | collective-permute-done | bytes 262176 | tf_op jit(solution)/shard_map/ppermute | solution.py:265
  77.4 0.1 add_convert_fusion.6
  77.5 0.5 collective-permute-start.28
  78.0 1.6 %collective-permute-start.26 = (bf16[64,2048]{1,0:T(8,128)(2,1)S(1)}, bf16[64,2048]{1,0:T(8,128)(2,1)S(1)}, u32[]{:S(2)}, u32[]{:S(2)}) collective-permute-start(bf16[64,2048]{1,0:T(8,128)(2,1)S(1)} %get-tuple-element.112), channel_id=1, source_target_pairs={{2,6},{3,7},{6,10},{7,11},{10,14},{11,15},{14,12},{15,13},{12,8},{... | collective-permute-start | bytes 786440 | tf_op jit(solution)/shard_map/ppermute | solution.py:265
  79.6 0.5 collective-permute-start.23
  80.2 1.6 %collective-permute-start.25 = (bf16[64,2048]{1,0:T(8,128)(2,1)S(1)}, bf16[64,2048]{1,0:T(8,128)(2,1)S(1)}, u32[]{:S(2)}, u32[]{:S(2)}) collective-permute-start(bf16[64,2048]{1,0:T(8,128)(2,1)S(1)} %add_convert_fusion.4), channel_id=1, source_target_pairs={{2,6},{3,7},{6,10},{7,11},{10,14},{11,15},{14,12},{15,13},{12,8},{... | collective-permute-start | bytes 786440 | tf_op jit(solution)/shard_map/ppermute | solution.py:265
  81.8 5.0 %collective-permute-done.28 = bf16[64,2048]{1,0:T(8,128)(2,1)S(1)} collective-permute-done((bf16[64,2048]{1,0:T(8,128)(2,1)S(1)}, bf16[64,2048]{1,0:T(8,128)(2,1)S(1)}, u32[]{:S(2)}, u32[]{:S(2)}) %collective-permute-start.28) | collective-permute-done | bytes 262176 | tf_op jit(solution)/shard_map/ppermute | solution.py:265
  86.8 0.5 collective-permute-start.30
  87.4 1.6 %collective-permute-start.27 = (bf16[64,2048]{1,0:T(8,128)(2,1)S(1)}, bf16[64,2048]{1,0:T(8,128)(2,1)S(1)}, u32[]{:S(2)}, u32[]{:S(2)}) collective-permute-start(bf16[64,2048]{1,0:T(8,128)(2,1)S(1)} %add_convert_fusion.3), channel_id=1, source_target_pairs={{2,6},{3,7},{6,10},{7,11},{10,14},{11,15},{14,12},{15,13},{12,8},{... | collective-permute-start | bytes 786440 | tf_op jit(solution)/shard_map/ppermute | solution.py:265
  89.0 1.9 %collective-permute-done.23 = bf16[64,2048]{1,0:T(8,128)(2,1)S(1)} collective-permute-done((bf16[64,2048]{1,0:T(8,128)(2,1)S(1)}, bf16[64,2048]{1,0:T(8,128)(2,1)S(1)}, u32[]{:S(2)}, u32[]{:S(2)}) %collective-permute-start.23) | collective-permute-done | bytes 262176 | tf_op jit(solution)/shard_map/ppermute | solution.py:265
  90.9 0.1 add_add_fusion.1.near0_ref
  91.0 4.1 %collective-permute-done.30 = bf16[64,2048]{1,0:T(8,128)(2,1)S(1)} collective-permute-done((bf16[64,2048]{1,0:T(8,128)(2,1)S(1)}, bf16[64,2048]{1,0:T(8,128)(2,1)S(1)}, u32[]{:S(2)}, u32[]{:S(2)}) %collective-permute-start.30) | collective-permute-done | bytes 262176 | tf_op jit(solution)/shard_map/ppermute | solution.py:265
  95.2 0.5 collective-permute-start.31
  95.8 1.6 %collective-permute-start.29 = (bf16[64,2048]{1,0:T(8,128)(2,1)S(1)}, bf16[64,2048]{1,0:T(8,128)(2,1)S(1)}, u32[]{:S(2)}, u32[]{:S(2)}) collective-permute-start(bf16[64,2048]{1,0:T(8,128)(2,1)S(1)} %add_convert_fusion.1), channel_id=1, source_target_pairs={{2,6},{3,7},{6,10},{7,11},{10,14},{11,15},{14,12},{15,13},{12,8},{... | collective-permute-start | bytes 786440 | tf_op jit(solution)/shard_map/ppermute | solution.py:265
  97.4 0.1 add_add_fusion.near1_ref
  97.5 4.2 %collective-permute-done.31.total1_ref = bf16[64,2048]{1,0:T(8,128)(2,1)S(1)} collective-permute-done((bf16[64,2048]{1,0:T(8,128)(2,1)S(1)}, bf16[64,2048]{1,0:T(8,128)(2,1)S(1)}, u32[]{:S(2)}, u32[]{:S(2)}) %collective-permute-start.31) | collective-permute-done | bytes 262176 | tf_op jit(solution)/shard_map/ppermute | solution.py:265
  101.6 0.6 collective-permute-done.29.total0_ref
  102.2 0.9 last_rows.1
  (40 shorter events, 0.7 us)
Async XLA Ops:
  0.0 20.2 %copy-start.1 = (bf16[1,1,768,2048]{3,2,1,0:T(8,128)(2,1)S(1)}, bf16[1,1,768,2048]{3,2,1,0:T(8,128)(2,1)}, u32[]{:S(2)}) copy-start(bf16[1,1,768,2048]{3,2,1,0:T(8,128)(2,1)} %param.13) | copy-start | bytes 9437188
  0.0 20.2 %collective-permute-start.2 = (bf16[2048,1536]{1,0:T(8,128)(2,1)}, bf16[2048,1536]{1,0:T(8,128)(2,1)S(1)}, u32[]{:S(2)}, u32[]{:S(2)}) collective-permute-start(bf16[2048,1536]{1,0:T(8,128)(2,1)} %bitcast.15), channel_id=1, source_target_pairs={{0,1},{1,0},{2,3},{3,2},{4,5},{5,4},{6,7},{7,6},{8,9},{9,8},{10,11... | collective-permute-start | bytes 18874376 | tf_op jit(solution)/shard_map/ppermute | solution.py:265
  0.5 19.2 %collective-permute-start.3 = (bf16[768,2048]{1,0:T(8,128)(2,1)}, bf16[768,2048]{1,0:T(8,128)(2,1)S(1)}, u32[]{:S(2)}, u32[]{:S(2)}) collective-permute-start(bf16[768,2048]{1,0:T(8,128)(2,1)} %bitcast.24), channel_id=1, source_target_pairs={{0,1},{1,0},{2,3},{3,2},{4,5},{5,4},{6,7},{7,6},{8,9},{9,8},{10,11... | collective-permute-start | bytes 9437192 | tf_op jit(solution)/shard_map/ppermute | solution.py:265
  1.9 11.5 %collective-permute-start = (bf16[64,2048]{1,0:T(8,128)(2,1)S(1)}, bf16[64,2048]{1,0:T(8,128)(2,1)S(1)}, u32[]{:S(2)}, u32[]{:S(2)}) collective-permute-start(bf16[64,2048]{1,0:T(8,128)(2,1)S(1)} %get-tuple-element.110), channel_id=1, source_target_pairs={{0,16},{1,17},{2,18},{3,19},{4,20},{5,21},{6,22},{7,23},{8,24},{9,... | collective-permute-start | bytes 786440 | tf_op jit(solution)/shard_map/ppermute | solution.py:20
  6.7 11.3 %collective-permute-start.1 = (bf16[64,2048]{1,0:T(8,128)(2,1)S(1)}, bf16[64,2048]{1,0:T(8,128)(2,1)S(1)}, u32[]{:S(2)}, u32[]{:S(2)}) collective-permute-start(bf16[64,2048]{1,0:T(8,128)(2,1)S(1)} %get-tuple-element.109), channel_id=1, source_target_pairs={{0,16},{1,17},{2,18},{3,19},{4,20},{5,21},{6,22},{7,23},{8,24},{9,... | collective-permute-start | bytes 786440 | tf_op jit(solution)/shard_map/ppermute | solution.py:20
  8.1 1.0 %copy-start.2 = (bf16[128,2048]{1,0:T(8,128)(2,1)S(1)}, bf16[128,2048]{1,0:T(8,128)(2,1)}, u32[]{:S(2)}) copy-start(bf16[128,2048]{1,0:T(8,128)(2,1)} %fresh_ref.1) | copy-start | bytes 1572868
  9.1 0.7 copy-start.3
  9.8 0.7 copy-start.4
  10.5 0.7 copy-start.5
  13.5 12.4 %collective-permute-start.4 = (bf16[1040,128]{1,0:T(8,128)(2,1)S(1)}, bf16[1040,128]{1,0:T(8,128)(2,1)S(1)}, u32[]{:S(2)}, u32[]{:S(2)}) collective-permute-start(bf16[1040,128]{1,0:T(8,128)(2,1)S(1)} %get-tuple-element.68.refs_0_), channel_id=1, source_target_pairs={{2,6},{3,7},{6,10},{7,11},{10,14},{11,15},{14,12},{15,13},{12,8},{... | collective-permute-start | bytes 798728 | tf_op jit(solution)/shard_map/ppermute | solution.py:265
  15.0 10.8 %collective-permute-start.5 = (bf16[1040,128]{1,0:T(8,128)(2,1)S(1)}, bf16[1040,128]{1,0:T(8,128)(2,1)S(1)}, u32[]{:S(2)}, u32[]{:S(2)}) collective-permute-start(bf16[1040,128]{1,0:T(8,128)(2,1)S(1)} %get-tuple-element.68.refs_0_), channel_id=1, source_target_pairs={{6,2},{7,3},{10,6},{11,7},{14,10},{15,11},{12,14},{13,15},{8,12},{... | collective-permute-start | bytes 798728 | tf_op jit(solution)/shard_map/ppermute | solution.py:265
  18.1 12.6 %collective-permute-start.8 = (bf16[1040,128]{1,0:T(8,128)(2,1)S(1)}, bf16[1040,128]{1,0:T(8,128)(2,1)S(1)}, u32[]{:S(2)}, u32[]{:S(2)}) collective-permute-start(bf16[1040,128]{1,0:T(8,128)(2,1)S(1)} %get-tuple-element.73.refs_1_), channel_id=1, source_target_pairs={{2,6},{3,7},{6,10},{7,11},{10,14},{11,15},{14,12},{15,13},{12,8},{... | collective-permute-start | bytes 798728 | tf_op jit(solution)/shard_map/ppermute | solution.py:265
  19.7 11.0 %collective-permute-start.9 = (bf16[1040,128]{1,0:T(8,128)(2,1)S(1)}, bf16[1040,128]{1,0:T(8,128)(2,1)S(1)}, u32[]{:S(2)}, u32[]{:S(2)}) collective-permute-start(bf16[1040,128]{1,0:T(8,128)(2,1)S(1)} %get-tuple-element.73.refs_1_), channel_id=1, source_target_pairs={{6,2},{7,3},{10,6},{11,7},{14,10},{15,11},{12,14},{13,15},{8,12},{... | collective-permute-start | bytes 798728 | tf_op jit(solution)/shard_map/ppermute | solution.py:265
  20.2 2.8 %copy-start = (bf16[1,1,2048,1536]{3,2,1,0:T(8,128)(2,1)S(1)}, bf16[1,1,2048,1536]{3,2,1,0:T(8,128)(2,1)}, u32[]{:S(2)}) copy-start(bf16[1,1,2048,1536]{3,2,1,0:T(8,128)(2,1)} %param.12) | copy-start | bytes 18874372
  25.8 9.7 %collective-permute-start.6 = (bf16[1040,128]{1,0:T(8,128)(2,1)S(1)}, bf16[1040,128]{1,0:T(8,128)(2,1)S(1)}, u32[]{:S(2)}, u32[]{:S(2)}) collective-permute-start(bf16[1040,128]{1,0:T(8,128)(2,1)S(1)} %collective-permute-done.4.refs_0_), channel_id=1, source_target_pairs={{2,6},{3,7},{6,10},{7,11},{10,14},{11,15},{14,12},{15,13},{12,8},{... | collective-permute-start | bytes 798728 | tf_op jit(solution)/shard_map/ppermute | solution.py:265
  27.4 8.2 %collective-permute-start.7 = (bf16[1040,128]{1,0:T(8,128)(2,1)S(1)}, bf16[1040,128]{1,0:T(8,128)(2,1)S(1)}, u32[]{:S(2)}, u32[]{:S(2)}) collective-permute-start(bf16[1040,128]{1,0:T(8,128)(2,1)S(1)} %collective-permute-done.5.refs_1_), channel_id=1, source_target_pairs={{6,2},{7,3},{10,6},{11,7},{14,10},{15,11},{12,14},{13,15},{8,12},{... | collective-permute-start | bytes 798728 | tf_op jit(solution)/shard_map/ppermute | solution.py:265
  30.7 9.8 %collective-permute-start.12 = (bf16[1040,128]{1,0:T(8,128)(2,1)S(1)}, bf16[1040,128]{1,0:T(8,128)(2,1)S(1)}, u32[]{:S(2)}, u32[]{:S(2)}) collective-permute-start(bf16[1040,128]{1,0:T(8,128)(2,1)S(1)} %collective-permute-done.8.refs_0_), channel_id=1, source_target_pairs={{2,6},{3,7},{6,10},{7,11},{10,14},{11,15},{14,12},{15,13},{12,8},{... | collective-permute-start | bytes 798728 | tf_op jit(solution)/shard_map/ppermute | solution.py:265
  32.3 9.3 %collective-permute-start.13 = (bf16[1040,128]{1,0:T(8,128)(2,1)S(1)}, bf16[1040,128]{1,0:T(8,128)(2,1)S(1)}, u32[]{:S(2)}, u32[]{:S(2)}) collective-permute-start(bf16[1040,128]{1,0:T(8,128)(2,1)S(1)} %collective-permute-done.9.refs_1_), channel_id=1, source_target_pairs={{6,2},{7,3},{10,6},{11,7},{14,10},{15,11},{12,14},{13,15},{8,12},{... | collective-permute-start | bytes 798728 | tf_op jit(solution)/shard_map/ppermute | solution.py:265
  35.6 10.8 %collective-permute-start.10 = (bf16[1040,128]{1,0:T(8,128)(2,1)S(1)}, bf16[1040,128]{1,0:T(8,128)(2,1)S(1)}, u32[]{:S(2)}, u32[]{:S(2)}) collective-permute-start(bf16[1040,128]{1,0:T(8,128)(2,1)S(1)} %collective-permute-done.6.refs_0_), channel_id=1, source_target_pairs={{2,6},{3,7},{6,10},{7,11},{10,14},{11,15},{14,12},{15,13},{12,8},{... | collective-permute-start | bytes 798728 | tf_op jit(solution)/shard_map/ppermute | solution.py:265
  37.1 10.2 %collective-permute-start.11 = (bf16[1040,128]{1,0:T(8,128)(2,1)S(1)}, bf16[1040,128]{1,0:T(8,128)(2,1)S(1)}, u32[]{:S(2)}, u32[]{:S(2)}) collective-permute-start(bf16[1040,128]{1,0:T(8,128)(2,1)S(1)} %collective-permute-done.7.refs_1_), channel_id=1, source_target_pairs={{6,2},{7,3},{10,6},{11,7},{14,10},{15,11},{12,14},{13,15},{8,12},{... | collective-permute-start | bytes 798728 | tf_op jit(solution)/shard_map/ppermute | solution.py:265
  41.6 10.1 %collective-permute-start.16 = (bf16[1040,128]{1,0:T(8,128)(2,1)S(1)}, bf16[1040,128]{1,0:T(8,128)(2,1)S(1)}, u32[]{:S(2)}, u32[]{:S(2)}) collective-permute-start(bf16[1040,128]{1,0:T(8,128)(2,1)S(1)} %collective-permute-done.12.refs_0_), channel_id=1, source_target_pairs={{2,6},{3,7},{6,10},{7,11},{10,14},{11,15},{14,12},{15,13},{12,8},{... | collective-permute-start | bytes 798728 | tf_op jit(solution)/shard_map/ppermute | solution.py:265
  43.2 8.5 %collective-permute-start.17 = (bf16[1040,128]{1,0:T(8,128)(2,1)S(1)}, bf16[1040,128]{1,0:T(8,128)(2,1)S(1)}, u32[]{:S(2)}, u32[]{:S(2)}) collective-permute-start(bf16[1040,128]{1,0:T(8,128)(2,1)S(1)} %collective-permute-done.13.refs_1_), channel_id=1, source_target_pairs={{6,2},{7,3},{10,6},{11,7},{14,10},{15,11},{12,14},{13,15},{8,12},{... | collective-permute-start | bytes 798728 | tf_op jit(solution)/shard_map/ppermute | solution.py:265
  47.3 10.8 %collective-permute-start.15 = (bf16[1040,128]{1,0:T(8,128)(2,1)S(1)}, bf16[1040,128]{1,0:T(8,128)(2,1)S(1)}, u32[]{:S(2)}, u32[]{:S(2)}) collective-permute-start(bf16[1040,128]{1,0:T(8,128)(2,1)S(1)} %collective-permute-done.10.refs_0_), channel_id=1, source_target_pairs={{2,6},{3,7},{6,10},{7,11},{10,14},{11,15},{14,12},{15,13},{12,8},{... | collective-permute-start | bytes 798728 | tf_op jit(solution)/shard_map/ppermute | solution.py:265
  51.7 8.2 %collective-permute-start.18 = (bf16[1040,128]{1,0:T(8,128)(2,1)S(1)}, bf16[1040,128]{1,0:T(8,128)(2,1)S(1)}, u32[]{:S(2)}, u32[]{:S(2)}) collective-permute-start(bf16[1040,128]{1,0:T(8,128)(2,1)S(1)} %collective-permute-done.17.refs_1_), channel_id=1, source_target_pairs={{6,2},{7,3},{10,6},{11,7},{14,10},{15,11},{12,14},{13,15},{8,12},{... | collective-permute-start | bytes 798728 | tf_op jit(solution)/shard_map/ppermute | solution.py:265
  55.9 6.8 %collective-permute-start.21 = (bf16[64,2048]{1,0:T(8,128)(2,1)S(1)}, bf16[64,2048]{1,0:T(8,128)(2,1)S(1)}, u32[]{:S(2)}, u32[]{:S(2)}) collective-permute-start(bf16[64,2048]{1,0:T(8,128)(2,1)S(1)} %convert_element_type.89), channel_id=1, source_target_pairs={{2,6},{3,7},{6,10},{7,11},{10,14},{11,15},{14,12},{15,13},{12,8},{... | collective-permute-start | bytes 786440 | tf_op jit(solution)/shard_map/ppermute | solution.py:265
  56.7 7.1 %collective-permute-start.14 = (bf16[64,2048]{1,0:T(8,128)(2,1)S(1)}, bf16[64,2048]{1,0:T(8,128)(2,1)S(1)}, u32[]{:S(2)}, u32[]{:S(2)}) collective-permute-start(bf16[64,2048]{1,0:T(8,128)(2,1)S(1)} %convert_element_type.85), channel_id=1, source_target_pairs={{6,2},{7,3},{10,6},{11,7},{14,10},{15,11},{12,14},{13,15},{8,12},{... | collective-permute-start | bytes 786440 | tf_op jit(solution)/shard_map/ppermute | solution.py:265
  63.8 9.0 %collective-permute-start.20 = (bf16[64,2048]{1,0:T(8,128)(2,1)S(1)}, bf16[64,2048]{1,0:T(8,128)(2,1)S(1)}, u32[]{:S(2)}, u32[]{:S(2)}) collective-permute-start(bf16[64,2048]{1,0:T(8,128)(2,1)S(1)} %convert_element_type.88), channel_id=1, source_target_pairs={{2,6},{3,7},{6,10},{7,11},{10,14},{11,15},{14,12},{15,13},{12,8},{... | collective-permute-start | bytes 786440 | tf_op jit(solution)/shard_map/ppermute | solution.py:265
  65.4 14.1 %collective-permute-start.19 = (bf16[64,2048]{1,0:T(8,128)(2,1)S(1)}, bf16[64,2048]{1,0:T(8,128)(2,1)S(1)}, u32[]{:S(2)}, u32[]{:S(2)}) collective-permute-start(bf16[64,2048]{1,0:T(8,128)(2,1)S(1)} %add_convert_fusion.9), channel_id=1, source_target_pairs={{6,2},{7,3},{10,6},{11,7},{14,10},{15,11},{12,14},{13,15},{8,12},{... | collective-permute-start | bytes 786440 | tf_op jit(solution)/shard_map/ppermute | solution.py:265
  65.9 11.5 %collective-permute-start.22 = (bf16[64,2048]{1,0:T(8,128)(2,1)S(1)}, bf16[64,2048]{1,0:T(8,128)(2,1)S(1)}, u32[]{:S(2)}, u32[]{:S(2)}) collective-permute-start(bf16[64,2048]{1,0:T(8,128)(2,1)S(1)} %convert_element_type.94), channel_id=1, source_target_pairs={{6,2},{7,3},{10,6},{11,7},{14,10},{15,11},{12,14},{13,15},{8,12},{... | collective-permute-start | bytes 786440 | tf_op jit(solution)/shard_map/ppermute | solution.py:265
  67.3 12.3 %collective-permute-start.24 = (bf16[64,2048]{1,0:T(8,128)(2,1)S(1)}, bf16[64,2048]{1,0:T(8,128)(2,1)S(1)}, u32[]{:S(2)}, u32[]{:S(2)}) collective-permute-start(bf16[64,2048]{1,0:T(8,128)(2,1)S(1)} %add_convert_fusion.8), channel_id=1, source_target_pairs={{2,6},{3,7},{6,10},{7,11},{10,14},{11,15},{14,12},{15,13},{12,8},{... | collective-permute-start | bytes 786440 | tf_op jit(solution)/shard_map/ppermute | solution.py:265
  77.5 9.3 %collective-permute-start.28 = (bf16[64,2048]{1,0:T(8,128)(2,1)S(1)}, bf16[64,2048]{1,0:T(8,128)(2,1)S(1)}, u32[]{:S(2)}, u32[]{:S(2)}) collective-permute-start(bf16[64,2048]{1,0:T(8,128)(2,1)S(1)} %get-tuple-element.111), channel_id=1, source_target_pairs={{6,2},{7,3},{10,6},{11,7},{14,10},{15,11},{12,14},{13,15},{8,12},{... | collective-permute-start | bytes 786440 | tf_op jit(solution)/shard_map/ppermute | solution.py:265
  78.0 9.4 %collective-permute-start.26 = (bf16[64,2048]{1,0:T(8,128)(2,1)S(1)}, bf16[64,2048]{1,0:T(8,128)(2,1)S(1)}, u32[]{:S(2)}, u32[]{:S(2)}) collective-permute-start(bf16[64,2048]{1,0:T(8,128)(2,1)S(1)} %get-tuple-element.112), channel_id=1, source_target_pairs={{2,6},{3,7},{6,10},{7,11},{10,14},{11,15},{14,12},{15,13},{12,8},{... | collective-permute-start | bytes 786440 | tf_op jit(solution)/shard_map/ppermute | solution.py:265
  79.6 11.3 %collective-permute-start.23 = (bf16[64,2048]{1,0:T(8,128)(2,1)S(1)}, bf16[64,2048]{1,0:T(8,128)(2,1)S(1)}, u32[]{:S(2)}, u32[]{:S(2)}) collective-permute-start(bf16[64,2048]{1,0:T(8,128)(2,1)S(1)} %add_convert_fusion.5), channel_id=1, source_target_pairs={{6,2},{7,3},{10,6},{11,7},{14,10},{15,11},{12,14},{13,15},{8,12},{... | collective-permute-start | bytes 786440 | tf_op jit(solution)/shard_map/ppermute | solution.py:265
  80.2 17.2 %collective-permute-start.25 = (bf16[64,2048]{1,0:T(8,128)(2,1)S(1)}, bf16[64,2048]{1,0:T(8,128)(2,1)S(1)}, u32[]{:S(2)}, u32[]{:S(2)}) collective-permute-start(bf16[64,2048]{1,0:T(8,128)(2,1)S(1)} %add_convert_fusion.4), channel_id=1, source_target_pairs={{2,6},{3,7},{6,10},{7,11},{10,14},{11,15},{14,12},{15,13},{12,8},{... | collective-permute-start | bytes 786440 | tf_op jit(solution)/shard_map/ppermute | solution.py:265
  86.8 8.3 %collective-permute-start.30 = (bf16[64,2048]{1,0:T(8,128)(2,1)S(1)}, bf16[64,2048]{1,0:T(8,128)(2,1)S(1)}, u32[]{:S(2)}, u32[]{:S(2)}) collective-permute-start(bf16[64,2048]{1,0:T(8,128)(2,1)S(1)} %add_convert_fusion.2), channel_id=1, source_target_pairs={{6,2},{7,3},{10,6},{11,7},{14,10},{15,11},{12,14},{13,15},{8,12},{... | collective-permute-start | bytes 786440 | tf_op jit(solution)/shard_map/ppermute | solution.py:265
  87.4 8.3 %collective-permute-start.27 = (bf16[64,2048]{1,0:T(8,128)(2,1)S(1)}, bf16[64,2048]{1,0:T(8,128)(2,1)S(1)}, u32[]{:S(2)}, u32[]{:S(2)}) collective-permute-start(bf16[64,2048]{1,0:T(8,128)(2,1)S(1)} %add_convert_fusion.3), channel_id=1, source_target_pairs={{2,6},{3,7},{6,10},{7,11},{10,14},{11,15},{14,12},{15,13},{12,8},{... | collective-permute-start | bytes 786440 | tf_op jit(solution)/shard_map/ppermute | solution.py:265
  95.2 6.4 %collective-permute-start.31 = (bf16[64,2048]{1,0:T(8,128)(2,1)S(1)}, bf16[64,2048]{1,0:T(8,128)(2,1)S(1)}, u32[]{:S(2)}, u32[]{:S(2)}) collective-permute-start(bf16[64,2048]{1,0:T(8,128)(2,1)S(1)} %add_convert_fusion), channel_id=1, source_target_pairs={{6,2},{7,3},{10,6},{11,7},{14,10},{15,11},{12,14},{13,15},{8,12},{... | collective-permute-start | bytes 786440 | tf_op jit(solution)/shard_map/ppermute | solution.py:265
  95.8 6.4 %collective-permute-start.29 = (bf16[64,2048]{1,0:T(8,128)(2,1)S(1)}, bf16[64,2048]{1,0:T(8,128)(2,1)S(1)}, u32[]{:S(2)}, u32[]{:S(2)}) collective-permute-start(bf16[64,2048]{1,0:T(8,128)(2,1)S(1)} %add_convert_fusion.1), channel_id=1, source_target_pairs={{2,6},{3,7},{6,10},{7,11},{10,14},{11,15},{14,12},{15,13},{12,8},{... | collective-permute-start | bytes 786440 | tf_op jit(solution)/shard_map/ppermute | solution.py:265

commit v8 on v7

--- a/solution.py
+++ b/solution.py
@@ -294,13 +294,13 @@
 
     to_down, to_up = {}, {}
     pass_on(0, 0, None)
-    pass_on(0, 1, None)
-    own_sums = mlp(packed)
+    pass_on(0, 1, other)
     for s in range(1, hops):
         for c in range(2):
             pass_on(s, c, last)
             to_down[s, c], to_up[s, c] = mlp([ups[s][c], downs[s][c]])
     to_up[hops, 0], to_down[hops, 1] = mlp([ups[hops][0], downs[hops][1]])
+    own_sums = mlp(packed)
 
     def send_on(flow, place, total, after):
         terms, c, pairs = flow

time: 103 us -> 102 us (level)
  waiting for transfers between devices: 34.4 us -> 33.2 us
    ppermute x30, waiting for transfers between devices: 29.9 us -> 28.7 us  [move(): return lax.ppermute(value, 'expert', pairs)]
  transfers between devices with their start and end apart: 32 -> 32, of which waited for: 13 -> 15; matrix products, arithmetic and copies ran while one was open for 2% -> 2% of each run, Pallas kernels for 22% -> 22%
where the time goes in v8:
time: 102 us
  starting transfers between devices  37 us (36%)
  waiting for transfers between devices  33.2 us (33%)
  Pallas kernels  23.3 us (23%)
  local copies, waits for them, and re-layouts  7.22 us (7%)
    ppermute x30, starting transfers between devices, move(): return lax.ppermute(value, 'expert', pairs)  30.8 us
    ppermute x30, waiting for transfers between devices, move(): return lax.ppermute(value, 'expert', pairs)  28.7 us
    pallas_call x8, Pallas kernels, expert_rows(): pl.pallas_call(functools.partial(mlp_kernel, parts=len(payloads), chained...  22 us
    ppermute x2, starting transfers between devices, from_behind(): return lax.ppermute(value, axis, pairs)  6.18 us
    unnamed x12, local copies, waits for them, and re-layouts  5.89 us
    ppermute x2, waiting for transfers between devices, from_behind(): return lax.ppermute(value, axis, pairs)  4.5 us
  transfers between devices with their start and end apart: 32, of which 15 were waited for; matrix products, arithmetic and copies ran while one was open for 2% of the time, Pallas kernels for 22%

profile of v8, /device:TPU:0, one launch (start us, length us, event | category | flops | bytes accessed | tf_op | source)
XLA Modules:
  0.0 101.9 jit_solution(4283591042444766338)
XLA Ops:
  0.0 0.5 collective-permute-start.2
  0.5 1.3 %slice_bitcast_fusion = (bf16[64,2048]{1,0:T(8,128)(2,1)S(1)}, bf16[64,2048]{1,0:T(8,128)(2,1)S(1)}) fusion(bf16[1,128,2048]{2,1,0:T(8,128)(2,1)} %param.8), kind=kLoop, calls=%fused_computation.12 | loop fusion | bytes 1048576 | tf_op jit(solution)/shard_map/squeeze | solution.py:272
  1.8 4.9 %collective-permute-start = (bf16[64,2048]{1,0:T(8,128)(2,1)S(1)}, bf16[64,2048]{1,0:T(8,128)(2,1)S(1)}, u32[]{:S(2)}, u32[]{:S(2)}) collective-permute-start(bf16[64,2048]{1,0:T(8,128)(2,1)S(1)} %get-tuple-element.110), channel_id=1, source_target_pairs={{0,16},{1,17},{2,18},{3,19},{4,20},{5,21},{6,22},{7,23},{8,24},{9,... | collective-permute-start | bytes 786440 | tf_op jit(solution)/shard_map/ppermute | solution.py:20
  6.7 1.3 %collective-permute-start.1 = (bf16[64,2048]{1,0:T(8,128)(2,1)S(1)}, bf16[64,2048]{1,0:T(8,128)(2,1)S(1)}, u32[]{:S(2)}, u32[]{:S(2)}) collective-permute-start(bf16[64,2048]{1,0:T(8,128)(2,1)S(1)} %get-tuple-element.109), channel_id=1, source_target_pairs={{0,16},{1,17},{2,18},{3,19},{4,20},{5,21},{6,22},{7,23},{8,24},{9,... | collective-permute-start | bytes 786440 | tf_op jit(solution)/shard_map/ppermute | solution.py:20
  8.1 1.0 %copy-done.2 = bf16[128,2048]{1,0:T(8,128)(2,1)S(1)} copy-done((bf16[128,2048]{1,0:T(8,128)(2,1)S(1)}, bf16[128,2048]{1,0:T(8,128)(2,1)}, u32[]{:S(2)}) %copy-start.2) | copy-done | bytes 524312
  9.1 0.7 copy-done.3
  9.8 0.7 copy-done.4
  10.5 0.7 copy-done.5
  11.2 0.2 base_rows.1
  11.4 2.0 %collective-permute-done.arrived_ref = bf16[64,2048]{1,0:T(8,128)(2,1)S(1)} collective-permute-done((bf16[64,2048]{1,0:T(8,128)(2,1)S(1)}, bf16[64,2048]{1,0:T(8,128)(2,1)S(1)}, u32[]{:S(2)}, u32[]{:S(2)}) %collective-permute-start) | collective-permute-done | bytes 262176 | tf_op jit(solution)/shard_map/ppermute | solution.py:20
  13.5 1.5 %collective-permute-start.4 = (bf16[1040,128]{1,0:T(8,128)(2,1)S(1)}, bf16[1040,128]{1,0:T(8,128)(2,1)S(1)}, u32[]{:S(2)}, u32[]{:S(2)}) collective-permute-start(bf16[1040,128]{1,0:T(8,128)(2,1)S(1)} %get-tuple-element.67.refs_0_), channel_id=1, source_target_pairs={{2,6},{3,7},{6,10},{7,11},{10,14},{11,15},{14,12},{15,13},{12,8},{... | collective-permute-start | bytes 798728 | tf_op jit(solution)/shard_map/ppermute | solution.py:265
  15.0 0.5 collective-permute-start.5
  15.5 2.5 %collective-permute-done.1.arrived_ref = bf16[64,2048]{1,0:T(8,128)(2,1)S(1)} collective-permute-done((bf16[64,2048]{1,0:T(8,128)(2,1)S(1)}, bf16[64,2048]{1,0:T(8,128)(2,1)S(1)}, u32[]{:S(2)}, u32[]{:S(2)}) %collective-permute-start.1) | collective-permute-done | bytes 262176 | tf_op jit(solution)/shard_map/ppermute | solution.py:20
  18.1 1.5 %collective-permute-start.8 = (bf16[1040,128]{1,0:T(8,128)(2,1)S(1)}, bf16[1040,128]{1,0:T(8,128)(2,1)S(1)}, u32[]{:S(2)}, u32[]{:S(2)}) collective-permute-start(bf16[1040,128]{1,0:T(8,128)(2,1)S(1)} %get-tuple-element.71.refs_1_), channel_id=1, source_target_pairs={{2,6},{3,7},{6,10},{7,11},{10,14},{11,15},{14,12},{15,13},{12,8},{... | collective-permute-start | bytes 798728 | tf_op jit(solution)/shard_map/ppermute | solution.py:265
  19.7 0.5 collective-permute-start.9
  20.2 1.3 %collective-permute-done.5.refs_1_ = bf16[1040,128]{1,0:T(8,128)(2,1)S(1)} collective-permute-done((bf16[1040,128]{1,0:T(8,128)(2,1)S(1)}, bf16[1040,128]{1,0:T(8,128)(2,1)S(1)}, u32[]{:S(2)}, u32[]{:S(2)}) %collective-permute-start.5) | collective-permute-done | bytes 266272 | tf_op jit(solution)/shard_map/ppermute | solution.py:265
  21.6 1.6 %collective-permute-start.6 = (bf16[1040,128]{1,0:T(8,128)(2,1)S(1)}, bf16[1040,128]{1,0:T(8,128)(2,1)S(1)}, u32[]{:S(2)}, u32[]{:S(2)}) collective-permute-start(bf16[1040,128]{1,0:T(8,128)(2,1)S(1)} %collective-permute-done.4.refs_0_), channel_id=1, source_target_pairs={{2,6},{3,7},{6,10},{7,11},{10,14},{11,15},{14,12},{15,13},{12,8},{... | collective-permute-start | bytes 798728 | tf_op jit(solution)/shard_map/ppermute | solution.py:265
  23.2 0.4 collective-permute-start.7
  23.6 2.8 %copy-done = bf16[1,1,2048,1536]{3,2,1,0:T(8,128)(2,1)S(1)} copy-done((bf16[1,1,2048,1536]{3,2,1,0:T(8,128)(2,1)S(1)}, bf16[1,1,2048,1536]{3,2,1,0:T(8,128)(2,1)}, u32[]{:S(2)}) %copy-start) | copy-done | bytes 6291480
  26.4 2.8 %expert_rows.8 = (f32[64,2048]{1,0:T(8,128)S(1)}, f32[64,2048]{1,0:T(8,128)S(1)}) custom-call(s32[1]{0:T(128)} %bitcast.6.expert_ref, bf16[1040,128]{1,0:T(8,128)(2,1)S(1)} %collective-permute-done.4.refs_0_, bf16[1040,128]{1,0:T(8,128)(2,1)S(1)} %collective-permute-done.5.refs_1_, bf16[2048,1536]{1,0:T(8,128)(2,1)S(1)} %bitcast.16, ...), custom_call_target="tpu_custom_call" | custom-call | flops 2415919104 | bytes 1572864 | tf_op jit(solution)/shard_map/expert_rows/pallas_call | solution.py:200
  29.2 1.6 %collective-permute-start.12 = (bf16[1040,128]{1,0:T(8,128)(2,1)S(1)}, bf16[1040,128]{1,0:T(8,128)(2,1)S(1)}, u32[]{:S(2)}, u32[]{:S(2)}) collective-permute-start(bf16[1040,128]{1,0:T(8,128)(2,1)S(1)} %collective-permute-done.8.refs_0_), channel_id=1, source_target_pairs={{2,6},{3,7},{6,10},{7,11},{10,14},{11,15},{14,12},{15,13},{12,8},{... | collective-permute-start | bytes 798728 | tf_op jit(solution)/shard_map/ppermute | solution.py:265
  30.8 0.4 collective-permute-start.13
  31.3 2.7 %expert_rows.9 = (f32[64,2048]{1,0:T(8,128)S(1)}, f32[64,2048]{1,0:T(8,128)S(1)}) custom-call(s32[1]{0:T(128)} %bitcast.6.expert_ref, bf16[1040,128]{1,0:T(8,128)(2,1)S(1)} %collective-permute-done.8.refs_0_, bf16[1040,128]{1,0:T(8,128)(2,1)S(1)} %collective-permute-done.9.refs_1_, bf16[2048,1536]{1,0:T(8,128)(2,1)S(1)} %bitcast.17, ...), custom_call_target="tpu_custom_call" | custom-call | flops 2415919104 | bytes 1572864 | tf_op jit(solution)/shard_map/expert_rows/pallas_call | solution.py:200
  34.0 0.7 collective-permute-done.7.refs_1_
  34.7 1.6 %collective-permute-start.10 = (bf16[1040,128]{1,0:T(8,128)(2,1)S(1)}, bf16[1040,128]{1,0:T(8,128)(2,1)S(1)}, u32[]{:S(2)}, u32[]{:S(2)}) collective-permute-start(bf16[1040,128]{1,0:T(8,128)(2,1)S(1)} %collective-permute-done.6.refs_0_), channel_id=1, source_target_pairs={{2,6},{3,7},{6,10},{7,11},{10,14},{11,15},{14,12},{15,13},{12,8},{... | collective-permute-start | bytes 798728 | tf_op jit(solution)/shard_map/ppermute | solution.py:265
  36.3 0.4 collective-permute-start.11
  36.8 2.7 %expert_rows.10 = (f32[64,2048]{1,0:T(8,128)S(1)}, f32[64,2048]{1,0:T(8,128)S(1)}) custom-call(s32[1]{0:T(128)} %bitcast.6.expert_ref, bf16[1040,128]{1,0:T(8,128)(2,1)S(1)} %collective-permute-done.6.refs_0_, bf16[1040,128]{1,0:T(8,128)(2,1)S(1)} %collective-permute-done.7.refs_1_, bf16[2048,1536]{1,0:T(8,128)(2,1)S(1)} %bitcast.18, ...), custom_call_target="tpu_custom_call" | custom-call | flops 2415919104 | bytes 1572864 | tf_op jit(solution)/shard_map/expert_rows/pallas_call | solution.py:200
  39.5 0.9 collective-permute-done.13.refs_1_
  40.4 1.6 %collective-permute-start.15 = (bf16[1040,128]{1,0:T(8,128)(2,1)S(1)}, bf16[1040,128]{1,0:T(8,128)(2,1)S(1)}, u32[]{:S(2)}, u32[]{:S(2)}) collective-permute-start(bf16[1040,128]{1,0:T(8,128)(2,1)S(1)} %collective-permute-done.12.refs_0_), channel_id=1, source_target_pairs={{2,6},{3,7},{6,10},{7,11},{10,14},{11,15},{14,12},{15,13},{12,8},{... | collective-permute-start | bytes 798728 | tf_op jit(solution)/shard_map/ppermute | solution.py:265
  42.0 0.5 collective-permute-start.16
  42.5 2.8 %expert_rows.11 = (f32[64,2048]{1,0:T(8,128)S(1)}, f32[64,2048]{1,0:T(8,128)S(1)}) custom-call(s32[1]{0:T(128)} %bitcast.6.expert_ref, bf16[1040,128]{1,0:T(8,128)(2,1)S(1)} %collective-permute-done.12.refs_0_, bf16[1040,128]{1,0:T(8,128)(2,1)S(1)} %collective-permute-done.13.refs_1_, bf16[2048,1536]{1,0:T(8,128)(2,1)S(1)} %bitcast.19, ...), custom_call_target="tpu_custom_call" | custom-call | flops 2415919104 | bytes 1572864 | tf_op jit(solution)/shard_map/expert_rows/pallas_call | solution.py:200
  45.3 0.9 collective-permute-done.11.refs_1_
  46.2 1.6 %collective-permute-start.14 = (bf16[1040,128]{1,0:T(8,128)(2,1)S(1)}, bf16[1040,128]{1,0:T(8,128)(2,1)S(1)}, u32[]{:S(2)}, u32[]{:S(2)}) collective-permute-start(bf16[1040,128]{1,0:T(8,128)(2,1)S(1)} %collective-permute-done.10.refs_0_), channel_id=1, source_target_pairs={{2,6},{3,7},{6,10},{7,11},{10,14},{11,15},{14,12},{15,13},{12,8},{... | collective-permute-start | bytes 798728 | tf_op jit(solution)/shard_map/ppermute | solution.py:265
  47.7 2.7 %expert_rows.12 = (f32[64,2048]{1,0:T(8,128)S(1)}, f32[64,2048]{1,0:T(8,128)S(1)}) custom-call(s32[1]{0:T(128)} %bitcast.6.expert_ref, bf16[1040,128]{1,0:T(8,128)(2,1)S(1)} %collective-permute-done.10.refs_0_, bf16[1040,128]{1,0:T(8,128)(2,1)S(1)} %collective-permute-done.11.refs_1_, bf16[2048,1536]{1,0:T(8,128)(2,1)S(1)} %bitcast.20, ...), custom_call_target="tpu_custom_call" | custom-call | flops 2415919104 | bytes 1572864 | tf_op jit(solution)/shard_map/expert_rows/pallas_call | solution.py:200
  50.5 1.4 %collective-permute-start.17 = (bf16[1040,128]{1,0:T(8,128)(2,1)S(1)}, bf16[1040,128]{1,0:T(8,128)(2,1)S(1)}, u32[]{:S(2)}, u32[]{:S(2)}) collective-permute-start(bf16[1040,128]{1,0:T(8,128)(2,1)S(1)} %collective-permute-done.16.refs_1_), channel_id=1, source_target_pairs={{6,2},{7,3},{10,6},{11,7},{14,10},{15,11},{12,14},{13,15},{8,12},{... | collective-permute-start | bytes 798728 | tf_op jit(solution)/shard_map/ppermute | solution.py:265
  51.9 2.8 %expert_rows.13 = (f32[64,2048]{1,0:T(8,128)S(1)}, f32[64,2048]{1,0:T(8,128)S(1)}) custom-call(s32[1]{0:T(128)} %bitcast.6.expert_ref, bf16[1040,128]{1,0:T(8,128)(2,1)S(1)} %collective-permute-done.15.refs_0_, bf16[1040,128]{1,0:T(8,128)(2,1)S(1)} %collective-permute-done.16.refs_1_, bf16[2048,1536]{1,0:T(8,128)(2,1)S(1)} %bitcast.21, ...), custom_call_target="tpu_custom_call" | custom-call | flops 2415919104 | bytes 1572864 | tf_op jit(solution)/shard_map/expert_rows/pallas_call | solution.py:200
  54.7 0.7 collective-permute-start.21
  55.5 1.4 %collective-permute-start.18 = (bf16[64,2048]{1,0:T(8,128)(2,1)S(1)}, bf16[64,2048]{1,0:T(8,128)(2,1)S(1)}, u32[]{:S(2)}, u32[]{:S(2)}) collective-permute-start(bf16[64,2048]{1,0:T(8,128)(2,1)S(1)} %convert_element_type.85), channel_id=1, source_target_pairs={{6,2},{7,3},{10,6},{11,7},{14,10},{15,11},{12,14},{13,15},{8,12},{... | collective-permute-start | bytes 786440 | tf_op jit(solution)/shard_map/ppermute | solution.py:265
  56.9 1.9 %collective-permute-done.17.refs_1_ = bf16[1040,128]{1,0:T(8,128)(2,1)S(1)} collective-permute-done((bf16[1040,128]{1,0:T(8,128)(2,1)S(1)}, bf16[1040,128]{1,0:T(8,128)(2,1)S(1)}, u32[]{:S(2)}, u32[]{:S(2)}) %collective-permute-start.17) | collective-permute-done | bytes 266272 | tf_op jit(solution)/shard_map/ppermute | solution.py:265
  58.8 2.8 %expert_rows.14 = (f32[64,2048]{1,0:T(8,128)S(1)}, f32[64,2048]{1,0:T(8,128)S(1)}) custom-call(s32[1]{0:T(128)} %bitcast.6.expert_ref, bf16[1040,128]{1,0:T(8,128)(2,1)S(1)} %collective-permute-done.14.refs_0_, bf16[1040,128]{1,0:T(8,128)(2,1)S(1)} %collective-permute-done.17.refs_1_, bf16[2048,1536]{1,0:T(8,128)(2,1)S(1)} %bitcast.22, ...), custom_call_target="tpu_custom_call" | custom-call | flops 2415919104 | bytes 1572864 | tf_op jit(solution)/shard_map/expert_rows/pallas_call | solution.py:200
  61.7 0.9 collective-permute-done.18
  62.7 1.6 %collective-permute-start.20 = (bf16[64,2048]{1,0:T(8,128)(2,1)S(1)}, bf16[64,2048]{1,0:T(8,128)(2,1)S(1)}, u32[]{:S(2)}, u32[]{:S(2)}) collective-permute-start(bf16[64,2048]{1,0:T(8,128)(2,1)S(1)} %convert_element_type.88), channel_id=1, source_target_pairs={{2,6},{3,7},{6,10},{7,11},{10,14},{11,15},{14,12},{15,13},{12,8},{... | collective-permute-start | bytes 786440 | tf_op jit(solution)/shard_map/ppermute | solution.py:265
  64.3 0.4 collective-permute-start.19
  64.7 1.4 %collective-permute-start.22 = (bf16[64,2048]{1,0:T(8,128)(2,1)S(1)}, bf16[64,2048]{1,0:T(8,128)(2,1)S(1)}, u32[]{:S(2)}, u32[]{:S(2)}) collective-permute-start(bf16[64,2048]{1,0:T(8,128)(2,1)S(1)} %convert_element_type.94), channel_id=1, source_target_pairs={{6,2},{7,3},{10,6},{11,7},{14,10},{15,11},{12,14},{13,15},{8,12},{... | collective-permute-start | bytes 786440 | tf_op jit(solution)/shard_map/ppermute | solution.py:265
  66.2 0.9 collective-permute-start.24
  67.1 2.7 %expert_rows.15 = (f32[64,2048]{1,0:T(8,128)S(1)}, f32[64,2048]{1,0:T(8,128)S(1)}) custom-call(s32[1]{0:T(128)} %bitcast.6.expert_ref, bf16[1040,128]{1,0:T(8,128)(2,1)S(1)} %get-tuple-element.67.refs_0_, bf16[1040,128]{1,0:T(8,128)(2,1)S(1)} %get-tuple-element.71.refs_1_, bf16[2048,1536]{1,0:T(8,128)(2,1)S(1)} %bitcast.23, bf16[768,2048]{1,0:T(8,128)(2,1)S(1)} %bitcast.32, ...), custom_call_target="tpu_custom_call" | custom-call | flops 2415919104 | bytes 1572864 | tf_op jit(solution)/shard_map/expert_rows/pallas_call | solution.py:200
  69.8 1.8 %collective-permute-done.20 = bf16[64,2048]{1,0:T(8,128)(2,1)S(1)} collective-permute-done((bf16[64,2048]{1,0:T(8,128)(2,1)S(1)}, bf16[64,2048]{1,0:T(8,128)(2,1)S(1)}, u32[]{:S(2)}, u32[]{:S(2)}) %collective-permute-start.20) | collective-permute-done | bytes 262176 | tf_op jit(solution)/shard_map/ppermute | solution.py:265
  71.7 4.5 %collective-permute-done.22 = bf16[64,2048]{1,0:T(8,128)(2,1)S(1)} collective-permute-done((bf16[64,2048]{1,0:T(8,128)(2,1)S(1)}, bf16[64,2048]{1,0:T(8,128)(2,1)S(1)}, u32[]{:S(2)}, u32[]{:S(2)}) %collective-permute-start.22) | collective-permute-done | bytes 262176 | tf_op jit(solution)/shard_map/ppermute | solution.py:265
  76.2 0.1 add_convert_fusion.6
  76.3 0.5 collective-permute-start.28
  76.8 1.6 %collective-permute-start.26 = (bf16[64,2048]{1,0:T(8,128)(2,1)S(1)}, bf16[64,2048]{1,0:T(8,128)(2,1)S(1)}, u32[]{:S(2)}, u32[]{:S(2)}) collective-permute-start(bf16[64,2048]{1,0:T(8,128)(2,1)S(1)} %get-tuple-element.112), channel_id=1, source_target_pairs={{2,6},{3,7},{6,10},{7,11},{10,14},{11,15},{14,12},{15,13},{12,8},{... | collective-permute-start | bytes 786440 | tf_op jit(solution)/shard_map/ppermute | solution.py:265
  78.5 0.5 collective-permute-start.23
  79.0 1.6 %collective-permute-start.25 = (bf16[64,2048]{1,0:T(8,128)(2,1)S(1)}, bf16[64,2048]{1,0:T(8,128)(2,1)S(1)}, u32[]{:S(2)}, u32[]{:S(2)}) collective-permute-start(bf16[64,2048]{1,0:T(8,128)(2,1)S(1)} %add_convert_fusion.4), channel_id=1, source_target_pairs={{2,6},{3,7},{6,10},{7,11},{10,14},{11,15},{14,12},{15,13},{12,8},{... | collective-permute-start | bytes 786440 | tf_op jit(solution)/shard_map/ppermute | solution.py:265
  80.7 5.0 %collective-permute-done.28 = bf16[64,2048]{1,0:T(8,128)(2,1)S(1)} collective-permute-done((bf16[64,2048]{1,0:T(8,128)(2,1)S(1)}, bf16[64,2048]{1,0:T(8,128)(2,1)S(1)}, u32[]{:S(2)}, u32[]{:S(2)}) %collective-permute-start.28) | collective-permute-done | bytes 262176 | tf_op jit(solution)/shard_map/ppermute | solution.py:265
  85.7 0.5 collective-permute-start.30
  86.2 1.6 %collective-permute-start.27 = (bf16[64,2048]{1,0:T(8,128)(2,1)S(1)}, bf16[64,2048]{1,0:T(8,128)(2,1)S(1)}, u32[]{:S(2)}, u32[]{:S(2)}) collective-permute-start(bf16[64,2048]{1,0:T(8,128)(2,1)S(1)} %add_convert_fusion.3), channel_id=1, source_target_pairs={{2,6},{3,7},{6,10},{7,11},{10,14},{11,15},{14,12},{15,13},{12,8},{... | collective-permute-start | bytes 786440 | tf_op jit(solution)/shard_map/ppermute | solution.py:265
  87.9 1.9 %collective-permute-done.23 = bf16[64,2048]{1,0:T(8,128)(2,1)S(1)} collective-permute-done((bf16[64,2048]{1,0:T(8,128)(2,1)S(1)}, bf16[64,2048]{1,0:T(8,128)(2,1)S(1)}, u32[]{:S(2)}, u32[]{:S(2)}) %collective-permute-start.23) | collective-permute-done | bytes 262176 | tf_op jit(solution)/shard_map/ppermute | solution.py:265
  89.8 0.1 add_add_fusion.1.near0_ref
  89.9 4.1 %collective-permute-done.30 = bf16[64,2048]{1,0:T(8,128)(2,1)S(1)} collective-permute-done((bf16[64,2048]{1,0:T(8,128)(2,1)S(1)}, bf16[64,2048]{1,0:T(8,128)(2,1)S(1)}, u32[]{:S(2)}, u32[]{:S(2)}) %collective-permute-start.30) | collective-permute-done | bytes 262176 | tf_op jit(solution)/shard_map/ppermute | solution.py:265
  94.0 0.5 collective-permute-start.31
  94.6 1.6 %collective-permute-start.29 = (bf16[64,2048]{1,0:T(8,128)(2,1)S(1)}, bf16[64,2048]{1,0:T(8,128)(2,1)S(1)}, u32[]{:S(2)}, u32[]{:S(2)}) collective-permute-start(bf16[64,2048]{1,0:T(8,128)(2,1)S(1)} %add_convert_fusion.1), channel_id=1, source_target_pairs={{2,6},{3,7},{6,10},{7,11},{10,14},{11,15},{14,12},{15,13},{12,8},{... | collective-permute-start | bytes 786440 | tf_op jit(solution)/shard_map/ppermute | solution.py:265
  96.3 4.1 %collective-permute-done.31.total1_ref = bf16[64,2048]{1,0:T(8,128)(2,1)S(1)} collective-permute-done((bf16[64,2048]{1,0:T(8,128)(2,1)S(1)}, bf16[64,2048]{1,0:T(8,128)(2,1)S(1)}, u32[]{:S(2)}, u32[]{:S(2)}) %collective-permute-start.31) | collective-permute-done | bytes 262176 | tf_op jit(solution)/shard_map/ppermute | solution.py:265
  100.5 0.6 collective-permute-done.29.total0_ref
  101.0 0.9 last_rows.1
  (40 shorter events, 0.9 us)
Async XLA Ops:
  0.0 23.6 %copy-start.1 = (bf16[1,1,768,2048]{3,2,1,0:T(8,128)(2,1)S(1)}, bf16[1,1,768,2048]{3,2,1,0:T(8,128)(2,1)}, u32[]{:S(2)}) copy-start(bf16[1,1,768,2048]{3,2,1,0:T(8,128)(2,1)} %param.13) | copy-start | bytes 9437188
  0.0 18.1 %collective-permute-start.2 = (bf16[2048,1536]{1,0:T(8,128)(2,1)}, bf16[2048,1536]{1,0:T(8,128)(2,1)S(1)}, u32[]{:S(2)}, u32[]{:S(2)}) collective-permute-start(bf16[2048,1536]{1,0:T(8,128)(2,1)} %bitcast.15), channel_id=1, source_target_pairs={{0,1},{1,0},{2,3},{3,2},{4,5},{5,4},{6,7},{7,6},{8,9},{9,8},{10,11... | collective-permute-start | bytes 18874376 | tf_op jit(solution)/shard_map/ppermute | solution.py:265
  0.5 17.7 %collective-permute-start.3 = (bf16[768,2048]{1,0:T(8,128)(2,1)}, bf16[768,2048]{1,0:T(8,128)(2,1)S(1)}, u32[]{:S(2)}, u32[]{:S(2)}) collective-permute-start(bf16[768,2048]{1,0:T(8,128)(2,1)} %bitcast.24), channel_id=1, source_target_pairs={{0,1},{1,0},{2,3},{3,2},{4,5},{5,4},{6,7},{7,6},{8,9},{9,8},{10,11... | collective-permute-start | bytes 9437192 | tf_op jit(solution)/shard_map/ppermute | solution.py:265
  1.8 11.5 %collective-permute-start = (bf16[64,2048]{1,0:T(8,128)(2,1)S(1)}, bf16[64,2048]{1,0:T(8,128)(2,1)S(1)}, u32[]{:S(2)}, u32[]{:S(2)}) collective-permute-start(bf16[64,2048]{1,0:T(8,128)(2,1)S(1)} %get-tuple-element.110), channel_id=1, source_target_pairs={{0,16},{1,17},{2,18},{3,19},{4,20},{5,21},{6,22},{7,23},{8,24},{9,... | collective-permute-start | bytes 786440 | tf_op jit(solution)/shard_map/ppermute | solution.py:20
  6.7 11.3 %collective-permute-start.1 = (bf16[64,2048]{1,0:T(8,128)(2,1)S(1)}, bf16[64,2048]{1,0:T(8,128)(2,1)S(1)}, u32[]{:S(2)}, u32[]{:S(2)}) collective-permute-start(bf16[64,2048]{1,0:T(8,128)(2,1)S(1)} %get-tuple-element.109), channel_id=1, source_target_pairs={{0,16},{1,17},{2,18},{3,19},{4,20},{5,21},{6,22},{7,23},{8,24},{9,... | collective-permute-start | bytes 786440 | tf_op jit(solution)/shard_map/ppermute | solution.py:20
  8.0 1.0 %copy-start.2 = (bf16[128,2048]{1,0:T(8,128)(2,1)S(1)}, bf16[128,2048]{1,0:T(8,128)(2,1)}, u32[]{:S(2)}) copy-start(bf16[128,2048]{1,0:T(8,128)(2,1)} %fresh_ref.1) | copy-start | bytes 1572868
  9.1 0.7 copy-start.3
  9.8 0.7 copy-start.4
  10.5 0.7 copy-start.5
  13.5 6.8 %collective-permute-start.4 = (bf16[1040,128]{1,0:T(8,128)(2,1)S(1)}, bf16[1040,128]{1,0:T(8,128)(2,1)S(1)}, u32[]{:S(2)}, u32[]{:S(2)}) collective-permute-start(bf16[1040,128]{1,0:T(8,128)(2,1)S(1)} %get-tuple-element.67.refs_0_), channel_id=1, source_target_pairs={{2,6},{3,7},{6,10},{7,11},{10,14},{11,15},{14,12},{15,13},{12,8},{... | collective-permute-start | bytes 798728 | tf_op jit(solution)/shard_map/ppermute | solution.py:265
  15.0 6.6 %collective-permute-start.5 = (bf16[1040,128]{1,0:T(8,128)(2,1)S(1)}, bf16[1040,128]{1,0:T(8,128)(2,1)S(1)}, u32[]{:S(2)}, u32[]{:S(2)}) collective-permute-start(bf16[1040,128]{1,0:T(8,128)(2,1)S(1)} %get-tuple-element.67.refs_0_), channel_id=1, source_target_pairs={{6,2},{7,3},{10,6},{11,7},{14,10},{15,11},{12,14},{13,15},{8,12},{... | collective-permute-start | bytes 798728 | tf_op jit(solution)/shard_map/ppermute | solution.py:265
  18.1 11.0 %collective-permute-start.8 = (bf16[1040,128]{1,0:T(8,128)(2,1)S(1)}, bf16[1040,128]{1,0:T(8,128)(2,1)S(1)}, u32[]{:S(2)}, u32[]{:S(2)}) collective-permute-start(bf16[1040,128]{1,0:T(8,128)(2,1)S(1)} %get-tuple-element.71.refs_1_), channel_id=1, source_target_pairs={{2,6},{3,7},{6,10},{7,11},{10,14},{11,15},{14,12},{15,13},{12,8},{... | collective-permute-start | bytes 798728 | tf_op jit(solution)/shard_map/ppermute | solution.py:265
  19.7 9.5 %collective-permute-start.9 = (bf16[1040,128]{1,0:T(8,128)(2,1)S(1)}, bf16[1040,128]{1,0:T(8,128)(2,1)S(1)}, u32[]{:S(2)}, u32[]{:S(2)}) collective-permute-start(bf16[1040,128]{1,0:T(8,128)(2,1)S(1)} %get-tuple-element.71.refs_1_), channel_id=1, source_target_pairs={{6,2},{7,3},{10,6},{11,7},{14,10},{15,11},{12,14},{13,15},{8,12},{... | collective-permute-start | bytes 798728 | tf_op jit(solution)/shard_map/ppermute | solution.py:265
  21.6 12.4 %collective-permute-start.6 = (bf16[1040,128]{1,0:T(8,128)(2,1)S(1)}, bf16[1040,128]{1,0:T(8,128)(2,1)S(1)}, u32[]{:S(2)}, u32[]{:S(2)}) collective-permute-start(bf16[1040,128]{1,0:T(8,128)(2,1)S(1)} %collective-permute-done.4.refs_0_), channel_id=1, source_target_pairs={{2,6},{3,7},{6,10},{7,11},{10,14},{11,15},{14,12},{15,13},{12,8},{... | collective-permute-start | bytes 798728 | tf_op jit(solution)/shard_map/ppermute | solution.py:265
  23.2 11.6 %collective-permute-start.7 = (bf16[1040,128]{1,0:T(8,128)(2,1)S(1)}, bf16[1040,128]{1,0:T(8,128)(2,1)S(1)}, u32[]{:S(2)}, u32[]{:S(2)}) collective-permute-start(bf16[1040,128]{1,0:T(8,128)(2,1)S(1)} %collective-permute-done.5.refs_1_), channel_id=1, source_target_pairs={{6,2},{7,3},{10,6},{11,7},{14,10},{15,11},{12,14},{13,15},{8,12},{... | collective-permute-start | bytes 798728 | tf_op jit(solution)/shard_map/ppermute | solution.py:265
  23.6 2.8 %copy-start = (bf16[1,1,2048,1536]{3,2,1,0:T(8,128)(2,1)S(1)}, bf16[1,1,2048,1536]{3,2,1,0:T(8,128)(2,1)}, u32[]{:S(2)}) copy-start(bf16[1,1,2048,1536]{3,2,1,0:T(8,128)(2,1)} %param.12) | copy-start | bytes 18874372
  29.2 10.3 %collective-permute-start.12 = (bf16[1040,128]{1,0:T(8,128)(2,1)S(1)}, bf16[1040,128]{1,0:T(8,128)(2,1)S(1)}, u32[]{:S(2)}, u32[]{:S(2)}) collective-permute-start(bf16[1040,128]{1,0:T(8,128)(2,1)S(1)} %collective-permute-done.8.refs_0_), channel_id=1, source_target_pairs={{2,6},{3,7},{6,10},{7,11},{10,14},{11,15},{14,12},{15,13},{12,8},{... | collective-permute-start | bytes 798728 | tf_op jit(solution)/shard_map/ppermute | solution.py:265
  30.8 9.6 %collective-permute-start.13 = (bf16[1040,128]{1,0:T(8,128)(2,1)S(1)}, bf16[1040,128]{1,0:T(8,128)(2,1)S(1)}, u32[]{:S(2)}, u32[]{:S(2)}) collective-permute-start(bf16[1040,128]{1,0:T(8,128)(2,1)S(1)} %collective-permute-done.9.refs_1_), channel_id=1, source_target_pairs={{6,2},{7,3},{10,6},{11,7},{14,10},{15,11},{12,14},{13,15},{8,12},{... | collective-permute-start | bytes 798728 | tf_op jit(solution)/shard_map/ppermute | solution.py:265
  34.7 10.5 %collective-permute-start.10 = (bf16[1040,128]{1,0:T(8,128)(2,1)S(1)}, bf16[1040,128]{1,0:T(8,128)(2,1)S(1)}, u32[]{:S(2)}, u32[]{:S(2)}) collective-permute-start(bf16[1040,128]{1,0:T(8,128)(2,1)S(1)} %collective-permute-done.6.refs_0_), channel_id=1, source_target_pairs={{2,6},{3,7},{6,10},{7,11},{10,14},{11,15},{14,12},{15,13},{12,8},{... | collective-permute-start | bytes 798728 | tf_op jit(solution)/shard_map/ppermute | solution.py:265
  36.3 9.8 %collective-permute-start.11 = (bf16[1040,128]{1,0:T(8,128)(2,1)S(1)}, bf16[1040,128]{1,0:T(8,128)(2,1)S(1)}, u32[]{:S(2)}, u32[]{:S(2)}) collective-permute-start(bf16[1040,128]{1,0:T(8,128)(2,1)S(1)} %collective-permute-done.7.refs_1_), channel_id=1, source_target_pairs={{6,2},{7,3},{10,6},{11,7},{14,10},{15,11},{12,14},{13,15},{8,12},{... | collective-permute-start | bytes 798728 | tf_op jit(solution)/shard_map/ppermute | solution.py:265
  40.4 10.0 %collective-permute-start.15 = (bf16[1040,128]{1,0:T(8,128)(2,1)S(1)}, bf16[1040,128]{1,0:T(8,128)(2,1)S(1)}, u32[]{:S(2)}, u32[]{:S(2)}) collective-permute-start(bf16[1040,128]{1,0:T(8,128)(2,1)S(1)} %collective-permute-done.12.refs_0_), channel_id=1, source_target_pairs={{2,6},{3,7},{6,10},{7,11},{10,14},{11,15},{14,12},{15,13},{12,8},{... | collective-permute-start | bytes 798728 | tf_op jit(solution)/shard_map/ppermute | solution.py:265
  42.0 8.5 %collective-permute-start.16 = (bf16[1040,128]{1,0:T(8,128)(2,1)S(1)}, bf16[1040,128]{1,0:T(8,128)(2,1)S(1)}, u32[]{:S(2)}, u32[]{:S(2)}) collective-permute-start(bf16[1040,128]{1,0:T(8,128)(2,1)S(1)} %collective-permute-done.13.refs_1_), channel_id=1, source_target_pairs={{6,2},{7,3},{10,6},{11,7},{14,10},{15,11},{12,14},{13,15},{8,12},{... | collective-permute-start | bytes 798728 | tf_op jit(solution)/shard_map/ppermute | solution.py:265
  46.2 10.8 %collective-permute-start.14 = (bf16[1040,128]{1,0:T(8,128)(2,1)S(1)}, bf16[1040,128]{1,0:T(8,128)(2,1)S(1)}, u32[]{:S(2)}, u32[]{:S(2)}) collective-permute-start(bf16[1040,128]{1,0:T(8,128)(2,1)S(1)} %collective-permute-done.10.refs_0_), channel_id=1, source_target_pairs={{2,6},{3,7},{6,10},{7,11},{10,14},{11,15},{14,12},{15,13},{12,8},{... | collective-permute-start | bytes 798728 | tf_op jit(solution)/shard_map/ppermute | solution.py:265
  50.5 8.3 %collective-permute-start.17 = (bf16[1040,128]{1,0:T(8,128)(2,1)S(1)}, bf16[1040,128]{1,0:T(8,128)(2,1)S(1)}, u32[]{:S(2)}, u32[]{:S(2)}) collective-permute-start(bf16[1040,128]{1,0:T(8,128)(2,1)S(1)} %collective-permute-done.16.refs_1_), channel_id=1, source_target_pairs={{6,2},{7,3},{10,6},{11,7},{14,10},{15,11},{12,14},{13,15},{8,12},{... | collective-permute-start | bytes 798728 | tf_op jit(solution)/shard_map/ppermute | solution.py:265
  54.7 6.9 %collective-permute-start.21 = (bf16[64,2048]{1,0:T(8,128)(2,1)S(1)}, bf16[64,2048]{1,0:T(8,128)(2,1)S(1)}, u32[]{:S(2)}, u32[]{:S(2)}) collective-permute-start(bf16[64,2048]{1,0:T(8,128)(2,1)S(1)} %convert_element_type.89), channel_id=1, source_target_pairs={{2,6},{3,7},{6,10},{7,11},{10,14},{11,15},{14,12},{15,13},{12,8},{... | collective-permute-start | bytes 786440 | tf_op jit(solution)/shard_map/ppermute | solution.py:265
  55.5 7.1 %collective-permute-start.18 = (bf16[64,2048]{1,0:T(8,128)(2,1)S(1)}, bf16[64,2048]{1,0:T(8,128)(2,1)S(1)}, u32[]{:S(2)}, u32[]{:S(2)}) collective-permute-start(bf16[64,2048]{1,0:T(8,128)(2,1)S(1)} %convert_element_type.85), channel_id=1, source_target_pairs={{6,2},{7,3},{10,6},{11,7},{14,10},{15,11},{12,14},{13,15},{8,12},{... | collective-permute-start | bytes 786440 | tf_op jit(solution)/shard_map/ppermute | solution.py:265
  62.7 9.0 %collective-permute-start.20 = (bf16[64,2048]{1,0:T(8,128)(2,1)S(1)}, bf16[64,2048]{1,0:T(8,128)(2,1)S(1)}, u32[]{:S(2)}, u32[]{:S(2)}) collective-permute-start(bf16[64,2048]{1,0:T(8,128)(2,1)S(1)} %convert_element_type.88), channel_id=1, source_target_pairs={{2,6},{3,7},{6,10},{7,11},{10,14},{11,15},{14,12},{15,13},{12,8},{... | collective-permute-start | bytes 786440 | tf_op jit(solution)/shard_map/ppermute | solution.py:265
  64.3 14.1 %collective-permute-start.19 = (bf16[64,2048]{1,0:T(8,128)(2,1)S(1)}, bf16[64,2048]{1,0:T(8,128)(2,1)S(1)}, u32[]{:S(2)}, u32[]{:S(2)}) collective-permute-start(bf16[64,2048]{1,0:T(8,128)(2,1)S(1)} %add_convert_fusion.9), channel_id=1, source_target_pairs={{6,2},{7,3},{10,6},{11,7},{14,10},{15,11},{12,14},{13,15},{8,12},{... | collective-permute-start | bytes 786440 | tf_op jit(solution)/shard_map/ppermute | solution.py:265
  64.7 11.5 %collective-permute-start.22 = (bf16[64,2048]{1,0:T(8,128)(2,1)S(1)}, bf16[64,2048]{1,0:T(8,128)(2,1)S(1)}, u32[]{:S(2)}, u32[]{:S(2)}) collective-permute-start(bf16[64,2048]{1,0:T(8,128)(2,1)S(1)} %convert_element_type.94), channel_id=1, source_target_pairs={{6,2},{7,3},{10,6},{11,7},{14,10},{15,11},{12,14},{13,15},{8,12},{... | collective-permute-start | bytes 786440 | tf_op jit(solution)/shard_map/ppermute | solution.py:265
  66.2 12.2 %collective-permute-start.24 = (bf16[64,2048]{1,0:T(8,128)(2,1)S(1)}, bf16[64,2048]{1,0:T(8,128)(2,1)S(1)}, u32[]{:S(2)}, u32[]{:S(2)}) collective-permute-start(bf16[64,2048]{1,0:T(8,128)(2,1)S(1)} %add_convert_fusion.8), channel_id=1, source_target_pairs={{2,6},{3,7},{6,10},{7,11},{10,14},{11,15},{14,12},{15,13},{12,8},{... | collective-permute-start | bytes 786440 | tf_op jit(solution)/shard_map/ppermute | solution.py:265
  76.3 9.3 %collective-permute-start.28 = (bf16[64,2048]{1,0:T(8,128)(2,1)S(1)}, bf16[64,2048]{1,0:T(8,128)(2,1)S(1)}, u32[]{:S(2)}, u32[]{:S(2)}) collective-permute-start(bf16[64,2048]{1,0:T(8,128)(2,1)S(1)} %get-tuple-element.111), channel_id=1, source_target_pairs={{6,2},{7,3},{10,6},{11,7},{14,10},{15,11},{12,14},{13,15},{8,12},{... | collective-permute-start | bytes 786440 | tf_op jit(solution)/shard_map/ppermute | solution.py:265
  76.8 9.4 %collective-permute-start.26 = (bf16[64,2048]{1,0:T(8,128)(2,1)S(1)}, bf16[64,2048]{1,0:T(8,128)(2,1)S(1)}, u32[]{:S(2)}, u32[]{:S(2)}) collective-permute-start(bf16[64,2048]{1,0:T(8,128)(2,1)S(1)} %get-tuple-element.112), channel_id=1, source_target_pairs={{2,6},{3,7},{6,10},{7,11},{10,14},{11,15},{14,12},{15,13},{12,8},{... | collective-permute-start | bytes 786440 | tf_op jit(solution)/shard_map/ppermute | solution.py:265
  78.5 11.3 %collective-permute-start.23 = (bf16[64,2048]{1,0:T(8,128)(2,1)S(1)}, bf16[64,2048]{1,0:T(8,128)(2,1)S(1)}, u32[]{:S(2)}, u32[]{:S(2)}) collective-permute-start(bf16[64,2048]{1,0:T(8,128)(2,1)S(1)} %add_convert_fusion.5), channel_id=1, source_target_pairs={{6,2},{7,3},{10,6},{11,7},{14,10},{15,11},{12,14},{13,15},{8,12},{... | collective-permute-start | bytes 786440 | tf_op jit(solution)/shard_map/ppermute | solution.py:265
  79.0 17.2 %collective-permute-start.25 = (bf16[64,2048]{1,0:T(8,128)(2,1)S(1)}, bf16[64,2048]{1,0:T(8,128)(2,1)S(1)}, u32[]{:S(2)}, u32[]{:S(2)}) collective-permute-start(bf16[64,2048]{1,0:T(8,128)(2,1)S(1)} %add_convert_fusion.4), channel_id=1, source_target_pairs={{2,6},{3,7},{6,10},{7,11},{10,14},{11,15},{14,12},{15,13},{12,8},{... | collective-permute-start | bytes 786440 | tf_op jit(solution)/shard_map/ppermute | solution.py:265
  85.7 8.3 %collective-permute-start.30 = (bf16[64,2048]{1,0:T(8,128)(2,1)S(1)}, bf16[64,2048]{1,0:T(8,128)(2,1)S(1)}, u32[]{:S(2)}, u32[]{:S(2)}) collective-permute-start(bf16[64,2048]{1,0:T(8,128)(2,1)S(1)} %add_convert_fusion.2), channel_id=1, source_target_pairs={{6,2},{7,3},{10,6},{11,7},{14,10},{15,11},{12,14},{13,15},{8,12},{... | collective-permute-start | bytes 786440 | tf_op jit(solution)/shard_map/ppermute | solution.py:265
  86.2 8.3 %collective-permute-start.27 = (bf16[64,2048]{1,0:T(8,128)(2,1)S(1)}, bf16[64,2048]{1,0:T(8,128)(2,1)S(1)}, u32[]{:S(2)}, u32[]{:S(2)}) collective-permute-start(bf16[64,2048]{1,0:T(8,128)(2,1)S(1)} %add_convert_fusion.3), channel_id=1, source_target_pairs={{2,6},{3,7},{6,10},{7,11},{10,14},{11,15},{14,12},{15,13},{12,8},{... | collective-permute-start | bytes 786440 | tf_op jit(solution)/shard_map/ppermute | solution.py:265
  94.0 6.4 %collective-permute-start.31 = (bf16[64,2048]{1,0:T(8,128)(2,1)S(1)}, bf16[64,2048]{1,0:T(8,128)(2,1)S(1)}, u32[]{:S(2)}, u32[]{:S(2)}) collective-permute-start(bf16[64,2048]{1,0:T(8,128)(2,1)S(1)} %add_convert_fusion), channel_id=1, source_target_pairs={{6,2},{7,3},{10,6},{11,7},{14,10},{15,11},{12,14},{13,15},{8,12},{... | collective-permute-start | bytes 786440 | tf_op jit(solution)/shard_map/ppermute | solution.py:265
  94.6 6.4 %collective-permute-start.29 = (bf16[64,2048]{1,0:T(8,128)(2,1)S(1)}, bf16[64,2048]{1,0:T(8,128)(2,1)S(1)}, u32[]{:S(2)}, u32[]{:S(2)}) collective-permute-start(bf16[64,2048]{1,0:T(8,128)(2,1)S(1)} %add_convert_fusion.1), channel_id=1, source_target_pairs={{2,6},{3,7},{6,10},{7,11},{10,14},{11,15},{14,12},{15,13},{12,8},{... | collective-permute-start | bytes 786440 | tf_op jit(solution)/shard_map/ppermute | solution.py:265

commit v9 on v8

--- a/solution.py
+++ b/solution.py
@@ -316,12 +316,18 @@
     long = [(to_up, 0, up), (to_down, 1, down)]
     short_totals = [send_on(flow, hops - 1, None, None)[1] for flow in short]
     long_totals = [send_on(flow, hops, None, None)[1] for flow in long]
-    after = to_up[hops, 0]
+    sent = to_up[hops, 0]
     for s in reversed(range(1, hops)):
-        if s > 1:
-            sent, short_totals = zip(*(send_on(f, s - 1, t, after) for f, t in zip(short, short_totals)))
-        sent, long_totals = zip(*(send_on(f, s, t, sent) for f, t in zip(long, long_totals)))
-        after = sent
+        order = [(short, s - 1), (long, s)] if s == hops - 1 else [(long, s), (short, s - 1)]
+        for flows, place in order:
+            if place == 0:
+                continue
+            totals = short_totals if flows is short else long_totals
+            sent, totals = zip(*(send_on(flow, place, total, sent) for flow, total in zip(flows, totals)))
+            if flows is short:
+                short_totals = totals
+            else:
+                long_totals = totals
 
     nears = [
         arrival[c].astype(jnp.float32) + (own_sums[c] + short_totals[c].astype(jnp.float32)) for c in range(2)

time: 102 us -> 103 us (level)
  transfers between devices with their start and end apart: 32 -> 32, of which waited for: 15 -> 16; matrix products, arithmetic and copies ran while one was open for 2% -> 2% of each run, Pallas kernels for 22% -> 22%
where the time goes in v9:
time: 103 us
  starting transfers between devices  36.9 us (36%)
  waiting for transfers between devices  34.2 us (33%)
  Pallas kernels  23.2 us (23%)
  local copies, waits for them, and re-layouts  7.21 us (7%)
    ppermute x30, starting transfers between devices, move(): return lax.ppermute(value, 'expert', pairs)  30.7 us
    ppermute x30, waiting for transfers between devices, move(): return lax.ppermute(value, 'expert', pairs)  29.7 us
    pallas_call x8, Pallas kernels, expert_rows(): pl.pallas_call(functools.partial(mlp_kernel, parts=len(payloads), chained...  22 us
    ppermute x2, starting transfers between devices, from_behind(): return lax.ppermute(value, axis, pairs)  6.18 us
    unnamed x12, local copies, waits for them, and re-layouts  5.89 us
    ppermute x2, waiting for transfers between devices, from_behind(): return lax.ppermute(value, axis, pairs)  4.5 us
  transfers between devices with their start and end apart: 32, of which 16 were waited for; matrix products, arithmetic and copies ran while one was open for 2% of the time, Pallas kernels for 22%

profile of v9, /device:TPU:0, one launch (start us, length us, event | category | flops | bytes accessed | tf_op | source)
XLA Modules:
  0.0 102.7 jit_solution(16742617658957668432)
XLA Ops:
  0.0 0.5 collective-permute-start.2
  0.5 1.3 %slice_bitcast_fusion = (bf16[64,2048]{1,0:T(8,128)(2,1)S(1)}, bf16[64,2048]{1,0:T(8,128)(2,1)S(1)}) fusion(bf16[1,128,2048]{2,1,0:T(8,128)(2,1)} %param.8), kind=kLoop, calls=%fused_computation.12 | loop fusion | bytes 1048576 | tf_op jit(solution)/shard_map/squeeze | solution.py:272
  1.8 4.9 %collective-permute-start = (bf16[64,2048]{1,0:T(8,128)(2,1)S(1)}, bf16[64,2048]{1,0:T(8,128)(2,1)S(1)}, u32[]{:S(2)}, u32[]{:S(2)}) collective-permute-start(bf16[64,2048]{1,0:T(8,128)(2,1)S(1)} %get-tuple-element.110), channel_id=1, source_target_pairs={{0,16},{1,17},{2,18},{3,19},{4,20},{5,21},{6,22},{7,23},{8,24},{9,... | collective-permute-start | bytes 786440 | tf_op jit(solution)/shard_map/ppermute | solution.py:20
  6.7 1.3 %collective-permute-start.1 = (bf16[64,2048]{1,0:T(8,128)(2,1)S(1)}, bf16[64,2048]{1,0:T(8,128)(2,1)S(1)}, u32[]{:S(2)}, u32[]{:S(2)}) collective-permute-start(bf16[64,2048]{1,0:T(8,128)(2,1)S(1)} %get-tuple-element.109), channel_id=1, source_target_pairs={{0,16},{1,17},{2,18},{3,19},{4,20},{5,21},{6,22},{7,23},{8,24},{9,... | collective-permute-start | bytes 786440 | tf_op jit(solution)/shard_map/ppermute | solution.py:20
  8.1 1.0 %copy-done.2 = bf16[128,2048]{1,0:T(8,128)(2,1)S(1)} copy-done((bf16[128,2048]{1,0:T(8,128)(2,1)S(1)}, bf16[128,2048]{1,0:T(8,128)(2,1)}, u32[]{:S(2)}) %copy-start.2) | copy-done | bytes 524312
  9.1 0.7 copy-done.3
  9.8 0.7 copy-done.4
  10.5 0.7 copy-done.5
  11.2 0.2 base_rows.1
  11.4 2.0 %collective-permute-done.arrived_ref = bf16[64,2048]{1,0:T(8,128)(2,1)S(1)} collective-permute-done((bf16[64,2048]{1,0:T(8,128)(2,1)S(1)}, bf16[64,2048]{1,0:T(8,128)(2,1)S(1)}, u32[]{:S(2)}, u32[]{:S(2)}) %collective-permute-start) | collective-permute-done | bytes 262176 | tf_op jit(solution)/shard_map/ppermute | solution.py:20
  13.4 1.5 %collective-permute-start.4 = (bf16[1040,128]{1,0:T(8,128)(2,1)S(1)}, bf16[1040,128]{1,0:T(8,128)(2,1)S(1)}, u32[]{:S(2)}, u32[]{:S(2)}) collective-permute-start(bf16[1040,128]{1,0:T(8,128)(2,1)S(1)} %get-tuple-element.67.refs_0_), channel_id=1, source_target_pairs={{2,6},{3,7},{6,10},{7,11},{10,14},{11,15},{14,12},{15,13},{12,8},{... | collective-permute-start | bytes 798728 | tf_op jit(solution)/shard_map/ppermute | solution.py:265
  15.0 0.5 collective-permute-start.5
  15.5 2.5 %collective-permute-done.1.arrived_ref = bf16[64,2048]{1,0:T(8,128)(2,1)S(1)} collective-permute-done((bf16[64,2048]{1,0:T(8,128)(2,1)S(1)}, bf16[64,2048]{1,0:T(8,128)(2,1)S(1)}, u32[]{:S(2)}, u32[]{:S(2)}) %collective-permute-start.1) | collective-permute-done | bytes 262176 | tf_op jit(solution)/shard_map/ppermute | solution.py:20
  18.1 1.5 %collective-permute-start.8 = (bf16[1040,128]{1,0:T(8,128)(2,1)S(1)}, bf16[1040,128]{1,0:T(8,128)(2,1)S(1)}, u32[]{:S(2)}, u32[]{:S(2)}) collective-permute-start(bf16[1040,128]{1,0:T(8,128)(2,1)S(1)} %get-tuple-element.71.refs_1_), channel_id=1, source_target_pairs={{2,6},{3,7},{6,10},{7,11},{10,14},{11,15},{14,12},{15,13},{12,8},{... | collective-permute-start | bytes 798728 | tf_op jit(solution)/shard_map/ppermute | solution.py:265
  19.7 0.5 collective-permute-start.9
  20.2 1.3 %collective-permute-done.5.refs_1_ = bf16[1040,128]{1,0:T(8,128)(2,1)S(1)} collective-permute-done((bf16[1040,128]{1,0:T(8,128)(2,1)S(1)}, bf16[1040,128]{1,0:T(8,128)(2,1)S(1)}, u32[]{:S(2)}, u32[]{:S(2)}) %collective-permute-start.5) | collective-permute-done | bytes 266272 | tf_op jit(solution)/shard_map/ppermute | solution.py:265
  21.6 1.6 %collective-permute-start.6 = (bf16[1040,128]{1,0:T(8,128)(2,1)S(1)}, bf16[1040,128]{1,0:T(8,128)(2,1)S(1)}, u32[]{:S(2)}, u32[]{:S(2)}) collective-permute-start(bf16[1040,128]{1,0:T(8,128)(2,1)S(1)} %collective-permute-done.4.refs_0_), channel_id=1, source_target_pairs={{2,6},{3,7},{6,10},{7,11},{10,14},{11,15},{14,12},{15,13},{12,8},{... | collective-permute-start | bytes 798728 | tf_op jit(solution)/shard_map/ppermute | solution.py:265
  23.2 0.4 collective-permute-start.7
  23.6 2.8 %copy-done = bf16[1,1,2048,1536]{3,2,1,0:T(8,128)(2,1)S(1)} copy-done((bf16[1,1,2048,1536]{3,2,1,0:T(8,128)(2,1)S(1)}, bf16[1,1,2048,1536]{3,2,1,0:T(8,128)(2,1)}, u32[]{:S(2)}) %copy-start) | copy-done | bytes 6291480
  26.4 2.8 %expert_rows.8 = (f32[64,2048]{1,0:T(8,128)S(1)}, f32[64,2048]{1,0:T(8,128)S(1)}) custom-call(s32[1]{0:T(128)} %bitcast.6.expert_ref, bf16[1040,128]{1,0:T(8,128)(2,1)S(1)} %collective-permute-done.4.refs_0_, bf16[1040,128]{1,0:T(8,128)(2,1)S(1)} %collective-permute-done.5.refs_1_, bf16[2048,1536]{1,0:T(8,128)(2,1)S(1)} %bitcast.16, ...), custom_call_target="tpu_custom_call" | custom-call | flops 2415919104 | bytes 1572864 | tf_op jit(solution)/shard_map/expert_rows/pallas_call | solution.py:200
  29.2 1.6 %collective-permute-start.12 = (bf16[1040,128]{1,0:T(8,128)(2,1)S(1)}, bf16[1040,128]{1,0:T(8,128)(2,1)S(1)}, u32[]{:S(2)}, u32[]{:S(2)}) collective-permute-start(bf16[1040,128]{1,0:T(8,128)(2,1)S(1)} %collective-permute-done.8.refs_0_), channel_id=1, source_target_pairs={{2,6},{3,7},{6,10},{7,11},{10,14},{11,15},{14,12},{15,13},{12,8},{... | collective-permute-start | bytes 798728 | tf_op jit(solution)/shard_map/ppermute | solution.py:265
  30.8 0.5 collective-permute-start.13
  31.3 2.7 %expert_rows.9 = (f32[64,2048]{1,0:T(8,128)S(1)}, f32[64,2048]{1,0:T(8,128)S(1)}) custom-call(s32[1]{0:T(128)} %bitcast.6.expert_ref, bf16[1040,128]{1,0:T(8,128)(2,1)S(1)} %collective-permute-done.8.refs_0_, bf16[1040,128]{1,0:T(8,128)(2,1)S(1)} %collective-permute-done.9.refs_1_, bf16[2048,1536]{1,0:T(8,128)(2,1)S(1)} %bitcast.17, ...), custom_call_target="tpu_custom_call" | custom-call | flops 2415919104 | bytes 1572864 | tf_op jit(solution)/shard_map/expert_rows/pallas_call | solution.py:200
  34.0 0.7 collective-permute-done.7.refs_1_
  34.7 1.6 %collective-permute-start.10 = (bf16[1040,128]{1,0:T(8,128)(2,1)S(1)}, bf16[1040,128]{1,0:T(8,128)(2,1)S(1)}, u32[]{:S(2)}, u32[]{:S(2)}) collective-permute-start(bf16[1040,128]{1,0:T(8,128)(2,1)S(1)} %collective-permute-done.6.refs_0_), channel_id=1, source_target_pairs={{2,6},{3,7},{6,10},{7,11},{10,14},{11,15},{14,12},{15,13},{12,8},{... | collective-permute-start | bytes 798728 | tf_op jit(solution)/shard_map/ppermute | solution.py:265
  36.3 0.4 collective-permute-start.11
  36.8 2.8 %expert_rows.10 = (f32[64,2048]{1,0:T(8,128)S(1)}, f32[64,2048]{1,0:T(8,128)S(1)}) custom-call(s32[1]{0:T(128)} %bitcast.6.expert_ref, bf16[1040,128]{1,0:T(8,128)(2,1)S(1)} %collective-permute-done.6.refs_0_, bf16[1040,128]{1,0:T(8,128)(2,1)S(1)} %collective-permute-done.7.refs_1_, bf16[2048,1536]{1,0:T(8,128)(2,1)S(1)} %bitcast.18, ...), custom_call_target="tpu_custom_call" | custom-call | flops 2415919104 | bytes 1572864 | tf_op jit(solution)/shard_map/expert_rows/pallas_call | solution.py:200
  39.5 0.9 collective-permute-done.13.refs_1_
  40.4 1.6 %collective-permute-start.15 = (bf16[1040,128]{1,0:T(8,128)(2,1)S(1)}, bf16[1040,128]{1,0:T(8,128)(2,1)S(1)}, u32[]{:S(2)}, u32[]{:S(2)}) collective-permute-start(bf16[1040,128]{1,0:T(8,128)(2,1)S(1)} %collective-permute-done.12.refs_0_), channel_id=1, source_target_pairs={{2,6},{3,7},{6,10},{7,11},{10,14},{11,15},{14,12},{15,13},{12,8},{... | collective-permute-start | bytes 798728 | tf_op jit(solution)/shard_map/ppermute | solution.py:265
  42.0 0.5 collective-permute-start.16
  42.5 2.7 %expert_rows.11 = (f32[64,2048]{1,0:T(8,128)S(1)}, f32[64,2048]{1,0:T(8,128)S(1)}) custom-call(s32[1]{0:T(128)} %bitcast.6.expert_ref, bf16[1040,128]{1,0:T(8,128)(2,1)S(1)} %collective-permute-done.12.refs_0_, bf16[1040,128]{1,0:T(8,128)(2,1)S(1)} %collective-permute-done.13.refs_1_, bf16[2048,1536]{1,0:T(8,128)(2,1)S(1)} %bitcast.19, ...), custom_call_target="tpu_custom_call" | custom-call | flops 2415919104 | bytes 1572864 | tf_op jit(solution)/shard_map/expert_rows/pallas_call | solution.py:200
  45.2 0.9 collective-permute-done.11.refs_1_
  46.1 1.6 %collective-permute-start.14 = (bf16[1040,128]{1,0:T(8,128)(2,1)S(1)}, bf16[1040,128]{1,0:T(8,128)(2,1)S(1)}, u32[]{:S(2)}, u32[]{:S(2)}) collective-permute-start(bf16[1040,128]{1,0:T(8,128)(2,1)S(1)} %collective-permute-done.10.refs_0_), channel_id=1, source_target_pairs={{2,6},{3,7},{6,10},{7,11},{10,14},{11,15},{14,12},{15,13},{12,8},{... | collective-permute-start | bytes 798728 | tf_op jit(solution)/shard_map/ppermute | solution.py:265
  47.7 2.7 %expert_rows.12 = (f32[64,2048]{1,0:T(8,128)S(1)}, f32[64,2048]{1,0:T(8,128)S(1)}) custom-call(s32[1]{0:T(128)} %bitcast.6.expert_ref, bf16[1040,128]{1,0:T(8,128)(2,1)S(1)} %collective-permute-done.10.refs_0_, bf16[1040,128]{1,0:T(8,128)(2,1)S(1)} %collective-permute-done.11.refs_1_, bf16[2048,1536]{1,0:T(8,128)(2,1)S(1)} %bitcast.20, ...), custom_call_target="tpu_custom_call" | custom-call | flops 2415919104 | bytes 1572864 | tf_op jit(solution)/shard_map/expert_rows/pallas_call | solution.py:200
  50.5 1.4 %collective-permute-start.17 = (bf16[1040,128]{1,0:T(8,128)(2,1)S(1)}, bf16[1040,128]{1,0:T(8,128)(2,1)S(1)}, u32[]{:S(2)}, u32[]{:S(2)}) collective-permute-start(bf16[1040,128]{1,0:T(8,128)(2,1)S(1)} %collective-permute-done.16.refs_1_), channel_id=1, source_target_pairs={{6,2},{7,3},{10,6},{11,7},{14,10},{15,11},{12,14},{13,15},{8,12},{... | collective-permute-start | bytes 798728 | tf_op jit(solution)/shard_map/ppermute | solution.py:265
  51.9 2.7 %expert_rows.13 = (f32[64,2048]{1,0:T(8,128)S(1)}, f32[64,2048]{1,0:T(8,128)S(1)}) custom-call(s32[1]{0:T(128)} %bitcast.6.expert_ref, bf16[1040,128]{1,0:T(8,128)(2,1)S(1)} %collective-permute-done.15.refs_0_, bf16[1040,128]{1,0:T(8,128)(2,1)S(1)} %collective-permute-done.16.refs_1_, bf16[2048,1536]{1,0:T(8,128)(2,1)S(1)} %bitcast.21, ...), custom_call_target="tpu_custom_call" | custom-call | flops 2415919104 | bytes 1572864 | tf_op jit(solution)/shard_map/expert_rows/pallas_call | solution.py:200
  54.7 0.7 collective-permute-start.21
  55.4 1.4 %collective-permute-start.18 = (bf16[64,2048]{1,0:T(8,128)(2,1)S(1)}, bf16[64,2048]{1,0:T(8,128)(2,1)S(1)}, u32[]{:S(2)}, u32[]{:S(2)}) collective-permute-start(bf16[64,2048]{1,0:T(8,128)(2,1)S(1)} %convert_element_type.85), channel_id=1, source_target_pairs={{6,2},{7,3},{10,6},{11,7},{14,10},{15,11},{12,14},{13,15},{8,12},{... | collective-permute-start | bytes 786440 | tf_op jit(solution)/shard_map/ppermute | solution.py:265
  56.9 1.9 %collective-permute-done.17.refs_1_ = bf16[1040,128]{1,0:T(8,128)(2,1)S(1)} collective-permute-done((bf16[1040,128]{1,0:T(8,128)(2,1)S(1)}, bf16[1040,128]{1,0:T(8,128)(2,1)S(1)}, u32[]{:S(2)}, u32[]{:S(2)}) %collective-permute-start.17) | collective-permute-done | bytes 266272 | tf_op jit(solution)/shard_map/ppermute | solution.py:265
  58.8 2.8 %expert_rows.14 = (f32[64,2048]{1,0:T(8,128)S(1)}, f32[64,2048]{1,0:T(8,128)S(1)}) custom-call(s32[1]{0:T(128)} %bitcast.6.expert_ref, bf16[1040,128]{1,0:T(8,128)(2,1)S(1)} %collective-permute-done.14.refs_0_, bf16[1040,128]{1,0:T(8,128)(2,1)S(1)} %collective-permute-done.17.refs_1_, bf16[2048,1536]{1,0:T(8,128)(2,1)S(1)} %bitcast.22, ...), custom_call_target="tpu_custom_call" | custom-call | flops 2415919104 | bytes 1572864 | tf_op jit(solution)/shard_map/expert_rows/pallas_call | solution.py:200
  61.6 0.9 collective-permute-done.18
  62.6 1.6 %collective-permute-start.20 = (bf16[64,2048]{1,0:T(8,128)(2,1)S(1)}, bf16[64,2048]{1,0:T(8,128)(2,1)S(1)}, u32[]{:S(2)}, u32[]{:S(2)}) collective-permute-start(bf16[64,2048]{1,0:T(8,128)(2,1)S(1)} %convert_element_type.88), channel_id=1, source_target_pairs={{2,6},{3,7},{6,10},{7,11},{10,14},{11,15},{14,12},{15,13},{12,8},{... | collective-permute-start | bytes 786440 | tf_op jit(solution)/shard_map/ppermute | solution.py:265
  64.2 0.1 add_convert_fusion.8
  64.4 1.6 %collective-permute-start.26 = (bf16[64,2048]{1,0:T(8,128)(2,1)S(1)}, bf16[64,2048]{1,0:T(8,128)(2,1)S(1)}, u32[]{:S(2)}, u32[]{:S(2)}) collective-permute-start(bf16[64,2048]{1,0:T(8,128)(2,1)S(1)} %get-tuple-element.111), channel_id=1, source_target_pairs={{2,6},{3,7},{6,10},{7,11},{10,14},{11,15},{14,12},{15,13},{12,8},{... | collective-permute-start | bytes 786440 | tf_op jit(solution)/shard_map/ppermute | solution.py:265
  66.0 0.5 collective-permute-start.19
  66.4 0.4 collective-permute-start.23
  66.9 2.8 %expert_rows.15 = (f32[64,2048]{1,0:T(8,128)S(1)}, f32[64,2048]{1,0:T(8,128)S(1)}) custom-call(s32[1]{0:T(128)} %bitcast.6.expert_ref, bf16[1040,128]{1,0:T(8,128)(2,1)S(1)} %get-tuple-element.67.refs_0_, bf16[1040,128]{1,0:T(8,128)(2,1)S(1)} %get-tuple-element.71.refs_1_, bf16[2048,1536]{1,0:T(8,128)(2,1)S(1)} %bitcast.23, bf16[768,2048]{1,0:T(8,128)(2,1)S(1)} %bitcast.32, ...), custom_call_target="tpu_custom_call" | custom-call | flops 2415919104 | bytes 1572864 | tf_op jit(solution)/shard_map/expert_rows/pallas_call | solution.py:200
  69.6 2.2 %collective-permute-done.20 = bf16[64,2048]{1,0:T(8,128)(2,1)S(1)} collective-permute-done((bf16[64,2048]{1,0:T(8,128)(2,1)S(1)}, bf16[64,2048]{1,0:T(8,128)(2,1)S(1)}, u32[]{:S(2)}, u32[]{:S(2)}) %collective-permute-start.20) | collective-permute-done | bytes 262176 | tf_op jit(solution)/shard_map/ppermute | solution.py:265
  71.9 1.6 %collective-permute-start.22 = (bf16[64,2048]{1,0:T(8,128)(2,1)S(1)}, bf16[64,2048]{1,0:T(8,128)(2,1)S(1)}, u32[]{:S(2)}, u32[]{:S(2)}) collective-permute-start(bf16[64,2048]{1,0:T(8,128)(2,1)S(1)} %add_convert_fusion.7), channel_id=1, source_target_pairs={{2,6},{3,7},{6,10},{7,11},{10,14},{11,15},{14,12},{15,13},{12,8},{... | collective-permute-start | bytes 786440 | tf_op jit(solution)/shard_map/ppermute | solution.py:265
  73.5 4.4 %collective-permute-done.23 = bf16[64,2048]{1,0:T(8,128)(2,1)S(1)} collective-permute-done((bf16[64,2048]{1,0:T(8,128)(2,1)S(1)}, bf16[64,2048]{1,0:T(8,128)(2,1)S(1)}, u32[]{:S(2)}, u32[]{:S(2)}) %collective-permute-start.23) | collective-permute-done | bytes 262176 | tf_op jit(solution)/shard_map/ppermute | solution.py:265
  78.0 0.5 collective-permute-start.24
  78.5 1.6 %collective-permute-done.22 = bf16[64,2048]{1,0:T(8,128)(2,1)S(1)} collective-permute-done((bf16[64,2048]{1,0:T(8,128)(2,1)S(1)}, bf16[64,2048]{1,0:T(8,128)(2,1)S(1)}, u32[]{:S(2)}, u32[]{:S(2)}) %collective-permute-start.22) | collective-permute-done | bytes 262176 | tf_op jit(solution)/shard_map/ppermute | solution.py:265
  80.2 1.6 %collective-permute-start.28 = (bf16[64,2048]{1,0:T(8,128)(2,1)S(1)}, bf16[64,2048]{1,0:T(8,128)(2,1)S(1)}, u32[]{:S(2)}, u32[]{:S(2)}) collective-permute-start(bf16[64,2048]{1,0:T(8,128)(2,1)S(1)} %add_convert_fusion.5), channel_id=1, source_target_pairs={{2,6},{3,7},{6,10},{7,11},{10,14},{11,15},{14,12},{15,13},{12,8},{... | collective-permute-start | bytes 786440 | tf_op jit(solution)/shard_map/ppermute | solution.py:265
  81.9 4.1 %collective-permute-done.24 = bf16[64,2048]{1,0:T(8,128)(2,1)S(1)} collective-permute-done((bf16[64,2048]{1,0:T(8,128)(2,1)S(1)}, bf16[64,2048]{1,0:T(8,128)(2,1)S(1)}, u32[]{:S(2)}, u32[]{:S(2)}) %collective-permute-start.24) | collective-permute-done | bytes 262176 | tf_op jit(solution)/shard_map/ppermute | solution.py:265
  86.1 0.5 collective-permute-start.30
  86.7 0.5 collective-permute-start.25
  87.2 1.7 %collective-permute-start.27 = (bf16[64,2048]{1,0:T(8,128)(2,1)S(1)}, bf16[64,2048]{1,0:T(8,128)(2,1)S(1)}, u32[]{:S(2)}, u32[]{:S(2)}) collective-permute-start(bf16[64,2048]{1,0:T(8,128)(2,1)S(1)} %add_convert_fusion.2), channel_id=1, source_target_pairs={{2,6},{3,7},{6,10},{7,11},{10,14},{11,15},{14,12},{15,13},{12,8},{... | collective-permute-start | bytes 786440 | tf_op jit(solution)/shard_map/ppermute | solution.py:265
  88.9 0.5 collective-permute-done.28
  89.4 1.6 %collective-permute-start.29 = (bf16[64,2048]{1,0:T(8,128)(2,1)S(1)}, bf16[64,2048]{1,0:T(8,128)(2,1)S(1)}, u32[]{:S(2)}, u32[]{:S(2)}) collective-permute-start(bf16[64,2048]{1,0:T(8,128)(2,1)S(1)} %add_convert_fusion.1), channel_id=1, source_target_pairs={{2,6},{3,7},{6,10},{7,11},{10,14},{11,15},{14,12},{15,13},{12,8},{... | collective-permute-start | bytes 786440 | tf_op jit(solution)/shard_map/ppermute | solution.py:265
  91.1 4.3 %collective-permute-done.30 = bf16[64,2048]{1,0:T(8,128)(2,1)S(1)} collective-permute-done((bf16[64,2048]{1,0:T(8,128)(2,1)S(1)}, bf16[64,2048]{1,0:T(8,128)(2,1)S(1)}, u32[]{:S(2)}, u32[]{:S(2)}) %collective-permute-start.30) | collective-permute-done | bytes 262176 | tf_op jit(solution)/shard_map/ppermute | solution.py:265
  95.4 0.5 collective-permute-start.31
  96.0 2.5 %collective-permute-done.25 = bf16[64,2048]{1,0:T(8,128)(2,1)S(1)} collective-permute-done((bf16[64,2048]{1,0:T(8,128)(2,1)S(1)}, bf16[64,2048]{1,0:T(8,128)(2,1)S(1)}, u32[]{:S(2)}, u32[]{:S(2)}) %collective-permute-start.25) | collective-permute-done | bytes 262176 | tf_op jit(solution)/shard_map/ppermute | solution.py:265
  98.7 3.2 %collective-permute-done.31.total1_ref = bf16[64,2048]{1,0:T(8,128)(2,1)S(1)} collective-permute-done((bf16[64,2048]{1,0:T(8,128)(2,1)S(1)}, bf16[64,2048]{1,0:T(8,128)(2,1)S(1)}, u32[]{:S(2)}, u32[]{:S(2)}) %collective-permute-start.31) | collective-permute-done | bytes 262176 | tf_op jit(solution)/shard_map/ppermute | solution.py:265
  101.9 0.9 last_rows.1
  (40 shorter events, 1.0 us)
Async XLA Ops:
  0.0 23.6 %copy-start.1 = (bf16[1,1,768,2048]{3,2,1,0:T(8,128)(2,1)S(1)}, bf16[1,1,768,2048]{3,2,1,0:T(8,128)(2,1)}, u32[]{:S(2)}) copy-start(bf16[1,1,768,2048]{3,2,1,0:T(8,128)(2,1)} %param.13) | copy-start | bytes 9437188
  0.0 18.1 %collective-permute-start.2 = (bf16[2048,1536]{1,0:T(8,128)(2,1)}, bf16[2048,1536]{1,0:T(8,128)(2,1)S(1)}, u32[]{:S(2)}, u32[]{:S(2)}) collective-permute-start(bf16[2048,1536]{1,0:T(8,128)(2,1)} %bitcast.15), channel_id=1, source_target_pairs={{0,1},{1,0},{2,3},{3,2},{4,5},{5,4},{6,7},{7,6},{8,9},{9,8},{10,11... | collective-permute-start | bytes 18874376 | tf_op jit(solution)/shard_map/ppermute | solution.py:265
  0.5 17.7 %collective-permute-start.3 = (bf16[768,2048]{1,0:T(8,128)(2,1)}, bf16[768,2048]{1,0:T(8,128)(2,1)S(1)}, u32[]{:S(2)}, u32[]{:S(2)}) collective-permute-start(bf16[768,2048]{1,0:T(8,128)(2,1)} %bitcast.24), channel_id=1, source_target_pairs={{0,1},{1,0},{2,3},{3,2},{4,5},{5,4},{6,7},{7,6},{8,9},{9,8},{10,11... | collective-permute-start | bytes 9437192 | tf_op jit(solution)/shard_map/ppermute | solution.py:265
  1.8 11.5 %collective-permute-start = (bf16[64,2048]{1,0:T(8,128)(2,1)S(1)}, bf16[64,2048]{1,0:T(8,128)(2,1)S(1)}, u32[]{:S(2)}, u32[]{:S(2)}) collective-permute-start(bf16[64,2048]{1,0:T(8,128)(2,1)S(1)} %get-tuple-element.110), channel_id=1, source_target_pairs={{0,16},{1,17},{2,18},{3,19},{4,20},{5,21},{6,22},{7,23},{8,24},{9,... | collective-permute-start | bytes 786440 | tf_op jit(solution)/shard_map/ppermute | solution.py:20
  6.7 11.3 %collective-permute-start.1 = (bf16[64,2048]{1,0:T(8,128)(2,1)S(1)}, bf16[64,2048]{1,0:T(8,128)(2,1)S(1)}, u32[]{:S(2)}, u32[]{:S(2)}) collective-permute-start(bf16[64,2048]{1,0:T(8,128)(2,1)S(1)} %get-tuple-element.109), channel_id=1, source_target_pairs={{0,16},{1,17},{2,18},{3,19},{4,20},{5,21},{6,22},{7,23},{8,24},{9,... | collective-permute-start | bytes 786440 | tf_op jit(solution)/shard_map/ppermute | solution.py:20
  8.0 1.0 %copy-start.2 = (bf16[128,2048]{1,0:T(8,128)(2,1)S(1)}, bf16[128,2048]{1,0:T(8,128)(2,1)}, u32[]{:S(2)}) copy-start(bf16[128,2048]{1,0:T(8,128)(2,1)} %fresh_ref.1) | copy-start | bytes 1572868
  9.1 0.7 copy-start.3
  9.8 0.7 copy-start.4
  10.5 0.7 copy-start.5
  13.4 6.8 %collective-permute-start.4 = (bf16[1040,128]{1,0:T(8,128)(2,1)S(1)}, bf16[1040,128]{1,0:T(8,128)(2,1)S(1)}, u32[]{:S(2)}, u32[]{:S(2)}) collective-permute-start(bf16[1040,128]{1,0:T(8,128)(2,1)S(1)} %get-tuple-element.67.refs_0_), channel_id=1, source_target_pairs={{2,6},{3,7},{6,10},{7,11},{10,14},{11,15},{14,12},{15,13},{12,8},{... | collective-permute-start | bytes 798728 | tf_op jit(solution)/shard_map/ppermute | solution.py:265
  15.0 6.6 %collective-permute-start.5 = (bf16[1040,128]{1,0:T(8,128)(2,1)S(1)}, bf16[1040,128]{1,0:T(8,128)(2,1)S(1)}, u32[]{:S(2)}, u32[]{:S(2)}) collective-permute-start(bf16[1040,128]{1,0:T(8,128)(2,1)S(1)} %get-tuple-element.67.refs_0_), channel_id=1, source_target_pairs={{6,2},{7,3},{10,6},{11,7},{14,10},{15,11},{12,14},{13,15},{8,12},{... | collective-permute-start | bytes 798728 | tf_op jit(solution)/shard_map/ppermute | solution.py:265
  18.1 11.0 %collective-permute-start.8 = (bf16[1040,128]{1,0:T(8,128)(2,1)S(1)}, bf16[1040,128]{1,0:T(8,128)(2,1)S(1)}, u32[]{:S(2)}, u32[]{:S(2)}) collective-permute-start(bf16[1040,128]{1,0:T(8,128)(2,1)S(1)} %get-tuple-element.71.refs_1_), channel_id=1, source_target_pairs={{2,6},{3,7},{6,10},{7,11},{10,14},{11,15},{14,12},{15,13},{12,8},{... | collective-permute-start | bytes 798728 | tf_op jit(solution)/shard_map/ppermute | solution.py:265
  19.7 9.5 %collective-permute-start.9 = (bf16[1040,128]{1,0:T(8,128)(2,1)S(1)}, bf16[1040,128]{1,0:T(8,128)(2,1)S(1)}, u32[]{:S(2)}, u32[]{:S(2)}) collective-permute-start(bf16[1040,128]{1,0:T(8,128)(2,1)S(1)} %get-tuple-element.71.refs_1_), channel_id=1, source_target_pairs={{6,2},{7,3},{10,6},{11,7},{14,10},{15,11},{12,14},{13,15},{8,12},{... | collective-permute-start | bytes 798728 | tf_op jit(solution)/shard_map/ppermute | solution.py:265
  21.6 12.4 %collective-permute-start.6 = (bf16[1040,128]{1,0:T(8,128)(2,1)S(1)}, bf16[1040,128]{1,0:T(8,128)(2,1)S(1)}, u32[]{:S(2)}, u32[]{:S(2)}) collective-permute-start(bf16[1040,128]{1,0:T(8,128)(2,1)S(1)} %collective-permute-done.4.refs_0_), channel_id=1, source_target_pairs={{2,6},{3,7},{6,10},{7,11},{10,14},{11,15},{14,12},{15,13},{12,8},{... | collective-permute-start | bytes 798728 | tf_op jit(solution)/shard_map/ppermute | solution.py:265
  23.2 11.6 %collective-permute-start.7 = (bf16[1040,128]{1,0:T(8,128)(2,1)S(1)}, bf16[1040,128]{1,0:T(8,128)(2,1)S(1)}, u32[]{:S(2)}, u32[]{:S(2)}) collective-permute-start(bf16[1040,128]{1,0:T(8,128)(2,1)S(1)} %collective-permute-done.5.refs_1_), channel_id=1, source_target_pairs={{6,2},{7,3},{10,6},{11,7},{14,10},{15,11},{12,14},{13,15},{8,12},{... | collective-permute-start | bytes 798728 | tf_op jit(solution)/shard_map/ppermute | solution.py:265
  23.6 2.8 %copy-start = (bf16[1,1,2048,1536]{3,2,1,0:T(8,128)(2,1)S(1)}, bf16[1,1,2048,1536]{3,2,1,0:T(8,128)(2,1)}, u32[]{:S(2)}) copy-start(bf16[1,1,2048,1536]{3,2,1,0:T(8,128)(2,1)} %param.12) | copy-start | bytes 18874372
  29.2 10.4 %collective-permute-start.12 = (bf16[1040,128]{1,0:T(8,128)(2,1)S(1)}, bf16[1040,128]{1,0:T(8,128)(2,1)S(1)}, u32[]{:S(2)}, u32[]{:S(2)}) collective-permute-start(bf16[1040,128]{1,0:T(8,128)(2,1)S(1)} %collective-permute-done.8.refs_0_), channel_id=1, source_target_pairs={{2,6},{3,7},{6,10},{7,11},{10,14},{11,15},{14,12},{15,13},{12,8},{... | collective-permute-start | bytes 798728 | tf_op jit(solution)/shard_map/ppermute | solution.py:265
  30.8 9.7 %collective-permute-start.13 = (bf16[1040,128]{1,0:T(8,128)(2,1)S(1)}, bf16[1040,128]{1,0:T(8,128)(2,1)S(1)}, u32[]{:S(2)}, u32[]{:S(2)}) collective-permute-start(bf16[1040,128]{1,0:T(8,128)(2,1)S(1)} %collective-permute-done.9.refs_1_), channel_id=1, source_target_pairs={{6,2},{7,3},{10,6},{11,7},{14,10},{15,11},{12,14},{13,15},{8,12},{... | collective-permute-start | bytes 798728 | tf_op jit(solution)/shard_map/ppermute | solution.py:265
  34.7 10.5 %collective-permute-start.10 = (bf16[1040,128]{1,0:T(8,128)(2,1)S(1)}, bf16[1040,128]{1,0:T(8,128)(2,1)S(1)}, u32[]{:S(2)}, u32[]{:S(2)}) collective-permute-start(bf16[1040,128]{1,0:T(8,128)(2,1)S(1)} %collective-permute-done.6.refs_0_), channel_id=1, source_target_pairs={{2,6},{3,7},{6,10},{7,11},{10,14},{11,15},{14,12},{15,13},{12,8},{... | collective-permute-start | bytes 798728 | tf_op jit(solution)/shard_map/ppermute | solution.py:265
  36.3 9.8 %collective-permute-start.11 = (bf16[1040,128]{1,0:T(8,128)(2,1)S(1)}, bf16[1040,128]{1,0:T(8,128)(2,1)S(1)}, u32[]{:S(2)}, u32[]{:S(2)}) collective-permute-start(bf16[1040,128]{1,0:T(8,128)(2,1)S(1)} %collective-permute-done.7.refs_1_), channel_id=1, source_target_pairs={{6,2},{7,3},{10,6},{11,7},{14,10},{15,11},{12,14},{13,15},{8,12},{... | collective-permute-start | bytes 798728 | tf_op jit(solution)/shard_map/ppermute | solution.py:265
  40.4 10.0 %collective-permute-start.15 = (bf16[1040,128]{1,0:T(8,128)(2,1)S(1)}, bf16[1040,128]{1,0:T(8,128)(2,1)S(1)}, u32[]{:S(2)}, u32[]{:S(2)}) collective-permute-start(bf16[1040,128]{1,0:T(8,128)(2,1)S(1)} %collective-permute-done.12.refs_0_), channel_id=1, source_target_pairs={{2,6},{3,7},{6,10},{7,11},{10,14},{11,15},{14,12},{15,13},{12,8},{... | collective-permute-start | bytes 798728 | tf_op jit(solution)/shard_map/ppermute | solution.py:265
  42.0 8.5 %collective-permute-start.16 = (bf16[1040,128]{1,0:T(8,128)(2,1)S(1)}, bf16[1040,128]{1,0:T(8,128)(2,1)S(1)}, u32[]{:S(2)}, u32[]{:S(2)}) collective-permute-start(bf16[1040,128]{1,0:T(8,128)(2,1)S(1)} %collective-permute-done.13.refs_1_), channel_id=1, source_target_pairs={{6,2},{7,3},{10,6},{11,7},{14,10},{15,11},{12,14},{13,15},{8,12},{... | collective-permute-start | bytes 798728 | tf_op jit(solution)/shard_map/ppermute | solution.py:265
  46.1 10.7 %collective-permute-start.14 = (bf16[1040,128]{1,0:T(8,128)(2,1)S(1)}, bf16[1040,128]{1,0:T(8,128)(2,1)S(1)}, u32[]{:S(2)}, u32[]{:S(2)}) collective-permute-start(bf16[1040,128]{1,0:T(8,128)(2,1)S(1)} %collective-permute-done.10.refs_0_), channel_id=1, source_target_pairs={{2,6},{3,7},{6,10},{7,11},{10,14},{11,15},{14,12},{15,13},{12,8},{... | collective-permute-start | bytes 798728 | tf_op jit(solution)/shard_map/ppermute | solution.py:265
  50.5 8.3 %collective-permute-start.17 = (bf16[1040,128]{1,0:T(8,128)(2,1)S(1)}, bf16[1040,128]{1,0:T(8,128)(2,1)S(1)}, u32[]{:S(2)}, u32[]{:S(2)}) collective-permute-start(bf16[1040,128]{1,0:T(8,128)(2,1)S(1)} %collective-permute-done.16.refs_1_), channel_id=1, source_target_pairs={{6,2},{7,3},{10,6},{11,7},{14,10},{15,11},{12,14},{13,15},{8,12},{... | collective-permute-start | bytes 798728 | tf_op jit(solution)/shard_map/ppermute | solution.py:265
  54.7 6.9 %collective-permute-start.21 = (bf16[64,2048]{1,0:T(8,128)(2,1)S(1)}, bf16[64,2048]{1,0:T(8,128)(2,1)S(1)}, u32[]{:S(2)}, u32[]{:S(2)}) collective-permute-start(bf16[64,2048]{1,0:T(8,128)(2,1)S(1)} %convert_element_type.89), channel_id=1, source_target_pairs={{2,6},{3,7},{6,10},{7,11},{10,14},{11,15},{14,12},{15,13},{12,8},{... | collective-permute-start | bytes 786440 | tf_op jit(solution)/shard_map/ppermute | solution.py:265
  55.4 7.1 %collective-permute-start.18 = (bf16[64,2048]{1,0:T(8,128)(2,1)S(1)}, bf16[64,2048]{1,0:T(8,128)(2,1)S(1)}, u32[]{:S(2)}, u32[]{:S(2)}) collective-permute-start(bf16[64,2048]{1,0:T(8,128)(2,1)S(1)} %convert_element_type.85), channel_id=1, source_target_pairs={{6,2},{7,3},{10,6},{11,7},{14,10},{15,11},{12,14},{13,15},{8,12},{... | collective-permute-start | bytes 786440 | tf_op jit(solution)/shard_map/ppermute | solution.py:265
  62.6 9.2 %collective-permute-start.20 = (bf16[64,2048]{1,0:T(8,128)(2,1)S(1)}, bf16[64,2048]{1,0:T(8,128)(2,1)S(1)}, u32[]{:S(2)}, u32[]{:S(2)}) collective-permute-start(bf16[64,2048]{1,0:T(8,128)(2,1)S(1)} %convert_element_type.88), channel_id=1, source_target_pairs={{2,6},{3,7},{6,10},{7,11},{10,14},{11,15},{14,12},{15,13},{12,8},{... | collective-permute-start | bytes 786440 | tf_op jit(solution)/shard_map/ppermute | solution.py:265
  64.4 22.2 %collective-permute-start.26 = (bf16[64,2048]{1,0:T(8,128)(2,1)S(1)}, bf16[64,2048]{1,0:T(8,128)(2,1)S(1)}, u32[]{:S(2)}, u32[]{:S(2)}) collective-permute-start(bf16[64,2048]{1,0:T(8,128)(2,1)S(1)} %get-tuple-element.111), channel_id=1, source_target_pairs={{2,6},{3,7},{6,10},{7,11},{10,14},{11,15},{14,12},{15,13},{12,8},{... | collective-permute-start | bytes 786440 | tf_op jit(solution)/shard_map/ppermute | solution.py:265
  66.0 20.6 %collective-permute-start.19 = (bf16[64,2048]{1,0:T(8,128)(2,1)S(1)}, bf16[64,2048]{1,0:T(8,128)(2,1)S(1)}, u32[]{:S(2)}, u32[]{:S(2)}) collective-permute-start(bf16[64,2048]{1,0:T(8,128)(2,1)S(1)} %get-tuple-element.112), channel_id=1, source_target_pairs={{6,2},{7,3},{10,6},{11,7},{14,10},{15,11},{12,14},{13,15},{8,12},{... | collective-permute-start | bytes 786440 | tf_op jit(solution)/shard_map/ppermute | solution.py:265
  66.4 11.5 %collective-permute-start.23 = (bf16[64,2048]{1,0:T(8,128)(2,1)S(1)}, bf16[64,2048]{1,0:T(8,128)(2,1)S(1)}, u32[]{:S(2)}, u32[]{:S(2)}) collective-permute-start(bf16[64,2048]{1,0:T(8,128)(2,1)S(1)} %convert_element_type.94), channel_id=1, source_target_pairs={{6,2},{7,3},{10,6},{11,7},{14,10},{15,11},{12,14},{13,15},{8,12},{... | collective-permute-start | bytes 786440 | tf_op jit(solution)/shard_map/ppermute | solution.py:265
  71.9 8.3 %collective-permute-start.22 = (bf16[64,2048]{1,0:T(8,128)(2,1)S(1)}, bf16[64,2048]{1,0:T(8,128)(2,1)S(1)}, u32[]{:S(2)}, u32[]{:S(2)}) collective-permute-start(bf16[64,2048]{1,0:T(8,128)(2,1)S(1)} %add_convert_fusion.7), channel_id=1, source_target_pairs={{2,6},{3,7},{6,10},{7,11},{10,14},{11,15},{14,12},{15,13},{12,8},{... | collective-permute-start | bytes 786440 | tf_op jit(solution)/shard_map/ppermute | solution.py:265
  78.0 8.0 %collective-permute-start.24 = (bf16[64,2048]{1,0:T(8,128)(2,1)S(1)}, bf16[64,2048]{1,0:T(8,128)(2,1)S(1)}, u32[]{:S(2)}, u32[]{:S(2)}) collective-permute-start(bf16[64,2048]{1,0:T(8,128)(2,1)S(1)} %add_convert_fusion.6), channel_id=1, source_target_pairs={{6,2},{7,3},{10,6},{11,7},{14,10},{15,11},{12,14},{13,15},{8,12},{... | collective-permute-start | bytes 786440 | tf_op jit(solution)/shard_map/ppermute | solution.py:265
  80.2 9.2 %collective-permute-start.28 = (bf16[64,2048]{1,0:T(8,128)(2,1)S(1)}, bf16[64,2048]{1,0:T(8,128)(2,1)S(1)}, u32[]{:S(2)}, u32[]{:S(2)}) collective-permute-start(bf16[64,2048]{1,0:T(8,128)(2,1)S(1)} %add_convert_fusion.5), channel_id=1, source_target_pairs={{2,6},{3,7},{6,10},{7,11},{10,14},{11,15},{14,12},{15,13},{12,8},{... | collective-permute-start | bytes 786440 | tf_op jit(solution)/shard_map/ppermute | solution.py:265
  86.1 9.3 %collective-permute-start.30 = (bf16[64,2048]{1,0:T(8,128)(2,1)S(1)}, bf16[64,2048]{1,0:T(8,128)(2,1)S(1)}, u32[]{:S(2)}, u32[]{:S(2)}) collective-permute-start(bf16[64,2048]{1,0:T(8,128)(2,1)S(1)} %add_convert_fusion.4), channel_id=1, source_target_pairs={{6,2},{7,3},{10,6},{11,7},{14,10},{15,11},{12,14},{13,15},{8,12},{... | collective-permute-start | bytes 786440 | tf_op jit(solution)/shard_map/ppermute | solution.py:265
  86.7 11.8 %collective-permute-start.25 = (bf16[64,2048]{1,0:T(8,128)(2,1)S(1)}, bf16[64,2048]{1,0:T(8,128)(2,1)S(1)}, u32[]{:S(2)}, u32[]{:S(2)}) collective-permute-start(bf16[64,2048]{1,0:T(8,128)(2,1)S(1)} %add_convert_fusion.3), channel_id=1, source_target_pairs={{6,2},{7,3},{10,6},{11,7},{14,10},{15,11},{12,14},{13,15},{8,12},{... | collective-permute-start | bytes 786440 | tf_op jit(solution)/shard_map/ppermute | solution.py:265
  87.2 11.4 %collective-permute-start.27 = (bf16[64,2048]{1,0:T(8,128)(2,1)S(1)}, bf16[64,2048]{1,0:T(8,128)(2,1)S(1)}, u32[]{:S(2)}, u32[]{:S(2)}) collective-permute-start(bf16[64,2048]{1,0:T(8,128)(2,1)S(1)} %add_convert_fusion.2), channel_id=1, source_target_pairs={{2,6},{3,7},{6,10},{7,11},{10,14},{11,15},{14,12},{15,13},{12,8},{... | collective-permute-start | bytes 786440 | tf_op jit(solution)/shard_map/ppermute | solution.py:265
  89.4 9.2 %collective-permute-start.29 = (bf16[64,2048]{1,0:T(8,128)(2,1)S(1)}, bf16[64,2048]{1,0:T(8,128)(2,1)S(1)}, u32[]{:S(2)}, u32[]{:S(2)}) collective-permute-start(bf16[64,2048]{1,0:T(8,128)(2,1)S(1)} %add_convert_fusion.1), channel_id=1, source_target_pairs={{2,6},{3,7},{6,10},{7,11},{10,14},{11,15},{14,12},{15,13},{12,8},{... | collective-permute-start | bytes 786440 | tf_op jit(solution)/shard_map/ppermute | solution.py:265
  95.4 6.4 %collective-permute-start.31 = (bf16[64,2048]{1,0:T(8,128)(2,1)S(1)}, bf16[64,2048]{1,0:T(8,128)(2,1)S(1)}, u32[]{:S(2)}, u32[]{:S(2)}) collective-permute-start(bf16[64,2048]{1,0:T(8,128)(2,1)S(1)} %add_convert_fusion), channel_id=1, source_target_pairs={{6,2},{7,3},{10,6},{11,7},{14,10},{15,11},{12,14},{13,15},{8,12},{... | collective-permute-start | bytes 786440 | tf_op jit(solution)/shard_map/ppermute | solution.py:265

commit v10 on v8

--- a/solution.py
+++ b/solution.py
@@ -152,12 +152,16 @@
     )(section_id, base, coefs, fresh, arrived, gain)
 
 
-def mlp_kernel(expert_ref, *refs, parts, chained):
+def mlp_kernel(expert_ref, *refs, parts, adds, chained):
     payloads = refs[:parts]
     weights = (refs[parts : parts + 2], refs[parts + 2 : parts + 4])
-    refs = refs[parts + 4 + chained :]
-    outs = refs[:parts]
-    x_ref, coef_ref, hidden_ref = refs[parts:]
+    refs = refs[parts + 4 :]
+    terms, totals = refs[:adds], refs[adds : 2 * adds]
+    refs = refs[2 * adds + chained :]
+    outs, added = refs[:parts], refs[parts : parts + adds]
+    x_ref, coef_ref, hidden_ref = refs[parts + adds :]
+    for term, total, result in zip(terms, totals, added):
+        result[...] = (term[...] + total[...].astype(jnp.float32)).astype(jnp.bfloat16)
     width = x_ref.shape[1]
     hidden = weights[0][1].shape[0]
     line = lax.broadcasted_iota(jnp.int32, (HALF, LANES), 0)
@@ -191,19 +195,20 @@
             out[:, t : t + tile] = total[here, :]
 
 
-def expert_rows(expert_id, payloads, own, other, after):
+def expert_rows(expert_id, payloads, own, other, after, terms=(), totals=()):
     width = own[0].shape[0]
     hidden = own[1].shape[0]
     rows = HALF * len(payloads)
     vmem = pl.BlockSpec(memory_space=pltpu.VMEM)
     chain = [] if after is None else [after]
     return pl.pallas_call(
-        functools.partial(mlp_kernel, parts=len(payloads), chained=len(chain)),
-        out_shape=[jax.ShapeDtypeStruct((HALF, width), jnp.float32)] * len(payloads),
+        functools.partial(mlp_kernel, parts=len(payloads), adds=len(terms), chained=len(chain)),
+        out_shape=[jax.ShapeDtypeStruct((HALF, width), jnp.float32)] * len(payloads)
+        + [jax.ShapeDtypeStruct((HALF, width), jnp.bfloat16)] * len(terms),
         in_specs=[pl.BlockSpec(memory_space=pltpu.SMEM)]
-        + [vmem] * (len(payloads) + 4)
+        + [vmem] * (len(payloads) + 4 + 2 * len(terms))
         + [pl.BlockSpec(memory_space=pl.ANY)] * len(chain),
-        out_specs=[vmem] * len(payloads),
+        out_specs=[vmem] * (len(payloads) + len(terms)),
         scratch_shapes=[
             pltpu.VMEM((rows, width), jnp.bfloat16),
             pltpu.VMEM((2, rows, LANES), jnp.float32),
@@ -216,7 +221,7 @@
             transcendentals=rows * hidden * 2,
         ),
         name="expert_rows",
-    )(expert_id, *payloads, *own, *other, *chain)
+    )(expert_id, *payloads, *own, *other, *terms, *totals, *chain)
 
 
 def last_kernel(near0_ref, near1_ref, total0_ref, total1_ref, out_ref):
@@ -286,9 +291,9 @@
 
     last = None
 
-    def mlp(payloads):
+    def mlp(payloads, terms=(), totals=()):
         nonlocal last
-        sums = expert_rows(expert_id, payloads, own, other, last)
+        sums = expert_rows(expert_id, payloads, own, other, last, terms, totals)
         last = sums[0]
         return sums
 
@@ -300,7 +305,6 @@
             pass_on(s, c, last)
             to_down[s, c], to_up[s, c] = mlp([ups[s][c], downs[s][c]])
     to_up[hops, 0], to_down[hops, 1] = mlp([ups[hops][0], downs[hops][1]])
-    own_sums = mlp(packed)
 
     def send_on(flow, place, total, after):
         terms, c, pairs = flow
@@ -316,12 +320,13 @@
     long = [(to_up, 0, up), (to_down, 1, down)]
     short_totals = [send_on(flow, hops - 1, None, None)[1] for flow in short]
     long_totals = [send_on(flow, hops, None, None)[1] for flow in long]
-    after = to_up[hops, 0]
+    *own_sums, down_sum, up_sum = mlp(packed, [f[0][hops - 2, f[1]] for f in short], short_totals)
+    short_totals = [move(total, flow[2]) for total, flow in zip((down_sum, up_sum), short)]
+    after = None
     for s in reversed(range(1, hops)):
-        if s > 1:
-            sent, short_totals = zip(*(send_on(f, s - 1, t, after) for f, t in zip(short, short_totals)))
-        sent, long_totals = zip(*(send_on(f, s, t, sent) for f, t in zip(long, long_totals)))
-        after = sent
+        if 1 < s < hops - 1:
+            after, short_totals = zip(*(send_on(f, s - 1, t, after) for f, t in zip(short, short_totals)))
+        after, long_totals = zip(*(send_on(f, s, t, after) for f, t in zip(long, long_totals)))
 
     nears = [
         arrival[c].astype(jnp.float32) + (own_sums[c] + short_totals[c].astype(jnp.float32)) for c in range(2)
@@ -336,7 +341,7 @@
 
     def body(*args):
         topk_count, local_experts = args[3].shape[2], args[5].shape[1]
-        regular = devices_exp % (2 * CORES * across) == 0 and devices_exp % 16 == 0 and args[0].shape[0] == LANES
+        regular = devices_exp % (2 * CORES * across) == 0 and devices_exp >= 6 * CORES and devices_exp % 16 == 0 and args[0].shape[0] == LANES
         if local_experts == 1 and devices_exp <= 2 * topk_count and regular:
             return relay_body(*args, across=across)
         return routed_body(*args)

time: 102 us -> 102 us (level)
  transfers between devices with their start and end apart: 32 -> 32, of which waited for: 15 -> 19; matrix products, arithmetic and copies ran while one was open for 2% -> 2% of each run, Pallas kernels for 22% -> 22%
where the time goes in v10:
time: 102 us; the launch traced here: 101 us
  starting transfers between devices  36.1 us (35%)
  waiting for transfers between devices  33.5 us (33%)
  Pallas kernels  23.5 us (23%)
  local copies, waits for them, and re-layouts  7.21 us (7%)
    ppermute x30, starting transfers between devices, move(): return lax.ppermute(value, 'expert', pairs)  29.9 us
    ppermute x30, waiting for transfers between devices, move(): return lax.ppermute(value, 'expert', pairs)  29 us
    pallas_call x8, Pallas kernels, expert_rows(): pl.pallas_call(functools.partial(mlp_kernel, parts=len(payloads), adds=le...  22.2 us
    ppermute x2, starting transfers between devices, from_behind(): return lax.ppermute(value, axis, pairs)  6.18 us
    unnamed x12, local copies, waits for them, and re-layouts  5.89 us
    ppermute x2, waiting for transfers between devices, from_behind(): return lax.ppermute(value, axis, pairs)  4.5 us
  transfers between devices with their start and end apart: 32, of which 19 were waited for; matrix products, arithmetic and copies ran while one was open for 2% of the time, Pallas kernels for 22%

profile of v10, /device:TPU:0, one launch (start us, length us, event | category | flops | bytes accessed | tf_op | source)
XLA Modules:
  0.0 101.3 jit_solution(4921275841457812273)
XLA Ops:
  0.0 0.5 collective-permute-start.2
  0.5 1.3 %slice_bitcast_fusion = (bf16[64,2048]{1,0:T(8,128)(2,1)S(1)}, bf16[64,2048]{1,0:T(8,128)(2,1)S(1)}) fusion(bf16[1,128,2048]{2,1,0:T(8,128)(2,1)} %param.8), kind=kLoop, calls=%fused_computation.10 | loop fusion | bytes 1048576 | tf_op jit(solution)/shard_map/squeeze | solution.py:277
  1.8 4.9 %collective-permute-start = (bf16[64,2048]{1,0:T(8,128)(2,1)S(1)}, bf16[64,2048]{1,0:T(8,128)(2,1)S(1)}, u32[]{:S(2)}, u32[]{:S(2)}) collective-permute-start(bf16[64,2048]{1,0:T(8,128)(2,1)S(1)} %get-tuple-element.106), channel_id=1, source_target_pairs={{0,16},{1,17},{2,18},{3,19},{4,20},{5,21},{6,22},{7,23},{8,24},{9,... | collective-permute-start | bytes 786440 | tf_op jit(solution)/shard_map/ppermute | solution.py:20
  6.7 1.3 %collective-permute-start.1 = (bf16[64,2048]{1,0:T(8,128)(2,1)S(1)}, bf16[64,2048]{1,0:T(8,128)(2,1)S(1)}, u32[]{:S(2)}, u32[]{:S(2)}) collective-permute-start(bf16[64,2048]{1,0:T(8,128)(2,1)S(1)} %get-tuple-element.105), channel_id=1, source_target_pairs={{0,16},{1,17},{2,18},{3,19},{4,20},{5,21},{6,22},{7,23},{8,24},{9,... | collective-permute-start | bytes 786440 | tf_op jit(solution)/shard_map/ppermute | solution.py:20
  8.1 1.0 %copy-done.2 = bf16[128,2048]{1,0:T(8,128)(2,1)S(1)} copy-done((bf16[128,2048]{1,0:T(8,128)(2,1)S(1)}, bf16[128,2048]{1,0:T(8,128)(2,1)}, u32[]{:S(2)}) %copy-start.2) | copy-done | bytes 524312
  9.1 0.7 copy-done.3
  9.8 0.7 copy-done.4
  10.5 0.7 copy-done.5
  11.4 2.0 %collective-permute-done.arrived_ref = bf16[64,2048]{1,0:T(8,128)(2,1)S(1)} collective-permute-done((bf16[64,2048]{1,0:T(8,128)(2,1)S(1)}, bf16[64,2048]{1,0:T(8,128)(2,1)S(1)}, u32[]{:S(2)}, u32[]{:S(2)}) %collective-permute-start) | collective-permute-done | bytes 262176 | tf_op jit(solution)/shard_map/ppermute | solution.py:20
  13.4 1.5 %collective-permute-start.4 = (bf16[1040,128]{1,0:T(8,128)(2,1)S(1)}, bf16[1040,128]{1,0:T(8,128)(2,1)S(1)}, u32[]{:S(2)}, u32[]{:S(2)}) collective-permute-start(bf16[1040,128]{1,0:T(8,128)(2,1)S(1)} %get-tuple-element.65.refs_0_), channel_id=1, source_target_pairs={{2,6},{3,7},{6,10},{7,11},{10,14},{11,15},{14,12},{15,13},{12,8},{... | collective-permute-start | bytes 798728 | tf_op jit(solution)/shard_map/ppermute | solution.py:270
  15.0 0.5 collective-permute-start.5
  15.5 2.5 %collective-permute-done.1.arrived_ref = bf16[64,2048]{1,0:T(8,128)(2,1)S(1)} collective-permute-done((bf16[64,2048]{1,0:T(8,128)(2,1)S(1)}, bf16[64,2048]{1,0:T(8,128)(2,1)S(1)}, u32[]{:S(2)}, u32[]{:S(2)}) %collective-permute-start.1) | collective-permute-done | bytes 262176 | tf_op jit(solution)/shard_map/ppermute | solution.py:20
  18.1 1.5 %collective-permute-start.8 = (bf16[1040,128]{1,0:T(8,128)(2,1)S(1)}, bf16[1040,128]{1,0:T(8,128)(2,1)S(1)}, u32[]{:S(2)}, u32[]{:S(2)}) collective-permute-start(bf16[1040,128]{1,0:T(8,128)(2,1)S(1)} %get-tuple-element.69.refs_1_), channel_id=1, source_target_pairs={{2,6},{3,7},{6,10},{7,11},{10,14},{11,15},{14,12},{15,13},{12,8},{... | collective-permute-start | bytes 798728 | tf_op jit(solution)/shard_map/ppermute | solution.py:270
  19.7 0.5 collective-permute-start.9
  20.2 1.3 %collective-permute-done.5.refs_1_ = bf16[1040,128]{1,0:T(8,128)(2,1)S(1)} collective-permute-done((bf16[1040,128]{1,0:T(8,128)(2,1)S(1)}, bf16[1040,128]{1,0:T(8,128)(2,1)S(1)}, u32[]{:S(2)}, u32[]{:S(2)}) %collective-permute-start.5) | collective-permute-done | bytes 266272 | tf_op jit(solution)/shard_map/ppermute | solution.py:270
  21.6 1.6 %collective-permute-start.6 = (bf16[1040,128]{1,0:T(8,128)(2,1)S(1)}, bf16[1040,128]{1,0:T(8,128)(2,1)S(1)}, u32[]{:S(2)}, u32[]{:S(2)}) collective-permute-start(bf16[1040,128]{1,0:T(8,128)(2,1)S(1)} %collective-permute-done.4.refs_0_), channel_id=1, source_target_pairs={{2,6},{3,7},{6,10},{7,11},{10,14},{11,15},{14,12},{15,13},{12,8},{... | collective-permute-start | bytes 798728 | tf_op jit(solution)/shard_map/ppermute | solution.py:270
  23.2 0.4 collective-permute-start.7
  23.6 2.8 %copy-done = bf16[1,1,2048,1536]{3,2,1,0:T(8,128)(2,1)S(1)} copy-done((bf16[1,1,2048,1536]{3,2,1,0:T(8,128)(2,1)S(1)}, bf16[1,1,2048,1536]{3,2,1,0:T(8,128)(2,1)}, u32[]{:S(2)}) %copy-start) | copy-done | bytes 6291480
  26.4 2.8 %expert_rows.8 = (f32[64,2048]{1,0:T(8,128)S(1)}, f32[64,2048]{1,0:T(8,128)S(1)}) custom-call(s32[1]{0:T(128)} %bitcast.6.expert_ref, bf16[1040,128]{1,0:T(8,128)(2,1)S(1)} %collective-permute-done.4.refs_0_, bf16[1040,128]{1,0:T(8,128)(2,1)S(1)} %collective-permute-done.5.refs_1_, bf16[2048,1536]{1,0:T(8,128)(2,1)S(1)} %bitcast.16, ...), custom_call_target="tpu_custom_call" | custom-call | flops 2415919104 | bytes 1572864 | tf_op jit(solution)/shard_map/expert_rows/pallas_call | solution.py:204
  29.2 1.6 %collective-permute-start.10 = (bf16[1040,128]{1,0:T(8,128)(2,1)S(1)}, bf16[1040,128]{1,0:T(8,128)(2,1)S(1)}, u32[]{:S(2)}, u32[]{:S(2)}) collective-permute-start(bf16[1040,128]{1,0:T(8,128)(2,1)S(1)} %collective-permute-done.8.refs_0_), channel_id=1, source_target_pairs={{2,6},{3,7},{6,10},{7,11},{10,14},{11,15},{14,12},{15,13},{12,8},{... | collective-permute-start | bytes 798728 | tf_op jit(solution)/shard_map/ppermute | solution.py:270
  30.8 0.5 collective-permute-start.11
  31.3 2.8 %expert_rows.9 = (f32[64,2048]{1,0:T(8,128)S(1)}, f32[64,2048]{1,0:T(8,128)S(1)}) custom-call(s32[1]{0:T(128)} %bitcast.6.expert_ref, bf16[1040,128]{1,0:T(8,128)(2,1)S(1)} %collective-permute-done.8.refs_0_, bf16[1040,128]{1,0:T(8,128)(2,1)S(1)} %collective-permute-done.9.refs_1_, bf16[2048,1536]{1,0:T(8,128)(2,1)S(1)} %bitcast.17, ...), custom_call_target="tpu_custom_call" | custom-call | flops 2415919104 | bytes 1572864 | tf_op jit(solution)/shard_map/expert_rows/pallas_call | solution.py:204
  34.0 0.7 collective-permute-done.7.refs_1_
  34.7 1.6 %collective-permute-start.12 = (bf16[1040,128]{1,0:T(8,128)(2,1)S(1)}, bf16[1040,128]{1,0:T(8,128)(2,1)S(1)}, u32[]{:S(2)}, u32[]{:S(2)}) collective-permute-start(bf16[1040,128]{1,0:T(8,128)(2,1)S(1)} %collective-permute-done.6.refs_0_), channel_id=1, source_target_pairs={{2,6},{3,7},{6,10},{7,11},{10,14},{11,15},{14,12},{15,13},{12,8},{... | collective-permute-start | bytes 798728 | tf_op jit(solution)/shard_map/ppermute | solution.py:270
  36.3 0.4 collective-permute-start.13
  36.8 2.8 %expert_rows.10 = (f32[64,2048]{1,0:T(8,128)S(1)}, f32[64,2048]{1,0:T(8,128)S(1)}) custom-call(s32[1]{0:T(128)} %bitcast.6.expert_ref, bf16[1040,128]{1,0:T(8,128)(2,1)S(1)} %collective-permute-done.6.refs_0_, bf16[1040,128]{1,0:T(8,128)(2,1)S(1)} %collective-permute-done.7.refs_1_, bf16[2048,1536]{1,0:T(8,128)(2,1)S(1)} %bitcast.18, ...), custom_call_target="tpu_custom_call" | custom-call | flops 2415919104 | bytes 1572864 | tf_op jit(solution)/shard_map/expert_rows/pallas_call | solution.py:204
  39.5 0.9 collective-permute-done.11.refs_1_
  40.4 1.6 %collective-permute-start.15 = (bf16[1040,128]{1,0:T(8,128)(2,1)S(1)}, bf16[1040,128]{1,0:T(8,128)(2,1)S(1)}, u32[]{:S(2)}, u32[]{:S(2)}) collective-permute-start(bf16[1040,128]{1,0:T(8,128)(2,1)S(1)} %collective-permute-done.10.refs_0_), channel_id=1, source_target_pairs={{2,6},{3,7},{6,10},{7,11},{10,14},{11,15},{14,12},{15,13},{12,8},{... | collective-permute-start | bytes 798728 | tf_op jit(solution)/shard_map/ppermute | solution.py:270
  42.0 0.5 collective-permute-start.16
  42.5 2.7 %expert_rows.11 = (f32[64,2048]{1,0:T(8,128)S(1)}, f32[64,2048]{1,0:T(8,128)S(1)}) custom-call(s32[1]{0:T(128)} %bitcast.6.expert_ref, bf16[1040,128]{1,0:T(8,128)(2,1)S(1)} %collective-permute-done.10.refs_0_, bf16[1040,128]{1,0:T(8,128)(2,1)S(1)} %collective-permute-done.11.refs_1_, bf16[2048,1536]{1,0:T(8,128)(2,1)S(1)} %bitcast.19, ...), custom_call_target="tpu_custom_call" | custom-call | flops 2415919104 | bytes 1572864 | tf_op jit(solution)/shard_map/expert_rows/pallas_call | solution.py:204
  45.2 0.9 collective-permute-done.13.refs_1_
  46.1 1.6 %collective-permute-start.18 = (bf16[1040,128]{1,0:T(8,128)(2,1)S(1)}, bf16[1040,128]{1,0:T(8,128)(2,1)S(1)}, u32[]{:S(2)}, u32[]{:S(2)}) collective-permute-start(bf16[1040,128]{1,0:T(8,128)(2,1)S(1)} %collective-permute-done.12.refs_0_), channel_id=1, source_target_pairs={{2,6},{3,7},{6,10},{7,11},{10,14},{11,15},{14,12},{15,13},{12,8},{... | collective-permute-start | bytes 798728 | tf_op jit(solution)/shard_map/ppermute | solution.py:270
  47.7 2.8 %expert_rows.12 = (f32[64,2048]{1,0:T(8,128)S(1)}, f32[64,2048]{1,0:T(8,128)S(1)}) custom-call(s32[1]{0:T(128)} %bitcast.6.expert_ref, bf16[1040,128]{1,0:T(8,128)(2,1)S(1)} %collective-permute-done.12.refs_0_, bf16[1040,128]{1,0:T(8,128)(2,1)S(1)} %collective-permute-done.13.refs_1_, bf16[2048,1536]{1,0:T(8,128)(2,1)S(1)} %bitcast.20, ...), custom_call_target="tpu_custom_call" | custom-call | flops 2415919104 | bytes 1572864 | tf_op jit(solution)/shard_map/expert_rows/pallas_call | solution.py:204
  50.5 1.4 %collective-permute-start.19 = (bf16[1040,128]{1,0:T(8,128)(2,1)S(1)}, bf16[1040,128]{1,0:T(8,128)(2,1)S(1)}, u32[]{:S(2)}, u32[]{:S(2)}) collective-permute-start(bf16[1040,128]{1,0:T(8,128)(2,1)S(1)} %collective-permute-done.16.refs_1_), channel_id=1, source_target_pairs={{6,2},{7,3},{10,6},{11,7},{14,10},{15,11},{12,14},{13,15},{8,12},{... | collective-permute-start | bytes 798728 | tf_op jit(solution)/shard_map/ppermute | solution.py:270
  52.0 1.6 %collective-permute-start.14 = (bf16[64,2048]{1,0:T(8,128)(2,1)S(1)}, bf16[64,2048]{1,0:T(8,128)(2,1)S(1)}, u32[]{:S(2)}, u32[]{:S(2)}) collective-permute-start(bf16[64,2048]{1,0:T(8,128)(2,1)S(1)} %convert_element_type.73), channel_id=1, source_target_pairs={{6,2},{7,3},{10,6},{11,7},{14,10},{15,11},{12,14},{13,15},{8,12},{... | collective-permute-start | bytes 786440 | tf_op jit(solution)/shard_map/ppermute | solution.py:270
  53.6 2.7 %expert_rows.13 = (f32[64,2048]{1,0:T(8,128)S(1)}, f32[64,2048]{1,0:T(8,128)S(1)}) custom-call(s32[1]{0:T(128)} %bitcast.6.expert_ref, bf16[1040,128]{1,0:T(8,128)(2,1)S(1)} %collective-permute-done.15.refs_0_, bf16[1040,128]{1,0:T(8,128)(2,1)S(1)} %collective-permute-done.16.refs_1_, bf16[2048,1536]{1,0:T(8,128)(2,1)S(1)} %bitcast.21, ...), custom_call_target="tpu_custom_call" | custom-call | flops 2415919104 | bytes 1572864 | tf_op jit(solution)/shard_map/expert_rows/pallas_call | solution.py:204
  56.4 0.5 collective-permute-start.17
  56.9 2.4 %collective-permute-done.19.refs_1_ = bf16[1040,128]{1,0:T(8,128)(2,1)S(1)} collective-permute-done((bf16[1040,128]{1,0:T(8,128)(2,1)S(1)}, bf16[1040,128]{1,0:T(8,128)(2,1)S(1)}, u32[]{:S(2)}, u32[]{:S(2)}) %collective-permute-start.19) | collective-permute-done | bytes 266272 | tf_op jit(solution)/shard_map/ppermute | solution.py:270
  59.2 2.8 %expert_rows.14 = (f32[64,2048]{1,0:T(8,128)S(1)}, f32[64,2048]{1,0:T(8,128)S(1)}) custom-call(s32[1]{0:T(128)} %bitcast.6.expert_ref, bf16[1040,128]{1,0:T(8,128)(2,1)S(1)} %collective-permute-done.18.refs_0_, bf16[1040,128]{1,0:T(8,128)(2,1)S(1)} %collective-permute-done.19.refs_1_, bf16[2048,1536]{1,0:T(8,128)(2,1)S(1)} %bitcast.22, ...), custom_call_target="tpu_custom_call" | custom-call | flops 2415919104 | bytes 1572864 | tf_op jit(solution)/shard_map/expert_rows/pallas_call | solution.py:204
  62.1 0.6 collective-permute-start.22
  62.7 1.8 %collective-permute-start.21 = (bf16[64,2048]{1,0:T(8,128)(2,1)S(1)}, bf16[64,2048]{1,0:T(8,128)(2,1)S(1)}, u32[]{:S(2)}, u32[]{:S(2)}) collective-permute-start(bf16[64,2048]{1,0:T(8,128)(2,1)S(1)} %convert_element_type.75), channel_id=1, source_target_pairs={{2,6},{3,7},{6,10},{7,11},{10,14},{11,15},{14,12},{15,13},{12,8},{... | collective-permute-start | bytes 786440 | tf_op jit(solution)/shard_map/ppermute | solution.py:270
  64.4 0.4 collective-permute-done.14.refs_8_
  64.9 0.8 collective-permute-done.17.refs_9_
  65.6 2.9 %expert_rows.15 = (f32[64,2048]{1,0:T(8,128)S(1)}, f32[64,2048]{1,0:T(8,128)S(1)}, bf16[64,2048]{1,0:T(8,128)(2,1)S(1)}, bf16[64,2048]{1,0:T(8,128)(2,1)S(1)}) custom-call(s32[1]{0:T(128)} %bitcast.6.expert_ref, bf16[1040,128]{1,0:T(8,128)(2,1)S(1)} %get-tuple-element.65.refs_0_, bf16[1040,128]{1,0:T(8,128)(2,1)S(1)} %get-tuple-element.69.refs_1_, ...), custom_call_target="tpu_custom_call" | custom-call | flops 2415919104 | bytes 1572864 | tf_op jit(solution)/shard_map/expert_rows/pallas_call | solution.py:204
  68.5 1.6 %collective-permute-start.20 = (bf16[64,2048]{1,0:T(8,128)(2,1)S(1)}, bf16[64,2048]{1,0:T(8,128)(2,1)S(1)}, u32[]{:S(2)}, u32[]{:S(2)}) collective-permute-start(bf16[64,2048]{1,0:T(8,128)(2,1)S(1)} %get-tuple-element.88), channel_id=1, source_target_pairs={{6,2},{7,3},{10,6},{11,7},{14,10},{15,11},{12,14},{13,15},{8,12},{... | collective-permute-start | bytes 786440 | tf_op jit(solution)/shard_map/ppermute | solution.py:270
  70.2 0.5 collective-permute-start.24
  70.6 0.7 collective-permute-done.22
  71.4 0.9 collective-permute-start.28
  72.4 1.5 %collective-permute-start.26 = (bf16[64,2048]{1,0:T(8,128)(2,1)S(1)}, bf16[64,2048]{1,0:T(8,128)(2,1)S(1)}, u32[]{:S(2)}, u32[]{:S(2)}) collective-permute-start(bf16[64,2048]{1,0:T(8,128)(2,1)S(1)} %add_convert_fusion.7), channel_id=1, source_target_pairs={{2,6},{3,7},{6,10},{7,11},{10,14},{11,15},{14,12},{15,13},{12,8},{... | collective-permute-start | bytes 786440 | tf_op jit(solution)/shard_map/ppermute | solution.py:270
  73.8 4.0 %collective-permute-done.20 = bf16[64,2048]{1,0:T(8,128)(2,1)S(1)} collective-permute-done((bf16[64,2048]{1,0:T(8,128)(2,1)S(1)}, bf16[64,2048]{1,0:T(8,128)(2,1)S(1)}, u32[]{:S(2)}, u32[]{:S(2)}) %collective-permute-start.20) | collective-permute-done | bytes 262176 | tf_op jit(solution)/shard_map/ppermute | solution.py:270
  77.8 1.6 %collective-permute-done.24 = bf16[64,2048]{1,0:T(8,128)(2,1)S(1)} collective-permute-done((bf16[64,2048]{1,0:T(8,128)(2,1)S(1)}, bf16[64,2048]{1,0:T(8,128)(2,1)S(1)}, u32[]{:S(2)}, u32[]{:S(2)}) %collective-permute-start.24) | collective-permute-done | bytes 262176 | tf_op jit(solution)/shard_map/ppermute | solution.py:270
  79.5 0.5 collective-permute-start.25
  80.0 1.6 %collective-permute-start.23 = (bf16[64,2048]{1,0:T(8,128)(2,1)S(1)}, bf16[64,2048]{1,0:T(8,128)(2,1)S(1)}, u32[]{:S(2)}, u32[]{:S(2)}) collective-permute-start(bf16[64,2048]{1,0:T(8,128)(2,1)S(1)} %get-tuple-element.108), channel_id=1, source_target_pairs={{6,2},{7,3},{10,6},{11,7},{14,10},{15,11},{12,14},{13,15},{8,12},{... | collective-permute-start | bytes 786440 | tf_op jit(solution)/shard_map/ppermute | solution.py:270
  81.6 1.9 %collective-permute-done.28 = bf16[64,2048]{1,0:T(8,128)(2,1)S(1)} collective-permute-done((bf16[64,2048]{1,0:T(8,128)(2,1)S(1)}, bf16[64,2048]{1,0:T(8,128)(2,1)S(1)}, u32[]{:S(2)}, u32[]{:S(2)}) %collective-permute-start.28) | collective-permute-done | bytes 262176 | tf_op jit(solution)/shard_map/ppermute | solution.py:270
  83.5 0.9 collective-permute-start.30
  84.4 0.6 collective-permute-done.26
  85.1 0.6 collective-permute-start.27
  85.7 2.2 %collective-permute-done.25 = bf16[64,2048]{1,0:T(8,128)(2,1)S(1)} collective-permute-done((bf16[64,2048]{1,0:T(8,128)(2,1)S(1)}, bf16[64,2048]{1,0:T(8,128)(2,1)S(1)}, u32[]{:S(2)}, u32[]{:S(2)}) %collective-permute-start.25) | collective-permute-done | bytes 262176 | tf_op jit(solution)/shard_map/ppermute | solution.py:270
  88.0 3.5 %collective-permute-done.30 = bf16[64,2048]{1,0:T(8,128)(2,1)S(1)} collective-permute-done((bf16[64,2048]{1,0:T(8,128)(2,1)S(1)}, bf16[64,2048]{1,0:T(8,128)(2,1)S(1)}, u32[]{:S(2)}, u32[]{:S(2)}) %collective-permute-start.30) | collective-permute-done | bytes 262176 | tf_op jit(solution)/shard_map/ppermute | solution.py:270
  91.6 1.5 %collective-permute-start.31 = (bf16[64,2048]{1,0:T(8,128)(2,1)S(1)}, bf16[64,2048]{1,0:T(8,128)(2,1)S(1)}, u32[]{:S(2)}, u32[]{:S(2)}) collective-permute-start(bf16[64,2048]{1,0:T(8,128)(2,1)S(1)} %add_convert_fusion), channel_id=1, source_target_pairs={{6,2},{7,3},{10,6},{11,7},{14,10},{15,11},{12,14},{13,15},{8,12},{... | collective-permute-start | bytes 786440 | tf_op jit(solution)/shard_map/ppermute | solution.py:270
  93.1 0.8 collective-permute-done.27
  94.2 3.9 %collective-permute-done.31.total1_ref = bf16[64,2048]{1,0:T(8,128)(2,1)S(1)} collective-permute-done((bf16[64,2048]{1,0:T(8,128)(2,1)S(1)}, bf16[64,2048]{1,0:T(8,128)(2,1)S(1)}, u32[]{:S(2)}, u32[]{:S(2)}) %collective-permute-start.31) | collective-permute-done | bytes 262176 | tf_op jit(solution)/shard_map/ppermute | solution.py:270
  98.0 2.4 %collective-permute-done.29.total0_ref = bf16[64,2048]{1,0:T(8,128)(2,1)S(1)} collective-permute-done((bf16[64,2048]{1,0:T(8,128)(2,1)S(1)}, bf16[64,2048]{1,0:T(8,128)(2,1)S(1)}, u32[]{:S(2)}, u32[]{:S(2)}) %collective-permute-start.29) | collective-permute-done | bytes 262176 | tf_op jit(solution)/shard_map/ppermute | solution.py:270
  100.4 0.9 last_rows.1
  (38 shorter events, 1.3 us)
Async XLA Ops:
  0.0 23.6 %copy-start.1 = (bf16[1,1,768,2048]{3,2,1,0:T(8,128)(2,1)S(1)}, bf16[1,1,768,2048]{3,2,1,0:T(8,128)(2,1)}, u32[]{:S(2)}) copy-start(bf16[1,1,768,2048]{3,2,1,0:T(8,128)(2,1)} %param.13) | copy-start | bytes 9437188
  0.0 18.1 %collective-permute-start.2 = (bf16[2048,1536]{1,0:T(8,128)(2,1)}, bf16[2048,1536]{1,0:T(8,128)(2,1)S(1)}, u32[]{:S(2)}, u32[]{:S(2)}) collective-permute-start(bf16[2048,1536]{1,0:T(8,128)(2,1)} %bitcast.15), channel_id=1, source_target_pairs={{0,1},{1,0},{2,3},{3,2},{4,5},{5,4},{6,7},{7,6},{8,9},{9,8},{10,11... | collective-permute-start | bytes 18874376 | tf_op jit(solution)/shard_map/ppermute | solution.py:270
  0.5 17.7 %collective-permute-start.3 = (bf16[768,2048]{1,0:T(8,128)(2,1)}, bf16[768,2048]{1,0:T(8,128)(2,1)S(1)}, u32[]{:S(2)}, u32[]{:S(2)}) collective-permute-start(bf16[768,2048]{1,0:T(8,128)(2,1)} %bitcast.24), channel_id=1, source_target_pairs={{0,1},{1,0},{2,3},{3,2},{4,5},{5,4},{6,7},{7,6},{8,9},{9,8},{10,11... | collective-permute-start | bytes 9437192 | tf_op jit(solution)/shard_map/ppermute | solution.py:270
  1.8 11.5 %collective-permute-start = (bf16[64,2048]{1,0:T(8,128)(2,1)S(1)}, bf16[64,2048]{1,0:T(8,128)(2,1)S(1)}, u32[]{:S(2)}, u32[]{:S(2)}) collective-permute-start(bf16[64,2048]{1,0:T(8,128)(2,1)S(1)} %get-tuple-element.106), channel_id=1, source_target_pairs={{0,16},{1,17},{2,18},{3,19},{4,20},{5,21},{6,22},{7,23},{8,24},{9,... | collective-permute-start | bytes 786440 | tf_op jit(solution)/shard_map/ppermute | solution.py:20
  6.7 11.3 %collective-permute-start.1 = (bf16[64,2048]{1,0:T(8,128)(2,1)S(1)}, bf16[64,2048]{1,0:T(8,128)(2,1)S(1)}, u32[]{:S(2)}, u32[]{:S(2)}) collective-permute-start(bf16[64,2048]{1,0:T(8,128)(2,1)S(1)} %get-tuple-element.105), channel_id=1, source_target_pairs={{0,16},{1,17},{2,18},{3,19},{4,20},{5,21},{6,22},{7,23},{8,24},{9,... | collective-permute-start | bytes 786440 | tf_op jit(solution)/shard_map/ppermute | solution.py:20
  8.0 1.0 %copy-start.2 = (bf16[128,2048]{1,0:T(8,128)(2,1)S(1)}, bf16[128,2048]{1,0:T(8,128)(2,1)}, u32[]{:S(2)}) copy-start(bf16[128,2048]{1,0:T(8,128)(2,1)} %fresh_ref.1) | copy-start | bytes 1572868
  9.1 0.7 copy-start.3
  9.8 0.7 copy-start.4
  10.5 0.7 copy-start.5
  13.4 6.8 %collective-permute-start.4 = (bf16[1040,128]{1,0:T(8,128)(2,1)S(1)}, bf16[1040,128]{1,0:T(8,128)(2,1)S(1)}, u32[]{:S(2)}, u32[]{:S(2)}) collective-permute-start(bf16[1040,128]{1,0:T(8,128)(2,1)S(1)} %get-tuple-element.65.refs_0_), channel_id=1, source_target_pairs={{2,6},{3,7},{6,10},{7,11},{10,14},{11,15},{14,12},{15,13},{12,8},{... | collective-permute-start | bytes 798728 | tf_op jit(solution)/shard_map/ppermute | solution.py:270
  15.0 6.6 %collective-permute-start.5 = (bf16[1040,128]{1,0:T(8,128)(2,1)S(1)}, bf16[1040,128]{1,0:T(8,128)(2,1)S(1)}, u32[]{:S(2)}, u32[]{:S(2)}) collective-permute-start(bf16[1040,128]{1,0:T(8,128)(2,1)S(1)} %get-tuple-element.65.refs_0_), channel_id=1, source_target_pairs={{6,2},{7,3},{10,6},{11,7},{14,10},{15,11},{12,14},{13,15},{8,12},{... | collective-permute-start | bytes 798728 | tf_op jit(solution)/shard_map/ppermute | solution.py:270
  18.1 11.0 %collective-permute-start.8 = (bf16[1040,128]{1,0:T(8,128)(2,1)S(1)}, bf16[1040,128]{1,0:T(8,128)(2,1)S(1)}, u32[]{:S(2)}, u32[]{:S(2)}) collective-permute-start(bf16[1040,128]{1,0:T(8,128)(2,1)S(1)} %get-tuple-element.69.refs_1_), channel_id=1, source_target_pairs={{2,6},{3,7},{6,10},{7,11},{10,14},{11,15},{14,12},{15,13},{12,8},{... | collective-permute-start | bytes 798728 | tf_op jit(solution)/shard_map/ppermute | solution.py:270
  19.7 9.5 %collective-permute-start.9 = (bf16[1040,128]{1,0:T(8,128)(2,1)S(1)}, bf16[1040,128]{1,0:T(8,128)(2,1)S(1)}, u32[]{:S(2)}, u32[]{:S(2)}) collective-permute-start(bf16[1040,128]{1,0:T(8,128)(2,1)S(1)} %get-tuple-element.69.refs_1_), channel_id=1, source_target_pairs={{6,2},{7,3},{10,6},{11,7},{14,10},{15,11},{12,14},{13,15},{8,12},{... | collective-permute-start | bytes 798728 | tf_op jit(solution)/shard_map/ppermute | solution.py:270
  21.6 12.5 %collective-permute-start.6 = (bf16[1040,128]{1,0:T(8,128)(2,1)S(1)}, bf16[1040,128]{1,0:T(8,128)(2,1)S(1)}, u32[]{:S(2)}, u32[]{:S(2)}) collective-permute-start(bf16[1040,128]{1,0:T(8,128)(2,1)S(1)} %collective-permute-done.4.refs_0_), channel_id=1, source_target_pairs={{2,6},{3,7},{6,10},{7,11},{10,14},{11,15},{14,12},{15,13},{12,8},{... | collective-permute-start | bytes 798728 | tf_op jit(solution)/shard_map/ppermute | solution.py:270
  23.2 11.6 %collective-permute-start.7 = (bf16[1040,128]{1,0:T(8,128)(2,1)S(1)}, bf16[1040,128]{1,0:T(8,128)(2,1)S(1)}, u32[]{:S(2)}, u32[]{:S(2)}) collective-permute-start(bf16[1040,128]{1,0:T(8,128)(2,1)S(1)} %collective-permute-done.5.refs_1_), channel_id=1, source_target_pairs={{6,2},{7,3},{10,6},{11,7},{14,10},{15,11},{12,14},{13,15},{8,12},{... | collective-permute-start | bytes 798728 | tf_op jit(solution)/shard_map/ppermute | solution.py:270
  23.6 2.8 %copy-start = (bf16[1,1,2048,1536]{3,2,1,0:T(8,128)(2,1)S(1)}, bf16[1,1,2048,1536]{3,2,1,0:T(8,128)(2,1)}, u32[]{:S(2)}) copy-start(bf16[1,1,2048,1536]{3,2,1,0:T(8,128)(2,1)} %param.12) | copy-start | bytes 18874372
  29.2 10.3 %collective-permute-start.10 = (bf16[1040,128]{1,0:T(8,128)(2,1)S(1)}, bf16[1040,128]{1,0:T(8,128)(2,1)S(1)}, u32[]{:S(2)}, u32[]{:S(2)}) collective-permute-start(bf16[1040,128]{1,0:T(8,128)(2,1)S(1)} %collective-permute-done.8.refs_0_), channel_id=1, source_target_pairs={{2,6},{3,7},{6,10},{7,11},{10,14},{11,15},{14,12},{15,13},{12,8},{... | collective-permute-start | bytes 798728 | tf_op jit(solution)/shard_map/ppermute | solution.py:270
  30.8 9.6 %collective-permute-start.11 = (bf16[1040,128]{1,0:T(8,128)(2,1)S(1)}, bf16[1040,128]{1,0:T(8,128)(2,1)S(1)}, u32[]{:S(2)}, u32[]{:S(2)}) collective-permute-start(bf16[1040,128]{1,0:T(8,128)(2,1)S(1)} %collective-permute-done.9.refs_1_), channel_id=1, source_target_pairs={{6,2},{7,3},{10,6},{11,7},{14,10},{15,11},{12,14},{13,15},{8,12},{... | collective-permute-start | bytes 798728 | tf_op jit(solution)/shard_map/ppermute | solution.py:270
  34.7 10.5 %collective-permute-start.12 = (bf16[1040,128]{1,0:T(8,128)(2,1)S(1)}, bf16[1040,128]{1,0:T(8,128)(2,1)S(1)}, u32[]{:S(2)}, u32[]{:S(2)}) collective-permute-start(bf16[1040,128]{1,0:T(8,128)(2,1)S(1)} %collective-permute-done.6.refs_0_), channel_id=1, source_target_pairs={{2,6},{3,7},{6,10},{7,11},{10,14},{11,15},{14,12},{15,13},{12,8},{... | collective-permute-start | bytes 798728 | tf_op jit(solution)/shard_map/ppermute | solution.py:270
  36.3 9.8 %collective-permute-start.13 = (bf16[1040,128]{1,0:T(8,128)(2,1)S(1)}, bf16[1040,128]{1,0:T(8,128)(2,1)S(1)}, u32[]{:S(2)}, u32[]{:S(2)}) collective-permute-start(bf16[1040,128]{1,0:T(8,128)(2,1)S(1)} %collective-permute-done.7.refs_1_), channel_id=1, source_target_pairs={{6,2},{7,3},{10,6},{11,7},{14,10},{15,11},{12,14},{13,15},{8,12},{... | collective-permute-start | bytes 798728 | tf_op jit(solution)/shard_map/ppermute | solution.py:270
  40.4 10.0 %collective-permute-start.15 = (bf16[1040,128]{1,0:T(8,128)(2,1)S(1)}, bf16[1040,128]{1,0:T(8,128)(2,1)S(1)}, u32[]{:S(2)}, u32[]{:S(2)}) collective-permute-start(bf16[1040,128]{1,0:T(8,128)(2,1)S(1)} %collective-permute-done.10.refs_0_), channel_id=1, source_target_pairs={{2,6},{3,7},{6,10},{7,11},{10,14},{11,15},{14,12},{15,13},{12,8},{... | collective-permute-start | bytes 798728 | tf_op jit(solution)/shard_map/ppermute | solution.py:270
  42.0 8.5 %collective-permute-start.16 = (bf16[1040,128]{1,0:T(8,128)(2,1)S(1)}, bf16[1040,128]{1,0:T(8,128)(2,1)S(1)}, u32[]{:S(2)}, u32[]{:S(2)}) collective-permute-start(bf16[1040,128]{1,0:T(8,128)(2,1)S(1)} %collective-permute-done.11.refs_1_), channel_id=1, source_target_pairs={{6,2},{7,3},{10,6},{11,7},{14,10},{15,11},{12,14},{13,15},{8,12},{... | collective-permute-start | bytes 798728 | tf_op jit(solution)/shard_map/ppermute | solution.py:270
  46.1 10.7 %collective-permute-start.18 = (bf16[1040,128]{1,0:T(8,128)(2,1)S(1)}, bf16[1040,128]{1,0:T(8,128)(2,1)S(1)}, u32[]{:S(2)}, u32[]{:S(2)}) collective-permute-start(bf16[1040,128]{1,0:T(8,128)(2,1)S(1)} %collective-permute-done.12.refs_0_), channel_id=1, source_target_pairs={{2,6},{3,7},{6,10},{7,11},{10,14},{11,15},{14,12},{15,13},{12,8},{... | collective-permute-start | bytes 798728 | tf_op jit(solution)/shard_map/ppermute | solution.py:270
  50.5 8.7 %collective-permute-start.19 = (bf16[1040,128]{1,0:T(8,128)(2,1)S(1)}, bf16[1040,128]{1,0:T(8,128)(2,1)S(1)}, u32[]{:S(2)}, u32[]{:S(2)}) collective-permute-start(bf16[1040,128]{1,0:T(8,128)(2,1)S(1)} %collective-permute-done.16.refs_1_), channel_id=1, source_target_pairs={{6,2},{7,3},{10,6},{11,7},{14,10},{15,11},{12,14},{13,15},{8,12},{... | collective-permute-start | bytes 798728 | tf_op jit(solution)/shard_map/ppermute | solution.py:270
  52.0 12.9 %collective-permute-start.14 = (bf16[64,2048]{1,0:T(8,128)(2,1)S(1)}, bf16[64,2048]{1,0:T(8,128)(2,1)S(1)}, u32[]{:S(2)}, u32[]{:S(2)}) collective-permute-start(bf16[64,2048]{1,0:T(8,128)(2,1)S(1)} %convert_element_type.73), channel_id=1, source_target_pairs={{6,2},{7,3},{10,6},{11,7},{14,10},{15,11},{12,14},{13,15},{8,12},{... | collective-permute-start | bytes 786440 | tf_op jit(solution)/shard_map/ppermute | solution.py:270
  56.4 9.2 %collective-permute-start.17 = (bf16[64,2048]{1,0:T(8,128)(2,1)S(1)}, bf16[64,2048]{1,0:T(8,128)(2,1)S(1)}, u32[]{:S(2)}, u32[]{:S(2)}) collective-permute-start(bf16[64,2048]{1,0:T(8,128)(2,1)S(1)} %convert_element_type.74), channel_id=1, source_target_pairs={{2,6},{3,7},{6,10},{7,11},{10,14},{11,15},{14,12},{15,13},{12,8},{... | collective-permute-start | bytes 786440 | tf_op jit(solution)/shard_map/ppermute | solution.py:270
  62.1 9.3 %collective-permute-start.22 = (bf16[64,2048]{1,0:T(8,128)(2,1)S(1)}, bf16[64,2048]{1,0:T(8,128)(2,1)S(1)}, u32[]{:S(2)}, u32[]{:S(2)}) collective-permute-start(bf16[64,2048]{1,0:T(8,128)(2,1)S(1)} %convert_element_type.78), channel_id=1, source_target_pairs={{6,2},{7,3},{10,6},{11,7},{14,10},{15,11},{12,14},{13,15},{8,12},{... | collective-permute-start | bytes 786440 | tf_op jit(solution)/shard_map/ppermute | solution.py:270
  62.7 9.6 %collective-permute-start.21 = (bf16[64,2048]{1,0:T(8,128)(2,1)S(1)}, bf16[64,2048]{1,0:T(8,128)(2,1)S(1)}, u32[]{:S(2)}, u32[]{:S(2)}) collective-permute-start(bf16[64,2048]{1,0:T(8,128)(2,1)S(1)} %convert_element_type.75), channel_id=1, source_target_pairs={{2,6},{3,7},{6,10},{7,11},{10,14},{11,15},{14,12},{15,13},{12,8},{... | collective-permute-start | bytes 786440 | tf_op jit(solution)/shard_map/ppermute | solution.py:270
  68.5 9.3 %collective-permute-start.20 = (bf16[64,2048]{1,0:T(8,128)(2,1)S(1)}, bf16[64,2048]{1,0:T(8,128)(2,1)S(1)}, u32[]{:S(2)}, u32[]{:S(2)}) collective-permute-start(bf16[64,2048]{1,0:T(8,128)(2,1)S(1)} %get-tuple-element.88), channel_id=1, source_target_pairs={{6,2},{7,3},{10,6},{11,7},{14,10},{15,11},{12,14},{13,15},{8,12},{... | collective-permute-start | bytes 786440 | tf_op jit(solution)/shard_map/ppermute | solution.py:270
  70.2 9.2 %collective-permute-start.24 = (bf16[64,2048]{1,0:T(8,128)(2,1)S(1)}, bf16[64,2048]{1,0:T(8,128)(2,1)S(1)}, u32[]{:S(2)}, u32[]{:S(2)}) collective-permute-start(bf16[64,2048]{1,0:T(8,128)(2,1)S(1)} %get-tuple-element.95), channel_id=1, source_target_pairs={{2,6},{3,7},{6,10},{7,11},{10,14},{11,15},{14,12},{15,13},{12,8},{... | collective-permute-start | bytes 786440 | tf_op jit(solution)/shard_map/ppermute | solution.py:270
  71.4 12.0 %collective-permute-start.28 = (bf16[64,2048]{1,0:T(8,128)(2,1)S(1)}, bf16[64,2048]{1,0:T(8,128)(2,1)S(1)}, u32[]{:S(2)}, u32[]{:S(2)}) collective-permute-start(bf16[64,2048]{1,0:T(8,128)(2,1)S(1)} %add_convert_fusion.6), channel_id=1, source_target_pairs={{6,2},{7,3},{10,6},{11,7},{14,10},{15,11},{12,14},{13,15},{8,12},{... | collective-permute-start | bytes 786440 | tf_op jit(solution)/shard_map/ppermute | solution.py:270
  72.4 12.7 %collective-permute-start.26 = (bf16[64,2048]{1,0:T(8,128)(2,1)S(1)}, bf16[64,2048]{1,0:T(8,128)(2,1)S(1)}, u32[]{:S(2)}, u32[]{:S(2)}) collective-permute-start(bf16[64,2048]{1,0:T(8,128)(2,1)S(1)} %add_convert_fusion.7), channel_id=1, source_target_pairs={{2,6},{3,7},{6,10},{7,11},{10,14},{11,15},{14,12},{15,13},{12,8},{... | collective-permute-start | bytes 786440 | tf_op jit(solution)/shard_map/ppermute | solution.py:270
  79.5 8.4 %collective-permute-start.25 = (bf16[64,2048]{1,0:T(8,128)(2,1)S(1)}, bf16[64,2048]{1,0:T(8,128)(2,1)S(1)}, u32[]{:S(2)}, u32[]{:S(2)}) collective-permute-start(bf16[64,2048]{1,0:T(8,128)(2,1)S(1)} %get-tuple-element.107), channel_id=1, source_target_pairs={{2,6},{3,7},{6,10},{7,11},{10,14},{11,15},{14,12},{15,13},{12,8},{... | collective-permute-start | bytes 786440 | tf_op jit(solution)/shard_map/ppermute | solution.py:270
  80.0 14.0 %collective-permute-start.23 = (bf16[64,2048]{1,0:T(8,128)(2,1)S(1)}, bf16[64,2048]{1,0:T(8,128)(2,1)S(1)}, u32[]{:S(2)}, u32[]{:S(2)}) collective-permute-start(bf16[64,2048]{1,0:T(8,128)(2,1)S(1)} %get-tuple-element.108), channel_id=1, source_target_pairs={{6,2},{7,3},{10,6},{11,7},{14,10},{15,11},{12,14},{13,15},{8,12},{... | collective-permute-start | bytes 786440 | tf_op jit(solution)/shard_map/ppermute | solution.py:270
  83.5 8.0 %collective-permute-start.30 = (bf16[64,2048]{1,0:T(8,128)(2,1)S(1)}, bf16[64,2048]{1,0:T(8,128)(2,1)S(1)}, u32[]{:S(2)}, u32[]{:S(2)}) collective-permute-start(bf16[64,2048]{1,0:T(8,128)(2,1)S(1)} %add_convert_fusion.2), channel_id=1, source_target_pairs={{6,2},{7,3},{10,6},{11,7},{14,10},{15,11},{12,14},{13,15},{8,12},{... | collective-permute-start | bytes 786440 | tf_op jit(solution)/shard_map/ppermute | solution.py:270
  85.1 8.9 %collective-permute-start.27 = (bf16[64,2048]{1,0:T(8,128)(2,1)S(1)}, bf16[64,2048]{1,0:T(8,128)(2,1)S(1)}, u32[]{:S(2)}, u32[]{:S(2)}) collective-permute-start(bf16[64,2048]{1,0:T(8,128)(2,1)S(1)} %add_convert_fusion.3), channel_id=1, source_target_pairs={{2,6},{3,7},{6,10},{7,11},{10,14},{11,15},{14,12},{15,13},{12,8},{... | collective-permute-start | bytes 786440 | tf_op jit(solution)/shard_map/ppermute | solution.py:270
  91.6 6.4 %collective-permute-start.31 = (bf16[64,2048]{1,0:T(8,128)(2,1)S(1)}, bf16[64,2048]{1,0:T(8,128)(2,1)S(1)}, u32[]{:S(2)}, u32[]{:S(2)}) collective-permute-start(bf16[64,2048]{1,0:T(8,128)(2,1)S(1)} %add_convert_fusion), channel_id=1, source_target_pairs={{6,2},{7,3},{10,6},{11,7},{14,10},{15,11},{12,14},{13,15},{8,12},{... | collective-permute-start | bytes 786440 | tf_op jit(solution)/shard_map/ppermute | solution.py:270
  94.0 6.4 %collective-permute-start.29 = (bf16[64,2048]{1,0:T(8,128)(2,1)S(1)}, bf16[64,2048]{1,0:T(8,128)(2,1)S(1)}, u32[]{:S(2)}, u32[]{:S(2)}) collective-permute-start(bf16[64,2048]{1,0:T(8,128)(2,1)S(1)} %add_convert_fusion.1), channel_id=1, source_target_pairs={{2,6},{3,7},{6,10},{7,11},{10,14},{11,15},{14,12},{15,13},{12,8},{... | collective-permute-start | bytes 786440 | tf_op jit(solution)/shard_map/ppermute | solution.py:270

commit v11 on v10

--- a/solution.py
+++ b/solution.py
@@ -324,9 +324,9 @@
     short_totals = [move(total, flow[2]) for total, flow in zip((down_sum, up_sum), short)]
     after = None
     for s in reversed(range(1, hops)):
+        sent, long_totals = zip(*(send_on(f, s, t, None) for f, t in zip(long, long_totals)))
         if 1 < s < hops - 1:
-            after, short_totals = zip(*(send_on(f, s - 1, t, after) for f, t in zip(short, short_totals)))
-        after, long_totals = zip(*(send_on(f, s, t, after) for f, t in zip(long, long_totals)))
+            short_totals = [send_on(f, s - 1, t, sent)[1] for f, t in zip(short, short_totals)]
 
     nears = [
         arrival[c].astype(jnp.float32) + (own_sums[c] + short_totals[c].astype(jnp.float32)) for c in range(2)

time: 102 us -> 99.1 us (0.972)
  waiting for transfers between devices: 33.5 us -> 29.8 us
  starting transfers between devices: 36.1 us -> 37.4 us
    ppermute x30, waiting for transfers between devices: 29 us -> 25.3 us  [move(): return lax.ppermute(value, 'expert', pairs)]
    ppermute x30, starting transfers between devices: 29.9 us -> 31.2 us  [move(): return lax.ppermute(value, 'expert', pairs)]
  transfers between devices with their start and end apart: 32 -> 32, of which waited for: 19 -> 15; matrix products, arithmetic and copies ran while one was open for 2% -> 2% of each run, Pallas kernels for 22% -> 23%
where the time goes in v11:
time: 99.1 us; the launch traced here: 98.8 us
  starting transfers between devices  37.4 us (38%)
  waiting for transfers between devices  29.8 us (30%)
  Pallas kernels  23.4 us (24%)
  local copies, waits for them, and re-layouts  7.22 us (7%)
    ppermute x30, starting transfers between devices, move(): return lax.ppermute(value, 'expert', pairs)  31.2 us
    ppermute x30, waiting for transfers between devices, move(): return lax.ppermute(value, 'expert', pairs)  25.3 us
    pallas_call x8, Pallas kernels, expert_rows(): pl.pallas_call(functools.partial(mlp_kernel, parts=len(payloads), adds=le...  22.2 us
    ppermute x2, starting transfers between devices, from_behind(): return lax.ppermute(value, axis, pairs)  6.18 us
    unnamed x12, local copies, waits for them, and re-layouts  5.89 us
    ppermute x2, waiting for transfers between devices, from_behind(): return lax.ppermute(value, axis, pairs)  4.5 us
  transfers between devices with their start and end apart: 32, of which 15 were waited for; matrix products, arithmetic and copies ran while one was open for 2% of the time, Pallas kernels for 23%

profile of v11, /device:TPU:0, one launch (start us, length us, event | category | flops | bytes accessed | tf_op | source)
XLA Modules:
  0.0 98.8 jit_solution(12947512142322591817)
XLA Ops:
  0.0 0.5 collective-permute-start.2
  0.5 1.3 %slice_bitcast_fusion = (bf16[64,2048]{1,0:T(8,128)(2,1)S(1)}, bf16[64,2048]{1,0:T(8,128)(2,1)S(1)}) fusion(bf16[1,128,2048]{2,1,0:T(8,128)(2,1)} %param.8), kind=kLoop, calls=%fused_computation.10 | loop fusion | bytes 1048576 | tf_op jit(solution)/shard_map/squeeze | solution.py:277
  1.9 4.9 %collective-permute-start = (bf16[64,2048]{1,0:T(8,128)(2,1)S(1)}, bf16[64,2048]{1,0:T(8,128)(2,1)S(1)}, u32[]{:S(2)}, u32[]{:S(2)}) collective-permute-start(bf16[64,2048]{1,0:T(8,128)(2,1)S(1)} %get-tuple-element.98), channel_id=1, source_target_pairs={{0,16},{1,17},{2,18},{3,19},{4,20},{5,21},{6,22},{7,23},{8,24},{9,... | collective-permute-start | bytes 786440 | tf_op jit(solution)/shard_map/ppermute | solution.py:20
  6.7 1.3 %collective-permute-start.1 = (bf16[64,2048]{1,0:T(8,128)(2,1)S(1)}, bf16[64,2048]{1,0:T(8,128)(2,1)S(1)}, u32[]{:S(2)}, u32[]{:S(2)}) collective-permute-start(bf16[64,2048]{1,0:T(8,128)(2,1)S(1)} %get-tuple-element.97), channel_id=1, source_target_pairs={{0,16},{1,17},{2,18},{3,19},{4,20},{5,21},{6,22},{7,23},{8,24},{9,... | collective-permute-start | bytes 786440 | tf_op jit(solution)/shard_map/ppermute | solution.py:20
  8.1 1.0 %copy-done.2 = bf16[128,2048]{1,0:T(8,128)(2,1)S(1)} copy-done((bf16[128,2048]{1,0:T(8,128)(2,1)S(1)}, bf16[128,2048]{1,0:T(8,128)(2,1)}, u32[]{:S(2)}) %copy-start.2) | copy-done | bytes 524312
  9.1 0.7 copy-done.3
  9.8 0.7 copy-done.4
  10.5 0.7 copy-done.5
  11.2 0.2 base_rows.1
  11.4 2.0 %collective-permute-done.arrived_ref = bf16[64,2048]{1,0:T(8,128)(2,1)S(1)} collective-permute-done((bf16[64,2048]{1,0:T(8,128)(2,1)S(1)}, bf16[64,2048]{1,0:T(8,128)(2,1)S(1)}, u32[]{:S(2)}, u32[]{:S(2)}) %collective-permute-start) | collective-permute-done | bytes 262176 | tf_op jit(solution)/shard_map/ppermute | solution.py:20
  13.5 1.5 %collective-permute-start.4 = (bf16[1040,128]{1,0:T(8,128)(2,1)S(1)}, bf16[1040,128]{1,0:T(8,128)(2,1)S(1)}, u32[]{:S(2)}, u32[]{:S(2)}) collective-permute-start(bf16[1040,128]{1,0:T(8,128)(2,1)S(1)} %get-tuple-element.61.refs_0_), channel_id=1, source_target_pairs={{2,6},{3,7},{6,10},{7,11},{10,14},{11,15},{14,12},{15,13},{12,8},{... | collective-permute-start | bytes 798728 | tf_op jit(solution)/shard_map/ppermute | solution.py:270
  15.0 0.5 collective-permute-start.5
  15.5 2.5 %collective-permute-done.1.arrived_ref = bf16[64,2048]{1,0:T(8,128)(2,1)S(1)} collective-permute-done((bf16[64,2048]{1,0:T(8,128)(2,1)S(1)}, bf16[64,2048]{1,0:T(8,128)(2,1)S(1)}, u32[]{:S(2)}, u32[]{:S(2)}) %collective-permute-start.1) | collective-permute-done | bytes 262176 | tf_op jit(solution)/shard_map/ppermute | solution.py:20
  18.2 1.5 %collective-permute-start.8 = (bf16[1040,128]{1,0:T(8,128)(2,1)S(1)}, bf16[1040,128]{1,0:T(8,128)(2,1)S(1)}, u32[]{:S(2)}, u32[]{:S(2)}) collective-permute-start(bf16[1040,128]{1,0:T(8,128)(2,1)S(1)} %get-tuple-element.65.refs_1_), channel_id=1, source_target_pairs={{2,6},{3,7},{6,10},{7,11},{10,14},{11,15},{14,12},{15,13},{12,8},{... | collective-permute-start | bytes 798728 | tf_op jit(solution)/shard_map/ppermute | solution.py:270
  19.7 0.5 collective-permute-start.9
  20.2 1.3 %collective-permute-done.5.refs_1_ = bf16[1040,128]{1,0:T(8,128)(2,1)S(1)} collective-permute-done((bf16[1040,128]{1,0:T(8,128)(2,1)S(1)}, bf16[1040,128]{1,0:T(8,128)(2,1)S(1)}, u32[]{:S(2)}, u32[]{:S(2)}) %collective-permute-start.5) | collective-permute-done | bytes 266272 | tf_op jit(solution)/shard_map/ppermute | solution.py:270
  21.6 1.6 %collective-permute-start.6 = (bf16[1040,128]{1,0:T(8,128)(2,1)S(1)}, bf16[1040,128]{1,0:T(8,128)(2,1)S(1)}, u32[]{:S(2)}, u32[]{:S(2)}) collective-permute-start(bf16[1040,128]{1,0:T(8,128)(2,1)S(1)} %collective-permute-done.4.refs_0_), channel_id=1, source_target_pairs={{2,6},{3,7},{6,10},{7,11},{10,14},{11,15},{14,12},{15,13},{12,8},{... | collective-permute-start | bytes 798728 | tf_op jit(solution)/shard_map/ppermute | solution.py:270
  23.2 0.4 collective-permute-start.7
  23.6 2.8 %copy-done = bf16[1,1,2048,1536]{3,2,1,0:T(8,128)(2,1)S(1)} copy-done((bf16[1,1,2048,1536]{3,2,1,0:T(8,128)(2,1)S(1)}, bf16[1,1,2048,1536]{3,2,1,0:T(8,128)(2,1)}, u32[]{:S(2)}) %copy-start) | copy-done | bytes 6291480
  26.4 2.8 %expert_rows.8 = (f32[64,2048]{1,0:T(8,128)S(1)}, f32[64,2048]{1,0:T(8,128)S(1)}) custom-call(s32[1]{0:T(128)} %bitcast.6.expert_ref, bf16[1040,128]{1,0:T(8,128)(2,1)S(1)} %collective-permute-done.4.refs_0_, bf16[1040,128]{1,0:T(8,128)(2,1)S(1)} %collective-permute-done.5.refs_1_, bf16[2048,1536]{1,0:T(8,128)(2,1)S(1)} %bitcast.16, ...), custom_call_target="tpu_custom_call" | custom-call | flops 2415919104 | bytes 1572864 | tf_op jit(solution)/shard_map/expert_rows/pallas_call | solution.py:204
  29.2 1.6 %collective-permute-start.10 = (bf16[1040,128]{1,0:T(8,128)(2,1)S(1)}, bf16[1040,128]{1,0:T(8,128)(2,1)S(1)}, u32[]{:S(2)}, u32[]{:S(2)}) collective-permute-start(bf16[1040,128]{1,0:T(8,128)(2,1)S(1)} %collective-permute-done.8.refs_0_), channel_id=1, source_target_pairs={{2,6},{3,7},{6,10},{7,11},{10,14},{11,15},{14,12},{15,13},{12,8},{... | collective-permute-start | bytes 798728 | tf_op jit(solution)/shard_map/ppermute | solution.py:270
  30.8 0.5 collective-permute-start.11
  31.3 2.8 %expert_rows.9 = (f32[64,2048]{1,0:T(8,128)S(1)}, f32[64,2048]{1,0:T(8,128)S(1)}) custom-call(s32[1]{0:T(128)} %bitcast.6.expert_ref, bf16[1040,128]{1,0:T(8,128)(2,1)S(1)} %collective-permute-done.8.refs_0_, bf16[1040,128]{1,0:T(8,128)(2,1)S(1)} %collective-permute-done.9.refs_1_, bf16[2048,1536]{1,0:T(8,128)(2,1)S(1)} %bitcast.17, ...), custom_call_target="tpu_custom_call" | custom-call | flops 2415919104 | bytes 1572864 | tf_op jit(solution)/shard_map/expert_rows/pallas_call | solution.py:204
  34.0 0.7 collective-permute-done.7.refs_1_
  34.7 1.6 %collective-permute-start.12 = (bf16[1040,128]{1,0:T(8,128)(2,1)S(1)}, bf16[1040,128]{1,0:T(8,128)(2,1)S(1)}, u32[]{:S(2)}, u32[]{:S(2)}) collective-permute-start(bf16[1040,128]{1,0:T(8,128)(2,1)S(1)} %collective-permute-done.6.refs_0_), channel_id=1, source_target_pairs={{2,6},{3,7},{6,10},{7,11},{10,14},{11,15},{14,12},{15,13},{12,8},{... | collective-permute-start | bytes 798728 | tf_op jit(solution)/shard_map/ppermute | solution.py:270
  36.3 0.4 collective-permute-start.13
  36.8 2.8 %expert_rows.10 = (f32[64,2048]{1,0:T(8,128)S(1)}, f32[64,2048]{1,0:T(8,128)S(1)}) custom-call(s32[1]{0:T(128)} %bitcast.6.expert_ref, bf16[1040,128]{1,0:T(8,128)(2,1)S(1)} %collective-permute-done.6.refs_0_, bf16[1040,128]{1,0:T(8,128)(2,1)S(1)} %collective-permute-done.7.refs_1_, bf16[2048,1536]{1,0:T(8,128)(2,1)S(1)} %bitcast.18, ...), custom_call_target="tpu_custom_call" | custom-call | flops 2415919104 | bytes 1572864 | tf_op jit(solution)/shard_map/expert_rows/pallas_call | solution.py:204
  39.5 0.9 collective-permute-done.11.refs_1_
  40.5 1.6 %collective-permute-start.15 = (bf16[1040,128]{1,0:T(8,128)(2,1)S(1)}, bf16[1040,128]{1,0:T(8,128)(2,1)S(1)}, u32[]{:S(2)}, u32[]{:S(2)}) collective-permute-start(bf16[1040,128]{1,0:T(8,128)(2,1)S(1)} %collective-permute-done.10.refs_0_), channel_id=1, source_target_pairs={{2,6},{3,7},{6,10},{7,11},{10,14},{11,15},{14,12},{15,13},{12,8},{... | collective-permute-start | bytes 798728 | tf_op jit(solution)/shard_map/ppermute | solution.py:270
  42.0 0.5 collective-permute-start.16
  42.5 2.7 %expert_rows.11 = (f32[64,2048]{1,0:T(8,128)S(1)}, f32[64,2048]{1,0:T(8,128)S(1)}) custom-call(s32[1]{0:T(128)} %bitcast.6.expert_ref, bf16[1040,128]{1,0:T(8,128)(2,1)S(1)} %collective-permute-done.10.refs_0_, bf16[1040,128]{1,0:T(8,128)(2,1)S(1)} %collective-permute-done.11.refs_1_, bf16[2048,1536]{1,0:T(8,128)(2,1)S(1)} %bitcast.19, ...), custom_call_target="tpu_custom_call" | custom-call | flops 2415919104 | bytes 1572864 | tf_op jit(solution)/shard_map/expert_rows/pallas_call | solution.py:204
  45.2 0.9 collective-permute-done.13.refs_1_
  46.2 1.6 %collective-permute-start.18 = (bf16[1040,128]{1,0:T(8,128)(2,1)S(1)}, bf16[1040,128]{1,0:T(8,128)(2,1)S(1)}, u32[]{:S(2)}, u32[]{:S(2)}) collective-permute-start(bf16[1040,128]{1,0:T(8,128)(2,1)S(1)} %collective-permute-done.12.refs_0_), channel_id=1, source_target_pairs={{2,6},{3,7},{6,10},{7,11},{10,14},{11,15},{14,12},{15,13},{12,8},{... | collective-permute-start | bytes 798728 | tf_op jit(solution)/shard_map/ppermute | solution.py:270
  47.7 2.7 %expert_rows.12 = (f32[64,2048]{1,0:T(8,128)S(1)}, f32[64,2048]{1,0:T(8,128)S(1)}) custom-call(s32[1]{0:T(128)} %bitcast.6.expert_ref, bf16[1040,128]{1,0:T(8,128)(2,1)S(1)} %collective-permute-done.12.refs_0_, bf16[1040,128]{1,0:T(8,128)(2,1)S(1)} %collective-permute-done.13.refs_1_, bf16[2048,1536]{1,0:T(8,128)(2,1)S(1)} %bitcast.20, ...), custom_call_target="tpu_custom_call" | custom-call | flops 2415919104 | bytes 1572864 | tf_op jit(solution)/shard_map/expert_rows/pallas_call | solution.py:204
  50.5 1.4 %collective-permute-start.19 = (bf16[1040,128]{1,0:T(8,128)(2,1)S(1)}, bf16[1040,128]{1,0:T(8,128)(2,1)S(1)}, u32[]{:S(2)}, u32[]{:S(2)}) collective-permute-start(bf16[1040,128]{1,0:T(8,128)(2,1)S(1)} %collective-permute-done.16.refs_1_), channel_id=1, source_target_pairs={{6,2},{7,3},{10,6},{11,7},{14,10},{15,11},{12,14},{13,15},{8,12},{... | collective-permute-start | bytes 798728 | tf_op jit(solution)/shard_map/ppermute | solution.py:270
  52.0 1.6 %collective-permute-start.14 = (bf16[64,2048]{1,0:T(8,128)(2,1)S(1)}, bf16[64,2048]{1,0:T(8,128)(2,1)S(1)}, u32[]{:S(2)}, u32[]{:S(2)}) collective-permute-start(bf16[64,2048]{1,0:T(8,128)(2,1)S(1)} %convert_element_type.73), channel_id=1, source_target_pairs={{6,2},{7,3},{10,6},{11,7},{14,10},{15,11},{12,14},{13,15},{8,12},{... | collective-permute-start | bytes 786440 | tf_op jit(solution)/shard_map/ppermute | solution.py:270
  53.6 2.8 %expert_rows.13 = (f32[64,2048]{1,0:T(8,128)S(1)}, f32[64,2048]{1,0:T(8,128)S(1)}) custom-call(s32[1]{0:T(128)} %bitcast.6.expert_ref, bf16[1040,128]{1,0:T(8,128)(2,1)S(1)} %collective-permute-done.15.refs_0_, bf16[1040,128]{1,0:T(8,128)(2,1)S(1)} %collective-permute-done.16.refs_1_, bf16[2048,1536]{1,0:T(8,128)(2,1)S(1)} %bitcast.21, ...), custom_call_target="tpu_custom_call" | custom-call | flops 2415919104 | bytes 1572864 | tf_op jit(solution)/shard_map/expert_rows/pallas_call | solution.py:204
  56.4 0.5 collective-permute-start.17
  56.9 2.4 %collective-permute-done.19.refs_1_ = bf16[1040,128]{1,0:T(8,128)(2,1)S(1)} collective-permute-done((bf16[1040,128]{1,0:T(8,128)(2,1)S(1)}, bf16[1040,128]{1,0:T(8,128)(2,1)S(1)}, u32[]{:S(2)}, u32[]{:S(2)}) %collective-permute-start.19) | collective-permute-done | bytes 266272 | tf_op jit(solution)/shard_map/ppermute | solution.py:270
  59.3 2.8 %expert_rows.14 = (f32[64,2048]{1,0:T(8,128)S(1)}, f32[64,2048]{1,0:T(8,128)S(1)}) custom-call(s32[1]{0:T(128)} %bitcast.6.expert_ref, bf16[1040,128]{1,0:T(8,128)(2,1)S(1)} %collective-permute-done.18.refs_0_, bf16[1040,128]{1,0:T(8,128)(2,1)S(1)} %collective-permute-done.19.refs_1_, bf16[2048,1536]{1,0:T(8,128)(2,1)S(1)} %bitcast.22, ...), custom_call_target="tpu_custom_call" | custom-call | flops 2415919104 | bytes 1572864 | tf_op jit(solution)/shard_map/expert_rows/pallas_call | solution.py:204
  62.1 0.6 collective-permute-start.23
  62.7 1.8 %collective-permute-start.21 = (bf16[64,2048]{1,0:T(8,128)(2,1)S(1)}, bf16[64,2048]{1,0:T(8,128)(2,1)S(1)}, u32[]{:S(2)}, u32[]{:S(2)}) collective-permute-start(bf16[64,2048]{1,0:T(8,128)(2,1)S(1)} %convert_element_type.75), channel_id=1, source_target_pairs={{2,6},{3,7},{6,10},{7,11},{10,14},{11,15},{14,12},{15,13},{12,8},{... | collective-permute-start | bytes 786440 | tf_op jit(solution)/shard_map/ppermute | solution.py:270
  64.5 0.4 collective-permute-done.14.refs_8_
  64.9 0.8 collective-permute-done.17.refs_9_
  65.6 2.9 %expert_rows.15 = (f32[64,2048]{1,0:T(8,128)S(1)}, f32[64,2048]{1,0:T(8,128)S(1)}, bf16[64,2048]{1,0:T(8,128)(2,1)S(1)}, bf16[64,2048]{1,0:T(8,128)(2,1)S(1)}) custom-call(s32[1]{0:T(128)} %bitcast.6.expert_ref, bf16[1040,128]{1,0:T(8,128)(2,1)S(1)} %get-tuple-element.61.refs_0_, bf16[1040,128]{1,0:T(8,128)(2,1)S(1)} %get-tuple-element.65.refs_1_, ...), custom_call_target="tpu_custom_call" | custom-call | flops 2415919104 | bytes 1572864 | tf_op jit(solution)/shard_map/expert_rows/pallas_call | solution.py:204
  68.5 0.9 collective-permute-start.26
  69.4 1.2 %collective-permute-start.20 = (bf16[64,2048]{1,0:T(8,128)(2,1)S(1)}, bf16[64,2048]{1,0:T(8,128)(2,1)S(1)}, u32[]{:S(2)}, u32[]{:S(2)}) collective-permute-start(bf16[64,2048]{1,0:T(8,128)(2,1)S(1)} %get-tuple-element.84), channel_id=1, source_target_pairs={{6,2},{7,3},{10,6},{11,7},{14,10},{15,11},{12,14},{13,15},{8,12},{... | collective-permute-start | bytes 786440 | tf_op jit(solution)/shard_map/ppermute | solution.py:270
  70.6 0.7 collective-permute-done.23
  71.4 0.9 collective-permute-start.24
  72.4 1.4 %collective-permute-start.22 = (bf16[64,2048]{1,0:T(8,128)(2,1)S(1)}, bf16[64,2048]{1,0:T(8,128)(2,1)S(1)}, u32[]{:S(2)}, u32[]{:S(2)}) collective-permute-start(bf16[64,2048]{1,0:T(8,128)(2,1)S(1)} %add_convert_fusion.7), channel_id=1, source_target_pairs={{2,6},{3,7},{6,10},{7,11},{10,14},{11,15},{14,12},{15,13},{12,8},{... | collective-permute-start | bytes 786440 | tf_op jit(solution)/shard_map/ppermute | solution.py:270
  73.8 7.5 %collective-permute-done.24 = bf16[64,2048]{1,0:T(8,128)(2,1)S(1)} collective-permute-done((bf16[64,2048]{1,0:T(8,128)(2,1)S(1)}, bf16[64,2048]{1,0:T(8,128)(2,1)S(1)}, u32[]{:S(2)}, u32[]{:S(2)}) %collective-permute-start.24) | collective-permute-done | bytes 262176 | tf_op jit(solution)/shard_map/ppermute | solution.py:270
  81.4 0.8 collective-permute-start.30
  82.2 1.4 %collective-permute-start.28 = (bf16[64,2048]{1,0:T(8,128)(2,1)S(1)}, bf16[64,2048]{1,0:T(8,128)(2,1)S(1)}, u32[]{:S(2)}, u32[]{:S(2)}) collective-permute-start(bf16[64,2048]{1,0:T(8,128)(2,1)S(1)} %add_convert_fusion.6), channel_id=1, source_target_pairs={{2,6},{3,7},{6,10},{7,11},{10,14},{11,15},{14,12},{15,13},{12,8},{... | collective-permute-start | bytes 786440 | tf_op jit(solution)/shard_map/ppermute | solution.py:270
  83.6 1.7 %collective-permute-start.27 = (bf16[64,2048]{1,0:T(8,128)(2,1)S(1)}, bf16[64,2048]{1,0:T(8,128)(2,1)S(1)}, u32[]{:S(2)}, u32[]{:S(2)}) collective-permute-start(bf16[64,2048]{1,0:T(8,128)(2,1)S(1)} %add_convert_fusion.2), channel_id=1, source_target_pairs={{2,6},{3,7},{6,10},{7,11},{10,14},{11,15},{14,12},{15,13},{12,8},{... | collective-permute-start | bytes 786440 | tf_op jit(solution)/shard_map/ppermute | solution.py:270
  85.4 0.4 collective-permute-start.25
  85.8 4.8 %collective-permute-done.30 = bf16[64,2048]{1,0:T(8,128)(2,1)S(1)} collective-permute-done((bf16[64,2048]{1,0:T(8,128)(2,1)S(1)}, bf16[64,2048]{1,0:T(8,128)(2,1)S(1)}, u32[]{:S(2)}, u32[]{:S(2)}) %collective-permute-start.30) | collective-permute-done | bytes 262176 | tf_op jit(solution)/shard_map/ppermute | solution.py:270
  90.7 0.7 collective-permute-start.31
  91.5 1.4 %collective-permute-start.29 = (bf16[64,2048]{1,0:T(8,128)(2,1)S(1)}, bf16[64,2048]{1,0:T(8,128)(2,1)S(1)}, u32[]{:S(2)}, u32[]{:S(2)}) collective-permute-start(bf16[64,2048]{1,0:T(8,128)(2,1)S(1)} %add_convert_fusion.1), channel_id=1, source_target_pairs={{2,6},{3,7},{6,10},{7,11},{10,14},{11,15},{14,12},{15,13},{12,8},{... | collective-permute-start | bytes 786440 | tf_op jit(solution)/shard_map/ppermute | solution.py:270
  92.9 0.8 collective-permute-done.27
  93.7 0.1 add_add_fusion.near1_ref
  93.8 0.1 add_add_fusion.1.near0_ref
  93.9 3.3 %collective-permute-done.31.total1_ref = bf16[64,2048]{1,0:T(8,128)(2,1)S(1)} collective-permute-done((bf16[64,2048]{1,0:T(8,128)(2,1)S(1)}, bf16[64,2048]{1,0:T(8,128)(2,1)S(1)}, u32[]{:S(2)}, u32[]{:S(2)}) %collective-permute-start.31) | collective-permute-done | bytes 262176 | tf_op jit(solution)/shard_map/ppermute | solution.py:270
  97.1 0.8 collective-permute-done.29.total0_ref
  97.9 0.9 last_rows.1
  (39 shorter events, 0.8 us)
Async XLA Ops:
  0.0 23.6 %copy-start.1 = (bf16[1,1,768,2048]{3,2,1,0:T(8,128)(2,1)S(1)}, bf16[1,1,768,2048]{3,2,1,0:T(8,128)(2,1)}, u32[]{:S(2)}) copy-start(bf16[1,1,768,2048]{3,2,1,0:T(8,128)(2,1)} %param.13) | copy-start | bytes 9437188
  0.0 18.1 %collective-permute-start.2 = (bf16[2048,1536]{1,0:T(8,128)(2,1)}, bf16[2048,1536]{1,0:T(8,128)(2,1)S(1)}, u32[]{:S(2)}, u32[]{:S(2)}) collective-permute-start(bf16[2048,1536]{1,0:T(8,128)(2,1)} %bitcast.15), channel_id=1, source_target_pairs={{0,1},{1,0},{2,3},{3,2},{4,5},{5,4},{6,7},{7,6},{8,9},{9,8},{10,11... | collective-permute-start | bytes 18874376 | tf_op jit(solution)/shard_map/ppermute | solution.py:270
  0.5 17.7 %collective-permute-start.3 = (bf16[768,2048]{1,0:T(8,128)(2,1)}, bf16[768,2048]{1,0:T(8,128)(2,1)S(1)}, u32[]{:S(2)}, u32[]{:S(2)}) collective-permute-start(bf16[768,2048]{1,0:T(8,128)(2,1)} %bitcast.24), channel_id=1, source_target_pairs={{0,1},{1,0},{2,3},{3,2},{4,5},{5,4},{6,7},{7,6},{8,9},{9,8},{10,11... | collective-permute-start | bytes 9437192 | tf_op jit(solution)/shard_map/ppermute | solution.py:270
  1.9 11.5 %collective-permute-start = (bf16[64,2048]{1,0:T(8,128)(2,1)S(1)}, bf16[64,2048]{1,0:T(8,128)(2,1)S(1)}, u32[]{:S(2)}, u32[]{:S(2)}) collective-permute-start(bf16[64,2048]{1,0:T(8,128)(2,1)S(1)} %get-tuple-element.98), channel_id=1, source_target_pairs={{0,16},{1,17},{2,18},{3,19},{4,20},{5,21},{6,22},{7,23},{8,24},{9,... | collective-permute-start | bytes 786440 | tf_op jit(solution)/shard_map/ppermute | solution.py:20
  6.7 11.3 %collective-permute-start.1 = (bf16[64,2048]{1,0:T(8,128)(2,1)S(1)}, bf16[64,2048]{1,0:T(8,128)(2,1)S(1)}, u32[]{:S(2)}, u32[]{:S(2)}) collective-permute-start(bf16[64,2048]{1,0:T(8,128)(2,1)S(1)} %get-tuple-element.97), channel_id=1, source_target_pairs={{0,16},{1,17},{2,18},{3,19},{4,20},{5,21},{6,22},{7,23},{8,24},{9,... | collective-permute-start | bytes 786440 | tf_op jit(solution)/shard_map/ppermute | solution.py:20
  8.1 1.0 %copy-start.2 = (bf16[128,2048]{1,0:T(8,128)(2,1)S(1)}, bf16[128,2048]{1,0:T(8,128)(2,1)}, u32[]{:S(2)}) copy-start(bf16[128,2048]{1,0:T(8,128)(2,1)} %fresh_ref.1) | copy-start | bytes 1572868
  9.1 0.7 copy-start.3
  9.8 0.7 copy-start.4
  10.5 0.7 copy-start.5
  13.5 6.8 %collective-permute-start.4 = (bf16[1040,128]{1,0:T(8,128)(2,1)S(1)}, bf16[1040,128]{1,0:T(8,128)(2,1)S(1)}, u32[]{:S(2)}, u32[]{:S(2)}) collective-permute-start(bf16[1040,128]{1,0:T(8,128)(2,1)S(1)} %get-tuple-element.61.refs_0_), channel_id=1, source_target_pairs={{2,6},{3,7},{6,10},{7,11},{10,14},{11,15},{14,12},{15,13},{12,8},{... | collective-permute-start | bytes 798728 | tf_op jit(solution)/shard_map/ppermute | solution.py:270
  15.0 6.6 %collective-permute-start.5 = (bf16[1040,128]{1,0:T(8,128)(2,1)S(1)}, bf16[1040,128]{1,0:T(8,128)(2,1)S(1)}, u32[]{:S(2)}, u32[]{:S(2)}) collective-permute-start(bf16[1040,128]{1,0:T(8,128)(2,1)S(1)} %get-tuple-element.61.refs_0_), channel_id=1, source_target_pairs={{6,2},{7,3},{10,6},{11,7},{14,10},{15,11},{12,14},{13,15},{8,12},{... | collective-permute-start | bytes 798728 | tf_op jit(solution)/shard_map/ppermute | solution.py:270
  18.2 11.0 %collective-permute-start.8 = (bf16[1040,128]{1,0:T(8,128)(2,1)S(1)}, bf16[1040,128]{1,0:T(8,128)(2,1)S(1)}, u32[]{:S(2)}, u32[]{:S(2)}) collective-permute-start(bf16[1040,128]{1,0:T(8,128)(2,1)S(1)} %get-tuple-element.65.refs_1_), channel_id=1, source_target_pairs={{2,6},{3,7},{6,10},{7,11},{10,14},{11,15},{14,12},{15,13},{12,8},{... | collective-permute-start | bytes 798728 | tf_op jit(solution)/shard_map/ppermute | solution.py:270
  19.7 9.5 %collective-permute-start.9 = (bf16[1040,128]{1,0:T(8,128)(2,1)S(1)}, bf16[1040,128]{1,0:T(8,128)(2,1)S(1)}, u32[]{:S(2)}, u32[]{:S(2)}) collective-permute-start(bf16[1040,128]{1,0:T(8,128)(2,1)S(1)} %get-tuple-element.65.refs_1_), channel_id=1, source_target_pairs={{6,2},{7,3},{10,6},{11,7},{14,10},{15,11},{12,14},{13,15},{8,12},{... | collective-permute-start | bytes 798728 | tf_op jit(solution)/shard_map/ppermute | solution.py:270
  21.6 12.4 %collective-permute-start.6 = (bf16[1040,128]{1,0:T(8,128)(2,1)S(1)}, bf16[1040,128]{1,0:T(8,128)(2,1)S(1)}, u32[]{:S(2)}, u32[]{:S(2)}) collective-permute-start(bf16[1040,128]{1,0:T(8,128)(2,1)S(1)} %collective-permute-done.4.refs_0_), channel_id=1, source_target_pairs={{2,6},{3,7},{6,10},{7,11},{10,14},{11,15},{14,12},{15,13},{12,8},{... | collective-permute-start | bytes 798728 | tf_op jit(solution)/shard_map/ppermute | solution.py:270
  23.2 11.6 %collective-permute-start.7 = (bf16[1040,128]{1,0:T(8,128)(2,1)S(1)}, bf16[1040,128]{1,0:T(8,128)(2,1)S(1)}, u32[]{:S(2)}, u32[]{:S(2)}) collective-permute-start(bf16[1040,128]{1,0:T(8,128)(2,1)S(1)} %collective-permute-done.5.refs_1_), channel_id=1, source_target_pairs={{6,2},{7,3},{10,6},{11,7},{14,10},{15,11},{12,14},{13,15},{8,12},{... | collective-permute-start | bytes 798728 | tf_op jit(solution)/shard_map/ppermute | solution.py:270
  23.6 2.8 %copy-start = (bf16[1,1,2048,1536]{3,2,1,0:T(8,128)(2,1)S(1)}, bf16[1,1,2048,1536]{3,2,1,0:T(8,128)(2,1)}, u32[]{:S(2)}) copy-start(bf16[1,1,2048,1536]{3,2,1,0:T(8,128)(2,1)} %param.12) | copy-start | bytes 18874372
  29.2 10.4 %collective-permute-start.10 = (bf16[1040,128]{1,0:T(8,128)(2,1)S(1)}, bf16[1040,128]{1,0:T(8,128)(2,1)S(1)}, u32[]{:S(2)}, u32[]{:S(2)}) collective-permute-start(bf16[1040,128]{1,0:T(8,128)(2,1)S(1)} %collective-permute-done.8.refs_0_), channel_id=1, source_target_pairs={{2,6},{3,7},{6,10},{7,11},{10,14},{11,15},{14,12},{15,13},{12,8},{... | collective-permute-start | bytes 798728 | tf_op jit(solution)/shard_map/ppermute | solution.py:270
  30.8 9.6 %collective-permute-start.11 = (bf16[1040,128]{1,0:T(8,128)(2,1)S(1)}, bf16[1040,128]{1,0:T(8,128)(2,1)S(1)}, u32[]{:S(2)}, u32[]{:S(2)}) collective-permute-start(bf16[1040,128]{1,0:T(8,128)(2,1)S(1)} %collective-permute-done.9.refs_1_), channel_id=1, source_target_pairs={{6,2},{7,3},{10,6},{11,7},{14,10},{15,11},{12,14},{13,15},{8,12},{... | collective-permute-start | bytes 798728 | tf_op jit(solution)/shard_map/ppermute | solution.py:270
  34.7 10.5 %collective-permute-start.12 = (bf16[1040,128]{1,0:T(8,128)(2,1)S(1)}, bf16[1040,128]{1,0:T(8,128)(2,1)S(1)}, u32[]{:S(2)}, u32[]{:S(2)}) collective-permute-start(bf16[1040,128]{1,0:T(8,128)(2,1)S(1)} %collective-permute-done.6.refs_0_), channel_id=1, source_target_pairs={{2,6},{3,7},{6,10},{7,11},{10,14},{11,15},{14,12},{15,13},{12,8},{... | collective-permute-start | bytes 798728 | tf_op jit(solution)/shard_map/ppermute | solution.py:270
  36.3 9.8 %collective-permute-start.13 = (bf16[1040,128]{1,0:T(8,128)(2,1)S(1)}, bf16[1040,128]{1,0:T(8,128)(2,1)S(1)}, u32[]{:S(2)}, u32[]{:S(2)}) collective-permute-start(bf16[1040,128]{1,0:T(8,128)(2,1)S(1)} %collective-permute-done.7.refs_1_), channel_id=1, source_target_pairs={{6,2},{7,3},{10,6},{11,7},{14,10},{15,11},{12,14},{13,15},{8,12},{... | collective-permute-start | bytes 798728 | tf_op jit(solution)/shard_map/ppermute | solution.py:270
  40.5 10.0 %collective-permute-start.15 = (bf16[1040,128]{1,0:T(8,128)(2,1)S(1)}, bf16[1040,128]{1,0:T(8,128)(2,1)S(1)}, u32[]{:S(2)}, u32[]{:S(2)}) collective-permute-start(bf16[1040,128]{1,0:T(8,128)(2,1)S(1)} %collective-permute-done.10.refs_0_), channel_id=1, source_target_pairs={{2,6},{3,7},{6,10},{7,11},{10,14},{11,15},{14,12},{15,13},{12,8},{... | collective-permute-start | bytes 798728 | tf_op jit(solution)/shard_map/ppermute | solution.py:270
  42.0 8.5 %collective-permute-start.16 = (bf16[1040,128]{1,0:T(8,128)(2,1)S(1)}, bf16[1040,128]{1,0:T(8,128)(2,1)S(1)}, u32[]{:S(2)}, u32[]{:S(2)}) collective-permute-start(bf16[1040,128]{1,0:T(8,128)(2,1)S(1)} %collective-permute-done.11.refs_1_), channel_id=1, source_target_pairs={{6,2},{7,3},{10,6},{11,7},{14,10},{15,11},{12,14},{13,15},{8,12},{... | collective-permute-start | bytes 798728 | tf_op jit(solution)/shard_map/ppermute | solution.py:270
  46.2 10.7 %collective-permute-start.18 = (bf16[1040,128]{1,0:T(8,128)(2,1)S(1)}, bf16[1040,128]{1,0:T(8,128)(2,1)S(1)}, u32[]{:S(2)}, u32[]{:S(2)}) collective-permute-start(bf16[1040,128]{1,0:T(8,128)(2,1)S(1)} %collective-permute-done.12.refs_0_), channel_id=1, source_target_pairs={{2,6},{3,7},{6,10},{7,11},{10,14},{11,15},{14,12},{15,13},{12,8},{... | collective-permute-start | bytes 798728 | tf_op jit(solution)/shard_map/ppermute | solution.py:270
  50.5 8.8 %collective-permute-start.19 = (bf16[1040,128]{1,0:T(8,128)(2,1)S(1)}, bf16[1040,128]{1,0:T(8,128)(2,1)S(1)}, u32[]{:S(2)}, u32[]{:S(2)}) collective-permute-start(bf16[1040,128]{1,0:T(8,128)(2,1)S(1)} %collective-permute-done.16.refs_1_), channel_id=1, source_target_pairs={{6,2},{7,3},{10,6},{11,7},{14,10},{15,11},{12,14},{13,15},{8,12},{... | collective-permute-start | bytes 798728 | tf_op jit(solution)/shard_map/ppermute | solution.py:270
  52.0 12.9 %collective-permute-start.14 = (bf16[64,2048]{1,0:T(8,128)(2,1)S(1)}, bf16[64,2048]{1,0:T(8,128)(2,1)S(1)}, u32[]{:S(2)}, u32[]{:S(2)}) collective-permute-start(bf16[64,2048]{1,0:T(8,128)(2,1)S(1)} %convert_element_type.73), channel_id=1, source_target_pairs={{6,2},{7,3},{10,6},{11,7},{14,10},{15,11},{12,14},{13,15},{8,12},{... | collective-permute-start | bytes 786440 | tf_op jit(solution)/shard_map/ppermute | solution.py:270
  56.4 9.2 %collective-permute-start.17 = (bf16[64,2048]{1,0:T(8,128)(2,1)S(1)}, bf16[64,2048]{1,0:T(8,128)(2,1)S(1)}, u32[]{:S(2)}, u32[]{:S(2)}) collective-permute-start(bf16[64,2048]{1,0:T(8,128)(2,1)S(1)} %convert_element_type.74), channel_id=1, source_target_pairs={{2,6},{3,7},{6,10},{7,11},{10,14},{11,15},{14,12},{15,13},{12,8},{... | collective-permute-start | bytes 786440 | tf_op jit(solution)/shard_map/ppermute | solution.py:270
  62.1 9.2 %collective-permute-start.23 = (bf16[64,2048]{1,0:T(8,128)(2,1)S(1)}, bf16[64,2048]{1,0:T(8,128)(2,1)S(1)}, u32[]{:S(2)}, u32[]{:S(2)}) collective-permute-start(bf16[64,2048]{1,0:T(8,128)(2,1)S(1)} %convert_element_type.80), channel_id=1, source_target_pairs={{6,2},{7,3},{10,6},{11,7},{14,10},{15,11},{12,14},{13,15},{8,12},{... | collective-permute-start | bytes 786440 | tf_op jit(solution)/shard_map/ppermute | solution.py:270
  62.7 9.6 %collective-permute-start.21 = (bf16[64,2048]{1,0:T(8,128)(2,1)S(1)}, bf16[64,2048]{1,0:T(8,128)(2,1)S(1)}, u32[]{:S(2)}, u32[]{:S(2)}) collective-permute-start(bf16[64,2048]{1,0:T(8,128)(2,1)S(1)} %convert_element_type.75), channel_id=1, source_target_pairs={{2,6},{3,7},{6,10},{7,11},{10,14},{11,15},{14,12},{15,13},{12,8},{... | collective-permute-start | bytes 786440 | tf_op jit(solution)/shard_map/ppermute | solution.py:270
  68.5 15.0 %collective-permute-start.26 = (bf16[64,2048]{1,0:T(8,128)(2,1)S(1)}, bf16[64,2048]{1,0:T(8,128)(2,1)S(1)}, u32[]{:S(2)}, u32[]{:S(2)}) collective-permute-start(bf16[64,2048]{1,0:T(8,128)(2,1)S(1)} %get-tuple-element.92), channel_id=1, source_target_pairs={{2,6},{3,7},{6,10},{7,11},{10,14},{11,15},{14,12},{15,13},{12,8},{... | collective-permute-start | bytes 786440 | tf_op jit(solution)/shard_map/ppermute | solution.py:270
  69.4 15.9 %collective-permute-start.20 = (bf16[64,2048]{1,0:T(8,128)(2,1)S(1)}, bf16[64,2048]{1,0:T(8,128)(2,1)S(1)}, u32[]{:S(2)}, u32[]{:S(2)}) collective-permute-start(bf16[64,2048]{1,0:T(8,128)(2,1)S(1)} %get-tuple-element.84), channel_id=1, source_target_pairs={{6,2},{7,3},{10,6},{11,7},{14,10},{15,11},{12,14},{13,15},{8,12},{... | collective-permute-start | bytes 786440 | tf_op jit(solution)/shard_map/ppermute | solution.py:270
  71.4 9.9 %collective-permute-start.24 = (bf16[64,2048]{1,0:T(8,128)(2,1)S(1)}, bf16[64,2048]{1,0:T(8,128)(2,1)S(1)}, u32[]{:S(2)}, u32[]{:S(2)}) collective-permute-start(bf16[64,2048]{1,0:T(8,128)(2,1)S(1)} %add_convert_fusion.5), channel_id=1, source_target_pairs={{6,2},{7,3},{10,6},{11,7},{14,10},{15,11},{12,14},{13,15},{8,12},{... | collective-permute-start | bytes 786440 | tf_op jit(solution)/shard_map/ppermute | solution.py:270
  72.4 9.8 %collective-permute-start.22 = (bf16[64,2048]{1,0:T(8,128)(2,1)S(1)}, bf16[64,2048]{1,0:T(8,128)(2,1)S(1)}, u32[]{:S(2)}, u32[]{:S(2)}) collective-permute-start(bf16[64,2048]{1,0:T(8,128)(2,1)S(1)} %add_convert_fusion.7), channel_id=1, source_target_pairs={{2,6},{3,7},{6,10},{7,11},{10,14},{11,15},{14,12},{15,13},{12,8},{... | collective-permute-start | bytes 786440 | tf_op jit(solution)/shard_map/ppermute | solution.py:270
  81.4 9.3 %collective-permute-start.30 = (bf16[64,2048]{1,0:T(8,128)(2,1)S(1)}, bf16[64,2048]{1,0:T(8,128)(2,1)S(1)}, u32[]{:S(2)}, u32[]{:S(2)}) collective-permute-start(bf16[64,2048]{1,0:T(8,128)(2,1)S(1)} %add_convert_fusion.4), channel_id=1, source_target_pairs={{6,2},{7,3},{10,6},{11,7},{14,10},{15,11},{12,14},{13,15},{8,12},{... | collective-permute-start | bytes 786440 | tf_op jit(solution)/shard_map/ppermute | solution.py:270
  82.2 9.2 %collective-permute-start.28 = (bf16[64,2048]{1,0:T(8,128)(2,1)S(1)}, bf16[64,2048]{1,0:T(8,128)(2,1)S(1)}, u32[]{:S(2)}, u32[]{:S(2)}) collective-permute-start(bf16[64,2048]{1,0:T(8,128)(2,1)S(1)} %add_convert_fusion.6), channel_id=1, source_target_pairs={{2,6},{3,7},{6,10},{7,11},{10,14},{11,15},{14,12},{15,13},{12,8},{... | collective-permute-start | bytes 786440 | tf_op jit(solution)/shard_map/ppermute | solution.py:270
  83.6 10.1 %collective-permute-start.27 = (bf16[64,2048]{1,0:T(8,128)(2,1)S(1)}, bf16[64,2048]{1,0:T(8,128)(2,1)S(1)}, u32[]{:S(2)}, u32[]{:S(2)}) collective-permute-start(bf16[64,2048]{1,0:T(8,128)(2,1)S(1)} %add_convert_fusion.2), channel_id=1, source_target_pairs={{2,6},{3,7},{6,10},{7,11},{10,14},{11,15},{14,12},{15,13},{12,8},{... | collective-permute-start | bytes 786440 | tf_op jit(solution)/shard_map/ppermute | solution.py:270
  85.4 8.4 %collective-permute-start.25 = (bf16[64,2048]{1,0:T(8,128)(2,1)S(1)}, bf16[64,2048]{1,0:T(8,128)(2,1)S(1)}, u32[]{:S(2)}, u32[]{:S(2)}) collective-permute-start(bf16[64,2048]{1,0:T(8,128)(2,1)S(1)} %add_convert_fusion.3), channel_id=1, source_target_pairs={{6,2},{7,3},{10,6},{11,7},{14,10},{15,11},{12,14},{13,15},{8,12},{... | collective-permute-start | bytes 786440 | tf_op jit(solution)/shard_map/ppermute | solution.py:270
  90.7 6.4 %collective-permute-start.31 = (bf16[64,2048]{1,0:T(8,128)(2,1)S(1)}, bf16[64,2048]{1,0:T(8,128)(2,1)S(1)}, u32[]{:S(2)}, u32[]{:S(2)}) collective-permute-start(bf16[64,2048]{1,0:T(8,128)(2,1)S(1)} %add_convert_fusion), channel_id=1, source_target_pairs={{6,2},{7,3},{10,6},{11,7},{14,10},{15,11},{12,14},{13,15},{8,12},{... | collective-permute-start | bytes 786440 | tf_op jit(solution)/shard_map/ppermute | solution.py:270
  91.5 6.4 %collective-permute-start.29 = (bf16[64,2048]{1,0:T(8,128)(2,1)S(1)}, bf16[64,2048]{1,0:T(8,128)(2,1)S(1)}, u32[]{:S(2)}, u32[]{:S(2)}) collective-permute-start(bf16[64,2048]{1,0:T(8,128)(2,1)S(1)} %add_convert_fusion.1), channel_id=1, source_target_pairs={{2,6},{3,7},{6,10},{7,11},{10,14},{11,15},{14,12},{15,13},{12,8},{... | collective-permute-start | bytes 786440 | tf_op jit(solution)/shard_map/ppermute | solution.py:270

commit v12 on v11

--- a/solution.py
+++ b/solution.py
@@ -320,12 +320,13 @@
     long = [(to_up, 0, up), (to_down, 1, down)]
     short_totals = [send_on(flow, hops - 1, None, None)[1] for flow in short]
     long_totals = [send_on(flow, hops, None, None)[1] for flow in long]
-    *own_sums, down_sum, up_sum = mlp(packed, [f[0][hops - 2, f[1]] for f in short], short_totals)
-    short_totals = [move(total, flow[2]) for total, flow in zip((down_sum, up_sum), short)]
-    after = None
     for s in reversed(range(1, hops)):
-        sent, long_totals = zip(*(send_on(f, s, t, None) for f, t in zip(long, long_totals)))
-        if 1 < s < hops - 1:
+        sent, long_totals = zip(*(send_on(f, s, t, short_totals if s == hops - 1 else None) for f, t in zip(long, long_totals)))
+        if s == hops - 1:
+            totals = lax.optimization_barrier((short_totals, sent))[0]
+            *own_sums, down_sum, up_sum = mlp(packed, [f[0][s - 1, f[1]] for f in short], totals)
+            short_totals = [move(total, flow[2]) for total, flow in zip((down_sum, up_sum), short)]
+        elif s > 1:
             short_totals = [send_on(f, s - 1, t, sent)[1] for f, t in zip(short, short_totals)]
 
     nears = [

time: 99.1 us -> 101 us (1.019)
  waiting for transfers between devices: 29.8 us -> 32 us
    ppermute x30, waiting for transfers between devices: 25.3 us -> 27.5 us  [move(): return lax.ppermute(value, 'expert', pairs)]
  transfers between devices with their start and end apart: 32 -> 32, of which waited for: 15 -> 16; matrix products, arithmetic and copies ran while one was open for 2% -> 2% of each run, Pallas kernels for 23% -> 22%
where the time goes in v12:
time: 101 us
  starting transfers between devices  36.9 us (37%)
  waiting for transfers between devices  32 us (32%)
  Pallas kernels  23.4 us (23%)
  local copies, waits for them, and re-layouts  7.21 us (7%)
    ppermute x30, starting transfers between devices, move(): return lax.ppermute(value, 'expert', pairs)  30.7 us
    ppermute x30, waiting for transfers between devices, move(): return lax.ppermute(value, 'expert', pairs)  27.5 us
    pallas_call x8, Pallas kernels, expert_rows(): pl.pallas_call(functools.partial(mlp_kernel, parts=len(payloads), adds=le...  22.1 us
    ppermute x2, starting transfers between devices, from_behind(): return lax.ppermute(value, axis, pairs)  6.18 us
    unnamed x12, local copies, waits for them, and re-layouts  5.89 us
    ppermute x2, waiting for transfers between devices, from_behind(): return lax.ppermute(value, axis, pairs)  4.5 us
  transfers between devices with their start and end apart: 32, of which 16 were waited for; matrix products, arithmetic and copies ran while one was open for 2% of the time, Pallas kernels for 22%

profile of v12, /device:TPU:0, one launch (start us, length us, event | category | flops | bytes accessed | tf_op | source)
XLA Modules:
  0.0 100.5 jit_solution(13723514329329258748)
XLA Ops:
  0.0 0.5 collective-permute-start.2
  0.5 1.3 %slice_bitcast_fusion = (bf16[64,2048]{1,0:T(8,128)(2,1)S(1)}, bf16[64,2048]{1,0:T(8,128)(2,1)S(1)}) fusion(bf16[1,128,2048]{2,1,0:T(8,128)(2,1)} %param.8), kind=kLoop, calls=%fused_computation.10 | loop fusion | bytes 1048576 | tf_op jit(solution)/shard_map/squeeze | solution.py:277
  1.8 4.9 %collective-permute-start = (bf16[64,2048]{1,0:T(8,128)(2,1)S(1)}, bf16[64,2048]{1,0:T(8,128)(2,1)S(1)}, u32[]{:S(2)}, u32[]{:S(2)}) collective-permute-start(bf16[64,2048]{1,0:T(8,128)(2,1)S(1)} %get-tuple-element.106), channel_id=1, source_target_pairs={{0,16},{1,17},{2,18},{3,19},{4,20},{5,21},{6,22},{7,23},{8,24},{9,... | collective-permute-start | bytes 786440 | tf_op jit(solution)/shard_map/ppermute | solution.py:20
  6.7 1.3 %collective-permute-start.1 = (bf16[64,2048]{1,0:T(8,128)(2,1)S(1)}, bf16[64,2048]{1,0:T(8,128)(2,1)S(1)}, u32[]{:S(2)}, u32[]{:S(2)}) collective-permute-start(bf16[64,2048]{1,0:T(8,128)(2,1)S(1)} %get-tuple-element.105), channel_id=1, source_target_pairs={{0,16},{1,17},{2,18},{3,19},{4,20},{5,21},{6,22},{7,23},{8,24},{9,... | collective-permute-start | bytes 786440 | tf_op jit(solution)/shard_map/ppermute | solution.py:20
  8.1 1.0 %copy-done.2 = bf16[128,2048]{1,0:T(8,128)(2,1)S(1)} copy-done((bf16[128,2048]{1,0:T(8,128)(2,1)S(1)}, bf16[128,2048]{1,0:T(8,128)(2,1)}, u32[]{:S(2)}) %copy-start.2) | copy-done | bytes 524312
  9.1 0.7 copy-done.3
  9.8 0.7 copy-done.4
  10.5 0.7 copy-done.5
  11.2 0.2 base_rows.1
  11.4 2.0 %collective-permute-done.arrived_ref = bf16[64,2048]{1,0:T(8,128)(2,1)S(1)} collective-permute-done((bf16[64,2048]{1,0:T(8,128)(2,1)S(1)}, bf16[64,2048]{1,0:T(8,128)(2,1)S(1)}, u32[]{:S(2)}, u32[]{:S(2)}) %collective-permute-start) | collective-permute-done | bytes 262176 | tf_op jit(solution)/shard_map/ppermute | solution.py:20
  13.5 1.5 %collective-permute-start.4 = (bf16[1040,128]{1,0:T(8,128)(2,1)S(1)}, bf16[1040,128]{1,0:T(8,128)(2,1)S(1)}, u32[]{:S(2)}, u32[]{:S(2)}) collective-permute-start(bf16[1040,128]{1,0:T(8,128)(2,1)S(1)} %get-tuple-element.65.refs_0_), channel_id=1, source_target_pairs={{2,6},{3,7},{6,10},{7,11},{10,14},{11,15},{14,12},{15,13},{12,8},{... | collective-permute-start | bytes 798728 | tf_op jit(solution)/shard_map/ppermute | solution.py:270
  15.0 0.5 collective-permute-start.5
  15.5 2.5 %collective-permute-done.1.arrived_ref = bf16[64,2048]{1,0:T(8,128)(2,1)S(1)} collective-permute-done((bf16[64,2048]{1,0:T(8,128)(2,1)S(1)}, bf16[64,2048]{1,0:T(8,128)(2,1)S(1)}, u32[]{:S(2)}, u32[]{:S(2)}) %collective-permute-start.1) | collective-permute-done | bytes 262176 | tf_op jit(solution)/shard_map/ppermute | solution.py:20
  18.1 1.5 %collective-permute-start.8 = (bf16[1040,128]{1,0:T(8,128)(2,1)S(1)}, bf16[1040,128]{1,0:T(8,128)(2,1)S(1)}, u32[]{:S(2)}, u32[]{:S(2)}) collective-permute-start(bf16[1040,128]{1,0:T(8,128)(2,1)S(1)} %get-tuple-element.69.refs_1_), channel_id=1, source_target_pairs={{2,6},{3,7},{6,10},{7,11},{10,14},{11,15},{14,12},{15,13},{12,8},{... | collective-permute-start | bytes 798728 | tf_op jit(solution)/shard_map/ppermute | solution.py:270
  19.7 0.5 collective-permute-start.9
  20.2 1.3 %collective-permute-done.5.refs_1_ = bf16[1040,128]{1,0:T(8,128)(2,1)S(1)} collective-permute-done((bf16[1040,128]{1,0:T(8,128)(2,1)S(1)}, bf16[1040,128]{1,0:T(8,128)(2,1)S(1)}, u32[]{:S(2)}, u32[]{:S(2)}) %collective-permute-start.5) | collective-permute-done | bytes 266272 | tf_op jit(solution)/shard_map/ppermute | solution.py:270
  21.6 1.6 %collective-permute-start.6 = (bf16[1040,128]{1,0:T(8,128)(2,1)S(1)}, bf16[1040,128]{1,0:T(8,128)(2,1)S(1)}, u32[]{:S(2)}, u32[]{:S(2)}) collective-permute-start(bf16[1040,128]{1,0:T(8,128)(2,1)S(1)} %collective-permute-done.4.refs_0_), channel_id=1, source_target_pairs={{2,6},{3,7},{6,10},{7,11},{10,14},{11,15},{14,12},{15,13},{12,8},{... | collective-permute-start | bytes 798728 | tf_op jit(solution)/shard_map/ppermute | solution.py:270
  23.2 0.4 collective-permute-start.7
  23.6 2.8 %copy-done = bf16[1,1,2048,1536]{3,2,1,0:T(8,128)(2,1)S(1)} copy-done((bf16[1,1,2048,1536]{3,2,1,0:T(8,128)(2,1)S(1)}, bf16[1,1,2048,1536]{3,2,1,0:T(8,128)(2,1)}, u32[]{:S(2)}) %copy-start) | copy-done | bytes 6291480
  26.4 2.8 %expert_rows.8 = (f32[64,2048]{1,0:T(8,128)S(1)}, f32[64,2048]{1,0:T(8,128)S(1)}) custom-call(s32[1]{0:T(128)} %bitcast.6.expert_ref, bf16[1040,128]{1,0:T(8,128)(2,1)S(1)} %collective-permute-done.4.refs_0_, bf16[1040,128]{1,0:T(8,128)(2,1)S(1)} %collective-permute-done.5.refs_1_, bf16[2048,1536]{1,0:T(8,128)(2,1)S(1)} %bitcast.16, ...), custom_call_target="tpu_custom_call" | custom-call | flops 2415919104 | bytes 1572864 | tf_op jit(solution)/shard_map/expert_rows/pallas_call | solution.py:204
  29.2 1.6 %collective-permute-start.10 = (bf16[1040,128]{1,0:T(8,128)(2,1)S(1)}, bf16[1040,128]{1,0:T(8,128)(2,1)S(1)}, u32[]{:S(2)}, u32[]{:S(2)}) collective-permute-start(bf16[1040,128]{1,0:T(8,128)(2,1)S(1)} %collective-permute-done.8.refs_0_), channel_id=1, source_target_pairs={{2,6},{3,7},{6,10},{7,11},{10,14},{11,15},{14,12},{15,13},{12,8},{... | collective-permute-start | bytes 798728 | tf_op jit(solution)/shard_map/ppermute | solution.py:270
  30.8 0.4 collective-permute-start.11
  31.3 2.7 %expert_rows.9 = (f32[64,2048]{1,0:T(8,128)S(1)}, f32[64,2048]{1,0:T(8,128)S(1)}) custom-call(s32[1]{0:T(128)} %bitcast.6.expert_ref, bf16[1040,128]{1,0:T(8,128)(2,1)S(1)} %collective-permute-done.8.refs_0_, bf16[1040,128]{1,0:T(8,128)(2,1)S(1)} %collective-permute-done.9.refs_1_, bf16[2048,1536]{1,0:T(8,128)(2,1)S(1)} %bitcast.17, ...), custom_call_target="tpu_custom_call" | custom-call | flops 2415919104 | bytes 1572864 | tf_op jit(solution)/shard_map/expert_rows/pallas_call | solution.py:204
  34.0 0.7 collective-permute-done.7.refs_1_
  34.7 1.6 %collective-permute-start.12 = (bf16[1040,128]{1,0:T(8,128)(2,1)S(1)}, bf16[1040,128]{1,0:T(8,128)(2,1)S(1)}, u32[]{:S(2)}, u32[]{:S(2)}) collective-permute-start(bf16[1040,128]{1,0:T(8,128)(2,1)S(1)} %collective-permute-done.6.refs_0_), channel_id=1, source_target_pairs={{2,6},{3,7},{6,10},{7,11},{10,14},{11,15},{14,12},{15,13},{12,8},{... | collective-permute-start | bytes 798728 | tf_op jit(solution)/shard_map/ppermute | solution.py:270
  36.3 0.4 collective-permute-start.13
  36.8 2.7 %expert_rows.10 = (f32[64,2048]{1,0:T(8,128)S(1)}, f32[64,2048]{1,0:T(8,128)S(1)}) custom-call(s32[1]{0:T(128)} %bitcast.6.expert_ref, bf16[1040,128]{1,0:T(8,128)(2,1)S(1)} %collective-permute-done.6.refs_0_, bf16[1040,128]{1,0:T(8,128)(2,1)S(1)} %collective-permute-done.7.refs_1_, bf16[2048,1536]{1,0:T(8,128)(2,1)S(1)} %bitcast.18, ...), custom_call_target="tpu_custom_call" | custom-call | flops 2415919104 | bytes 1572864 | tf_op jit(solution)/shard_map/expert_rows/pallas_call | solution.py:204
  39.5 0.9 collective-permute-done.11.refs_1_
  40.4 1.6 %collective-permute-start.15 = (bf16[1040,128]{1,0:T(8,128)(2,1)S(1)}, bf16[1040,128]{1,0:T(8,128)(2,1)S(1)}, u32[]{:S(2)}, u32[]{:S(2)}) collective-permute-start(bf16[1040,128]{1,0:T(8,128)(2,1)S(1)} %collective-permute-done.10.refs_0_), channel_id=1, source_target_pairs={{2,6},{3,7},{6,10},{7,11},{10,14},{11,15},{14,12},{15,13},{12,8},{... | collective-permute-start | bytes 798728 | tf_op jit(solution)/shard_map/ppermute | solution.py:270
  42.0 0.5 collective-permute-start.16
  42.5 2.7 %expert_rows.11 = (f32[64,2048]{1,0:T(8,128)S(1)}, f32[64,2048]{1,0:T(8,128)S(1)}) custom-call(s32[1]{0:T(128)} %bitcast.6.expert_ref, bf16[1040,128]{1,0:T(8,128)(2,1)S(1)} %collective-permute-done.10.refs_0_, bf16[1040,128]{1,0:T(8,128)(2,1)S(1)} %collective-permute-done.11.refs_1_, bf16[2048,1536]{1,0:T(8,128)(2,1)S(1)} %bitcast.19, ...), custom_call_target="tpu_custom_call" | custom-call | flops 2415919104 | bytes 1572864 | tf_op jit(solution)/shard_map/expert_rows/pallas_call | solution.py:204
  45.2 0.9 collective-permute-done.13.refs_1_
  46.2 1.6 %collective-permute-start.18 = (bf16[1040,128]{1,0:T(8,128)(2,1)S(1)}, bf16[1040,128]{1,0:T(8,128)(2,1)S(1)}, u32[]{:S(2)}, u32[]{:S(2)}) collective-permute-start(bf16[1040,128]{1,0:T(8,128)(2,1)S(1)} %collective-permute-done.12.refs_0_), channel_id=1, source_target_pairs={{2,6},{3,7},{6,10},{7,11},{10,14},{11,15},{14,12},{15,13},{12,8},{... | collective-permute-start | bytes 798728 | tf_op jit(solution)/shard_map/ppermute | solution.py:270
  47.7 2.8 %expert_rows.12 = (f32[64,2048]{1,0:T(8,128)S(1)}, f32[64,2048]{1,0:T(8,128)S(1)}) custom-call(s32[1]{0:T(128)} %bitcast.6.expert_ref, bf16[1040,128]{1,0:T(8,128)(2,1)S(1)} %collective-permute-done.12.refs_0_, bf16[1040,128]{1,0:T(8,128)(2,1)S(1)} %collective-permute-done.13.refs_1_, bf16[2048,1536]{1,0:T(8,128)(2,1)S(1)} %bitcast.20, ...), custom_call_target="tpu_custom_call" | custom-call | flops 2415919104 | bytes 1572864 | tf_op jit(solution)/shard_map/expert_rows/pallas_call | solution.py:204
  50.5 1.4 %collective-permute-start.19 = (bf16[1040,128]{1,0:T(8,128)(2,1)S(1)}, bf16[1040,128]{1,0:T(8,128)(2,1)S(1)}, u32[]{:S(2)}, u32[]{:S(2)}) collective-permute-start(bf16[1040,128]{1,0:T(8,128)(2,1)S(1)} %collective-permute-done.16.refs_1_), channel_id=1, source_target_pairs={{6,2},{7,3},{10,6},{11,7},{14,10},{15,11},{12,14},{13,15},{8,12},{... | collective-permute-start | bytes 798728 | tf_op jit(solution)/shard_map/ppermute | solution.py:270
  52.0 1.6 %collective-permute-start.14 = (bf16[64,2048]{1,0:T(8,128)(2,1)S(1)}, bf16[64,2048]{1,0:T(8,128)(2,1)S(1)}, u32[]{:S(2)}, u32[]{:S(2)}) collective-permute-start(bf16[64,2048]{1,0:T(8,128)(2,1)S(1)} %convert_element_type.73), channel_id=1, source_target_pairs={{6,2},{7,3},{10,6},{11,7},{14,10},{15,11},{12,14},{13,15},{8,12},{... | collective-permute-start | bytes 786440 | tf_op jit(solution)/shard_map/ppermute | solution.py:270
  53.6 2.8 %expert_rows.13 = (f32[64,2048]{1,0:T(8,128)S(1)}, f32[64,2048]{1,0:T(8,128)S(1)}) custom-call(s32[1]{0:T(128)} %bitcast.6.expert_ref, bf16[1040,128]{1,0:T(8,128)(2,1)S(1)} %collective-permute-done.15.refs_0_, bf16[1040,128]{1,0:T(8,128)(2,1)S(1)} %collective-permute-done.16.refs_1_, bf16[2048,1536]{1,0:T(8,128)(2,1)S(1)} %bitcast.21, ...), custom_call_target="tpu_custom_call" | custom-call | flops 2415919104 | bytes 1572864 | tf_op jit(solution)/shard_map/expert_rows/pallas_call | solution.py:204
  56.4 0.5 collective-permute-start.17
  56.9 2.3 %collective-permute-done.19.refs_1_ = bf16[1040,128]{1,0:T(8,128)(2,1)S(1)} collective-permute-done((bf16[1040,128]{1,0:T(8,128)(2,1)S(1)}, bf16[1040,128]{1,0:T(8,128)(2,1)S(1)}, u32[]{:S(2)}, u32[]{:S(2)}) %collective-permute-start.19) | collective-permute-done | bytes 266272 | tf_op jit(solution)/shard_map/ppermute | solution.py:270
  59.2 2.7 %expert_rows.14 = (f32[64,2048]{1,0:T(8,128)S(1)}, f32[64,2048]{1,0:T(8,128)S(1)}) custom-call(s32[1]{0:T(128)} %bitcast.6.expert_ref, bf16[1040,128]{1,0:T(8,128)(2,1)S(1)} %collective-permute-done.18.refs_0_, bf16[1040,128]{1,0:T(8,128)(2,1)S(1)} %collective-permute-done.19.refs_1_, bf16[2048,1536]{1,0:T(8,128)(2,1)S(1)} %bitcast.22, ...), custom_call_target="tpu_custom_call" | custom-call | flops 2415919104 | bytes 1572864 | tf_op jit(solution)/shard_map/expert_rows/pallas_call | solution.py:204
  62.0 1.6 %collective-permute-start.20 = (bf16[64,2048]{1,0:T(8,128)(2,1)S(1)}, bf16[64,2048]{1,0:T(8,128)(2,1)S(1)}, u32[]{:S(2)}, u32[]{:S(2)}) collective-permute-start(bf16[64,2048]{1,0:T(8,128)(2,1)S(1)} %convert_element_type.75), channel_id=1, source_target_pairs={{2,6},{3,7},{6,10},{7,11},{10,14},{11,15},{14,12},{15,13},{12,8},{... | collective-permute-start | bytes 786440 | tf_op jit(solution)/shard_map/ppermute | solution.py:270
  63.7 0.5 collective-permute-start.21
  64.2 0.6 collective-permute-done.17.refs_9_
  64.7 4.1 %collective-permute-done.20 = bf16[64,2048]{1,0:T(8,128)(2,1)S(1)} collective-permute-done((bf16[64,2048]{1,0:T(8,128)(2,1)S(1)}, bf16[64,2048]{1,0:T(8,128)(2,1)S(1)}, u32[]{:S(2)}, u32[]{:S(2)}) %collective-permute-start.20) | collective-permute-done | bytes 262176 | tf_op jit(solution)/shard_map/ppermute | solution.py:270
  68.8 3.7 %collective-permute-done.21 = bf16[64,2048]{1,0:T(8,128)(2,1)S(1)} collective-permute-done((bf16[64,2048]{1,0:T(8,128)(2,1)S(1)}, bf16[64,2048]{1,0:T(8,128)(2,1)S(1)}, u32[]{:S(2)}, u32[]{:S(2)}) %collective-permute-start.21) | collective-permute-done | bytes 262176 | tf_op jit(solution)/shard_map/ppermute | solution.py:270
  72.6 0.1 add_convert_fusion.6
  72.7 0.4 collective-permute-start.24
  73.1 1.7 %collective-permute-start.23 = (bf16[64,2048]{1,0:T(8,128)(2,1)S(1)}, bf16[64,2048]{1,0:T(8,128)(2,1)S(1)}, u32[]{:S(2)}, u32[]{:S(2)}) collective-permute-start(bf16[64,2048]{1,0:T(8,128)(2,1)S(1)} %get-tuple-element.108), channel_id=1, source_target_pairs={{2,6},{3,7},{6,10},{7,11},{10,14},{11,15},{14,12},{15,13},{12,8},{... | collective-permute-start | bytes 786440 | tf_op jit(solution)/shard_map/ppermute | solution.py:270
  74.8 2.9 %expert_rows.15 = (f32[64,2048]{1,0:T(8,128)S(1)}, f32[64,2048]{1,0:T(8,128)S(1)}, bf16[64,2048]{1,0:T(8,128)(2,1)S(1)}, bf16[64,2048]{1,0:T(8,128)(2,1)S(1)}) custom-call(s32[1]{0:T(128)} %bitcast.6.expert_ref, bf16[1040,128]{1,0:T(8,128)(2,1)S(1)} %get-tuple-element.65.refs_0_, bf16[1040,128]{1,0:T(8,128)(2,1)S(1)} %get-tuple-element.69.refs_1_, ...), custom_call_target="tpu_custom_call" | custom-call | flops 2415919104 | bytes 1572864 | tf_op jit(solution)/shard_map/expert_rows/pallas_call | solution.py:204
  77.7 0.3 collective-permute-start.22
  78.1 1.7 %collective-permute-start.26 = (bf16[64,2048]{1,0:T(8,128)(2,1)S(1)}, bf16[64,2048]{1,0:T(8,128)(2,1)S(1)}, u32[]{:S(2)}, u32[]{:S(2)}) collective-permute-start(bf16[64,2048]{1,0:T(8,128)(2,1)S(1)} %get-tuple-element.100), channel_id=1, source_target_pairs={{2,6},{3,7},{6,10},{7,11},{10,14},{11,15},{14,12},{15,13},{12,8},{... | collective-permute-start | bytes 786440 | tf_op jit(solution)/shard_map/ppermute | solution.py:270
  79.8 2.2 %collective-permute-done.24 = bf16[64,2048]{1,0:T(8,128)(2,1)S(1)} collective-permute-done((bf16[64,2048]{1,0:T(8,128)(2,1)S(1)}, bf16[64,2048]{1,0:T(8,128)(2,1)S(1)}, u32[]{:S(2)}, u32[]{:S(2)}) %collective-permute-start.24) | collective-permute-done | bytes 262176 | tf_op jit(solution)/shard_map/ppermute | solution.py:270
  82.1 0.4 collective-permute-start.30
  82.5 1.7 %collective-permute-start.28 = (bf16[64,2048]{1,0:T(8,128)(2,1)S(1)}, bf16[64,2048]{1,0:T(8,128)(2,1)S(1)}, u32[]{:S(2)}, u32[]{:S(2)}) collective-permute-start(bf16[64,2048]{1,0:T(8,128)(2,1)S(1)} %add_convert_fusion.5), channel_id=1, source_target_pairs={{2,6},{3,7},{6,10},{7,11},{10,14},{11,15},{14,12},{15,13},{12,8},{... | collective-permute-start | bytes 786440 | tf_op jit(solution)/shard_map/ppermute | solution.py:270
  84.3 3.6 %collective-permute-done.26 = bf16[64,2048]{1,0:T(8,128)(2,1)S(1)} collective-permute-done((bf16[64,2048]{1,0:T(8,128)(2,1)S(1)}, bf16[64,2048]{1,0:T(8,128)(2,1)S(1)}, u32[]{:S(2)}, u32[]{:S(2)}) %collective-permute-start.26) | collective-permute-done | bytes 262176 | tf_op jit(solution)/shard_map/ppermute | solution.py:270
  87.9 0.4 collective-permute-start.25
  88.4 1.7 %collective-permute-start.27 = (bf16[64,2048]{1,0:T(8,128)(2,1)S(1)}, bf16[64,2048]{1,0:T(8,128)(2,1)S(1)}, u32[]{:S(2)}, u32[]{:S(2)}) collective-permute-start(bf16[64,2048]{1,0:T(8,128)(2,1)S(1)} %add_convert_fusion.2), channel_id=1, source_target_pairs={{2,6},{3,7},{6,10},{7,11},{10,14},{11,15},{14,12},{15,13},{12,8},{... | collective-permute-start | bytes 786440 | tf_op jit(solution)/shard_map/ppermute | solution.py:270
  90.1 2.4 %collective-permute-done.30 = bf16[64,2048]{1,0:T(8,128)(2,1)S(1)} collective-permute-done((bf16[64,2048]{1,0:T(8,128)(2,1)S(1)}, bf16[64,2048]{1,0:T(8,128)(2,1)S(1)}, u32[]{:S(2)}, u32[]{:S(2)}) %collective-permute-start.30) | collective-permute-done | bytes 262176 | tf_op jit(solution)/shard_map/ppermute | solution.py:270
  92.6 0.5 collective-permute-start.31
  93.2 1.6 %collective-permute-start.29 = (bf16[64,2048]{1,0:T(8,128)(2,1)S(1)}, bf16[64,2048]{1,0:T(8,128)(2,1)S(1)}, u32[]{:S(2)}, u32[]{:S(2)}) collective-permute-start(bf16[64,2048]{1,0:T(8,128)(2,1)S(1)} %add_convert_fusion.1), channel_id=1, source_target_pairs={{2,6},{3,7},{6,10},{7,11},{10,14},{11,15},{14,12},{15,13},{12,8},{... | collective-permute-start | bytes 786440 | tf_op jit(solution)/shard_map/ppermute | solution.py:270
  94.8 0.5 collective-permute-done.25
  95.6 3.5 %collective-permute-done.31.total1_ref = bf16[64,2048]{1,0:T(8,128)(2,1)S(1)} collective-permute-done((bf16[64,2048]{1,0:T(8,128)(2,1)S(1)}, bf16[64,2048]{1,0:T(8,128)(2,1)S(1)}, u32[]{:S(2)}, u32[]{:S(2)}) %collective-permute-start.31) | collective-permute-done | bytes 262176 | tf_op jit(solution)/shard_map/ppermute | solution.py:270
  99.1 0.6 collective-permute-done.29.total0_ref
  99.6 0.9 last_rows.1
  (38 shorter events, 0.9 us)
Async XLA Ops:
  0.0 23.6 %copy-start.1 = (bf16[1,1,768,2048]{3,2,1,0:T(8,128)(2,1)S(1)}, bf16[1,1,768,2048]{3,2,1,0:T(8,128)(2,1)}, u32[]{:S(2)}) copy-start(bf16[1,1,768,2048]{3,2,1,0:T(8,128)(2,1)} %param.13) | copy-start | bytes 9437188
  0.0 18.1 %collective-permute-start.2 = (bf16[2048,1536]{1,0:T(8,128)(2,1)}, bf16[2048,1536]{1,0:T(8,128)(2,1)S(1)}, u32[]{:S(2)}, u32[]{:S(2)}) collective-permute-start(bf16[2048,1536]{1,0:T(8,128)(2,1)} %bitcast.15), channel_id=1, source_target_pairs={{0,1},{1,0},{2,3},{3,2},{4,5},{5,4},{6,7},{7,6},{8,9},{9,8},{10,11... | collective-permute-start | bytes 18874376 | tf_op jit(solution)/shard_map/ppermute | solution.py:270
  0.5 17.7 %collective-permute-start.3 = (bf16[768,2048]{1,0:T(8,128)(2,1)}, bf16[768,2048]{1,0:T(8,128)(2,1)S(1)}, u32[]{:S(2)}, u32[]{:S(2)}) collective-permute-start(bf16[768,2048]{1,0:T(8,128)(2,1)} %bitcast.24), channel_id=1, source_target_pairs={{0,1},{1,0},{2,3},{3,2},{4,5},{5,4},{6,7},{7,6},{8,9},{9,8},{10,11... | collective-permute-start | bytes 9437192 | tf_op jit(solution)/shard_map/ppermute | solution.py:270
  1.8 11.5 %collective-permute-start = (bf16[64,2048]{1,0:T(8,128)(2,1)S(1)}, bf16[64,2048]{1,0:T(8,128)(2,1)S(1)}, u32[]{:S(2)}, u32[]{:S(2)}) collective-permute-start(bf16[64,2048]{1,0:T(8,128)(2,1)S(1)} %get-tuple-element.106), channel_id=1, source_target_pairs={{0,16},{1,17},{2,18},{3,19},{4,20},{5,21},{6,22},{7,23},{8,24},{9,... | collective-permute-start | bytes 786440 | tf_op jit(solution)/shard_map/ppermute | solution.py:20
  6.7 11.3 %collective-permute-start.1 = (bf16[64,2048]{1,0:T(8,128)(2,1)S(1)}, bf16[64,2048]{1,0:T(8,128)(2,1)S(1)}, u32[]{:S(2)}, u32[]{:S(2)}) collective-permute-start(bf16[64,2048]{1,0:T(8,128)(2,1)S(1)} %get-tuple-element.105), channel_id=1, source_target_pairs={{0,16},{1,17},{2,18},{3,19},{4,20},{5,21},{6,22},{7,23},{8,24},{9,... | collective-permute-start | bytes 786440 | tf_op jit(solution)/shard_map/ppermute | solution.py:20
  8.0 1.0 %copy-start.2 = (bf16[128,2048]{1,0:T(8,128)(2,1)S(1)}, bf16[128,2048]{1,0:T(8,128)(2,1)}, u32[]{:S(2)}) copy-start(bf16[128,2048]{1,0:T(8,128)(2,1)} %fresh_ref.1) | copy-start | bytes 1572868
  9.1 0.7 copy-start.3
  9.8 0.7 copy-start.4
  10.5 0.7 copy-start.5
  13.5 6.8 %collective-permute-start.4 = (bf16[1040,128]{1,0:T(8,128)(2,1)S(1)}, bf16[1040,128]{1,0:T(8,128)(2,1)S(1)}, u32[]{:S(2)}, u32[]{:S(2)}) collective-permute-start(bf16[1040,128]{1,0:T(8,128)(2,1)S(1)} %get-tuple-element.65.refs_0_), channel_id=1, source_target_pairs={{2,6},{3,7},{6,10},{7,11},{10,14},{11,15},{14,12},{15,13},{12,8},{... | collective-permute-start | bytes 798728 | tf_op jit(solution)/shard_map/ppermute | solution.py:270
  15.0 6.6 %collective-permute-start.5 = (bf16[1040,128]{1,0:T(8,128)(2,1)S(1)}, bf16[1040,128]{1,0:T(8,128)(2,1)S(1)}, u32[]{:S(2)}, u32[]{:S(2)}) collective-permute-start(bf16[1040,128]{1,0:T(8,128)(2,1)S(1)} %get-tuple-element.65.refs_0_), channel_id=1, source_target_pairs={{6,2},{7,3},{10,6},{11,7},{14,10},{15,11},{12,14},{13,15},{8,12},{... | collective-permute-start | bytes 798728 | tf_op jit(solution)/shard_map/ppermute | solution.py:270
  18.1 11.0 %collective-permute-start.8 = (bf16[1040,128]{1,0:T(8,128)(2,1)S(1)}, bf16[1040,128]{1,0:T(8,128)(2,1)S(1)}, u32[]{:S(2)}, u32[]{:S(2)}) collective-permute-start(bf16[1040,128]{1,0:T(8,128)(2,1)S(1)} %get-tuple-element.69.refs_1_), channel_id=1, source_target_pairs={{2,6},{3,7},{6,10},{7,11},{10,14},{11,15},{14,12},{15,13},{12,8},{... | collective-permute-start | bytes 798728 | tf_op jit(solution)/shard_map/ppermute | solution.py:270
  19.7 9.5 %collective-permute-start.9 = (bf16[1040,128]{1,0:T(8,128)(2,1)S(1)}, bf16[1040,128]{1,0:T(8,128)(2,1)S(1)}, u32[]{:S(2)}, u32[]{:S(2)}) collective-permute-start(bf16[1040,128]{1,0:T(8,128)(2,1)S(1)} %get-tuple-element.69.refs_1_), channel_id=1, source_target_pairs={{6,2},{7,3},{10,6},{11,7},{14,10},{15,11},{12,14},{13,15},{8,12},{... | collective-permute-start | bytes 798728 | tf_op jit(solution)/shard_map/ppermute | solution.py:270
  21.6 12.4 %collective-permute-start.6 = (bf16[1040,128]{1,0:T(8,128)(2,1)S(1)}, bf16[1040,128]{1,0:T(8,128)(2,1)S(1)}, u32[]{:S(2)}, u32[]{:S(2)}) collective-permute-start(bf16[1040,128]{1,0:T(8,128)(2,1)S(1)} %collective-permute-done.4.refs_0_), channel_id=1, source_target_pairs={{2,6},{3,7},{6,10},{7,11},{10,14},{11,15},{14,12},{15,13},{12,8},{... | collective-permute-start | bytes 798728 | tf_op jit(solution)/shard_map/ppermute | solution.py:270
  23.2 11.6 %collective-permute-start.7 = (bf16[1040,128]{1,0:T(8,128)(2,1)S(1)}, bf16[1040,128]{1,0:T(8,128)(2,1)S(1)}, u32[]{:S(2)}, u32[]{:S(2)}) collective-permute-start(bf16[1040,128]{1,0:T(8,128)(2,1)S(1)} %collective-permute-done.5.refs_1_), channel_id=1, source_target_pairs={{6,2},{7,3},{10,6},{11,7},{14,10},{15,11},{12,14},{13,15},{8,12},{... | collective-permute-start | bytes 798728 | tf_op jit(solution)/shard_map/ppermute | solution.py:270
  23.6 2.8 %copy-start = (bf16[1,1,2048,1536]{3,2,1,0:T(8,128)(2,1)S(1)}, bf16[1,1,2048,1536]{3,2,1,0:T(8,128)(2,1)}, u32[]{:S(2)}) copy-start(bf16[1,1,2048,1536]{3,2,1,0:T(8,128)(2,1)} %param.12) | copy-start | bytes 18874372
  29.2 10.3 %collective-permute-start.10 = (bf16[1040,128]{1,0:T(8,128)(2,1)S(1)}, bf16[1040,128]{1,0:T(8,128)(2,1)S(1)}, u32[]{:S(2)}, u32[]{:S(2)}) collective-permute-start(bf16[1040,128]{1,0:T(8,128)(2,1)S(1)} %collective-permute-done.8.refs_0_), channel_id=1, source_target_pairs={{2,6},{3,7},{6,10},{7,11},{10,14},{11,15},{14,12},{15,13},{12,8},{... | collective-permute-start | bytes 798728 | tf_op jit(solution)/shard_map/ppermute | solution.py:270
  30.8 9.6 %collective-permute-start.11 = (bf16[1040,128]{1,0:T(8,128)(2,1)S(1)}, bf16[1040,128]{1,0:T(8,128)(2,1)S(1)}, u32[]{:S(2)}, u32[]{:S(2)}) collective-permute-start(bf16[1040,128]{1,0:T(8,128)(2,1)S(1)} %collective-permute-done.9.refs_1_), channel_id=1, source_target_pairs={{6,2},{7,3},{10,6},{11,7},{14,10},{15,11},{12,14},{13,15},{8,12},{... | collective-permute-start | bytes 798728 | tf_op jit(solution)/shard_map/ppermute | solution.py:270
  34.7 10.5 %collective-permute-start.12 = (bf16[1040,128]{1,0:T(8,128)(2,1)S(1)}, bf16[1040,128]{1,0:T(8,128)(2,1)S(1)}, u32[]{:S(2)}, u32[]{:S(2)}) collective-permute-start(bf16[1040,128]{1,0:T(8,128)(2,1)S(1)} %collective-permute-done.6.refs_0_), channel_id=1, source_target_pairs={{2,6},{3,7},{6,10},{7,11},{10,14},{11,15},{14,12},{15,13},{12,8},{... | collective-permute-start | bytes 798728 | tf_op jit(solution)/shard_map/ppermute | solution.py:270
  36.3 9.8 %collective-permute-start.13 = (bf16[1040,128]{1,0:T(8,128)(2,1)S(1)}, bf16[1040,128]{1,0:T(8,128)(2,1)S(1)}, u32[]{:S(2)}, u32[]{:S(2)}) collective-permute-start(bf16[1040,128]{1,0:T(8,128)(2,1)S(1)} %collective-permute-done.7.refs_1_), channel_id=1, source_target_pairs={{6,2},{7,3},{10,6},{11,7},{14,10},{15,11},{12,14},{13,15},{8,12},{... | collective-permute-start | bytes 798728 | tf_op jit(solution)/shard_map/ppermute | solution.py:270
  40.4 10.0 %collective-permute-start.15 = (bf16[1040,128]{1,0:T(8,128)(2,1)S(1)}, bf16[1040,128]{1,0:T(8,128)(2,1)S(1)}, u32[]{:S(2)}, u32[]{:S(2)}) collective-permute-start(bf16[1040,128]{1,0:T(8,128)(2,1)S(1)} %collective-permute-done.10.refs_0_), channel_id=1, source_target_pairs={{2,6},{3,7},{6,10},{7,11},{10,14},{11,15},{14,12},{15,13},{12,8},{... | collective-permute-start | bytes 798728 | tf_op jit(solution)/shard_map/ppermute | solution.py:270
  42.0 8.5 %collective-permute-start.16 = (bf16[1040,128]{1,0:T(8,128)(2,1)S(1)}, bf16[1040,128]{1,0:T(8,128)(2,1)S(1)}, u32[]{:S(2)}, u32[]{:S(2)}) collective-permute-start(bf16[1040,128]{1,0:T(8,128)(2,1)S(1)} %collective-permute-done.11.refs_1_), channel_id=1, source_target_pairs={{6,2},{7,3},{10,6},{11,7},{14,10},{15,11},{12,14},{13,15},{8,12},{... | collective-permute-start | bytes 798728 | tf_op jit(solution)/shard_map/ppermute | solution.py:270
  46.2 10.8 %collective-permute-start.18 = (bf16[1040,128]{1,0:T(8,128)(2,1)S(1)}, bf16[1040,128]{1,0:T(8,128)(2,1)S(1)}, u32[]{:S(2)}, u32[]{:S(2)}) collective-permute-start(bf16[1040,128]{1,0:T(8,128)(2,1)S(1)} %collective-permute-done.12.refs_0_), channel_id=1, source_target_pairs={{2,6},{3,7},{6,10},{7,11},{10,14},{11,15},{14,12},{15,13},{12,8},{... | collective-permute-start | bytes 798728 | tf_op jit(solution)/shard_map/ppermute | solution.py:270
  50.5 8.7 %collective-permute-start.19 = (bf16[1040,128]{1,0:T(8,128)(2,1)S(1)}, bf16[1040,128]{1,0:T(8,128)(2,1)S(1)}, u32[]{:S(2)}, u32[]{:S(2)}) collective-permute-start(bf16[1040,128]{1,0:T(8,128)(2,1)S(1)} %collective-permute-done.16.refs_1_), channel_id=1, source_target_pairs={{6,2},{7,3},{10,6},{11,7},{14,10},{15,11},{12,14},{13,15},{8,12},{... | collective-permute-start | bytes 798728 | tf_op jit(solution)/shard_map/ppermute | solution.py:270
  52.0 12.2 %collective-permute-start.14 = (bf16[64,2048]{1,0:T(8,128)(2,1)S(1)}, bf16[64,2048]{1,0:T(8,128)(2,1)S(1)}, u32[]{:S(2)}, u32[]{:S(2)}) collective-permute-start(bf16[64,2048]{1,0:T(8,128)(2,1)S(1)} %convert_element_type.73), channel_id=1, source_target_pairs={{6,2},{7,3},{10,6},{11,7},{14,10},{15,11},{12,14},{13,15},{8,12},{... | collective-permute-start | bytes 786440 | tf_op jit(solution)/shard_map/ppermute | solution.py:270
  56.4 8.3 %collective-permute-start.17 = (bf16[64,2048]{1,0:T(8,128)(2,1)S(1)}, bf16[64,2048]{1,0:T(8,128)(2,1)S(1)}, u32[]{:S(2)}, u32[]{:S(2)}) collective-permute-start(bf16[64,2048]{1,0:T(8,128)(2,1)S(1)} %convert_element_type.74), channel_id=1, source_target_pairs={{2,6},{3,7},{6,10},{7,11},{10,14},{11,15},{14,12},{15,13},{12,8},{... | collective-permute-start | bytes 786440 | tf_op jit(solution)/shard_map/ppermute | solution.py:270
  62.0 6.8 %collective-permute-start.20 = (bf16[64,2048]{1,0:T(8,128)(2,1)S(1)}, bf16[64,2048]{1,0:T(8,128)(2,1)S(1)}, u32[]{:S(2)}, u32[]{:S(2)}) collective-permute-start(bf16[64,2048]{1,0:T(8,128)(2,1)S(1)} %convert_element_type.75), channel_id=1, source_target_pairs={{2,6},{3,7},{6,10},{7,11},{10,14},{11,15},{14,12},{15,13},{12,8},{... | collective-permute-start | bytes 786440 | tf_op jit(solution)/shard_map/ppermute | solution.py:270
  63.7 8.9 %collective-permute-start.21 = (bf16[64,2048]{1,0:T(8,128)(2,1)S(1)}, bf16[64,2048]{1,0:T(8,128)(2,1)S(1)}, u32[]{:S(2)}, u32[]{:S(2)}) collective-permute-start(bf16[64,2048]{1,0:T(8,128)(2,1)S(1)} %convert_element_type.78), channel_id=1, source_target_pairs={{6,2},{7,3},{10,6},{11,7},{14,10},{15,11},{12,14},{13,15},{8,12},{... | collective-permute-start | bytes 786440 | tf_op jit(solution)/shard_map/ppermute | solution.py:270
  72.7 9.3 %collective-permute-start.24 = (bf16[64,2048]{1,0:T(8,128)(2,1)S(1)}, bf16[64,2048]{1,0:T(8,128)(2,1)S(1)}, u32[]{:S(2)}, u32[]{:S(2)}) collective-permute-start(bf16[64,2048]{1,0:T(8,128)(2,1)S(1)} %get-tuple-element.107), channel_id=1, source_target_pairs={{6,2},{7,3},{10,6},{11,7},{14,10},{15,11},{12,14},{13,15},{8,12},{... | collective-permute-start | bytes 786440 | tf_op jit(solution)/shard_map/ppermute | solution.py:270
  73.1 9.4 %collective-permute-start.23 = (bf16[64,2048]{1,0:T(8,128)(2,1)S(1)}, bf16[64,2048]{1,0:T(8,128)(2,1)S(1)}, u32[]{:S(2)}, u32[]{:S(2)}) collective-permute-start(bf16[64,2048]{1,0:T(8,128)(2,1)S(1)} %get-tuple-element.108), channel_id=1, source_target_pairs={{2,6},{3,7},{6,10},{7,11},{10,14},{11,15},{14,12},{15,13},{12,8},{... | collective-permute-start | bytes 786440 | tf_op jit(solution)/shard_map/ppermute | solution.py:270
  77.7 10.1 %collective-permute-start.22 = (bf16[64,2048]{1,0:T(8,128)(2,1)S(1)}, bf16[64,2048]{1,0:T(8,128)(2,1)S(1)}, u32[]{:S(2)}, u32[]{:S(2)}) collective-permute-start(bf16[64,2048]{1,0:T(8,128)(2,1)S(1)} %get-tuple-element.94), channel_id=1, source_target_pairs={{6,2},{7,3},{10,6},{11,7},{14,10},{15,11},{12,14},{13,15},{8,12},{... | collective-permute-start | bytes 786440 | tf_op jit(solution)/shard_map/ppermute | solution.py:270
  78.1 9.8 %collective-permute-start.26 = (bf16[64,2048]{1,0:T(8,128)(2,1)S(1)}, bf16[64,2048]{1,0:T(8,128)(2,1)S(1)}, u32[]{:S(2)}, u32[]{:S(2)}) collective-permute-start(bf16[64,2048]{1,0:T(8,128)(2,1)S(1)} %get-tuple-element.100), channel_id=1, source_target_pairs={{2,6},{3,7},{6,10},{7,11},{10,14},{11,15},{14,12},{15,13},{12,8},{... | collective-permute-start | bytes 786440 | tf_op jit(solution)/shard_map/ppermute | solution.py:270
  82.1 10.5 %collective-permute-start.30 = (bf16[64,2048]{1,0:T(8,128)(2,1)S(1)}, bf16[64,2048]{1,0:T(8,128)(2,1)S(1)}, u32[]{:S(2)}, u32[]{:S(2)}) collective-permute-start(bf16[64,2048]{1,0:T(8,128)(2,1)S(1)} %add_convert_fusion.4), channel_id=1, source_target_pairs={{6,2},{7,3},{10,6},{11,7},{14,10},{15,11},{12,14},{13,15},{8,12},{... | collective-permute-start | bytes 786440 | tf_op jit(solution)/shard_map/ppermute | solution.py:270
  82.5 10.6 %collective-permute-start.28 = (bf16[64,2048]{1,0:T(8,128)(2,1)S(1)}, bf16[64,2048]{1,0:T(8,128)(2,1)S(1)}, u32[]{:S(2)}, u32[]{:S(2)}) collective-permute-start(bf16[64,2048]{1,0:T(8,128)(2,1)S(1)} %add_convert_fusion.5), channel_id=1, source_target_pairs={{2,6},{3,7},{6,10},{7,11},{10,14},{11,15},{14,12},{15,13},{12,8},{... | collective-permute-start | bytes 786440 | tf_op jit(solution)/shard_map/ppermute | solution.py:270
  87.9 7.4 %collective-permute-start.25 = (bf16[64,2048]{1,0:T(8,128)(2,1)S(1)}, bf16[64,2048]{1,0:T(8,128)(2,1)S(1)}, u32[]{:S(2)}, u32[]{:S(2)}) collective-permute-start(bf16[64,2048]{1,0:T(8,128)(2,1)S(1)} %add_convert_fusion.3), channel_id=1, source_target_pairs={{6,2},{7,3},{10,6},{11,7},{14,10},{15,11},{12,14},{13,15},{8,12},{... | collective-permute-start | bytes 786440 | tf_op jit(solution)/shard_map/ppermute | solution.py:270
  88.4 7.0 %collective-permute-start.27 = (bf16[64,2048]{1,0:T(8,128)(2,1)S(1)}, bf16[64,2048]{1,0:T(8,128)(2,1)S(1)}, u32[]{:S(2)}, u32[]{:S(2)}) collective-permute-start(bf16[64,2048]{1,0:T(8,128)(2,1)S(1)} %add_convert_fusion.2), channel_id=1, source_target_pairs={{2,6},{3,7},{6,10},{7,11},{10,14},{11,15},{14,12},{15,13},{12,8},{... | collective-permute-start | bytes 786440 | tf_op jit(solution)/shard_map/ppermute | solution.py:270
  92.6 6.4 %collective-permute-start.31 = (bf16[64,2048]{1,0:T(8,128)(2,1)S(1)}, bf16[64,2048]{1,0:T(8,128)(2,1)S(1)}, u32[]{:S(2)}, u32[]{:S(2)}) collective-permute-start(bf16[64,2048]{1,0:T(8,128)(2,1)S(1)} %add_convert_fusion), channel_id=1, source_target_pairs={{6,2},{7,3},{10,6},{11,7},{14,10},{15,11},{12,14},{13,15},{8,12},{... | collective-permute-start | bytes 786440 | tf_op jit(solution)/shard_map/ppermute | solution.py:270
  93.2 6.4 %collective-permute-start.29 = (bf16[64,2048]{1,0:T(8,128)(2,1)S(1)}, bf16[64,2048]{1,0:T(8,128)(2,1)S(1)}, u32[]{:S(2)}, u32[]{:S(2)}) collective-permute-start(bf16[64,2048]{1,0:T(8,128)(2,1)S(1)} %add_convert_fusion.1), channel_id=1, source_target_pairs={{2,6},{3,7},{6,10},{7,11},{10,14},{11,15},{14,12},{15,13},{12,8},{... | collective-permute-start | bytes 786440 | tf_op jit(solution)/shard_map/ppermute | solution.py:270

commit v13 on v11

--- a/solution.py
+++ b/solution.py
@@ -283,7 +283,11 @@
     downs = [packed] + [[None, None] for _ in range(hops)]
 
     def pass_on(s, c, after):
-        rising, falling = lax.optimization_barrier((ups[s][c], downs[s][c], after))[:2]
+        if s < 2:
+            rising = lax.optimization_barrier((ups[s][c], after))[0]
+            falling = lax.optimization_barrier((downs[s][c], after))[0]
+        else:
+            rising, falling = lax.optimization_barrier((ups[s][c], downs[s][c], after))[:2]
         if s < hops - 1 or c == 0:
             ups[s + 1][c] = move(rising, up)
         if s < hops - 1 or c == 1:

time: 99.1 us -> 100 us (level)
  waiting for transfers between devices: 29.8 us -> 31.7 us
    ppermute x30, waiting for transfers between devices: 25.3 us -> 27.2 us  [move(): return lax.ppermute(value, 'expert', pairs)]
  transfers between devices with their start and end apart: 32 -> 32, of which waited for: 15 -> 17; matrix products, arithmetic and copies ran while one was open for 2% -> 2% of each run, Pallas kernels for 23% -> 22%
where the time goes in v13:
time: 100 us
  starting transfers between devices  36.8 us (37%)
  waiting for transfers between devices  31.7 us (32%)
  Pallas kernels  23.4 us (23%)
  local copies, waits for them, and re-layouts  7.22 us (7%)
    ppermute x30, starting transfers between devices, move(): return lax.ppermute(value, 'expert', pairs)  30.6 us
    ppermute x30, waiting for transfers between devices, move(): return lax.ppermute(value, 'expert', pairs)  27.2 us
    pallas_call x8, Pallas kernels, expert_rows(): pl.pallas_call(functools.partial(mlp_kernel, parts=len(payloads), adds=le...  22.1 us
    ppermute x2, starting transfers between devices, from_behind(): return lax.ppermute(value, axis, pairs)  6.18 us
    unnamed x12, local copies, waits for them, and re-layouts  5.89 us
    ppermute x2, waiting for transfers between devices, from_behind(): return lax.ppermute(value, axis, pairs)  4.5 us
  transfers between devices with their start and end apart: 32, of which 17 were waited for; matrix products, arithmetic and copies ran while one was open for 2% of the time, Pallas kernels for 22%

profile of v13, /device:TPU:0, one launch (start us, length us, event | category | flops | bytes accessed | tf_op | source)
XLA Modules:
  0.0 100.1 jit_solution(14548500400680157112)
XLA Ops:
  0.0 0.5 collective-permute-start.2
  0.5 1.3 %slice_bitcast_fusion = (bf16[64,2048]{1,0:T(8,128)(2,1)S(1)}, bf16[64,2048]{1,0:T(8,128)(2,1)S(1)}) fusion(bf16[1,128,2048]{2,1,0:T(8,128)(2,1)} %param.8), kind=kLoop, calls=%fused_computation.10 | loop fusion | bytes 1048576 | tf_op jit(solution)/shard_map/squeeze | solution.py:277
  1.9 4.9 %collective-permute-start = (bf16[64,2048]{1,0:T(8,128)(2,1)S(1)}, bf16[64,2048]{1,0:T(8,128)(2,1)S(1)}, u32[]{:S(2)}, u32[]{:S(2)}) collective-permute-start(bf16[64,2048]{1,0:T(8,128)(2,1)S(1)} %get-tuple-element.88), channel_id=1, source_target_pairs={{0,16},{1,17},{2,18},{3,19},{4,20},{5,21},{6,22},{7,23},{8,24},{9,... | collective-permute-start | bytes 786440 | tf_op jit(solution)/shard_map/ppermute | solution.py:20
  6.7 1.3 %collective-permute-start.1 = (bf16[64,2048]{1,0:T(8,128)(2,1)S(1)}, bf16[64,2048]{1,0:T(8,128)(2,1)S(1)}, u32[]{:S(2)}, u32[]{:S(2)}) collective-permute-start(bf16[64,2048]{1,0:T(8,128)(2,1)S(1)} %get-tuple-element.87), channel_id=1, source_target_pairs={{0,16},{1,17},{2,18},{3,19},{4,20},{5,21},{6,22},{7,23},{8,24},{9,... | collective-permute-start | bytes 786440 | tf_op jit(solution)/shard_map/ppermute | solution.py:20
  8.1 1.0 %copy-done.2 = bf16[128,2048]{1,0:T(8,128)(2,1)S(1)} copy-done((bf16[128,2048]{1,0:T(8,128)(2,1)S(1)}, bf16[128,2048]{1,0:T(8,128)(2,1)}, u32[]{:S(2)}) %copy-start.2) | copy-done | bytes 524312
  9.1 0.7 copy-done.3
  9.8 0.7 copy-done.4
  10.5 0.7 copy-done.5
  11.2 0.2 base_rows.1
  11.4 2.0 %collective-permute-done.arrived_ref = bf16[64,2048]{1,0:T(8,128)(2,1)S(1)} collective-permute-done((bf16[64,2048]{1,0:T(8,128)(2,1)S(1)}, bf16[64,2048]{1,0:T(8,128)(2,1)S(1)}, u32[]{:S(2)}, u32[]{:S(2)}) %collective-permute-start) | collective-permute-done | bytes 262176 | tf_op jit(solution)/shard_map/ppermute | solution.py:20
  13.5 1.5 %collective-permute-start.4 = (bf16[1040,128]{1,0:T(8,128)(2,1)S(1)}, bf16[1040,128]{1,0:T(8,128)(2,1)S(1)}, u32[]{:S(2)}, u32[]{:S(2)}) collective-permute-start(bf16[1040,128]{1,0:T(8,128)(2,1)S(1)} %get-tuple-element.51.refs_0_), channel_id=1, source_target_pairs={{2,6},{3,7},{6,10},{7,11},{10,14},{11,15},{14,12},{15,13},{12,8},{... | collective-permute-start | bytes 798728 | tf_op jit(solution)/shard_map/ppermute | solution.py:270
  15.0 0.5 collective-permute-start.6
  15.5 2.5 %collective-permute-done.1.arrived_ref = bf16[64,2048]{1,0:T(8,128)(2,1)S(1)} collective-permute-done((bf16[64,2048]{1,0:T(8,128)(2,1)S(1)}, bf16[64,2048]{1,0:T(8,128)(2,1)S(1)}, u32[]{:S(2)}, u32[]{:S(2)}) %collective-permute-start.1) | collective-permute-done | bytes 262176 | tf_op jit(solution)/shard_map/ppermute | solution.py:20
  18.2 1.6 %collective-permute-start.9 = (bf16[1040,128]{1,0:T(8,128)(2,1)S(1)}, bf16[1040,128]{1,0:T(8,128)(2,1)S(1)}, u32[]{:S(2)}, u32[]{:S(2)}) collective-permute-start(bf16[1040,128]{1,0:T(8,128)(2,1)S(1)} %get-tuple-element.55.refs_1_), channel_id=1, source_target_pairs={{6,2},{7,3},{10,6},{11,7},{14,10},{15,11},{12,14},{13,15},{8,12},{... | collective-permute-start | bytes 798728 | tf_op jit(solution)/shard_map/ppermute | solution.py:270
  19.8 0.4 collective-permute-start.8
  20.2 1.5 %collective-permute-start.5 = (bf16[1040,128]{1,0:T(8,128)(2,1)S(1)}, bf16[1040,128]{1,0:T(8,128)(2,1)S(1)}, u32[]{:S(2)}, u32[]{:S(2)}) collective-permute-start(bf16[1040,128]{1,0:T(8,128)(2,1)S(1)} %collective-permute-done.4.refs_0_), channel_id=1, source_target_pairs={{2,6},{3,7},{6,10},{7,11},{10,14},{11,15},{14,12},{15,13},{12,8},{... | collective-permute-start | bytes 798728 | tf_op jit(solution)/shard_map/ppermute | solution.py:270
  21.7 1.1 %collective-permute-done.6.refs_1_ = bf16[1040,128]{1,0:T(8,128)(2,1)S(1)} collective-permute-done((bf16[1040,128]{1,0:T(8,128)(2,1)S(1)}, bf16[1040,128]{1,0:T(8,128)(2,1)S(1)}, u32[]{:S(2)}, u32[]{:S(2)}) %collective-permute-start.6) | collective-permute-done | bytes 266272 | tf_op jit(solution)/shard_map/ppermute | solution.py:270
  22.8 2.8 %copy-done = bf16[1,1,2048,1536]{3,2,1,0:T(8,128)(2,1)S(1)} copy-done((bf16[1,1,2048,1536]{3,2,1,0:T(8,128)(2,1)S(1)}, bf16[1,1,2048,1536]{3,2,1,0:T(8,128)(2,1)}, u32[]{:S(2)}) %copy-start) | copy-done | bytes 6291480
  25.6 2.7 %expert_rows.8 = (f32[64,2048]{1,0:T(8,128)S(1)}, f32[64,2048]{1,0:T(8,128)S(1)}) custom-call(s32[1]{0:T(128)} %bitcast.6.expert_ref, bf16[1040,128]{1,0:T(8,128)(2,1)S(1)} %collective-permute-done.4.refs_0_, bf16[1040,128]{1,0:T(8,128)(2,1)S(1)} %collective-permute-done.6.refs_1_, bf16[2048,1536]{1,0:T(8,128)(2,1)S(1)} %bitcast.16, ...), custom_call_target="tpu_custom_call" | custom-call | flops 2415919104 | bytes 1572864 | tf_op jit(solution)/shard_map/expert_rows/pallas_call | solution.py:204
  28.4 0.2 collective-permute-done.9.refs_1_
  28.5 1.0 collective-permute-start.11
  29.5 1.1 %collective-permute-start.10 = (bf16[1040,128]{1,0:T(8,128)(2,1)S(1)}, bf16[1040,128]{1,0:T(8,128)(2,1)S(1)}, u32[]{:S(2)}, u32[]{:S(2)}) collective-permute-start(bf16[1040,128]{1,0:T(8,128)(2,1)S(1)} %collective-permute-done.8.refs_0_), channel_id=1, source_target_pairs={{2,6},{3,7},{6,10},{7,11},{10,14},{11,15},{14,12},{15,13},{12,8},{... | collective-permute-start | bytes 798728 | tf_op jit(solution)/shard_map/ppermute | solution.py:270
  30.5 2.8 %expert_rows.9 = (f32[64,2048]{1,0:T(8,128)S(1)}, f32[64,2048]{1,0:T(8,128)S(1)}) custom-call(s32[1]{0:T(128)} %bitcast.6.expert_ref, bf16[1040,128]{1,0:T(8,128)(2,1)S(1)} %collective-permute-done.8.refs_0_, bf16[1040,128]{1,0:T(8,128)(2,1)S(1)} %collective-permute-done.9.refs_1_, bf16[2048,1536]{1,0:T(8,128)(2,1)S(1)} %bitcast.17, ...), custom_call_target="tpu_custom_call" | custom-call | flops 2415919104 | bytes 1572864 | tf_op jit(solution)/shard_map/expert_rows/pallas_call | solution.py:204
  33.3 1.5 %collective-permute-done.5.refs_0_ = bf16[1040,128]{1,0:T(8,128)(2,1)S(1)} collective-permute-done((bf16[1040,128]{1,0:T(8,128)(2,1)S(1)}, bf16[1040,128]{1,0:T(8,128)(2,1)S(1)}, u32[]{:S(2)}, u32[]{:S(2)}) %collective-permute-start.5) | collective-permute-done | bytes 266272 | tf_op jit(solution)/shard_map/ppermute | solution.py:270
  34.8 1.1 %collective-permute-start.12 = (bf16[1040,128]{1,0:T(8,128)(2,1)S(1)}, bf16[1040,128]{1,0:T(8,128)(2,1)S(1)}, u32[]{:S(2)}, u32[]{:S(2)}) collective-permute-start(bf16[1040,128]{1,0:T(8,128)(2,1)S(1)} %collective-permute-done.5.refs_0_), channel_id=1, source_target_pairs={{2,6},{3,7},{6,10},{7,11},{10,14},{11,15},{14,12},{15,13},{12,8},{... | collective-permute-start | bytes 798728 | tf_op jit(solution)/shard_map/ppermute | solution.py:270
  35.9 1.0 collective-permute-start.13
  36.8 2.7 %expert_rows.10 = (f32[64,2048]{1,0:T(8,128)S(1)}, f32[64,2048]{1,0:T(8,128)S(1)}) custom-call(s32[1]{0:T(128)} %bitcast.6.expert_ref, bf16[1040,128]{1,0:T(8,128)(2,1)S(1)} %collective-permute-done.5.refs_0_, bf16[1040,128]{1,0:T(8,128)(2,1)S(1)} %collective-permute-done.7.refs_1_, bf16[2048,1536]{1,0:T(8,128)(2,1)S(1)} %bitcast.18, ...), custom_call_target="tpu_custom_call" | custom-call | flops 2415919104 | bytes 1572864 | tf_op jit(solution)/shard_map/expert_rows/pallas_call | solution.py:204
  39.6 0.3 collective-permute-done.11.refs_1_
  39.9 0.6 collective-permute-done.10.refs_0_
  40.5 1.1 %collective-permute-start.15 = (bf16[1040,128]{1,0:T(8,128)(2,1)S(1)}, bf16[1040,128]{1,0:T(8,128)(2,1)S(1)}, u32[]{:S(2)}, u32[]{:S(2)}) collective-permute-start(bf16[1040,128]{1,0:T(8,128)(2,1)S(1)} %collective-permute-done.10.refs_0_), channel_id=1, source_target_pairs={{2,6},{3,7},{6,10},{7,11},{10,14},{11,15},{14,12},{15,13},{12,8},{... | collective-permute-start | bytes 798728 | tf_op jit(solution)/shard_map/ppermute | solution.py:270
  41.6 0.9 collective-permute-start.16
  42.5 2.7 %expert_rows.11 = (f32[64,2048]{1,0:T(8,128)S(1)}, f32[64,2048]{1,0:T(8,128)S(1)}) custom-call(s32[1]{0:T(128)} %bitcast.6.expert_ref, bf16[1040,128]{1,0:T(8,128)(2,1)S(1)} %collective-permute-done.10.refs_0_, bf16[1040,128]{1,0:T(8,128)(2,1)S(1)} %collective-permute-done.11.refs_1_, bf16[2048,1536]{1,0:T(8,128)(2,1)S(1)} %bitcast.19, ...), custom_call_target="tpu_custom_call" | custom-call | flops 2415919104 | bytes 1572864 | tf_op jit(solution)/shard_map/expert_rows/pallas_call | solution.py:204
  45.3 0.9 collective-permute-done.12.refs_0_
  46.2 1.1 %collective-permute-start.18 = (bf16[1040,128]{1,0:T(8,128)(2,1)S(1)}, bf16[1040,128]{1,0:T(8,128)(2,1)S(1)}, u32[]{:S(2)}, u32[]{:S(2)}) collective-permute-start(bf16[1040,128]{1,0:T(8,128)(2,1)S(1)} %collective-permute-done.12.refs_0_), channel_id=1, source_target_pairs={{2,6},{3,7},{6,10},{7,11},{10,14},{11,15},{14,12},{15,13},{12,8},{... | collective-permute-start | bytes 798728 | tf_op jit(solution)/shard_map/ppermute | solution.py:270
  47.3 2.7 %expert_rows.12 = (f32[64,2048]{1,0:T(8,128)S(1)}, f32[64,2048]{1,0:T(8,128)S(1)}) custom-call(s32[1]{0:T(128)} %bitcast.6.expert_ref, bf16[1040,128]{1,0:T(8,128)(2,1)S(1)} %collective-permute-done.12.refs_0_, bf16[1040,128]{1,0:T(8,128)(2,1)S(1)} %collective-permute-done.13.refs_1_, bf16[2048,1536]{1,0:T(8,128)(2,1)S(1)} %bitcast.20, ...), custom_call_target="tpu_custom_call" | custom-call | flops 2415919104 | bytes 1572864 | tf_op jit(solution)/shard_map/expert_rows/pallas_call | solution.py:204
  50.1 1.9 %collective-permute-done.15.refs_0_ = bf16[1040,128]{1,0:T(8,128)(2,1)S(1)} collective-permute-done((bf16[1040,128]{1,0:T(8,128)(2,1)S(1)}, bf16[1040,128]{1,0:T(8,128)(2,1)S(1)}, u32[]{:S(2)}, u32[]{:S(2)}) %collective-permute-start.15) | collective-permute-done | bytes 266272 | tf_op jit(solution)/shard_map/ppermute | solution.py:270
  51.9 1.6 %collective-permute-start.19 = (bf16[1040,128]{1,0:T(8,128)(2,1)S(1)}, bf16[1040,128]{1,0:T(8,128)(2,1)S(1)}, u32[]{:S(2)}, u32[]{:S(2)}) collective-permute-start(bf16[1040,128]{1,0:T(8,128)(2,1)S(1)} %collective-permute-done.16.refs_1_), channel_id=1, source_target_pairs={{6,2},{7,3},{10,6},{11,7},{14,10},{15,11},{12,14},{13,15},{8,12},{... | collective-permute-start | bytes 798728 | tf_op jit(solution)/shard_map/ppermute | solution.py:270
  53.5 1.6 %collective-permute-start.14 = (bf16[64,2048]{1,0:T(8,128)(2,1)S(1)}, bf16[64,2048]{1,0:T(8,128)(2,1)S(1)}, u32[]{:S(2)}, u32[]{:S(2)}) collective-permute-start(bf16[64,2048]{1,0:T(8,128)(2,1)S(1)} %convert_element_type.73), channel_id=1, source_target_pairs={{6,2},{7,3},{10,6},{11,7},{14,10},{15,11},{12,14},{13,15},{8,12},{... | collective-permute-start | bytes 786440 | tf_op jit(solution)/shard_map/ppermute | solution.py:270
  55.2 2.8 %expert_rows.13 = (f32[64,2048]{1,0:T(8,128)S(1)}, f32[64,2048]{1,0:T(8,128)S(1)}) custom-call(s32[1]{0:T(128)} %bitcast.6.expert_ref, bf16[1040,128]{1,0:T(8,128)(2,1)S(1)} %collective-permute-done.15.refs_0_, bf16[1040,128]{1,0:T(8,128)(2,1)S(1)} %collective-permute-done.16.refs_1_, bf16[2048,1536]{1,0:T(8,128)(2,1)S(1)} %bitcast.21, ...), custom_call_target="tpu_custom_call" | custom-call | flops 2415919104 | bytes 1572864 | tf_op jit(solution)/shard_map/expert_rows/pallas_call | solution.py:204
  58.0 0.5 collective-permute-start.17
  58.5 1.3 %collective-permute-done.19.refs_1_ = bf16[1040,128]{1,0:T(8,128)(2,1)S(1)} collective-permute-done((bf16[1040,128]{1,0:T(8,128)(2,1)S(1)}, bf16[1040,128]{1,0:T(8,128)(2,1)S(1)}, u32[]{:S(2)}, u32[]{:S(2)}) %collective-permute-start.19) | collective-permute-done | bytes 266272 | tf_op jit(solution)/shard_map/ppermute | solution.py:270
  59.8 2.7 %expert_rows.14 = (f32[64,2048]{1,0:T(8,128)S(1)}, f32[64,2048]{1,0:T(8,128)S(1)}) custom-call(s32[1]{0:T(128)} %bitcast.6.expert_ref, bf16[1040,128]{1,0:T(8,128)(2,1)S(1)} %collective-permute-done.18.refs_0_, bf16[1040,128]{1,0:T(8,128)(2,1)S(1)} %collective-permute-done.19.refs_1_, bf16[2048,1536]{1,0:T(8,128)(2,1)S(1)} %bitcast.22, ...), custom_call_target="tpu_custom_call" | custom-call | flops 2415919104 | bytes 1572864 | tf_op jit(solution)/shard_map/expert_rows/pallas_call | solution.py:204
  62.6 0.7 collective-permute-start.23
  63.3 1.7 %collective-permute-start.21 = (bf16[64,2048]{1,0:T(8,128)(2,1)S(1)}, bf16[64,2048]{1,0:T(8,128)(2,1)S(1)}, u32[]{:S(2)}, u32[]{:S(2)}) collective-permute-start(bf16[64,2048]{1,0:T(8,128)(2,1)S(1)} %convert_element_type.75), channel_id=1, source_target_pairs={{2,6},{3,7},{6,10},{7,11},{10,14},{11,15},{14,12},{15,13},{12,8},{... | collective-permute-start | bytes 786440 | tf_op jit(solution)/shard_map/ppermute | solution.py:270
  65.0 0.4 collective-permute-done.14.refs_8_
  65.4 1.8 %collective-permute-done.17.refs_9_ = bf16[64,2048]{1,0:T(8,128)(2,1)S(1)} collective-permute-done((bf16[64,2048]{1,0:T(8,128)(2,1)S(1)}, bf16[64,2048]{1,0:T(8,128)(2,1)S(1)}, u32[]{:S(2)}, u32[]{:S(2)}) %collective-permute-start.17) | collective-permute-done | bytes 262176 | tf_op jit(solution)/shard_map/ppermute | solution.py:270
  67.2 2.9 %expert_rows.15 = (f32[64,2048]{1,0:T(8,128)S(1)}, f32[64,2048]{1,0:T(8,128)S(1)}, bf16[64,2048]{1,0:T(8,128)(2,1)S(1)}, bf16[64,2048]{1,0:T(8,128)(2,1)S(1)}) custom-call(s32[1]{0:T(128)} %bitcast.6.expert_ref, bf16[1040,128]{1,0:T(8,128)(2,1)S(1)} %get-tuple-element.51.refs_0_, bf16[1040,128]{1,0:T(8,128)(2,1)S(1)} %get-tuple-element.55.refs_1_, ...), custom_call_target="tpu_custom_call" | custom-call | flops 2415919104 | bytes 1572864 | tf_op jit(solution)/shard_map/expert_rows/pallas_call | solution.py:204
  70.1 0.5 collective-permute-start.26
  70.6 1.6 %collective-permute-start.20 = (bf16[64,2048]{1,0:T(8,128)(2,1)S(1)}, bf16[64,2048]{1,0:T(8,128)(2,1)S(1)}, u32[]{:S(2)}, u32[]{:S(2)}) collective-permute-start(bf16[64,2048]{1,0:T(8,128)(2,1)S(1)} %get-tuple-element.74), channel_id=1, source_target_pairs={{6,2},{7,3},{10,6},{11,7},{14,10},{15,11},{12,14},{13,15},{8,12},{... | collective-permute-start | bytes 786440 | tf_op jit(solution)/shard_map/ppermute | solution.py:270
  72.3 1.5 %collective-permute-start.24 = (bf16[64,2048]{1,0:T(8,128)(2,1)S(1)}, bf16[64,2048]{1,0:T(8,128)(2,1)S(1)}, u32[]{:S(2)}, u32[]{:S(2)}) collective-permute-start(bf16[64,2048]{1,0:T(8,128)(2,1)S(1)} %add_convert_fusion.5), channel_id=1, source_target_pairs={{6,2},{7,3},{10,6},{11,7},{14,10},{15,11},{12,14},{13,15},{8,12},{... | collective-permute-start | bytes 786440 | tf_op jit(solution)/shard_map/ppermute | solution.py:270
  73.9 0.6 collective-permute-start.22
  74.5 7.7 %collective-permute-done.24 = bf16[64,2048]{1,0:T(8,128)(2,1)S(1)} collective-permute-done((bf16[64,2048]{1,0:T(8,128)(2,1)S(1)}, bf16[64,2048]{1,0:T(8,128)(2,1)S(1)}, u32[]{:S(2)}, u32[]{:S(2)}) %collective-permute-start.24) | collective-permute-done | bytes 262176 | tf_op jit(solution)/shard_map/ppermute | solution.py:270
  82.2 2.5 %collective-permute-start.30 = (bf16[64,2048]{1,0:T(8,128)(2,1)S(1)}, bf16[64,2048]{1,0:T(8,128)(2,1)S(1)}, u32[]{:S(2)}, u32[]{:S(2)}) collective-permute-start(bf16[64,2048]{1,0:T(8,128)(2,1)S(1)} %add_convert_fusion.4), channel_id=1, source_target_pairs={{6,2},{7,3},{10,6},{11,7},{14,10},{15,11},{12,14},{13,15},{8,12},{... | collective-permute-start | bytes 786440 | tf_op jit(solution)/shard_map/ppermute | solution.py:270
  84.9 0.8 collective-permute-start.27
  85.8 1.5 %collective-permute-start.25 = (bf16[64,2048]{1,0:T(8,128)(2,1)S(1)}, bf16[64,2048]{1,0:T(8,128)(2,1)S(1)}, u32[]{:S(2)}, u32[]{:S(2)}) collective-permute-start(bf16[64,2048]{1,0:T(8,128)(2,1)S(1)} %add_convert_fusion.3), channel_id=1, source_target_pairs={{6,2},{7,3},{10,6},{11,7},{14,10},{15,11},{12,14},{13,15},{8,12},{... | collective-permute-start | bytes 786440 | tf_op jit(solution)/shard_map/ppermute | solution.py:270
  87.3 4.2 %collective-permute-done.30 = bf16[64,2048]{1,0:T(8,128)(2,1)S(1)} collective-permute-done((bf16[64,2048]{1,0:T(8,128)(2,1)S(1)}, bf16[64,2048]{1,0:T(8,128)(2,1)S(1)}, u32[]{:S(2)}, u32[]{:S(2)}) %collective-permute-start.30) | collective-permute-done | bytes 262176 | tf_op jit(solution)/shard_map/ppermute | solution.py:270
  91.5 1.2 %collective-permute-start.31 = (bf16[64,2048]{1,0:T(8,128)(2,1)S(1)}, bf16[64,2048]{1,0:T(8,128)(2,1)S(1)}, u32[]{:S(2)}, u32[]{:S(2)}) collective-permute-start(bf16[64,2048]{1,0:T(8,128)(2,1)S(1)} %add_convert_fusion), channel_id=1, source_target_pairs={{6,2},{7,3},{10,6},{11,7},{14,10},{15,11},{12,14},{13,15},{8,12},{... | collective-permute-start | bytes 786440 | tf_op jit(solution)/shard_map/ppermute | solution.py:270
  92.8 0.9 collective-permute-start.29
  93.7 1.1 %collective-permute-done.27 = bf16[64,2048]{1,0:T(8,128)(2,1)S(1)} collective-permute-done((bf16[64,2048]{1,0:T(8,128)(2,1)S(1)}, bf16[64,2048]{1,0:T(8,128)(2,1)S(1)}, u32[]{:S(2)}, u32[]{:S(2)}) %collective-permute-start.27) | collective-permute-done | bytes 262176 | tf_op jit(solution)/shard_map/ppermute | solution.py:270
  94.8 0.1 add_add_fusion.near1_ref
  94.9 0.1 add_add_fusion.1.near0_ref
  95.0 2.9 %collective-permute-done.31.total1_ref = bf16[64,2048]{1,0:T(8,128)(2,1)S(1)} collective-permute-done((bf16[64,2048]{1,0:T(8,128)(2,1)S(1)}, bf16[64,2048]{1,0:T(8,128)(2,1)S(1)}, u32[]{:S(2)}, u32[]{:S(2)}) %collective-permute-start.31) | collective-permute-done | bytes 262176 | tf_op jit(solution)/shard_map/ppermute | solution.py:270
  97.9 1.3 %collective-permute-done.29.total0_ref = bf16[64,2048]{1,0:T(8,128)(2,1)S(1)} collective-permute-done((bf16[64,2048]{1,0:T(8,128)(2,1)S(1)}, bf16[64,2048]{1,0:T(8,128)(2,1)S(1)}, u32[]{:S(2)}, u32[]{:S(2)}) %collective-permute-start.29) | collective-permute-done | bytes 262176 | tf_op jit(solution)/shard_map/ppermute | solution.py:270
  99.2 0.9 last_rows.1
  (39 shorter events, 0.9 us)
Async XLA Ops:
  0.0 22.8 %copy-start.1 = (bf16[1,1,768,2048]{3,2,1,0:T(8,128)(2,1)S(1)}, bf16[1,1,768,2048]{3,2,1,0:T(8,128)(2,1)}, u32[]{:S(2)}) copy-start(bf16[1,1,768,2048]{3,2,1,0:T(8,128)(2,1)} %param.13) | copy-start | bytes 9437188
  0.0 18.1 %collective-permute-start.2 = (bf16[2048,1536]{1,0:T(8,128)(2,1)}, bf16[2048,1536]{1,0:T(8,128)(2,1)S(1)}, u32[]{:S(2)}, u32[]{:S(2)}) collective-permute-start(bf16[2048,1536]{1,0:T(8,128)(2,1)} %bitcast.15), channel_id=1, source_target_pairs={{0,1},{1,0},{2,3},{3,2},{4,5},{5,4},{6,7},{7,6},{8,9},{9,8},{10,11... | collective-permute-start | bytes 18874376 | tf_op jit(solution)/shard_map/ppermute | solution.py:270
  0.5 17.7 %collective-permute-start.3 = (bf16[768,2048]{1,0:T(8,128)(2,1)}, bf16[768,2048]{1,0:T(8,128)(2,1)S(1)}, u32[]{:S(2)}, u32[]{:S(2)}) collective-permute-start(bf16[768,2048]{1,0:T(8,128)(2,1)} %bitcast.24), channel_id=1, source_target_pairs={{0,1},{1,0},{2,3},{3,2},{4,5},{5,4},{6,7},{7,6},{8,9},{9,8},{10,11... | collective-permute-start | bytes 9437192 | tf_op jit(solution)/shard_map/ppermute | solution.py:270
  1.9 11.5 %collective-permute-start = (bf16[64,2048]{1,0:T(8,128)(2,1)S(1)}, bf16[64,2048]{1,0:T(8,128)(2,1)S(1)}, u32[]{:S(2)}, u32[]{:S(2)}) collective-permute-start(bf16[64,2048]{1,0:T(8,128)(2,1)S(1)} %get-tuple-element.88), channel_id=1, source_target_pairs={{0,16},{1,17},{2,18},{3,19},{4,20},{5,21},{6,22},{7,23},{8,24},{9,... | collective-permute-start | bytes 786440 | tf_op jit(solution)/shard_map/ppermute | solution.py:20
  6.7 11.3 %collective-permute-start.1 = (bf16[64,2048]{1,0:T(8,128)(2,1)S(1)}, bf16[64,2048]{1,0:T(8,128)(2,1)S(1)}, u32[]{:S(2)}, u32[]{:S(2)}) collective-permute-start(bf16[64,2048]{1,0:T(8,128)(2,1)S(1)} %get-tuple-element.87), channel_id=1, source_target_pairs={{0,16},{1,17},{2,18},{3,19},{4,20},{5,21},{6,22},{7,23},{8,24},{9,... | collective-permute-start | bytes 786440 | tf_op jit(solution)/shard_map/ppermute | solution.py:20
  8.1 1.0 %copy-start.2 = (bf16[128,2048]{1,0:T(8,128)(2,1)S(1)}, bf16[128,2048]{1,0:T(8,128)(2,1)}, u32[]{:S(2)}) copy-start(bf16[128,2048]{1,0:T(8,128)(2,1)} %fresh_ref.1) | copy-start | bytes 1572868
  9.1 0.7 copy-start.3
  9.8 0.7 copy-start.4
  10.5 0.7 copy-start.5
  13.5 6.8 %collective-permute-start.4 = (bf16[1040,128]{1,0:T(8,128)(2,1)S(1)}, bf16[1040,128]{1,0:T(8,128)(2,1)S(1)}, u32[]{:S(2)}, u32[]{:S(2)}) collective-permute-start(bf16[1040,128]{1,0:T(8,128)(2,1)S(1)} %get-tuple-element.51.refs_0_), channel_id=1, source_target_pairs={{2,6},{3,7},{6,10},{7,11},{10,14},{11,15},{14,12},{15,13},{12,8},{... | collective-permute-start | bytes 798728 | tf_op jit(solution)/shard_map/ppermute | solution.py:270
  15.0 7.8 %collective-permute-start.6 = (bf16[1040,128]{1,0:T(8,128)(2,1)S(1)}, bf16[1040,128]{1,0:T(8,128)(2,1)S(1)}, u32[]{:S(2)}, u32[]{:S(2)}) collective-permute-start(bf16[1040,128]{1,0:T(8,128)(2,1)S(1)} %get-tuple-element.51.refs_0_), channel_id=1, source_target_pairs={{6,2},{7,3},{10,6},{11,7},{14,10},{15,11},{12,14},{13,15},{8,12},{... | collective-permute-start | bytes 798728 | tf_op jit(solution)/shard_map/ppermute | solution.py:270
  18.2 10.4 %collective-permute-start.9 = (bf16[1040,128]{1,0:T(8,128)(2,1)S(1)}, bf16[1040,128]{1,0:T(8,128)(2,1)S(1)}, u32[]{:S(2)}, u32[]{:S(2)}) collective-permute-start(bf16[1040,128]{1,0:T(8,128)(2,1)S(1)} %get-tuple-element.55.refs_1_), channel_id=1, source_target_pairs={{6,2},{7,3},{10,6},{11,7},{14,10},{15,11},{12,14},{13,15},{8,12},{... | collective-permute-start | bytes 798728 | tf_op jit(solution)/shard_map/ppermute | solution.py:270
  19.8 9.7 %collective-permute-start.8 = (bf16[1040,128]{1,0:T(8,128)(2,1)S(1)}, bf16[1040,128]{1,0:T(8,128)(2,1)S(1)}, u32[]{:S(2)}, u32[]{:S(2)}) collective-permute-start(bf16[1040,128]{1,0:T(8,128)(2,1)S(1)} %get-tuple-element.55.refs_1_), channel_id=1, source_target_pairs={{2,6},{3,7},{6,10},{7,11},{10,14},{11,15},{14,12},{15,13},{12,8},{... | collective-permute-start | bytes 798728 | tf_op jit(solution)/shard_map/ppermute | solution.py:270
  20.2 14.6 %collective-permute-start.5 = (bf16[1040,128]{1,0:T(8,128)(2,1)S(1)}, bf16[1040,128]{1,0:T(8,128)(2,1)S(1)}, u32[]{:S(2)}, u32[]{:S(2)}) collective-permute-start(bf16[1040,128]{1,0:T(8,128)(2,1)S(1)} %collective-permute-done.4.refs_0_), channel_id=1, source_target_pairs={{2,6},{3,7},{6,10},{7,11},{10,14},{11,15},{14,12},{15,13},{12,8},{... | collective-permute-start | bytes 798728 | tf_op jit(solution)/shard_map/ppermute | solution.py:270
  22.8 12.0 %collective-permute-start.7 = (bf16[1040,128]{1,0:T(8,128)(2,1)S(1)}, bf16[1040,128]{1,0:T(8,128)(2,1)S(1)}, u32[]{:S(2)}, u32[]{:S(2)}) collective-permute-start(bf16[1040,128]{1,0:T(8,128)(2,1)S(1)} %collective-permute-done.6.refs_1_), channel_id=1, source_target_pairs={{6,2},{7,3},{10,6},{11,7},{14,10},{15,11},{12,14},{13,15},{8,12},{... | collective-permute-start | bytes 798728 | tf_op jit(solution)/shard_map/ppermute | solution.py:270
  22.8 2.8 %copy-start = (bf16[1,1,2048,1536]{3,2,1,0:T(8,128)(2,1)S(1)}, bf16[1,1,2048,1536]{3,2,1,0:T(8,128)(2,1)}, u32[]{:S(2)}) copy-start(bf16[1,1,2048,1536]{3,2,1,0:T(8,128)(2,1)} %param.12) | copy-start | bytes 18874372
  28.5 11.4 %collective-permute-start.11 = (bf16[1040,128]{1,0:T(8,128)(2,1)S(1)}, bf16[1040,128]{1,0:T(8,128)(2,1)S(1)}, u32[]{:S(2)}, u32[]{:S(2)}) collective-permute-start(bf16[1040,128]{1,0:T(8,128)(2,1)S(1)} %collective-permute-done.9.refs_1_), channel_id=1, source_target_pairs={{6,2},{7,3},{10,6},{11,7},{14,10},{15,11},{12,14},{13,15},{8,12},{... | collective-permute-start | bytes 798728 | tf_op jit(solution)/shard_map/ppermute | solution.py:270
  29.5 11.0 %collective-permute-start.10 = (bf16[1040,128]{1,0:T(8,128)(2,1)S(1)}, bf16[1040,128]{1,0:T(8,128)(2,1)S(1)}, u32[]{:S(2)}, u32[]{:S(2)}) collective-permute-start(bf16[1040,128]{1,0:T(8,128)(2,1)S(1)} %collective-permute-done.8.refs_0_), channel_id=1, source_target_pairs={{2,6},{3,7},{6,10},{7,11},{10,14},{11,15},{14,12},{15,13},{12,8},{... | collective-permute-start | bytes 798728 | tf_op jit(solution)/shard_map/ppermute | solution.py:270
  34.8 11.4 %collective-permute-start.12 = (bf16[1040,128]{1,0:T(8,128)(2,1)S(1)}, bf16[1040,128]{1,0:T(8,128)(2,1)S(1)}, u32[]{:S(2)}, u32[]{:S(2)}) collective-permute-start(bf16[1040,128]{1,0:T(8,128)(2,1)S(1)} %collective-permute-done.5.refs_0_), channel_id=1, source_target_pairs={{2,6},{3,7},{6,10},{7,11},{10,14},{11,15},{14,12},{15,13},{12,8},{... | collective-permute-start | bytes 798728 | tf_op jit(solution)/shard_map/ppermute | solution.py:270
  35.9 10.3 %collective-permute-start.13 = (bf16[1040,128]{1,0:T(8,128)(2,1)S(1)}, bf16[1040,128]{1,0:T(8,128)(2,1)S(1)}, u32[]{:S(2)}, u32[]{:S(2)}) collective-permute-start(bf16[1040,128]{1,0:T(8,128)(2,1)S(1)} %collective-permute-done.7.refs_1_), channel_id=1, source_target_pairs={{6,2},{7,3},{10,6},{11,7},{14,10},{15,11},{12,14},{13,15},{8,12},{... | collective-permute-start | bytes 798728 | tf_op jit(solution)/shard_map/ppermute | solution.py:270
  40.5 11.4 %collective-permute-start.15 = (bf16[1040,128]{1,0:T(8,128)(2,1)S(1)}, bf16[1040,128]{1,0:T(8,128)(2,1)S(1)}, u32[]{:S(2)}, u32[]{:S(2)}) collective-permute-start(bf16[1040,128]{1,0:T(8,128)(2,1)S(1)} %collective-permute-done.10.refs_0_), channel_id=1, source_target_pairs={{2,6},{3,7},{6,10},{7,11},{10,14},{11,15},{14,12},{15,13},{12,8},{... | collective-permute-start | bytes 798728 | tf_op jit(solution)/shard_map/ppermute | solution.py:270
  41.6 10.3 %collective-permute-start.16 = (bf16[1040,128]{1,0:T(8,128)(2,1)S(1)}, bf16[1040,128]{1,0:T(8,128)(2,1)S(1)}, u32[]{:S(2)}, u32[]{:S(2)}) collective-permute-start(bf16[1040,128]{1,0:T(8,128)(2,1)S(1)} %collective-permute-done.11.refs_1_), channel_id=1, source_target_pairs={{6,2},{7,3},{10,6},{11,7},{14,10},{15,11},{12,14},{13,15},{8,12},{... | collective-permute-start | bytes 798728 | tf_op jit(solution)/shard_map/ppermute | solution.py:270
  46.2 12.2 %collective-permute-start.18 = (bf16[1040,128]{1,0:T(8,128)(2,1)S(1)}, bf16[1040,128]{1,0:T(8,128)(2,1)S(1)}, u32[]{:S(2)}, u32[]{:S(2)}) collective-permute-start(bf16[1040,128]{1,0:T(8,128)(2,1)S(1)} %collective-permute-done.12.refs_0_), channel_id=1, source_target_pairs={{2,6},{3,7},{6,10},{7,11},{10,14},{11,15},{14,12},{15,13},{12,8},{... | collective-permute-start | bytes 798728 | tf_op jit(solution)/shard_map/ppermute | solution.py:270
  51.9 7.9 %collective-permute-start.19 = (bf16[1040,128]{1,0:T(8,128)(2,1)S(1)}, bf16[1040,128]{1,0:T(8,128)(2,1)S(1)}, u32[]{:S(2)}, u32[]{:S(2)}) collective-permute-start(bf16[1040,128]{1,0:T(8,128)(2,1)S(1)} %collective-permute-done.16.refs_1_), channel_id=1, source_target_pairs={{6,2},{7,3},{10,6},{11,7},{14,10},{15,11},{12,14},{13,15},{8,12},{... | collective-permute-start | bytes 798728 | tf_op jit(solution)/shard_map/ppermute | solution.py:270
  53.5 11.8 %collective-permute-start.14 = (bf16[64,2048]{1,0:T(8,128)(2,1)S(1)}, bf16[64,2048]{1,0:T(8,128)(2,1)S(1)}, u32[]{:S(2)}, u32[]{:S(2)}) collective-permute-start(bf16[64,2048]{1,0:T(8,128)(2,1)S(1)} %convert_element_type.73), channel_id=1, source_target_pairs={{6,2},{7,3},{10,6},{11,7},{14,10},{15,11},{12,14},{13,15},{8,12},{... | collective-permute-start | bytes 786440 | tf_op jit(solution)/shard_map/ppermute | solution.py:270
  58.0 9.2 %collective-permute-start.17 = (bf16[64,2048]{1,0:T(8,128)(2,1)S(1)}, bf16[64,2048]{1,0:T(8,128)(2,1)S(1)}, u32[]{:S(2)}, u32[]{:S(2)}) collective-permute-start(bf16[64,2048]{1,0:T(8,128)(2,1)S(1)} %convert_element_type.74), channel_id=1, source_target_pairs={{2,6},{3,7},{6,10},{7,11},{10,14},{11,15},{14,12},{15,13},{12,8},{... | collective-permute-start | bytes 786440 | tf_op jit(solution)/shard_map/ppermute | solution.py:270
  62.6 9.6 %collective-permute-start.23 = (bf16[64,2048]{1,0:T(8,128)(2,1)S(1)}, bf16[64,2048]{1,0:T(8,128)(2,1)S(1)}, u32[]{:S(2)}, u32[]{:S(2)}) collective-permute-start(bf16[64,2048]{1,0:T(8,128)(2,1)S(1)} %convert_element_type.80), channel_id=1, source_target_pairs={{6,2},{7,3},{10,6},{11,7},{14,10},{15,11},{12,14},{13,15},{8,12},{... | collective-permute-start | bytes 786440 | tf_op jit(solution)/shard_map/ppermute | solution.py:270
  63.3 10.5 %collective-permute-start.21 = (bf16[64,2048]{1,0:T(8,128)(2,1)S(1)}, bf16[64,2048]{1,0:T(8,128)(2,1)S(1)}, u32[]{:S(2)}, u32[]{:S(2)}) collective-permute-start(bf16[64,2048]{1,0:T(8,128)(2,1)S(1)} %convert_element_type.75), channel_id=1, source_target_pairs={{2,6},{3,7},{6,10},{7,11},{10,14},{11,15},{14,12},{15,13},{12,8},{... | collective-permute-start | bytes 786440 | tf_op jit(solution)/shard_map/ppermute | solution.py:270
  70.1 14.7 %collective-permute-start.26 = (bf16[64,2048]{1,0:T(8,128)(2,1)S(1)}, bf16[64,2048]{1,0:T(8,128)(2,1)S(1)}, u32[]{:S(2)}, u32[]{:S(2)}) collective-permute-start(bf16[64,2048]{1,0:T(8,128)(2,1)S(1)} %get-tuple-element.82), channel_id=1, source_target_pairs={{2,6},{3,7},{6,10},{7,11},{10,14},{11,15},{14,12},{15,13},{12,8},{... | collective-permute-start | bytes 786440 | tf_op jit(solution)/shard_map/ppermute | solution.py:270
  70.6 15.2 %collective-permute-start.20 = (bf16[64,2048]{1,0:T(8,128)(2,1)S(1)}, bf16[64,2048]{1,0:T(8,128)(2,1)S(1)}, u32[]{:S(2)}, u32[]{:S(2)}) collective-permute-start(bf16[64,2048]{1,0:T(8,128)(2,1)S(1)} %get-tuple-element.74), channel_id=1, source_target_pairs={{6,2},{7,3},{10,6},{11,7},{14,10},{15,11},{12,14},{13,15},{8,12},{... | collective-permute-start | bytes 786440 | tf_op jit(solution)/shard_map/ppermute | solution.py:270
  72.3 9.9 %collective-permute-start.24 = (bf16[64,2048]{1,0:T(8,128)(2,1)S(1)}, bf16[64,2048]{1,0:T(8,128)(2,1)S(1)}, u32[]{:S(2)}, u32[]{:S(2)}) collective-permute-start(bf16[64,2048]{1,0:T(8,128)(2,1)S(1)} %add_convert_fusion.5), channel_id=1, source_target_pairs={{6,2},{7,3},{10,6},{11,7},{14,10},{15,11},{12,14},{13,15},{8,12},{... | collective-permute-start | bytes 786440 | tf_op jit(solution)/shard_map/ppermute | solution.py:270
  73.9 10.9 %collective-permute-start.22 = (bf16[64,2048]{1,0:T(8,128)(2,1)S(1)}, bf16[64,2048]{1,0:T(8,128)(2,1)S(1)}, u32[]{:S(2)}, u32[]{:S(2)}) collective-permute-start(bf16[64,2048]{1,0:T(8,128)(2,1)S(1)} %add_convert_fusion.7), channel_id=1, source_target_pairs={{2,6},{3,7},{6,10},{7,11},{10,14},{11,15},{14,12},{15,13},{12,8},{... | collective-permute-start | bytes 786440 | tf_op jit(solution)/shard_map/ppermute | solution.py:270
  82.2 9.3 %collective-permute-start.30 = (bf16[64,2048]{1,0:T(8,128)(2,1)S(1)}, bf16[64,2048]{1,0:T(8,128)(2,1)S(1)}, u32[]{:S(2)}, u32[]{:S(2)}) collective-permute-start(bf16[64,2048]{1,0:T(8,128)(2,1)S(1)} %add_convert_fusion.4), channel_id=1, source_target_pairs={{6,2},{7,3},{10,6},{11,7},{14,10},{15,11},{12,14},{13,15},{8,12},{... | collective-permute-start | bytes 786440 | tf_op jit(solution)/shard_map/ppermute | solution.py:270
  84.8 7.9 %collective-permute-start.28 = (bf16[64,2048]{1,0:T(8,128)(2,1)S(1)}, bf16[64,2048]{1,0:T(8,128)(2,1)S(1)}, u32[]{:S(2)}, u32[]{:S(2)}) collective-permute-start(bf16[64,2048]{1,0:T(8,128)(2,1)S(1)} %add_convert_fusion.6), channel_id=1, source_target_pairs={{2,6},{3,7},{6,10},{7,11},{10,14},{11,15},{14,12},{15,13},{12,8},{... | collective-permute-start | bytes 786440 | tf_op jit(solution)/shard_map/ppermute | solution.py:270
  84.9 9.9 %collective-permute-start.27 = (bf16[64,2048]{1,0:T(8,128)(2,1)S(1)}, bf16[64,2048]{1,0:T(8,128)(2,1)S(1)}, u32[]{:S(2)}, u32[]{:S(2)}) collective-permute-start(bf16[64,2048]{1,0:T(8,128)(2,1)S(1)} %add_convert_fusion.2), channel_id=1, source_target_pairs={{2,6},{3,7},{6,10},{7,11},{10,14},{11,15},{14,12},{15,13},{12,8},{... | collective-permute-start | bytes 786440 | tf_op jit(solution)/shard_map/ppermute | solution.py:270
  85.8 9.1 %collective-permute-start.25 = (bf16[64,2048]{1,0:T(8,128)(2,1)S(1)}, bf16[64,2048]{1,0:T(8,128)(2,1)S(1)}, u32[]{:S(2)}, u32[]{:S(2)}) collective-permute-start(bf16[64,2048]{1,0:T(8,128)(2,1)S(1)} %add_convert_fusion.3), channel_id=1, source_target_pairs={{6,2},{7,3},{10,6},{11,7},{14,10},{15,11},{12,14},{13,15},{8,12},{... | collective-permute-start | bytes 786440 | tf_op jit(solution)/shard_map/ppermute | solution.py:270
  91.5 6.4 %collective-permute-start.31 = (bf16[64,2048]{1,0:T(8,128)(2,1)S(1)}, bf16[64,2048]{1,0:T(8,128)(2,1)S(1)}, u32[]{:S(2)}, u32[]{:S(2)}) collective-permute-start(bf16[64,2048]{1,0:T(8,128)(2,1)S(1)} %add_convert_fusion), channel_id=1, source_target_pairs={{6,2},{7,3},{10,6},{11,7},{14,10},{15,11},{12,14},{13,15},{8,12},{... | collective-permute-start | bytes 786440 | tf_op jit(solution)/shard_map/ppermute | solution.py:270
  92.8 6.4 %collective-permute-start.29 = (bf16[64,2048]{1,0:T(8,128)(2,1)S(1)}, bf16[64,2048]{1,0:T(8,128)(2,1)S(1)}, u32[]{:S(2)}, u32[]{:S(2)}) collective-permute-start(bf16[64,2048]{1,0:T(8,128)(2,1)S(1)} %add_convert_fusion.1), channel_id=1, source_target_pairs={{2,6},{3,7},{6,10},{7,11},{10,14},{11,15},{14,12},{15,13},{12,8},{... | collective-permute-start | bytes 786440 | tf_op jit(solution)/shard_map/ppermute | solution.py:270

commit v14 on v11

--- a/solution.py
+++ b/solution.py
@@ -152,61 +152,76 @@
     )(section_id, base, coefs, fresh, arrived, gain)
 
 
-def mlp_kernel(expert_ref, *refs, parts, adds, chained):
+def mlp_kernel(expert_ref, *refs, parts, adds, chained, core, given):
     payloads = refs[:parts]
     weights = (refs[parts : parts + 2], refs[parts + 2 : parts + 4])
     refs = refs[parts + 4 :]
     terms, totals = refs[:adds], refs[adds : 2 * adds]
-    refs = refs[2 * adds + chained :]
+    earlier, refs = refs[2 * adds : 2 * adds + given], refs[2 * adds + given + chained :]
     outs, added = refs[:parts], refs[parts : parts + adds]
     x_ref, coef_ref, hidden_ref = refs[parts + adds :]
     for term, total, result in zip(terms, totals, added):
         result[...] = (term[...] + total[...].astype(jnp.float32)).astype(jnp.bfloat16)
-    width = x_ref.shape[1]
-    hidden = weights[0][1].shape[0]
-    line = lax.broadcasted_iota(jnp.int32, (HALF, LANES), 0)
-    token = line == lax.broadcasted_iota(jnp.int32, (HALF, LANES), 1) % HALF
-    bounds = []
-    for part, payload in enumerate(payloads):
-        here = slice(part * HALF, (part + 1) * HALF)
-        bounds.append(here)
-        for i in range(width // LANES):
-            x_ref[here, i * LANES : (i + 1) * LANES] = payload[i * HALF : (i + 1) * HALF, :]
-        block = payload[HALF * (width // LANES) :, :].astype(jnp.float32)
-        expert = lax.broadcasted_iota(jnp.int32, block.shape, 0)
-        for which in range(2):
-            terms = jnp.sum(jnp.where(expert == expert_ref[0] ^ which, block, 0.0), axis=0, keepdims=True)
-            value = jnp.sum(jnp.where(token, terms, 0.0), axis=1, keepdims=True)
-            coef_ref[which, here, :] = jnp.broadcast_to(value, (HALF, LANES))
-    tile = 256
-    for which, (gate_up, _) in enumerate(weights):
-        for t in range(0, hidden, tile):
-            gate = jnp.dot(x_ref[...], gate_up[:, t : t + tile], preferred_element_type=jnp.float32)
-            up = jnp.dot(x_ref[...], gate_up[:, hidden + t : hidden + t + tile], preferred_element_type=jnp.float32)
-            value = jax.nn.silu(gate) * up * coef_ref[which][:, :1]
-            hidden_ref[:, which * hidden + t : which * hidden + t + tile] = value.astype(jnp.bfloat16)
-    tile = 512
-    for t in range(0, width, tile):
-        total = jnp.zeros((x_ref.shape[0], tile), jnp.float32)
-        for which, (_, down) in enumerate(weights):
-            rows = hidden_ref[:, which * hidden : (which + 1) * hidden]
-            total += jnp.dot(rows, down[:, t : t + tile], preferred_element_type=jnp.float32)
-        for here, out in zip(bounds, outs):
-            out[:, t : t + tile] = total[here, :]
-
-
-def expert_rows(expert_id, payloads, own, other, after, terms=(), totals=()):
+
+    def experts():
+        width = x_ref.shape[1]
+        hidden = weights[0][1].shape[0]
+        line = lax.broadcasted_iota(jnp.int32, (HALF, LANES), 0)
+        token = line == lax.broadcasted_iota(jnp.int32, (HALF, LANES), 1) % HALF
+        bounds = []
+        for part, payload in enumerate(payloads):
+            here = slice(part * HALF, (part + 1) * HALF)
+            bounds.append(here)
+            for i in range(width // LANES):
+                x_ref[here, i * LANES : (i + 1) * LANES] = payload[i * HALF : (i + 1) * HALF, :]
+            block = payload[HALF * (width // LANES) :, :].astype(jnp.float32)
+            expert = lax.broadcasted_iota(jnp.int32, block.shape, 0)
+            for which in range(2):
+                terms = jnp.sum(jnp.where(expert == expert_ref[0] ^ which, block, 0.0), axis=0, keepdims=True)
+                value = jnp.sum(jnp.where(token, terms, 0.0), axis=1, keepdims=True)
+                coef_ref[which, here, :] = jnp.broadcast_to(value, (HALF, LANES))
+        tile = 256
+        for which, (gate_up, _) in enumerate(weights):
+            for t in range(0, hidden, tile):
+                gate = jnp.dot(x_ref[...], gate_up[:, t : t + tile], preferred_element_type=jnp.float32)
+                up = jnp.dot(x_ref[...], gate_up[:, hidden + t : hidden + t + tile], preferred_element_type=jnp.float32)
+                value = jax.nn.silu(gate) * up * coef_ref[which][:, :1]
+                hidden_ref[:, which * hidden + t : which * hidden + t + tile] = value.astype(jnp.bfloat16)
+        tile = 512
+        for t in range(0, width, tile):
+            total = jnp.zeros((x_ref.shape[0], tile), jnp.float32)
+            for which, (_, down) in enumerate(weights):
+                rows = hidden_ref[:, which * hidden : (which + 1) * hidden]
+                total += jnp.dot(rows, down[:, t : t + tile], preferred_element_type=jnp.float32)
+            for here, out in zip(bounds, outs):
+                out[:, t : t + tile] = total[here, :]
+
+    if core is None:
+        experts()
+    else:
+        here = expert_ref[0] % CORES == core
+        pl.when(here)(experts)
+
+        @pl.when(jnp.logical_not(here))
+        def _():
+            for source, out in zip(earlier, outs):
+                out[...] = source[...]
+
+
+def expert_rows(expert_id, payloads, own, other, after, terms=(), totals=(), core=None, earlier=()):
     width = own[0].shape[0]
     hidden = own[1].shape[0]
     rows = HALF * len(payloads)
     vmem = pl.BlockSpec(memory_space=pltpu.VMEM)
     chain = [] if after is None else [after]
     return pl.pallas_call(
-        functools.partial(mlp_kernel, parts=len(payloads), adds=len(terms), chained=len(chain)),
+        functools.partial(
+            mlp_kernel, parts=len(payloads), adds=len(terms), chained=len(chain), core=core, given=len(earlier)
+        ),
         out_shape=[jax.ShapeDtypeStruct((HALF, width), jnp.float32)] * len(payloads)
         + [jax.ShapeDtypeStruct((HALF, width), jnp.bfloat16)] * len(terms),
         in_specs=[pl.BlockSpec(memory_space=pltpu.SMEM)]
-        + [vmem] * (len(payloads) + 4 + 2 * len(terms))
+        + [vmem] * (len(payloads) + 4 + 2 * len(terms) + len(earlier))
         + [pl.BlockSpec(memory_space=pl.ANY)] * len(chain),
         out_specs=[vmem] * (len(payloads) + len(terms)),
         scratch_shapes=[
@@ -221,7 +236,7 @@
             transcendentals=rows * hidden * 2,
         ),
         name="expert_rows",
-    )(expert_id, *payloads, *own, *other, *terms, *totals, *chain)
+    )(expert_id, *payloads, *own, *other, *terms, *totals, *earlier, *chain)
 
 
 def last_kernel(near0_ref, near1_ref, total0_ref, total1_ref, out_ref):
@@ -291,9 +306,9 @@
 
     last = None
 
-    def mlp(payloads, terms=(), totals=()):
+    def mlp(payloads, *args):
         nonlocal last
-        sums = expert_rows(expert_id, payloads, own, other, last, terms, totals)
+        sums = expert_rows(expert_id, payloads, own, other, last, *args)
         last = sums[0]
         return sums
 
@@ -304,12 +319,13 @@
         for c in range(2):
             pass_on(s, c, last)
             to_down[s, c], to_up[s, c] = mlp([ups[s][c], downs[s][c]])
+    early_sums = mlp(packed, (), (), 1)
     to_up[hops, 0], to_down[hops, 1] = mlp([ups[hops][0], downs[hops][1]])
 
     def send_on(flow, place, total, after):
         terms, c, pairs = flow
         if total is None:
-            total = terms[place, c]
+            total = lax.optimization_barrier((terms[place, c], after))[0]
         else:
             carried = lax.optimization_barrier((total, after))[0]
             total = terms[place, c] + carried.astype(jnp.float32)
@@ -318,9 +334,9 @@
 
     short = [(to_down, 0, down), (to_up, 1, up)]
     long = [(to_up, 0, up), (to_down, 1, down)]
-    short_totals = [send_on(flow, hops - 1, None, None)[1] for flow in short]
+    short_totals = [send_on(flow, hops - 1, None, to_up[hops - 1, 1])[1] for flow in short]
     long_totals = [send_on(flow, hops, None, None)[1] for flow in long]
-    *own_sums, down_sum, up_sum = mlp(packed, [f[0][hops - 2, f[1]] for f in short], short_totals)
+    *own_sums, down_sum, up_sum = mlp(packed, [f[0][hops - 2, f[1]] for f in short], short_totals, 0, early_sums)
     short_totals = [move(total, flow[2]) for total, flow in zip((down_sum, up_sum), short)]
     after = None
     for s in reversed(range(1, hops)):

time: 99.1 us -> 98.7 us (level)
    pallas_call x8 -> x9, Pallas kernels: 22.2 us -> 22.4 us  [expert_rows(): pl.pallas_call(functools.partial(mlp_kernel, parts=len(payloads), adds=le...]
  transfers between devices with their start and end apart: 32 -> 32, of which waited for: 15 -> 13; matrix products, arithmetic and copies ran while one was open for 2% -> 2% of each run, Pallas kernels for 23% -> 23%
where the time goes in v14:
time: 98.7 us; the launch traced here: 98.4 us
  starting transfers between devices  36.9 us (37%)
  waiting for transfers between devices  29.7 us (30%)
  Pallas kernels  23.6 us (24%)
  local copies, waits for them, and re-layouts  7.21 us (7%)
    ppermute x30, starting transfers between devices, move(): return lax.ppermute(value, 'expert', pairs)  30.7 us
    ppermute x30, waiting for transfers between devices, move(): return lax.ppermute(value, 'expert', pairs)  25.2 us
    pallas_call x9, Pallas kernels, expert_rows(): pl.pallas_call(functools.partial(mlp_kernel, parts=len(payloads), adds=le...  22.4 us
    ppermute x2, starting transfers between devices, from_behind(): return lax.ppermute(value, axis, pairs)  6.18 us
    unnamed x12, local copies, waits for them, and re-layouts  5.89 us
    ppermute x2, waiting for transfers between devices, from_behind(): return lax.ppermute(value, axis, pairs)  4.5 us
  transfers between devices with their start and end apart: 32, of which 13 were waited for; matrix products, arithmetic and copies ran while one was open for 2% of the time, Pallas kernels for 23%

profile of v14, /device:TPU:0, one launch (start us, length us, event | category | flops | bytes accessed | tf_op | source)
XLA Modules:
  0.0 98.4 jit_solution(17480859158997524453)
XLA Ops:
  0.0 0.5 collective-permute-start.2
  0.5 0.1 collective-permute-start.3
  0.5 1.3 %slice_bitcast_fusion = (bf16[64,2048]{1,0:T(8,128)(2,1)S(1)}, bf16[64,2048]{1,0:T(8,128)(2,1)S(1)}) fusion(bf16[1,128,2048]{2,1,0:T(8,128)(2,1)} %param.8), kind=kLoop, calls=%fused_computation.10 | loop fusion | bytes 1048576 | tf_op jit(solution)/shard_map/squeeze | solution.py:292
  1.8 4.9 %collective-permute-start = (bf16[64,2048]{1,0:T(8,128)(2,1)S(1)}, bf16[64,2048]{1,0:T(8,128)(2,1)S(1)}, u32[]{:S(2)}, u32[]{:S(2)}) collective-permute-start(bf16[64,2048]{1,0:T(8,128)(2,1)S(1)} %get-tuple-element.106), channel_id=1, source_target_pairs={{0,16},{1,17},{2,18},{3,19},{4,20},{5,21},{6,22},{7,23},{8,24},{9,... | collective-permute-start | bytes 786440 | tf_op jit(solution)/shard_map/ppermute | solution.py:20
  6.7 1.3 %collective-permute-start.1 = (bf16[64,2048]{1,0:T(8,128)(2,1)S(1)}, bf16[64,2048]{1,0:T(8,128)(2,1)S(1)}, u32[]{:S(2)}, u32[]{:S(2)}) collective-permute-start(bf16[64,2048]{1,0:T(8,128)(2,1)S(1)} %get-tuple-element.105), channel_id=1, source_target_pairs={{0,16},{1,17},{2,18},{3,19},{4,20},{5,21},{6,22},{7,23},{8,24},{9,... | collective-permute-start | bytes 786440 | tf_op jit(solution)/shard_map/ppermute | solution.py:20
  8.1 1.0 %copy-done.2 = bf16[128,2048]{1,0:T(8,128)(2,1)S(1)} copy-done((bf16[128,2048]{1,0:T(8,128)(2,1)S(1)}, bf16[128,2048]{1,0:T(8,128)(2,1)}, u32[]{:S(2)}) %copy-start.2) | copy-done | bytes 524312
  9.1 0.7 copy-done.3
  9.8 0.7 copy-done.4
  10.5 0.7 copy-done.5
  11.2 0.2 base_rows.1
  11.4 2.0 %collective-permute-done.arrived_ref = bf16[64,2048]{1,0:T(8,128)(2,1)S(1)} collective-permute-done((bf16[64,2048]{1,0:T(8,128)(2,1)S(1)}, bf16[64,2048]{1,0:T(8,128)(2,1)S(1)}, u32[]{:S(2)}, u32[]{:S(2)}) %collective-permute-start) | collective-permute-done | bytes 262176 | tf_op jit(solution)/shard_map/ppermute | solution.py:20
  13.4 1.5 %collective-permute-start.4 = (bf16[1040,128]{1,0:T(8,128)(2,1)S(1)}, bf16[1040,128]{1,0:T(8,128)(2,1)S(1)}, u32[]{:S(2)}, u32[]{:S(2)}) collective-permute-start(bf16[1040,128]{1,0:T(8,128)(2,1)S(1)} %get-tuple-element.65.refs_0_), channel_id=1, source_target_pairs={{2,6},{3,7},{6,10},{7,11},{10,14},{11,15},{14,12},{15,13},{12,8},{... | collective-permute-start | bytes 798728 | tf_op jit(solution)/shard_map/ppermute | solution.py:285
  15.0 0.5 collective-permute-start.5
  15.5 2.5 %collective-permute-done.1.arrived_ref = bf16[64,2048]{1,0:T(8,128)(2,1)S(1)} collective-permute-done((bf16[64,2048]{1,0:T(8,128)(2,1)S(1)}, bf16[64,2048]{1,0:T(8,128)(2,1)S(1)}, u32[]{:S(2)}, u32[]{:S(2)}) %collective-permute-start.1) | collective-permute-done | bytes 262176 | tf_op jit(solution)/shard_map/ppermute | solution.py:20
  18.1 1.5 %collective-permute-start.8 = (bf16[1040,128]{1,0:T(8,128)(2,1)S(1)}, bf16[1040,128]{1,0:T(8,128)(2,1)S(1)}, u32[]{:S(2)}, u32[]{:S(2)}) collective-permute-start(bf16[1040,128]{1,0:T(8,128)(2,1)S(1)} %get-tuple-element.69.refs_1_), channel_id=1, source_target_pairs={{2,6},{3,7},{6,10},{7,11},{10,14},{11,15},{14,12},{15,13},{12,8},{... | collective-permute-start | bytes 798728 | tf_op jit(solution)/shard_map/ppermute | solution.py:285
  19.7 0.5 collective-permute-start.9
  20.2 1.3 %collective-permute-done.5.refs_1_ = bf16[1040,128]{1,0:T(8,128)(2,1)S(1)} collective-permute-done((bf16[1040,128]{1,0:T(8,128)(2,1)S(1)}, bf16[1040,128]{1,0:T(8,128)(2,1)S(1)}, u32[]{:S(2)}, u32[]{:S(2)}) %collective-permute-start.5) | collective-permute-done | bytes 266272 | tf_op jit(solution)/shard_map/ppermute | solution.py:285
  21.6 1.6 %collective-permute-start.6 = (bf16[1040,128]{1,0:T(8,128)(2,1)S(1)}, bf16[1040,128]{1,0:T(8,128)(2,1)S(1)}, u32[]{:S(2)}, u32[]{:S(2)}) collective-permute-start(bf16[1040,128]{1,0:T(8,128)(2,1)S(1)} %collective-permute-done.4.refs_0_), channel_id=1, source_target_pairs={{2,6},{3,7},{6,10},{7,11},{10,14},{11,15},{14,12},{15,13},{12,8},{... | collective-permute-start | bytes 798728 | tf_op jit(solution)/shard_map/ppermute | solution.py:285
  23.2 0.4 collective-permute-start.7
  23.6 2.8 %copy-done = bf16[1,1,2048,1536]{3,2,1,0:T(8,128)(2,1)S(1)} copy-done((bf16[1,1,2048,1536]{3,2,1,0:T(8,128)(2,1)S(1)}, bf16[1,1,2048,1536]{3,2,1,0:T(8,128)(2,1)}, u32[]{:S(2)}) %copy-start) | copy-done | bytes 6291480
  26.4 2.8 %expert_rows.9 = (f32[64,2048]{1,0:T(8,128)S(1)}, f32[64,2048]{1,0:T(8,128)S(1)}) custom-call(s32[1]{0:T(128)} %bitcast.6.expert_ref, bf16[1040,128]{1,0:T(8,128)(2,1)S(1)} %collective-permute-done.4.refs_0_, bf16[1040,128]{1,0:T(8,128)(2,1)S(1)} %collective-permute-done.5.refs_1_, bf16[2048,1536]{1,0:T(8,128)(2,1)S(1)} %bitcast.16, ...), custom_call_target="tpu_custom_call" | custom-call | flops 2415919104 | bytes 1572864 | tf_op jit(solution)/shard_map/expert_rows/pallas_call | solution.py:217
  29.2 1.6 %collective-permute-start.10 = (bf16[1040,128]{1,0:T(8,128)(2,1)S(1)}, bf16[1040,128]{1,0:T(8,128)(2,1)S(1)}, u32[]{:S(2)}, u32[]{:S(2)}) collective-permute-start(bf16[1040,128]{1,0:T(8,128)(2,1)S(1)} %collective-permute-done.8.refs_0_), channel_id=1, source_target_pairs={{2,6},{3,7},{6,10},{7,11},{10,14},{11,15},{14,12},{15,13},{12,8},{... | collective-permute-start | bytes 798728 | tf_op jit(solution)/shard_map/ppermute | solution.py:285
  30.8 0.5 collective-permute-start.11
  31.3 2.8 %expert_rows.10 = (f32[64,2048]{1,0:T(8,128)S(1)}, f32[64,2048]{1,0:T(8,128)S(1)}) custom-call(s32[1]{0:T(128)} %bitcast.6.expert_ref, bf16[1040,128]{1,0:T(8,128)(2,1)S(1)} %collective-permute-done.8.refs_0_, bf16[1040,128]{1,0:T(8,128)(2,1)S(1)} %collective-permute-done.9.refs_1_, bf16[2048,1536]{1,0:T(8,128)(2,1)S(1)} %bitcast.17, ...), custom_call_target="tpu_custom_call" | custom-call | flops 2415919104 | bytes 1572864 | tf_op jit(solution)/shard_map/expert_rows/pallas_call | solution.py:217
  34.1 0.6 collective-permute-done.7.refs_1_
  34.7 1.6 %collective-permute-start.12 = (bf16[1040,128]{1,0:T(8,128)(2,1)S(1)}, bf16[1040,128]{1,0:T(8,128)(2,1)S(1)}, u32[]{:S(2)}, u32[]{:S(2)}) collective-permute-start(bf16[1040,128]{1,0:T(8,128)(2,1)S(1)} %collective-permute-done.6.refs_0_), channel_id=1, source_target_pairs={{2,6},{3,7},{6,10},{7,11},{10,14},{11,15},{14,12},{15,13},{12,8},{... | collective-permute-start | bytes 798728 | tf_op jit(solution)/shard_map/ppermute | solution.py:285
  36.3 0.4 collective-permute-start.13
  36.8 2.8 %expert_rows.11 = (f32[64,2048]{1,0:T(8,128)S(1)}, f32[64,2048]{1,0:T(8,128)S(1)}) custom-call(s32[1]{0:T(128)} %bitcast.6.expert_ref, bf16[1040,128]{1,0:T(8,128)(2,1)S(1)} %collective-permute-done.6.refs_0_, bf16[1040,128]{1,0:T(8,128)(2,1)S(1)} %collective-permute-done.7.refs_1_, bf16[2048,1536]{1,0:T(8,128)(2,1)S(1)} %bitcast.18, ...), custom_call_target="tpu_custom_call" | custom-call | flops 2415919104 | bytes 1572864 | tf_op jit(solution)/shard_map/expert_rows/pallas_call | solution.py:217
  39.6 0.9 collective-permute-done.11.refs_1_
  40.4 1.6 %collective-permute-start.14 = (bf16[1040,128]{1,0:T(8,128)(2,1)S(1)}, bf16[1040,128]{1,0:T(8,128)(2,1)S(1)}, u32[]{:S(2)}, u32[]{:S(2)}) collective-permute-start(bf16[1040,128]{1,0:T(8,128)(2,1)S(1)} %collective-permute-done.10.refs_0_), channel_id=1, source_target_pairs={{2,6},{3,7},{6,10},{7,11},{10,14},{11,15},{14,12},{15,13},{12,8},{... | collective-permute-start | bytes 798728 | tf_op jit(solution)/shard_map/ppermute | solution.py:285
  42.0 0.5 collective-permute-start.15
  42.5 2.8 %expert_rows.12 = (f32[64,2048]{1,0:T(8,128)S(1)}, f32[64,2048]{1,0:T(8,128)S(1)}) custom-call(s32[1]{0:T(128)} %bitcast.6.expert_ref, bf16[1040,128]{1,0:T(8,128)(2,1)S(1)} %collective-permute-done.10.refs_0_, bf16[1040,128]{1,0:T(8,128)(2,1)S(1)} %collective-permute-done.11.refs_1_, bf16[2048,1536]{1,0:T(8,128)(2,1)S(1)} %bitcast.19, ...), custom_call_target="tpu_custom_call" | custom-call | flops 2415919104 | bytes 1572864 | tf_op jit(solution)/shard_map/expert_rows/pallas_call | solution.py:217
  45.3 0.9 collective-permute-done.13.refs_1_
  46.1 1.6 %collective-permute-start.18 = (bf16[1040,128]{1,0:T(8,128)(2,1)S(1)}, bf16[1040,128]{1,0:T(8,128)(2,1)S(1)}, u32[]{:S(2)}, u32[]{:S(2)}) collective-permute-start(bf16[1040,128]{1,0:T(8,128)(2,1)S(1)} %collective-permute-done.12.refs_0_), channel_id=1, source_target_pairs={{2,6},{3,7},{6,10},{7,11},{10,14},{11,15},{14,12},{15,13},{12,8},{... | collective-permute-start | bytes 798728 | tf_op jit(solution)/shard_map/ppermute | solution.py:285
  47.7 2.8 %expert_rows.13 = (f32[64,2048]{1,0:T(8,128)S(1)}, f32[64,2048]{1,0:T(8,128)S(1)}) custom-call(s32[1]{0:T(128)} %bitcast.6.expert_ref, bf16[1040,128]{1,0:T(8,128)(2,1)S(1)} %collective-permute-done.12.refs_0_, bf16[1040,128]{1,0:T(8,128)(2,1)S(1)} %collective-permute-done.13.refs_1_, bf16[2048,1536]{1,0:T(8,128)(2,1)S(1)} %bitcast.20, ...), custom_call_target="tpu_custom_call" | custom-call | flops 2415919104 | bytes 1572864 | tf_op jit(solution)/shard_map/expert_rows/pallas_call | solution.py:217
  50.5 1.4 %collective-permute-start.19 = (bf16[1040,128]{1,0:T(8,128)(2,1)S(1)}, bf16[1040,128]{1,0:T(8,128)(2,1)S(1)}, u32[]{:S(2)}, u32[]{:S(2)}) collective-permute-start(bf16[1040,128]{1,0:T(8,128)(2,1)S(1)} %collective-permute-done.15.refs_1_), channel_id=1, source_target_pairs={{6,2},{7,3},{10,6},{11,7},{14,10},{15,11},{12,14},{13,15},{8,12},{... | collective-permute-start | bytes 798728 | tf_op jit(solution)/shard_map/ppermute | solution.py:285
  51.9 2.8 %expert_rows.14 = (f32[64,2048]{1,0:T(8,128)S(1)}, f32[64,2048]{1,0:T(8,128)S(1)}) custom-call(s32[1]{0:T(128)} %bitcast.6.expert_ref, bf16[1040,128]{1,0:T(8,128)(2,1)S(1)} %collective-permute-done.14.refs_0_, bf16[1040,128]{1,0:T(8,128)(2,1)S(1)} %collective-permute-done.15.refs_1_, bf16[2048,1536]{1,0:T(8,128)(2,1)S(1)} %bitcast.21, ...), custom_call_target="tpu_custom_call" | custom-call | flops 2415919104 | bytes 1572864 | tf_op jit(solution)/shard_map/expert_rows/pallas_call | solution.py:217
  54.8 1.6 %collective-permute-start.16 = (bf16[64,2048]{1,0:T(8,128)(2,1)S(1)}, bf16[64,2048]{1,0:T(8,128)(2,1)S(1)}, u32[]{:S(2)}, u32[]{:S(2)}) collective-permute-start(bf16[64,2048]{1,0:T(8,128)(2,1)S(1)} %convert_element_type.73), channel_id=1, source_target_pairs={{6,2},{7,3},{10,6},{11,7},{14,10},{15,11},{12,14},{13,15},{8,12},{... | collective-permute-start | bytes 786440 | tf_op jit(solution)/shard_map/ppermute | solution.py:285
  56.4 0.5 collective-permute-start.17
  56.9 2.6 %collective-permute-done.19.refs_1_ = bf16[1040,128]{1,0:T(8,128)(2,1)S(1)} collective-permute-done((bf16[1040,128]{1,0:T(8,128)(2,1)S(1)}, bf16[1040,128]{1,0:T(8,128)(2,1)S(1)}, u32[]{:S(2)}, u32[]{:S(2)}) %collective-permute-start.19) | collective-permute-done | bytes 266272 | tf_op jit(solution)/shard_map/ppermute | solution.py:285
  59.5 2.8 %expert_rows.16 = (f32[64,2048]{1,0:T(8,128)S(1)}, f32[64,2048]{1,0:T(8,128)S(1)}) custom-call(s32[1]{0:T(128)} %bitcast.6.expert_ref, bf16[1040,128]{1,0:T(8,128)(2,1)S(1)} %collective-permute-done.18.refs_0_, bf16[1040,128]{1,0:T(8,128)(2,1)S(1)} %collective-permute-done.19.refs_1_, bf16[2048,1536]{1,0:T(8,128)(2,1)S(1)} %bitcast.23, ...), custom_call_target="tpu_custom_call" | custom-call | flops 2415919104 | bytes 1572864 | tf_op jit(solution)/shard_map/expert_rows/pallas_call | solution.py:217
  62.3 1.6 %collective-permute-start.23 = (bf16[64,2048]{1,0:T(8,128)(2,1)S(1)}, bf16[64,2048]{1,0:T(8,128)(2,1)S(1)}, u32[]{:S(2)}, u32[]{:S(2)}) collective-permute-start(bf16[64,2048]{1,0:T(8,128)(2,1)S(1)} %convert_element_type.80), channel_id=1, source_target_pairs={{6,2},{7,3},{10,6},{11,7},{14,10},{15,11},{12,14},{13,15},{8,12},{... | collective-permute-start | bytes 786440 | tf_op jit(solution)/shard_map/ppermute | solution.py:285
  64.0 0.5 collective-permute-start.21
  64.5 2.9 %expert_rows.17 = (f32[64,2048]{1,0:T(8,128)S(1)}, f32[64,2048]{1,0:T(8,128)S(1)}, bf16[64,2048]{1,0:T(8,128)(2,1)S(1)}, bf16[64,2048]{1,0:T(8,128)(2,1)S(1)}) custom-call(s32[1]{0:T(128)} %bitcast.6.expert_ref, bf16[1040,128]{1,0:T(8,128)(2,1)S(1)} %get-tuple-element.65.refs_0_, bf16[1040,128]{1,0:T(8,128)(2,1)S(1)} %get-tuple-element.69.refs_1_, ...), custom_call_target="tpu_custom_call" | custom-call | flops 2415919104 | bytes 1572864 | tf_op jit(solution)/shard_map/expert_rows/pallas_call | solution.py:217
  67.4 1.5 %collective-permute-start.26 = (bf16[64,2048]{1,0:T(8,128)(2,1)S(1)}, bf16[64,2048]{1,0:T(8,128)(2,1)S(1)}, u32[]{:S(2)}, u32[]{:S(2)}) collective-permute-start(bf16[64,2048]{1,0:T(8,128)(2,1)S(1)} %get-tuple-element.100), channel_id=1, source_target_pairs={{2,6},{3,7},{6,10},{7,11},{10,14},{11,15},{14,12},{15,13},{12,8},{... | collective-permute-start | bytes 786440 | tf_op jit(solution)/shard_map/ppermute | solution.py:285
  69.0 0.5 collective-permute-start.20
  69.5 2.1 %collective-permute-done.23 = bf16[64,2048]{1,0:T(8,128)(2,1)S(1)} collective-permute-done((bf16[64,2048]{1,0:T(8,128)(2,1)S(1)}, bf16[64,2048]{1,0:T(8,128)(2,1)S(1)}, u32[]{:S(2)}, u32[]{:S(2)}) %collective-permute-start.23) | collective-permute-done | bytes 262176 | tf_op jit(solution)/shard_map/ppermute | solution.py:285
  71.7 1.6 %collective-permute-start.24 = (bf16[64,2048]{1,0:T(8,128)(2,1)S(1)}, bf16[64,2048]{1,0:T(8,128)(2,1)S(1)}, u32[]{:S(2)}, u32[]{:S(2)}) collective-permute-start(bf16[64,2048]{1,0:T(8,128)(2,1)S(1)} %add_convert_fusion.5), channel_id=1, source_target_pairs={{6,2},{7,3},{10,6},{11,7},{14,10},{15,11},{12,14},{13,15},{8,12},{... | collective-permute-start | bytes 786440 | tf_op jit(solution)/shard_map/ppermute | solution.py:285
  73.4 0.5 collective-permute-start.22
  73.9 7.0 %collective-permute-done.24 = bf16[64,2048]{1,0:T(8,128)(2,1)S(1)} collective-permute-done((bf16[64,2048]{1,0:T(8,128)(2,1)S(1)}, bf16[64,2048]{1,0:T(8,128)(2,1)S(1)}, u32[]{:S(2)}, u32[]{:S(2)}) %collective-permute-start.24) | collective-permute-done | bytes 262176 | tf_op jit(solution)/shard_map/ppermute | solution.py:285
  80.9 0.7 collective-permute-start.30
  81.7 1.4 %collective-permute-start.28 = (bf16[64,2048]{1,0:T(8,128)(2,1)S(1)}, bf16[64,2048]{1,0:T(8,128)(2,1)S(1)}, u32[]{:S(2)}, u32[]{:S(2)}) collective-permute-start(bf16[64,2048]{1,0:T(8,128)(2,1)S(1)} %add_convert_fusion.6), channel_id=1, source_target_pairs={{2,6},{3,7},{6,10},{7,11},{10,14},{11,15},{14,12},{15,13},{12,8},{... | collective-permute-start | bytes 786440 | tf_op jit(solution)/shard_map/ppermute | solution.py:285
  83.2 1.7 %collective-permute-start.27 = (bf16[64,2048]{1,0:T(8,128)(2,1)S(1)}, bf16[64,2048]{1,0:T(8,128)(2,1)S(1)}, u32[]{:S(2)}, u32[]{:S(2)}) collective-permute-start(bf16[64,2048]{1,0:T(8,128)(2,1)S(1)} %add_convert_fusion.2), channel_id=1, source_target_pairs={{2,6},{3,7},{6,10},{7,11},{10,14},{11,15},{14,12},{15,13},{12,8},{... | collective-permute-start | bytes 786440 | tf_op jit(solution)/shard_map/ppermute | solution.py:285
  84.9 0.1 add_convert_fusion.3
  84.9 0.4 collective-permute-start.25
  85.4 4.9 %collective-permute-done.30 = bf16[64,2048]{1,0:T(8,128)(2,1)S(1)} collective-permute-done((bf16[64,2048]{1,0:T(8,128)(2,1)S(1)}, bf16[64,2048]{1,0:T(8,128)(2,1)S(1)}, u32[]{:S(2)}, u32[]{:S(2)}) %collective-permute-start.30) | collective-permute-done | bytes 262176 | tf_op jit(solution)/shard_map/ppermute | solution.py:285
  90.3 0.7 collective-permute-start.31
  91.1 1.4 %collective-permute-start.29 = (bf16[64,2048]{1,0:T(8,128)(2,1)S(1)}, bf16[64,2048]{1,0:T(8,128)(2,1)S(1)}, u32[]{:S(2)}, u32[]{:S(2)}) collective-permute-start(bf16[64,2048]{1,0:T(8,128)(2,1)S(1)} %add_convert_fusion.1), channel_id=1, source_target_pairs={{2,6},{3,7},{6,10},{7,11},{10,14},{11,15},{14,12},{15,13},{12,8},{... | collective-permute-start | bytes 786440 | tf_op jit(solution)/shard_map/ppermute | solution.py:285
  92.5 1.4 %collective-permute-done.27 = bf16[64,2048]{1,0:T(8,128)(2,1)S(1)} collective-permute-done((bf16[64,2048]{1,0:T(8,128)(2,1)S(1)}, bf16[64,2048]{1,0:T(8,128)(2,1)S(1)}, u32[]{:S(2)}, u32[]{:S(2)}) %collective-permute-start.27) | collective-permute-done | bytes 262176 | tf_op jit(solution)/shard_map/ppermute | solution.py:285
  93.8 0.1 add_add_fusion.near1_ref
  93.9 0.1 add_add_fusion.1.near0_ref
  94.0 2.7 %collective-permute-done.31.total1_ref = bf16[64,2048]{1,0:T(8,128)(2,1)S(1)} collective-permute-done((bf16[64,2048]{1,0:T(8,128)(2,1)S(1)}, bf16[64,2048]{1,0:T(8,128)(2,1)S(1)}, u32[]{:S(2)}, u32[]{:S(2)}) %collective-permute-start.31) | collective-permute-done | bytes 262176 | tf_op jit(solution)/shard_map/ppermute | solution.py:285
  96.7 0.8 collective-permute-done.29.total0_ref
  97.5 0.9 last_rows.1
  (40 shorter events, 0.6 us)
Async XLA Ops:
  0.0 23.6 %copy-start.1 = (bf16[1,1,768,2048]{3,2,1,0:T(8,128)(2,1)S(1)}, bf16[1,1,768,2048]{3,2,1,0:T(8,128)(2,1)}, u32[]{:S(2)}) copy-start(bf16[1,1,768,2048]{3,2,1,0:T(8,128)(2,1)} %param.13) | copy-start | bytes 9437188
  0.0 18.1 %collective-permute-start.2 = (bf16[2048,1536]{1,0:T(8,128)(2,1)}, bf16[2048,1536]{1,0:T(8,128)(2,1)S(1)}, u32[]{:S(2)}, u32[]{:S(2)}) collective-permute-start(bf16[2048,1536]{1,0:T(8,128)(2,1)} %bitcast.15), channel_id=1, source_target_pairs={{0,1},{1,0},{2,3},{3,2},{4,5},{5,4},{6,7},{7,6},{8,9},{9,8},{10,11... | collective-permute-start | bytes 18874376 | tf_op jit(solution)/shard_map/ppermute | solution.py:285
  0.5 17.7 %collective-permute-start.3 = (bf16[768,2048]{1,0:T(8,128)(2,1)}, bf16[768,2048]{1,0:T(8,128)(2,1)S(1)}, u32[]{:S(2)}, u32[]{:S(2)}) collective-permute-start(bf16[768,2048]{1,0:T(8,128)(2,1)} %bitcast.25), channel_id=1, source_target_pairs={{0,1},{1,0},{2,3},{3,2},{4,5},{5,4},{6,7},{7,6},{8,9},{9,8},{10,11... | collective-permute-start | bytes 9437192 | tf_op jit(solution)/shard_map/ppermute | solution.py:285
  1.8 11.5 %collective-permute-start = (bf16[64,2048]{1,0:T(8,128)(2,1)S(1)}, bf16[64,2048]{1,0:T(8,128)(2,1)S(1)}, u32[]{:S(2)}, u32[]{:S(2)}) collective-permute-start(bf16[64,2048]{1,0:T(8,128)(2,1)S(1)} %get-tuple-element.106), channel_id=1, source_target_pairs={{0,16},{1,17},{2,18},{3,19},{4,20},{5,21},{6,22},{7,23},{8,24},{9,... | collective-permute-start | bytes 786440 | tf_op jit(solution)/shard_map/ppermute | solution.py:20
  6.7 11.3 %collective-permute-start.1 = (bf16[64,2048]{1,0:T(8,128)(2,1)S(1)}, bf16[64,2048]{1,0:T(8,128)(2,1)S(1)}, u32[]{:S(2)}, u32[]{:S(2)}) collective-permute-start(bf16[64,2048]{1,0:T(8,128)(2,1)S(1)} %get-tuple-element.105), channel_id=1, source_target_pairs={{0,16},{1,17},{2,18},{3,19},{4,20},{5,21},{6,22},{7,23},{8,24},{9,... | collective-permute-start | bytes 786440 | tf_op jit(solution)/shard_map/ppermute | solution.py:20
  8.0 1.0 %copy-start.2 = (bf16[128,2048]{1,0:T(8,128)(2,1)S(1)}, bf16[128,2048]{1,0:T(8,128)(2,1)}, u32[]{:S(2)}) copy-start(bf16[128,2048]{1,0:T(8,128)(2,1)} %fresh_ref.1) | copy-start | bytes 1572868
  9.1 0.7 copy-start.3
  9.8 0.7 copy-start.4
  10.5 0.7 copy-start.5
  13.4 6.8 %collective-permute-start.4 = (bf16[1040,128]{1,0:T(8,128)(2,1)S(1)}, bf16[1040,128]{1,0:T(8,128)(2,1)S(1)}, u32[]{:S(2)}, u32[]{:S(2)}) collective-permute-start(bf16[1040,128]{1,0:T(8,128)(2,1)S(1)} %get-tuple-element.65.refs_0_), channel_id=1, source_target_pairs={{2,6},{3,7},{6,10},{7,11},{10,14},{11,15},{14,12},{15,13},{12,8},{... | collective-permute-start | bytes 798728 | tf_op jit(solution)/shard_map/ppermute | solution.py:285
  15.0 6.6 %collective-permute-start.5 = (bf16[1040,128]{1,0:T(8,128)(2,1)S(1)}, bf16[1040,128]{1,0:T(8,128)(2,1)S(1)}, u32[]{:S(2)}, u32[]{:S(2)}) collective-permute-start(bf16[1040,128]{1,0:T(8,128)(2,1)S(1)} %get-tuple-element.65.refs_0_), channel_id=1, source_target_pairs={{6,2},{7,3},{10,6},{11,7},{14,10},{15,11},{12,14},{13,15},{8,12},{... | collective-permute-start | bytes 798728 | tf_op jit(solution)/shard_map/ppermute | solution.py:285
  18.1 11.0 %collective-permute-start.8 = (bf16[1040,128]{1,0:T(8,128)(2,1)S(1)}, bf16[1040,128]{1,0:T(8,128)(2,1)S(1)}, u32[]{:S(2)}, u32[]{:S(2)}) collective-permute-start(bf16[1040,128]{1,0:T(8,128)(2,1)S(1)} %get-tuple-element.69.refs_1_), channel_id=1, source_target_pairs={{2,6},{3,7},{6,10},{7,11},{10,14},{11,15},{14,12},{15,13},{12,8},{... | collective-permute-start | bytes 798728 | tf_op jit(solution)/shard_map/ppermute | solution.py:285
  19.7 9.5 %collective-permute-start.9 = (bf16[1040,128]{1,0:T(8,128)(2,1)S(1)}, bf16[1040,128]{1,0:T(8,128)(2,1)S(1)}, u32[]{:S(2)}, u32[]{:S(2)}) collective-permute-start(bf16[1040,128]{1,0:T(8,128)(2,1)S(1)} %get-tuple-element.69.refs_1_), channel_id=1, source_target_pairs={{6,2},{7,3},{10,6},{11,7},{14,10},{15,11},{12,14},{13,15},{8,12},{... | collective-permute-start | bytes 798728 | tf_op jit(solution)/shard_map/ppermute | solution.py:285
  21.6 12.5 %collective-permute-start.6 = (bf16[1040,128]{1,0:T(8,128)(2,1)S(1)}, bf16[1040,128]{1,0:T(8,128)(2,1)S(1)}, u32[]{:S(2)}, u32[]{:S(2)}) collective-permute-start(bf16[1040,128]{1,0:T(8,128)(2,1)S(1)} %collective-permute-done.4.refs_0_), channel_id=1, source_target_pairs={{2,6},{3,7},{6,10},{7,11},{10,14},{11,15},{14,12},{15,13},{12,8},{... | collective-permute-start | bytes 798728 | tf_op jit(solution)/shard_map/ppermute | solution.py:285
  23.2 11.6 %collective-permute-start.7 = (bf16[1040,128]{1,0:T(8,128)(2,1)S(1)}, bf16[1040,128]{1,0:T(8,128)(2,1)S(1)}, u32[]{:S(2)}, u32[]{:S(2)}) collective-permute-start(bf16[1040,128]{1,0:T(8,128)(2,1)S(1)} %collective-permute-done.5.refs_1_), channel_id=1, source_target_pairs={{6,2},{7,3},{10,6},{11,7},{14,10},{15,11},{12,14},{13,15},{8,12},{... | collective-permute-start | bytes 798728 | tf_op jit(solution)/shard_map/ppermute | solution.py:285
  23.6 2.8 %copy-start = (bf16[1,1,2048,1536]{3,2,1,0:T(8,128)(2,1)S(1)}, bf16[1,1,2048,1536]{3,2,1,0:T(8,128)(2,1)}, u32[]{:S(2)}) copy-start(bf16[1,1,2048,1536]{3,2,1,0:T(8,128)(2,1)} %param.12) | copy-start | bytes 18874372
  29.2 10.3 %collective-permute-start.10 = (bf16[1040,128]{1,0:T(8,128)(2,1)S(1)}, bf16[1040,128]{1,0:T(8,128)(2,1)S(1)}, u32[]{:S(2)}, u32[]{:S(2)}) collective-permute-start(bf16[1040,128]{1,0:T(8,128)(2,1)S(1)} %collective-permute-done.8.refs_0_), channel_id=1, source_target_pairs={{2,6},{3,7},{6,10},{7,11},{10,14},{11,15},{14,12},{15,13},{12,8},{... | collective-permute-start | bytes 798728 | tf_op jit(solution)/shard_map/ppermute | solution.py:285
  30.8 9.6 %collective-permute-start.11 = (bf16[1040,128]{1,0:T(8,128)(2,1)S(1)}, bf16[1040,128]{1,0:T(8,128)(2,1)S(1)}, u32[]{:S(2)}, u32[]{:S(2)}) collective-permute-start(bf16[1040,128]{1,0:T(8,128)(2,1)S(1)} %collective-permute-done.9.refs_1_), channel_id=1, source_target_pairs={{6,2},{7,3},{10,6},{11,7},{14,10},{15,11},{12,14},{13,15},{8,12},{... | collective-permute-start | bytes 798728 | tf_op jit(solution)/shard_map/ppermute | solution.py:285
  34.7 10.5 %collective-permute-start.12 = (bf16[1040,128]{1,0:T(8,128)(2,1)S(1)}, bf16[1040,128]{1,0:T(8,128)(2,1)S(1)}, u32[]{:S(2)}, u32[]{:S(2)}) collective-permute-start(bf16[1040,128]{1,0:T(8,128)(2,1)S(1)} %collective-permute-done.6.refs_0_), channel_id=1, source_target_pairs={{2,6},{3,7},{6,10},{7,11},{10,14},{11,15},{14,12},{15,13},{12,8},{... | collective-permute-start | bytes 798728 | tf_op jit(solution)/shard_map/ppermute | solution.py:285
  36.3 9.8 %collective-permute-start.13 = (bf16[1040,128]{1,0:T(8,128)(2,1)S(1)}, bf16[1040,128]{1,0:T(8,128)(2,1)S(1)}, u32[]{:S(2)}, u32[]{:S(2)}) collective-permute-start(bf16[1040,128]{1,0:T(8,128)(2,1)S(1)} %collective-permute-done.7.refs_1_), channel_id=1, source_target_pairs={{6,2},{7,3},{10,6},{11,7},{14,10},{15,11},{12,14},{13,15},{8,12},{... | collective-permute-start | bytes 798728 | tf_op jit(solution)/shard_map/ppermute | solution.py:285
  40.4 10.1 %collective-permute-start.14 = (bf16[1040,128]{1,0:T(8,128)(2,1)S(1)}, bf16[1040,128]{1,0:T(8,128)(2,1)S(1)}, u32[]{:S(2)}, u32[]{:S(2)}) collective-permute-start(bf16[1040,128]{1,0:T(8,128)(2,1)S(1)} %collective-permute-done.10.refs_0_), channel_id=1, source_target_pairs={{2,6},{3,7},{6,10},{7,11},{10,14},{11,15},{14,12},{15,13},{12,8},{... | collective-permute-start | bytes 798728 | tf_op jit(solution)/shard_map/ppermute | solution.py:285
  42.0 8.5 %collective-permute-start.15 = (bf16[1040,128]{1,0:T(8,128)(2,1)S(1)}, bf16[1040,128]{1,0:T(8,128)(2,1)S(1)}, u32[]{:S(2)}, u32[]{:S(2)}) collective-permute-start(bf16[1040,128]{1,0:T(8,128)(2,1)S(1)} %collective-permute-done.11.refs_1_), channel_id=1, source_target_pairs={{6,2},{7,3},{10,6},{11,7},{14,10},{15,11},{12,14},{13,15},{8,12},{... | collective-permute-start | bytes 798728 | tf_op jit(solution)/shard_map/ppermute | solution.py:285
  46.1 10.8 %collective-permute-start.18 = (bf16[1040,128]{1,0:T(8,128)(2,1)S(1)}, bf16[1040,128]{1,0:T(8,128)(2,1)S(1)}, u32[]{:S(2)}, u32[]{:S(2)}) collective-permute-start(bf16[1040,128]{1,0:T(8,128)(2,1)S(1)} %collective-permute-done.12.refs_0_), channel_id=1, source_target_pairs={{2,6},{3,7},{6,10},{7,11},{10,14},{11,15},{14,12},{15,13},{12,8},{... | collective-permute-start | bytes 798728 | tf_op jit(solution)/shard_map/ppermute | solution.py:285
  50.5 9.0 %collective-permute-start.19 = (bf16[1040,128]{1,0:T(8,128)(2,1)S(1)}, bf16[1040,128]{1,0:T(8,128)(2,1)S(1)}, u32[]{:S(2)}, u32[]{:S(2)}) collective-permute-start(bf16[1040,128]{1,0:T(8,128)(2,1)S(1)} %collective-permute-done.15.refs_1_), channel_id=1, source_target_pairs={{6,2},{7,3},{10,6},{11,7},{14,10},{15,11},{12,14},{13,15},{8,12},{... | collective-permute-start | bytes 798728 | tf_op jit(solution)/shard_map/ppermute | solution.py:285
  54.8 9.7 %collective-permute-start.16 = (bf16[64,2048]{1,0:T(8,128)(2,1)S(1)}, bf16[64,2048]{1,0:T(8,128)(2,1)S(1)}, u32[]{:S(2)}, u32[]{:S(2)}) collective-permute-start(bf16[64,2048]{1,0:T(8,128)(2,1)S(1)} %convert_element_type.73), channel_id=1, source_target_pairs={{6,2},{7,3},{10,6},{11,7},{14,10},{15,11},{12,14},{13,15},{8,12},{... | collective-permute-start | bytes 786440 | tf_op jit(solution)/shard_map/ppermute | solution.py:285
  56.4 8.1 %collective-permute-start.17 = (bf16[64,2048]{1,0:T(8,128)(2,1)S(1)}, bf16[64,2048]{1,0:T(8,128)(2,1)S(1)}, u32[]{:S(2)}, u32[]{:S(2)}) collective-permute-start(bf16[64,2048]{1,0:T(8,128)(2,1)S(1)} %convert_element_type.74), channel_id=1, source_target_pairs={{2,6},{3,7},{6,10},{7,11},{10,14},{11,15},{14,12},{15,13},{12,8},{... | collective-permute-start | bytes 786440 | tf_op jit(solution)/shard_map/ppermute | solution.py:285
  62.3 9.3 %collective-permute-start.23 = (bf16[64,2048]{1,0:T(8,128)(2,1)S(1)}, bf16[64,2048]{1,0:T(8,128)(2,1)S(1)}, u32[]{:S(2)}, u32[]{:S(2)}) collective-permute-start(bf16[64,2048]{1,0:T(8,128)(2,1)S(1)} %convert_element_type.80), channel_id=1, source_target_pairs={{6,2},{7,3},{10,6},{11,7},{14,10},{15,11},{12,14},{13,15},{8,12},{... | collective-permute-start | bytes 786440 | tf_op jit(solution)/shard_map/ppermute | solution.py:285
  64.0 9.3 %collective-permute-start.21 = (bf16[64,2048]{1,0:T(8,128)(2,1)S(1)}, bf16[64,2048]{1,0:T(8,128)(2,1)S(1)}, u32[]{:S(2)}, u32[]{:S(2)}) collective-permute-start(bf16[64,2048]{1,0:T(8,128)(2,1)S(1)} %convert_element_type.75), channel_id=1, source_target_pairs={{2,6},{3,7},{6,10},{7,11},{10,14},{11,15},{14,12},{15,13},{12,8},{... | collective-permute-start | bytes 786440 | tf_op jit(solution)/shard_map/ppermute | solution.py:285
  67.4 15.7 %collective-permute-start.26 = (bf16[64,2048]{1,0:T(8,128)(2,1)S(1)}, bf16[64,2048]{1,0:T(8,128)(2,1)S(1)}, u32[]{:S(2)}, u32[]{:S(2)}) collective-permute-start(bf16[64,2048]{1,0:T(8,128)(2,1)S(1)} %get-tuple-element.100), channel_id=1, source_target_pairs={{2,6},{3,7},{6,10},{7,11},{10,14},{11,15},{14,12},{15,13},{12,8},{... | collective-permute-start | bytes 786440 | tf_op jit(solution)/shard_map/ppermute | solution.py:285
  69.0 15.9 %collective-permute-start.20 = (bf16[64,2048]{1,0:T(8,128)(2,1)S(1)}, bf16[64,2048]{1,0:T(8,128)(2,1)S(1)}, u32[]{:S(2)}, u32[]{:S(2)}) collective-permute-start(bf16[64,2048]{1,0:T(8,128)(2,1)S(1)} %get-tuple-element.92), channel_id=1, source_target_pairs={{6,2},{7,3},{10,6},{11,7},{14,10},{15,11},{12,14},{13,15},{8,12},{... | collective-permute-start | bytes 786440 | tf_op jit(solution)/shard_map/ppermute | solution.py:285
  71.7 9.2 %collective-permute-start.24 = (bf16[64,2048]{1,0:T(8,128)(2,1)S(1)}, bf16[64,2048]{1,0:T(8,128)(2,1)S(1)}, u32[]{:S(2)}, u32[]{:S(2)}) collective-permute-start(bf16[64,2048]{1,0:T(8,128)(2,1)S(1)} %add_convert_fusion.5), channel_id=1, source_target_pairs={{6,2},{7,3},{10,6},{11,7},{14,10},{15,11},{12,14},{13,15},{8,12},{... | collective-permute-start | bytes 786440 | tf_op jit(solution)/shard_map/ppermute | solution.py:285
  73.4 8.3 %collective-permute-start.22 = (bf16[64,2048]{1,0:T(8,128)(2,1)S(1)}, bf16[64,2048]{1,0:T(8,128)(2,1)S(1)}, u32[]{:S(2)}, u32[]{:S(2)}) collective-permute-start(bf16[64,2048]{1,0:T(8,128)(2,1)S(1)} %add_convert_fusion.7), channel_id=1, source_target_pairs={{2,6},{3,7},{6,10},{7,11},{10,14},{11,15},{14,12},{15,13},{12,8},{... | collective-permute-start | bytes 786440 | tf_op jit(solution)/shard_map/ppermute | solution.py:285
  80.9 9.3 %collective-permute-start.30 = (bf16[64,2048]{1,0:T(8,128)(2,1)S(1)}, bf16[64,2048]{1,0:T(8,128)(2,1)S(1)}, u32[]{:S(2)}, u32[]{:S(2)}) collective-permute-start(bf16[64,2048]{1,0:T(8,128)(2,1)S(1)} %add_convert_fusion.4), channel_id=1, source_target_pairs={{6,2},{7,3},{10,6},{11,7},{14,10},{15,11},{12,14},{13,15},{8,12},{... | collective-permute-start | bytes 786440 | tf_op jit(solution)/shard_map/ppermute | solution.py:285
  81.7 9.3 %collective-permute-start.28 = (bf16[64,2048]{1,0:T(8,128)(2,1)S(1)}, bf16[64,2048]{1,0:T(8,128)(2,1)S(1)}, u32[]{:S(2)}, u32[]{:S(2)}) collective-permute-start(bf16[64,2048]{1,0:T(8,128)(2,1)S(1)} %add_convert_fusion.6), channel_id=1, source_target_pairs={{2,6},{3,7},{6,10},{7,11},{10,14},{11,15},{14,12},{15,13},{12,8},{... | collective-permute-start | bytes 786440 | tf_op jit(solution)/shard_map/ppermute | solution.py:285
  83.2 10.7 %collective-permute-start.27 = (bf16[64,2048]{1,0:T(8,128)(2,1)S(1)}, bf16[64,2048]{1,0:T(8,128)(2,1)S(1)}, u32[]{:S(2)}, u32[]{:S(2)}) collective-permute-start(bf16[64,2048]{1,0:T(8,128)(2,1)S(1)} %add_convert_fusion.2), channel_id=1, source_target_pairs={{2,6},{3,7},{6,10},{7,11},{10,14},{11,15},{14,12},{15,13},{12,8},{... | collective-permute-start | bytes 786440 | tf_op jit(solution)/shard_map/ppermute | solution.py:285
  84.9 9.0 %collective-permute-start.25 = (bf16[64,2048]{1,0:T(8,128)(2,1)S(1)}, bf16[64,2048]{1,0:T(8,128)(2,1)S(1)}, u32[]{:S(2)}, u32[]{:S(2)}) collective-permute-start(bf16[64,2048]{1,0:T(8,128)(2,1)S(1)} %add_convert_fusion.3), channel_id=1, source_target_pairs={{6,2},{7,3},{10,6},{11,7},{14,10},{15,11},{12,14},{13,15},{8,12},{... | collective-permute-start | bytes 786440 | tf_op jit(solution)/shard_map/ppermute | solution.py:285
  90.3 6.4 %collective-permute-start.31 = (bf16[64,2048]{1,0:T(8,128)(2,1)S(1)}, bf16[64,2048]{1,0:T(8,128)(2,1)S(1)}, u32[]{:S(2)}, u32[]{:S(2)}) collective-permute-start(bf16[64,2048]{1,0:T(8,128)(2,1)S(1)} %add_convert_fusion), channel_id=1, source_target_pairs={{6,2},{7,3},{10,6},{11,7},{14,10},{15,11},{12,14},{13,15},{8,12},{... | collective-permute-start | bytes 786440 | tf_op jit(solution)/shard_map/ppermute | solution.py:285
  91.1 6.4 %collective-permute-start.29 = (bf16[64,2048]{1,0:T(8,128)(2,1)S(1)}, bf16[64,2048]{1,0:T(8,128)(2,1)S(1)}, u32[]{:S(2)}, u32[]{:S(2)}) collective-permute-start(bf16[64,2048]{1,0:T(8,128)(2,1)S(1)} %add_convert_fusion.1), channel_id=1, source_target_pairs={{2,6},{3,7},{6,10},{7,11},{10,14},{11,15},{14,12},{15,13},{12,8},{... | collective-permute-start | bytes 786440 | tf_op jit(solution)/shard_map/ppermute | solution.py:285

commit v15 on v14

--- a/solution.py
+++ b/solution.py
@@ -71,6 +71,32 @@
     picked = flat_back[position].reshape(tok_dev, topk_count, width).astype(jnp.float32)
     mixed = jnp.sum(picked * gate_weights[0][:, :, None], axis=1)
     return (wide_input + mixed).astype(jnp.bfloat16)[None]
+
+
+def chunks_kernel(rows_ref, first_ref, second_ref, sems):
+    half = first_ref.shape[0]
+    copies = [
+        pltpu.make_async_copy(rows_ref.at[i * half : (i + 1) * half, :], out_ref, sems.at[i])
+        for i, out_ref in enumerate((first_ref, second_ref))
+    ]
+    for copy in copies:
+        copy.start()
+    for copy in copies:
+        copy.wait()
+
+
+def two_chunks(rows):
+    half = jax.ShapeDtypeStruct((rows.shape[0] // 2, rows.shape[1]), rows.dtype)
+    return pl.pallas_call(
+        chunks_kernel,
+        out_shape=(half, half),
+        in_specs=[pl.BlockSpec(memory_space=pltpu.HBM)],
+        out_specs=(pl.BlockSpec(memory_space=pltpu.HBM),) * 2,
+        scratch_shapes=[pltpu.SemaphoreType.DMA((2,))],
+        compiler_params=pltpu.CompilerParams(vmem_limit_bytes=60 * MIB),
+        cost_estimate=pl.CostEstimate(flops=0, bytes_accessed=4 * half.size * 2, transcendentals=0),
+        name="two_chunks",
+    )(rows)
 
 
 def normed_rows(rows, gain):
@@ -286,10 +312,11 @@
 
     cuts = [slice(0, half), slice(half, rows)]
     own = (w_gate_up[0, 0], w_down[0, 0])
-    swapped = lax.optimization_barrier((*own, section_id, expert_id))[:2]
+    leaving = two_chunks(previous[0])
+    swapped = lax.optimization_barrier((*own, section_id, expert_id, leaving))[:2]
     other = tuple(move(w, swap) for w in swapped)
     base, coefs, fresh, gain = base_rows(fresh, norm_gain, routes[0].T, gate_weights[0].T, devices_exp)
-    arrived = [from_behind(previous[0, cut], "section", 1) for cut in cuts]
+    arrived = [from_behind(chunk, "section", 1) for chunk in leaving]
     packed, arrival = zip(*(norm_rows(section_id, base, coefs, fresh, arrived[c], gain, c) for c in range(2)))
     packed = list(packed)
 

time: 98.7 us -> 115 us (1.17)
  Pallas kernels: 23.6 us -> 40.6 us
    pallas_call x0 -> x1, Pallas kernels: none -> 17 us  [two_chunks(): pl.pallas_call(chunks_kernel, out_shape=(half, half), in_specs=[pl.BlockS...]
    unnamed x12, local copies, waits for them, and re-layouts: 5.89 us -> 7.78 us
    ppermute x30, waiting for transfers between devices: 25.2 us -> 23.9 us  [move(): return lax.ppermute(value, 'expert', pairs)]
    squeeze x1 -> x0, local copies, waits for them, and re-layouts: 1.32 us -> none  [relay_body(): arrived = [from_behind(previous[0, cut], 'section', 1) for cut in cuts]]
  transfers between devices with their start and end apart: 32 -> 32, of which waited for: 13 -> 12; matrix products, arithmetic and copies ran while one was open for 2% -> 1% of each run, Pallas kernels for 23% -> 20%
where the time goes in v15:
time: 115 us; the launch traced here: 114 us
  Pallas kernels  40.6 us (35%)
  starting transfers between devices  36.1 us (31%)
  waiting for transfers between devices  28.8 us (25%)
  local copies, waits for them, and re-layouts  7.78 us (7%)
    ppermute x30, starting transfers between devices, move(): return lax.ppermute(value, 'expert', pairs)  29.9 us
    ppermute x30, waiting for transfers between devices, move(): return lax.ppermute(value, 'expert', pairs)  23.9 us
    pallas_call x9, Pallas kernels, expert_rows(): pl.pallas_call(functools.partial(mlp_kernel, parts=len(payloads), adds=le...  22.3 us
    pallas_call x1, Pallas kernels, two_chunks(): pl.pallas_call(chunks_kernel, out_shape=(half, half), in_specs=[pl.BlockS...  17 us
    unnamed x12, local copies, waits for them, and re-layouts  7.78 us
    ppermute x2, starting transfers between devices, from_behind(): return lax.ppermute(value, axis, pairs)  6.16 us
    ppermute x2, waiting for transfers between devices, from_behind(): return lax.ppermute(value, axis, pairs)  4.88 us
  transfers between devices with their start and end apart: 32, of which 12 were waited for; matrix products, arithmetic and copies ran while one was open for 1% of the time, Pallas kernels for 20%

profile of v15, /device:TPU:0, one launch (start us, length us, event | category | flops | bytes accessed | tf_op | source)
XLA Modules:
  0.0 114.2 jit_solution(13173201049800590176)
XLA Ops:
  0.0 17.0 %two_chunks.1 = (bf16[64,2048]{1,0:T(8,128)(2,1)}, bf16[64,2048]{1,0:T(8,128)(2,1)}) custom-call(bf16[128,2048]{1,0:T(8,128)(2,1)} %bitcast.34), custom_call_target="tpu_custom_call" | custom-call | bytes 1048576 | tf_op jit(solution)/shard_map/two_chunks/pallas_call | solution.py:90
  17.0 0.5 collective-permute-start.2
  17.5 0.1 collective-permute-start.3
  17.6 4.9 %collective-permute-start = (bf16[64,2048]{1,0:T(8,128)(2,1)}, bf16[64,2048]{1,0:T(8,128)(2,1)S(1)}, u32[]{:S(2)}, u32[]{:S(2)}) collective-permute-start(bf16[64,2048]{1,0:T(8,128)(2,1)} %get-tuple-element.60), channel_id=1, source_target_pairs={{0,16},{1,17},{2,18},{3,19},{4,20},{5,21},{6,22},{7,23},{8,24},{9,... | collective-permute-start | bytes 786440 | tf_op jit(solution)/shard_map/ppermute | solution.py:20
  22.5 1.3 %collective-permute-start.1 = (bf16[64,2048]{1,0:T(8,128)(2,1)}, bf16[64,2048]{1,0:T(8,128)(2,1)S(1)}, u32[]{:S(2)}, u32[]{:S(2)}) collective-permute-start(bf16[64,2048]{1,0:T(8,128)(2,1)} %get-tuple-element.64), channel_id=1, source_target_pairs={{0,16},{1,17},{2,18},{3,19},{4,20},{5,21},{6,22},{7,23},{8,24},{9,... | collective-permute-start | bytes 786440 | tf_op jit(solution)/shard_map/ppermute | solution.py:20
  23.8 1.0 copy-done.2
  24.8 0.7 copy-done.3
  25.5 0.7 copy-done.4
  26.2 0.7 copy-done.5
  26.9 0.2 base_rows.1
  27.2 2.3 %collective-permute-done.arrived_ref = bf16[64,2048]{1,0:T(8,128)(2,1)S(1)} collective-permute-done((bf16[64,2048]{1,0:T(8,128)(2,1)}, bf16[64,2048]{1,0:T(8,128)(2,1)S(1)}, u32[]{:S(2)}, u32[]{:S(2)}) %collective-permute-start) | collective-permute-done | bytes 262176 | tf_op jit(solution)/shard_map/ppermute | solution.py:20
  29.5 1.5 %collective-permute-start.4 = (bf16[1040,128]{1,0:T(8,128)(2,1)S(1)}, bf16[1040,128]{1,0:T(8,128)(2,1)S(1)}, u32[]{:S(2)}, u32[]{:S(2)}) collective-permute-start(bf16[1040,128]{1,0:T(8,128)(2,1)S(1)} %get-tuple-element.69.refs_0_), channel_id=1, source_target_pairs={{2,6},{3,7},{6,10},{7,11},{10,14},{11,15},{14,12},{15,13},{12,8},{... | collective-permute-start | bytes 798728 | tf_op jit(solution)/shard_map/ppermute | solution.py:311
  31.0 0.5 collective-permute-start.5
  31.6 2.6 %collective-permute-done.1.arrived_ref = bf16[64,2048]{1,0:T(8,128)(2,1)S(1)} collective-permute-done((bf16[64,2048]{1,0:T(8,128)(2,1)}, bf16[64,2048]{1,0:T(8,128)(2,1)S(1)}, u32[]{:S(2)}, u32[]{:S(2)}) %collective-permute-start.1) | collective-permute-done | bytes 262176 | tf_op jit(solution)/shard_map/ppermute | solution.py:20
  34.3 1.5 %collective-permute-start.8 = (bf16[1040,128]{1,0:T(8,128)(2,1)S(1)}, bf16[1040,128]{1,0:T(8,128)(2,1)S(1)}, u32[]{:S(2)}, u32[]{:S(2)}) collective-permute-start(bf16[1040,128]{1,0:T(8,128)(2,1)S(1)} %get-tuple-element.73.refs_1_), channel_id=1, source_target_pairs={{2,6},{3,7},{6,10},{7,11},{10,14},{11,15},{14,12},{15,13},{12,8},{... | collective-permute-start | bytes 798728 | tf_op jit(solution)/shard_map/ppermute | solution.py:311
  35.8 0.5 collective-permute-start.9
  36.3 1.1 collective-permute-done.5.refs_1_
  37.5 1.6 %collective-permute-start.6 = (bf16[1040,128]{1,0:T(8,128)(2,1)S(1)}, bf16[1040,128]{1,0:T(8,128)(2,1)S(1)}, u32[]{:S(2)}, u32[]{:S(2)}) collective-permute-start(bf16[1040,128]{1,0:T(8,128)(2,1)S(1)} %collective-permute-done.4.refs_0_), channel_id=1, source_target_pairs={{2,6},{3,7},{6,10},{7,11},{10,14},{11,15},{14,12},{15,13},{12,8},{... | collective-permute-start | bytes 798728 | tf_op jit(solution)/shard_map/ppermute | solution.py:311
  39.1 0.4 collective-permute-start.7
  39.5 2.8 %copy-done = bf16[1,1,2048,1536]{3,2,1,0:T(8,128)(2,1)S(1)} copy-done((bf16[1,1,2048,1536]{3,2,1,0:T(8,128)(2,1)S(1)}, bf16[1,1,2048,1536]{3,2,1,0:T(8,128)(2,1)}, u32[]{:S(2)}) %copy-start) | copy-done | bytes 6291480
  42.3 1.9 %copy-done.1 = bf16[1,1,768,2048]{3,2,1,0:T(8,128)(2,1)S(1)} copy-done((bf16[1,1,768,2048]{3,2,1,0:T(8,128)(2,1)S(1)}, bf16[1,1,768,2048]{3,2,1,0:T(8,128)(2,1)}, u32[]{:S(2)}) %copy-start.1) | copy-done | bytes 3145752
  44.2 2.8 %expert_rows.9 = (f32[64,2048]{1,0:T(8,128)S(1)}, f32[64,2048]{1,0:T(8,128)S(1)}) custom-call(s32[1]{0:T(128)} %bitcast.6.expert_ref, bf16[1040,128]{1,0:T(8,128)(2,1)S(1)} %collective-permute-done.4.refs_0_, bf16[1040,128]{1,0:T(8,128)(2,1)S(1)} %collective-permute-done.5.refs_1_, bf16[2048,1536]{1,0:T(8,128)(2,1)S(1)} %bitcast.13, ...), custom_call_target="tpu_custom_call" | custom-call | flops 2415919104 | bytes 1572864 | tf_op jit(solution)/shard_map/expert_rows/pallas_call | solution.py:243
  47.0 1.6 %collective-permute-start.10 = (bf16[1040,128]{1,0:T(8,128)(2,1)S(1)}, bf16[1040,128]{1,0:T(8,128)(2,1)S(1)}, u32[]{:S(2)}, u32[]{:S(2)}) collective-permute-start(bf16[1040,128]{1,0:T(8,128)(2,1)S(1)} %collective-permute-done.8.refs_0_), channel_id=1, source_target_pairs={{2,6},{3,7},{6,10},{7,11},{10,14},{11,15},{14,12},{15,13},{12,8},{... | collective-permute-start | bytes 798728 | tf_op jit(solution)/shard_map/ppermute | solution.py:311
  48.6 0.5 collective-permute-start.11
  49.1 2.8 %expert_rows.10 = (f32[64,2048]{1,0:T(8,128)S(1)}, f32[64,2048]{1,0:T(8,128)S(1)}) custom-call(s32[1]{0:T(128)} %bitcast.6.expert_ref, bf16[1040,128]{1,0:T(8,128)(2,1)S(1)} %collective-permute-done.8.refs_0_, bf16[1040,128]{1,0:T(8,128)(2,1)S(1)} %collective-permute-done.9.refs_1_, bf16[2048,1536]{1,0:T(8,128)(2,1)S(1)} %bitcast.14, ...), custom_call_target="tpu_custom_call" | custom-call | flops 2415919104 | bytes 1572864 | tf_op jit(solution)/shard_map/expert_rows/pallas_call | solution.py:243
  51.9 1.6 %collective-permute-start.12 = (bf16[1040,128]{1,0:T(8,128)(2,1)S(1)}, bf16[1040,128]{1,0:T(8,128)(2,1)S(1)}, u32[]{:S(2)}, u32[]{:S(2)}) collective-permute-start(bf16[1040,128]{1,0:T(8,128)(2,1)S(1)} %collective-permute-done.6.refs_0_), channel_id=1, source_target_pairs={{2,6},{3,7},{6,10},{7,11},{10,14},{11,15},{14,12},{15,13},{12,8},{... | collective-permute-start | bytes 798728 | tf_op jit(solution)/shard_map/ppermute | solution.py:311
  53.5 0.5 collective-permute-start.13
  54.0 2.8 %expert_rows.11 = (f32[64,2048]{1,0:T(8,128)S(1)}, f32[64,2048]{1,0:T(8,128)S(1)}) custom-call(s32[1]{0:T(128)} %bitcast.6.expert_ref, bf16[1040,128]{1,0:T(8,128)(2,1)S(1)} %collective-permute-done.6.refs_0_, bf16[1040,128]{1,0:T(8,128)(2,1)S(1)} %collective-permute-done.7.refs_1_, bf16[2048,1536]{1,0:T(8,128)(2,1)S(1)} %bitcast.15, ...), custom_call_target="tpu_custom_call" | custom-call | flops 2415919104 | bytes 1572864 | tf_op jit(solution)/shard_map/expert_rows/pallas_call | solution.py:243
  56.7 1.1 collective-permute-done.11.refs_1_
  57.9 1.6 %collective-permute-start.14 = (bf16[1040,128]{1,0:T(8,128)(2,1)S(1)}, bf16[1040,128]{1,0:T(8,128)(2,1)S(1)}, u32[]{:S(2)}, u32[]{:S(2)}) collective-permute-start(bf16[1040,128]{1,0:T(8,128)(2,1)S(1)} %collective-permute-done.10.refs_0_), channel_id=1, source_target_pairs={{2,6},{3,7},{6,10},{7,11},{10,14},{11,15},{14,12},{15,13},{12,8},{... | collective-permute-start | bytes 798728 | tf_op jit(solution)/shard_map/ppermute | solution.py:311
  59.5 0.4 collective-permute-start.15
  59.9 2.8 %expert_rows.12 = (f32[64,2048]{1,0:T(8,128)S(1)}, f32[64,2048]{1,0:T(8,128)S(1)}) custom-call(s32[1]{0:T(128)} %bitcast.6.expert_ref, bf16[1040,128]{1,0:T(8,128)(2,1)S(1)} %collective-permute-done.10.refs_0_, bf16[1040,128]{1,0:T(8,128)(2,1)S(1)} %collective-permute-done.11.refs_1_, bf16[2048,1536]{1,0:T(8,128)(2,1)S(1)} %bitcast.16, ...), custom_call_target="tpu_custom_call" | custom-call | flops 2415919104 | bytes 1572864 | tf_op jit(solution)/shard_map/expert_rows/pallas_call | solution.py:243
  62.7 0.9 collective-permute-done.13.refs_1_
  63.6 1.6 %collective-permute-start.18 = (bf16[1040,128]{1,0:T(8,128)(2,1)S(1)}, bf16[1040,128]{1,0:T(8,128)(2,1)S(1)}, u32[]{:S(2)}, u32[]{:S(2)}) collective-permute-start(bf16[1040,128]{1,0:T(8,128)(2,1)S(1)} %collective-permute-done.12.refs_0_), channel_id=1, source_target_pairs={{2,6},{3,7},{6,10},{7,11},{10,14},{11,15},{14,12},{15,13},{12,8},{... | collective-permute-start | bytes 798728 | tf_op jit(solution)/shard_map/ppermute | solution.py:311
  65.2 2.8 %expert_rows.13 = (f32[64,2048]{1,0:T(8,128)S(1)}, f32[64,2048]{1,0:T(8,128)S(1)}) custom-call(s32[1]{0:T(128)} %bitcast.6.expert_ref, bf16[1040,128]{1,0:T(8,128)(2,1)S(1)} %collective-permute-done.12.refs_0_, bf16[1040,128]{1,0:T(8,128)(2,1)S(1)} %collective-permute-done.13.refs_1_, bf16[2048,1536]{1,0:T(8,128)(2,1)S(1)} %bitcast.17, ...), custom_call_target="tpu_custom_call" | custom-call | flops 2415919104 | bytes 1572864 | tf_op jit(solution)/shard_map/expert_rows/pallas_call | solution.py:243
  68.0 0.5 collective-permute-start.19
  68.5 2.8 %expert_rows.14 = (f32[64,2048]{1,0:T(8,128)S(1)}, f32[64,2048]{1,0:T(8,128)S(1)}) custom-call(s32[1]{0:T(128)} %bitcast.6.expert_ref, bf16[1040,128]{1,0:T(8,128)(2,1)S(1)} %collective-permute-done.14.refs_0_, bf16[1040,128]{1,0:T(8,128)(2,1)S(1)} %collective-permute-done.15.refs_1_, bf16[2048,1536]{1,0:T(8,128)(2,1)S(1)} %bitcast.18, ...), custom_call_target="tpu_custom_call" | custom-call | flops 2415919104 | bytes 1572864 | tf_op jit(solution)/shard_map/expert_rows/pallas_call | solution.py:243
  71.3 1.5 %collective-permute-start.16 = (bf16[64,2048]{1,0:T(8,128)(2,1)S(1)}, bf16[64,2048]{1,0:T(8,128)(2,1)S(1)}, u32[]{:S(2)}, u32[]{:S(2)}) collective-permute-start(bf16[64,2048]{1,0:T(8,128)(2,1)S(1)} %convert_element_type.73), channel_id=1, source_target_pairs={{6,2},{7,3},{10,6},{11,7},{14,10},{15,11},{12,14},{13,15},{8,12},{... | collective-permute-start | bytes 786440 | tf_op jit(solution)/shard_map/ppermute | solution.py:311
  72.8 0.7 collective-permute-start.17
  73.5 1.8 %collective-permute-done.19.refs_1_ = bf16[1040,128]{1,0:T(8,128)(2,1)S(1)} collective-permute-done((bf16[1040,128]{1,0:T(8,128)(2,1)S(1)}, bf16[1040,128]{1,0:T(8,128)(2,1)S(1)}, u32[]{:S(2)}, u32[]{:S(2)}) %collective-permute-start.19) | collective-permute-done | bytes 266272 | tf_op jit(solution)/shard_map/ppermute | solution.py:311
  75.3 2.8 %expert_rows.16 = (f32[64,2048]{1,0:T(8,128)S(1)}, f32[64,2048]{1,0:T(8,128)S(1)}) custom-call(s32[1]{0:T(128)} %bitcast.6.expert_ref, bf16[1040,128]{1,0:T(8,128)(2,1)S(1)} %collective-permute-done.18.refs_0_, bf16[1040,128]{1,0:T(8,128)(2,1)S(1)} %collective-permute-done.19.refs_1_, bf16[2048,1536]{1,0:T(8,128)(2,1)S(1)} %bitcast.20, ...), custom_call_target="tpu_custom_call" | custom-call | flops 2415919104 | bytes 1572864 | tf_op jit(solution)/shard_map/expert_rows/pallas_call | solution.py:243
  78.1 1.6 %collective-permute-start.23 = (bf16[64,2048]{1,0:T(8,128)(2,1)S(1)}, bf16[64,2048]{1,0:T(8,128)(2,1)S(1)}, u32[]{:S(2)}, u32[]{:S(2)}) collective-permute-start(bf16[64,2048]{1,0:T(8,128)(2,1)S(1)} %convert_element_type.80), channel_id=1, source_target_pairs={{6,2},{7,3},{10,6},{11,7},{14,10},{15,11},{12,14},{13,15},{8,12},{... | collective-permute-start | bytes 786440 | tf_op jit(solution)/shard_map/ppermute | solution.py:311
  79.8 0.5 collective-permute-start.21
  80.3 2.9 %expert_rows.17 = (f32[64,2048]{1,0:T(8,128)S(1)}, f32[64,2048]{1,0:T(8,128)S(1)}, bf16[64,2048]{1,0:T(8,128)(2,1)S(1)}, bf16[64,2048]{1,0:T(8,128)(2,1)S(1)}) custom-call(s32[1]{0:T(128)} %bitcast.6.expert_ref, bf16[1040,128]{1,0:T(8,128)(2,1)S(1)} %get-tuple-element.69.refs_0_, bf16[1040,128]{1,0:T(8,128)(2,1)S(1)} %get-tuple-element.73.refs_1_, ...), custom_call_target="tpu_custom_call" | custom-call | flops 2415919104 | bytes 1572864 | tf_op jit(solution)/shard_map/expert_rows/pallas_call | solution.py:243
  83.1 1.4 %collective-permute-start.26 = (bf16[64,2048]{1,0:T(8,128)(2,1)S(1)}, bf16[64,2048]{1,0:T(8,128)(2,1)S(1)}, u32[]{:S(2)}, u32[]{:S(2)}) collective-permute-start(bf16[64,2048]{1,0:T(8,128)(2,1)S(1)} %get-tuple-element.104), channel_id=1, source_target_pairs={{2,6},{3,7},{6,10},{7,11},{10,14},{11,15},{14,12},{15,13},{12,8},{... | collective-permute-start | bytes 786440 | tf_op jit(solution)/shard_map/ppermute | solution.py:311
  84.5 0.7 collective-permute-start.20
  85.2 2.2 %collective-permute-done.23 = bf16[64,2048]{1,0:T(8,128)(2,1)S(1)} collective-permute-done((bf16[64,2048]{1,0:T(8,128)(2,1)S(1)}, bf16[64,2048]{1,0:T(8,128)(2,1)S(1)}, u32[]{:S(2)}, u32[]{:S(2)}) %collective-permute-start.23) | collective-permute-done | bytes 262176 | tf_op jit(solution)/shard_map/ppermute | solution.py:311
  87.4 0.1 add_convert_fusion.5
  87.5 1.6 %collective-permute-start.24 = (bf16[64,2048]{1,0:T(8,128)(2,1)S(1)}, bf16[64,2048]{1,0:T(8,128)(2,1)S(1)}, u32[]{:S(2)}, u32[]{:S(2)}) collective-permute-start(bf16[64,2048]{1,0:T(8,128)(2,1)S(1)} %add_convert_fusion.5), channel_id=1, source_target_pairs={{6,2},{7,3},{10,6},{11,7},{14,10},{15,11},{12,14},{13,15},{8,12},{... | collective-permute-start | bytes 786440 | tf_op jit(solution)/shard_map/ppermute | solution.py:311
  89.2 0.5 collective-permute-start.22
  89.7 6.8 %collective-permute-done.24 = bf16[64,2048]{1,0:T(8,128)(2,1)S(1)} collective-permute-done((bf16[64,2048]{1,0:T(8,128)(2,1)S(1)}, bf16[64,2048]{1,0:T(8,128)(2,1)S(1)}, u32[]{:S(2)}, u32[]{:S(2)}) %collective-permute-start.24) | collective-permute-done | bytes 262176 | tf_op jit(solution)/shard_map/ppermute | solution.py:311
  96.6 0.9 collective-permute-start.30
  97.5 1.2 %collective-permute-start.28 = (bf16[64,2048]{1,0:T(8,128)(2,1)S(1)}, bf16[64,2048]{1,0:T(8,128)(2,1)S(1)}, u32[]{:S(2)}, u32[]{:S(2)}) collective-permute-start(bf16[64,2048]{1,0:T(8,128)(2,1)S(1)} %add_convert_fusion.6), channel_id=1, source_target_pairs={{2,6},{3,7},{6,10},{7,11},{10,14},{11,15},{14,12},{15,13},{12,8},{... | collective-permute-start | bytes 786440 | tf_op jit(solution)/shard_map/ppermute | solution.py:311
  98.8 1.6 %collective-permute-start.27 = (bf16[64,2048]{1,0:T(8,128)(2,1)S(1)}, bf16[64,2048]{1,0:T(8,128)(2,1)S(1)}, u32[]{:S(2)}, u32[]{:S(2)}) collective-permute-start(bf16[64,2048]{1,0:T(8,128)(2,1)S(1)} %add_convert_fusion.2), channel_id=1, source_target_pairs={{2,6},{3,7},{6,10},{7,11},{10,14},{11,15},{14,12},{15,13},{12,8},{... | collective-permute-start | bytes 786440 | tf_op jit(solution)/shard_map/ppermute | solution.py:311
  100.5 0.5 collective-permute-start.25
  101.0 4.9 %collective-permute-done.30 = bf16[64,2048]{1,0:T(8,128)(2,1)S(1)} collective-permute-done((bf16[64,2048]{1,0:T(8,128)(2,1)S(1)}, bf16[64,2048]{1,0:T(8,128)(2,1)S(1)}, u32[]{:S(2)}, u32[]{:S(2)}) %collective-permute-start.30) | collective-permute-done | bytes 262176 | tf_op jit(solution)/shard_map/ppermute | solution.py:311
  105.9 0.9 collective-permute-start.31
  106.9 1.2 %collective-permute-start.29 = (bf16[64,2048]{1,0:T(8,128)(2,1)S(1)}, bf16[64,2048]{1,0:T(8,128)(2,1)S(1)}, u32[]{:S(2)}, u32[]{:S(2)}) collective-permute-start(bf16[64,2048]{1,0:T(8,128)(2,1)S(1)} %add_convert_fusion.1), channel_id=1, source_target_pairs={{2,6},{3,7},{6,10},{7,11},{10,14},{11,15},{14,12},{15,13},{12,8},{... | collective-permute-start | bytes 786440 | tf_op jit(solution)/shard_map/ppermute | solution.py:311
  108.1 2.0 %collective-permute-done.27 = bf16[64,2048]{1,0:T(8,128)(2,1)S(1)} collective-permute-done((bf16[64,2048]{1,0:T(8,128)(2,1)S(1)}, bf16[64,2048]{1,0:T(8,128)(2,1)S(1)}, u32[]{:S(2)}, u32[]{:S(2)}) %collective-permute-start.27) | collective-permute-done | bytes 262176 | tf_op jit(solution)/shard_map/ppermute | solution.py:311
  110.1 0.1 add_add_fusion.near1_ref
  110.2 0.1 add_add_fusion.1.near0_ref
  110.3 2.0 %collective-permute-done.31.total1_ref = bf16[64,2048]{1,0:T(8,128)(2,1)S(1)} collective-permute-done((bf16[64,2048]{1,0:T(8,128)(2,1)S(1)}, bf16[64,2048]{1,0:T(8,128)(2,1)S(1)}, u32[]{:S(2)}, u32[]{:S(2)}) %collective-permute-start.31) | collective-permute-done | bytes 262176 | tf_op jit(solution)/shard_map/ppermute | solution.py:311
  112.3 1.0 collective-permute-done.29.total0_ref
  113.3 0.9 last_rows.1
  (40 shorter events, 0.6 us)
Async XLA Ops:
  17.0 17.2 %collective-permute-start.2 = (bf16[2048,1536]{1,0:T(8,128)(2,1)}, bf16[2048,1536]{1,0:T(8,128)(2,1)S(1)}, u32[]{:S(2)}, u32[]{:S(2)}) collective-permute-start(bf16[2048,1536]{1,0:T(8,128)(2,1)} %bitcast.12), channel_id=1, source_target_pairs={{0,1},{1,0},{2,3},{3,2},{4,5},{5,4},{6,7},{7,6},{8,9},{9,8},{10,11... | collective-permute-start | bytes 18874376 | tf_op jit(solution)/shard_map/ppermute | solution.py:311
  17.5 16.7 %collective-permute-start.3 = (bf16[768,2048]{1,0:T(8,128)(2,1)}, bf16[768,2048]{1,0:T(8,128)(2,1)S(1)}, u32[]{:S(2)}, u32[]{:S(2)}) collective-permute-start(bf16[768,2048]{1,0:T(8,128)(2,1)} %bitcast.22), channel_id=1, source_target_pairs={{0,1},{1,0},{2,3},{3,2},{4,5},{5,4},{6,7},{7,6},{8,9},{9,8},{10,11... | collective-permute-start | bytes 9437192 | tf_op jit(solution)/shard_map/ppermute | solution.py:311
  17.6 11.8 %collective-permute-start = (bf16[64,2048]{1,0:T(8,128)(2,1)}, bf16[64,2048]{1,0:T(8,128)(2,1)S(1)}, u32[]{:S(2)}, u32[]{:S(2)}) collective-permute-start(bf16[64,2048]{1,0:T(8,128)(2,1)} %get-tuple-element.60), channel_id=1, source_target_pairs={{0,16},{1,17},{2,18},{3,19},{4,20},{5,21},{6,22},{7,23},{8,24},{9,... | collective-permute-start | bytes 786440 | tf_op jit(solution)/shard_map/ppermute | solution.py:20
  22.5 11.7 %collective-permute-start.1 = (bf16[64,2048]{1,0:T(8,128)(2,1)}, bf16[64,2048]{1,0:T(8,128)(2,1)S(1)}, u32[]{:S(2)}, u32[]{:S(2)}) collective-permute-start(bf16[64,2048]{1,0:T(8,128)(2,1)} %get-tuple-element.64), channel_id=1, source_target_pairs={{0,16},{1,17},{2,18},{3,19},{4,20},{5,21},{6,22},{7,23},{8,24},{9,... | collective-permute-start | bytes 786440 | tf_op jit(solution)/shard_map/ppermute | solution.py:20
  23.8 1.0 copy-start.2
  24.8 0.7 copy-start.3
  25.5 0.7 copy-start.4
  26.2 0.7 copy-start.5
  29.5 6.8 %collective-permute-start.4 = (bf16[1040,128]{1,0:T(8,128)(2,1)S(1)}, bf16[1040,128]{1,0:T(8,128)(2,1)S(1)}, u32[]{:S(2)}, u32[]{:S(2)}) collective-permute-start(bf16[1040,128]{1,0:T(8,128)(2,1)S(1)} %get-tuple-element.69.refs_0_), channel_id=1, source_target_pairs={{2,6},{3,7},{6,10},{7,11},{10,14},{11,15},{14,12},{15,13},{12,8},{... | collective-permute-start | bytes 798728 | tf_op jit(solution)/shard_map/ppermute | solution.py:311
  31.0 6.4 %collective-permute-start.5 = (bf16[1040,128]{1,0:T(8,128)(2,1)S(1)}, bf16[1040,128]{1,0:T(8,128)(2,1)S(1)}, u32[]{:S(2)}, u32[]{:S(2)}) collective-permute-start(bf16[1040,128]{1,0:T(8,128)(2,1)S(1)} %get-tuple-element.69.refs_0_), channel_id=1, source_target_pairs={{6,2},{7,3},{10,6},{11,7},{14,10},{15,11},{12,14},{13,15},{8,12},{... | collective-permute-start | bytes 798728 | tf_op jit(solution)/shard_map/ppermute | solution.py:311
  34.3 12.7 %collective-permute-start.8 = (bf16[1040,128]{1,0:T(8,128)(2,1)S(1)}, bf16[1040,128]{1,0:T(8,128)(2,1)S(1)}, u32[]{:S(2)}, u32[]{:S(2)}) collective-permute-start(bf16[1040,128]{1,0:T(8,128)(2,1)S(1)} %get-tuple-element.73.refs_1_), channel_id=1, source_target_pairs={{2,6},{3,7},{6,10},{7,11},{10,14},{11,15},{14,12},{15,13},{12,8},{... | collective-permute-start | bytes 798728 | tf_op jit(solution)/shard_map/ppermute | solution.py:311
  35.8 11.2 %collective-permute-start.9 = (bf16[1040,128]{1,0:T(8,128)(2,1)S(1)}, bf16[1040,128]{1,0:T(8,128)(2,1)S(1)}, u32[]{:S(2)}, u32[]{:S(2)}) collective-permute-start(bf16[1040,128]{1,0:T(8,128)(2,1)S(1)} %get-tuple-element.73.refs_1_), channel_id=1, source_target_pairs={{6,2},{7,3},{10,6},{11,7},{14,10},{15,11},{12,14},{13,15},{8,12},{... | collective-permute-start | bytes 798728 | tf_op jit(solution)/shard_map/ppermute | solution.py:311
  37.5 14.4 %collective-permute-start.6 = (bf16[1040,128]{1,0:T(8,128)(2,1)S(1)}, bf16[1040,128]{1,0:T(8,128)(2,1)S(1)}, u32[]{:S(2)}, u32[]{:S(2)}) collective-permute-start(bf16[1040,128]{1,0:T(8,128)(2,1)S(1)} %collective-permute-done.4.refs_0_), channel_id=1, source_target_pairs={{2,6},{3,7},{6,10},{7,11},{10,14},{11,15},{14,12},{15,13},{12,8},{... | collective-permute-start | bytes 798728 | tf_op jit(solution)/shard_map/ppermute | solution.py:311
  39.1 12.8 %collective-permute-start.7 = (bf16[1040,128]{1,0:T(8,128)(2,1)S(1)}, bf16[1040,128]{1,0:T(8,128)(2,1)S(1)}, u32[]{:S(2)}, u32[]{:S(2)}) collective-permute-start(bf16[1040,128]{1,0:T(8,128)(2,1)S(1)} %collective-permute-done.5.refs_1_), channel_id=1, source_target_pairs={{6,2},{7,3},{10,6},{11,7},{14,10},{15,11},{12,14},{13,15},{8,12},{... | collective-permute-start | bytes 798728 | tf_op jit(solution)/shard_map/ppermute | solution.py:311
  39.5 2.8 %copy-start = (bf16[1,1,2048,1536]{3,2,1,0:T(8,128)(2,1)S(1)}, bf16[1,1,2048,1536]{3,2,1,0:T(8,128)(2,1)}, u32[]{:S(2)}) copy-start(bf16[1,1,2048,1536]{3,2,1,0:T(8,128)(2,1)} %param.12) | copy-start | bytes 18874372
  42.3 1.9 %copy-start.1 = (bf16[1,1,768,2048]{3,2,1,0:T(8,128)(2,1)S(1)}, bf16[1,1,768,2048]{3,2,1,0:T(8,128)(2,1)}, u32[]{:S(2)}) copy-start(bf16[1,1,768,2048]{3,2,1,0:T(8,128)(2,1)} %param.13) | copy-start | bytes 9437188
  47.0 9.8 %collective-permute-start.10 = (bf16[1040,128]{1,0:T(8,128)(2,1)S(1)}, bf16[1040,128]{1,0:T(8,128)(2,1)S(1)}, u32[]{:S(2)}, u32[]{:S(2)}) collective-permute-start(bf16[1040,128]{1,0:T(8,128)(2,1)S(1)} %collective-permute-done.8.refs_0_), channel_id=1, source_target_pairs={{2,6},{3,7},{6,10},{7,11},{10,14},{11,15},{14,12},{15,13},{12,8},{... | collective-permute-start | bytes 798728 | tf_op jit(solution)/shard_map/ppermute | solution.py:311
  48.6 9.3 %collective-permute-start.11 = (bf16[1040,128]{1,0:T(8,128)(2,1)S(1)}, bf16[1040,128]{1,0:T(8,128)(2,1)S(1)}, u32[]{:S(2)}, u32[]{:S(2)}) collective-permute-start(bf16[1040,128]{1,0:T(8,128)(2,1)S(1)} %collective-permute-done.9.refs_1_), channel_id=1, source_target_pairs={{6,2},{7,3},{10,6},{11,7},{14,10},{15,11},{12,14},{13,15},{8,12},{... | collective-permute-start | bytes 798728 | tf_op jit(solution)/shard_map/ppermute | solution.py:311
  51.9 10.8 %collective-permute-start.12 = (bf16[1040,128]{1,0:T(8,128)(2,1)S(1)}, bf16[1040,128]{1,0:T(8,128)(2,1)S(1)}, u32[]{:S(2)}, u32[]{:S(2)}) collective-permute-start(bf16[1040,128]{1,0:T(8,128)(2,1)S(1)} %collective-permute-done.6.refs_0_), channel_id=1, source_target_pairs={{2,6},{3,7},{6,10},{7,11},{10,14},{11,15},{14,12},{15,13},{12,8},{... | collective-permute-start | bytes 798728 | tf_op jit(solution)/shard_map/ppermute | solution.py:311
  53.5 10.1 %collective-permute-start.13 = (bf16[1040,128]{1,0:T(8,128)(2,1)S(1)}, bf16[1040,128]{1,0:T(8,128)(2,1)S(1)}, u32[]{:S(2)}, u32[]{:S(2)}) collective-permute-start(bf16[1040,128]{1,0:T(8,128)(2,1)S(1)} %collective-permute-done.7.refs_1_), channel_id=1, source_target_pairs={{6,2},{7,3},{10,6},{11,7},{14,10},{15,11},{12,14},{13,15},{8,12},{... | collective-permute-start | bytes 798728 | tf_op jit(solution)/shard_map/ppermute | solution.py:311
  57.9 10.1 %collective-permute-start.14 = (bf16[1040,128]{1,0:T(8,128)(2,1)S(1)}, bf16[1040,128]{1,0:T(8,128)(2,1)S(1)}, u32[]{:S(2)}, u32[]{:S(2)}) collective-permute-start(bf16[1040,128]{1,0:T(8,128)(2,1)S(1)} %collective-permute-done.10.refs_0_), channel_id=1, source_target_pairs={{2,6},{3,7},{6,10},{7,11},{10,14},{11,15},{14,12},{15,13},{12,8},{... | collective-permute-start | bytes 798728 | tf_op jit(solution)/shard_map/ppermute | solution.py:311
  59.5 8.5 %collective-permute-start.15 = (bf16[1040,128]{1,0:T(8,128)(2,1)S(1)}, bf16[1040,128]{1,0:T(8,128)(2,1)S(1)}, u32[]{:S(2)}, u32[]{:S(2)}) collective-permute-start(bf16[1040,128]{1,0:T(8,128)(2,1)S(1)} %collective-permute-done.11.refs_1_), channel_id=1, source_target_pairs={{6,2},{7,3},{10,6},{11,7},{14,10},{15,11},{12,14},{13,15},{8,12},{... | collective-permute-start | bytes 798728 | tf_op jit(solution)/shard_map/ppermute | solution.py:311
  63.6 9.9 %collective-permute-start.18 = (bf16[1040,128]{1,0:T(8,128)(2,1)S(1)}, bf16[1040,128]{1,0:T(8,128)(2,1)S(1)}, u32[]{:S(2)}, u32[]{:S(2)}) collective-permute-start(bf16[1040,128]{1,0:T(8,128)(2,1)S(1)} %collective-permute-done.12.refs_0_), channel_id=1, source_target_pairs={{2,6},{3,7},{6,10},{7,11},{10,14},{11,15},{14,12},{15,13},{12,8},{... | collective-permute-start | bytes 798728 | tf_op jit(solution)/shard_map/ppermute | solution.py:311
  68.0 7.3 %collective-permute-start.19 = (bf16[1040,128]{1,0:T(8,128)(2,1)S(1)}, bf16[1040,128]{1,0:T(8,128)(2,1)S(1)}, u32[]{:S(2)}, u32[]{:S(2)}) collective-permute-start(bf16[1040,128]{1,0:T(8,128)(2,1)S(1)} %collective-permute-done.15.refs_1_), channel_id=1, source_target_pairs={{6,2},{7,3},{10,6},{11,7},{14,10},{15,11},{12,14},{13,15},{8,12},{... | collective-permute-start | bytes 798728 | tf_op jit(solution)/shard_map/ppermute | solution.py:311
  71.3 9.0 %collective-permute-start.16 = (bf16[64,2048]{1,0:T(8,128)(2,1)S(1)}, bf16[64,2048]{1,0:T(8,128)(2,1)S(1)}, u32[]{:S(2)}, u32[]{:S(2)}) collective-permute-start(bf16[64,2048]{1,0:T(8,128)(2,1)S(1)} %convert_element_type.73), channel_id=1, source_target_pairs={{6,2},{7,3},{10,6},{11,7},{14,10},{15,11},{12,14},{13,15},{8,12},{... | collective-permute-start | bytes 786440 | tf_op jit(solution)/shard_map/ppermute | solution.py:311
  72.8 7.5 %collective-permute-start.17 = (bf16[64,2048]{1,0:T(8,128)(2,1)S(1)}, bf16[64,2048]{1,0:T(8,128)(2,1)S(1)}, u32[]{:S(2)}, u32[]{:S(2)}) collective-permute-start(bf16[64,2048]{1,0:T(8,128)(2,1)S(1)} %convert_element_type.74), channel_id=1, source_target_pairs={{2,6},{3,7},{6,10},{7,11},{10,14},{11,15},{14,12},{15,13},{12,8},{... | collective-permute-start | bytes 786440 | tf_op jit(solution)/shard_map/ppermute | solution.py:311
  78.1 9.3 %collective-permute-start.23 = (bf16[64,2048]{1,0:T(8,128)(2,1)S(1)}, bf16[64,2048]{1,0:T(8,128)(2,1)S(1)}, u32[]{:S(2)}, u32[]{:S(2)}) collective-permute-start(bf16[64,2048]{1,0:T(8,128)(2,1)S(1)} %convert_element_type.80), channel_id=1, source_target_pairs={{6,2},{7,3},{10,6},{11,7},{14,10},{15,11},{12,14},{13,15},{8,12},{... | collective-permute-start | bytes 786440 | tf_op jit(solution)/shard_map/ppermute | solution.py:311
  79.8 9.3 %collective-permute-start.21 = (bf16[64,2048]{1,0:T(8,128)(2,1)S(1)}, bf16[64,2048]{1,0:T(8,128)(2,1)S(1)}, u32[]{:S(2)}, u32[]{:S(2)}) collective-permute-start(bf16[64,2048]{1,0:T(8,128)(2,1)S(1)} %convert_element_type.75), channel_id=1, source_target_pairs={{2,6},{3,7},{6,10},{7,11},{10,14},{11,15},{14,12},{15,13},{12,8},{... | collective-permute-start | bytes 786440 | tf_op jit(solution)/shard_map/ppermute | solution.py:311
  83.1 15.6 %collective-permute-start.26 = (bf16[64,2048]{1,0:T(8,128)(2,1)S(1)}, bf16[64,2048]{1,0:T(8,128)(2,1)S(1)}, u32[]{:S(2)}, u32[]{:S(2)}) collective-permute-start(bf16[64,2048]{1,0:T(8,128)(2,1)S(1)} %get-tuple-element.104), channel_id=1, source_target_pairs={{2,6},{3,7},{6,10},{7,11},{10,14},{11,15},{14,12},{15,13},{12,8},{... | collective-permute-start | bytes 786440 | tf_op jit(solution)/shard_map/ppermute | solution.py:311
  84.5 15.9 %collective-permute-start.20 = (bf16[64,2048]{1,0:T(8,128)(2,1)S(1)}, bf16[64,2048]{1,0:T(8,128)(2,1)S(1)}, u32[]{:S(2)}, u32[]{:S(2)}) collective-permute-start(bf16[64,2048]{1,0:T(8,128)(2,1)S(1)} %get-tuple-element.96), channel_id=1, source_target_pairs={{6,2},{7,3},{10,6},{11,7},{14,10},{15,11},{12,14},{13,15},{8,12},{... | collective-permute-start | bytes 786440 | tf_op jit(solution)/shard_map/ppermute | solution.py:311
  87.5 9.0 %collective-permute-start.24 = (bf16[64,2048]{1,0:T(8,128)(2,1)S(1)}, bf16[64,2048]{1,0:T(8,128)(2,1)S(1)}, u32[]{:S(2)}, u32[]{:S(2)}) collective-permute-start(bf16[64,2048]{1,0:T(8,128)(2,1)S(1)} %add_convert_fusion.5), channel_id=1, source_target_pairs={{6,2},{7,3},{10,6},{11,7},{14,10},{15,11},{12,14},{13,15},{8,12},{... | collective-permute-start | bytes 786440 | tf_op jit(solution)/shard_map/ppermute | solution.py:311
  89.2 8.3 %collective-permute-start.22 = (bf16[64,2048]{1,0:T(8,128)(2,1)S(1)}, bf16[64,2048]{1,0:T(8,128)(2,1)S(1)}, u32[]{:S(2)}, u32[]{:S(2)}) collective-permute-start(bf16[64,2048]{1,0:T(8,128)(2,1)S(1)} %add_convert_fusion.7), channel_id=1, source_target_pairs={{2,6},{3,7},{6,10},{7,11},{10,14},{11,15},{14,12},{15,13},{12,8},{... | collective-permute-start | bytes 786440 | tf_op jit(solution)/shard_map/ppermute | solution.py:311
  96.6 9.3 %collective-permute-start.30 = (bf16[64,2048]{1,0:T(8,128)(2,1)S(1)}, bf16[64,2048]{1,0:T(8,128)(2,1)S(1)}, u32[]{:S(2)}, u32[]{:S(2)}) collective-permute-start(bf16[64,2048]{1,0:T(8,128)(2,1)S(1)} %add_convert_fusion.4), channel_id=1, source_target_pairs={{6,2},{7,3},{10,6},{11,7},{14,10},{15,11},{12,14},{13,15},{8,12},{... | collective-permute-start | bytes 786440 | tf_op jit(solution)/shard_map/ppermute | solution.py:311
  97.5 9.3 %collective-permute-start.28 = (bf16[64,2048]{1,0:T(8,128)(2,1)S(1)}, bf16[64,2048]{1,0:T(8,128)(2,1)S(1)}, u32[]{:S(2)}, u32[]{:S(2)}) collective-permute-start(bf16[64,2048]{1,0:T(8,128)(2,1)S(1)} %add_convert_fusion.6), channel_id=1, source_target_pairs={{2,6},{3,7},{6,10},{7,11},{10,14},{11,15},{14,12},{15,13},{12,8},{... | collective-permute-start | bytes 786440 | tf_op jit(solution)/shard_map/ppermute | solution.py:311
  98.8 11.3 %collective-permute-start.27 = (bf16[64,2048]{1,0:T(8,128)(2,1)S(1)}, bf16[64,2048]{1,0:T(8,128)(2,1)S(1)}, u32[]{:S(2)}, u32[]{:S(2)}) collective-permute-start(bf16[64,2048]{1,0:T(8,128)(2,1)S(1)} %add_convert_fusion.2), channel_id=1, source_target_pairs={{2,6},{3,7},{6,10},{7,11},{10,14},{11,15},{14,12},{15,13},{12,8},{... | collective-permute-start | bytes 786440 | tf_op jit(solution)/shard_map/ppermute | solution.py:311
  100.5 9.8 %collective-permute-start.25 = (bf16[64,2048]{1,0:T(8,128)(2,1)S(1)}, bf16[64,2048]{1,0:T(8,128)(2,1)S(1)}, u32[]{:S(2)}, u32[]{:S(2)}) collective-permute-start(bf16[64,2048]{1,0:T(8,128)(2,1)S(1)} %add_convert_fusion.3), channel_id=1, source_target_pairs={{6,2},{7,3},{10,6},{11,7},{14,10},{15,11},{12,14},{13,15},{8,12},{... | collective-permute-start | bytes 786440 | tf_op jit(solution)/shard_map/ppermute | solution.py:311
  105.9 6.4 %collective-permute-start.31 = (bf16[64,2048]{1,0:T(8,128)(2,1)S(1)}, bf16[64,2048]{1,0:T(8,128)(2,1)S(1)}, u32[]{:S(2)}, u32[]{:S(2)}) collective-permute-start(bf16[64,2048]{1,0:T(8,128)(2,1)S(1)} %add_convert_fusion), channel_id=1, source_target_pairs={{6,2},{7,3},{10,6},{11,7},{14,10},{15,11},{12,14},{13,15},{8,12},{... | collective-permute-start | bytes 786440 | tf_op jit(solution)/shard_map/ppermute | solution.py:311
  106.9 6.4 %collective-permute-start.29 = (bf16[64,2048]{1,0:T(8,128)(2,1)S(1)}, bf16[64,2048]{1,0:T(8,128)(2,1)S(1)}, u32[]{:S(2)}, u32[]{:S(2)}) collective-permute-start(bf16[64,2048]{1,0:T(8,128)(2,1)S(1)} %add_convert_fusion.1), channel_id=1, source_target_pairs={{2,6},{3,7},{6,10},{7,11},{10,14},{11,15},{14,12},{15,13},{12,8},{... | collective-permute-start | bytes 786440 | tf_op jit(solution)/shard_map/ppermute | solution.py:311

commit v16 on v14

--- a/solution.py
+++ b/solution.py
@@ -317,8 +317,13 @@
     pass_on(0, 1, other)
     for s in range(1, hops):
         for c in range(2):
-            pass_on(s, c, last)
-            to_down[s, c], to_up[s, c] = mlp([ups[s][c], downs[s][c]])
+            if (s, c) != (hops - 1, 1):
+                pass_on(s, c, last)
+            came = [ups[s][c], downs[s][c]]
+            if s == hops - 1 and c == 0:
+                pass_on(s, 1, last)
+                came = lax.optimization_barrier((*came, ups[s][1], downs[s][1]))[:2]
+            to_down[s, c], to_up[s, c] = mlp(came)
     early_sums = mlp(packed, (), (), 1)
     to_up[hops, 0], to_down[hops, 1] = mlp([ups[hops][0], downs[hops][1]])
 

time: 98.7 us -> 102 us (1.033)
  waiting for transfers between devices: 29.7 us -> 31.3 us
    ppermute x30, waiting for transfers between devices: 25.2 us -> 26.8 us  [move(): return lax.ppermute(value, 'expert', pairs)]
  transfers between devices with their start and end apart: 32 -> 32, of which waited for: 13 -> 15; matrix products, arithmetic and copies ran while one was open for 2% -> 2% of each run, Pallas kernels for 23% -> 23%
where the time goes in v16:
time: 102 us; the launch traced here: 101 us
  starting transfers between devices  37.8 us (37%)
  waiting for transfers between devices  31.3 us (31%)
  Pallas kernels  23.6 us (23%)
  local copies, waits for them, and re-layouts  7.21 us (7%)
    ppermute x30, starting transfers between devices, move(): return lax.ppermute(value, 'expert', pairs)  31.6 us
    ppermute x30, waiting for transfers between devices, move(): return lax.ppermute(value, 'expert', pairs)  26.8 us
    pallas_call x9, Pallas kernels, expert_rows(): pl.pallas_call(functools.partial(mlp_kernel, parts=len(payloads), adds=le...  22.4 us
    ppermute x2, starting transfers between devices, from_behind(): return lax.ppermute(value, axis, pairs)  6.18 us
    unnamed x12, local copies, waits for them, and re-layouts  5.89 us
    ppermute x2, waiting for transfers between devices, from_behind(): return lax.ppermute(value, axis, pairs)  4.5 us
  transfers between devices with their start and end apart: 32, of which 15 were waited for; matrix products, arithmetic and copies ran while one was open for 2% of the time, Pallas kernels for 23%

profile of v16, /device:TPU:0, one launch (start us, length us, event | category | flops | bytes accessed | tf_op | source)
XLA Modules:
  0.0 100.8 jit_solution(10548322521697364059)
XLA Ops:
  0.0 0.5 collective-permute-start.2
  0.5 1.3 %slice_bitcast_fusion = (bf16[64,2048]{1,0:T(8,128)(2,1)S(1)}, bf16[64,2048]{1,0:T(8,128)(2,1)S(1)}) fusion(bf16[1,128,2048]{2,1,0:T(8,128)(2,1)} %param.8), kind=kLoop, calls=%fused_computation.10 | loop fusion | bytes 1048576 | tf_op jit(solution)/shard_map/squeeze | solution.py:292
  1.8 4.9 %collective-permute-start = (bf16[64,2048]{1,0:T(8,128)(2,1)S(1)}, bf16[64,2048]{1,0:T(8,128)(2,1)S(1)}, u32[]{:S(2)}, u32[]{:S(2)}) collective-permute-start(bf16[64,2048]{1,0:T(8,128)(2,1)S(1)} %get-tuple-element.110), channel_id=1, source_target_pairs={{0,16},{1,17},{2,18},{3,19},{4,20},{5,21},{6,22},{7,23},{8,24},{9,... | collective-permute-start | bytes 786440 | tf_op jit(solution)/shard_map/ppermute | solution.py:20
  6.7 1.3 %collective-permute-start.1 = (bf16[64,2048]{1,0:T(8,128)(2,1)S(1)}, bf16[64,2048]{1,0:T(8,128)(2,1)S(1)}, u32[]{:S(2)}, u32[]{:S(2)}) collective-permute-start(bf16[64,2048]{1,0:T(8,128)(2,1)S(1)} %get-tuple-element.109), channel_id=1, source_target_pairs={{0,16},{1,17},{2,18},{3,19},{4,20},{5,21},{6,22},{7,23},{8,24},{9,... | collective-permute-start | bytes 786440 | tf_op jit(solution)/shard_map/ppermute | solution.py:20
  8.1 1.0 %copy-done.2 = bf16[128,2048]{1,0:T(8,128)(2,1)S(1)} copy-done((bf16[128,2048]{1,0:T(8,128)(2,1)S(1)}, bf16[128,2048]{1,0:T(8,128)(2,1)}, u32[]{:S(2)}) %copy-start.2) | copy-done | bytes 524312
  9.1 0.7 copy-done.3
  9.8 0.7 copy-done.4
  10.5 0.7 copy-done.5
  11.2 0.2 base_rows.1
  11.4 2.0 %collective-permute-done.arrived_ref = bf16[64,2048]{1,0:T(8,128)(2,1)S(1)} collective-permute-done((bf16[64,2048]{1,0:T(8,128)(2,1)S(1)}, bf16[64,2048]{1,0:T(8,128)(2,1)S(1)}, u32[]{:S(2)}, u32[]{:S(2)}) %collective-permute-start) | collective-permute-done | bytes 262176 | tf_op jit(solution)/shard_map/ppermute | solution.py:20
  13.4 1.5 %collective-permute-start.4 = (bf16[1040,128]{1,0:T(8,128)(2,1)S(1)}, bf16[1040,128]{1,0:T(8,128)(2,1)S(1)}, u32[]{:S(2)}, u32[]{:S(2)}) collective-permute-start(bf16[1040,128]{1,0:T(8,128)(2,1)S(1)} %get-tuple-element.67.refs_0_), channel_id=1, source_target_pairs={{2,6},{3,7},{6,10},{7,11},{10,14},{11,15},{14,12},{15,13},{12,8},{... | collective-permute-start | bytes 798728 | tf_op jit(solution)/shard_map/ppermute | solution.py:285
  15.0 0.5 collective-permute-start.5
  15.5 2.5 %collective-permute-done.1.arrived_ref = bf16[64,2048]{1,0:T(8,128)(2,1)S(1)} collective-permute-done((bf16[64,2048]{1,0:T(8,128)(2,1)S(1)}, bf16[64,2048]{1,0:T(8,128)(2,1)S(1)}, u32[]{:S(2)}, u32[]{:S(2)}) %collective-permute-start.1) | collective-permute-done | bytes 262176 | tf_op jit(solution)/shard_map/ppermute | solution.py:20
  18.1 1.5 %collective-permute-start.8 = (bf16[1040,128]{1,0:T(8,128)(2,1)S(1)}, bf16[1040,128]{1,0:T(8,128)(2,1)S(1)}, u32[]{:S(2)}, u32[]{:S(2)}) collective-permute-start(bf16[1040,128]{1,0:T(8,128)(2,1)S(1)} %get-tuple-element.71.refs_1_), channel_id=1, source_target_pairs={{2,6},{3,7},{6,10},{7,11},{10,14},{11,15},{14,12},{15,13},{12,8},{... | collective-permute-start | bytes 798728 | tf_op jit(solution)/shard_map/ppermute | solution.py:285
  19.7 0.5 collective-permute-start.9
  20.2 1.3 %collective-permute-done.5.refs_1_ = bf16[1040,128]{1,0:T(8,128)(2,1)S(1)} collective-permute-done((bf16[1040,128]{1,0:T(8,128)(2,1)S(1)}, bf16[1040,128]{1,0:T(8,128)(2,1)S(1)}, u32[]{:S(2)}, u32[]{:S(2)}) %collective-permute-start.5) | collective-permute-done | bytes 266272 | tf_op jit(solution)/shard_map/ppermute | solution.py:285
  21.6 1.6 %collective-permute-start.6 = (bf16[1040,128]{1,0:T(8,128)(2,1)S(1)}, bf16[1040,128]{1,0:T(8,128)(2,1)S(1)}, u32[]{:S(2)}, u32[]{:S(2)}) collective-permute-start(bf16[1040,128]{1,0:T(8,128)(2,1)S(1)} %collective-permute-done.4.refs_0_), channel_id=1, source_target_pairs={{2,6},{3,7},{6,10},{7,11},{10,14},{11,15},{14,12},{15,13},{12,8},{... | collective-permute-start | bytes 798728 | tf_op jit(solution)/shard_map/ppermute | solution.py:285
  23.2 0.4 collective-permute-start.7
  23.6 2.8 %copy-done = bf16[1,1,2048,1536]{3,2,1,0:T(8,128)(2,1)S(1)} copy-done((bf16[1,1,2048,1536]{3,2,1,0:T(8,128)(2,1)S(1)}, bf16[1,1,2048,1536]{3,2,1,0:T(8,128)(2,1)}, u32[]{:S(2)}) %copy-start) | copy-done | bytes 6291480
  26.4 2.8 %expert_rows.9 = (f32[64,2048]{1,0:T(8,128)S(1)}, f32[64,2048]{1,0:T(8,128)S(1)}) custom-call(s32[1]{0:T(128)} %bitcast.6.expert_ref, bf16[1040,128]{1,0:T(8,128)(2,1)S(1)} %collective-permute-done.4.refs_0_, bf16[1040,128]{1,0:T(8,128)(2,1)S(1)} %collective-permute-done.5.refs_1_, bf16[2048,1536]{1,0:T(8,128)(2,1)S(1)} %bitcast.16, ...), custom_call_target="tpu_custom_call" | custom-call | flops 2415919104 | bytes 1572864 | tf_op jit(solution)/shard_map/expert_rows/pallas_call | solution.py:217
  29.2 1.6 %collective-permute-start.10 = (bf16[1040,128]{1,0:T(8,128)(2,1)S(1)}, bf16[1040,128]{1,0:T(8,128)(2,1)S(1)}, u32[]{:S(2)}, u32[]{:S(2)}) collective-permute-start(bf16[1040,128]{1,0:T(8,128)(2,1)S(1)} %collective-permute-done.8.refs_0_), channel_id=1, source_target_pairs={{2,6},{3,7},{6,10},{7,11},{10,14},{11,15},{14,12},{15,13},{12,8},{... | collective-permute-start | bytes 798728 | tf_op jit(solution)/shard_map/ppermute | solution.py:285
  30.8 0.5 collective-permute-start.11
  31.3 2.8 %expert_rows.10 = (f32[64,2048]{1,0:T(8,128)S(1)}, f32[64,2048]{1,0:T(8,128)S(1)}) custom-call(s32[1]{0:T(128)} %bitcast.6.expert_ref, bf16[1040,128]{1,0:T(8,128)(2,1)S(1)} %collective-permute-done.8.refs_0_, bf16[1040,128]{1,0:T(8,128)(2,1)S(1)} %collective-permute-done.9.refs_1_, bf16[2048,1536]{1,0:T(8,128)(2,1)S(1)} %bitcast.17, ...), custom_call_target="tpu_custom_call" | custom-call | flops 2415919104 | bytes 1572864 | tf_op jit(solution)/shard_map/expert_rows/pallas_call | solution.py:217
  34.1 0.6 collective-permute-done.7.refs_1_
  34.7 1.6 %collective-permute-start.12 = (bf16[1040,128]{1,0:T(8,128)(2,1)S(1)}, bf16[1040,128]{1,0:T(8,128)(2,1)S(1)}, u32[]{:S(2)}, u32[]{:S(2)}) collective-permute-start(bf16[1040,128]{1,0:T(8,128)(2,1)S(1)} %collective-permute-done.6.refs_0_), channel_id=1, source_target_pairs={{2,6},{3,7},{6,10},{7,11},{10,14},{11,15},{14,12},{15,13},{12,8},{... | collective-permute-start | bytes 798728 | tf_op jit(solution)/shard_map/ppermute | solution.py:285
  36.3 0.4 collective-permute-start.13
  36.8 2.8 %expert_rows.11 = (f32[64,2048]{1,0:T(8,128)S(1)}, f32[64,2048]{1,0:T(8,128)S(1)}) custom-call(s32[1]{0:T(128)} %bitcast.6.expert_ref, bf16[1040,128]{1,0:T(8,128)(2,1)S(1)} %collective-permute-done.6.refs_0_, bf16[1040,128]{1,0:T(8,128)(2,1)S(1)} %collective-permute-done.7.refs_1_, bf16[2048,1536]{1,0:T(8,128)(2,1)S(1)} %bitcast.18, ...), custom_call_target="tpu_custom_call" | custom-call | flops 2415919104 | bytes 1572864 | tf_op jit(solution)/shard_map/expert_rows/pallas_call | solution.py:217
  39.6 0.9 collective-permute-done.11.refs_1_
  40.4 1.6 %collective-permute-start.14 = (bf16[1040,128]{1,0:T(8,128)(2,1)S(1)}, bf16[1040,128]{1,0:T(8,128)(2,1)S(1)}, u32[]{:S(2)}, u32[]{:S(2)}) collective-permute-start(bf16[1040,128]{1,0:T(8,128)(2,1)S(1)} %collective-permute-done.10.refs_0_), channel_id=1, source_target_pairs={{2,6},{3,7},{6,10},{7,11},{10,14},{11,15},{14,12},{15,13},{12,8},{... | collective-permute-start | bytes 798728 | tf_op jit(solution)/shard_map/ppermute | solution.py:285
  42.0 0.5 collective-permute-start.15
  42.5 2.8 %expert_rows.12 = (f32[64,2048]{1,0:T(8,128)S(1)}, f32[64,2048]{1,0:T(8,128)S(1)}) custom-call(s32[1]{0:T(128)} %bitcast.6.expert_ref, bf16[1040,128]{1,0:T(8,128)(2,1)S(1)} %collective-permute-done.10.refs_0_, bf16[1040,128]{1,0:T(8,128)(2,1)S(1)} %collective-permute-done.11.refs_1_, bf16[2048,1536]{1,0:T(8,128)(2,1)S(1)} %bitcast.19, ...), custom_call_target="tpu_custom_call" | custom-call | flops 2415919104 | bytes 1572864 | tf_op jit(solution)/shard_map/expert_rows/pallas_call | solution.py:217
  45.3 0.9 collective-permute-done.13.refs_1_
  46.1 1.6 %collective-permute-start.18 = (bf16[1040,128]{1,0:T(8,128)(2,1)S(1)}, bf16[1040,128]{1,0:T(8,128)(2,1)S(1)}, u32[]{:S(2)}, u32[]{:S(2)}) collective-permute-start(bf16[1040,128]{1,0:T(8,128)(2,1)S(1)} %collective-permute-done.12.refs_0_), channel_id=1, source_target_pairs={{2,6},{3,7},{6,10},{7,11},{10,14},{11,15},{14,12},{15,13},{12,8},{... | collective-permute-start | bytes 798728 | tf_op jit(solution)/shard_map/ppermute | solution.py:285
  47.7 2.6 %collective-permute-done.14.refs_0_ = bf16[1040,128]{1,0:T(8,128)(2,1)S(1)} collective-permute-done((bf16[1040,128]{1,0:T(8,128)(2,1)S(1)}, bf16[1040,128]{1,0:T(8,128)(2,1)S(1)}, u32[]{:S(2)}, u32[]{:S(2)}) %collective-permute-start.14) | collective-permute-done | bytes 266272 | tf_op jit(solution)/shard_map/ppermute | solution.py:285
  50.4 1.6 %collective-permute-start.19 = (bf16[1040,128]{1,0:T(8,128)(2,1)S(1)}, bf16[1040,128]{1,0:T(8,128)(2,1)S(1)}, u32[]{:S(2)}, u32[]{:S(2)}) collective-permute-start(bf16[1040,128]{1,0:T(8,128)(2,1)S(1)} %collective-permute-done.15.refs_1_), channel_id=1, source_target_pairs={{6,2},{7,3},{10,6},{11,7},{14,10},{15,11},{12,14},{13,15},{8,12},{... | collective-permute-start | bytes 798728 | tf_op jit(solution)/shard_map/ppermute | solution.py:285
  51.9 2.8 %expert_rows.13 = (f32[64,2048]{1,0:T(8,128)S(1)}, f32[64,2048]{1,0:T(8,128)S(1)}) custom-call(s32[1]{0:T(128)} %bitcast.6.expert_ref, bf16[1040,128]{1,0:T(8,128)(2,1)S(1)} %collective-permute-done.12.refs_0_, bf16[1040,128]{1,0:T(8,128)(2,1)S(1)} %collective-permute-done.13.refs_1_, bf16[2048,1536]{1,0:T(8,128)(2,1)S(1)} %bitcast.20, ...), custom_call_target="tpu_custom_call" | custom-call | flops 2415919104 | bytes 1572864 | tf_op jit(solution)/shard_map/expert_rows/pallas_call | solution.py:217
  54.7 2.8 %expert_rows.14 = (f32[64,2048]{1,0:T(8,128)S(1)}, f32[64,2048]{1,0:T(8,128)S(1)}) custom-call(s32[1]{0:T(128)} %bitcast.6.expert_ref, bf16[1040,128]{1,0:T(8,128)(2,1)S(1)} %collective-permute-done.14.refs_0_, bf16[1040,128]{1,0:T(8,128)(2,1)S(1)} %collective-permute-done.15.refs_1_, bf16[2048,1536]{1,0:T(8,128)(2,1)S(1)} %bitcast.21, ...), custom_call_target="tpu_custom_call" | custom-call | flops 2415919104 | bytes 1572864 | tf_op jit(solution)/shard_map/expert_rows/pallas_call | solution.py:217
  57.5 1.6 %collective-permute-start.16 = (bf16[64,2048]{1,0:T(8,128)(2,1)S(1)}, bf16[64,2048]{1,0:T(8,128)(2,1)S(1)}, u32[]{:S(2)}, u32[]{:S(2)}) collective-permute-start(bf16[64,2048]{1,0:T(8,128)(2,1)S(1)} %convert_element_type.73), channel_id=1, source_target_pairs={{6,2},{7,3},{10,6},{11,7},{14,10},{15,11},{12,14},{13,15},{8,12},{... | collective-permute-start | bytes 786440 | tf_op jit(solution)/shard_map/ppermute | solution.py:285
  59.2 0.5 collective-permute-start.17
  59.7 2.8 %expert_rows.16 = (f32[64,2048]{1,0:T(8,128)S(1)}, f32[64,2048]{1,0:T(8,128)S(1)}) custom-call(s32[1]{0:T(128)} %bitcast.6.expert_ref, bf16[1040,128]{1,0:T(8,128)(2,1)S(1)} %collective-permute-done.18.refs_0_, bf16[1040,128]{1,0:T(8,128)(2,1)S(1)} %collective-permute-done.19.refs_1_, bf16[2048,1536]{1,0:T(8,128)(2,1)S(1)} %bitcast.23, ...), custom_call_target="tpu_custom_call" | custom-call | flops 2415919104 | bytes 1572864 | tf_op jit(solution)/shard_map/expert_rows/pallas_call | solution.py:217
  62.5 1.6 %collective-permute-start.23 = (bf16[64,2048]{1,0:T(8,128)(2,1)S(1)}, bf16[64,2048]{1,0:T(8,128)(2,1)S(1)}, u32[]{:S(2)}, u32[]{:S(2)}) collective-permute-start(bf16[64,2048]{1,0:T(8,128)(2,1)S(1)} %convert_element_type.80), channel_id=1, source_target_pairs={{6,2},{7,3},{10,6},{11,7},{14,10},{15,11},{12,14},{13,15},{8,12},{... | collective-permute-start | bytes 786440 | tf_op jit(solution)/shard_map/ppermute | solution.py:285
  64.2 0.5 collective-permute-start.21
  64.7 1.0 %collective-permute-done.17.refs_9_ = bf16[64,2048]{1,0:T(8,128)(2,1)S(1)} collective-permute-done((bf16[64,2048]{1,0:T(8,128)(2,1)S(1)}, bf16[64,2048]{1,0:T(8,128)(2,1)S(1)}, u32[]{:S(2)}, u32[]{:S(2)}) %collective-permute-start.17) | collective-permute-done | bytes 262176 | tf_op jit(solution)/shard_map/ppermute | solution.py:285
  65.7 2.9 %expert_rows.17 = (f32[64,2048]{1,0:T(8,128)S(1)}, f32[64,2048]{1,0:T(8,128)S(1)}, bf16[64,2048]{1,0:T(8,128)(2,1)S(1)}, bf16[64,2048]{1,0:T(8,128)(2,1)S(1)}) custom-call(s32[1]{0:T(128)} %bitcast.6.expert_ref, bf16[1040,128]{1,0:T(8,128)(2,1)S(1)} %get-tuple-element.67.refs_0_, bf16[1040,128]{1,0:T(8,128)(2,1)S(1)} %get-tuple-element.71.refs_1_, ...), custom_call_target="tpu_custom_call" | custom-call | flops 2415919104 | bytes 1572864 | tf_op jit(solution)/shard_map/expert_rows/pallas_call | solution.py:217
  68.6 0.5 collective-permute-start.26
  69.1 1.6 %collective-permute-start.20 = (bf16[64,2048]{1,0:T(8,128)(2,1)S(1)}, bf16[64,2048]{1,0:T(8,128)(2,1)S(1)}, u32[]{:S(2)}, u32[]{:S(2)}) collective-permute-start(bf16[64,2048]{1,0:T(8,128)(2,1)S(1)} %get-tuple-element.96), channel_id=1, source_target_pairs={{6,2},{7,3},{10,6},{11,7},{14,10},{15,11},{12,14},{13,15},{8,12},{... | collective-permute-start | bytes 786440 | tf_op jit(solution)/shard_map/ppermute | solution.py:285
  70.7 1.1 %collective-permute-done.23 = bf16[64,2048]{1,0:T(8,128)(2,1)S(1)} collective-permute-done((bf16[64,2048]{1,0:T(8,128)(2,1)S(1)}, bf16[64,2048]{1,0:T(8,128)(2,1)S(1)}, u32[]{:S(2)}, u32[]{:S(2)}) %collective-permute-start.23) | collective-permute-done | bytes 262176 | tf_op jit(solution)/shard_map/ppermute | solution.py:285
  71.9 1.6 %collective-permute-start.24 = (bf16[64,2048]{1,0:T(8,128)(2,1)S(1)}, bf16[64,2048]{1,0:T(8,128)(2,1)S(1)}, u32[]{:S(2)}, u32[]{:S(2)}) collective-permute-start(bf16[64,2048]{1,0:T(8,128)(2,1)S(1)} %add_convert_fusion.5), channel_id=1, source_target_pairs={{6,2},{7,3},{10,6},{11,7},{14,10},{15,11},{12,14},{13,15},{8,12},{... | collective-permute-start | bytes 786440 | tf_op jit(solution)/shard_map/ppermute | solution.py:285
  73.6 0.5 collective-permute-start.22
  74.1 6.9 %collective-permute-done.24 = bf16[64,2048]{1,0:T(8,128)(2,1)S(1)} collective-permute-done((bf16[64,2048]{1,0:T(8,128)(2,1)S(1)}, bf16[64,2048]{1,0:T(8,128)(2,1)S(1)}, u32[]{:S(2)}, u32[]{:S(2)}) %collective-permute-start.24) | collective-permute-done | bytes 262176 | tf_op jit(solution)/shard_map/ppermute | solution.py:285
  81.0 1.8 %collective-permute-start.30 = (bf16[64,2048]{1,0:T(8,128)(2,1)S(1)}, bf16[64,2048]{1,0:T(8,128)(2,1)S(1)}, u32[]{:S(2)}, u32[]{:S(2)}) collective-permute-start(bf16[64,2048]{1,0:T(8,128)(2,1)S(1)} %add_convert_fusion.4), channel_id=1, source_target_pairs={{6,2},{7,3},{10,6},{11,7},{14,10},{15,11},{12,14},{13,15},{8,12},{... | collective-permute-start | bytes 786440 | tf_op jit(solution)/shard_map/ppermute | solution.py:285
  82.8 0.3 collective-permute-start.28
  83.3 1.5 %collective-permute-start.27 = (bf16[64,2048]{1,0:T(8,128)(2,1)S(1)}, bf16[64,2048]{1,0:T(8,128)(2,1)S(1)}, u32[]{:S(2)}, u32[]{:S(2)}) collective-permute-start(bf16[64,2048]{1,0:T(8,128)(2,1)S(1)} %add_convert_fusion.2), channel_id=1, source_target_pairs={{2,6},{3,7},{6,10},{7,11},{10,14},{11,15},{14,12},{15,13},{12,8},{... | collective-permute-start | bytes 786440 | tf_op jit(solution)/shard_map/ppermute | solution.py:285
  84.9 0.6 collective-permute-start.25
  85.5 4.0 %collective-permute-done.30 = bf16[64,2048]{1,0:T(8,128)(2,1)S(1)} collective-permute-done((bf16[64,2048]{1,0:T(8,128)(2,1)S(1)}, bf16[64,2048]{1,0:T(8,128)(2,1)S(1)}, u32[]{:S(2)}, u32[]{:S(2)}) %collective-permute-start.30) | collective-permute-done | bytes 262176 | tf_op jit(solution)/shard_map/ppermute | solution.py:285
  89.5 2.5 %collective-permute-start.31 = (bf16[64,2048]{1,0:T(8,128)(2,1)S(1)}, bf16[64,2048]{1,0:T(8,128)(2,1)S(1)}, u32[]{:S(2)}, u32[]{:S(2)}) collective-permute-start(bf16[64,2048]{1,0:T(8,128)(2,1)S(1)} %add_convert_fusion), channel_id=1, source_target_pairs={{6,2},{7,3},{10,6},{11,7},{14,10},{15,11},{12,14},{13,15},{8,12},{... | collective-permute-start | bytes 786440 | tf_op jit(solution)/shard_map/ppermute | solution.py:285
  92.0 0.1 collective-permute-done.28
  92.2 0.3 collective-permute-start.29
  92.5 4.5 %collective-permute-done.27 = bf16[64,2048]{1,0:T(8,128)(2,1)S(1)} collective-permute-done((bf16[64,2048]{1,0:T(8,128)(2,1)S(1)}, bf16[64,2048]{1,0:T(8,128)(2,1)S(1)}, u32[]{:S(2)}, u32[]{:S(2)}) %collective-permute-start.27) | collective-permute-done | bytes 262176 | tf_op jit(solution)/shard_map/ppermute | solution.py:285
  97.1 0.1 add_add_fusion.near1_ref
  97.2 0.1 add_add_fusion.1.near0_ref
  97.3 1.4 %collective-permute-done.31.total1_ref = bf16[64,2048]{1,0:T(8,128)(2,1)S(1)} collective-permute-done((bf16[64,2048]{1,0:T(8,128)(2,1)S(1)}, bf16[64,2048]{1,0:T(8,128)(2,1)S(1)}, u32[]{:S(2)}, u32[]{:S(2)}) %collective-permute-start.31) | collective-permute-done | bytes 262176 | tf_op jit(solution)/shard_map/ppermute | solution.py:285
  98.7 1.2 %collective-permute-done.29.total0_ref = bf16[64,2048]{1,0:T(8,128)(2,1)S(1)} collective-permute-done((bf16[64,2048]{1,0:T(8,128)(2,1)S(1)}, bf16[64,2048]{1,0:T(8,128)(2,1)S(1)}, u32[]{:S(2)}, u32[]{:S(2)}) %collective-permute-start.29) | collective-permute-done | bytes 262176 | tf_op jit(solution)/shard_map/ppermute | solution.py:285
  99.9 0.9 last_rows.1
  (40 shorter events, 0.7 us)
Async XLA Ops:
  0.0 23.6 %copy-start.1 = (bf16[1,1,768,2048]{3,2,1,0:T(8,128)(2,1)S(1)}, bf16[1,1,768,2048]{3,2,1,0:T(8,128)(2,1)}, u32[]{:S(2)}) copy-start(bf16[1,1,768,2048]{3,2,1,0:T(8,128)(2,1)} %param.13) | copy-start | bytes 9437188
  0.0 18.1 %collective-permute-start.2 = (bf16[2048,1536]{1,0:T(8,128)(2,1)}, bf16[2048,1536]{1,0:T(8,128)(2,1)S(1)}, u32[]{:S(2)}, u32[]{:S(2)}) collective-permute-start(bf16[2048,1536]{1,0:T(8,128)(2,1)} %bitcast.15), channel_id=1, source_target_pairs={{0,1},{1,0},{2,3},{3,2},{4,5},{5,4},{6,7},{7,6},{8,9},{9,8},{10,11... | collective-permute-start | bytes 18874376 | tf_op jit(solution)/shard_map/ppermute | solution.py:285
  0.5 17.7 %collective-permute-start.3 = (bf16[768,2048]{1,0:T(8,128)(2,1)}, bf16[768,2048]{1,0:T(8,128)(2,1)S(1)}, u32[]{:S(2)}, u32[]{:S(2)}) collective-permute-start(bf16[768,2048]{1,0:T(8,128)(2,1)} %bitcast.25), channel_id=1, source_target_pairs={{0,1},{1,0},{2,3},{3,2},{4,5},{5,4},{6,7},{7,6},{8,9},{9,8},{10,11... | collective-permute-start | bytes 9437192 | tf_op jit(solution)/shard_map/ppermute | solution.py:285
  1.8 11.5 %collective-permute-start = (bf16[64,2048]{1,0:T(8,128)(2,1)S(1)}, bf16[64,2048]{1,0:T(8,128)(2,1)S(1)}, u32[]{:S(2)}, u32[]{:S(2)}) collective-permute-start(bf16[64,2048]{1,0:T(8,128)(2,1)S(1)} %get-tuple-element.110), channel_id=1, source_target_pairs={{0,16},{1,17},{2,18},{3,19},{4,20},{5,21},{6,22},{7,23},{8,24},{9,... | collective-permute-start | bytes 786440 | tf_op jit(solution)/shard_map/ppermute | solution.py:20
  6.7 11.3 %collective-permute-start.1 = (bf16[64,2048]{1,0:T(8,128)(2,1)S(1)}, bf16[64,2048]{1,0:T(8,128)(2,1)S(1)}, u32[]{:S(2)}, u32[]{:S(2)}) collective-permute-start(bf16[64,2048]{1,0:T(8,128)(2,1)S(1)} %get-tuple-element.109), channel_id=1, source_target_pairs={{0,16},{1,17},{2,18},{3,19},{4,20},{5,21},{6,22},{7,23},{8,24},{9,... | collective-permute-start | bytes 786440 | tf_op jit(solution)/shard_map/ppermute | solution.py:20
  8.0 1.0 %copy-start.2 = (bf16[128,2048]{1,0:T(8,128)(2,1)S(1)}, bf16[128,2048]{1,0:T(8,128)(2,1)}, u32[]{:S(2)}) copy-start(bf16[128,2048]{1,0:T(8,128)(2,1)} %fresh_ref.1) | copy-start | bytes 1572868
  9.1 0.7 copy-start.3
  9.8 0.7 copy-start.4
  10.5 0.7 copy-start.5
  13.4 6.8 %collective-permute-start.4 = (bf16[1040,128]{1,0:T(8,128)(2,1)S(1)}, bf16[1040,128]{1,0:T(8,128)(2,1)S(1)}, u32[]{:S(2)}, u32[]{:S(2)}) collective-permute-start(bf16[1040,128]{1,0:T(8,128)(2,1)S(1)} %get-tuple-element.67.refs_0_), channel_id=1, source_target_pairs={{2,6},{3,7},{6,10},{7,11},{10,14},{11,15},{14,12},{15,13},{12,8},{... | collective-permute-start | bytes 798728 | tf_op jit(solution)/shard_map/ppermute | solution.py:285
  15.0 6.6 %collective-permute-start.5 = (bf16[1040,128]{1,0:T(8,128)(2,1)S(1)}, bf16[1040,128]{1,0:T(8,128)(2,1)S(1)}, u32[]{:S(2)}, u32[]{:S(2)}) collective-permute-start(bf16[1040,128]{1,0:T(8,128)(2,1)S(1)} %get-tuple-element.67.refs_0_), channel_id=1, source_target_pairs={{6,2},{7,3},{10,6},{11,7},{14,10},{15,11},{12,14},{13,15},{8,12},{... | collective-permute-start | bytes 798728 | tf_op jit(solution)/shard_map/ppermute | solution.py:285
  18.1 11.0 %collective-permute-start.8 = (bf16[1040,128]{1,0:T(8,128)(2,1)S(1)}, bf16[1040,128]{1,0:T(8,128)(2,1)S(1)}, u32[]{:S(2)}, u32[]{:S(2)}) collective-permute-start(bf16[1040,128]{1,0:T(8,128)(2,1)S(1)} %get-tuple-element.71.refs_1_), channel_id=1, source_target_pairs={{2,6},{3,7},{6,10},{7,11},{10,14},{11,15},{14,12},{15,13},{12,8},{... | collective-permute-start | bytes 798728 | tf_op jit(solution)/shard_map/ppermute | solution.py:285
  19.7 9.5 %collective-permute-start.9 = (bf16[1040,128]{1,0:T(8,128)(2,1)S(1)}, bf16[1040,128]{1,0:T(8,128)(2,1)S(1)}, u32[]{:S(2)}, u32[]{:S(2)}) collective-permute-start(bf16[1040,128]{1,0:T(8,128)(2,1)S(1)} %get-tuple-element.71.refs_1_), channel_id=1, source_target_pairs={{6,2},{7,3},{10,6},{11,7},{14,10},{15,11},{12,14},{13,15},{8,12},{... | collective-permute-start | bytes 798728 | tf_op jit(solution)/shard_map/ppermute | solution.py:285
  21.6 12.5 %collective-permute-start.6 = (bf16[1040,128]{1,0:T(8,128)(2,1)S(1)}, bf16[1040,128]{1,0:T(8,128)(2,1)S(1)}, u32[]{:S(2)}, u32[]{:S(2)}) collective-permute-start(bf16[1040,128]{1,0:T(8,128)(2,1)S(1)} %collective-permute-done.4.refs_0_), channel_id=1, source_target_pairs={{2,6},{3,7},{6,10},{7,11},{10,14},{11,15},{14,12},{15,13},{12,8},{... | collective-permute-start | bytes 798728 | tf_op jit(solution)/shard_map/ppermute | solution.py:285
  23.2 11.6 %collective-permute-start.7 = (bf16[1040,128]{1,0:T(8,128)(2,1)S(1)}, bf16[1040,128]{1,0:T(8,128)(2,1)S(1)}, u32[]{:S(2)}, u32[]{:S(2)}) collective-permute-start(bf16[1040,128]{1,0:T(8,128)(2,1)S(1)} %collective-permute-done.5.refs_1_), channel_id=1, source_target_pairs={{6,2},{7,3},{10,6},{11,7},{14,10},{15,11},{12,14},{13,15},{8,12},{... | collective-permute-start | bytes 798728 | tf_op jit(solution)/shard_map/ppermute | solution.py:285
  23.6 2.8 %copy-start = (bf16[1,1,2048,1536]{3,2,1,0:T(8,128)(2,1)S(1)}, bf16[1,1,2048,1536]{3,2,1,0:T(8,128)(2,1)}, u32[]{:S(2)}) copy-start(bf16[1,1,2048,1536]{3,2,1,0:T(8,128)(2,1)} %param.12) | copy-start | bytes 18874372
  29.2 10.3 %collective-permute-start.10 = (bf16[1040,128]{1,0:T(8,128)(2,1)S(1)}, bf16[1040,128]{1,0:T(8,128)(2,1)S(1)}, u32[]{:S(2)}, u32[]{:S(2)}) collective-permute-start(bf16[1040,128]{1,0:T(8,128)(2,1)S(1)} %collective-permute-done.8.refs_0_), channel_id=1, source_target_pairs={{2,6},{3,7},{6,10},{7,11},{10,14},{11,15},{14,12},{15,13},{12,8},{... | collective-permute-start | bytes 798728 | tf_op jit(solution)/shard_map/ppermute | solution.py:285
  30.8 9.6 %collective-permute-start.11 = (bf16[1040,128]{1,0:T(8,128)(2,1)S(1)}, bf16[1040,128]{1,0:T(8,128)(2,1)S(1)}, u32[]{:S(2)}, u32[]{:S(2)}) collective-permute-start(bf16[1040,128]{1,0:T(8,128)(2,1)S(1)} %collective-permute-done.9.refs_1_), channel_id=1, source_target_pairs={{6,2},{7,3},{10,6},{11,7},{14,10},{15,11},{12,14},{13,15},{8,12},{... | collective-permute-start | bytes 798728 | tf_op jit(solution)/shard_map/ppermute | solution.py:285
  34.7 10.5 %collective-permute-start.12 = (bf16[1040,128]{1,0:T(8,128)(2,1)S(1)}, bf16[1040,128]{1,0:T(8,128)(2,1)S(1)}, u32[]{:S(2)}, u32[]{:S(2)}) collective-permute-start(bf16[1040,128]{1,0:T(8,128)(2,1)S(1)} %collective-permute-done.6.refs_0_), channel_id=1, source_target_pairs={{2,6},{3,7},{6,10},{7,11},{10,14},{11,15},{14,12},{15,13},{12,8},{... | collective-permute-start | bytes 798728 | tf_op jit(solution)/shard_map/ppermute | solution.py:285
  36.3 9.8 %collective-permute-start.13 = (bf16[1040,128]{1,0:T(8,128)(2,1)S(1)}, bf16[1040,128]{1,0:T(8,128)(2,1)S(1)}, u32[]{:S(2)}, u32[]{:S(2)}) collective-permute-start(bf16[1040,128]{1,0:T(8,128)(2,1)S(1)} %collective-permute-done.7.refs_1_), channel_id=1, source_target_pairs={{6,2},{7,3},{10,6},{11,7},{14,10},{15,11},{12,14},{13,15},{8,12},{... | collective-permute-start | bytes 798728 | tf_op jit(solution)/shard_map/ppermute | solution.py:285
  40.4 9.9 %collective-permute-start.14 = (bf16[1040,128]{1,0:T(8,128)(2,1)S(1)}, bf16[1040,128]{1,0:T(8,128)(2,1)S(1)}, u32[]{:S(2)}, u32[]{:S(2)}) collective-permute-start(bf16[1040,128]{1,0:T(8,128)(2,1)S(1)} %collective-permute-done.10.refs_0_), channel_id=1, source_target_pairs={{2,6},{3,7},{6,10},{7,11},{10,14},{11,15},{14,12},{15,13},{12,8},{... | collective-permute-start | bytes 798728 | tf_op jit(solution)/shard_map/ppermute | solution.py:285
  42.0 8.3 %collective-permute-start.15 = (bf16[1040,128]{1,0:T(8,128)(2,1)S(1)}, bf16[1040,128]{1,0:T(8,128)(2,1)S(1)}, u32[]{:S(2)}, u32[]{:S(2)}) collective-permute-start(bf16[1040,128]{1,0:T(8,128)(2,1)S(1)} %collective-permute-done.11.refs_1_), channel_id=1, source_target_pairs={{6,2},{7,3},{10,6},{11,7},{14,10},{15,11},{12,14},{13,15},{8,12},{... | collective-permute-start | bytes 798728 | tf_op jit(solution)/shard_map/ppermute | solution.py:285
  46.1 13.6 %collective-permute-start.18 = (bf16[1040,128]{1,0:T(8,128)(2,1)S(1)}, bf16[1040,128]{1,0:T(8,128)(2,1)S(1)}, u32[]{:S(2)}, u32[]{:S(2)}) collective-permute-start(bf16[1040,128]{1,0:T(8,128)(2,1)S(1)} %collective-permute-done.12.refs_0_), channel_id=1, source_target_pairs={{2,6},{3,7},{6,10},{7,11},{10,14},{11,15},{14,12},{15,13},{12,8},{... | collective-permute-start | bytes 798728 | tf_op jit(solution)/shard_map/ppermute | solution.py:285
  50.4 9.4 %collective-permute-start.19 = (bf16[1040,128]{1,0:T(8,128)(2,1)S(1)}, bf16[1040,128]{1,0:T(8,128)(2,1)S(1)}, u32[]{:S(2)}, u32[]{:S(2)}) collective-permute-start(bf16[1040,128]{1,0:T(8,128)(2,1)S(1)} %collective-permute-done.15.refs_1_), channel_id=1, source_target_pairs={{6,2},{7,3},{10,6},{11,7},{14,10},{15,11},{12,14},{13,15},{8,12},{... | collective-permute-start | bytes 798728 | tf_op jit(solution)/shard_map/ppermute | solution.py:285
  57.5 7.2 %collective-permute-start.16 = (bf16[64,2048]{1,0:T(8,128)(2,1)S(1)}, bf16[64,2048]{1,0:T(8,128)(2,1)S(1)}, u32[]{:S(2)}, u32[]{:S(2)}) collective-permute-start(bf16[64,2048]{1,0:T(8,128)(2,1)S(1)} %convert_element_type.73), channel_id=1, source_target_pairs={{6,2},{7,3},{10,6},{11,7},{14,10},{15,11},{12,14},{13,15},{8,12},{... | collective-permute-start | bytes 786440 | tf_op jit(solution)/shard_map/ppermute | solution.py:285
  59.2 6.5 %collective-permute-start.17 = (bf16[64,2048]{1,0:T(8,128)(2,1)S(1)}, bf16[64,2048]{1,0:T(8,128)(2,1)S(1)}, u32[]{:S(2)}, u32[]{:S(2)}) collective-permute-start(bf16[64,2048]{1,0:T(8,128)(2,1)S(1)} %convert_element_type.74), channel_id=1, source_target_pairs={{2,6},{3,7},{6,10},{7,11},{10,14},{11,15},{14,12},{15,13},{12,8},{... | collective-permute-start | bytes 786440 | tf_op jit(solution)/shard_map/ppermute | solution.py:285
  62.5 9.3 %collective-permute-start.23 = (bf16[64,2048]{1,0:T(8,128)(2,1)S(1)}, bf16[64,2048]{1,0:T(8,128)(2,1)S(1)}, u32[]{:S(2)}, u32[]{:S(2)}) collective-permute-start(bf16[64,2048]{1,0:T(8,128)(2,1)S(1)} %convert_element_type.80), channel_id=1, source_target_pairs={{6,2},{7,3},{10,6},{11,7},{14,10},{15,11},{12,14},{13,15},{8,12},{... | collective-permute-start | bytes 786440 | tf_op jit(solution)/shard_map/ppermute | solution.py:285
  64.2 9.3 %collective-permute-start.21 = (bf16[64,2048]{1,0:T(8,128)(2,1)S(1)}, bf16[64,2048]{1,0:T(8,128)(2,1)S(1)}, u32[]{:S(2)}, u32[]{:S(2)}) collective-permute-start(bf16[64,2048]{1,0:T(8,128)(2,1)S(1)} %convert_element_type.75), channel_id=1, source_target_pairs={{2,6},{3,7},{6,10},{7,11},{10,14},{11,15},{14,12},{15,13},{12,8},{... | collective-permute-start | bytes 786440 | tf_op jit(solution)/shard_map/ppermute | solution.py:285
  68.6 14.6 %collective-permute-start.26 = (bf16[64,2048]{1,0:T(8,128)(2,1)S(1)}, bf16[64,2048]{1,0:T(8,128)(2,1)S(1)}, u32[]{:S(2)}, u32[]{:S(2)}) collective-permute-start(bf16[64,2048]{1,0:T(8,128)(2,1)S(1)} %get-tuple-element.104), channel_id=1, source_target_pairs={{2,6},{3,7},{6,10},{7,11},{10,14},{11,15},{14,12},{15,13},{12,8},{... | collective-permute-start | bytes 786440 | tf_op jit(solution)/shard_map/ppermute | solution.py:285
  69.1 15.7 %collective-permute-start.20 = (bf16[64,2048]{1,0:T(8,128)(2,1)S(1)}, bf16[64,2048]{1,0:T(8,128)(2,1)S(1)}, u32[]{:S(2)}, u32[]{:S(2)}) collective-permute-start(bf16[64,2048]{1,0:T(8,128)(2,1)S(1)} %get-tuple-element.96), channel_id=1, source_target_pairs={{6,2},{7,3},{10,6},{11,7},{14,10},{15,11},{12,14},{13,15},{8,12},{... | collective-permute-start | bytes 786440 | tf_op jit(solution)/shard_map/ppermute | solution.py:285
  71.9 9.1 %collective-permute-start.24 = (bf16[64,2048]{1,0:T(8,128)(2,1)S(1)}, bf16[64,2048]{1,0:T(8,128)(2,1)S(1)}, u32[]{:S(2)}, u32[]{:S(2)}) collective-permute-start(bf16[64,2048]{1,0:T(8,128)(2,1)S(1)} %add_convert_fusion.5), channel_id=1, source_target_pairs={{6,2},{7,3},{10,6},{11,7},{14,10},{15,11},{12,14},{13,15},{8,12},{... | collective-permute-start | bytes 786440 | tf_op jit(solution)/shard_map/ppermute | solution.py:285
  73.6 9.2 %collective-permute-start.22 = (bf16[64,2048]{1,0:T(8,128)(2,1)S(1)}, bf16[64,2048]{1,0:T(8,128)(2,1)S(1)}, u32[]{:S(2)}, u32[]{:S(2)}) collective-permute-start(bf16[64,2048]{1,0:T(8,128)(2,1)S(1)} %add_convert_fusion.7), channel_id=1, source_target_pairs={{2,6},{3,7},{6,10},{7,11},{10,14},{11,15},{14,12},{15,13},{12,8},{... | collective-permute-start | bytes 786440 | tf_op jit(solution)/shard_map/ppermute | solution.py:285
  81.0 8.5 %collective-permute-start.30 = (bf16[64,2048]{1,0:T(8,128)(2,1)S(1)}, bf16[64,2048]{1,0:T(8,128)(2,1)S(1)}, u32[]{:S(2)}, u32[]{:S(2)}) collective-permute-start(bf16[64,2048]{1,0:T(8,128)(2,1)S(1)} %add_convert_fusion.4), channel_id=1, source_target_pairs={{6,2},{7,3},{10,6},{11,7},{14,10},{15,11},{12,14},{13,15},{8,12},{... | collective-permute-start | bytes 786440 | tf_op jit(solution)/shard_map/ppermute | solution.py:285
  82.8 9.3 %collective-permute-start.28 = (bf16[64,2048]{1,0:T(8,128)(2,1)S(1)}, bf16[64,2048]{1,0:T(8,128)(2,1)S(1)}, u32[]{:S(2)}, u32[]{:S(2)}) collective-permute-start(bf16[64,2048]{1,0:T(8,128)(2,1)S(1)} %add_convert_fusion.6), channel_id=1, source_target_pairs={{2,6},{3,7},{6,10},{7,11},{10,14},{11,15},{14,12},{15,13},{12,8},{... | collective-permute-start | bytes 786440 | tf_op jit(solution)/shard_map/ppermute | solution.py:285
  83.3 13.8 %collective-permute-start.27 = (bf16[64,2048]{1,0:T(8,128)(2,1)S(1)}, bf16[64,2048]{1,0:T(8,128)(2,1)S(1)}, u32[]{:S(2)}, u32[]{:S(2)}) collective-permute-start(bf16[64,2048]{1,0:T(8,128)(2,1)S(1)} %add_convert_fusion.2), channel_id=1, source_target_pairs={{2,6},{3,7},{6,10},{7,11},{10,14},{11,15},{14,12},{15,13},{12,8},{... | collective-permute-start | bytes 786440 | tf_op jit(solution)/shard_map/ppermute | solution.py:285
  84.9 12.3 %collective-permute-start.25 = (bf16[64,2048]{1,0:T(8,128)(2,1)S(1)}, bf16[64,2048]{1,0:T(8,128)(2,1)S(1)}, u32[]{:S(2)}, u32[]{:S(2)}) collective-permute-start(bf16[64,2048]{1,0:T(8,128)(2,1)S(1)} %add_convert_fusion.3), channel_id=1, source_target_pairs={{6,2},{7,3},{10,6},{11,7},{14,10},{15,11},{12,14},{13,15},{8,12},{... | collective-permute-start | bytes 786440 | tf_op jit(solution)/shard_map/ppermute | solution.py:285
  89.5 9.2 %collective-permute-start.31 = (bf16[64,2048]{1,0:T(8,128)(2,1)S(1)}, bf16[64,2048]{1,0:T(8,128)(2,1)S(1)}, u32[]{:S(2)}, u32[]{:S(2)}) collective-permute-start(bf16[64,2048]{1,0:T(8,128)(2,1)S(1)} %add_convert_fusion), channel_id=1, source_target_pairs={{6,2},{7,3},{10,6},{11,7},{14,10},{15,11},{12,14},{13,15},{8,12},{... | collective-permute-start | bytes 786440 | tf_op jit(solution)/shard_map/ppermute | solution.py:285
  92.2 7.7 %collective-permute-start.29 = (bf16[64,2048]{1,0:T(8,128)(2,1)S(1)}, bf16[64,2048]{1,0:T(8,128)(2,1)S(1)}, u32[]{:S(2)}, u32[]{:S(2)}) collective-permute-start(bf16[64,2048]{1,0:T(8,128)(2,1)S(1)} %add_convert_fusion.1), channel_id=1, source_target_pairs={{2,6},{3,7},{6,10},{7,11},{10,14},{11,15},{14,12},{15,13},{12,8},{... | collective-permute-start | bytes 786440 | tf_op jit(solution)/shard_map/ppermute | solution.py:285

commit v17 on v14

--- a/solution.py
+++ b/solution.py
@@ -318,8 +318,9 @@
     for s in range(1, hops):
         for c in range(2):
             pass_on(s, c, last)
+            if (s, c) == (2, 0):
+                early_sums = mlp(packed, (), (), 1)
             to_down[s, c], to_up[s, c] = mlp([ups[s][c], downs[s][c]])
-    early_sums = mlp(packed, (), (), 1)
     to_up[hops, 0], to_down[hops, 1] = mlp([ups[hops][0], downs[hops][1]])
 
     def send_on(flow, place, total, after):

time: 98.7 us -> 99.8 us (1.011)
  transfers between devices with their start and end apart: 32 -> 32, of which waited for: 13 -> 15; matrix products, arithmetic and copies ran while one was open for 2% -> 2% of each run, Pallas kernels for 23% -> 23%
where the time goes in v17:
time: 99.8 us; the launch traced here: 99.5 us
  starting transfers between devices  36.9 us (37%)
  waiting for transfers between devices  30.6 us (31%)
  Pallas kernels  23.9 us (24%)
  local copies, waits for them, and re-layouts  7.22 us (7%)
    ppermute x30, starting transfers between devices, move(): return lax.ppermute(value, 'expert', pairs)  30.7 us
    ppermute x30, waiting for transfers between devices, move(): return lax.ppermute(value, 'expert', pairs)  26.1 us
    pallas_call x9, Pallas kernels, expert_rows(): pl.pallas_call(functools.partial(mlp_kernel, parts=len(payloads), adds=le...  22.6 us
    ppermute x2, starting transfers between devices, from_behind(): return lax.ppermute(value, axis, pairs)  6.18 us
    unnamed x12, local copies, waits for them, and re-layouts  5.89 us
    ppermute x2, waiting for transfers between devices, from_behind(): return lax.ppermute(value, axis, pairs)  4.5 us
  transfers between devices with their start and end apart: 32, of which 15 were waited for; matrix products, arithmetic and copies ran while one was open for 2% of the time, Pallas kernels for 23%

profile of v17, /device:TPU:0, one launch (start us, length us, event | category | flops | bytes accessed | tf_op | source)
XLA Modules:
  0.0 99.5 jit_solution(13065614906281322097)
XLA Ops:
  0.0 0.5 collective-permute-start.2
  0.5 1.3 %slice_bitcast_fusion = (bf16[64,2048]{1,0:T(8,128)(2,1)S(1)}, bf16[64,2048]{1,0:T(8,128)(2,1)S(1)}) fusion(bf16[1,128,2048]{2,1,0:T(8,128)(2,1)} %param.8), kind=kLoop, calls=%fused_computation.10 | loop fusion | bytes 1048576 | tf_op jit(solution)/shard_map/squeeze | solution.py:292
  1.9 4.9 %collective-permute-start = (bf16[64,2048]{1,0:T(8,128)(2,1)S(1)}, bf16[64,2048]{1,0:T(8,128)(2,1)S(1)}, u32[]{:S(2)}, u32[]{:S(2)}) collective-permute-start(bf16[64,2048]{1,0:T(8,128)(2,1)S(1)} %get-tuple-element.106), channel_id=1, source_target_pairs={{0,16},{1,17},{2,18},{3,19},{4,20},{5,21},{6,22},{7,23},{8,24},{9,... | collective-permute-start | bytes 786440 | tf_op jit(solution)/shard_map/ppermute | solution.py:20
  6.7 1.3 %collective-permute-start.1 = (bf16[64,2048]{1,0:T(8,128)(2,1)S(1)}, bf16[64,2048]{1,0:T(8,128)(2,1)S(1)}, u32[]{:S(2)}, u32[]{:S(2)}) collective-permute-start(bf16[64,2048]{1,0:T(8,128)(2,1)S(1)} %get-tuple-element.105), channel_id=1, source_target_pairs={{0,16},{1,17},{2,18},{3,19},{4,20},{5,21},{6,22},{7,23},{8,24},{9,... | collective-permute-start | bytes 786440 | tf_op jit(solution)/shard_map/ppermute | solution.py:20
  8.1 1.0 %copy-done.2 = bf16[128,2048]{1,0:T(8,128)(2,1)S(1)} copy-done((bf16[128,2048]{1,0:T(8,128)(2,1)S(1)}, bf16[128,2048]{1,0:T(8,128)(2,1)}, u32[]{:S(2)}) %copy-start.2) | copy-done | bytes 524312
  9.1 0.7 copy-done.3
  9.8 0.7 copy-done.4
  10.5 0.7 copy-done.5
  11.2 0.2 base_rows.1
  11.4 2.0 %collective-permute-done.arrived_ref = bf16[64,2048]{1,0:T(8,128)(2,1)S(1)} collective-permute-done((bf16[64,2048]{1,0:T(8,128)(2,1)S(1)}, bf16[64,2048]{1,0:T(8,128)(2,1)S(1)}, u32[]{:S(2)}, u32[]{:S(2)}) %collective-permute-start) | collective-permute-done | bytes 262176 | tf_op jit(solution)/shard_map/ppermute | solution.py:20
  13.5 1.5 %collective-permute-start.4 = (bf16[1040,128]{1,0:T(8,128)(2,1)S(1)}, bf16[1040,128]{1,0:T(8,128)(2,1)S(1)}, u32[]{:S(2)}, u32[]{:S(2)}) collective-permute-start(bf16[1040,128]{1,0:T(8,128)(2,1)S(1)} %get-tuple-element.65.refs_0_), channel_id=1, source_target_pairs={{2,6},{3,7},{6,10},{7,11},{10,14},{11,15},{14,12},{15,13},{12,8},{... | collective-permute-start | bytes 798728 | tf_op jit(solution)/shard_map/ppermute | solution.py:285
  15.0 0.5 collective-permute-start.5
  15.5 2.5 %collective-permute-done.1.arrived_ref = bf16[64,2048]{1,0:T(8,128)(2,1)S(1)} collective-permute-done((bf16[64,2048]{1,0:T(8,128)(2,1)S(1)}, bf16[64,2048]{1,0:T(8,128)(2,1)S(1)}, u32[]{:S(2)}, u32[]{:S(2)}) %collective-permute-start.1) | collective-permute-done | bytes 262176 | tf_op jit(solution)/shard_map/ppermute | solution.py:20
  18.2 1.5 %collective-permute-start.8 = (bf16[1040,128]{1,0:T(8,128)(2,1)S(1)}, bf16[1040,128]{1,0:T(8,128)(2,1)S(1)}, u32[]{:S(2)}, u32[]{:S(2)}) collective-permute-start(bf16[1040,128]{1,0:T(8,128)(2,1)S(1)} %get-tuple-element.69.refs_1_), channel_id=1, source_target_pairs={{2,6},{3,7},{6,10},{7,11},{10,14},{11,15},{14,12},{15,13},{12,8},{... | collective-permute-start | bytes 798728 | tf_op jit(solution)/shard_map/ppermute | solution.py:285
  19.7 0.5 collective-permute-start.9
  20.2 1.3 %collective-permute-done.5.refs_1_ = bf16[1040,128]{1,0:T(8,128)(2,1)S(1)} collective-permute-done((bf16[1040,128]{1,0:T(8,128)(2,1)S(1)}, bf16[1040,128]{1,0:T(8,128)(2,1)S(1)}, u32[]{:S(2)}, u32[]{:S(2)}) %collective-permute-start.5) | collective-permute-done | bytes 266272 | tf_op jit(solution)/shard_map/ppermute | solution.py:285
  21.6 1.6 %collective-permute-start.6 = (bf16[1040,128]{1,0:T(8,128)(2,1)S(1)}, bf16[1040,128]{1,0:T(8,128)(2,1)S(1)}, u32[]{:S(2)}, u32[]{:S(2)}) collective-permute-start(bf16[1040,128]{1,0:T(8,128)(2,1)S(1)} %collective-permute-done.4.refs_0_), channel_id=1, source_target_pairs={{2,6},{3,7},{6,10},{7,11},{10,14},{11,15},{14,12},{15,13},{12,8},{... | collective-permute-start | bytes 798728 | tf_op jit(solution)/shard_map/ppermute | solution.py:285
  23.2 0.4 collective-permute-start.7
  23.6 2.8 %copy-done = bf16[1,1,2048,1536]{3,2,1,0:T(8,128)(2,1)S(1)} copy-done((bf16[1,1,2048,1536]{3,2,1,0:T(8,128)(2,1)S(1)}, bf16[1,1,2048,1536]{3,2,1,0:T(8,128)(2,1)}, u32[]{:S(2)}) %copy-start) | copy-done | bytes 6291480
  26.4 2.8 %expert_rows.9 = (f32[64,2048]{1,0:T(8,128)S(1)}, f32[64,2048]{1,0:T(8,128)S(1)}) custom-call(s32[1]{0:T(128)} %bitcast.6.expert_ref, bf16[1040,128]{1,0:T(8,128)(2,1)S(1)} %collective-permute-done.4.refs_0_, bf16[1040,128]{1,0:T(8,128)(2,1)S(1)} %collective-permute-done.5.refs_1_, bf16[2048,1536]{1,0:T(8,128)(2,1)S(1)} %bitcast.16, ...), custom_call_target="tpu_custom_call" | custom-call | flops 2415919104 | bytes 1572864 | tf_op jit(solution)/shard_map/expert_rows/pallas_call | solution.py:217
  29.2 1.6 %collective-permute-start.10 = (bf16[1040,128]{1,0:T(8,128)(2,1)S(1)}, bf16[1040,128]{1,0:T(8,128)(2,1)S(1)}, u32[]{:S(2)}, u32[]{:S(2)}) collective-permute-start(bf16[1040,128]{1,0:T(8,128)(2,1)S(1)} %collective-permute-done.8.refs_0_), channel_id=1, source_target_pairs={{2,6},{3,7},{6,10},{7,11},{10,14},{11,15},{14,12},{15,13},{12,8},{... | collective-permute-start | bytes 798728 | tf_op jit(solution)/shard_map/ppermute | solution.py:285
  30.8 0.5 collective-permute-start.11
  31.3 2.8 %expert_rows.10 = (f32[64,2048]{1,0:T(8,128)S(1)}, f32[64,2048]{1,0:T(8,128)S(1)}) custom-call(s32[1]{0:T(128)} %bitcast.6.expert_ref, bf16[1040,128]{1,0:T(8,128)(2,1)S(1)} %collective-permute-done.8.refs_0_, bf16[1040,128]{1,0:T(8,128)(2,1)S(1)} %collective-permute-done.9.refs_1_, bf16[2048,1536]{1,0:T(8,128)(2,1)S(1)} %bitcast.17, ...), custom_call_target="tpu_custom_call" | custom-call | flops 2415919104 | bytes 1572864 | tf_op jit(solution)/shard_map/expert_rows/pallas_call | solution.py:217
  34.1 0.6 collective-permute-done.7.refs_1_
  34.7 1.6 %collective-permute-start.12 = (bf16[1040,128]{1,0:T(8,128)(2,1)S(1)}, bf16[1040,128]{1,0:T(8,128)(2,1)S(1)}, u32[]{:S(2)}, u32[]{:S(2)}) collective-permute-start(bf16[1040,128]{1,0:T(8,128)(2,1)S(1)} %collective-permute-done.6.refs_0_), channel_id=1, source_target_pairs={{2,6},{3,7},{6,10},{7,11},{10,14},{11,15},{14,12},{15,13},{12,8},{... | collective-permute-start | bytes 798728 | tf_op jit(solution)/shard_map/ppermute | solution.py:285
  36.3 0.4 collective-permute-start.13
  36.8 2.8 %expert_rows.12 = (f32[64,2048]{1,0:T(8,128)S(1)}, f32[64,2048]{1,0:T(8,128)S(1)}) custom-call(s32[1]{0:T(128)} %bitcast.6.expert_ref, bf16[1040,128]{1,0:T(8,128)(2,1)S(1)} %collective-permute-done.6.refs_0_, bf16[1040,128]{1,0:T(8,128)(2,1)S(1)} %collective-permute-done.7.refs_1_, bf16[2048,1536]{1,0:T(8,128)(2,1)S(1)} %bitcast.19, ...), custom_call_target="tpu_custom_call" | custom-call | flops 2415919104 | bytes 1572864 | tf_op jit(solution)/shard_map/expert_rows/pallas_call | solution.py:217
  39.6 0.9 collective-permute-done.11.refs_1_
  40.5 1.6 %collective-permute-start.14 = (bf16[1040,128]{1,0:T(8,128)(2,1)S(1)}, bf16[1040,128]{1,0:T(8,128)(2,1)S(1)}, u32[]{:S(2)}, u32[]{:S(2)}) collective-permute-start(bf16[1040,128]{1,0:T(8,128)(2,1)S(1)} %collective-permute-done.10.refs_0_), channel_id=1, source_target_pairs={{2,6},{3,7},{6,10},{7,11},{10,14},{11,15},{14,12},{15,13},{12,8},{... | collective-permute-start | bytes 798728 | tf_op jit(solution)/shard_map/ppermute | solution.py:285
  42.0 0.5 collective-permute-start.15
  42.5 2.8 %expert_rows.13 = (f32[64,2048]{1,0:T(8,128)S(1)}, f32[64,2048]{1,0:T(8,128)S(1)}) custom-call(s32[1]{0:T(128)} %bitcast.6.expert_ref, bf16[1040,128]{1,0:T(8,128)(2,1)S(1)} %collective-permute-done.10.refs_0_, bf16[1040,128]{1,0:T(8,128)(2,1)S(1)} %collective-permute-done.11.refs_1_, bf16[2048,1536]{1,0:T(8,128)(2,1)S(1)} %bitcast.20, ...), custom_call_target="tpu_custom_call" | custom-call | flops 2415919104 | bytes 1572864 | tf_op jit(solution)/shard_map/expert_rows/pallas_call | solution.py:217
  45.3 0.9 collective-permute-done.13.refs_1_
  46.2 1.6 %collective-permute-start.18 = (bf16[1040,128]{1,0:T(8,128)(2,1)S(1)}, bf16[1040,128]{1,0:T(8,128)(2,1)S(1)}, u32[]{:S(2)}, u32[]{:S(2)}) collective-permute-start(bf16[1040,128]{1,0:T(8,128)(2,1)S(1)} %collective-permute-done.12.refs_0_), channel_id=1, source_target_pairs={{2,6},{3,7},{6,10},{7,11},{10,14},{11,15},{14,12},{15,13},{12,8},{... | collective-permute-start | bytes 798728 | tf_op jit(solution)/shard_map/ppermute | solution.py:285
  47.7 2.8 %expert_rows.14 = (f32[64,2048]{1,0:T(8,128)S(1)}, f32[64,2048]{1,0:T(8,128)S(1)}) custom-call(s32[1]{0:T(128)} %bitcast.6.expert_ref, bf16[1040,128]{1,0:T(8,128)(2,1)S(1)} %collective-permute-done.12.refs_0_, bf16[1040,128]{1,0:T(8,128)(2,1)S(1)} %collective-permute-done.13.refs_1_, bf16[2048,1536]{1,0:T(8,128)(2,1)S(1)} %bitcast.21, ...), custom_call_target="tpu_custom_call" | custom-call | flops 2415919104 | bytes 1572864 | tf_op jit(solution)/shard_map/expert_rows/pallas_call | solution.py:217
  50.5 1.4 %collective-permute-start.19 = (bf16[1040,128]{1,0:T(8,128)(2,1)S(1)}, bf16[1040,128]{1,0:T(8,128)(2,1)S(1)}, u32[]{:S(2)}, u32[]{:S(2)}) collective-permute-start(bf16[1040,128]{1,0:T(8,128)(2,1)S(1)} %collective-permute-done.15.refs_1_), channel_id=1, source_target_pairs={{6,2},{7,3},{10,6},{11,7},{14,10},{15,11},{12,14},{13,15},{8,12},{... | collective-permute-start | bytes 798728 | tf_op jit(solution)/shard_map/ppermute | solution.py:285
  51.9 2.8 %expert_rows.15 = (f32[64,2048]{1,0:T(8,128)S(1)}, f32[64,2048]{1,0:T(8,128)S(1)}) custom-call(s32[1]{0:T(128)} %bitcast.6.expert_ref, bf16[1040,128]{1,0:T(8,128)(2,1)S(1)} %collective-permute-done.14.refs_0_, bf16[1040,128]{1,0:T(8,128)(2,1)S(1)} %collective-permute-done.15.refs_1_, bf16[2048,1536]{1,0:T(8,128)(2,1)S(1)} %bitcast.22, ...), custom_call_target="tpu_custom_call" | custom-call | flops 2415919104 | bytes 1572864 | tf_op jit(solution)/shard_map/expert_rows/pallas_call | solution.py:217
  54.8 1.6 %collective-permute-start.16 = (bf16[64,2048]{1,0:T(8,128)(2,1)S(1)}, bf16[64,2048]{1,0:T(8,128)(2,1)S(1)}, u32[]{:S(2)}, u32[]{:S(2)}) collective-permute-start(bf16[64,2048]{1,0:T(8,128)(2,1)S(1)} %convert_element_type.73), channel_id=1, source_target_pairs={{6,2},{7,3},{10,6},{11,7},{14,10},{15,11},{12,14},{13,15},{8,12},{... | collective-permute-start | bytes 786440 | tf_op jit(solution)/shard_map/ppermute | solution.py:285
  56.4 0.5 collective-permute-start.17
  57.0 2.9 %collective-permute-done.19.refs_1_ = bf16[1040,128]{1,0:T(8,128)(2,1)S(1)} collective-permute-done((bf16[1040,128]{1,0:T(8,128)(2,1)S(1)}, bf16[1040,128]{1,0:T(8,128)(2,1)S(1)}, u32[]{:S(2)}, u32[]{:S(2)}) %collective-permute-start.19) | collective-permute-done | bytes 266272 | tf_op jit(solution)/shard_map/ppermute | solution.py:285
  59.9 2.8 %expert_rows.16 = (f32[64,2048]{1,0:T(8,128)S(1)}, f32[64,2048]{1,0:T(8,128)S(1)}) custom-call(s32[1]{0:T(128)} %bitcast.6.expert_ref, bf16[1040,128]{1,0:T(8,128)(2,1)S(1)} %collective-permute-done.18.refs_0_, bf16[1040,128]{1,0:T(8,128)(2,1)S(1)} %collective-permute-done.19.refs_1_, bf16[2048,1536]{1,0:T(8,128)(2,1)S(1)} %bitcast.23, ...), custom_call_target="tpu_custom_call" | custom-call | flops 2415919104 | bytes 1572864 | tf_op jit(solution)/shard_map/expert_rows/pallas_call | solution.py:217
  62.7 1.4 %collective-permute-start.23 = (bf16[64,2048]{1,0:T(8,128)(2,1)S(1)}, bf16[64,2048]{1,0:T(8,128)(2,1)S(1)}, u32[]{:S(2)}, u32[]{:S(2)}) collective-permute-start(bf16[64,2048]{1,0:T(8,128)(2,1)S(1)} %convert_element_type.80), channel_id=1, source_target_pairs={{6,2},{7,3},{10,6},{11,7},{14,10},{15,11},{12,14},{13,15},{8,12},{... | collective-permute-start | bytes 786440 | tf_op jit(solution)/shard_map/ppermute | solution.py:285
  64.1 0.7 collective-permute-start.21
  64.8 0.6 collective-permute-done.16.refs_8_
  65.5 0.1 collective-permute-done.17.refs_9_
  65.6 3.1 %expert_rows.17 = (f32[64,2048]{1,0:T(8,128)S(1)}, f32[64,2048]{1,0:T(8,128)S(1)}, bf16[64,2048]{1,0:T(8,128)(2,1)S(1)}, bf16[64,2048]{1,0:T(8,128)(2,1)S(1)}) custom-call(s32[1]{0:T(128)} %bitcast.6.expert_ref, bf16[1040,128]{1,0:T(8,128)(2,1)S(1)} %get-tuple-element.65.refs_0_, bf16[1040,128]{1,0:T(8,128)(2,1)S(1)} %get-tuple-element.69.refs_1_, ...), custom_call_target="tpu_custom_call" | custom-call | flops 2415919104 | bytes 1572864 | tf_op jit(solution)/shard_map/expert_rows/pallas_call | solution.py:217
  68.7 1.3 %collective-permute-start.26 = (bf16[64,2048]{1,0:T(8,128)(2,1)S(1)}, bf16[64,2048]{1,0:T(8,128)(2,1)S(1)}, u32[]{:S(2)}, u32[]{:S(2)}) collective-permute-start(bf16[64,2048]{1,0:T(8,128)(2,1)S(1)} %get-tuple-element.100), channel_id=1, source_target_pairs={{2,6},{3,7},{6,10},{7,11},{10,14},{11,15},{14,12},{15,13},{12,8},{... | collective-permute-start | bytes 786440 | tf_op jit(solution)/shard_map/ppermute | solution.py:285
  70.1 0.7 collective-permute-start.20
  70.8 1.1 %collective-permute-done.23 = bf16[64,2048]{1,0:T(8,128)(2,1)S(1)} collective-permute-done((bf16[64,2048]{1,0:T(8,128)(2,1)S(1)}, bf16[64,2048]{1,0:T(8,128)(2,1)S(1)}, u32[]{:S(2)}, u32[]{:S(2)}) %collective-permute-start.23) | collective-permute-done | bytes 262176 | tf_op jit(solution)/shard_map/ppermute | solution.py:285
  72.0 1.4 %collective-permute-start.24 = (bf16[64,2048]{1,0:T(8,128)(2,1)S(1)}, bf16[64,2048]{1,0:T(8,128)(2,1)S(1)}, u32[]{:S(2)}, u32[]{:S(2)}) collective-permute-start(bf16[64,2048]{1,0:T(8,128)(2,1)S(1)} %add_convert_fusion.5), channel_id=1, source_target_pairs={{6,2},{7,3},{10,6},{11,7},{14,10},{15,11},{12,14},{13,15},{8,12},{... | collective-permute-start | bytes 786440 | tf_op jit(solution)/shard_map/ppermute | solution.py:285
  73.5 0.7 collective-permute-start.22
  74.2 7.8 %collective-permute-done.24 = bf16[64,2048]{1,0:T(8,128)(2,1)S(1)} collective-permute-done((bf16[64,2048]{1,0:T(8,128)(2,1)S(1)}, bf16[64,2048]{1,0:T(8,128)(2,1)S(1)}, u32[]{:S(2)}, u32[]{:S(2)}) %collective-permute-start.24) | collective-permute-done | bytes 262176 | tf_op jit(solution)/shard_map/ppermute | solution.py:285
  82.1 0.8 collective-permute-start.30
  83.0 1.3 %collective-permute-start.28 = (bf16[64,2048]{1,0:T(8,128)(2,1)S(1)}, bf16[64,2048]{1,0:T(8,128)(2,1)S(1)}, u32[]{:S(2)}, u32[]{:S(2)}) collective-permute-start(bf16[64,2048]{1,0:T(8,128)(2,1)S(1)} %add_convert_fusion.6), channel_id=1, source_target_pairs={{2,6},{3,7},{6,10},{7,11},{10,14},{11,15},{14,12},{15,13},{12,8},{... | collective-permute-start | bytes 786440 | tf_op jit(solution)/shard_map/ppermute | solution.py:285
  84.4 1.7 %collective-permute-start.27 = (bf16[64,2048]{1,0:T(8,128)(2,1)S(1)}, bf16[64,2048]{1,0:T(8,128)(2,1)S(1)}, u32[]{:S(2)}, u32[]{:S(2)}) collective-permute-start(bf16[64,2048]{1,0:T(8,128)(2,1)S(1)} %add_convert_fusion.2), channel_id=1, source_target_pairs={{2,6},{3,7},{6,10},{7,11},{10,14},{11,15},{14,12},{15,13},{12,8},{... | collective-permute-start | bytes 786440 | tf_op jit(solution)/shard_map/ppermute | solution.py:285
  86.1 0.4 collective-permute-start.25
  86.6 4.0 %collective-permute-done.30 = bf16[64,2048]{1,0:T(8,128)(2,1)S(1)} collective-permute-done((bf16[64,2048]{1,0:T(8,128)(2,1)S(1)}, bf16[64,2048]{1,0:T(8,128)(2,1)S(1)}, u32[]{:S(2)}, u32[]{:S(2)}) %collective-permute-start.30) | collective-permute-done | bytes 262176 | tf_op jit(solution)/shard_map/ppermute | solution.py:285
  90.6 1.6 %collective-permute-start.31 = (bf16[64,2048]{1,0:T(8,128)(2,1)S(1)}, bf16[64,2048]{1,0:T(8,128)(2,1)S(1)}, u32[]{:S(2)}, u32[]{:S(2)}) collective-permute-start(bf16[64,2048]{1,0:T(8,128)(2,1)S(1)} %add_convert_fusion), channel_id=1, source_target_pairs={{6,2},{7,3},{10,6},{11,7},{14,10},{15,11},{12,14},{13,15},{8,12},{... | collective-permute-start | bytes 786440 | tf_op jit(solution)/shard_map/ppermute | solution.py:285
  92.2 0.6 collective-permute-start.29
  92.7 1.6 %collective-permute-done.27 = bf16[64,2048]{1,0:T(8,128)(2,1)S(1)} collective-permute-done((bf16[64,2048]{1,0:T(8,128)(2,1)S(1)}, bf16[64,2048]{1,0:T(8,128)(2,1)S(1)}, u32[]{:S(2)}, u32[]{:S(2)}) %collective-permute-start.27) | collective-permute-done | bytes 262176 | tf_op jit(solution)/shard_map/ppermute | solution.py:285
  94.4 0.1 add_add_fusion.near1_ref
  94.5 0.1 add_add_fusion.1.near0_ref
  94.6 2.4 %collective-permute-done.31.total1_ref = bf16[64,2048]{1,0:T(8,128)(2,1)S(1)} collective-permute-done((bf16[64,2048]{1,0:T(8,128)(2,1)S(1)}, bf16[64,2048]{1,0:T(8,128)(2,1)S(1)}, u32[]{:S(2)}, u32[]{:S(2)}) %collective-permute-start.31) | collective-permute-done | bytes 262176 | tf_op jit(solution)/shard_map/ppermute | solution.py:285
  97.0 1.6 %collective-permute-done.29.total0_ref = bf16[64,2048]{1,0:T(8,128)(2,1)S(1)} collective-permute-done((bf16[64,2048]{1,0:T(8,128)(2,1)S(1)}, bf16[64,2048]{1,0:T(8,128)(2,1)S(1)}, u32[]{:S(2)}, u32[]{:S(2)}) %collective-permute-start.29) | collective-permute-done | bytes 262176 | tf_op jit(solution)/shard_map/ppermute | solution.py:285
  98.6 0.9 last_rows.1
  (40 shorter events, 0.8 us)
Async XLA Ops:
  0.0 23.6 %copy-start.1 = (bf16[1,1,768,2048]{3,2,1,0:T(8,128)(2,1)S(1)}, bf16[1,1,768,2048]{3,2,1,0:T(8,128)(2,1)}, u32[]{:S(2)}) copy-start(bf16[1,1,768,2048]{3,2,1,0:T(8,128)(2,1)} %param.13) | copy-start | bytes 9437188
  0.0 18.1 %collective-permute-start.2 = (bf16[2048,1536]{1,0:T(8,128)(2,1)}, bf16[2048,1536]{1,0:T(8,128)(2,1)S(1)}, u32[]{:S(2)}, u32[]{:S(2)}) collective-permute-start(bf16[2048,1536]{1,0:T(8,128)(2,1)} %bitcast.15), channel_id=1, source_target_pairs={{0,1},{1,0},{2,3},{3,2},{4,5},{5,4},{6,7},{7,6},{8,9},{9,8},{10,11... | collective-permute-start | bytes 18874376 | tf_op jit(solution)/shard_map/ppermute | solution.py:285
  0.5 17.7 %collective-permute-start.3 = (bf16[768,2048]{1,0:T(8,128)(2,1)}, bf16[768,2048]{1,0:T(8,128)(2,1)S(1)}, u32[]{:S(2)}, u32[]{:S(2)}) collective-permute-start(bf16[768,2048]{1,0:T(8,128)(2,1)} %bitcast.25), channel_id=1, source_target_pairs={{0,1},{1,0},{2,3},{3,2},{4,5},{5,4},{6,7},{7,6},{8,9},{9,8},{10,11... | collective-permute-start | bytes 9437192 | tf_op jit(solution)/shard_map/ppermute | solution.py:285
  1.9 11.5 %collective-permute-start = (bf16[64,2048]{1,0:T(8,128)(2,1)S(1)}, bf16[64,2048]{1,0:T(8,128)(2,1)S(1)}, u32[]{:S(2)}, u32[]{:S(2)}) collective-permute-start(bf16[64,2048]{1,0:T(8,128)(2,1)S(1)} %get-tuple-element.106), channel_id=1, source_target_pairs={{0,16},{1,17},{2,18},{3,19},{4,20},{5,21},{6,22},{7,23},{8,24},{9,... | collective-permute-start | bytes 786440 | tf_op jit(solution)/shard_map/ppermute | solution.py:20
  6.7 11.3 %collective-permute-start.1 = (bf16[64,2048]{1,0:T(8,128)(2,1)S(1)}, bf16[64,2048]{1,0:T(8,128)(2,1)S(1)}, u32[]{:S(2)}, u32[]{:S(2)}) collective-permute-start(bf16[64,2048]{1,0:T(8,128)(2,1)S(1)} %get-tuple-element.105), channel_id=1, source_target_pairs={{0,16},{1,17},{2,18},{3,19},{4,20},{5,21},{6,22},{7,23},{8,24},{9,... | collective-permute-start | bytes 786440 | tf_op jit(solution)/shard_map/ppermute | solution.py:20
  8.1 1.0 %copy-start.2 = (bf16[128,2048]{1,0:T(8,128)(2,1)S(1)}, bf16[128,2048]{1,0:T(8,128)(2,1)}, u32[]{:S(2)}) copy-start(bf16[128,2048]{1,0:T(8,128)(2,1)} %fresh_ref.1) | copy-start | bytes 1572868
  9.1 0.7 copy-start.3
  9.8 0.7 copy-start.4
  10.5 0.7 copy-start.5
  13.5 6.8 %collective-permute-start.4 = (bf16[1040,128]{1,0:T(8,128)(2,1)S(1)}, bf16[1040,128]{1,0:T(8,128)(2,1)S(1)}, u32[]{:S(2)}, u32[]{:S(2)}) collective-permute-start(bf16[1040,128]{1,0:T(8,128)(2,1)S(1)} %get-tuple-element.65.refs_0_), channel_id=1, source_target_pairs={{2,6},{3,7},{6,10},{7,11},{10,14},{11,15},{14,12},{15,13},{12,8},{... | collective-permute-start | bytes 798728 | tf_op jit(solution)/shard_map/ppermute | solution.py:285
  15.0 6.6 %collective-permute-start.5 = (bf16[1040,128]{1,0:T(8,128)(2,1)S(1)}, bf16[1040,128]{1,0:T(8,128)(2,1)S(1)}, u32[]{:S(2)}, u32[]{:S(2)}) collective-permute-start(bf16[1040,128]{1,0:T(8,128)(2,1)S(1)} %get-tuple-element.65.refs_0_), channel_id=1, source_target_pairs={{6,2},{7,3},{10,6},{11,7},{14,10},{15,11},{12,14},{13,15},{8,12},{... | collective-permute-start | bytes 798728 | tf_op jit(solution)/shard_map/ppermute | solution.py:285
  18.2 11.0 %collective-permute-start.8 = (bf16[1040,128]{1,0:T(8,128)(2,1)S(1)}, bf16[1040,128]{1,0:T(8,128)(2,1)S(1)}, u32[]{:S(2)}, u32[]{:S(2)}) collective-permute-start(bf16[1040,128]{1,0:T(8,128)(2,1)S(1)} %get-tuple-element.69.refs_1_), channel_id=1, source_target_pairs={{2,6},{3,7},{6,10},{7,11},{10,14},{11,15},{14,12},{15,13},{12,8},{... | collective-permute-start | bytes 798728 | tf_op jit(solution)/shard_map/ppermute | solution.py:285
  19.7 9.5 %collective-permute-start.9 = (bf16[1040,128]{1,0:T(8,128)(2,1)S(1)}, bf16[1040,128]{1,0:T(8,128)(2,1)S(1)}, u32[]{:S(2)}, u32[]{:S(2)}) collective-permute-start(bf16[1040,128]{1,0:T(8,128)(2,1)S(1)} %get-tuple-element.69.refs_1_), channel_id=1, source_target_pairs={{6,2},{7,3},{10,6},{11,7},{14,10},{15,11},{12,14},{13,15},{8,12},{... | collective-permute-start | bytes 798728 | tf_op jit(solution)/shard_map/ppermute | solution.py:285
  21.6 12.5 %collective-permute-start.6 = (bf16[1040,128]{1,0:T(8,128)(2,1)S(1)}, bf16[1040,128]{1,0:T(8,128)(2,1)S(1)}, u32[]{:S(2)}, u32[]{:S(2)}) collective-permute-start(bf16[1040,128]{1,0:T(8,128)(2,1)S(1)} %collective-permute-done.4.refs_0_), channel_id=1, source_target_pairs={{2,6},{3,7},{6,10},{7,11},{10,14},{11,15},{14,12},{15,13},{12,8},{... | collective-permute-start | bytes 798728 | tf_op jit(solution)/shard_map/ppermute | solution.py:285
  23.2 11.6 %collective-permute-start.7 = (bf16[1040,128]{1,0:T(8,128)(2,1)S(1)}, bf16[1040,128]{1,0:T(8,128)(2,1)S(1)}, u32[]{:S(2)}, u32[]{:S(2)}) collective-permute-start(bf16[1040,128]{1,0:T(8,128)(2,1)S(1)} %collective-permute-done.5.refs_1_), channel_id=1, source_target_pairs={{6,2},{7,3},{10,6},{11,7},{14,10},{15,11},{12,14},{13,15},{8,12},{... | collective-permute-start | bytes 798728 | tf_op jit(solution)/shard_map/ppermute | solution.py:285
  23.6 2.8 %copy-start = (bf16[1,1,2048,1536]{3,2,1,0:T(8,128)(2,1)S(1)}, bf16[1,1,2048,1536]{3,2,1,0:T(8,128)(2,1)}, u32[]{:S(2)}) copy-start(bf16[1,1,2048,1536]{3,2,1,0:T(8,128)(2,1)} %param.12) | copy-start | bytes 18874372
  29.2 10.3 %collective-permute-start.10 = (bf16[1040,128]{1,0:T(8,128)(2,1)S(1)}, bf16[1040,128]{1,0:T(8,128)(2,1)S(1)}, u32[]{:S(2)}, u32[]{:S(2)}) collective-permute-start(bf16[1040,128]{1,0:T(8,128)(2,1)S(1)} %collective-permute-done.8.refs_0_), channel_id=1, source_target_pairs={{2,6},{3,7},{6,10},{7,11},{10,14},{11,15},{14,12},{15,13},{12,8},{... | collective-permute-start | bytes 798728 | tf_op jit(solution)/shard_map/ppermute | solution.py:285
  30.8 9.6 %collective-permute-start.11 = (bf16[1040,128]{1,0:T(8,128)(2,1)S(1)}, bf16[1040,128]{1,0:T(8,128)(2,1)S(1)}, u32[]{:S(2)}, u32[]{:S(2)}) collective-permute-start(bf16[1040,128]{1,0:T(8,128)(2,1)S(1)} %collective-permute-done.9.refs_1_), channel_id=1, source_target_pairs={{6,2},{7,3},{10,6},{11,7},{14,10},{15,11},{12,14},{13,15},{8,12},{... | collective-permute-start | bytes 798728 | tf_op jit(solution)/shard_map/ppermute | solution.py:285
  34.7 10.5 %collective-permute-start.12 = (bf16[1040,128]{1,0:T(8,128)(2,1)S(1)}, bf16[1040,128]{1,0:T(8,128)(2,1)S(1)}, u32[]{:S(2)}, u32[]{:S(2)}) collective-permute-start(bf16[1040,128]{1,0:T(8,128)(2,1)S(1)} %collective-permute-done.6.refs_0_), channel_id=1, source_target_pairs={{2,6},{3,7},{6,10},{7,11},{10,14},{11,15},{14,12},{15,13},{12,8},{... | collective-permute-start | bytes 798728 | tf_op jit(solution)/shard_map/ppermute | solution.py:285
  36.3 9.8 %collective-permute-start.13 = (bf16[1040,128]{1,0:T(8,128)(2,1)S(1)}, bf16[1040,128]{1,0:T(8,128)(2,1)S(1)}, u32[]{:S(2)}, u32[]{:S(2)}) collective-permute-start(bf16[1040,128]{1,0:T(8,128)(2,1)S(1)} %collective-permute-done.7.refs_1_), channel_id=1, source_target_pairs={{6,2},{7,3},{10,6},{11,7},{14,10},{15,11},{12,14},{13,15},{8,12},{... | collective-permute-start | bytes 798728 | tf_op jit(solution)/shard_map/ppermute | solution.py:285
  40.5 10.1 %collective-permute-start.14 = (bf16[1040,128]{1,0:T(8,128)(2,1)S(1)}, bf16[1040,128]{1,0:T(8,128)(2,1)S(1)}, u32[]{:S(2)}, u32[]{:S(2)}) collective-permute-start(bf16[1040,128]{1,0:T(8,128)(2,1)S(1)} %collective-permute-done.10.refs_0_), channel_id=1, source_target_pairs={{2,6},{3,7},{6,10},{7,11},{10,14},{11,15},{14,12},{15,13},{12,8},{... | collective-permute-start | bytes 798728 | tf_op jit(solution)/shard_map/ppermute | solution.py:285
  42.0 8.5 %collective-permute-start.15 = (bf16[1040,128]{1,0:T(8,128)(2,1)S(1)}, bf16[1040,128]{1,0:T(8,128)(2,1)S(1)}, u32[]{:S(2)}, u32[]{:S(2)}) collective-permute-start(bf16[1040,128]{1,0:T(8,128)(2,1)S(1)} %collective-permute-done.11.refs_1_), channel_id=1, source_target_pairs={{6,2},{7,3},{10,6},{11,7},{14,10},{15,11},{12,14},{13,15},{8,12},{... | collective-permute-start | bytes 798728 | tf_op jit(solution)/shard_map/ppermute | solution.py:285
  46.2 10.8 %collective-permute-start.18 = (bf16[1040,128]{1,0:T(8,128)(2,1)S(1)}, bf16[1040,128]{1,0:T(8,128)(2,1)S(1)}, u32[]{:S(2)}, u32[]{:S(2)}) collective-permute-start(bf16[1040,128]{1,0:T(8,128)(2,1)S(1)} %collective-permute-done.12.refs_0_), channel_id=1, source_target_pairs={{2,6},{3,7},{6,10},{7,11},{10,14},{11,15},{14,12},{15,13},{12,8},{... | collective-permute-start | bytes 798728 | tf_op jit(solution)/shard_map/ppermute | solution.py:285
  50.5 9.3 %collective-permute-start.19 = (bf16[1040,128]{1,0:T(8,128)(2,1)S(1)}, bf16[1040,128]{1,0:T(8,128)(2,1)S(1)}, u32[]{:S(2)}, u32[]{:S(2)}) collective-permute-start(bf16[1040,128]{1,0:T(8,128)(2,1)S(1)} %collective-permute-done.15.refs_1_), channel_id=1, source_target_pairs={{6,2},{7,3},{10,6},{11,7},{14,10},{15,11},{12,14},{13,15},{8,12},{... | collective-permute-start | bytes 798728 | tf_op jit(solution)/shard_map/ppermute | solution.py:285
  54.8 10.7 %collective-permute-start.16 = (bf16[64,2048]{1,0:T(8,128)(2,1)S(1)}, bf16[64,2048]{1,0:T(8,128)(2,1)S(1)}, u32[]{:S(2)}, u32[]{:S(2)}) collective-permute-start(bf16[64,2048]{1,0:T(8,128)(2,1)S(1)} %convert_element_type.73), channel_id=1, source_target_pairs={{6,2},{7,3},{10,6},{11,7},{14,10},{15,11},{12,14},{13,15},{8,12},{... | collective-permute-start | bytes 786440 | tf_op jit(solution)/shard_map/ppermute | solution.py:285
  56.4 9.1 %collective-permute-start.17 = (bf16[64,2048]{1,0:T(8,128)(2,1)S(1)}, bf16[64,2048]{1,0:T(8,128)(2,1)S(1)}, u32[]{:S(2)}, u32[]{:S(2)}) collective-permute-start(bf16[64,2048]{1,0:T(8,128)(2,1)S(1)} %convert_element_type.74), channel_id=1, source_target_pairs={{2,6},{3,7},{6,10},{7,11},{10,14},{11,15},{14,12},{15,13},{12,8},{... | collective-permute-start | bytes 786440 | tf_op jit(solution)/shard_map/ppermute | solution.py:285
  62.7 9.3 %collective-permute-start.23 = (bf16[64,2048]{1,0:T(8,128)(2,1)S(1)}, bf16[64,2048]{1,0:T(8,128)(2,1)S(1)}, u32[]{:S(2)}, u32[]{:S(2)}) collective-permute-start(bf16[64,2048]{1,0:T(8,128)(2,1)S(1)} %convert_element_type.80), channel_id=1, source_target_pairs={{6,2},{7,3},{10,6},{11,7},{14,10},{15,11},{12,14},{13,15},{8,12},{... | collective-permute-start | bytes 786440 | tf_op jit(solution)/shard_map/ppermute | solution.py:285
  64.1 9.3 %collective-permute-start.21 = (bf16[64,2048]{1,0:T(8,128)(2,1)S(1)}, bf16[64,2048]{1,0:T(8,128)(2,1)S(1)}, u32[]{:S(2)}, u32[]{:S(2)}) collective-permute-start(bf16[64,2048]{1,0:T(8,128)(2,1)S(1)} %convert_element_type.75), channel_id=1, source_target_pairs={{2,6},{3,7},{6,10},{7,11},{10,14},{11,15},{14,12},{15,13},{12,8},{... | collective-permute-start | bytes 786440 | tf_op jit(solution)/shard_map/ppermute | solution.py:285
  68.7 15.6 %collective-permute-start.26 = (bf16[64,2048]{1,0:T(8,128)(2,1)S(1)}, bf16[64,2048]{1,0:T(8,128)(2,1)S(1)}, u32[]{:S(2)}, u32[]{:S(2)}) collective-permute-start(bf16[64,2048]{1,0:T(8,128)(2,1)S(1)} %get-tuple-element.100), channel_id=1, source_target_pairs={{2,6},{3,7},{6,10},{7,11},{10,14},{11,15},{14,12},{15,13},{12,8},{... | collective-permute-start | bytes 786440 | tf_op jit(solution)/shard_map/ppermute | solution.py:285
  70.1 16.0 %collective-permute-start.20 = (bf16[64,2048]{1,0:T(8,128)(2,1)S(1)}, bf16[64,2048]{1,0:T(8,128)(2,1)S(1)}, u32[]{:S(2)}, u32[]{:S(2)}) collective-permute-start(bf16[64,2048]{1,0:T(8,128)(2,1)S(1)} %get-tuple-element.92), channel_id=1, source_target_pairs={{6,2},{7,3},{10,6},{11,7},{14,10},{15,11},{12,14},{13,15},{8,12},{... | collective-permute-start | bytes 786440 | tf_op jit(solution)/shard_map/ppermute | solution.py:285
  72.0 10.0 %collective-permute-start.24 = (bf16[64,2048]{1,0:T(8,128)(2,1)S(1)}, bf16[64,2048]{1,0:T(8,128)(2,1)S(1)}, u32[]{:S(2)}, u32[]{:S(2)}) collective-permute-start(bf16[64,2048]{1,0:T(8,128)(2,1)S(1)} %add_convert_fusion.5), channel_id=1, source_target_pairs={{6,2},{7,3},{10,6},{11,7},{14,10},{15,11},{12,14},{13,15},{8,12},{... | collective-permute-start | bytes 786440 | tf_op jit(solution)/shard_map/ppermute | solution.py:285
  73.5 9.4 %collective-permute-start.22 = (bf16[64,2048]{1,0:T(8,128)(2,1)S(1)}, bf16[64,2048]{1,0:T(8,128)(2,1)S(1)}, u32[]{:S(2)}, u32[]{:S(2)}) collective-permute-start(bf16[64,2048]{1,0:T(8,128)(2,1)S(1)} %add_convert_fusion.7), channel_id=1, source_target_pairs={{2,6},{3,7},{6,10},{7,11},{10,14},{11,15},{14,12},{15,13},{12,8},{... | collective-permute-start | bytes 786440 | tf_op jit(solution)/shard_map/ppermute | solution.py:285
  82.1 8.4 %collective-permute-start.30 = (bf16[64,2048]{1,0:T(8,128)(2,1)S(1)}, bf16[64,2048]{1,0:T(8,128)(2,1)S(1)}, u32[]{:S(2)}, u32[]{:S(2)}) collective-permute-start(bf16[64,2048]{1,0:T(8,128)(2,1)S(1)} %add_convert_fusion.4), channel_id=1, source_target_pairs={{6,2},{7,3},{10,6},{11,7},{14,10},{15,11},{12,14},{13,15},{8,12},{... | collective-permute-start | bytes 786440 | tf_op jit(solution)/shard_map/ppermute | solution.py:285
  83.0 9.2 %collective-permute-start.28 = (bf16[64,2048]{1,0:T(8,128)(2,1)S(1)}, bf16[64,2048]{1,0:T(8,128)(2,1)S(1)}, u32[]{:S(2)}, u32[]{:S(2)}) collective-permute-start(bf16[64,2048]{1,0:T(8,128)(2,1)S(1)} %add_convert_fusion.6), channel_id=1, source_target_pairs={{2,6},{3,7},{6,10},{7,11},{10,14},{11,15},{14,12},{15,13},{12,8},{... | collective-permute-start | bytes 786440 | tf_op jit(solution)/shard_map/ppermute | solution.py:285
  84.4 10.0 %collective-permute-start.27 = (bf16[64,2048]{1,0:T(8,128)(2,1)S(1)}, bf16[64,2048]{1,0:T(8,128)(2,1)S(1)}, u32[]{:S(2)}, u32[]{:S(2)}) collective-permute-start(bf16[64,2048]{1,0:T(8,128)(2,1)S(1)} %add_convert_fusion.2), channel_id=1, source_target_pairs={{2,6},{3,7},{6,10},{7,11},{10,14},{11,15},{14,12},{15,13},{12,8},{... | collective-permute-start | bytes 786440 | tf_op jit(solution)/shard_map/ppermute | solution.py:285
  86.1 8.3 %collective-permute-start.25 = (bf16[64,2048]{1,0:T(8,128)(2,1)S(1)}, bf16[64,2048]{1,0:T(8,128)(2,1)S(1)}, u32[]{:S(2)}, u32[]{:S(2)}) collective-permute-start(bf16[64,2048]{1,0:T(8,128)(2,1)S(1)} %add_convert_fusion.3), channel_id=1, source_target_pairs={{6,2},{7,3},{10,6},{11,7},{14,10},{15,11},{12,14},{13,15},{8,12},{... | collective-permute-start | bytes 786440 | tf_op jit(solution)/shard_map/ppermute | solution.py:285
  90.6 6.4 %collective-permute-start.31 = (bf16[64,2048]{1,0:T(8,128)(2,1)S(1)}, bf16[64,2048]{1,0:T(8,128)(2,1)S(1)}, u32[]{:S(2)}, u32[]{:S(2)}) collective-permute-start(bf16[64,2048]{1,0:T(8,128)(2,1)S(1)} %add_convert_fusion), channel_id=1, source_target_pairs={{6,2},{7,3},{10,6},{11,7},{14,10},{15,11},{12,14},{13,15},{8,12},{... | collective-permute-start | bytes 786440 | tf_op jit(solution)/shard_map/ppermute | solution.py:285
  92.2 6.4 %collective-permute-start.29 = (bf16[64,2048]{1,0:T(8,128)(2,1)S(1)}, bf16[64,2048]{1,0:T(8,128)(2,1)S(1)}, u32[]{:S(2)}, u32[]{:S(2)}) collective-permute-start(bf16[64,2048]{1,0:T(8,128)(2,1)S(1)} %add_convert_fusion.1), channel_id=1, source_target_pairs={{2,6},{3,7},{6,10},{7,11},{10,14},{11,15},{14,12},{15,13},{12,8},{... | collective-permute-start | bytes 786440 | tf_op jit(solution)/shard_map/ppermute | solution.py:285

commit v18 on v14

--- a/solution.py
+++ b/solution.py
@@ -239,6 +239,24 @@
     )(expert_id, *payloads, *own, *other, *terms, *totals, *earlier, *chain)
 
 
+def add_kernel(*refs):
+    for term, total, out in ((refs[0], refs[2], refs[5]), (refs[1], refs[3], refs[6])):
+        out[...] = (term[...] + total[...].astype(jnp.float32)).astype(jnp.bfloat16)
+
+
+def add_rows(terms, totals, after):
+    vmem = pl.BlockSpec(memory_space=pltpu.VMEM)
+    return pl.pallas_call(
+        add_kernel,
+        out_shape=[jax.ShapeDtypeStruct(total.shape, jnp.bfloat16) for total in totals],
+        in_specs=[vmem] * 4 + [pl.BlockSpec(memory_space=pl.ANY)],
+        out_specs=[vmem] * 2,
+        compiler_params=pltpu.CompilerParams(vmem_limit_bytes=8 * MIB),
+        cost_estimate=pl.CostEstimate(flops=2 * terms[0].size, bytes_accessed=terms[0].size * 16, transcendentals=0),
+        name="add_rows",
+    )(*terms, *totals, after)
+
+
 def last_kernel(near0_ref, near1_ref, total0_ref, total1_ref, out_ref):
     half = near0_ref.shape[0]
     for start, near_ref, total_ref in ((0, near0_ref, total0_ref), (half, near1_ref, total1_ref)):
@@ -336,7 +354,9 @@
     long = [(to_up, 0, up), (to_down, 1, down)]
     short_totals = [send_on(flow, hops - 1, None, to_up[hops - 1, 1])[1] for flow in short]
     long_totals = [send_on(flow, hops, None, None)[1] for flow in long]
-    *own_sums, down_sum, up_sum = mlp(packed, [f[0][hops - 2, f[1]] for f in short], short_totals, 0, early_sums)
+    down_sum, up_sum = add_rows([f[0][hops - 2, f[1]] for f in short], short_totals, last)
+    last = down_sum
+    own_sums = mlp(packed, (), (), 0, early_sums)
     short_totals = [move(total, flow[2]) for total, flow in zip((down_sum, up_sum), short)]
     after = None
     for s in reversed(range(1, hops)):

time: 98.7 us -> 98.3 us (level)
  transfers between devices with their start and end apart: 32 -> 32, of which waited for: 13 -> 14; matrix products, arithmetic and copies ran while one was open for 2% -> 2% of each run, Pallas kernels for 23% -> 23%
where the time goes in v18:
time: 98.3 us; the launch traced here: 97.9 us
  starting transfers between devices  37 us (38%)
  waiting for transfers between devices  29 us (30%)
  Pallas kernels  23.6 us (24%)
  local copies, waits for them, and re-layouts  7.21 us (7%)
    ppermute x30, starting transfers between devices, move(): return lax.ppermute(value, 'expert', pairs)  30.8 us
    ppermute x30, waiting for transfers between devices, move(): return lax.ppermute(value, 'expert', pairs)  24.5 us
    pallas_call x9, Pallas kernels, expert_rows(): pl.pallas_call(functools.partial(mlp_kernel, parts=len(payloads), adds=le...  22.3 us
    ppermute x2, starting transfers between devices, from_behind(): return lax.ppermute(value, axis, pairs)  6.18 us
    unnamed x12, local copies, waits for them, and re-layouts  5.89 us
    ppermute x2, waiting for transfers between devices, from_behind(): return lax.ppermute(value, axis, pairs)  4.5 us
  transfers between devices with their start and end apart: 32, of which 14 were waited for; matrix products, arithmetic and copies ran while one was open for 2% of the time, Pallas kernels for 23%

profile of v18, /device:TPU:0, one launch (start us, length us, event | category | flops | bytes accessed | tf_op | source)
XLA Modules:
  0.0 97.9 jit_solution(9713919968295219673)
XLA Ops:
  0.0 0.5 collective-permute-start.2
  0.5 1.3 %slice_bitcast_fusion = (bf16[64,2048]{1,0:T(8,128)(2,1)S(1)}, bf16[64,2048]{1,0:T(8,128)(2,1)S(1)}) fusion(bf16[1,128,2048]{2,1,0:T(8,128)(2,1)} %param.8), kind=kLoop, calls=%fused_computation.10 | loop fusion | bytes 1048576 | tf_op jit(solution)/shard_map/squeeze | solution.py:310
  1.8 4.9 %collective-permute-start = (bf16[64,2048]{1,0:T(8,128)(2,1)S(1)}, bf16[64,2048]{1,0:T(8,128)(2,1)S(1)}, u32[]{:S(2)}, u32[]{:S(2)}) collective-permute-start(bf16[64,2048]{1,0:T(8,128)(2,1)S(1)} %get-tuple-element.106), channel_id=1, source_target_pairs={{0,16},{1,17},{2,18},{3,19},{4,20},{5,21},{6,22},{7,23},{8,24},{9,... | collective-permute-start | bytes 786440 | tf_op jit(solution)/shard_map/ppermute | solution.py:20
  6.7 1.3 %collective-permute-start.1 = (bf16[64,2048]{1,0:T(8,128)(2,1)S(1)}, bf16[64,2048]{1,0:T(8,128)(2,1)S(1)}, u32[]{:S(2)}, u32[]{:S(2)}) collective-permute-start(bf16[64,2048]{1,0:T(8,128)(2,1)S(1)} %get-tuple-element.105), channel_id=1, source_target_pairs={{0,16},{1,17},{2,18},{3,19},{4,20},{5,21},{6,22},{7,23},{8,24},{9,... | collective-permute-start | bytes 786440 | tf_op jit(solution)/shard_map/ppermute | solution.py:20
  8.1 1.0 %copy-done.2 = bf16[128,2048]{1,0:T(8,128)(2,1)S(1)} copy-done((bf16[128,2048]{1,0:T(8,128)(2,1)S(1)}, bf16[128,2048]{1,0:T(8,128)(2,1)}, u32[]{:S(2)}) %copy-start.2) | copy-done | bytes 524312
  9.1 0.7 copy-done.3
  9.8 0.7 copy-done.4
  10.5 0.7 copy-done.5
  11.2 0.2 base_rows.1
  11.4 2.0 %collective-permute-done.arrived_ref = bf16[64,2048]{1,0:T(8,128)(2,1)S(1)} collective-permute-done((bf16[64,2048]{1,0:T(8,128)(2,1)S(1)}, bf16[64,2048]{1,0:T(8,128)(2,1)S(1)}, u32[]{:S(2)}, u32[]{:S(2)}) %collective-permute-start) | collective-permute-done | bytes 262176 | tf_op jit(solution)/shard_map/ppermute | solution.py:20
  13.5 1.5 %collective-permute-start.6 = (bf16[1040,128]{1,0:T(8,128)(2,1)S(1)}, bf16[1040,128]{1,0:T(8,128)(2,1)S(1)}, u32[]{:S(2)}, u32[]{:S(2)}) collective-permute-start(bf16[1040,128]{1,0:T(8,128)(2,1)S(1)} %get-tuple-element.67.refs_0_), channel_id=1, source_target_pairs={{2,6},{3,7},{6,10},{7,11},{10,14},{11,15},{14,12},{15,13},{12,8},{... | collective-permute-start | bytes 798728 | tf_op jit(solution)/shard_map/ppermute | solution.py:303
  15.0 0.5 collective-permute-start.7
  15.5 2.5 %collective-permute-done.1.arrived_ref = bf16[64,2048]{1,0:T(8,128)(2,1)S(1)} collective-permute-done((bf16[64,2048]{1,0:T(8,128)(2,1)S(1)}, bf16[64,2048]{1,0:T(8,128)(2,1)S(1)}, u32[]{:S(2)}, u32[]{:S(2)}) %collective-permute-start.1) | collective-permute-done | bytes 262176 | tf_op jit(solution)/shard_map/ppermute | solution.py:20
  18.1 1.5 %collective-permute-start.4 = (bf16[1040,128]{1,0:T(8,128)(2,1)S(1)}, bf16[1040,128]{1,0:T(8,128)(2,1)S(1)}, u32[]{:S(2)}, u32[]{:S(2)}) collective-permute-start(bf16[1040,128]{1,0:T(8,128)(2,1)S(1)} %get-tuple-element.65.refs_1_), channel_id=1, source_target_pairs={{2,6},{3,7},{6,10},{7,11},{10,14},{11,15},{14,12},{15,13},{12,8},{... | collective-permute-start | bytes 798728 | tf_op jit(solution)/shard_map/ppermute | solution.py:303
  19.7 0.5 collective-permute-start.5
  20.2 1.3 %collective-permute-done.7.refs_1_ = bf16[1040,128]{1,0:T(8,128)(2,1)S(1)} collective-permute-done((bf16[1040,128]{1,0:T(8,128)(2,1)S(1)}, bf16[1040,128]{1,0:T(8,128)(2,1)S(1)}, u32[]{:S(2)}, u32[]{:S(2)}) %collective-permute-start.7) | collective-permute-done | bytes 266272 | tf_op jit(solution)/shard_map/ppermute | solution.py:303
  21.6 1.6 %collective-permute-start.10 = (bf16[1040,128]{1,0:T(8,128)(2,1)S(1)}, bf16[1040,128]{1,0:T(8,128)(2,1)S(1)}, u32[]{:S(2)}, u32[]{:S(2)}) collective-permute-start(bf16[1040,128]{1,0:T(8,128)(2,1)S(1)} %collective-permute-done.6.refs_0_), channel_id=1, source_target_pairs={{2,6},{3,7},{6,10},{7,11},{10,14},{11,15},{14,12},{15,13},{12,8},{... | collective-permute-start | bytes 798728 | tf_op jit(solution)/shard_map/ppermute | solution.py:303
  23.2 0.4 collective-permute-start.11
  23.6 2.8 %copy-done = bf16[1,1,2048,1536]{3,2,1,0:T(8,128)(2,1)S(1)} copy-done((bf16[1,1,2048,1536]{3,2,1,0:T(8,128)(2,1)S(1)}, bf16[1,1,2048,1536]{3,2,1,0:T(8,128)(2,1)}, u32[]{:S(2)}) %copy-start) | copy-done | bytes 6291480
  26.4 2.8 %expert_rows.9 = (f32[64,2048]{1,0:T(8,128)S(1)}, f32[64,2048]{1,0:T(8,128)S(1)}) custom-call(s32[1]{0:T(128)} %bitcast.6.expert_ref, bf16[1040,128]{1,0:T(8,128)(2,1)S(1)} %collective-permute-done.6.refs_0_, bf16[1040,128]{1,0:T(8,128)(2,1)S(1)} %collective-permute-done.7.refs_1_, bf16[2048,1536]{1,0:T(8,128)(2,1)S(1)} %bitcast.16, ...), custom_call_target="tpu_custom_call" | custom-call | flops 2415919104 | bytes 1572864 | tf_op jit(solution)/shard_map/expert_rows/pallas_call | solution.py:217
  29.2 1.6 %collective-permute-start.8 = (bf16[1040,128]{1,0:T(8,128)(2,1)S(1)}, bf16[1040,128]{1,0:T(8,128)(2,1)S(1)}, u32[]{:S(2)}, u32[]{:S(2)}) collective-permute-start(bf16[1040,128]{1,0:T(8,128)(2,1)S(1)} %collective-permute-done.4.refs_0_), channel_id=1, source_target_pairs={{2,6},{3,7},{6,10},{7,11},{10,14},{11,15},{14,12},{15,13},{12,8},{... | collective-permute-start | bytes 798728 | tf_op jit(solution)/shard_map/ppermute | solution.py:303
  30.8 0.4 collective-permute-start.9
  31.3 2.8 %expert_rows.10 = (f32[64,2048]{1,0:T(8,128)S(1)}, f32[64,2048]{1,0:T(8,128)S(1)}) custom-call(s32[1]{0:T(128)} %bitcast.6.expert_ref, bf16[1040,128]{1,0:T(8,128)(2,1)S(1)} %collective-permute-done.4.refs_0_, bf16[1040,128]{1,0:T(8,128)(2,1)S(1)} %collective-permute-done.5.refs_1_, bf16[2048,1536]{1,0:T(8,128)(2,1)S(1)} %bitcast.17, ...), custom_call_target="tpu_custom_call" | custom-call | flops 2415919104 | bytes 1572864 | tf_op jit(solution)/shard_map/expert_rows/pallas_call | solution.py:217
  34.1 0.7 collective-permute-done.11.refs_1_
  34.7 1.6 %collective-permute-start.14 = (bf16[1040,128]{1,0:T(8,128)(2,1)S(1)}, bf16[1040,128]{1,0:T(8,128)(2,1)S(1)}, u32[]{:S(2)}, u32[]{:S(2)}) collective-permute-start(bf16[1040,128]{1,0:T(8,128)(2,1)S(1)} %collective-permute-done.10.refs_0_), channel_id=1, source_target_pairs={{2,6},{3,7},{6,10},{7,11},{10,14},{11,15},{14,12},{15,13},{12,8},{... | collective-permute-start | bytes 798728 | tf_op jit(solution)/shard_map/ppermute | solution.py:303
  36.3 0.4 collective-permute-start.15
  36.8 2.8 %expert_rows.11 = (f32[64,2048]{1,0:T(8,128)S(1)}, f32[64,2048]{1,0:T(8,128)S(1)}) custom-call(s32[1]{0:T(128)} %bitcast.6.expert_ref, bf16[1040,128]{1,0:T(8,128)(2,1)S(1)} %collective-permute-done.10.refs_0_, bf16[1040,128]{1,0:T(8,128)(2,1)S(1)} %collective-permute-done.11.refs_1_, bf16[2048,1536]{1,0:T(8,128)(2,1)S(1)} %bitcast.18, ...), custom_call_target="tpu_custom_call" | custom-call | flops 2415919104 | bytes 1572864 | tf_op jit(solution)/shard_map/expert_rows/pallas_call | solution.py:217
  39.6 0.9 collective-permute-done.9.refs_1_
  40.4 1.6 %collective-permute-start.12 = (bf16[1040,128]{1,0:T(8,128)(2,1)S(1)}, bf16[1040,128]{1,0:T(8,128)(2,1)S(1)}, u32[]{:S(2)}, u32[]{:S(2)}) collective-permute-start(bf16[1040,128]{1,0:T(8,128)(2,1)S(1)} %collective-permute-done.8.refs_0_), channel_id=1, source_target_pairs={{2,6},{3,7},{6,10},{7,11},{10,14},{11,15},{14,12},{15,13},{12,8},{... | collective-permute-start | bytes 798728 | tf_op jit(solution)/shard_map/ppermute | solution.py:303
  42.0 0.5 collective-permute-start.13
  42.5 2.8 %expert_rows.12 = (f32[64,2048]{1,0:T(8,128)S(1)}, f32[64,2048]{1,0:T(8,128)S(1)}) custom-call(s32[1]{0:T(128)} %bitcast.6.expert_ref, bf16[1040,128]{1,0:T(8,128)(2,1)S(1)} %collective-permute-done.8.refs_0_, bf16[1040,128]{1,0:T(8,128)(2,1)S(1)} %collective-permute-done.9.refs_1_, bf16[2048,1536]{1,0:T(8,128)(2,1)S(1)} %bitcast.19, ...), custom_call_target="tpu_custom_call" | custom-call | flops 2415919104 | bytes 1572864 | tf_op jit(solution)/shard_map/expert_rows/pallas_call | solution.py:217
  45.3 0.9 collective-permute-done.15.refs_1_
  46.2 1.6 %collective-permute-start.18 = (bf16[1040,128]{1,0:T(8,128)(2,1)S(1)}, bf16[1040,128]{1,0:T(8,128)(2,1)S(1)}, u32[]{:S(2)}, u32[]{:S(2)}) collective-permute-start(bf16[1040,128]{1,0:T(8,128)(2,1)S(1)} %collective-permute-done.14.refs_0_), channel_id=1, source_target_pairs={{2,6},{3,7},{6,10},{7,11},{10,14},{11,15},{14,12},{15,13},{12,8},{... | collective-permute-start | bytes 798728 | tf_op jit(solution)/shard_map/ppermute | solution.py:303
  47.7 2.8 %expert_rows.13 = (f32[64,2048]{1,0:T(8,128)S(1)}, f32[64,2048]{1,0:T(8,128)S(1)}) custom-call(s32[1]{0:T(128)} %bitcast.6.expert_ref, bf16[1040,128]{1,0:T(8,128)(2,1)S(1)} %collective-permute-done.14.refs_0_, bf16[1040,128]{1,0:T(8,128)(2,1)S(1)} %collective-permute-done.15.refs_1_, bf16[2048,1536]{1,0:T(8,128)(2,1)S(1)} %bitcast.20, ...), custom_call_target="tpu_custom_call" | custom-call | flops 2415919104 | bytes 1572864 | tf_op jit(solution)/shard_map/expert_rows/pallas_call | solution.py:217
  50.6 1.4 %collective-permute-start.19 = (bf16[1040,128]{1,0:T(8,128)(2,1)S(1)}, bf16[1040,128]{1,0:T(8,128)(2,1)S(1)}, u32[]{:S(2)}, u32[]{:S(2)}) collective-permute-start(bf16[1040,128]{1,0:T(8,128)(2,1)S(1)} %collective-permute-done.13.refs_1_), channel_id=1, source_target_pairs={{6,2},{7,3},{10,6},{11,7},{14,10},{15,11},{12,14},{13,15},{8,12},{... | collective-permute-start | bytes 798728 | tf_op jit(solution)/shard_map/ppermute | solution.py:303
  51.9 2.8 %expert_rows.14 = (f32[64,2048]{1,0:T(8,128)S(1)}, f32[64,2048]{1,0:T(8,128)S(1)}) custom-call(s32[1]{0:T(128)} %bitcast.6.expert_ref, bf16[1040,128]{1,0:T(8,128)(2,1)S(1)} %collective-permute-done.12.refs_0_, bf16[1040,128]{1,0:T(8,128)(2,1)S(1)} %collective-permute-done.13.refs_1_, bf16[2048,1536]{1,0:T(8,128)(2,1)S(1)} %bitcast.21, ...), custom_call_target="tpu_custom_call" | custom-call | flops 2415919104 | bytes 1572864 | tf_op jit(solution)/shard_map/expert_rows/pallas_call | solution.py:217
  54.8 0.8 collective-permute-start.17
  55.6 1.3 %collective-permute-start.16 = (bf16[64,2048]{1,0:T(8,128)(2,1)S(1)}, bf16[64,2048]{1,0:T(8,128)(2,1)S(1)}, u32[]{:S(2)}, u32[]{:S(2)}) collective-permute-start(bf16[64,2048]{1,0:T(8,128)(2,1)S(1)} %convert_element_type.73), channel_id=1, source_target_pairs={{6,2},{7,3},{10,6},{11,7},{14,10},{15,11},{12,14},{13,15},{8,12},{... | collective-permute-start | bytes 786440 | tf_op jit(solution)/shard_map/ppermute | solution.py:303
  56.9 2.1 %collective-permute-done.19.refs_1_ = bf16[1040,128]{1,0:T(8,128)(2,1)S(1)} collective-permute-done((bf16[1040,128]{1,0:T(8,128)(2,1)S(1)}, bf16[1040,128]{1,0:T(8,128)(2,1)S(1)}, u32[]{:S(2)}, u32[]{:S(2)}) %collective-permute-start.19) | collective-permute-done | bytes 266272 | tf_op jit(solution)/shard_map/ppermute | solution.py:303
  59.0 2.8 %expert_rows.16 = (f32[64,2048]{1,0:T(8,128)S(1)}, f32[64,2048]{1,0:T(8,128)S(1)}) custom-call(s32[1]{0:T(128)} %bitcast.6.expert_ref, bf16[1040,128]{1,0:T(8,128)(2,1)S(1)} %collective-permute-done.18.refs_0_, bf16[1040,128]{1,0:T(8,128)(2,1)S(1)} %collective-permute-done.19.refs_1_, bf16[2048,1536]{1,0:T(8,128)(2,1)S(1)} %bitcast.23, ...), custom_call_target="tpu_custom_call" | custom-call | flops 2415919104 | bytes 1572864 | tf_op jit(solution)/shard_map/expert_rows/pallas_call | solution.py:217
  61.8 1.6 %collective-permute-start.21 = (bf16[64,2048]{1,0:T(8,128)(2,1)S(1)}, bf16[64,2048]{1,0:T(8,128)(2,1)S(1)}, u32[]{:S(2)}, u32[]{:S(2)}) collective-permute-start(bf16[64,2048]{1,0:T(8,128)(2,1)S(1)} %convert_element_type.75), channel_id=1, source_target_pairs={{2,6},{3,7},{6,10},{7,11},{10,14},{11,15},{14,12},{15,13},{12,8},{... | collective-permute-start | bytes 786440 | tf_op jit(solution)/shard_map/ppermute | solution.py:303
  63.4 0.6 collective-permute-start.23
  64.0 0.1 add_rows.1
  64.1 1.5 %collective-permute-start.26 = (bf16[64,2048]{1,0:T(8,128)(2,1)S(1)}, bf16[64,2048]{1,0:T(8,128)(2,1)S(1)}, u32[]{:S(2)}, u32[]{:S(2)}) collective-permute-start(bf16[64,2048]{1,0:T(8,128)(2,1)S(1)} %get-tuple-element.100), channel_id=1, source_target_pairs={{2,6},{3,7},{6,10},{7,11},{10,14},{11,15},{14,12},{15,13},{12,8},{... | collective-permute-start | bytes 786440 | tf_op jit(solution)/shard_map/ppermute | solution.py:303
  65.7 0.6 collective-permute-start.20
  66.3 2.8 %expert_rows.17 = (f32[64,2048]{1,0:T(8,128)S(1)}, f32[64,2048]{1,0:T(8,128)S(1)}) custom-call(s32[1]{0:T(128)} %bitcast.6.expert_ref, bf16[1040,128]{1,0:T(8,128)(2,1)S(1)} %get-tuple-element.67.refs_0_, bf16[1040,128]{1,0:T(8,128)(2,1)S(1)} %get-tuple-element.65.refs_1_, bf16[2048,1536]{1,0:T(8,128)(2,1)S(1)} %bitcast.24, bf16[768,2048]{1,0:T(8,128)(2,1)S(1)} %bitcast.34, ...), custom_call_target="tpu_custom_call" | custom-call | flops 2415919104 | bytes 1572864 | tf_op jit(solution)/shard_map/expert_rows/pallas_call | solution.py:217
  69.0 2.1 %collective-permute-done.21 = bf16[64,2048]{1,0:T(8,128)(2,1)S(1)} collective-permute-done((bf16[64,2048]{1,0:T(8,128)(2,1)S(1)}, bf16[64,2048]{1,0:T(8,128)(2,1)S(1)}, u32[]{:S(2)}, u32[]{:S(2)}) %collective-permute-start.21) | collective-permute-done | bytes 262176 | tf_op jit(solution)/shard_map/ppermute | solution.py:303
  71.2 1.6 %collective-permute-start.22 = (bf16[64,2048]{1,0:T(8,128)(2,1)S(1)}, bf16[64,2048]{1,0:T(8,128)(2,1)S(1)}, u32[]{:S(2)}, u32[]{:S(2)}) collective-permute-start(bf16[64,2048]{1,0:T(8,128)(2,1)S(1)} %add_convert_fusion.7), channel_id=1, source_target_pairs={{2,6},{3,7},{6,10},{7,11},{10,14},{11,15},{14,12},{15,13},{12,8},{... | collective-permute-start | bytes 786440 | tf_op jit(solution)/shard_map/ppermute | solution.py:303
  72.8 0.6 collective-permute-start.24
  73.4 6.1 %collective-permute-done.22 = bf16[64,2048]{1,0:T(8,128)(2,1)S(1)} collective-permute-done((bf16[64,2048]{1,0:T(8,128)(2,1)S(1)}, bf16[64,2048]{1,0:T(8,128)(2,1)S(1)}, u32[]{:S(2)}, u32[]{:S(2)}) %collective-permute-start.22) | collective-permute-done | bytes 262176 | tf_op jit(solution)/shard_map/ppermute | solution.py:303
  79.6 1.6 %collective-permute-start.28 = (bf16[64,2048]{1,0:T(8,128)(2,1)S(1)}, bf16[64,2048]{1,0:T(8,128)(2,1)S(1)}, u32[]{:S(2)}, u32[]{:S(2)}) collective-permute-start(bf16[64,2048]{1,0:T(8,128)(2,1)S(1)} %add_convert_fusion.6), channel_id=1, source_target_pairs={{2,6},{3,7},{6,10},{7,11},{10,14},{11,15},{14,12},{15,13},{12,8},{... | collective-permute-start | bytes 786440 | tf_op jit(solution)/shard_map/ppermute | solution.py:303
  81.2 0.6 collective-permute-start.30
  81.8 1.5 %collective-permute-start.27 = (bf16[64,2048]{1,0:T(8,128)(2,1)S(1)}, bf16[64,2048]{1,0:T(8,128)(2,1)S(1)}, u32[]{:S(2)}, u32[]{:S(2)}) collective-permute-start(bf16[64,2048]{1,0:T(8,128)(2,1)S(1)} %add_convert_fusion.2), channel_id=1, source_target_pairs={{2,6},{3,7},{6,10},{7,11},{10,14},{11,15},{14,12},{15,13},{12,8},{... | collective-permute-start | bytes 786440 | tf_op jit(solution)/shard_map/ppermute | solution.py:303
  83.4 0.6 collective-permute-start.25
  84.0 4.8 %collective-permute-done.28 = bf16[64,2048]{1,0:T(8,128)(2,1)S(1)} collective-permute-done((bf16[64,2048]{1,0:T(8,128)(2,1)S(1)}, bf16[64,2048]{1,0:T(8,128)(2,1)S(1)}, u32[]{:S(2)}, u32[]{:S(2)}) %collective-permute-start.28) | collective-permute-done | bytes 262176 | tf_op jit(solution)/shard_map/ppermute | solution.py:303
  88.9 1.6 %collective-permute-start.29 = (bf16[64,2048]{1,0:T(8,128)(2,1)S(1)}, bf16[64,2048]{1,0:T(8,128)(2,1)S(1)}, u32[]{:S(2)}, u32[]{:S(2)}) collective-permute-start(bf16[64,2048]{1,0:T(8,128)(2,1)S(1)} %add_convert_fusion.1), channel_id=1, source_target_pairs={{2,6},{3,7},{6,10},{7,11},{10,14},{11,15},{14,12},{15,13},{12,8},{... | collective-permute-start | bytes 786440 | tf_op jit(solution)/shard_map/ppermute | solution.py:303
  90.5 0.6 collective-permute-start.31
  91.1 1.0 %collective-permute-done.27 = bf16[64,2048]{1,0:T(8,128)(2,1)S(1)} collective-permute-done((bf16[64,2048]{1,0:T(8,128)(2,1)S(1)}, bf16[64,2048]{1,0:T(8,128)(2,1)S(1)}, u32[]{:S(2)}, u32[]{:S(2)}) %collective-permute-start.27) | collective-permute-done | bytes 262176 | tf_op jit(solution)/shard_map/ppermute | solution.py:303
  92.2 0.1 add_add_fusion.near1_ref
  92.3 1.3 %collective-permute-done.25 = bf16[64,2048]{1,0:T(8,128)(2,1)S(1)} collective-permute-done((bf16[64,2048]{1,0:T(8,128)(2,1)S(1)}, bf16[64,2048]{1,0:T(8,128)(2,1)S(1)}, u32[]{:S(2)}, u32[]{:S(2)}) %collective-permute-start.25) | collective-permute-done | bytes 262176 | tf_op jit(solution)/shard_map/ppermute | solution.py:303
  93.5 0.1 add_add_fusion.1.near0_ref
  93.6 1.7 %collective-permute-done.29.total0_ref = bf16[64,2048]{1,0:T(8,128)(2,1)S(1)} collective-permute-done((bf16[64,2048]{1,0:T(8,128)(2,1)S(1)}, bf16[64,2048]{1,0:T(8,128)(2,1)S(1)}, u32[]{:S(2)}, u32[]{:S(2)}) %collective-permute-start.29) | collective-permute-done | bytes 262176 | tf_op jit(solution)/shard_map/ppermute | solution.py:303
  95.3 1.6 %collective-permute-done.31.total1_ref = bf16[64,2048]{1,0:T(8,128)(2,1)S(1)} collective-permute-done((bf16[64,2048]{1,0:T(8,128)(2,1)S(1)}, bf16[64,2048]{1,0:T(8,128)(2,1)S(1)}, u32[]{:S(2)}, u32[]{:S(2)}) %collective-permute-start.31) | collective-permute-done | bytes 262176 | tf_op jit(solution)/shard_map/ppermute | solution.py:303
  97.0 0.9 last_rows.1
  (41 shorter events, 0.8 us)
Async XLA Ops:
  0.0 23.6 %copy-start.1 = (bf16[1,1,768,2048]{3,2,1,0:T(8,128)(2,1)S(1)}, bf16[1,1,768,2048]{3,2,1,0:T(8,128)(2,1)}, u32[]{:S(2)}) copy-start(bf16[1,1,768,2048]{3,2,1,0:T(8,128)(2,1)} %param.13) | copy-start | bytes 9437188
  0.0 18.1 %collective-permute-start.2 = (bf16[2048,1536]{1,0:T(8,128)(2,1)}, bf16[2048,1536]{1,0:T(8,128)(2,1)S(1)}, u32[]{:S(2)}, u32[]{:S(2)}) collective-permute-start(bf16[2048,1536]{1,0:T(8,128)(2,1)} %bitcast.15), channel_id=1, source_target_pairs={{0,1},{1,0},{2,3},{3,2},{4,5},{5,4},{6,7},{7,6},{8,9},{9,8},{10,11... | collective-permute-start | bytes 18874376 | tf_op jit(solution)/shard_map/ppermute | solution.py:303
  0.5 17.7 %collective-permute-start.3 = (bf16[768,2048]{1,0:T(8,128)(2,1)}, bf16[768,2048]{1,0:T(8,128)(2,1)S(1)}, u32[]{:S(2)}, u32[]{:S(2)}) collective-permute-start(bf16[768,2048]{1,0:T(8,128)(2,1)} %bitcast.25), channel_id=1, source_target_pairs={{0,1},{1,0},{2,3},{3,2},{4,5},{5,4},{6,7},{7,6},{8,9},{9,8},{10,11... | collective-permute-start | bytes 9437192 | tf_op jit(solution)/shard_map/ppermute | solution.py:303
  1.8 11.5 %collective-permute-start = (bf16[64,2048]{1,0:T(8,128)(2,1)S(1)}, bf16[64,2048]{1,0:T(8,128)(2,1)S(1)}, u32[]{:S(2)}, u32[]{:S(2)}) collective-permute-start(bf16[64,2048]{1,0:T(8,128)(2,1)S(1)} %get-tuple-element.106), channel_id=1, source_target_pairs={{0,16},{1,17},{2,18},{3,19},{4,20},{5,21},{6,22},{7,23},{8,24},{9,... | collective-permute-start | bytes 786440 | tf_op jit(solution)/shard_map/ppermute | solution.py:20
  6.7 11.3 %collective-permute-start.1 = (bf16[64,2048]{1,0:T(8,128)(2,1)S(1)}, bf16[64,2048]{1,0:T(8,128)(2,1)S(1)}, u32[]{:S(2)}, u32[]{:S(2)}) collective-permute-start(bf16[64,2048]{1,0:T(8,128)(2,1)S(1)} %get-tuple-element.105), channel_id=1, source_target_pairs={{0,16},{1,17},{2,18},{3,19},{4,20},{5,21},{6,22},{7,23},{8,24},{9,... | collective-permute-start | bytes 786440 | tf_op jit(solution)/shard_map/ppermute | solution.py:20
  8.0 1.0 %copy-start.2 = (bf16[128,2048]{1,0:T(8,128)(2,1)S(1)}, bf16[128,2048]{1,0:T(8,128)(2,1)}, u32[]{:S(2)}) copy-start(bf16[128,2048]{1,0:T(8,128)(2,1)} %fresh_ref.1) | copy-start | bytes 1572868
  9.1 0.7 copy-start.3
  9.8 0.7 copy-start.4
  10.5 0.7 copy-start.5
  13.5 6.8 %collective-permute-start.6 = (bf16[1040,128]{1,0:T(8,128)(2,1)S(1)}, bf16[1040,128]{1,0:T(8,128)(2,1)S(1)}, u32[]{:S(2)}, u32[]{:S(2)}) collective-permute-start(bf16[1040,128]{1,0:T(8,128)(2,1)S(1)} %get-tuple-element.67.refs_0_), channel_id=1, source_target_pairs={{2,6},{3,7},{6,10},{7,11},{10,14},{11,15},{14,12},{15,13},{12,8},{... | collective-permute-start | bytes 798728 | tf_op jit(solution)/shard_map/ppermute | solution.py:303
  15.0 6.6 %collective-permute-start.7 = (bf16[1040,128]{1,0:T(8,128)(2,1)S(1)}, bf16[1040,128]{1,0:T(8,128)(2,1)S(1)}, u32[]{:S(2)}, u32[]{:S(2)}) collective-permute-start(bf16[1040,128]{1,0:T(8,128)(2,1)S(1)} %get-tuple-element.67.refs_0_), channel_id=1, source_target_pairs={{6,2},{7,3},{10,6},{11,7},{14,10},{15,11},{12,14},{13,15},{8,12},{... | collective-permute-start | bytes 798728 | tf_op jit(solution)/shard_map/ppermute | solution.py:303
  18.1 11.0 %collective-permute-start.4 = (bf16[1040,128]{1,0:T(8,128)(2,1)S(1)}, bf16[1040,128]{1,0:T(8,128)(2,1)S(1)}, u32[]{:S(2)}, u32[]{:S(2)}) collective-permute-start(bf16[1040,128]{1,0:T(8,128)(2,1)S(1)} %get-tuple-element.65.refs_1_), channel_id=1, source_target_pairs={{2,6},{3,7},{6,10},{7,11},{10,14},{11,15},{14,12},{15,13},{12,8},{... | collective-permute-start | bytes 798728 | tf_op jit(solution)/shard_map/ppermute | solution.py:303
  19.7 9.5 %collective-permute-start.5 = (bf16[1040,128]{1,0:T(8,128)(2,1)S(1)}, bf16[1040,128]{1,0:T(8,128)(2,1)S(1)}, u32[]{:S(2)}, u32[]{:S(2)}) collective-permute-start(bf16[1040,128]{1,0:T(8,128)(2,1)S(1)} %get-tuple-element.65.refs_1_), channel_id=1, source_target_pairs={{6,2},{7,3},{10,6},{11,7},{14,10},{15,11},{12,14},{13,15},{8,12},{... | collective-permute-start | bytes 798728 | tf_op jit(solution)/shard_map/ppermute | solution.py:303
  21.6 12.5 %collective-permute-start.10 = (bf16[1040,128]{1,0:T(8,128)(2,1)S(1)}, bf16[1040,128]{1,0:T(8,128)(2,1)S(1)}, u32[]{:S(2)}, u32[]{:S(2)}) collective-permute-start(bf16[1040,128]{1,0:T(8,128)(2,1)S(1)} %collective-permute-done.6.refs_0_), channel_id=1, source_target_pairs={{2,6},{3,7},{6,10},{7,11},{10,14},{11,15},{14,12},{15,13},{12,8},{... | collective-permute-start | bytes 798728 | tf_op jit(solution)/shard_map/ppermute | solution.py:303
  23.2 11.6 %collective-permute-start.11 = (bf16[1040,128]{1,0:T(8,128)(2,1)S(1)}, bf16[1040,128]{1,0:T(8,128)(2,1)S(1)}, u32[]{:S(2)}, u32[]{:S(2)}) collective-permute-start(bf16[1040,128]{1,0:T(8,128)(2,1)S(1)} %collective-permute-done.7.refs_1_), channel_id=1, source_target_pairs={{6,2},{7,3},{10,6},{11,7},{14,10},{15,11},{12,14},{13,15},{8,12},{... | collective-permute-start | bytes 798728 | tf_op jit(solution)/shard_map/ppermute | solution.py:303
  23.6 2.8 %copy-start = (bf16[1,1,2048,1536]{3,2,1,0:T(8,128)(2,1)S(1)}, bf16[1,1,2048,1536]{3,2,1,0:T(8,128)(2,1)}, u32[]{:S(2)}) copy-start(bf16[1,1,2048,1536]{3,2,1,0:T(8,128)(2,1)} %param.12) | copy-start | bytes 18874372
  29.2 10.4 %collective-permute-start.8 = (bf16[1040,128]{1,0:T(8,128)(2,1)S(1)}, bf16[1040,128]{1,0:T(8,128)(2,1)S(1)}, u32[]{:S(2)}, u32[]{:S(2)}) collective-permute-start(bf16[1040,128]{1,0:T(8,128)(2,1)S(1)} %collective-permute-done.4.refs_0_), channel_id=1, source_target_pairs={{2,6},{3,7},{6,10},{7,11},{10,14},{11,15},{14,12},{15,13},{12,8},{... | collective-permute-start | bytes 798728 | tf_op jit(solution)/shard_map/ppermute | solution.py:303
  30.8 9.6 %collective-permute-start.9 = (bf16[1040,128]{1,0:T(8,128)(2,1)S(1)}, bf16[1040,128]{1,0:T(8,128)(2,1)S(1)}, u32[]{:S(2)}, u32[]{:S(2)}) collective-permute-start(bf16[1040,128]{1,0:T(8,128)(2,1)S(1)} %collective-permute-done.5.refs_1_), channel_id=1, source_target_pairs={{6,2},{7,3},{10,6},{11,7},{14,10},{15,11},{12,14},{13,15},{8,12},{... | collective-permute-start | bytes 798728 | tf_op jit(solution)/shard_map/ppermute | solution.py:303
  34.7 10.5 %collective-permute-start.14 = (bf16[1040,128]{1,0:T(8,128)(2,1)S(1)}, bf16[1040,128]{1,0:T(8,128)(2,1)S(1)}, u32[]{:S(2)}, u32[]{:S(2)}) collective-permute-start(bf16[1040,128]{1,0:T(8,128)(2,1)S(1)} %collective-permute-done.10.refs_0_), channel_id=1, source_target_pairs={{2,6},{3,7},{6,10},{7,11},{10,14},{11,15},{14,12},{15,13},{12,8},{... | collective-permute-start | bytes 798728 | tf_op jit(solution)/shard_map/ppermute | solution.py:303
  36.3 9.8 %collective-permute-start.15 = (bf16[1040,128]{1,0:T(8,128)(2,1)S(1)}, bf16[1040,128]{1,0:T(8,128)(2,1)S(1)}, u32[]{:S(2)}, u32[]{:S(2)}) collective-permute-start(bf16[1040,128]{1,0:T(8,128)(2,1)S(1)} %collective-permute-done.11.refs_1_), channel_id=1, source_target_pairs={{6,2},{7,3},{10,6},{11,7},{14,10},{15,11},{12,14},{13,15},{8,12},{... | collective-permute-start | bytes 798728 | tf_op jit(solution)/shard_map/ppermute | solution.py:303
  40.4 10.1 %collective-permute-start.12 = (bf16[1040,128]{1,0:T(8,128)(2,1)S(1)}, bf16[1040,128]{1,0:T(8,128)(2,1)S(1)}, u32[]{:S(2)}, u32[]{:S(2)}) collective-permute-start(bf16[1040,128]{1,0:T(8,128)(2,1)S(1)} %collective-permute-done.8.refs_0_), channel_id=1, source_target_pairs={{2,6},{3,7},{6,10},{7,11},{10,14},{11,15},{14,12},{15,13},{12,8},{... | collective-permute-start | bytes 798728 | tf_op jit(solution)/shard_map/ppermute | solution.py:303
  42.0 8.5 %collective-permute-start.13 = (bf16[1040,128]{1,0:T(8,128)(2,1)S(1)}, bf16[1040,128]{1,0:T(8,128)(2,1)S(1)}, u32[]{:S(2)}, u32[]{:S(2)}) collective-permute-start(bf16[1040,128]{1,0:T(8,128)(2,1)S(1)} %collective-permute-done.9.refs_1_), channel_id=1, source_target_pairs={{6,2},{7,3},{10,6},{11,7},{14,10},{15,11},{12,14},{13,15},{8,12},{... | collective-permute-start | bytes 798728 | tf_op jit(solution)/shard_map/ppermute | solution.py:303
  46.2 10.7 %collective-permute-start.18 = (bf16[1040,128]{1,0:T(8,128)(2,1)S(1)}, bf16[1040,128]{1,0:T(8,128)(2,1)S(1)}, u32[]{:S(2)}, u32[]{:S(2)}) collective-permute-start(bf16[1040,128]{1,0:T(8,128)(2,1)S(1)} %collective-permute-done.14.refs_0_), channel_id=1, source_target_pairs={{2,6},{3,7},{6,10},{7,11},{10,14},{11,15},{14,12},{15,13},{12,8},{... | collective-permute-start | bytes 798728 | tf_op jit(solution)/shard_map/ppermute | solution.py:303
  50.6 8.4 %collective-permute-start.19 = (bf16[1040,128]{1,0:T(8,128)(2,1)S(1)}, bf16[1040,128]{1,0:T(8,128)(2,1)S(1)}, u32[]{:S(2)}, u32[]{:S(2)}) collective-permute-start(bf16[1040,128]{1,0:T(8,128)(2,1)S(1)} %collective-permute-done.13.refs_1_), channel_id=1, source_target_pairs={{6,2},{7,3},{10,6},{11,7},{14,10},{15,11},{12,14},{13,15},{8,12},{... | collective-permute-start | bytes 798728 | tf_op jit(solution)/shard_map/ppermute | solution.py:303
  54.8 9.2 %collective-permute-start.17 = (bf16[64,2048]{1,0:T(8,128)(2,1)S(1)}, bf16[64,2048]{1,0:T(8,128)(2,1)S(1)}, u32[]{:S(2)}, u32[]{:S(2)}) collective-permute-start(bf16[64,2048]{1,0:T(8,128)(2,1)S(1)} %convert_element_type.74), channel_id=1, source_target_pairs={{2,6},{3,7},{6,10},{7,11},{10,14},{11,15},{14,12},{15,13},{12,8},{... | collective-permute-start | bytes 786440 | tf_op jit(solution)/shard_map/ppermute | solution.py:303
  55.6 8.5 %collective-permute-start.16 = (bf16[64,2048]{1,0:T(8,128)(2,1)S(1)}, bf16[64,2048]{1,0:T(8,128)(2,1)S(1)}, u32[]{:S(2)}, u32[]{:S(2)}) collective-permute-start(bf16[64,2048]{1,0:T(8,128)(2,1)S(1)} %convert_element_type.73), channel_id=1, source_target_pairs={{6,2},{7,3},{10,6},{11,7},{14,10},{15,11},{12,14},{13,15},{8,12},{... | collective-permute-start | bytes 786440 | tf_op jit(solution)/shard_map/ppermute | solution.py:303
  61.8 9.4 %collective-permute-start.21 = (bf16[64,2048]{1,0:T(8,128)(2,1)S(1)}, bf16[64,2048]{1,0:T(8,128)(2,1)S(1)}, u32[]{:S(2)}, u32[]{:S(2)}) collective-permute-start(bf16[64,2048]{1,0:T(8,128)(2,1)S(1)} %convert_element_type.75), channel_id=1, source_target_pairs={{2,6},{3,7},{6,10},{7,11},{10,14},{11,15},{14,12},{15,13},{12,8},{... | collective-permute-start | bytes 786440 | tf_op jit(solution)/shard_map/ppermute | solution.py:303
  63.4 9.3 %collective-permute-start.23 = (bf16[64,2048]{1,0:T(8,128)(2,1)S(1)}, bf16[64,2048]{1,0:T(8,128)(2,1)S(1)}, u32[]{:S(2)}, u32[]{:S(2)}) collective-permute-start(bf16[64,2048]{1,0:T(8,128)(2,1)S(1)} %convert_element_type.80), channel_id=1, source_target_pairs={{6,2},{7,3},{10,6},{11,7},{14,10},{15,11},{12,14},{13,15},{8,12},{... | collective-permute-start | bytes 786440 | tf_op jit(solution)/shard_map/ppermute | solution.py:303
  64.1 17.6 %collective-permute-start.26 = (bf16[64,2048]{1,0:T(8,128)(2,1)S(1)}, bf16[64,2048]{1,0:T(8,128)(2,1)S(1)}, u32[]{:S(2)}, u32[]{:S(2)}) collective-permute-start(bf16[64,2048]{1,0:T(8,128)(2,1)S(1)} %get-tuple-element.100), channel_id=1, source_target_pairs={{2,6},{3,7},{6,10},{7,11},{10,14},{11,15},{14,12},{15,13},{12,8},{... | collective-permute-start | bytes 786440 | tf_op jit(solution)/shard_map/ppermute | solution.py:303
  65.7 17.7 %collective-permute-start.20 = (bf16[64,2048]{1,0:T(8,128)(2,1)S(1)}, bf16[64,2048]{1,0:T(8,128)(2,1)S(1)}, u32[]{:S(2)}, u32[]{:S(2)}) collective-permute-start(bf16[64,2048]{1,0:T(8,128)(2,1)S(1)} %get-tuple-element.91.refs_8_), channel_id=1, source_target_pairs={{6,2},{7,3},{10,6},{11,7},{14,10},{15,11},{12,14},{13,15},{8,12},{... | collective-permute-start | bytes 786440 | tf_op jit(solution)/shard_map/ppermute | solution.py:303
  71.2 8.3 %collective-permute-start.22 = (bf16[64,2048]{1,0:T(8,128)(2,1)S(1)}, bf16[64,2048]{1,0:T(8,128)(2,1)S(1)}, u32[]{:S(2)}, u32[]{:S(2)}) collective-permute-start(bf16[64,2048]{1,0:T(8,128)(2,1)S(1)} %add_convert_fusion.7), channel_id=1, source_target_pairs={{2,6},{3,7},{6,10},{7,11},{10,14},{11,15},{14,12},{15,13},{12,8},{... | collective-permute-start | bytes 786440 | tf_op jit(solution)/shard_map/ppermute | solution.py:303
  72.8 8.3 %collective-permute-start.24 = (bf16[64,2048]{1,0:T(8,128)(2,1)S(1)}, bf16[64,2048]{1,0:T(8,128)(2,1)S(1)}, u32[]{:S(2)}, u32[]{:S(2)}) collective-permute-start(bf16[64,2048]{1,0:T(8,128)(2,1)S(1)} %add_convert_fusion.5), channel_id=1, source_target_pairs={{6,2},{7,3},{10,6},{11,7},{14,10},{15,11},{12,14},{13,15},{8,12},{... | collective-permute-start | bytes 786440 | tf_op jit(solution)/shard_map/ppermute | solution.py:303
  79.6 9.3 %collective-permute-start.28 = (bf16[64,2048]{1,0:T(8,128)(2,1)S(1)}, bf16[64,2048]{1,0:T(8,128)(2,1)S(1)}, u32[]{:S(2)}, u32[]{:S(2)}) collective-permute-start(bf16[64,2048]{1,0:T(8,128)(2,1)S(1)} %add_convert_fusion.6), channel_id=1, source_target_pairs={{2,6},{3,7},{6,10},{7,11},{10,14},{11,15},{14,12},{15,13},{12,8},{... | collective-permute-start | bytes 786440 | tf_op jit(solution)/shard_map/ppermute | solution.py:303
  81.2 9.3 %collective-permute-start.30 = (bf16[64,2048]{1,0:T(8,128)(2,1)S(1)}, bf16[64,2048]{1,0:T(8,128)(2,1)S(1)}, u32[]{:S(2)}, u32[]{:S(2)}) collective-permute-start(bf16[64,2048]{1,0:T(8,128)(2,1)S(1)} %add_convert_fusion.4), channel_id=1, source_target_pairs={{6,2},{7,3},{10,6},{11,7},{14,10},{15,11},{12,14},{13,15},{8,12},{... | collective-permute-start | bytes 786440 | tf_op jit(solution)/shard_map/ppermute | solution.py:303
  81.8 10.4 %collective-permute-start.27 = (bf16[64,2048]{1,0:T(8,128)(2,1)S(1)}, bf16[64,2048]{1,0:T(8,128)(2,1)S(1)}, u32[]{:S(2)}, u32[]{:S(2)}) collective-permute-start(bf16[64,2048]{1,0:T(8,128)(2,1)S(1)} %add_convert_fusion.2), channel_id=1, source_target_pairs={{2,6},{3,7},{6,10},{7,11},{10,14},{11,15},{14,12},{15,13},{12,8},{... | collective-permute-start | bytes 786440 | tf_op jit(solution)/shard_map/ppermute | solution.py:303
  83.4 10.1 %collective-permute-start.25 = (bf16[64,2048]{1,0:T(8,128)(2,1)S(1)}, bf16[64,2048]{1,0:T(8,128)(2,1)S(1)}, u32[]{:S(2)}, u32[]{:S(2)}) collective-permute-start(bf16[64,2048]{1,0:T(8,128)(2,1)S(1)} %add_convert_fusion.3), channel_id=1, source_target_pairs={{6,2},{7,3},{10,6},{11,7},{14,10},{15,11},{12,14},{13,15},{8,12},{... | collective-permute-start | bytes 786440 | tf_op jit(solution)/shard_map/ppermute | solution.py:303
  88.9 6.4 %collective-permute-start.29 = (bf16[64,2048]{1,0:T(8,128)(2,1)S(1)}, bf16[64,2048]{1,0:T(8,128)(2,1)S(1)}, u32[]{:S(2)}, u32[]{:S(2)}) collective-permute-start(bf16[64,2048]{1,0:T(8,128)(2,1)S(1)} %add_convert_fusion.1), channel_id=1, source_target_pairs={{2,6},{3,7},{6,10},{7,11},{10,14},{11,15},{14,12},{15,13},{12,8},{... | collective-permute-start | bytes 786440 | tf_op jit(solution)/shard_map/ppermute | solution.py:303
  90.5 6.4 %collective-permute-start.31 = (bf16[64,2048]{1,0:T(8,128)(2,1)S(1)}, bf16[64,2048]{1,0:T(8,128)(2,1)S(1)}, u32[]{:S(2)}, u32[]{:S(2)}) collective-permute-start(bf16[64,2048]{1,0:T(8,128)(2,1)S(1)} %add_convert_fusion), channel_id=1, source_target_pairs={{6,2},{7,3},{10,6},{11,7},{14,10},{15,11},{12,14},{13,15},{8,12},{... | collective-permute-start | bytes 786440 | tf_op jit(solution)/shard_map/ppermute | solution.py:303
